TPU v7x, 32 devices: a whole 2x2x4 slice. The times are simulated.
32 devices in a mesh: fsdp: 8 (over y, x, core), tp: 4 (over z).
Axes of the slice: x: 2, y: 2, z: 4, core: 2. Of those that a mesh axis runs over, the one named last changes fastest.
Arguments:
- learner_flat: bfloat16 [2, 39845888], P(None, ('fsdp', 'tp')), may hold values from -1.796875 to 1.796875
- param_offsets: int32 [2, 32, 4], replicated, may hold values from 0 to 1243136, as said below
- owner_map: int32 [2, 32], replicated, may hold values from 0 to 7, as said below
- slice_map: int32 [8, 4], replicated, may hold values from 0 to 3, each once within a row
Outputs:
- query_absorbed: bfloat16 [2, 32, 1536, 512], P(None, 'fsdp', 'tp')
- output_absorbed: bfloat16 [2, 32, 7168, 512], P(None, 'fsdp', 'tp')
Inputs may be any that keep to these rules, and one draw needn't show every extreme that they name: `param_offsets`: in each layer the pieces of all heads' four parameters lie in a rank's 1245184 entries one after another in some order, without gaps or intersections; a piece of a parameter holds that parameter's entries divided by 32; the last piece of each layer is a key up-projection piece. `owner_map`: in each layer every index of fsdp owns exactly 4 heads.
All inputs are finite; a program needn't handle non-finite values.
Results may differ from a plain program's by a relative error of at most 0.001.
Values may be sent and summed in bfloat16 or wider, within the bound.
No kernel may reach another device: no remote copies, remote signals or barrier semaphores. Data moves between devices by JAX's collectives and lax.ppermute only.
A program may use at most 64 MiB of HBM per device.

v0:
```python
import functools
import math

import jax
import jax.numpy as jnp
from jax import lax
from jax.experimental import pallas as pl
from jax.experimental.pallas import tpu as pltpu
from jax.sharding import PartitionSpec as P

D = 7168
QR = 1536
KVR = 512
QK_NOPE = 128
V_DIM = 128
LANES = 128
QUERY, KEY, VALUE, OUT = range(4)
VMEM_LIMIT = 48 * 1024 * 1024


def piece_widths(rank_total):
    return (
        QR * QK_NOPE // rank_total,
        QK_NOPE * KVR // rank_total,
        V_DIM * KVR // rank_total,
        D * V_DIM // rank_total,
    )


def pack(table, param_offsets, owner_map, ways, widths, granule, layers, kinds):
    head_count = owner_map.shape[1]
    per_group = head_count // ways
    steps = [widths[kind] // granule for kind in kinds]
    starts = [sum(steps[:i]) for i in range(len(kinds))]
    out = jax.ShapeDtypeStruct(
        (ways, len(layers), per_group, sum(steps)) + table.shape[2:], table.dtype
    )

    def kernel(offsets, owners, source, target, taken, sem):
        for at, layer in enumerate(layers):
            for way in range(ways):
                taken[way] = 0

            @pl.loop(0, head_count)
            def _(head):
                way = owners[layer, head]
                slot = taken[way]
                taken[way] = slot + 1
                for kind, step, start in zip(kinds, steps, starts):
                    begin = lax.div(offsets[layer, head, kind], jnp.int32(granule))
                    pltpu.make_async_copy(
                        source.at[layer, pl.ds(begin, step)],
                        target.at[way, at, slot, pl.ds(start, step)],
                        sem,
                    ).start()

        pltpu.make_async_copy(target, target, sem).wait()

    return pl.pallas_call(
        kernel,
        out_shape=out,
        in_specs=[
            pl.BlockSpec(memory_space=pltpu.SMEM),
            pl.BlockSpec(memory_space=pltpu.SMEM),
            pl.BlockSpec(memory_space=pl.ANY),
        ],
        out_specs=pl.BlockSpec(memory_space=pl.ANY),
        scratch_shapes=[pltpu.SMEM((ways,), jnp.int32), pltpu.SemaphoreType.DMA],
        cost_estimate=pl.CostEstimate(
            flops=0, transcendentals=0, bytes_accessed=2 * 2 * math.prod(out.shape)
        ),
        name="pack",
    )(param_offsets, owner_map, table)


def assemble(gathered):
    t_ways, f_ways, layers, heads, kinds, rows, _ = gathered.shape
    depth = t_ways * f_ways * rows * LANES // KVR
    cuts = KVR // LANES

    def kernel(pieces, out, scratch):
        for kind in range(kinds):
            for f in range(f_ways):
                for t in range(t_ways):
                    scratch[pl.ds((f * t_ways + t) * rows, rows), :] = pieces[t, f, 0, 0, kind].astype(
                        jnp.float32
                    )
            for cut in range(cuts):
                out[0, 0, kind, :, pl.ds(cut * LANES, LANES)] = scratch[
                    pl.ds(cut, depth, stride=cuts), :
                ].astype(jnp.bfloat16)

    return pl.pallas_call(
        kernel,
        grid=(layers, heads),
        out_shape=jax.ShapeDtypeStruct((layers, heads, kinds, depth, KVR), gathered.dtype),
        in_specs=[
            pl.BlockSpec(
                (t_ways, f_ways, 1, 1, kinds, rows, LANES), lambda l, j: (0, 0, l, j, 0, 0, 0)
            )
        ],
        out_specs=pl.BlockSpec((1, 1, kinds, depth, KVR), lambda l, j: (l, j, 0, 0, 0)),
        scratch_shapes=[pltpu.VMEM((depth * cuts, LANES), jnp.float32)],
        compiler_params=pltpu.CompilerParams(vmem_limit_bytes=VMEM_LIMIT),
        name="assemble",
    )(gathered)


def absorb(layer, came_from, part, matrices, outs, shapes, t_ways, rows):
    f_count, heads = part.shape[0], part.shape[1]
    q_rows, o_rows = rows

    def kernel(_, rows_in, mats, *refs):
        q_out, o_out = refs[-2:]
        q_out[0, 0] = jnp.dot(
            rows_in[0, 0, :q_rows], mats[0, 0, 0], preferred_element_type=jnp.float32
        ).astype(jnp.bfloat16)
        o_out[0, 0] = jnp.dot(
            rows_in[0, 0, q_rows:], mats[0, 0, 1], preferred_element_type=jnp.float32
        ).astype(jnp.bfloat16)

    in_specs = [
        pl.BlockSpec((1, 1, q_rows + o_rows, LANES), lambda j, f, t: (f, j, 0, 0)),
        pl.BlockSpec((1, 1) + matrices.shape[2:], lambda j, f, t: (layer, j, 0, 0, 0)),
    ]
    aliases = {}
    args = [part, matrices]
    if outs is not None:
        in_specs += [pl.BlockSpec(memory_space=pl.ANY)] * 2
        aliases = {3: 0, 4: 1}
        args += list(outs)
    work = f_count * heads * (q_rows + o_rows)
    return pl.pallas_call(
        kernel,
        grid_spec=pltpu.PrefetchScalarGridSpec(
            num_scalar_prefetch=1,
            grid=(heads, f_count),
            in_specs=in_specs,
            out_specs=[
                pl.BlockSpec((1, 1, q_rows, KVR), lambda j, f, t: (layer, j, f * t_ways + t[0], 0)),
                pl.BlockSpec((1, 1, o_rows, KVR), lambda j, f, t: (layer, j, f * t_ways + t[0], 0)),
            ],
        ),
        out_shape=shapes,
        input_output_aliases=aliases,
        compiler_params=pltpu.CompilerParams(vmem_limit_bytes=VMEM_LIMIT),
        cost_estimate=pl.CostEstimate(
            flops=2 * work * LANES * KVR,
            transcendentals=0,
            bytes_accessed=2 * work * (LANES + KVR),
        ),
        name="absorb",
    )(came_from.reshape(1), *args)


def absorb_plain(parts, me, matrices, layers, per_group, t_ways, steps, granule):
    results = []
    for kind, (start, step) in enumerate(steps):
        by_layer = []
        for layer in range(layers):
            stacked = jnp.stack([parts[layer][d] for d in range(t_ways)])
            order = lax.rem(me - jnp.arange(t_ways, dtype=jnp.int32) + t_ways, jnp.int32(t_ways))
            rows = jnp.take(stacked, order, axis=0)[:, :, :, start : start + step]
            rows = rows.transpose(2, 1, 0, 3, 4, 5).reshape(per_group, -1, LANES)
            by_layer.append(rows)
        results.append(
            jnp.einsum(
                "lhrc,lhck->lhrk",
                jnp.stack(by_layer),
                matrices[:, :, kind],
                preferred_element_type=jnp.float32,
            ).astype(jnp.bfloat16)
        )
    return tuple(results)


def per_device(learner_flat, param_offsets, owner_map, slice_map):
    f_ways, t_ways = lax.axis_size("fsdp"), lax.axis_size("tp")
    layer_count = learner_flat.shape[0]
    per_group = owner_map.shape[1] // f_ways
    widths = piece_widths(f_ways * t_ways)
    granule = functools.reduce(math.gcd, widths)
    table = learner_flat.reshape(layer_count, -1, granule // LANES, LANES)
    whole_tiles = granule % (16 * LANES) == 0
    steps = [width // granule for width in widths]

    me = lax.axis_index("tp")
    slice_row = lax.dynamic_index_in_dim(slice_map, lax.axis_index("fsdp"), 0, keepdims=False)
    blocks = f_ways // t_ways

    def packed(layers, kinds):
        return pack(table, param_offsets, owner_map, f_ways, widths, granule, layers, kinds)

    def over_fsdp(x):
        return lax.all_to_all(x, "fsdp", split_axis=0, concat_axis=0, tiled=True)

    pairs = packed(tuple(range(layer_count)), (KEY, VALUE))
    pairs = lax.all_gather(over_fsdp(pairs), "tp", axis=0)
    pairs = pairs.reshape(t_ways, f_ways, layer_count, per_group, 2, steps[KEY] * granule // LANES, LANES)
    if whole_tiles:
        matrices = assemble(pairs)
    else:
        matrices = pairs.transpose(2, 3, 4, 1, 0, 5, 6).reshape(layer_count, per_group, 2, -1, KVR)

    parts = []
    for layer in range(layer_count):
        rows = over_fsdp(packed((layer,), (QUERY, OUT)))[:, 0]
        got = []
        for shift in range(t_ways):
            target = lax.rem(me + shift, t_ways)
            piece = lax.dynamic_slice_in_dim(rows, slice_row[target] * blocks, blocks, 0)
            if shift:
                piece = lax.ppermute(
                    piece, "tp", [(i, (i + shift) % t_ways) for i in range(t_ways)]
                )
            got.append(piece)
        parts.append(got)

    if not whole_tiles:
        at = [(0, steps[QUERY]), (steps[QUERY], steps[OUT])]
        return absorb_plain(parts, me, matrices, layer_count, per_group, t_ways, at, granule)

    shapes = tuple(
        jax.ShapeDtypeStruct((layer_count, per_group, rows // t_ways, KVR), jnp.bfloat16)
        for rows in (QR, D)
    )
    rows = (widths[QUERY] // LANES, widths[OUT] // LANES)
    outs = None
    for layer in range(layer_count):
        for shift in range(t_ways):
            part = parts[layer][shift].reshape(blocks, per_group, sum(rows), LANES)
            came_from = lax.rem(me - shift + t_ways, t_ways)
            outs = absorb(layer, came_from, part, matrices, outs, shapes, t_ways, rows)
    return tuple(outs)


def solution(mesh):
    placed = (P(None, ("fsdp", "tp")), P(), P(), P())
    return jax.shard_map(
        per_device,
        mesh=mesh,
        in_specs=placed,
        out_specs=(P(None, "fsdp", "tp", None), P(None, "fsdp", "tp", None)),
        check_vma=False,
    )
```

profile of v0, /device:TPU:10, one launch (start us, length us, event | category | flops | bytes accessed | tf_op | source)
XLA Modules:
  0.0 301.9 jit_solution(9787271754754187240)
XLA Ops:
  7.2 1.4 copy.23.offsets
  8.5 4.6 %copy.26 = bf16[1,2,9728,128]{3,2,1,0:T(8,128)(2,1)} copy(bf16[1,2,9728,128]{3,1,2,0:T(2,128)(2,1)} %bitcast.43) | data formatting | bytes 9961472
  13.2 18.2 %pack.4 = bf16[8,2,4,2,16,128]{5,4,3,2,1,0:T(8,128)(2,1)} custom-call(s32[2,32,4]{2,1,0:T(8,128)} %copy.23.offsets, s32[2,32]{1,0:T(2,128)} %owners.5, bf16[2,608,16,128]{3,2,1,0:T(8,128)(2,1)} %bitcast.40), custom_call_target="tpu_custom_call" | custom-call | bytes 1048576 | tf_op jit(solution)/shard_map/pack/pallas_call | solution.py:59
  31.4 4.3 %all-to-all-start.1 = ((bf16[8,2,4,2,16,128]{5,4,3,2,1,0:T(8,128)(2,1)}), bf16[8,2,4,2,16,128]{5,4,3,2,1,0:T(8,128)(2,1)S(1)}, u32[]{:S(2)}, u32[]{:S(2)}) async-start(bf16[8,2,4,2,16,128]{5,4,3,2,1,0:T(8,128)(2,1)} %pack.4), calls=%async_computation.1 | async-start | bytes 1048576 | tf_op jit(solution)/shard_map/all_to_all | solution.py:195
  35.7 69.9 %pack.5 = bf16[8,1,4,17,16,128]{5,4,3,2,1,0:T(8,128)(2,1)} custom-call(s32[2,32,4]{2,1,0:T(8,128)} %copy.23.offsets, s32[2,32]{1,0:T(2,128)} %owners.5, bf16[2,608,16,128]{3,2,1,0:T(8,128)(2,1)} %bitcast.41), custom_call_target="tpu_custom_call" | custom-call | bytes 4456448 | tf_op jit(solution)/shard_map/pack/pallas_call | solution.py:59
  105.6 0.0 all-to-all-done.1
  105.6 0.0 copy-start.3
  105.6 4.2 %all-to-all-start.2 = ((bf16[8,1,4,17,16,128]{5,4,3,2,1,0:T(8,128)(2,1)}), bf16[8,1,4,17,16,128]{5,4,3,2,1,0:T(8,128)(2,1)S(1)}, u32[]{:S(2)}, u32[]{:S(2)}) async-start(bf16[8,1,4,17,16,128]{5,4,3,2,1,0:T(8,128)(2,1)} %pack.5), calls=%async_computation.2 | async-start | bytes 4456448 | tf_op jit(solution)/shard_map/all_to_all | solution.py:195
  109.8 0.0 all-gather.3.cloned.1.call-start
  109.8 0.0 copy-done.3
  109.8 0.7 all-gather.3.cloned.1.call-update
  110.5 69.9 %pack.3 = bf16[8,1,4,17,16,128]{5,4,3,2,1,0:T(8,128)(2,1)} custom-call(s32[2,32,4]{2,1,0:T(8,128)} %copy.23.offsets, s32[2,32]{1,0:T(2,128)} %owners.5, bf16[2,608,16,128]{3,2,1,0:T(8,128)(2,1)} %bitcast.42), custom_call_target="tpu_custom_call" | custom-call | bytes 4456448 | tf_op jit(solution)/shard_map/pack/pallas_call | solution.py:59
  180.4 0.0 copy-start.4
  180.4 0.0 all-to-all-done.2
  180.4 4.3 %all-to-all-start = ((bf16[8,1,4,17,16,128]{5,4,3,2,1,0:T(8,128)(2,1)}), bf16[8,1,4,17,16,128]{5,4,3,2,1,0:T(8,128)(2,1)}, u32[]{:S(2)}, u32[]{:S(2)}) async-start(bf16[8,1,4,17,16,128]{5,4,3,2,1,0:T(8,128)(2,1)} %pack.3), calls=%async_computation | async-start | bytes 4456448 | tf_op jit(solution)/shard_map/all_to_all | solution.py:195
  184.8 0.0 copy-done.4
  184.8 0.7 fusion
  188.2 1.3 constant_dynamic-slice_fusion
  189.5 1.6 collective-permute-start.5
  191.1 1.2 collective-permute-start.4
  192.3 1.8 collective-permute-start.3
  194.1 17.2 %all-to-all-done = bf16[8,1,4,17,16,128]{5,4,3,2,1,0:T(8,128)(2,1)} async-done(((bf16[8,1,4,17,16,128]{5,4,3,2,1,0:T(8,128)(2,1)}), bf16[8,1,4,17,16,128]{5,4,3,2,1,0:T(8,128)(2,1)}, u32[]{:S(2)}, u32[]{:S(2)}) %all-to-all-start) | async-done | bytes 2228256 | tf_op jit(solution)/shard_map/all_to_all | solution.py:195
  211.4 2.9 constant_dynamic-slice_fusion.1
  214.2 1.6 collective-permute-start.2
  215.8 1.2 collective-permute-start.1
  217.0 10.8 %collective-permute-done.5 = bf16[2,4,17,16,128]{4,3,2,1,0:T(8,128)(2,1)S(1)} collective-permute-done((bf16[2,4,17,16,128]{4,3,2,1,0:T(8,128)(2,1)}, bf16[2,4,17,16,128]{4,3,2,1,0:T(8,128)(2,1)S(1)}, u32[]{:S(2)}, u32[]{:S(2)}) %collective-permute-start.5) | collective-permute-done | bytes 557088 | tf_op jit(solution)/shard_map/ppermute | solution.py:213
  227.9 0.0 copy-start.1
  227.9 0.8 copy-done.1
  228.7 0.0 collective-permute-start
  228.7 0.0 all-gather.3.cloned.1.call-done
  228.7 0.0 copy-start
  228.7 1.6 copy-done
  230.3 0.0 copy-start.2
  230.3 0.9 assemble.1.mats
  231.2 3.9 %absorb.8 = (bf16[2,4,384,512]{3,2,1,0:T(8,128)(2,1)}, bf16[2,4,1792,512]{3,2,1,0:T(8,128)(2,1)}) custom-call(s32[1]{0:T(128)} %bitcast.13._, bf16[2,4,272,128]{3,2,1,0:T(8,128)(2,1)S(1)} %bitcast.33, bf16[2,4,2,128,512]{4,3,2,1,0:T(8,128)(2,1)S(1)} %assemble.1.mats), custom_call_target="tpu_custom_call" | custom-call | flops 285212672 | bytes 2785280 | tf_op jit(solution)/shard_map/absorb/pallas_call | solution.py:133
  235.2 0.0 copy-done.2
  235.2 3.9 %absorb.9 = (bf16[2,4,384,512]{3,2,1,0:T(8,128)(2,1)}, bf16[2,4,1792,512]{3,2,1,0:T(8,128)(2,1)}) custom-call(s32[1]{0:T(128)} %bitcast.9._, bf16[2,4,272,128]{3,2,1,0:T(8,128)(2,1)S(1)} %bitcast.39, bf16[2,4,2,128,512]{4,3,2,1,0:T(8,128)(2,1)S(1)} %assemble.1.mats, ...), custom_call_target="tpu_custom_call", output_to_operand_aliasing={{0}: (3, {}), {1}: (4, {})} | custom-call | flops 285212672 | bytes 2785280 | tf_op jit(solution)/shard_map/absorb/pallas_call | solution.py:133
  239.1 24.9 %collective-permute-done.4 = bf16[2,4,17,16,128]{4,3,2,1,0:T(8,128)(2,1)} collective-permute-done((bf16[2,4,17,16,128]{4,3,2,1,0:T(8,128)(2,1)}, bf16[2,4,17,16,128]{4,3,2,1,0:T(8,128)(2,1)}, u32[]{:S(2)}, u32[]{:S(2)}) %collective-permute-start.4) | collective-permute-done | bytes 557088 | tf_op jit(solution)/shard_map/ppermute | solution.py:213
  264.0 6.0 %absorb.10 = (bf16[2,4,384,512]{3,2,1,0:T(8,128)(2,1)}, bf16[2,4,1792,512]{3,2,1,0:T(8,128)(2,1)}) custom-call(s32[1]{0:T(128)} %bitcast.5._, bf16[2,4,272,128]{3,2,1,0:T(8,128)(2,1)} %bitcast.19.rows_in, bf16[2,4,2,128,512]{4,3,2,1,0:T(8,128)(2,1)S(1)} %assemble.1.mats, ...), custom_call_target="tpu_custom_call", output_to_operand_aliasing={{0}: (3, {}), {1}: (4, {})} | custom-call | flops 285212672 | bytes 2785280 | tf_op jit(solution)/shard_map/absorb/pallas_call | solution.py:133
  270.0 0.0 collective-permute-done.3
  270.0 3.9 %absorb.11 = (bf16[2,4,384,512]{3,2,1,0:T(8,128)(2,1)}, bf16[2,4,1792,512]{3,2,1,0:T(8,128)(2,1)}) custom-call(s32[1]{0:T(128)} %bitcast._, bf16[2,4,272,128]{3,2,1,0:T(8,128)(2,1)S(1)} %bitcast.38, bf16[2,4,2,128,512]{4,3,2,1,0:T(8,128)(2,1)S(1)} %assemble.1.mats, ...), custom_call_target="tpu_custom_call", output_to_operand_aliasing={{0}: (3, {}), {1}: (4, {})} | custom-call | flops 285212672 | bytes 2785280 | tf_op jit(solution)/shard_map/absorb/pallas_call | solution.py:133
  273.9 3.9 %absorb.12 = (bf16[2,4,384,512]{3,2,1,0:T(8,128)(2,1)}, bf16[2,4,1792,512]{3,2,1,0:T(8,128)(2,1)}) custom-call(s32[1]{0:T(128)} %bitcast.13._, bf16[2,4,272,128]{3,2,1,0:T(8,128)(2,1)S(1)} %bitcast.32, bf16[2,4,2,128,512]{4,3,2,1,0:T(8,128)(2,1)S(1)} %assemble.1.mats, ...), custom_call_target="tpu_custom_call", output_to_operand_aliasing={{0}: (3, {}), {1}: (4, {})} | custom-call | flops 285212672 | bytes 2785280 | tf_op jit(solution)/shard_map/absorb/pallas_call | solution.py:133
  277.8 0.0 collective-permute-done.2
  277.8 3.9 %absorb.13 = (bf16[2,4,384,512]{3,2,1,0:T(8,128)(2,1)}, bf16[2,4,1792,512]{3,2,1,0:T(8,128)(2,1)}) custom-call(s32[1]{0:T(128)} %bitcast.9._, bf16[2,4,272,128]{3,2,1,0:T(8,128)(2,1)S(1)} %bitcast.37, bf16[2,4,2,128,512]{4,3,2,1,0:T(8,128)(2,1)S(1)} %assemble.1.mats, ...), custom_call_target="tpu_custom_call", output_to_operand_aliasing={{0}: (3, {}), {1}: (4, {})} | custom-call | flops 285212672 | bytes 2785280 | tf_op jit(solution)/shard_map/absorb/pallas_call | solution.py:133
  281.8 5.4 %collective-permute-done.1 = bf16[2,4,17,16,128]{4,3,2,1,0:T(8,128)(2,1)S(1)} collective-permute-done((bf16[2,4,17,16,128]{4,3,2,1,0:T(8,128)(2,1)}, bf16[2,4,17,16,128]{4,3,2,1,0:T(8,128)(2,1)S(1)}, u32[]{:S(2)}, u32[]{:S(2)}) %collective-permute-start.1) | collective-permute-done | bytes 557088 | tf_op jit(solution)/shard_map/ppermute | solution.py:213
  287.2 3.9 %absorb.14 = (bf16[2,4,384,512]{3,2,1,0:T(8,128)(2,1)}, bf16[2,4,1792,512]{3,2,1,0:T(8,128)(2,1)}) custom-call(s32[1]{0:T(128)} %bitcast.5._, bf16[2,4,272,128]{3,2,1,0:T(8,128)(2,1)S(1)} %bitcast.36, bf16[2,4,2,128,512]{4,3,2,1,0:T(8,128)(2,1)S(1)} %assemble.1.mats, ...), custom_call_target="tpu_custom_call", output_to_operand_aliasing={{0}: (3, {}), {1}: (4, {})} | custom-call | flops 285212672 | bytes 2785280 | tf_op jit(solution)/shard_map/absorb/pallas_call | solution.py:133
  291.1 0.0 collective-permute-done
  291.1 3.9 %absorb.15 = (bf16[2,4,384,512]{3,2,1,0:T(8,128)(2,1)}, bf16[2,4,1792,512]{3,2,1,0:T(8,128)(2,1)}) custom-call(s32[1]{0:T(128)} %bitcast._, bf16[2,4,272,128]{3,2,1,0:T(8,128)(2,1)S(1)} %bitcast.35, bf16[2,4,2,128,512]{4,3,2,1,0:T(8,128)(2,1)S(1)} %assemble.1.mats, ...), custom_call_target="tpu_custom_call", output_to_operand_aliasing={{0}: (3, {}), {1}: (4, {})} | custom-call | flops 285212672 | bytes 2785280 | tf_op jit(solution)/shard_map/absorb/pallas_call | solution.py:133
Async XLA Ops:
  31.4 74.1 %all-to-all-start.1 = ((bf16[8,2,4,2,16,128]{5,4,3,2,1,0:T(8,128)(2,1)}), bf16[8,2,4,2,16,128]{5,4,3,2,1,0:T(8,128)(2,1)S(1)}, u32[]{:S(2)}, u32[]{:S(2)}) async-start(bf16[8,2,4,2,16,128]{5,4,3,2,1,0:T(8,128)(2,1)} %pack.4), calls=%async_computation.1 | async-start | bytes 1048576 | tf_op jit(solution)/shard_map/all_to_all | solution.py:195
  105.6 4.2 %copy-start.3 = (bf16[8,2,4,2,16,128]{5,4,3,2,1,0:T(8,128)(2,1)}, bf16[8,2,4,2,16,128]{5,4,3,2,1,0:T(8,128)(2,1)S(1)}, u32[]{:S(2)}) copy-start(bf16[8,2,4,2,16,128]{5,4,3,2,1,0:T(8,128)(2,1)S(1)} %all-to-all-done.1) | copy-start | bytes 1572868
  105.6 74.8 %all-to-all-start.2 = ((bf16[8,1,4,17,16,128]{5,4,3,2,1,0:T(8,128)(2,1)}), bf16[8,1,4,17,16,128]{5,4,3,2,1,0:T(8,128)(2,1)S(1)}, u32[]{:S(2)}, u32[]{:S(2)}) async-start(bf16[8,1,4,17,16,128]{5,4,3,2,1,0:T(8,128)(2,1)} %pack.5), calls=%async_computation.2 | async-start | bytes 4456448 | tf_op jit(solution)/shard_map/all_to_all | solution.py:195
  109.8 118.9 %all-gather.3.cloned.1.call-start = ((), (), s32[]{:S(2)}) async-start(), calls=%async_computation.3 | async-start | bytes 2621440 | tf_op jit(solution)/shard_map/all_gather | solution.py:198
  180.4 4.4 %copy-start.4 = (s32[8,4]{0,1:T(4,128)S(1)}, s32[8,4]{0,1:T(4,128)}, u32[]{:S(2)}) copy-start(s32[8,4]{0,1:T(4,128)} %param.7) | copy-start | bytes 388
  180.4 30.9 %all-to-all-start = ((bf16[8,1,4,17,16,128]{5,4,3,2,1,0:T(8,128)(2,1)}), bf16[8,1,4,17,16,128]{5,4,3,2,1,0:T(8,128)(2,1)}, u32[]{:S(2)}, u32[]{:S(2)}) async-start(bf16[8,1,4,17,16,128]{5,4,3,2,1,0:T(8,128)(2,1)} %pack.3), calls=%async_computation | async-start | bytes 4456448 | tf_op jit(solution)/shard_map/all_to_all | solution.py:195
  189.5 38.4 %collective-permute-start.5 = (bf16[2,4,17,16,128]{4,3,2,1,0:T(8,128)(2,1)}, bf16[2,4,17,16,128]{4,3,2,1,0:T(8,128)(2,1)S(1)}, u32[]{:S(2)}, u32[]{:S(2)}) collective-permute-start(bf16[2,4,17,16,128]{4,3,2,1,0:T(8,128)(2,1)} %get-tuple-element.31), channel_id=1, source_target_pairs={{0,1},{1,2},{2,3},{3,0},{4,5},{5,6},{6,7},{7,4},{8,9},{9,10},{10,1... | collective-permute-start | bytes 1671176 | tf_op jit(solution)/shard_map/ppermute | solution.py:213
  191.1 72.9 %collective-permute-start.4 = (bf16[2,4,17,16,128]{4,3,2,1,0:T(8,128)(2,1)}, bf16[2,4,17,16,128]{4,3,2,1,0:T(8,128)(2,1)}, u32[]{:S(2)}, u32[]{:S(2)}) collective-permute-start(bf16[2,4,17,16,128]{4,3,2,1,0:T(8,128)(2,1)} %get-tuple-element.32), channel_id=1, source_target_pairs={{0,2},{1,3},{2,0},{3,1},{4,6},{5,7},{6,4},{7,5},{8,10},{9,11},{10,... | collective-permute-start | bytes 1671176 | tf_op jit(solution)/shard_map/ppermute | solution.py:213
  192.3 77.7 %collective-permute-start.3 = (bf16[2,4,17,16,128]{4,3,2,1,0:T(8,128)(2,1)}, bf16[2,4,17,16,128]{4,3,2,1,0:T(8,128)(2,1)S(1)}, u32[]{:S(2)}, u32[]{:S(2)}) collective-permute-start(bf16[2,4,17,16,128]{4,3,2,1,0:T(8,128)(2,1)} %get-tuple-element.33), channel_id=1, source_target_pairs={{0,3},{1,0},{2,1},{3,2},{4,7},{5,4},{6,5},{7,6},{8,11},{9,8},{10,9... | collective-permute-start | bytes 1671176 | tf_op jit(solution)/shard_map/ppermute | solution.py:213
  214.2 63.6 %collective-permute-start.2 = (bf16[2,4,17,16,128]{4,3,2,1,0:T(8,128)(2,1)}, bf16[2,4,17,16,128]{4,3,2,1,0:T(8,128)(2,1)S(1)}, u32[]{:S(2)}, u32[]{:S(2)}) collective-permute-start(bf16[2,4,17,16,128]{4,3,2,1,0:T(8,128)(2,1)} %get-tuple-element.35), channel_id=1, source_target_pairs={{0,1},{1,2},{2,3},{3,0},{4,5},{5,6},{6,7},{7,4},{8,9},{9,10},{10,1... | collective-permute-start | bytes 1671176 | tf_op jit(solution)/shard_map/ppermute | solution.py:213
  215.8 71.4 %collective-permute-start.1 = (bf16[2,4,17,16,128]{4,3,2,1,0:T(8,128)(2,1)}, bf16[2,4,17,16,128]{4,3,2,1,0:T(8,128)(2,1)S(1)}, u32[]{:S(2)}, u32[]{:S(2)}) collective-permute-start(bf16[2,4,17,16,128]{4,3,2,1,0:T(8,128)(2,1)} %get-tuple-element.36), channel_id=1, source_target_pairs={{0,2},{1,3},{2,0},{3,1},{4,6},{5,7},{6,4},{7,5},{8,10},{9,11},{10,... | collective-permute-start | bytes 1671176 | tf_op jit(solution)/shard_map/ppermute | solution.py:213
  227.9 0.8 copy-start.1
  228.7 62.4 %collective-permute-start = (bf16[2,4,17,16,128]{4,3,2,1,0:T(8,128)(2,1)}, bf16[2,4,17,16,128]{4,3,2,1,0:T(8,128)(2,1)S(1)}, u32[]{:S(2)}, u32[]{:S(2)}) collective-permute-start(bf16[2,4,17,16,128]{4,3,2,1,0:T(8,128)(2,1)} %get-tuple-element.37), channel_id=1, source_target_pairs={{0,3},{1,0},{2,1},{3,2},{4,7},{5,4},{6,5},{7,6},{8,11},{9,8},{10,9... | collective-permute-start | bytes 1671176 | tf_op jit(solution)/shard_map/ppermute | solution.py:213
  228.7 1.6 copy-start
  230.3 4.9 %copy-start.2 = (bf16[2,4,17,16,128]{4,3,2,1,0:T(8,128)(2,1)S(1)}, bf16[2,4,17,16,128]{4,3,2,1,0:T(8,128)(2,1)}, u32[]{:S(2)}) copy-start(bf16[2,4,17,16,128]{4,3,2,1,0:T(8,128)(2,1)} %copy-done.1) | copy-start | bytes 1671172
Sparse Core Ops, SparseCore 0:
  112.2 45.4 all-gather.2
where the time goes:
time: 304 us; the launch traced here: 302 us
  Pallas kernels  192 us (63%)
  waiting for transfers between devices  59.1 us (19%)
  starting transfers between devices  20.2 us (7%)
  between operations  16.8 us (6%)
  local copies, waits for them, and re-layouts  13.3 us (4%)
    pallas_call x3, Pallas kernels, pack(): pl.pallas_call(kernel, out_shape=out, in_specs=[pl.BlockSpec(memory_space...  158 us
    ppermute x6, waiting for transfers between devices, per_device(): lax.ppermute(piece, 'tp', [(i, (i + shift) % t_ways) for i in range(t_way...  41.2 us
    pallas_call x8, Pallas kernels, absorb(): pl.pallas_call(kernel, grid_spec=pltpu.PrefetchScalarGridSpec(num_scalar_...  33.4 us
    all_to_all x3, waiting for transfers between devices, over_fsdp(): return lax.all_to_all(x, 'fsdp', split_axis=0, concat_axis=0, tiled=True)  17.2 us
    all_to_all x3, starting transfers between devices, over_fsdp(): return lax.all_to_all(x, 'fsdp', split_axis=0, concat_axis=0, tiled=True)  12.8 us
    unnamed x12, local copies, waits for them, and re-layouts  8.43 us
    ppermute x6, starting transfers between devices, per_device(): lax.ppermute(piece, 'tp', [(i, (i + shift) % t_ways) for i in range(t_way...  7.43 us
  transfers between devices with their start and end apart: 10, of which 4 were waited for; matrix products, arithmetic and copies ran while one was open for 2% of the time, Pallas kernels for 56%

commit v1 on v0

v1 whole, which is shorter than its diff:
```python
import functools
import math

import jax
import jax.numpy as jnp
from jax import lax
from jax.experimental import pallas as pl
from jax.experimental.pallas import tpu as pltpu
from jax.sharding import PartitionSpec as P

D = 7168
QR = 1536
KVR = 512
QK_NOPE = 128
V_DIM = 128
LANES = 128
QUERY, KEY, VALUE, OUT = range(4)
VMEM_LIMIT = 48 * 1024 * 1024


def piece_widths(rank_total):
    return (
        QR * QK_NOPE // rank_total,
        QK_NOPE * KVR // rank_total,
        V_DIM * KVR // rank_total,
        D * V_DIM // rank_total,
    )


def pack(table, param_offsets, owner_map, ways, widths, granule, layers, slots, kinds):
    head_count = owner_map.shape[1]
    steps = [widths[kind] // granule for kind in kinds]
    starts = [sum(steps[:i]) for i in range(len(kinds))]
    out = jax.ShapeDtypeStruct(
        (ways, len(layers), len(slots), sum(steps)) + table.shape[2:], table.dtype
    )

    def kernel(offsets, owners, source, target, taken):
        for at, layer in enumerate(layers):
            for way in range(ways):
                taken[way] = 0

            @pl.loop(0, head_count)
            def _(head):
                way = owners[layer, head]
                slot = taken[way]
                taken[way] = slot + 1

                @pl.when(jnp.logical_and(slot >= slots[0], slot <= slots[-1]))
                def _():
                    for kind, step, start in zip(kinds, steps, starts):
                        begin = lax.div(offsets[layer, head, kind], jnp.int32(granule))
                        target[way, at, slot - slots[0], pl.ds(start, step)] = source[
                            layer, pl.ds(begin, step)
                        ]

    return pl.pallas_call(
        kernel,
        out_shape=out,
        in_specs=[
            pl.BlockSpec(memory_space=pltpu.SMEM),
            pl.BlockSpec(memory_space=pltpu.SMEM),
            pl.BlockSpec(memory_space=pltpu.VMEM),
        ],
        out_specs=pl.BlockSpec(memory_space=pltpu.VMEM),
        scratch_shapes=[pltpu.SMEM((ways,), jnp.int32)],
        compiler_params=pltpu.CompilerParams(vmem_limit_bytes=VMEM_LIMIT),
        cost_estimate=pl.CostEstimate(
            flops=0, transcendentals=0, bytes_accessed=2 * 2 * math.prod(out.shape)
        ),
        name="pack",
    )(param_offsets, owner_map, table)


def spread(x, axis, ways, me):
    up, down = [x], [x]
    for _ in range(ways - 1):
        up.append(lax.ppermute(up[-1], axis, [(i, i + 1) for i in range(ways - 1)]))
        down.append(lax.ppermute(down[-1], axis, [(i + 1, i) for i in range(ways - 1)]))
    return [x] + [jnp.where(me >= d, up[d], down[ways - d]) for d in range(1, ways)]


def assemble(me, spread_parts):
    t_ways = len(spread_parts)
    f_ways, layers, heads, kinds, rows, _ = spread_parts[0].shape
    depth = t_ways * f_ways * rows * LANES // KVR
    cuts = KVR // LANES

    def kernel(me_ref, *refs):
        pieces, (out, scratch) = refs[:t_ways], refs[t_ways:]
        for kind in range(kinds):
            for d in range(t_ways):
                t = lax.rem(me_ref[0] - d + t_ways, t_ways)
                for f in range(f_ways):
                    scratch[pl.ds(pl.multiple_of((f * t_ways + t) * rows, rows), rows), :] = pieces[
                        d
                    ][f, 0, 0, kind].astype(jnp.float32)
            for cut in range(cuts):
                out[0, 0, kind, :, pl.ds(cut * LANES, LANES)] = scratch[
                    pl.ds(cut, depth, stride=cuts), :
                ].astype(jnp.bfloat16)

    return pl.pallas_call(
        kernel,
        grid_spec=pltpu.PrefetchScalarGridSpec(
            num_scalar_prefetch=1,
            grid=(layers, heads),
            in_specs=[
                pl.BlockSpec((f_ways, 1, 1, kinds, rows, LANES), lambda l, j, _: (0, l, j, 0, 0, 0))
            ]
            * t_ways,
            out_specs=pl.BlockSpec((1, 1, kinds, depth, KVR), lambda l, j, _: (l, j, 0, 0, 0)),
            scratch_shapes=[pltpu.VMEM((depth * cuts, LANES), jnp.float32)],
        ),
        out_shape=jax.ShapeDtypeStruct((layers, heads, kinds, depth, KVR), spread_parts[0].dtype),
        compiler_params=pltpu.CompilerParams(vmem_limit_bytes=VMEM_LIMIT),
        name="assemble",
    )(me.reshape(1), *spread_parts)


def absorb(where, layer, slots, own, came, matrices, outs, shapes):
    t_ways = len(came) + 1
    blocks = came[0].shape[0]
    q_rows, o_rows = shapes[0].shape[4], shapes[1].shape[4]

    def kernel(at, *refs):
        parts, mats = refs[:t_ways], refs[t_ways]
        q_out, o_out = refs[-2:]
        for d in range(t_ways):
            t = lax.rem(at[0] - d + t_ways, t_ways)
            for f in range(blocks):
                q_out[0, 0, f, t] = jnp.dot(
                    parts[d][f, 0, :q_rows], mats[0, 0, 0], preferred_element_type=jnp.float32
                ).astype(jnp.bfloat16)
                o_out[0, 0, f, t] = jnp.dot(
                    parts[d][f, 0, q_rows:], mats[0, 0, 1], preferred_element_type=jnp.float32
                ).astype(jnp.bfloat16)

    rows = q_rows + o_rows
    in_specs = [pl.BlockSpec((blocks, 1, rows, LANES), lambda j, at: (at[1], j, 0, 0))]
    in_specs += [pl.BlockSpec((blocks, 1, rows, LANES), lambda j, at: (0, j, 0, 0))] * len(came)
    in_specs += [
        pl.BlockSpec((1, 1) + matrices.shape[2:], lambda j, at: (layer, slots[0] + j, 0, 0, 0))
    ]
    args = [own, *came, matrices]
    aliases = {}
    if outs is not None:
        in_specs += [pl.BlockSpec(memory_space=pl.ANY)] * 2
        aliases = {1 + len(args): 0, 2 + len(args): 1}
        args += list(outs)
    work = t_ways * blocks * len(slots) * rows
    return pl.pallas_call(
        kernel,
        grid_spec=pltpu.PrefetchScalarGridSpec(
            num_scalar_prefetch=1,
            grid=(len(slots),),
            in_specs=in_specs,
            out_specs=[
                pl.BlockSpec(
                    (1, 1) + shape.shape[2:], lambda j, at: (layer, slots[0] + j, 0, 0, 0, 0)
                )
                for shape in shapes
            ],
        ),
        out_shape=shapes,
        input_output_aliases=aliases,
        compiler_params=pltpu.CompilerParams(vmem_limit_bytes=VMEM_LIMIT),
        cost_estimate=pl.CostEstimate(
            flops=2 * work * LANES * KVR,
            transcendentals=0,
            bytes_accessed=2 * work * (LANES + KVR),
        ),
        name="absorb",
    )(where, *args)


def absorb_plain(me, own, came, matrices):
    t_ways = len(came) + 1
    order = lax.rem(me - jnp.arange(t_ways, dtype=jnp.int32) + t_ways, jnp.int32(t_ways))
    rows = jnp.take(jnp.stack([own, *came]), order, axis=0).transpose(2, 1, 0, 3, 4)
    cut = rows.shape[3] * QR // (QR + D)
    return tuple(
        jnp.einsum("hrc,hck->hrk", part, mats, preferred_element_type=jnp.float32).astype(jnp.bfloat16)
        for part, mats in (
            (rows[:, :, :, :cut].reshape(rows.shape[0], -1, LANES), matrices[:, 0]),
            (rows[:, :, :, cut:].reshape(rows.shape[0], -1, LANES), matrices[:, 1]),
        )
    )


def per_device(learner_flat, param_offsets, owner_map, slice_map):
    f_ways, t_ways = lax.axis_size("fsdp"), lax.axis_size("tp")
    layer_count = learner_flat.shape[0]
    per_group = owner_map.shape[1] // f_ways
    widths = piece_widths(f_ways * t_ways)
    granule = functools.reduce(math.gcd, widths)
    table = learner_flat.reshape(layer_count, -1, granule // LANES, LANES)
    whole_tiles = granule % (16 * LANES) == 0
    row_counts = [width // LANES for width in widths]
    rows_total = row_counts[QUERY] + row_counts[OUT]

    me = lax.axis_index("tp")
    slice_row = lax.dynamic_index_in_dim(slice_map, lax.axis_index("fsdp"), 0, keepdims=False)
    blocks = f_ways // t_ways

    def packed(layers, slots, kinds):
        return pack(table, param_offsets, owner_map, f_ways, widths, granule, layers, slots, kinds)

    def over_fsdp(x):
        return lax.all_to_all(x, "fsdp", split_axis=0, concat_axis=0, tiled=True)

    pairs = over_fsdp(packed(range(layer_count), range(per_group), (KEY, VALUE)))
    pairs = pairs.reshape(f_ways, layer_count, per_group, 2, row_counts[KEY], LANES)
    pairs = spread(pairs, "tp", t_ways, me)

    half = max(1, per_group // 2)
    chunks = [
        (layer, range(at, at + half)) for layer in range(layer_count) for at in range(0, per_group, half)
    ]
    exchanged = []
    for layer, slots in chunks:
        rows = over_fsdp(packed((layer,), slots, (QUERY, OUT)))
        rows = rows.reshape(f_ways, len(slots), rows_total, LANES)
        came = []
        for shift in range(1, t_ways):
            block = slice_row[lax.rem(me + shift, t_ways)]
            piece = lax.dynamic_slice_in_dim(rows, block * blocks, blocks, 0)
            came.append(lax.ppermute(piece, "tp", [(i, (i + shift) % t_ways) for i in range(t_ways)]))
        exchanged.append((rows, came))

    if not whole_tiles:
        order = lax.rem(me - jnp.arange(t_ways, dtype=jnp.int32) + t_ways, jnp.int32(t_ways))
        matrices = jnp.take(jnp.stack(pairs), order, axis=0).transpose(2, 3, 4, 1, 0, 5, 6)
        matrices = matrices.reshape(layer_count, per_group, 2, -1, KVR)
        done = [
            absorb_plain(
                me,
                lax.dynamic_slice_in_dim(rows, slice_row[me] * blocks, blocks, 0),
                came,
                matrices[layer, slots[0] : slots[-1] + 1],
            )
            for (layer, slots), (rows, came) in zip(chunks, exchanged)
        ]
        return tuple(
            jnp.concatenate(kind).reshape(layer_count, per_group, -1, KVR) for kind in zip(*done)
        )

    matrices = assemble(me, pairs)
    shapes = tuple(
        jax.ShapeDtypeStruct(
            (layer_count, per_group, blocks, t_ways, row_counts[kind], KVR), jnp.bfloat16
        )
        for kind in (QUERY, OUT)
    )
    where = jnp.stack([me, slice_row[me]])
    outs = None
    for (layer, slots), (rows, came) in zip(chunks, exchanged):
        outs = absorb(where, layer, slots, rows, came, matrices, outs, shapes)
    return tuple(out.reshape(layer_count, per_group, -1, KVR) for out in outs)


def solution(mesh):
    placed = (P(None, ("fsdp", "tp")), P(), P(), P())
    return jax.shard_map(
        per_device,
        mesh=mesh,
        in_specs=placed,
        out_specs=(P(None, "fsdp", "tp", None), P(None, "fsdp", "tp", None)),
        check_vma=False,
    )
```

time: 304 us -> 231 us (0.76)
  Pallas kernels: 192 us -> 28.2 us
  starting transfers between devices: 20.2 us -> 76.2 us
  waiting for transfers between devices: 59.1 us -> 93.9 us
  between operations: 16.8 us -> 2.85 us
  local copies, waits for them, and re-layouts: 13.3 us -> 24.2 us
  other arithmetic: 0 us -> 4.1 us
    pallas_call x3 -> x5, Pallas kernels: 158 us -> 11.9 us  [pack(): pl.pallas_call(kernel, out_shape=out, in_specs=[pl.BlockSpec(memory_space...]
    ppermute x6 -> x12, starting transfers between devices: 7.43 us -> 32.6 us  [per_device(): lax.ppermute(piece, 'tp', [(i, (i + shift) % t_ways) for i in range(t_way...]
    ppermute x0 -> x6, starting transfers between devices: none -> 19.5 us  [the longest x3 10.9 us: spread(): up.append(lax.ppermute(up[-1], axis, [(i, i + 1) for i in range(ways - 1)]))]
    pallas_call x8 -> x4, Pallas kernels: 33.4 us -> 15 us  [absorb(): pl.pallas_call(kernel, grid_spec=pltpu.PrefetchScalarGridSpec(num_scalar_...]
    ppermute x6 -> x12, waiting for transfers between devices: 41.2 us -> 54 us  [per_device(): lax.ppermute(piece, 'tp', [(i, (i + shift) % t_ways) for i in range(t_way...]
    unnamed x12 -> x44, local copies, waits for them, and re-layouts: 8.43 us -> 20.7 us
    all_to_all x3 -> x5, waiting for transfers between devices: 17.2 us -> 28.7 us  [over_fsdp(): return lax.all_to_all(x, 'fsdp', split_axis=0, concat_axis=0, tiled=True)]
    all_to_all x3 -> x5, starting transfers between devices: 12.8 us -> 24.2 us  [over_fsdp(): return lax.all_to_all(x, 'fsdp', split_axis=0, concat_axis=0, tiled=True)]
  transfers between devices with their start and end apart: 10 -> 23, of which waited for: 4 -> 14; matrix products, arithmetic and copies ran while one was open for 2% -> 3% of each run, Pallas kernels for 56% -> 9%
where the time goes in v1:
time: 231 us; the launch traced here: 229 us
  waiting for transfers between devices  93.9 us (41%)
  starting transfers between devices  76.2 us (33%)
  Pallas kernels  28.2 us (12%)
  local copies, waits for them, and re-layouts  24.2 us (10%)
  other arithmetic  4.1 us (2%)
  between operations  2.85 us (1%)
    ppermute x12, waiting for transfers between devices, per_device(): lax.ppermute(piece, 'tp', [(i, (i + shift) % t_ways) for i in range(t_way...  54 us
    ppermute x12, starting transfers between devices, per_device(): lax.ppermute(piece, 'tp', [(i, (i + shift) % t_ways) for i in range(t_way...  32.6 us
    all_to_all x5, waiting for transfers between devices, over_fsdp(): return lax.all_to_all(x, 'fsdp', split_axis=0, concat_axis=0, tiled=True)  28.7 us
    all_to_all x5, starting transfers between devices, over_fsdp(): return lax.all_to_all(x, 'fsdp', split_axis=0, concat_axis=0, tiled=True)  24.2 us
    unnamed x44, local copies, waits for them, and re-layouts  20.7 us
    pallas_call x4, Pallas kernels, absorb(): pl.pallas_call(kernel, grid_spec=pltpu.PrefetchScalarGridSpec(num_scalar_...  15 us
    pallas_call x5, Pallas kernels, pack(): pl.pallas_call(kernel, out_shape=out, in_specs=[pl.BlockSpec(memory_space...  11.9 us
    ppermute x3, waiting for transfers between devices, spread(): up.append(lax.ppermute(up[-1], axis, [(i, i + 1) for i in range(ways - 1)]))  11.2 us
  transfers between devices with their start and end apart: 23, of which 14 were waited for; matrix products, arithmetic and copies ran while one was open for 3% of the time, Pallas kernels for 9%

profile of v1, /device:TPU:10, one launch (start us, length us, event | category | flops | bytes accessed | tf_op | source)
XLA Modules:
  0.0 229.4 jit_solution(18050295465364141307)
XLA Ops:
  0.6 0.8 copy.12.offsets
  1.4 3.1 %copy.17 = bf16[1,2,9728,128]{3,2,1,0:T(8,128)(2,1)S(1)} copy(bf16[1,2,9728,128]{3,1,2,0:T(2,128)(2,1)} %bitcast.29) | data formatting | bytes 9961472
  4.6 3.5 %pack.6 = bf16[8,2,4,2,16,128]{5,4,3,2,1,0:T(8,128)(2,1)} custom-call(s32[2,32,4]{2,1,0:T(8,128)S(1)} %copy.12.offsets, s32[2,32]{1,0:T(2,128)S(1)} %copy-done.13, bf16[2,608,16,128]{3,2,1,0:T(8,128)(2,1)S(1)} %bitcast.14), custom_call_target="tpu_custom_call" | custom-call | bytes 1048576 | tf_op jit(solution)/shard_map/pack/pallas_call | solution.py:57
  8.1 2.3 copy-done
  10.4 4.3 %all-to-all-start.1 = ((bf16[8,2,4,2,16,128]{5,4,3,2,1,0:T(8,128)(2,1)}), bf16[8,2,4,2,16,128]{5,4,3,2,1,0:T(8,128)(2,1)S(1)}, u32[]{:S(2)}, u32[]{:S(2)}) async-start(bf16[8,2,4,2,16,128]{5,4,3,2,1,0:T(8,128)(2,1)} %pack.6), calls=%async_computation.1 | async-start | bytes 1048576 | tf_op jit(solution)/shard_map/all_to_all | solution.py:210
  14.6 2.4 %copy-done.1 = bf16[1,2,9728,128]{3,2,1,0:T(8,128)(2,1)S(1)} copy-done((bf16[1,2,9728,128]{3,2,1,0:T(8,128)(2,1)S(1)}, bf16[1,2,9728,128]{3,2,1,0:T(8,128)(2,1)}, u32[]{:S(2)}) %copy-start.1) | copy-done | bytes 4980760
  17.0 2.9 %pack.9 = bf16[8,1,2,17,16,128]{5,4,3,2,1,0:T(8,128)(2,1)} custom-call(s32[2,32,4]{2,1,0:T(8,128)S(1)} %copy.12.offsets, s32[2,32]{1,0:T(2,128)S(1)} %copy-done.13, bf16[2,608,16,128]{3,2,1,0:T(8,128)(2,1)S(1)} %bitcast.15), custom_call_target="tpu_custom_call" | custom-call | bytes 2228224 | tf_op jit(solution)/shard_map/pack/pallas_call | solution.py:57
  19.9 3.0 %all-to-all-done.1.refs_0_ = bf16[8,2,4,2,16,128]{5,4,3,2,1,0:T(8,128)(2,1)S(1)} async-done(((bf16[8,2,4,2,16,128]{5,4,3,2,1,0:T(8,128)(2,1)}), bf16[8,2,4,2,16,128]{5,4,3,2,1,0:T(8,128)(2,1)S(1)}, u32[]{:S(2)}, u32[]{:S(2)}) %all-to-all-start.1) | async-done | bytes 524320 | tf_op jit(solution)/shard_map/all_to_all | solution.py:210
  22.9 0.8 copy-done.11
  23.7 4.9 %all-to-all-start.4 = ((bf16[8,1,2,17,16,128]{5,4,3,2,1,0:T(8,128)(2,1)}), bf16[8,1,2,17,16,128]{5,4,3,2,1,0:T(8,128)(2,1)S(1)}, u32[]{:S(2)}, u32[]{:S(2)}) async-start(bf16[8,1,2,17,16,128]{5,4,3,2,1,0:T(8,128)(2,1)} %pack.9), calls=%async_computation.4 | async-start | bytes 2228224 | tf_op jit(solution)/shard_map/all_to_all | solution.py:210
  28.6 2.4 %copy-done.2 = bf16[1,2,9728,128]{3,2,1,0:T(8,128)(2,1)S(1)} copy-done((bf16[1,2,9728,128]{3,2,1,0:T(8,128)(2,1)S(1)}, bf16[1,2,9728,128]{3,2,1,0:T(8,128)(2,1)}, u32[]{:S(2)}) %copy-start.2) | copy-done | bytes 4980760
  31.0 1.8 pack.8
  32.8 0.0 copy-start.10
  32.9 1.0 copy-done.10
  33.8 9.4 %all-to-all-done.4 = bf16[8,1,2,17,16,128]{5,4,3,2,1,0:T(8,128)(2,1)S(1)} async-done(((bf16[8,1,2,17,16,128]{5,4,3,2,1,0:T(8,128)(2,1)}), bf16[8,1,2,17,16,128]{5,4,3,2,1,0:T(8,128)(2,1)S(1)}, u32[]{:S(2)}, u32[]{:S(2)}) %all-to-all-start.4) | async-done | bytes 1114144 | tf_op jit(solution)/shard_map/all_to_all | solution.py:210
  43.2 5.0 %all-to-all-start.3 = ((bf16[8,1,2,17,16,128]{5,4,3,2,1,0:T(8,128)(2,1)}), bf16[8,1,2,17,16,128]{5,4,3,2,1,0:T(8,128)(2,1)S(1)}, u32[]{:S(2)}, u32[]{:S(2)}) async-start(bf16[8,1,2,17,16,128]{5,4,3,2,1,0:T(8,128)(2,1)} %copy-done.10), calls=%async_computation.3 | async-start | bytes 2228224 | tf_op jit(solution)/shard_map/all_to_all | solution.py:210
  48.2 2.4 %copy-done.3 = bf16[1,2,9728,128]{3,2,1,0:T(8,128)(2,1)S(1)} copy-done((bf16[1,2,9728,128]{3,2,1,0:T(8,128)(2,1)S(1)}, bf16[1,2,9728,128]{3,2,1,0:T(8,128)(2,1)}, u32[]{:S(2)}) %copy-start.3) | copy-done | bytes 4980760
  50.6 1.9 pack.7
  52.5 1.0 copy-done.9
  53.5 9.3 %all-to-all-done.3 = bf16[8,1,2,17,16,128]{5,4,3,2,1,0:T(8,128)(2,1)S(1)} async-done(((bf16[8,1,2,17,16,128]{5,4,3,2,1,0:T(8,128)(2,1)}), bf16[8,1,2,17,16,128]{5,4,3,2,1,0:T(8,128)(2,1)S(1)}, u32[]{:S(2)}, u32[]{:S(2)}) %all-to-all-start.3) | async-done | bytes 1114144 | tf_op jit(solution)/shard_map/all_to_all | solution.py:210
  62.9 1.0 copy-done.5
  63.9 5.0 %all-to-all-start.2 = ((bf16[8,1,2,17,16,128]{5,4,3,2,1,0:T(8,128)(2,1)}), bf16[8,1,2,17,16,128]{5,4,3,2,1,0:T(8,128)(2,1)S(1)}, u32[]{:S(2)}, u32[]{:S(2)}) async-start(bf16[8,1,2,17,16,128]{5,4,3,2,1,0:T(8,128)(2,1)} %copy-done.9), calls=%async_computation.2 | async-start | bytes 2228224 | tf_op jit(solution)/shard_map/all_to_all | solution.py:210
  68.9 2.3 %collective-permute-start.4 = (bf16[8,2,4,2,16,128]{5,4,3,2,1,0:T(8,128)(2,1)}, bf16[8,2,4,2,16,128]{5,4,3,2,1,0:T(8,128)(2,1)}, u32[]{:S(2)}, u32[]{:S(2)}) collective-permute-start(bf16[8,2,4,2,16,128]{5,4,3,2,1,0:T(8,128)(2,1)} %copy-done.11), channel_id=1, source_target_pairs={{1,0},{2,1},{3,2},{5,4},{6,5},{7,6},{9,8},{10,9},{11,10},{13,12},{... | collective-permute-start | bytes 1572872 | tf_op jit(solution)/shard_map/ppermute | solution.py:79
  71.3 2.4 %copy-done.4 = bf16[1,2,9728,128]{3,2,1,0:T(8,128)(2,1)S(1)} copy-done((bf16[1,2,9728,128]{3,2,1,0:T(8,128)(2,1)S(1)}, bf16[1,2,9728,128]{3,2,1,0:T(8,128)(2,1)}, u32[]{:S(2)}) %copy-start.4) | copy-done | bytes 4980760
  73.7 1.9 pack.5
  75.6 1.0 copy-done.8
  76.5 7.0 %all-to-all-done.2 = bf16[8,1,2,17,16,128]{5,4,3,2,1,0:T(8,128)(2,1)S(1)} async-done(((bf16[8,1,2,17,16,128]{5,4,3,2,1,0:T(8,128)(2,1)}), bf16[8,1,2,17,16,128]{5,4,3,2,1,0:T(8,128)(2,1)S(1)}, u32[]{:S(2)}, u32[]{:S(2)}) %all-to-all-start.2) | async-done | bytes 1114144 | tf_op jit(solution)/shard_map/all_to_all | solution.py:210
  83.5 5.0 %all-to-all-start = ((bf16[8,1,2,17,16,128]{5,4,3,2,1,0:T(8,128)(2,1)}), bf16[8,1,2,17,16,128]{5,4,3,2,1,0:T(8,128)(2,1)S(1)}, u32[]{:S(2)}, u32[]{:S(2)}) async-start(bf16[8,1,2,17,16,128]{5,4,3,2,1,0:T(8,128)(2,1)} %copy-done.8), calls=%async_computation | async-start | bytes 2228224 | tf_op jit(solution)/shard_map/all_to_all | solution.py:210
  88.5 3.5 %collective-permute-start.3 = (bf16[8,2,4,2,16,128]{5,4,3,2,1,0:T(8,128)(2,1)}, bf16[8,2,4,2,16,128]{5,4,3,2,1,0:T(8,128)(2,1)}, u32[]{:S(2)}, u32[]{:S(2)}) collective-permute-start(bf16[8,2,4,2,16,128]{5,4,3,2,1,0:T(8,128)(2,1)} %copy-done.11), channel_id=1, source_target_pairs={{0,1},{1,2},{2,3},{4,5},{5,6},{6,7},{8,9},{9,10},{10,11},{12,13},{... | collective-permute-start | bytes 1572872 | tf_op jit(solution)/shard_map/ppermute | solution.py:78
  92.0 3.1 %collective-permute-start.5 = (bf16[8,2,4,2,16,128]{5,4,3,2,1,0:T(8,128)(2,1)}, bf16[8,2,4,2,16,128]{5,4,3,2,1,0:T(8,128)(2,1)}, u32[]{:S(2)}, u32[]{:S(2)}) collective-permute-start(bf16[8,2,4,2,16,128]{5,4,3,2,1,0:T(8,128)(2,1)} %collective-permute-done.4), channel_id=1, source_target_pairs={{1,0},{2,1},{3,2},{5,4},{6,5},{7,6},{9,8},{10,9},{11,10},{13,12},{... | collective-permute-start | bytes 1572872 | tf_op jit(solution)/shard_map/ppermute | solution.py:79
  95.2 0.6 fusion
  97.7 0.7 pad_add_fusion.at
  98.4 6.2 %collective-permute-done.3 = bf16[8,2,4,2,16,128]{5,4,3,2,1,0:T(8,128)(2,1)} collective-permute-done((bf16[8,2,4,2,16,128]{5,4,3,2,1,0:T(8,128)(2,1)}, bf16[8,2,4,2,16,128]{5,4,3,2,1,0:T(8,128)(2,1)}, u32[]{:S(2)}, u32[]{:S(2)}) %collective-permute-start.3) | collective-permute-done | bytes 524320 | tf_op jit(solution)/shard_map/ppermute | solution.py:78
  104.7 3.5 %collective-permute-start.7 = (bf16[8,2,4,2,16,128]{5,4,3,2,1,0:T(8,128)(2,1)}, bf16[8,2,4,2,16,128]{5,4,3,2,1,0:T(8,128)(2,1)}, u32[]{:S(2)}, u32[]{:S(2)}) collective-permute-start(bf16[8,2,4,2,16,128]{5,4,3,2,1,0:T(8,128)(2,1)} %collective-permute-done.3), channel_id=1, source_target_pairs={{0,1},{1,2},{2,3},{4,5},{5,6},{6,7},{8,9},{9,10},{10,11},{12,13},{... | collective-permute-start | bytes 1572872 | tf_op jit(solution)/shard_map/ppermute | solution.py:78
  108.2 3.1 %collective-permute-start.6 = (bf16[8,2,4,2,16,128]{5,4,3,2,1,0:T(8,128)(2,1)}, bf16[8,2,4,2,16,128]{5,4,3,2,1,0:T(8,128)(2,1)}, u32[]{:S(2)}, u32[]{:S(2)}) collective-permute-start(bf16[8,2,4,2,16,128]{5,4,3,2,1,0:T(8,128)(2,1)} %collective-permute-done.5), channel_id=1, source_target_pairs={{1,0},{2,1},{3,2},{5,4},{6,5},{7,6},{9,8},{10,9},{11,10},{13,12},{... | collective-permute-start | bytes 1572872 | tf_op jit(solution)/shard_map/ppermute | solution.py:79
  111.3 1.0 constant_dynamic-slice_fusion
  112.3 2.6 %collective-permute-start.16 = (bf16[2,2,272,128]{3,2,1,0:T(8,128)(2,1)}, bf16[2,2,272,128]{3,2,1,0:T(8,128)(2,1)}, u32[]{:S(2)}, u32[]{:S(2)}) collective-permute-start(bf16[2,2,272,128]{3,2,1,0:T(8,128)(2,1)} %get-tuple-element.19), channel_id=1, source_target_pairs={{0,2},{1,3},{2,0},{3,1},{4,6},{5,7},{6,4},{7,5},{8,10},{9,11},{10,... | collective-permute-start | bytes 835592 | tf_op jit(solution)/shard_map/ppermute | solution.py:228
  114.9 2.9 %collective-permute-start.15 = (bf16[2,2,272,128]{3,2,1,0:T(8,128)(2,1)}, bf16[2,2,272,128]{3,2,1,0:T(8,128)(2,1)}, u32[]{:S(2)}, u32[]{:S(2)}) collective-permute-start(bf16[2,2,272,128]{3,2,1,0:T(8,128)(2,1)} %get-tuple-element.20), channel_id=1, source_target_pairs={{0,1},{1,2},{2,3},{3,0},{4,5},{5,6},{6,7},{7,4},{8,9},{9,10},{10,1... | collective-permute-start | bytes 835592 | tf_op jit(solution)/shard_map/ppermute | solution.py:228
  117.8 0.9 constant_dynamic-slice_fusion.3
  118.8 0.9 constant_dynamic-slice_fusion.6
  119.7 0.1 constant_dynamic-slice_fusion.9
  119.8 22.3 %collective-permute-done.17.refs_3_ = bf16[2,2,272,128]{3,2,1,0:T(8,128)(2,1)} collective-permute-done((bf16[2,2,272,128]{3,2,1,0:T(8,128)(2,1)}, bf16[2,2,272,128]{3,2,1,0:T(8,128)(2,1)}, u32[]{:S(2)}, u32[]{:S(2)}) %collective-permute-start.17) | collective-permute-done | bytes 278560 | tf_op jit(solution)/shard_map/ppermute | solution.py:228
  142.1 2.7 %collective-permute-done.16.refs_2_ = bf16[2,2,272,128]{3,2,1,0:T(8,128)(2,1)} collective-permute-done((bf16[2,2,272,128]{3,2,1,0:T(8,128)(2,1)}, bf16[2,2,272,128]{3,2,1,0:T(8,128)(2,1)}, u32[]{:S(2)}, u32[]{:S(2)}) %collective-permute-start.16) | collective-permute-done | bytes 278560 | tf_op jit(solution)/shard_map/ppermute | solution.py:228
  144.8 3.4 %collective-permute-start.13 = (bf16[2,2,272,128]{3,2,1,0:T(8,128)(2,1)S(1)}, bf16[2,2,272,128]{3,2,1,0:T(8,128)(2,1)S(1)}, u32[]{:S(2)}, u32[]{:S(2)}) collective-permute-start(bf16[2,2,272,128]{3,2,1,0:T(8,128)(2,1)S(1)} %copy-done.18), channel_id=1, source_target_pairs={{0,2},{1,3},{2,0},{3,1},{4,6},{5,7},{6,4},{7,5},{8,10},{9,11},{10,... | collective-permute-start | bytes 835592 | tf_op jit(solution)/shard_map/ppermute | solution.py:228
  148.1 5.6 %collective-permute-done.15.refs_1_ = bf16[2,2,272,128]{3,2,1,0:T(8,128)(2,1)} collective-permute-done((bf16[2,2,272,128]{3,2,1,0:T(8,128)(2,1)}, bf16[2,2,272,128]{3,2,1,0:T(8,128)(2,1)}, u32[]{:S(2)}, u32[]{:S(2)}) %collective-permute-start.15) | collective-permute-done | bytes 278560 | tf_op jit(solution)/shard_map/ppermute | solution.py:228
  153.7 7.3 %collective-permute-start.12 = (bf16[2,2,272,128]{3,2,1,0:T(8,128)(2,1)S(1)}, bf16[2,2,272,128]{3,2,1,0:T(8,128)(2,1)S(1)}, u32[]{:S(2)}, u32[]{:S(2)}) collective-permute-start(bf16[2,2,272,128]{3,2,1,0:T(8,128)(2,1)S(1)} %copy-done.17), channel_id=1, source_target_pairs={{0,1},{1,2},{2,3},{3,0},{4,5},{5,6},{6,7},{7,4},{8,9},{9,10},{10,1... | collective-permute-start | bytes 835592 | tf_op jit(solution)/shard_map/ppermute | solution.py:228
  161.0 3.9 %collective-permute-start.8 = (bf16[8,2,4,2,16,128]{5,4,3,2,1,0:T(8,128)(2,1)}, bf16[8,2,4,2,16,128]{5,4,3,2,1,0:T(8,128)(2,1)S(1)}, u32[]{:S(2)}, u32[]{:S(2)}) collective-permute-start(bf16[8,2,4,2,16,128]{5,4,3,2,1,0:T(8,128)(2,1)} %collective-permute-done.7), channel_id=1, source_target_pairs={{0,1},{1,2},{2,3},{4,5},{5,6},{6,7},{8,9},{9,10},{10,11},{12,13},{... | collective-permute-start | bytes 1572872 | tf_op jit(solution)/shard_map/ppermute | solution.py:78
  165.0 1.1 broadcast_select_fusion.1.refs_2_
  166.1 1.2 broadcast_select_fusion.2.refs_1_
  167.3 2.6 %collective-permute-done.14.refs_3_ = bf16[2,2,272,128]{3,2,1,0:T(8,128)(2,1)S(1)} collective-permute-done((bf16[2,2,272,128]{3,2,1,0:T(8,128)(2,1)S(1)}, bf16[2,2,272,128]{3,2,1,0:T(8,128)(2,1)S(1)}, u32[]{:S(2)}, u32[]{:S(2)}) %collective-permute-start.14) | collective-permute-done | bytes 278560 | tf_op jit(solution)/shard_map/ppermute | solution.py:228
  169.9 11.5 %collective-permute-start.9 = (bf16[2,2,272,128]{3,2,1,0:T(8,128)(2,1)S(1)}, bf16[2,2,272,128]{3,2,1,0:T(8,128)(2,1)S(1)}, u32[]{:S(2)}, u32[]{:S(2)}) collective-permute-start(bf16[2,2,272,128]{3,2,1,0:T(8,128)(2,1)S(1)} %copy-done.14), channel_id=1, source_target_pairs={{0,1},{1,2},{2,3},{3,0},{4,5},{5,6},{6,7},{7,4},{8,9},{9,10},{10,1... | collective-permute-start | bytes 835592 | tf_op jit(solution)/shard_map/ppermute | solution.py:228
  181.4 2.0 collective-permute-start.2
  183.4 10.7 %collective-permute-done.11.refs_3_ = bf16[2,2,272,128]{3,2,1,0:T(8,128)(2,1)S(1)} collective-permute-done((bf16[2,2,272,128]{3,2,1,0:T(8,128)(2,1)S(1)}, bf16[2,2,272,128]{3,2,1,0:T(8,128)(2,1)S(1)}, u32[]{:S(2)}, u32[]{:S(2)}) %collective-permute-start.11) | collective-permute-done | bytes 278560 | tf_op jit(solution)/shard_map/ppermute | solution.py:228
  194.2 5.0 %collective-permute-done.8 = bf16[8,2,4,2,16,128]{5,4,3,2,1,0:T(8,128)(2,1)S(1)} collective-permute-done((bf16[8,2,4,2,16,128]{5,4,3,2,1,0:T(8,128)(2,1)}, bf16[8,2,4,2,16,128]{5,4,3,2,1,0:T(8,128)(2,1)S(1)}, u32[]{:S(2)}, u32[]{:S(2)}) %collective-permute-start.8) | collective-permute-done | bytes 524320 | tf_op jit(solution)/shard_map/ppermute | solution.py:78
  199.1 2.9 %collective-permute-start = (bf16[2,2,272,128]{3,2,1,0:T(8,128)(2,1)S(1)}, bf16[2,2,272,128]{3,2,1,0:T(8,128)(2,1)S(1)}, u32[]{:S(2)}, u32[]{:S(2)}) collective-permute-start(bf16[2,2,272,128]{3,2,1,0:T(8,128)(2,1)S(1)} %get-tuple-element.29), channel_id=1, source_target_pairs={{0,1},{1,2},{2,3},{3,0},{4,5},{5,6},{6,7},{7,4},{8,9},{9,10},{10,1... | collective-permute-start | bytes 835592 | tf_op jit(solution)/shard_map/ppermute | solution.py:228
  202.0 1.1 broadcast_select_fusion.refs_3_
  203.1 1.2 assemble.1.refs_4_
  204.3 4.5 %absorb.4 = (bf16[2,4,2,4,48,512]{5,4,3,2,1,0:T(8,128)(2,1)}, bf16[2,4,2,4,224,512]{5,4,3,2,1,0:T(8,128)(2,1)}) custom-call(s32[2]{0:T(128)S(1)} %pad_add_fusion.at, bf16[8,2,272,128]{3,2,1,0:T(8,128)(2,1)S(1)} %bitcast.20, bf16[2,2,272,128]{3,2,1,0:T(8,128)(2,1)} %collective-permute-done.15.refs_1_, ...), custom_call_target="tpu_custom_call" | custom-call | flops 570425344 | bytes 5570560 | tf_op jit(solution)/shard_map/absorb/pallas_call | solution.py:152
  208.8 3.5 %absorb.5 = (bf16[2,4,2,4,48,512]{5,4,3,2,1,0:T(8,128)(2,1)}, bf16[2,4,2,4,224,512]{5,4,3,2,1,0:T(8,128)(2,1)}) custom-call(s32[2]{0:T(128)S(1)} %pad_add_fusion.at, bf16[8,2,272,128]{3,2,1,0:T(8,128)(2,1)S(1)} %bitcast.26, bf16[2,2,272,128]{3,2,1,0:T(8,128)(2,1)S(1)} %collective-permute-done.12.refs_1_, ...), custom_call_target="tpu_custom_call", output_to_operand_aliasing={{0}: (6, {}), {1}: (7, {})} | custom-call | flops 570425344 | bytes 5570560 | tf_op jit(solution)/shard_map/absorb/pallas_call | solution.py:152
  212.3 3.3 %collective-permute-done.9.refs_1_ = bf16[2,2,272,128]{3,2,1,0:T(8,128)(2,1)S(1)} collective-permute-done((bf16[2,2,272,128]{3,2,1,0:T(8,128)(2,1)S(1)}, bf16[2,2,272,128]{3,2,1,0:T(8,128)(2,1)S(1)}, u32[]{:S(2)}, u32[]{:S(2)}) %collective-permute-start.9) | collective-permute-done | bytes 278560 | tf_op jit(solution)/shard_map/ppermute | solution.py:228
  215.7 3.5 %absorb.6 = (bf16[2,4,2,4,48,512]{5,4,3,2,1,0:T(8,128)(2,1)}, bf16[2,4,2,4,224,512]{5,4,3,2,1,0:T(8,128)(2,1)}) custom-call(s32[2]{0:T(128)S(1)} %pad_add_fusion.at, bf16[8,2,272,128]{3,2,1,0:T(8,128)(2,1)S(1)} %bitcast.24, bf16[2,2,272,128]{3,2,1,0:T(8,128)(2,1)S(1)} %collective-permute-done.9.refs_1_, ...), custom_call_target="tpu_custom_call", output_to_operand_aliasing={{0}: (6, {}), {1}: (7, {})} | custom-call | flops 570425344 | bytes 5570560 | tf_op jit(solution)/shard_map/absorb/pallas_call | solution.py:152
  219.2 2.4 %collective-permute-done.1.refs_2_ = bf16[2,2,272,128]{3,2,1,0:T(8,128)(2,1)S(1)} collective-permute-done((bf16[2,2,272,128]{3,2,1,0:T(8,128)(2,1)S(1)}, bf16[2,2,272,128]{3,2,1,0:T(8,128)(2,1)S(1)}, u32[]{:S(2)}, u32[]{:S(2)}) %collective-permute-start.1) | collective-permute-done | bytes 278560 | tf_op jit(solution)/shard_map/ppermute | solution.py:228
  221.6 4.3 %collective-permute-done.refs_1_ = bf16[2,2,272,128]{3,2,1,0:T(8,128)(2,1)S(1)} collective-permute-done((bf16[2,2,272,128]{3,2,1,0:T(8,128)(2,1)S(1)}, bf16[2,2,272,128]{3,2,1,0:T(8,128)(2,1)S(1)}, u32[]{:S(2)}, u32[]{:S(2)}) %collective-permute-start) | collective-permute-done | bytes 278560 | tf_op jit(solution)/shard_map/ppermute | solution.py:228
  225.9 3.5 %absorb.7 = (bf16[2,4,2,4,48,512]{5,4,3,2,1,0:T(8,128)(2,1)}, bf16[2,4,2,4,224,512]{5,4,3,2,1,0:T(8,128)(2,1)}) custom-call(s32[2]{0:T(128)S(1)} %pad_add_fusion.at, bf16[8,2,272,128]{3,2,1,0:T(8,128)(2,1)S(1)} %bitcast.22, bf16[2,2,272,128]{3,2,1,0:T(8,128)(2,1)S(1)} %collective-permute-done.refs_1_, ...), custom_call_target="tpu_custom_call", output_to_operand_aliasing={{0}: (6, {}), {1}: (7, {})} | custom-call | flops 570425344 | bytes 5570560 | tf_op jit(solution)/shard_map/absorb/pallas_call | solution.py:152
  (45 shorter events, 0.1 us)
Async XLA Ops:
  1.4 3.1 %copy-start.13 = (s32[2,32]{1,0:T(2,128)S(1)}, s32[2,32]{1,0:T(2,128)}, u32[]{:S(2)}) copy-start(s32[2,32]{1,0:T(2,128)} %owners.9) | copy-start | bytes 772
  8.1 2.3 copy-start
  10.4 12.5 %all-to-all-start.1 = ((bf16[8,2,4,2,16,128]{5,4,3,2,1,0:T(8,128)(2,1)}), bf16[8,2,4,2,16,128]{5,4,3,2,1,0:T(8,128)(2,1)S(1)}, u32[]{:S(2)}, u32[]{:S(2)}) async-start(bf16[8,2,4,2,16,128]{5,4,3,2,1,0:T(8,128)(2,1)} %pack.6), calls=%async_computation.1 | async-start | bytes 1048576 | tf_op jit(solution)/shard_map/all_to_all | solution.py:210
  14.6 2.4 %copy-start.1 = (bf16[1,2,9728,128]{3,2,1,0:T(8,128)(2,1)S(1)}, bf16[1,2,9728,128]{3,2,1,0:T(8,128)(2,1)}, u32[]{:S(2)}) copy-start(bf16[1,2,9728,128]{3,2,1,0:T(8,128)(2,1)} %copy-done) | copy-start | bytes 14942212
  22.9 0.8 copy-start.11
  23.7 19.6 %all-to-all-start.4 = ((bf16[8,1,2,17,16,128]{5,4,3,2,1,0:T(8,128)(2,1)}), bf16[8,1,2,17,16,128]{5,4,3,2,1,0:T(8,128)(2,1)S(1)}, u32[]{:S(2)}, u32[]{:S(2)}) async-start(bf16[8,1,2,17,16,128]{5,4,3,2,1,0:T(8,128)(2,1)} %pack.9), calls=%async_computation.4 | async-start | bytes 2228224 | tf_op jit(solution)/shard_map/all_to_all | solution.py:210
  28.6 2.4 %copy-start.2 = (bf16[1,2,9728,128]{3,2,1,0:T(8,128)(2,1)S(1)}, bf16[1,2,9728,128]{3,2,1,0:T(8,128)(2,1)}, u32[]{:S(2)}) copy-start(bf16[1,2,9728,128]{3,2,1,0:T(8,128)(2,1)} %copy-done) | copy-start | bytes 14942212
  32.8 1.0 copy-start.10
  43.2 19.6 %all-to-all-start.3 = ((bf16[8,1,2,17,16,128]{5,4,3,2,1,0:T(8,128)(2,1)}), bf16[8,1,2,17,16,128]{5,4,3,2,1,0:T(8,128)(2,1)S(1)}, u32[]{:S(2)}, u32[]{:S(2)}) async-start(bf16[8,1,2,17,16,128]{5,4,3,2,1,0:T(8,128)(2,1)} %copy-done.10), calls=%async_computation.3 | async-start | bytes 2228224 | tf_op jit(solution)/shard_map/all_to_all | solution.py:210
  48.2 2.4 %copy-start.3 = (bf16[1,2,9728,128]{3,2,1,0:T(8,128)(2,1)S(1)}, bf16[1,2,9728,128]{3,2,1,0:T(8,128)(2,1)}, u32[]{:S(2)}) copy-start(bf16[1,2,9728,128]{3,2,1,0:T(8,128)(2,1)} %copy-done) | copy-start | bytes 14942212
  52.5 1.0 copy-start.9
  62.9 1.0 copy-start.5
  63.9 19.6 %all-to-all-start.2 = ((bf16[8,1,2,17,16,128]{5,4,3,2,1,0:T(8,128)(2,1)}), bf16[8,1,2,17,16,128]{5,4,3,2,1,0:T(8,128)(2,1)S(1)}, u32[]{:S(2)}, u32[]{:S(2)}) async-start(bf16[8,1,2,17,16,128]{5,4,3,2,1,0:T(8,128)(2,1)} %copy-done.9), calls=%async_computation.2 | async-start | bytes 2228224 | tf_op jit(solution)/shard_map/all_to_all | solution.py:210
  68.9 23.1 %collective-permute-start.4 = (bf16[8,2,4,2,16,128]{5,4,3,2,1,0:T(8,128)(2,1)}, bf16[8,2,4,2,16,128]{5,4,3,2,1,0:T(8,128)(2,1)}, u32[]{:S(2)}, u32[]{:S(2)}) collective-permute-start(bf16[8,2,4,2,16,128]{5,4,3,2,1,0:T(8,128)(2,1)} %copy-done.11), channel_id=1, source_target_pairs={{1,0},{2,1},{3,2},{5,4},{6,5},{7,6},{9,8},{10,9},{11,10},{13,12},{... | collective-permute-start | bytes 1572872 | tf_op jit(solution)/shard_map/ppermute | solution.py:79
  71.2 2.4 %copy-start.4 = (bf16[1,2,9728,128]{3,2,1,0:T(8,128)(2,1)S(1)}, bf16[1,2,9728,128]{3,2,1,0:T(8,128)(2,1)}, u32[]{:S(2)}) copy-start(bf16[1,2,9728,128]{3,2,1,0:T(8,128)(2,1)} %copy-done) | copy-start | bytes 14942212
  75.5 1.0 copy-start.8
  76.5 18.6 %copy-start.20 = (s32[8,4]{0,1:T(4,128)S(1)}, s32[8,4]{0,1:T(4,128)}, u32[]{:S(2)}) copy-start(s32[8,4]{0,1:T(4,128)} %param.7) | copy-start | bytes 388
  83.5 36.2 %all-to-all-start = ((bf16[8,1,2,17,16,128]{5,4,3,2,1,0:T(8,128)(2,1)}), bf16[8,1,2,17,16,128]{5,4,3,2,1,0:T(8,128)(2,1)S(1)}, u32[]{:S(2)}, u32[]{:S(2)}) async-start(bf16[8,1,2,17,16,128]{5,4,3,2,1,0:T(8,128)(2,1)} %copy-done.8), calls=%async_computation | async-start | bytes 2228224 | tf_op jit(solution)/shard_map/all_to_all | solution.py:210
  88.5 16.2 %collective-permute-start.3 = (bf16[8,2,4,2,16,128]{5,4,3,2,1,0:T(8,128)(2,1)}, bf16[8,2,4,2,16,128]{5,4,3,2,1,0:T(8,128)(2,1)}, u32[]{:S(2)}, u32[]{:S(2)}) collective-permute-start(bf16[8,2,4,2,16,128]{5,4,3,2,1,0:T(8,128)(2,1)} %copy-done.11), channel_id=1, source_target_pairs={{0,1},{1,2},{2,3},{4,5},{5,6},{6,7},{8,9},{9,10},{10,11},{12,13},{... | collective-permute-start | bytes 1572872 | tf_op jit(solution)/shard_map/ppermute | solution.py:78
  92.0 16.2 %collective-permute-start.5 = (bf16[8,2,4,2,16,128]{5,4,3,2,1,0:T(8,128)(2,1)}, bf16[8,2,4,2,16,128]{5,4,3,2,1,0:T(8,128)(2,1)}, u32[]{:S(2)}, u32[]{:S(2)}) collective-permute-start(bf16[8,2,4,2,16,128]{5,4,3,2,1,0:T(8,128)(2,1)} %collective-permute-done.4), channel_id=1, source_target_pairs={{1,0},{2,1},{3,2},{5,4},{6,5},{7,6},{9,8},{10,9},{11,10},{13,12},{... | collective-permute-start | bytes 1572872 | tf_op jit(solution)/shard_map/ppermute | solution.py:79
  97.7 20.1 %copy-start.6 = (bf16[8,1,2,17,16,128]{5,4,3,2,1,0:T(8,128)(2,1)S(1)}, bf16[8,1,2,17,16,128]{5,4,3,2,1,0:T(8,128)(2,1)}, u32[]{:S(2)}) copy-start(bf16[8,1,2,17,16,128]{5,4,3,2,1,0:T(8,128)(2,1)} %copy-done.5) | copy-start | bytes 3342340
  104.7 56.3 %collective-permute-start.7 = (bf16[8,2,4,2,16,128]{5,4,3,2,1,0:T(8,128)(2,1)}, bf16[8,2,4,2,16,128]{5,4,3,2,1,0:T(8,128)(2,1)}, u32[]{:S(2)}, u32[]{:S(2)}) collective-permute-start(bf16[8,2,4,2,16,128]{5,4,3,2,1,0:T(8,128)(2,1)} %collective-permute-done.3), channel_id=1, source_target_pairs={{0,1},{1,2},{2,3},{4,5},{5,6},{6,7},{8,9},{9,10},{10,11},{12,13},{... | collective-permute-start | bytes 1572872 | tf_op jit(solution)/shard_map/ppermute | solution.py:78
  108.2 52.8 %collective-permute-start.6 = (bf16[8,2,4,2,16,128]{5,4,3,2,1,0:T(8,128)(2,1)}, bf16[8,2,4,2,16,128]{5,4,3,2,1,0:T(8,128)(2,1)}, u32[]{:S(2)}, u32[]{:S(2)}) collective-permute-start(bf16[8,2,4,2,16,128]{5,4,3,2,1,0:T(8,128)(2,1)} %collective-permute-done.5), channel_id=1, source_target_pairs={{1,0},{2,1},{3,2},{5,4},{6,5},{7,6},{9,8},{10,9},{11,10},{13,12},{... | collective-permute-start | bytes 1572872 | tf_op jit(solution)/shard_map/ppermute | solution.py:79
  112.3 29.8 %collective-permute-start.17 = (bf16[2,2,272,128]{3,2,1,0:T(8,128)(2,1)}, bf16[2,2,272,128]{3,2,1,0:T(8,128)(2,1)}, u32[]{:S(2)}, u32[]{:S(2)}) collective-permute-start(bf16[2,2,272,128]{3,2,1,0:T(8,128)(2,1)} %get-tuple-element.18), channel_id=1, source_target_pairs={{0,3},{1,0},{2,1},{3,2},{4,7},{5,4},{6,5},{7,6},{8,11},{9,8},{10,9... | collective-permute-start | bytes 835592 | tf_op jit(solution)/shard_map/ppermute | solution.py:228
  112.3 32.5 %collective-permute-start.16 = (bf16[2,2,272,128]{3,2,1,0:T(8,128)(2,1)}, bf16[2,2,272,128]{3,2,1,0:T(8,128)(2,1)}, u32[]{:S(2)}, u32[]{:S(2)}) collective-permute-start(bf16[2,2,272,128]{3,2,1,0:T(8,128)(2,1)} %get-tuple-element.19), channel_id=1, source_target_pairs={{0,2},{1,3},{2,0},{3,1},{4,6},{5,7},{6,4},{7,5},{8,10},{9,11},{10,... | collective-permute-start | bytes 835592 | tf_op jit(solution)/shard_map/ppermute | solution.py:228
  114.9 38.8 %collective-permute-start.15 = (bf16[2,2,272,128]{3,2,1,0:T(8,128)(2,1)}, bf16[2,2,272,128]{3,2,1,0:T(8,128)(2,1)}, u32[]{:S(2)}, u32[]{:S(2)}) collective-permute-start(bf16[2,2,272,128]{3,2,1,0:T(8,128)(2,1)} %get-tuple-element.20), channel_id=1, source_target_pairs={{0,1},{1,2},{2,3},{3,0},{4,5},{5,6},{6,7},{7,4},{8,9},{9,10},{10,1... | collective-permute-start | bytes 835592 | tf_op jit(solution)/shard_map/ppermute | solution.py:228
  119.7 22.4 %copy-start.19 = (bf16[2,2,272,128]{3,2,1,0:T(8,128)(2,1)S(1)}, bf16[2,2,272,128]{3,2,1,0:T(8,128)(2,1)}, u32[]{:S(2)}) copy-start(bf16[2,2,272,128]{3,2,1,0:T(8,128)(2,1)} %get-tuple-element.21) | copy-start | bytes 835588
  119.7 25.1 %copy-start.18 = (bf16[2,2,272,128]{3,2,1,0:T(8,128)(2,1)S(1)}, bf16[2,2,272,128]{3,2,1,0:T(8,128)(2,1)}, u32[]{:S(2)}) copy-start(bf16[2,2,272,128]{3,2,1,0:T(8,128)(2,1)} %get-tuple-element.22) | copy-start | bytes 835588
  119.7 34.0 %copy-start.17 = (bf16[2,2,272,128]{3,2,1,0:T(8,128)(2,1)S(1)}, bf16[2,2,272,128]{3,2,1,0:T(8,128)(2,1)}, u32[]{:S(2)}) copy-start(bf16[2,2,272,128]{3,2,1,0:T(8,128)(2,1)} %get-tuple-element.23) | copy-start | bytes 835588
  119.7 41.3 %copy-start.16 = (bf16[2,2,272,128]{3,2,1,0:T(8,128)(2,1)S(1)}, bf16[2,2,272,128]{3,2,1,0:T(8,128)(2,1)}, u32[]{:S(2)}) copy-start(bf16[2,2,272,128]{3,2,1,0:T(8,128)(2,1)} %get-tuple-element.24) | copy-start | bytes 835588
  142.1 27.8 %collective-permute-start.14 = (bf16[2,2,272,128]{3,2,1,0:T(8,128)(2,1)S(1)}, bf16[2,2,272,128]{3,2,1,0:T(8,128)(2,1)S(1)}, u32[]{:S(2)}, u32[]{:S(2)}) collective-permute-start(bf16[2,2,272,128]{3,2,1,0:T(8,128)(2,1)S(1)} %copy-done.19), channel_id=1, source_target_pairs={{0,3},{1,0},{2,1},{3,2},{4,7},{5,4},{6,5},{7,6},{8,11},{9,8},{10,9... | collective-permute-start | bytes 835592 | tf_op jit(solution)/shard_map/ppermute | solution.py:228
  144.8 25.2 %collective-permute-start.13 = (bf16[2,2,272,128]{3,2,1,0:T(8,128)(2,1)S(1)}, bf16[2,2,272,128]{3,2,1,0:T(8,128)(2,1)S(1)}, u32[]{:S(2)}, u32[]{:S(2)}) collective-permute-start(bf16[2,2,272,128]{3,2,1,0:T(8,128)(2,1)S(1)} %copy-done.18), channel_id=1, source_target_pairs={{0,2},{1,3},{2,0},{3,1},{4,6},{5,7},{6,4},{7,5},{8,10},{9,11},{10,... | collective-permute-start | bytes 835592 | tf_op jit(solution)/shard_map/ppermute | solution.py:228
  153.7 27.7 %collective-permute-start.12 = (bf16[2,2,272,128]{3,2,1,0:T(8,128)(2,1)S(1)}, bf16[2,2,272,128]{3,2,1,0:T(8,128)(2,1)S(1)}, u32[]{:S(2)}, u32[]{:S(2)}) collective-permute-start(bf16[2,2,272,128]{3,2,1,0:T(8,128)(2,1)S(1)} %copy-done.17), channel_id=1, source_target_pairs={{0,1},{1,2},{2,3},{3,0},{4,5},{5,6},{6,7},{7,4},{8,9},{9,10},{10,1... | collective-permute-start | bytes 835592 | tf_op jit(solution)/shard_map/ppermute | solution.py:228
  161.0 33.1 %collective-permute-start.11 = (bf16[2,2,272,128]{3,2,1,0:T(8,128)(2,1)S(1)}, bf16[2,2,272,128]{3,2,1,0:T(8,128)(2,1)S(1)}, u32[]{:S(2)}, u32[]{:S(2)}) collective-permute-start(bf16[2,2,272,128]{3,2,1,0:T(8,128)(2,1)S(1)} %copy-done.16), channel_id=1, source_target_pairs={{0,3},{1,0},{2,1},{3,2},{4,7},{5,4},{6,5},{7,6},{8,11},{9,8},{10,9... | collective-permute-start | bytes 835592 | tf_op jit(solution)/shard_map/ppermute | solution.py:228
  161.0 38.1 %collective-permute-start.8 = (bf16[8,2,4,2,16,128]{5,4,3,2,1,0:T(8,128)(2,1)}, bf16[8,2,4,2,16,128]{5,4,3,2,1,0:T(8,128)(2,1)S(1)}, u32[]{:S(2)}, u32[]{:S(2)}) collective-permute-start(bf16[8,2,4,2,16,128]{5,4,3,2,1,0:T(8,128)(2,1)} %collective-permute-done.7), channel_id=1, source_target_pairs={{0,1},{1,2},{2,3},{4,5},{5,6},{6,7},{8,9},{9,10},{10,11},{12,13},{... | collective-permute-start | bytes 1572872 | tf_op jit(solution)/shard_map/ppermute | solution.py:78
  166.1 3.8 %copy-start.15 = (bf16[2,2,272,128]{3,2,1,0:T(8,128)(2,1)S(1)}, bf16[2,2,272,128]{3,2,1,0:T(8,128)(2,1)}, u32[]{:S(2)}) copy-start(bf16[2,2,272,128]{3,2,1,0:T(8,128)(2,1)} %get-tuple-element.25) | copy-start | bytes 835588
  166.1 3.8 %copy-start.14 = (bf16[2,2,272,128]{3,2,1,0:T(8,128)(2,1)S(1)}, bf16[2,2,272,128]{3,2,1,0:T(8,128)(2,1)}, u32[]{:S(2)}) copy-start(bf16[2,2,272,128]{3,2,1,0:T(8,128)(2,1)} %get-tuple-element.26) | copy-start | bytes 835588
  167.3 35.8 %copy-start.12 = (bf16[8,2,4,2,16,128]{5,4,3,2,1,0:T(8,128)(2,1)S(1)}, bf16[8,2,4,2,16,128]{5,4,3,2,1,0:T(8,128)(2,1)}, u32[]{:S(2)}) copy-start(bf16[8,2,4,2,16,128]{5,4,3,2,1,0:T(8,128)(2,1)} %copy-done.11) | copy-start | bytes 1572868
  169.9 42.4 %collective-permute-start.10 = (bf16[2,2,272,128]{3,2,1,0:T(8,128)(2,1)S(1)}, bf16[2,2,272,128]{3,2,1,0:T(8,128)(2,1)S(1)}, u32[]{:S(2)}, u32[]{:S(2)}) collective-permute-start(bf16[2,2,272,128]{3,2,1,0:T(8,128)(2,1)S(1)} %copy-done.15), channel_id=1, source_target_pairs={{0,2},{1,3},{2,0},{3,1},{4,6},{5,7},{6,4},{7,5},{8,10},{9,11},{10,... | collective-permute-start | bytes 835592 | tf_op jit(solution)/shard_map/ppermute | solution.py:228
  169.9 45.7 %collective-permute-start.9 = (bf16[2,2,272,128]{3,2,1,0:T(8,128)(2,1)S(1)}, bf16[2,2,272,128]{3,2,1,0:T(8,128)(2,1)S(1)}, u32[]{:S(2)}, u32[]{:S(2)}) collective-permute-start(bf16[2,2,272,128]{3,2,1,0:T(8,128)(2,1)S(1)} %copy-done.14), channel_id=1, source_target_pairs={{0,1},{1,2},{2,3},{3,0},{4,5},{5,6},{6,7},{7,4},{8,9},{9,10},{10,1... | collective-permute-start | bytes 835592 | tf_op jit(solution)/shard_map/ppermute | solution.py:228
  181.4 37.8 %collective-permute-start.2 = (bf16[2,2,272,128]{3,2,1,0:T(8,128)(2,1)S(1)}, bf16[2,2,272,128]{3,2,1,0:T(8,128)(2,1)S(1)}, u32[]{:S(2)}, u32[]{:S(2)}) collective-permute-start(bf16[2,2,272,128]{3,2,1,0:T(8,128)(2,1)S(1)} %get-tuple-element.27), channel_id=1, source_target_pairs={{0,3},{1,0},{2,1},{3,2},{4,7},{5,4},{6,5},{7,6},{8,11},{9,8},{10,9... | collective-permute-start | bytes 835592 | tf_op jit(solution)/shard_map/ppermute | solution.py:228
  194.2 27.5 %collective-permute-start.1 = (bf16[2,2,272,128]{3,2,1,0:T(8,128)(2,1)S(1)}, bf16[2,2,272,128]{3,2,1,0:T(8,128)(2,1)S(1)}, u32[]{:S(2)}, u32[]{:S(2)}) collective-permute-start(bf16[2,2,272,128]{3,2,1,0:T(8,128)(2,1)S(1)} %get-tuple-element.28), channel_id=1, source_target_pairs={{0,2},{1,3},{2,0},{3,1},{4,6},{5,7},{6,4},{7,5},{8,10},{9,11},{10,... | collective-permute-start | bytes 835592 | tf_op jit(solution)/shard_map/ppermute | solution.py:228
  199.1 26.8 %collective-permute-start = (bf16[2,2,272,128]{3,2,1,0:T(8,128)(2,1)S(1)}, bf16[2,2,272,128]{3,2,1,0:T(8,128)(2,1)S(1)}, u32[]{:S(2)}, u32[]{:S(2)}) collective-permute-start(bf16[2,2,272,128]{3,2,1,0:T(8,128)(2,1)S(1)} %get-tuple-element.29), channel_id=1, source_target_pairs={{0,1},{1,2},{2,3},{3,0},{4,5},{5,6},{6,7},{7,4},{8,9},{9,10},{10,1... | collective-permute-start | bytes 835592 | tf_op jit(solution)/shard_map/ppermute | solution.py:228
  204.3 4.5 %copy-start.7 = (bf16[8,1,2,17,16,128]{5,4,3,2,1,0:T(8,128)(2,1)S(1)}, bf16[8,1,2,17,16,128]{5,4,3,2,1,0:T(8,128)(2,1)}, u32[]{:S(2)}) copy-start(bf16[8,1,2,17,16,128]{5,4,3,2,1,0:T(8,128)(2,1)} %copy-done.5) | copy-start | bytes 3342340

commit v2 on v1

--- a/solution.py
+++ b/solution.py
@@ -15,7 +15,7 @@
 V_DIM = 128
 LANES = 128
 QUERY, KEY, VALUE, OUT = range(4)
-VMEM_LIMIT = 48 * 1024 * 1024
+VMEM_LIMIT = 16 * 1024 * 1024
 
 
 def piece_widths(rank_total):
@@ -27,57 +27,69 @@
     )
 
 
-def pack(table, param_offsets, owner_map, ways, widths, granule, layers, slots, kinds):
+def pack(table, param_offsets, owner_map, ways, widths, granule, chunks, kinds):
     head_count = owner_map.shape[1]
     steps = [widths[kind] // granule for kind in kinds]
     starts = [sum(steps[:i]) for i in range(len(kinds))]
-    out = jax.ShapeDtypeStruct(
-        (ways, len(layers), len(slots), sum(steps)) + table.shape[2:], table.dtype
-    )
-
-    def kernel(offsets, owners, source, target, taken):
-        for at, layer in enumerate(layers):
+    outs = [
+        jax.ShapeDtypeStruct(
+            (ways, len(layers), len(slots), sum(steps)) + table.shape[2:], table.dtype
+        )
+        for layers, slots in chunks
+    ]
+
+    def kernel(offsets, owners, source, *refs):
+        targets, taken = refs[:-1], refs[-1]
+        for layer in sorted({layer for layers, _ in chunks for layer in layers}):
             for way in range(ways):
                 taken[way] = 0
-
-            @pl.loop(0, head_count)
-            def _(head):
+            here = [
+                (target, layers.index(layer), slots)
+                for target, (layers, slots) in zip(targets, chunks)
+                if layer in layers
+            ]
+
+            def one_head(head):
                 way = owners[layer, head]
                 slot = taken[way]
                 taken[way] = slot + 1
-
-                @pl.when(jnp.logical_and(slot >= slots[0], slot <= slots[-1]))
-                def _():
-                    for kind, step, start in zip(kinds, steps, starts):
-                        begin = lax.div(offsets[layer, head, kind], jnp.int32(granule))
-                        target[way, at, slot - slots[0], pl.ds(start, step)] = source[
-                            layer, pl.ds(begin, step)
-                        ]
+                begins = [lax.div(offsets[layer, head, kind], jnp.int32(granule)) for kind in kinds]
+                for target, at, slots in here:
+
+                    @pl.when(jnp.logical_and(slot >= slots[0], slot <= slots[-1]))
+                    def _():
+                        for begin, step, start in zip(begins, steps, starts):
+                            target[way, at, slot - slots[0], pl.ds(start, step)] = source[
+                                layer, pl.ds(begin, step)
+                            ]
+
+            pl.loop(0, head_count, unroll=min(8, head_count))(one_head)
 
     return pl.pallas_call(
         kernel,
-        out_shape=out,
+        out_shape=outs,
         in_specs=[
             pl.BlockSpec(memory_space=pltpu.SMEM),
             pl.BlockSpec(memory_space=pltpu.SMEM),
             pl.BlockSpec(memory_space=pltpu.VMEM),
         ],
-        out_specs=pl.BlockSpec(memory_space=pltpu.VMEM),
+        out_specs=[pl.BlockSpec(memory_space=pltpu.VMEM)] * len(outs),
         scratch_shapes=[pltpu.SMEM((ways,), jnp.int32)],
         compiler_params=pltpu.CompilerParams(vmem_limit_bytes=VMEM_LIMIT),
         cost_estimate=pl.CostEstimate(
-            flops=0, transcendentals=0, bytes_accessed=2 * 2 * math.prod(out.shape)
+            flops=0,
+            transcendentals=0,
+            bytes_accessed=sum(2 * 2 * math.prod(out.shape) for out in outs),
         ),
         name="pack",
     )(param_offsets, owner_map, table)
 
 
-def spread(x, axis, ways, me):
-    up, down = [x], [x]
-    for _ in range(ways - 1):
-        up.append(lax.ppermute(up[-1], axis, [(i, i + 1) for i in range(ways - 1)]))
-        down.append(lax.ppermute(down[-1], axis, [(i + 1, i) for i in range(ways - 1)]))
-    return [x] + [jnp.where(me >= d, up[d], down[ways - d]) for d in range(1, ways)]
+def line_step(up, down, axis, ways):
+    return (
+        lax.ppermute(up, axis, [(i, i + 1) for i in range(ways - 1)]),
+        lax.ppermute(down, axis, [(i + 1, i) for i in range(ways - 1)]),
+    )
 
 
 def assemble(me, spread_parts):
@@ -203,49 +215,29 @@
     slice_row = lax.dynamic_index_in_dim(slice_map, lax.axis_index("fsdp"), 0, keepdims=False)
     blocks = f_ways // t_ways
 
-    def packed(layers, slots, kinds):
-        return pack(table, param_offsets, owner_map, f_ways, widths, granule, layers, slots, kinds)
-
-    def over_fsdp(x):
-        return lax.all_to_all(x, "fsdp", split_axis=0, concat_axis=0, tiled=True)
-
-    pairs = over_fsdp(packed(range(layer_count), range(per_group), (KEY, VALUE)))
-    pairs = pairs.reshape(f_ways, layer_count, per_group, 2, row_counts[KEY], LANES)
-    pairs = spread(pairs, "tp", t_ways, me)
-
     half = max(1, per_group // 2)
     chunks = [
         (layer, range(at, at + half)) for layer in range(layer_count) for at in range(0, per_group, half)
     ]
-    exchanged = []
-    for layer, slots in chunks:
-        rows = over_fsdp(packed((layer,), slots, (QUERY, OUT)))
-        rows = rows.reshape(f_ways, len(slots), rows_total, LANES)
+
+    def packed(of, kinds):
+        return pack(table, param_offsets, owner_map, f_ways, widths, granule, of, kinds)
+
+    def over_fsdp(x):
+        return lax.all_to_all(x, "fsdp", split_axis=0, concat_axis=0, tiled=True)
+
+    def over_tp(rows):
         came = []
         for shift in range(1, t_ways):
             block = slice_row[lax.rem(me + shift, t_ways)]
             piece = lax.dynamic_slice_in_dim(rows, block * blocks, blocks, 0)
             came.append(lax.ppermute(piece, "tp", [(i, (i + shift) % t_ways) for i in range(t_ways)]))
-        exchanged.append((rows, came))
-
-    if not whole_tiles:
-        order = lax.rem(me - jnp.arange(t_ways, dtype=jnp.int32) + t_ways, jnp.int32(t_ways))
-        matrices = jnp.take(jnp.stack(pairs), order, axis=0).transpose(2, 3, 4, 1, 0, 5, 6)
-        matrices = matrices.reshape(layer_count, per_group, 2, -1, KVR)
-        done = [
-            absorb_plain(
-                me,
-                lax.dynamic_slice_in_dim(rows, slice_row[me] * blocks, blocks, 0),
-                came,
-                matrices[layer, slots[0] : slots[-1] + 1],
-            )
-            for (layer, slots), (rows, came) in zip(chunks, exchanged)
-        ]
-        return tuple(
-            jnp.concatenate(kind).reshape(layer_count, per_group, -1, KVR) for kind in zip(*done)
-        )
-
-    matrices = assemble(me, pairs)
+        return came
+
+    (pairs,) = packed([(range(layer_count), range(per_group))], (KEY, VALUE))
+    to_send = packed([((layer,), slots) for layer, slots in chunks], (QUERY, OUT))
+    pairs = over_fsdp(pairs).reshape(f_ways, layer_count, per_group, 2, row_counts[KEY], LANES)
+
     shapes = tuple(
         jax.ShapeDtypeStruct(
             (layer_count, per_group, blocks, t_ways, row_counts[kind], KVR), jnp.bfloat16
@@ -253,10 +245,48 @@
         for kind in (QUERY, OUT)
     )
     where = jnp.stack([me, slice_row[me]])
-    outs = None
-    for (layer, slots), (rows, came) in zip(chunks, exchanged):
-        outs = absorb(where, layer, slots, rows, came, matrices, outs, shapes)
-    return tuple(out.reshape(layer_count, per_group, -1, KVR) for out in outs)
+    up, down = [pairs], [pairs]
+    exchanged, came, rows, outs, matrices = [], None, None, None, None
+    for stage in range(len(chunks) + 2):
+        arriving = over_tp(rows) if rows is not None else None
+        for _ in range(2 if stage == 0 else t_ways):
+            if len(up) < t_ways:
+                above, below = line_step(up[-1], down[-1], "tp", t_ways)
+                up.append(above)
+                down.append(below)
+        following = None
+        if stage < len(chunks):
+            following = over_fsdp(to_send[stage])
+            following = following.reshape(f_ways, len(chunks[stage][1]), rows_total, LANES)
+        if came is not None:
+            exchanged.append((settled, came))
+            if whole_tiles:
+                if matrices is None:
+                    near = [jnp.where(me >= d, up[d], down[t_ways - d]) for d in range(1, t_ways)]
+                    matrices = assemble(me, [pairs] + near)
+                layer, slots = chunks[stage - 2]
+                outs = absorb(where, layer, slots, settled, came, matrices, outs, shapes)
+        arriving, following, up, down, to_send, outs, matrices = lax.optimization_barrier(
+            (arriving, following, up, down, to_send, outs, matrices)
+        )
+        settled, came, rows = rows, arriving, following
+    if whole_tiles:
+        return tuple(out.reshape(layer_count, per_group, -1, KVR) for out in outs)
+
+    near = [jnp.where(me >= d, up[d], down[t_ways - d]) for d in range(1, t_ways)]
+    order = lax.rem(me - jnp.arange(t_ways, dtype=jnp.int32) + t_ways, jnp.int32(t_ways))
+    matrices = jnp.take(jnp.stack([pairs] + near), order, axis=0).transpose(2, 3, 4, 1, 0, 5, 6)
+    matrices = matrices.reshape(layer_count, per_group, 2, -1, KVR)
+    done = [
+        absorb_plain(
+            me,
+            lax.dynamic_slice_in_dim(rows, slice_row[me] * blocks, blocks, 0),
+            came,
+            matrices[layer, slots[0] : slots[-1] + 1],
+        )
+        for (layer, slots), (rows, came) in zip(chunks, exchanged)
+    ]
+    return tuple(jnp.concatenate(kind).reshape(layer_count, per_group, -1, KVR) for kind in zip(*done))
 
 
 def solution(mesh):

time: 231 us -> 201 us (0.87)
  starting transfers between devices: 76.2 us -> 60.5 us
  blocking collectives: 0 us -> 12.3 us
  waiting for transfers between devices: 93.9 us -> 83.4 us
  local copies, waits for them, and re-layouts: 24.2 us -> 15.1 us
  Pallas kernels: 28.2 us -> 21.9 us
    all_to_all x5 -> x4, waiting for transfers between devices: 28.7 us -> 8.74 us  [over_fsdp(): return lax.all_to_all(x, 'fsdp', split_axis=0, concat_axis=0, tiled=True)]
    all_to_all x0 -> x1, blocking collectives: none -> 12.3 us  [over_fsdp(): return lax.all_to_all(x, 'fsdp', split_axis=0, concat_axis=0, tiled=True)]
    ppermute x18, starting transfers between devices: 52.1 us -> 42.4 us  [the longest x12 24 us: over_tp(): lax.ppermute(piece, 'tp', [(i, (i + shift) % t_ways) for i in range(t_way...]
    ppermute x18, waiting for transfers between devices: 65.2 us -> 74.7 us  [the longest x12 71.1 us: over_tp(): lax.ppermute(piece, 'tp', [(i, (i + shift) % t_ways) for i in range(t_way...]
    unnamed x44 -> x60, local copies, waits for them, and re-layouts: 20.7 us -> 12.9 us
    pallas_call x5 -> x2, Pallas kernels: 11.9 us -> 5.79 us  [pack(): pl.pallas_call(kernel, out_shape=outs, in_specs=[pl.BlockSpec(memory_spac...]
    all_to_all x5 -> x4, starting transfers between devices: 24.2 us -> 18.1 us  [over_fsdp(): return lax.all_to_all(x, 'fsdp', split_axis=0, concat_axis=0, tiled=True)]
  transfers between devices with their start and end apart: 23 -> 22, of which waited for: 14 -> 14; matrix products, arithmetic and copies ran while one was open for 3% -> 2% of each run, Pallas kernels for 9% -> 8%
where the time goes in v2:
time: 201 us; the launch traced here: 198 us
  waiting for transfers between devices  83.4 us (41%)
  starting transfers between devices  60.5 us (30%)
  Pallas kernels  21.9 us (11%)
  local copies, waits for them, and re-layouts  15.1 us (8%)
  blocking collectives  12.3 us (6%)
  between operations  2.85 us (1%)
    ppermute x12, waiting for transfers between devices, over_tp(): lax.ppermute(piece, 'tp', [(i, (i + shift) % t_ways) for i in range(t_way...  71.1 us
    ppermute x12, starting transfers between devices, over_tp(): lax.ppermute(piece, 'tp', [(i, (i + shift) % t_ways) for i in range(t_way...  24 us
    all_to_all x4, starting transfers between devices, over_fsdp(): return lax.all_to_all(x, 'fsdp', split_axis=0, concat_axis=0, tiled=True)  18.1 us
    pallas_call x4, Pallas kernels, absorb(): pl.pallas_call(kernel, grid_spec=pltpu.PrefetchScalarGridSpec(num_scalar_...  14.9 us
    unnamed x60, local copies, waits for them, and re-layouts  12.9 us
    all_to_all x1, blocking collectives, over_fsdp(): return lax.all_to_all(x, 'fsdp', split_axis=0, concat_axis=0, tiled=True)  12.3 us
    ppermute x3, starting transfers between devices, line_step(): lax.ppermute(up, axis, [(i, i + 1) for i in range(ways - 1)])  10.4 us
    all_to_all x4, waiting for transfers between devices, over_fsdp(): return lax.all_to_all(x, 'fsdp', split_axis=0, concat_axis=0, tiled=True)  8.74 us
  transfers between devices with their start and end apart: 22, of which 14 were waited for; matrix products, arithmetic and copies ran while one was open for 2% of the time, Pallas kernels for 8%

profile of v2, /device:TPU:10, one launch (start us, length us, event | category | flops | bytes accessed | tf_op | source)
XLA Modules:
  0.0 198.0 jit_solution(1534482350734534659)
XLA Ops:
  0.6 0.8 copy.12.offsets
  1.4 3.1 %copy.14 = bf16[1,2,9728,128]{3,2,1,0:T(8,128)(2,1)S(1)} copy(bf16[1,2,9728,128]{3,1,2,0:T(2,128)(2,1)} %bitcast.24) | data formatting | bytes 9961472
  4.6 2.1 %pack.3 = bf16[8,2,4,2,16,128]{5,4,3,2,1,0:T(8,128)(2,1)S(1)} custom-call(s32[2,32,4]{2,1,0:T(8,128)S(1)} %copy.12.offsets, s32[2,32]{1,0:T(2,128)S(1)} %copy-done.23, bf16[2,608,16,128]{3,2,1,0:T(8,128)(2,1)S(1)} %bitcast.14), custom_call_target="tpu_custom_call" | custom-call | bytes 1048576 | tf_op jit(solution)/shard_map/pack/pallas_call | solution.py:68
  6.6 12.3 %all_to_all.25.refs_0_ = bf16[8,2,4,2,16,128]{5,4,3,2,1,0:T(8,128)(2,1)S(1)} all-to-all(bf16[8,2,4,2,16,128]{5,4,3,2,1,0:T(8,128)(2,1)S(1)} %pack.3), channel_id=1, replica_groups=mesh['fsdp'=8,'tp'=4] {'fsdp'}, dimensions={0} | all-to-all | bytes 1048576 | tf_op jit(solution)/shard_map/all_to_all | solution.py:227
  19.0 2.3 %collective-permute-start.2 = (bf16[8,2,4,2,16,128]{5,4,3,2,1,0:T(8,128)(2,1)S(1)}, bf16[8,2,4,2,16,128]{5,4,3,2,1,0:T(8,128)(2,1)S(1)}, u32[]{:S(2)}, u32[]{:S(2)}) collective-permute-start(bf16[8,2,4,2,16,128]{5,4,3,2,1,0:T(8,128)(2,1)S(1)} %all_to_all.25.refs_0_), channel_id=1, source_target_pairs={{1,0},{2,1},{3,2},{5,4},{6,5},{7,6},{9,8},{10,9},{11,10},{13,12},{... | collective-permute-start | bytes 1572872 | tf_op jit(solution)/shard_map/ppermute | solution.py:91
  21.3 3.5 %collective-permute-start = (bf16[8,2,4,2,16,128]{5,4,3,2,1,0:T(8,128)(2,1)S(1)}, bf16[8,2,4,2,16,128]{5,4,3,2,1,0:T(8,128)(2,1)S(1)}, u32[]{:S(2)}, u32[]{:S(2)}) collective-permute-start(bf16[8,2,4,2,16,128]{5,4,3,2,1,0:T(8,128)(2,1)S(1)} %all_to_all.25.refs_0_), channel_id=1, source_target_pairs={{0,1},{1,2},{2,3},{4,5},{5,6},{6,7},{8,9},{9,10},{10,11},{12,13},{... | collective-permute-start | bytes 1572872 | tf_op jit(solution)/shard_map/ppermute | solution.py:90
  24.8 3.7 %pack.2 = (bf16[8,1,2,17,16,128]{5,4,3,2,1,0:T(8,128)(2,1)}, bf16[8,1,2,17,16,128]{5,4,3,2,1,0:T(8,128)(2,1)S(1)}, bf16[8,1,2,17,16,128]{5,4,3,2,1,0:T(8,128)(2,1)S(1)}, bf16[8,1,2,17,16,128]{5,4,3,2,1,0:T(8,128)(2,1)S(1)}) custom-call(s32[2,32,4]{2,1,0:T(8,128)S(1)} %copy.12.offsets, s32[2,32]{1,0:T(2,128)S(1)} %copy-done.23, ...), custom_call_target="tpu_custom_call" | custom-call | bytes 8912896 | tf_op jit(solution)/shard_map/pack/pallas_call | solution.py:68
  28.5 1.0 copy-done.4
  29.6 1.0 copy-done.5
  30.6 1.0 copy-done.6
  31.6 4.9 %all-to-all-start = ((bf16[8,1,2,17,16,128]{5,4,3,2,1,0:T(8,128)(2,1)}), bf16[8,1,2,17,16,128]{5,4,3,2,1,0:T(8,128)(2,1)S(1)}, u32[]{:S(2)}, u32[]{:S(2)}) async-start(bf16[8,1,2,17,16,128]{5,4,3,2,1,0:T(8,128)(2,1)} %get-tuple-element.57), calls=%async_computation | async-start | bytes 2228224 | tf_op jit(solution)/shard_map/all_to_all | solution.py:227
  36.5 0.0 collective-permute-done.2
  36.5 2.4 %collective-permute-start.3 = (bf16[8,2,4,2,16,128]{5,4,3,2,1,0:T(8,128)(2,1)S(1)}, bf16[8,2,4,2,16,128]{5,4,3,2,1,0:T(8,128)(2,1)}, u32[]{:S(2)}, u32[]{:S(2)}) collective-permute-start(bf16[8,2,4,2,16,128]{5,4,3,2,1,0:T(8,128)(2,1)S(1)} %collective-permute-done.2), channel_id=1, source_target_pairs={{1,0},{2,1},{3,2},{5,4},{6,5},{7,6},{9,8},{10,9},{11,10},{13,12},{... | collective-permute-start | bytes 1572872 | tf_op jit(solution)/shard_map/ppermute | solution.py:91
  38.9 0.0 collective-permute-done
  38.9 3.5 %collective-permute-start.1 = (bf16[8,2,4,2,16,128]{5,4,3,2,1,0:T(8,128)(2,1)S(1)}, bf16[8,2,4,2,16,128]{5,4,3,2,1,0:T(8,128)(2,1)}, u32[]{:S(2)}, u32[]{:S(2)}) collective-permute-start(bf16[8,2,4,2,16,128]{5,4,3,2,1,0:T(8,128)(2,1)S(1)} %collective-permute-done), channel_id=1, source_target_pairs={{0,1},{1,2},{2,3},{4,5},{5,6},{6,7},{8,9},{9,10},{10,11},{12,13},{... | collective-permute-start | bytes 1572872 | tf_op jit(solution)/shard_map/ppermute | solution.py:90
  42.4 8.7 %all-to-all-done = bf16[8,1,2,17,16,128]{5,4,3,2,1,0:T(8,128)(2,1)S(1)} async-done(((bf16[8,1,2,17,16,128]{5,4,3,2,1,0:T(8,128)(2,1)}), bf16[8,1,2,17,16,128]{5,4,3,2,1,0:T(8,128)(2,1)S(1)}, u32[]{:S(2)}, u32[]{:S(2)}) %all-to-all-start) | async-done | bytes 1114144 | tf_op jit(solution)/shard_map/all_to_all | solution.py:227
  51.1 1.4 collective-permute-done.3
  52.5 2.1 %collective-permute-done.1 = bf16[8,2,4,2,16,128]{5,4,3,2,1,0:T(8,128)(2,1)} collective-permute-done((bf16[8,2,4,2,16,128]{5,4,3,2,1,0:T(8,128)(2,1)S(1)}, bf16[8,2,4,2,16,128]{5,4,3,2,1,0:T(8,128)(2,1)}, u32[]{:S(2)}, u32[]{:S(2)}) %collective-permute-start.1) | collective-permute-done | bytes 524320 | tf_op jit(solution)/shard_map/ppermute | solution.py:90
  54.6 4.4 %all-to-all-start.2 = ((bf16[8,1,2,17,16,128]{5,4,3,2,1,0:T(8,128)(2,1)}), bf16[8,1,2,17,16,128]{5,4,3,2,1,0:T(8,128)(2,1)S(1)}, u32[]{:S(2)}, u32[]{:S(2)}) async-start(bf16[8,1,2,17,16,128]{5,4,3,2,1,0:T(8,128)(2,1)} %copy-done.6), calls=%async_computation.2 | async-start | bytes 2228224 | tf_op jit(solution)/shard_map/all_to_all | solution.py:227
  59.0 3.4 %collective-permute-start.7 = (bf16[8,2,4,2,16,128]{5,4,3,2,1,0:T(8,128)(2,1)}, bf16[8,2,4,2,16,128]{5,4,3,2,1,0:T(8,128)(2,1)}, u32[]{:S(2)}, u32[]{:S(2)}) collective-permute-start(bf16[8,2,4,2,16,128]{5,4,3,2,1,0:T(8,128)(2,1)} %collective-permute-done.1), channel_id=1, source_target_pairs={{0,1},{1,2},{2,3},{4,5},{5,6},{6,7},{8,9},{9,10},{10,11},{12,13},{... | collective-permute-start | bytes 1572872 | tf_op jit(solution)/shard_map/ppermute | solution.py:90
  62.5 3.2 %collective-permute-start.8 = (bf16[8,2,4,2,16,128]{5,4,3,2,1,0:T(8,128)(2,1)}, bf16[8,2,4,2,16,128]{5,4,3,2,1,0:T(8,128)(2,1)}, u32[]{:S(2)}, u32[]{:S(2)}) collective-permute-start(bf16[8,2,4,2,16,128]{5,4,3,2,1,0:T(8,128)(2,1)} %collective-permute-done.3), channel_id=1, source_target_pairs={{1,0},{2,1},{3,2},{5,4},{6,5},{7,6},{9,8},{10,9},{11,10},{13,12},{... | collective-permute-start | bytes 1572872 | tf_op jit(solution)/shard_map/ppermute | solution.py:91
  65.7 0.7 fusion
  68.3 0.1 constant_dynamic-slice_fusion.9
  68.4 0.1 collective-permute-start.6
  68.5 3.3 %collective-permute-start.5 = (bf16[2,2,272,128]{3,2,1,0:T(8,128)(2,1)S(1)}, bf16[2,2,272,128]{3,2,1,0:T(8,128)(2,1)S(1)}, u32[]{:S(2)}, u32[]{:S(2)}) collective-permute-start(bf16[2,2,272,128]{3,2,1,0:T(8,128)(2,1)S(1)} %get-tuple-element.122), channel_id=1, source_target_pairs={{0,2},{1,3},{2,0},{3,1},{4,6},{5,7},{6,4},{7,5},{8,10},{9,11},{10,... | collective-permute-start | bytes 835592 | tf_op jit(solution)/shard_map/ppermute | solution.py:234
  71.8 2.8 %collective-permute-start.4 = (bf16[2,2,272,128]{3,2,1,0:T(8,128)(2,1)S(1)}, bf16[2,2,272,128]{3,2,1,0:T(8,128)(2,1)S(1)}, u32[]{:S(2)}, u32[]{:S(2)}) collective-permute-start(bf16[2,2,272,128]{3,2,1,0:T(8,128)(2,1)S(1)} %get-tuple-element.123), channel_id=1, source_target_pairs={{0,1},{1,2},{2,3},{3,0},{4,5},{5,6},{6,7},{7,4},{8,9},{9,10},{10,1... | collective-permute-start | bytes 835592 | tf_op jit(solution)/shard_map/ppermute | solution.py:234
  74.6 11.7 %collective-permute-done.6.refs_3_ = bf16[2,2,272,128]{3,2,1,0:T(8,128)(2,1)S(1)} collective-permute-done((bf16[2,2,272,128]{3,2,1,0:T(8,128)(2,1)S(1)}, bf16[2,2,272,128]{3,2,1,0:T(8,128)(2,1)S(1)}, u32[]{:S(2)}, u32[]{:S(2)}) %collective-permute-start.6) | collective-permute-done | bytes 278560 | tf_op jit(solution)/shard_map/ppermute | solution.py:234
  86.4 6.8 %collective-permute-done.5.refs_2_ = bf16[2,2,272,128]{3,2,1,0:T(8,128)(2,1)S(1)} collective-permute-done((bf16[2,2,272,128]{3,2,1,0:T(8,128)(2,1)S(1)}, bf16[2,2,272,128]{3,2,1,0:T(8,128)(2,1)S(1)}, u32[]{:S(2)}, u32[]{:S(2)}) %collective-permute-start.5) | collective-permute-done | bytes 278560 | tf_op jit(solution)/shard_map/ppermute | solution.py:234
  93.2 4.8 %collective-permute-done.4.refs_1_ = bf16[2,2,272,128]{3,2,1,0:T(8,128)(2,1)S(1)} collective-permute-done((bf16[2,2,272,128]{3,2,1,0:T(8,128)(2,1)S(1)}, bf16[2,2,272,128]{3,2,1,0:T(8,128)(2,1)S(1)}, u32[]{:S(2)}, u32[]{:S(2)}) %collective-permute-start.4) | collective-permute-done | bytes 278560 | tf_op jit(solution)/shard_map/ppermute | solution.py:234
  98.1 0.7 copy-done.9
  98.8 4.5 %all-to-all-start.3 = ((bf16[8,1,2,17,16,128]{5,4,3,2,1,0:T(8,128)(2,1)}), bf16[8,1,2,17,16,128]{5,4,3,2,1,0:T(8,128)(2,1)}, u32[]{:S(2)}, u32[]{:S(2)}) async-start(bf16[8,1,2,17,16,128]{5,4,3,2,1,0:T(8,128)(2,1)} %copy-done.5), calls=%async_computation.3 | async-start | bytes 2228224 | tf_op jit(solution)/shard_map/all_to_all | solution.py:227
  103.3 0.8 pad_add_fusion.at
  104.0 0.1 constant_dynamic-slice_fusion.6
  104.1 6.3 %collective-permute-start.11 = (bf16[2,2,272,128]{3,2,1,0:T(8,128)(2,1)S(1)}, bf16[2,2,272,128]{3,2,1,0:T(8,128)(2,1)S(1)}, u32[]{:S(2)}, u32[]{:S(2)}) collective-permute-start(bf16[2,2,272,128]{3,2,1,0:T(8,128)(2,1)S(1)} %get-tuple-element.118), channel_id=1, source_target_pairs={{0,3},{1,0},{2,1},{3,2},{4,7},{5,4},{6,5},{7,6},{8,11},{9,8},{10,9... | collective-permute-start | bytes 835592 | tf_op jit(solution)/shard_map/ppermute | solution.py:234
  110.4 1.5 collective-permute-start.9
  112.0 1.1 broadcast_select_fusion
  113.1 0.1 broadcast_select_fusion.2.refs_1_
  113.2 1.0 copy-done.3
  114.2 1.2 assemble.1.refs_4_
  115.4 3.5 %absorb.4 = (bf16[2,4,2,4,48,512]{5,4,3,2,1,0:T(8,128)(2,1)}, bf16[2,4,2,4,224,512]{5,4,3,2,1,0:T(8,128)(2,1)}) custom-call(s32[2]{0:T(128)S(1)} %pad_add_fusion.at, bf16[8,2,272,128]{3,2,1,0:T(8,128)(2,1)S(1)} %bitcast.17, bf16[2,2,272,128]{3,2,1,0:T(8,128)(2,1)S(1)} %copy-done.10, bf16[2,2,272,128]{3,2,1,0:T(8,128)(2,1)S(1)} %copy-done.8, ...), custom_call_target="tpu_custom_call" | custom-call | flops 570425344 | bytes 5570560 | tf_op jit(solution)/shard_map/absorb/pallas_call | solution.py:164
  118.9 0.7 copy-done.11
  119.6 8.8 %collective-permute-done.10.refs_2_ = bf16[2,2,272,128]{3,2,1,0:T(8,128)(2,1)S(1)} collective-permute-done((bf16[2,2,272,128]{3,2,1,0:T(8,128)(2,1)S(1)}, bf16[2,2,272,128]{3,2,1,0:T(8,128)(2,1)S(1)}, u32[]{:S(2)}, u32[]{:S(2)}) %collective-permute-start.10) | collective-permute-done | bytes 278560 | tf_op jit(solution)/shard_map/ppermute | solution.py:234
  128.4 0.7 copy-done.13
  129.2 5.2 %collective-permute-done.9.refs_1_ = bf16[2,2,272,128]{3,2,1,0:T(8,128)(2,1)S(1)} collective-permute-done((bf16[2,2,272,128]{3,2,1,0:T(8,128)(2,1)S(1)}, bf16[2,2,272,128]{3,2,1,0:T(8,128)(2,1)S(1)}, u32[]{:S(2)}, u32[]{:S(2)}) %collective-permute-start.9) | collective-permute-done | bytes 278560 | tf_op jit(solution)/shard_map/ppermute | solution.py:234
  134.3 0.7 copy-done.15
  135.0 4.4 %all-to-all-start.4 = ((bf16[8,1,2,17,16,128]{5,4,3,2,1,0:T(8,128)(2,1)}), bf16[8,1,2,17,16,128]{5,4,3,2,1,0:T(8,128)(2,1)S(1)}, u32[]{:S(2)}, u32[]{:S(2)}) async-start(bf16[8,1,2,17,16,128]{5,4,3,2,1,0:T(8,128)(2,1)} %copy-done.4), calls=%async_computation.4 | async-start | bytes 2228224 | tf_op jit(solution)/shard_map/all_to_all | solution.py:227
  139.4 1.3 constant_dynamic-slice_fusion.3
  140.7 1.3 collective-permute-start.14
  142.0 2.7 %collective-permute-start.13 = (bf16[2,2,272,128]{3,2,1,0:T(8,128)(2,1)S(1)}, bf16[2,2,272,128]{3,2,1,0:T(8,128)(2,1)S(1)}, u32[]{:S(2)}, u32[]{:S(2)}) collective-permute-start(bf16[2,2,272,128]{3,2,1,0:T(8,128)(2,1)S(1)} %get-tuple-element.116), channel_id=1, source_target_pairs={{0,2},{1,3},{2,0},{3,1},{4,6},{5,7},{6,4},{7,5},{8,10},{9,11},{10,... | collective-permute-start | bytes 835592 | tf_op jit(solution)/shard_map/ppermute | solution.py:234
  144.7 3.5 %absorb.5 = (bf16[2,4,2,4,48,512]{5,4,3,2,1,0:T(8,128)(2,1)}, bf16[2,4,2,4,224,512]{5,4,3,2,1,0:T(8,128)(2,1)}) custom-call(s32[2]{0:T(128)S(1)} %pad_add_fusion.at, bf16[8,2,272,128]{3,2,1,0:T(8,128)(2,1)S(1)} %bitcast.19, bf16[2,2,272,128]{3,2,1,0:T(8,128)(2,1)S(1)} %copy-done.16, ...), custom_call_target="tpu_custom_call", output_to_operand_aliasing={{0}: (6, {}), {1}: (7, {})} | custom-call | flops 570425344 | bytes 5570560 | tf_op jit(solution)/shard_map/absorb/pallas_call | solution.py:164
  148.3 2.5 %collective-permute-done.14.refs_3_ = bf16[2,2,272,128]{3,2,1,0:T(8,128)(2,1)S(1)} collective-permute-done((bf16[2,2,272,128]{3,2,1,0:T(8,128)(2,1)S(1)}, bf16[2,2,272,128]{3,2,1,0:T(8,128)(2,1)S(1)}, u32[]{:S(2)}, u32[]{:S(2)}) %collective-permute-start.14) | collective-permute-done | bytes 278560 | tf_op jit(solution)/shard_map/ppermute | solution.py:234
  150.8 0.7 copy-done.17
  151.5 8.6 %collective-permute-done.13.refs_2_ = bf16[2,2,272,128]{3,2,1,0:T(8,128)(2,1)S(1)} collective-permute-done((bf16[2,2,272,128]{3,2,1,0:T(8,128)(2,1)S(1)}, bf16[2,2,272,128]{3,2,1,0:T(8,128)(2,1)S(1)}, u32[]{:S(2)}, u32[]{:S(2)}) %collective-permute-start.13) | collective-permute-done | bytes 278560 | tf_op jit(solution)/shard_map/ppermute | solution.py:234
  160.1 0.7 copy-done.19
  160.8 5.2 %collective-permute-done.12.refs_1_ = bf16[2,2,272,128]{3,2,1,0:T(8,128)(2,1)S(1)} collective-permute-done((bf16[2,2,272,128]{3,2,1,0:T(8,128)(2,1)S(1)}, bf16[2,2,272,128]{3,2,1,0:T(8,128)(2,1)S(1)}, u32[]{:S(2)}, u32[]{:S(2)}) %collective-permute-start.12) | collective-permute-done | bytes 278560 | tf_op jit(solution)/shard_map/ppermute | solution.py:234
  165.9 0.7 copy-done.21
  166.6 0.1 constant_dynamic-slice_fusion
  166.7 4.4 %collective-permute-start.17 = (bf16[2,2,272,128]{3,2,1,0:T(8,128)(2,1)S(1)}, bf16[2,2,272,128]{3,2,1,0:T(8,128)(2,1)S(1)}, u32[]{:S(2)}, u32[]{:S(2)}) collective-permute-start(bf16[2,2,272,128]{3,2,1,0:T(8,128)(2,1)S(1)} %get-tuple-element.112), channel_id=1, source_target_pairs={{0,3},{1,0},{2,1},{3,2},{4,7},{5,4},{6,5},{7,6},{8,11},{9,8},{10,9... | collective-permute-start | bytes 835592 | tf_op jit(solution)/shard_map/ppermute | solution.py:234
  171.1 1.5 collective-permute-start.15
  172.7 4.3 %absorb.6 = (bf16[2,4,2,4,48,512]{5,4,3,2,1,0:T(8,128)(2,1)}, bf16[2,4,2,4,224,512]{5,4,3,2,1,0:T(8,128)(2,1)}) custom-call(s32[2]{0:T(128)S(1)} %pad_add_fusion.at, bf16[8,2,272,128]{3,2,1,0:T(8,128)(2,1)} %bitcast.7.refs_0_, bf16[2,2,272,128]{3,2,1,0:T(8,128)(2,1)S(1)} %copy-done.22, ...), custom_call_target="tpu_custom_call", output_to_operand_aliasing={{0}: (6, {}), {1}: (7, {})} | custom-call | flops 570425344 | bytes 5570560 | tf_op jit(solution)/shard_map/absorb/pallas_call | solution.py:164
  177.0 1.1 collective-permute-done.17.refs_3_
  178.1 10.5 %collective-permute-done.16.refs_2_ = bf16[2,2,272,128]{3,2,1,0:T(8,128)(2,1)S(1)} collective-permute-done((bf16[2,2,272,128]{3,2,1,0:T(8,128)(2,1)S(1)}, bf16[2,2,272,128]{3,2,1,0:T(8,128)(2,1)S(1)}, u32[]{:S(2)}, u32[]{:S(2)}) %collective-permute-start.16) | collective-permute-done | bytes 278560 | tf_op jit(solution)/shard_map/ppermute | solution.py:234
  188.6 5.9 %collective-permute-done.15.refs_1_ = bf16[2,2,272,128]{3,2,1,0:T(8,128)(2,1)S(1)} collective-permute-done((bf16[2,2,272,128]{3,2,1,0:T(8,128)(2,1)S(1)}, bf16[2,2,272,128]{3,2,1,0:T(8,128)(2,1)S(1)}, u32[]{:S(2)}, u32[]{:S(2)}) %collective-permute-start.15) | collective-permute-done | bytes 278560 | tf_op jit(solution)/shard_map/ppermute | solution.py:234
  194.5 3.5 %absorb.7 = (bf16[2,4,2,4,48,512]{5,4,3,2,1,0:T(8,128)(2,1)}, bf16[2,4,2,4,224,512]{5,4,3,2,1,0:T(8,128)(2,1)}) custom-call(s32[2]{0:T(128)S(1)} %pad_add_fusion.at, bf16[8,2,272,128]{3,2,1,0:T(8,128)(2,1)S(1)} %bitcast.21, bf16[2,2,272,128]{3,2,1,0:T(8,128)(2,1)S(1)} %collective-permute-done.15.refs_1_, ...), custom_call_target="tpu_custom_call", output_to_operand_aliasing={{0}: (6, {}), {1}: (7, {})} | custom-call | flops 570425344 | bytes 5570560 | tf_op jit(solution)/shard_map/absorb/pallas_call | solution.py:164
  (56 shorter events, 0.1 us)
Async XLA Ops:
  1.4 3.1 %copy-start.23 = (s32[2,32]{1,0:T(2,128)S(1)}, s32[2,32]{1,0:T(2,128)}, u32[]{:S(2)}) copy-start(s32[2,32]{1,0:T(2,128)} %owners.3) | copy-start | bytes 772
  19.0 9.6 %copy-start.2 = (bf16[8,2,4,2,16,128]{5,4,3,2,1,0:T(8,128)(2,1)}, bf16[8,2,4,2,16,128]{5,4,3,2,1,0:T(8,128)(2,1)S(1)}, u32[]{:S(2)}) copy-start(bf16[8,2,4,2,16,128]{5,4,3,2,1,0:T(8,128)(2,1)S(1)} %all_to_all.25.refs_0_) | copy-start | bytes 1572868
  19.0 17.5 %collective-permute-start.2 = (bf16[8,2,4,2,16,128]{5,4,3,2,1,0:T(8,128)(2,1)S(1)}, bf16[8,2,4,2,16,128]{5,4,3,2,1,0:T(8,128)(2,1)S(1)}, u32[]{:S(2)}, u32[]{:S(2)}) collective-permute-start(bf16[8,2,4,2,16,128]{5,4,3,2,1,0:T(8,128)(2,1)S(1)} %all_to_all.25.refs_0_), channel_id=1, source_target_pairs={{1,0},{2,1},{3,2},{5,4},{6,5},{7,6},{9,8},{10,9},{11,10},{13,12},{... | collective-permute-start | bytes 1572872 | tf_op jit(solution)/shard_map/ppermute | solution.py:91
  21.3 17.6 %collective-permute-start = (bf16[8,2,4,2,16,128]{5,4,3,2,1,0:T(8,128)(2,1)S(1)}, bf16[8,2,4,2,16,128]{5,4,3,2,1,0:T(8,128)(2,1)S(1)}, u32[]{:S(2)}, u32[]{:S(2)}) collective-permute-start(bf16[8,2,4,2,16,128]{5,4,3,2,1,0:T(8,128)(2,1)S(1)} %all_to_all.25.refs_0_), channel_id=1, source_target_pairs={{0,1},{1,2},{2,3},{4,5},{5,6},{6,7},{8,9},{9,10},{10,11},{12,13},{... | collective-permute-start | bytes 1572872 | tf_op jit(solution)/shard_map/ppermute | solution.py:90
  28.5 1.0 copy-start.4
  29.6 1.0 copy-start.5
  30.6 1.0 copy-start.6
  31.6 19.6 %all-to-all-start = ((bf16[8,1,2,17,16,128]{5,4,3,2,1,0:T(8,128)(2,1)}), bf16[8,1,2,17,16,128]{5,4,3,2,1,0:T(8,128)(2,1)S(1)}, u32[]{:S(2)}, u32[]{:S(2)}) async-start(bf16[8,1,2,17,16,128]{5,4,3,2,1,0:T(8,128)(2,1)} %get-tuple-element.57), calls=%async_computation | async-start | bytes 2228224 | tf_op jit(solution)/shard_map/all_to_all | solution.py:227
  36.5 18.1 %copy-start.26 = (bf16[8,2,4,2,16,128]{5,4,3,2,1,0:T(8,128)(2,1)}, bf16[8,2,4,2,16,128]{5,4,3,2,1,0:T(8,128)(2,1)S(1)}, u32[]{:S(2)}) copy-start(bf16[8,2,4,2,16,128]{5,4,3,2,1,0:T(8,128)(2,1)S(1)} %collective-permute-done.2) | copy-start | bytes 1572868
  36.5 16.0 %collective-permute-start.3 = (bf16[8,2,4,2,16,128]{5,4,3,2,1,0:T(8,128)(2,1)S(1)}, bf16[8,2,4,2,16,128]{5,4,3,2,1,0:T(8,128)(2,1)}, u32[]{:S(2)}, u32[]{:S(2)}) collective-permute-start(bf16[8,2,4,2,16,128]{5,4,3,2,1,0:T(8,128)(2,1)S(1)} %collective-permute-done.2), channel_id=1, source_target_pairs={{1,0},{2,1},{3,2},{5,4},{6,5},{7,6},{9,8},{10,9},{11,10},{13,12},{... | collective-permute-start | bytes 1572872 | tf_op jit(solution)/shard_map/ppermute | solution.py:91
  38.9 15.7 %copy-start.24 = (bf16[8,2,4,2,16,128]{5,4,3,2,1,0:T(8,128)(2,1)}, bf16[8,2,4,2,16,128]{5,4,3,2,1,0:T(8,128)(2,1)S(1)}, u32[]{:S(2)}) copy-start(bf16[8,2,4,2,16,128]{5,4,3,2,1,0:T(8,128)(2,1)S(1)} %collective-permute-done) | copy-start | bytes 1572868
  38.9 15.7 %collective-permute-start.1 = (bf16[8,2,4,2,16,128]{5,4,3,2,1,0:T(8,128)(2,1)S(1)}, bf16[8,2,4,2,16,128]{5,4,3,2,1,0:T(8,128)(2,1)}, u32[]{:S(2)}, u32[]{:S(2)}) collective-permute-start(bf16[8,2,4,2,16,128]{5,4,3,2,1,0:T(8,128)(2,1)S(1)} %collective-permute-done), channel_id=1, source_target_pairs={{0,1},{1,2},{2,3},{4,5},{5,6},{6,7},{8,9},{9,10},{10,11},{12,13},{... | collective-permute-start | bytes 1572872 | tf_op jit(solution)/shard_map/ppermute | solution.py:90
  54.6 11.1 %copy-start.28 = (s32[8,4]{0,1:T(4,128)S(1)}, s32[8,4]{0,1:T(4,128)}, u32[]{:S(2)}) copy-start(s32[8,4]{0,1:T(4,128)} %param.7) | copy-start | bytes 388
  54.6 43.4 %all-to-all-start.2 = ((bf16[8,1,2,17,16,128]{5,4,3,2,1,0:T(8,128)(2,1)}), bf16[8,1,2,17,16,128]{5,4,3,2,1,0:T(8,128)(2,1)S(1)}, u32[]{:S(2)}, u32[]{:S(2)}) async-start(bf16[8,1,2,17,16,128]{5,4,3,2,1,0:T(8,128)(2,1)} %copy-done.6), calls=%async_computation.2 | async-start | bytes 2228224 | tf_op jit(solution)/shard_map/all_to_all | solution.py:227
  59.0 39.1 %collective-permute-start.7 = (bf16[8,2,4,2,16,128]{5,4,3,2,1,0:T(8,128)(2,1)}, bf16[8,2,4,2,16,128]{5,4,3,2,1,0:T(8,128)(2,1)}, u32[]{:S(2)}, u32[]{:S(2)}) collective-permute-start(bf16[8,2,4,2,16,128]{5,4,3,2,1,0:T(8,128)(2,1)} %collective-permute-done.1), channel_id=1, source_target_pairs={{0,1},{1,2},{2,3},{4,5},{5,6},{6,7},{8,9},{9,10},{10,11},{12,13},{... | collective-permute-start | bytes 1572872 | tf_op jit(solution)/shard_map/ppermute | solution.py:90
  62.5 35.6 %collective-permute-start.8 = (bf16[8,2,4,2,16,128]{5,4,3,2,1,0:T(8,128)(2,1)}, bf16[8,2,4,2,16,128]{5,4,3,2,1,0:T(8,128)(2,1)}, u32[]{:S(2)}, u32[]{:S(2)}) collective-permute-start(bf16[8,2,4,2,16,128]{5,4,3,2,1,0:T(8,128)(2,1)} %collective-permute-done.3), channel_id=1, source_target_pairs={{1,0},{2,1},{3,2},{5,4},{6,5},{7,6},{9,8},{10,9},{11,10},{13,12},{... | collective-permute-start | bytes 1572872 | tf_op jit(solution)/shard_map/ppermute | solution.py:91
  68.4 18.0 %collective-permute-start.6 = (bf16[2,2,272,128]{3,2,1,0:T(8,128)(2,1)S(1)}, bf16[2,2,272,128]{3,2,1,0:T(8,128)(2,1)S(1)}, u32[]{:S(2)}, u32[]{:S(2)}) collective-permute-start(bf16[2,2,272,128]{3,2,1,0:T(8,128)(2,1)S(1)} %get-tuple-element.121), channel_id=1, source_target_pairs={{0,3},{1,0},{2,1},{3,2},{4,7},{5,4},{6,5},{7,6},{8,11},{9,8},{10,9... | collective-permute-start | bytes 835592 | tf_op jit(solution)/shard_map/ppermute | solution.py:234
  68.5 24.8 %collective-permute-start.5 = (bf16[2,2,272,128]{3,2,1,0:T(8,128)(2,1)S(1)}, bf16[2,2,272,128]{3,2,1,0:T(8,128)(2,1)S(1)}, u32[]{:S(2)}, u32[]{:S(2)}) collective-permute-start(bf16[2,2,272,128]{3,2,1,0:T(8,128)(2,1)S(1)} %get-tuple-element.122), channel_id=1, source_target_pairs={{0,2},{1,3},{2,0},{3,1},{4,6},{5,7},{6,4},{7,5},{8,10},{9,11},{10,... | collective-permute-start | bytes 835592 | tf_op jit(solution)/shard_map/ppermute | solution.py:234
  71.8 26.3 %collective-permute-start.4 = (bf16[2,2,272,128]{3,2,1,0:T(8,128)(2,1)S(1)}, bf16[2,2,272,128]{3,2,1,0:T(8,128)(2,1)S(1)}, u32[]{:S(2)}, u32[]{:S(2)}) collective-permute-start(bf16[2,2,272,128]{3,2,1,0:T(8,128)(2,1)S(1)} %get-tuple-element.123), channel_id=1, source_target_pairs={{0,1},{1,2},{2,3},{3,0},{4,5},{5,6},{6,7},{7,4},{8,9},{9,10},{10,1... | collective-permute-start | bytes 835592 | tf_op jit(solution)/shard_map/ppermute | solution.py:234
  93.2 4.9 %copy-start.7 = (bf16[2,2,272,128]{3,2,1,0:T(8,128)(2,1)}, bf16[2,2,272,128]{3,2,1,0:T(8,128)(2,1)S(1)}, u32[]{:S(2)}) copy-start(bf16[2,2,272,128]{3,2,1,0:T(8,128)(2,1)S(1)} %collective-permute-done.5.refs_2_) | copy-start | bytes 835588
  98.1 0.7 copy-start.9
  98.1 5.9 %copy-start = (bf16[8,1,2,17,16,128]{5,4,3,2,1,0:T(8,128)(2,1)}, bf16[8,1,2,17,16,128]{5,4,3,2,1,0:T(8,128)(2,1)S(1)}, u32[]{:S(2)}) copy-start(bf16[8,1,2,17,16,128]{5,4,3,2,1,0:T(8,128)(2,1)S(1)} %all-to-all-done.2) | copy-start | bytes 3342340
  98.8 36.3 %all-to-all-start.3 = ((bf16[8,1,2,17,16,128]{5,4,3,2,1,0:T(8,128)(2,1)}), bf16[8,1,2,17,16,128]{5,4,3,2,1,0:T(8,128)(2,1)}, u32[]{:S(2)}, u32[]{:S(2)}) async-start(bf16[8,1,2,17,16,128]{5,4,3,2,1,0:T(8,128)(2,1)} %copy-done.5), calls=%async_computation.3 | async-start | bytes 2228224 | tf_op jit(solution)/shard_map/all_to_all | solution.py:227
  103.3 8.7 %copy-start.27 = (bf16[8,2,4,2,16,128]{5,4,3,2,1,0:T(8,128)(2,1)S(1)}, bf16[8,2,4,2,16,128]{5,4,3,2,1,0:T(8,128)(2,1)}, u32[]{:S(2)}) copy-start(bf16[8,2,4,2,16,128]{5,4,3,2,1,0:T(8,128)(2,1)} %copy-done.26) | copy-start | bytes 1572868
  104.1 14.8 %collective-permute-start.11 = (bf16[2,2,272,128]{3,2,1,0:T(8,128)(2,1)S(1)}, bf16[2,2,272,128]{3,2,1,0:T(8,128)(2,1)S(1)}, u32[]{:S(2)}, u32[]{:S(2)}) collective-permute-start(bf16[2,2,272,128]{3,2,1,0:T(8,128)(2,1)S(1)} %get-tuple-element.118), channel_id=1, source_target_pairs={{0,3},{1,0},{2,1},{3,2},{4,7},{5,4},{6,5},{7,6},{8,11},{9,8},{10,9... | collective-permute-start | bytes 835592 | tf_op jit(solution)/shard_map/ppermute | solution.py:234
  110.4 18.0 %collective-permute-start.10 = (bf16[2,2,272,128]{3,2,1,0:T(8,128)(2,1)S(1)}, bf16[2,2,272,128]{3,2,1,0:T(8,128)(2,1)S(1)}, u32[]{:S(2)}, u32[]{:S(2)}) collective-permute-start(bf16[2,2,272,128]{3,2,1,0:T(8,128)(2,1)S(1)} %get-tuple-element.119), channel_id=1, source_target_pairs={{0,2},{1,3},{2,0},{3,1},{4,6},{5,7},{6,4},{7,5},{8,10},{9,11},{10,... | collective-permute-start | bytes 835592 | tf_op jit(solution)/shard_map/ppermute | solution.py:234
  110.4 2.7 %copy-start.25 = (bf16[8,2,4,2,16,128]{5,4,3,2,1,0:T(8,128)(2,1)S(1)}, bf16[8,2,4,2,16,128]{5,4,3,2,1,0:T(8,128)(2,1)}, u32[]{:S(2)}) copy-start(bf16[8,2,4,2,16,128]{5,4,3,2,1,0:T(8,128)(2,1)} %copy-done.24) | copy-start | bytes 1572868
  110.4 23.9 %collective-permute-start.9 = (bf16[2,2,272,128]{3,2,1,0:T(8,128)(2,1)S(1)}, bf16[2,2,272,128]{3,2,1,0:T(8,128)(2,1)S(1)}, u32[]{:S(2)}, u32[]{:S(2)}) collective-permute-start(bf16[2,2,272,128]{3,2,1,0:T(8,128)(2,1)S(1)} %get-tuple-element.120), channel_id=1, source_target_pairs={{0,1},{1,2},{2,3},{3,0},{4,5},{5,6},{6,7},{7,4},{8,9},{9,10},{10,1... | collective-permute-start | bytes 835592 | tf_op jit(solution)/shard_map/ppermute | solution.py:234
  113.1 1.0 copy-start.3
  114.2 1.2 copy-start.8
  114.2 1.2 copy-start.10
  118.9 0.7 copy-start.11
  128.4 0.7 copy-start.13
  134.3 0.7 copy-start.15
  135.0 9.7 %copy-start.16 = (bf16[2,2,272,128]{3,2,1,0:T(8,128)(2,1)S(1)}, bf16[2,2,272,128]{3,2,1,0:T(8,128)(2,1)}, u32[]{:S(2)}) copy-start(bf16[2,2,272,128]{3,2,1,0:T(8,128)(2,1)} %copy-done.15) | copy-start | bytes 835588
  135.0 31.6 %all-to-all-start.4 = ((bf16[8,1,2,17,16,128]{5,4,3,2,1,0:T(8,128)(2,1)}), bf16[8,1,2,17,16,128]{5,4,3,2,1,0:T(8,128)(2,1)S(1)}, u32[]{:S(2)}, u32[]{:S(2)}) async-start(bf16[8,1,2,17,16,128]{5,4,3,2,1,0:T(8,128)(2,1)} %copy-done.4), calls=%async_computation.4 | async-start | bytes 2228224 | tf_op jit(solution)/shard_map/all_to_all | solution.py:227
  139.4 5.3 %copy-start.1 = (bf16[8,1,2,17,16,128]{5,4,3,2,1,0:T(8,128)(2,1)S(1)}, bf16[8,1,2,17,16,128]{5,4,3,2,1,0:T(8,128)(2,1)}, u32[]{:S(2)}) copy-start(bf16[8,1,2,17,16,128]{5,4,3,2,1,0:T(8,128)(2,1)} %copy-done) | copy-start | bytes 3342340
  139.4 5.3 %copy-start.12 = (bf16[2,2,272,128]{3,2,1,0:T(8,128)(2,1)S(1)}, bf16[2,2,272,128]{3,2,1,0:T(8,128)(2,1)}, u32[]{:S(2)}) copy-start(bf16[2,2,272,128]{3,2,1,0:T(8,128)(2,1)} %copy-done.11) | copy-start | bytes 835588
  139.4 5.3 %copy-start.14 = (bf16[2,2,272,128]{3,2,1,0:T(8,128)(2,1)S(1)}, bf16[2,2,272,128]{3,2,1,0:T(8,128)(2,1)}, u32[]{:S(2)}) copy-start(bf16[2,2,272,128]{3,2,1,0:T(8,128)(2,1)} %copy-done.13) | copy-start | bytes 835588
  140.7 10.0 %collective-permute-start.14 = (bf16[2,2,272,128]{3,2,1,0:T(8,128)(2,1)S(1)}, bf16[2,2,272,128]{3,2,1,0:T(8,128)(2,1)S(1)}, u32[]{:S(2)}, u32[]{:S(2)}) collective-permute-start(bf16[2,2,272,128]{3,2,1,0:T(8,128)(2,1)S(1)} %get-tuple-element.115), channel_id=1, source_target_pairs={{0,3},{1,0},{2,1},{3,2},{4,7},{5,4},{6,5},{7,6},{8,11},{9,8},{10,9... | collective-permute-start | bytes 835592 | tf_op jit(solution)/shard_map/ppermute | solution.py:234
  142.0 18.0 %collective-permute-start.13 = (bf16[2,2,272,128]{3,2,1,0:T(8,128)(2,1)S(1)}, bf16[2,2,272,128]{3,2,1,0:T(8,128)(2,1)S(1)}, u32[]{:S(2)}, u32[]{:S(2)}) collective-permute-start(bf16[2,2,272,128]{3,2,1,0:T(8,128)(2,1)S(1)} %get-tuple-element.116), channel_id=1, source_target_pairs={{0,2},{1,3},{2,0},{3,1},{4,6},{5,7},{6,4},{7,5},{8,10},{9,11},{10,... | collective-permute-start | bytes 835592 | tf_op jit(solution)/shard_map/ppermute | solution.py:234
  144.7 21.2 %collective-permute-start.12 = (bf16[2,2,272,128]{3,2,1,0:T(8,128)(2,1)S(1)}, bf16[2,2,272,128]{3,2,1,0:T(8,128)(2,1)S(1)}, u32[]{:S(2)}, u32[]{:S(2)}) collective-permute-start(bf16[2,2,272,128]{3,2,1,0:T(8,128)(2,1)S(1)} %get-tuple-element.117), channel_id=1, source_target_pairs={{0,1},{1,2},{2,3},{3,0},{4,5},{5,6},{6,7},{7,4},{8,9},{9,10},{10,1... | collective-permute-start | bytes 835592 | tf_op jit(solution)/shard_map/ppermute | solution.py:234
  150.8 0.7 copy-start.17
  160.1 0.7 copy-start.19
  160.8 11.9 %copy-start.18 = (bf16[2,2,272,128]{3,2,1,0:T(8,128)(2,1)S(1)}, bf16[2,2,272,128]{3,2,1,0:T(8,128)(2,1)}, u32[]{:S(2)}) copy-start(bf16[2,2,272,128]{3,2,1,0:T(8,128)(2,1)} %copy-done.17) | copy-start | bytes 835588
  165.9 0.7 copy-start.21
  166.6 6.0 %copy-start.20 = (bf16[2,2,272,128]{3,2,1,0:T(8,128)(2,1)S(1)}, bf16[2,2,272,128]{3,2,1,0:T(8,128)(2,1)}, u32[]{:S(2)}) copy-start(bf16[2,2,272,128]{3,2,1,0:T(8,128)(2,1)} %copy-done.19) | copy-start | bytes 835588
  166.6 6.0 %copy-start.22 = (bf16[2,2,272,128]{3,2,1,0:T(8,128)(2,1)S(1)}, bf16[2,2,272,128]{3,2,1,0:T(8,128)(2,1)}, u32[]{:S(2)}) copy-start(bf16[2,2,272,128]{3,2,1,0:T(8,128)(2,1)} %copy-done.21) | copy-start | bytes 835588
  166.7 11.4 %collective-permute-start.17 = (bf16[2,2,272,128]{3,2,1,0:T(8,128)(2,1)S(1)}, bf16[2,2,272,128]{3,2,1,0:T(8,128)(2,1)S(1)}, u32[]{:S(2)}, u32[]{:S(2)}) collective-permute-start(bf16[2,2,272,128]{3,2,1,0:T(8,128)(2,1)S(1)} %get-tuple-element.112), channel_id=1, source_target_pairs={{0,3},{1,0},{2,1},{3,2},{4,7},{5,4},{6,5},{7,6},{8,11},{9,8},{10,9... | collective-permute-start | bytes 835592 | tf_op jit(solution)/shard_map/ppermute | solution.py:234
  171.1 17.5 %collective-permute-start.16 = (bf16[2,2,272,128]{3,2,1,0:T(8,128)(2,1)S(1)}, bf16[2,2,272,128]{3,2,1,0:T(8,128)(2,1)S(1)}, u32[]{:S(2)}, u32[]{:S(2)}) collective-permute-start(bf16[2,2,272,128]{3,2,1,0:T(8,128)(2,1)S(1)} %get-tuple-element.113), channel_id=1, source_target_pairs={{0,2},{1,3},{2,0},{3,1},{4,6},{5,7},{6,4},{7,5},{8,10},{9,11},{10,... | collective-permute-start | bytes 835592 | tf_op jit(solution)/shard_map/ppermute | solution.py:234
  171.1 23.4 %collective-permute-start.15 = (bf16[2,2,272,128]{3,2,1,0:T(8,128)(2,1)S(1)}, bf16[2,2,272,128]{3,2,1,0:T(8,128)(2,1)S(1)}, u32[]{:S(2)}, u32[]{:S(2)}) collective-permute-start(bf16[2,2,272,128]{3,2,1,0:T(8,128)(2,1)S(1)} %get-tuple-element.114), channel_id=1, source_target_pairs={{0,1},{1,2},{2,3},{3,0},{4,5},{5,6},{6,7},{7,4},{8,9},{9,10},{10,1... | collective-permute-start | bytes 835592 | tf_op jit(solution)/shard_map/ppermute | solution.py:234

commit v3 on v2

--- a/solution.py
+++ b/solution.py
@@ -27,7 +27,7 @@
     )
 
 
-def pack(table, param_offsets, owner_map, ways, widths, granule, chunks, kinds):
+def pack(table, param_offsets, owner_map, ways, widths, granule, chunks, kinds, waits=()):
     head_count = owner_map.shape[1]
     steps = [widths[kind] // granule for kind in kinds]
     starts = [sum(steps[:i]) for i in range(len(kinds))]
@@ -39,7 +39,7 @@
     ]
 
     def kernel(offsets, owners, source, *refs):
-        targets, taken = refs[:-1], refs[-1]
+        targets, taken = refs[len(waits) : -1], refs[-1]
         for layer in sorted({layer for layers, _ in chunks for layer in layers}):
             for way in range(ways):
                 taken[way] = 0
@@ -72,7 +72,8 @@
             pl.BlockSpec(memory_space=pltpu.SMEM),
             pl.BlockSpec(memory_space=pltpu.SMEM),
             pl.BlockSpec(memory_space=pltpu.VMEM),
-        ],
+        ]
+        + [pl.BlockSpec(memory_space=pl.ANY)] * len(waits),
         out_specs=[pl.BlockSpec(memory_space=pltpu.VMEM)] * len(outs),
         scratch_shapes=[pltpu.SMEM((ways,), jnp.int32)],
         compiler_params=pltpu.CompilerParams(vmem_limit_bytes=VMEM_LIMIT),
@@ -82,7 +83,7 @@
             bytes_accessed=sum(2 * 2 * math.prod(out.shape) for out in outs),
         ),
         name="pack",
-    )(param_offsets, owner_map, table)
+    )(param_offsets, owner_map, table, *waits)
 
 
 def line_step(up, down, axis, ways):
@@ -140,19 +141,18 @@
         q_out, o_out = refs[-2:]
         for d in range(t_ways):
             t = lax.rem(at[0] - d + t_ways, t_ways)
-            for f in range(blocks):
-                q_out[0, 0, f, t] = jnp.dot(
-                    parts[d][f, 0, :q_rows], mats[0, 0, 0], preferred_element_type=jnp.float32
-                ).astype(jnp.bfloat16)
-                o_out[0, 0, f, t] = jnp.dot(
-                    parts[d][f, 0, q_rows:], mats[0, 0, 1], preferred_element_type=jnp.float32
-                ).astype(jnp.bfloat16)
+            q_out[0, 0, 0, t] = jnp.dot(
+                parts[d][0, 0, :q_rows], mats[0, 0, 0], preferred_element_type=jnp.float32
+            ).astype(jnp.bfloat16)
+            o_out[0, 0, 0, t] = jnp.dot(
+                parts[d][0, 0, q_rows:], mats[0, 0, 1], preferred_element_type=jnp.float32
+            ).astype(jnp.bfloat16)
 
     rows = q_rows + o_rows
-    in_specs = [pl.BlockSpec((blocks, 1, rows, LANES), lambda j, at: (at[1], j, 0, 0))]
-    in_specs += [pl.BlockSpec((blocks, 1, rows, LANES), lambda j, at: (0, j, 0, 0))] * len(came)
+    in_specs = [pl.BlockSpec((1, 1, rows, LANES), lambda j, f, at: (at[1] * blocks + f, j, 0, 0))]
+    in_specs += [pl.BlockSpec((1, 1, rows, LANES), lambda j, f, at: (f, j, 0, 0))] * len(came)
     in_specs += [
-        pl.BlockSpec((1, 1) + matrices.shape[2:], lambda j, at: (layer, slots[0] + j, 0, 0, 0))
+        pl.BlockSpec((1, 1) + matrices.shape[2:], lambda j, f, at: (layer, slots[0] + j, 0, 0, 0))
     ]
     args = [own, *came, matrices]
     aliases = {}
@@ -165,11 +165,11 @@
         kernel,
         grid_spec=pltpu.PrefetchScalarGridSpec(
             num_scalar_prefetch=1,
-            grid=(len(slots),),
+            grid=(len(slots), blocks),
             in_specs=in_specs,
             out_specs=[
                 pl.BlockSpec(
-                    (1, 1) + shape.shape[2:], lambda j, at: (layer, slots[0] + j, 0, 0, 0, 0)
+                    (1, 1, 1) + shape.shape[3:], lambda j, f, at: (layer, slots[0] + j, f, 0, 0, 0)
                 )
                 for shape in shapes
             ],
@@ -214,73 +214,71 @@
     me = lax.axis_index("tp")
     slice_row = lax.dynamic_index_in_dim(slice_map, lax.axis_index("fsdp"), 0, keepdims=False)
     blocks = f_ways // t_ways
-
     half = max(1, per_group // 2)
     chunks = [
         (layer, range(at, at + half)) for layer in range(layer_count) for at in range(0, per_group, half)
     ]
-
-    def packed(of, kinds):
-        return pack(table, param_offsets, owner_map, f_ways, widths, granule, of, kinds)
+    shifts = range(1, t_ways)
+    early = [shift for shift in shifts if 2 * shift != t_ways]
+
+    def packed(of, kinds, waits=()):
+        return pack(table, param_offsets, owner_map, f_ways, widths, granule, of, kinds, waits)
 
     def over_fsdp(x):
         return lax.all_to_all(x, "fsdp", split_axis=0, concat_axis=0, tiled=True)
 
-    def over_tp(rows):
-        came = []
-        for shift in range(1, t_ways):
-            block = slice_row[lax.rem(me + shift, t_ways)]
-            piece = lax.dynamic_slice_in_dim(rows, block * blocks, blocks, 0)
-            came.append(lax.ppermute(piece, "tp", [(i, (i + shift) % t_ways) for i in range(t_ways)]))
-        return came
-
     (pairs,) = packed([(range(layer_count), range(per_group))], (KEY, VALUE))
-    to_send = packed([((layer,), slots) for layer, slots in chunks], (QUERY, OUT))
     pairs = over_fsdp(pairs).reshape(f_ways, layer_count, per_group, 2, row_counts[KEY], LANES)
-
-    shapes = tuple(
-        jax.ShapeDtypeStruct(
-            (layer_count, per_group, blocks, t_ways, row_counts[kind], KVR), jnp.bfloat16
-        )
-        for kind in (QUERY, OUT)
-    )
-    where = jnp.stack([me, slice_row[me]])
     up, down = [pairs], [pairs]
-    exchanged, came, rows, outs, matrices = [], None, None, None, None
-    for stage in range(len(chunks) + 2):
-        arriving = over_tp(rows) if rows is not None else None
-        for _ in range(2 if stage == 0 else t_ways):
-            if len(up) < t_ways:
-                above, below = line_step(up[-1], down[-1], "tp", t_ways)
-                up.append(above)
-                down.append(below)
-        following = None
-        if stage < len(chunks):
-            following = over_fsdp(to_send[stage])
-            following = following.reshape(f_ways, len(chunks[stage][1]), rows_total, LANES)
-        if came is not None:
-            exchanged.append((settled, came))
-            if whole_tiles:
-                if matrices is None:
-                    near = [jnp.where(me >= d, up[d], down[t_ways - d]) for d in range(1, t_ways)]
-                    matrices = assemble(me, [pairs] + near)
-                layer, slots = chunks[stage - 2]
-                outs = absorb(where, layer, slots, settled, came, matrices, outs, shapes)
-        arriving, following, up, down, to_send, outs, matrices = lax.optimization_barrier(
-            (arriving, following, up, down, to_send, outs, matrices)
-        )
-        settled, came, rows = rows, arriving, following
+    for _ in shifts:
+        above, below = line_step(up[-1], down[-1], "tp", t_ways)
+        up.append(above)
+        down.append(below)
+
+    targets = jnp.stack([slice_row[lax.rem(me + shift, t_ways)] for shift in range(t_ways)])
+    exchanged, sent = [], []
+    for at, (layer, slots) in enumerate(chunks):
+        waits = [targets]
+        if at >= 1:
+            waits += sent[at - 1] + up[1:3] + down[1:3]
+        if at >= 2:
+            waits += up[3:] + down[3:] + [exchanged[at - 2][1][shift - 1] for shift in early]
+        if at >= 3:
+            waits += exchanged[at - 3][1]
+        (rows,) = packed([((layer,), slots)], (QUERY, OUT), waits)
+        rows = over_fsdp(rows).reshape(f_ways, len(slots), rows_total, LANES)
+        pieces = [
+            lax.dynamic_slice_in_dim(rows, targets[shift] * blocks, blocks, 0) for shift in shifts
+        ]
+        sent.append(pieces)
+        came = [
+            lax.ppermute(piece, "tp", [(i, (i + shift) % t_ways) for i in range(t_ways)])
+            for shift, piece in zip(shifts, pieces)
+        ]
+        exchanged.append((rows, came))
+    near = [jnp.where(me >= d, up[d], down[t_ways - d]) for d in shifts]
+
     if whole_tiles:
+        shapes = tuple(
+            jax.ShapeDtypeStruct(
+                (layer_count, per_group, blocks, t_ways, row_counts[kind], KVR), jnp.bfloat16
+            )
+            for kind in (QUERY, OUT)
+        )
+        where = jnp.stack([me, targets[0]])
+        matrices = assemble(me, [pairs] + near)
+        outs = None
+        for (layer, slots), (rows, came) in zip(chunks, exchanged):
+            outs = absorb(where, layer, slots, rows, came, matrices, outs, shapes)
         return tuple(out.reshape(layer_count, per_group, -1, KVR) for out in outs)
 
-    near = [jnp.where(me >= d, up[d], down[t_ways - d]) for d in range(1, t_ways)]
     order = lax.rem(me - jnp.arange(t_ways, dtype=jnp.int32) + t_ways, jnp.int32(t_ways))
     matrices = jnp.take(jnp.stack([pairs] + near), order, axis=0).transpose(2, 3, 4, 1, 0, 5, 6)
     matrices = matrices.reshape(layer_count, per_group, 2, -1, KVR)
     done = [
         absorb_plain(
             me,
-            lax.dynamic_slice_in_dim(rows, slice_row[me] * blocks, blocks, 0),
+            lax.dynamic_slice_in_dim(rows, targets[0] * blocks, blocks, 0),
             came,
             matrices[layer, slots[0] : slots[-1] + 1],
         )

time: 201 us -> 230 us (1.14)
  the two profiles are of different devices: /device:TPU:10 before, /device:TPU:0 now
where the time goes in v3:
time: 230 us; the launch traced here: 228 us
  waiting for transfers between devices  78.3 us (34%)
  starting transfers between devices  74.9 us (33%)
  Pallas kernels  32.4 us (14%)
  local copies, waits for them, and re-layouts  31.8 us (14%)
  other arithmetic  7.15 us (3%)
  between operations  3.09 us (1%)
    ppermute x12, waiting for transfers between devices, per_device(): lax.ppermute(piece, 'tp', [(i, (i + shift) % t_ways) for i in range(t_way...  37.1 us
    ppermute x12, starting transfers between devices, per_device(): lax.ppermute(piece, 'tp', [(i, (i + shift) % t_ways) for i in range(t_way...  35.5 us
    unnamed x90, local copies, waits for them, and re-layouts  28.1 us
    all_to_all x5, waiting for transfers between devices, over_fsdp(): return lax.all_to_all(x, 'fsdp', split_axis=0, concat_axis=0, tiled=True)  23.3 us
    pallas_call x4, Pallas kernels, absorb(): pl.pallas_call(kernel, grid_spec=pltpu.PrefetchScalarGridSpec(num_scalar_...  20.8 us
    all_to_all x5, starting transfers between devices, over_fsdp(): return lax.all_to_all(x, 'fsdp', split_axis=0, concat_axis=0, tiled=True)  20.6 us
    ppermute x3, waiting for transfers between devices, line_step(): lax.ppermute(down, axis, [(i + 1, i) for i in range(ways - 1)])  17.5 us
    ppermute x3, starting transfers between devices, line_step(): lax.ppermute(up, axis, [(i, i + 1) for i in range(ways - 1)])  15 us
  transfers between devices with their start and end apart: 23, of which 14 were waited for; matrix products, arithmetic and copies ran while one was open for 5% of the time, Pallas kernels for 9%

profile of v3, /device:TPU:0, one launch (start us, length us, event | category | flops | bytes accessed | tf_op | source)
XLA Modules:
  0.0 227.7 jit_solution(9682725531604359752)
XLA Ops:
  0.6 0.8 copy.16.offsets
  1.4 3.1 %copy.17 = bf16[1,2,9728,128]{3,2,1,0:T(8,128)(2,1)S(1)} copy(bf16[1,2,9728,128]{3,1,2,0:T(2,128)(2,1)} %bitcast.30) | data formatting | bytes 9961472
  4.6 2.9 %pack.6 = bf16[8,2,4,2,16,128]{5,4,3,2,1,0:T(8,128)(2,1)} custom-call(s32[2,32,4]{2,1,0:T(8,128)S(1)} %copy.16.offsets, s32[2,32]{1,0:T(2,128)S(1)} %copy-done.37, bf16[2,608,16,128]{3,2,1,0:T(8,128)(2,1)S(1)} %bitcast.17), custom_call_target="tpu_custom_call" | custom-call | bytes 1048576 | tf_op jit(solution)/shard_map/pack/pallas_call | solution.py:68
  7.5 2.3 copy-done
  9.7 5.3 %all-to-all-start.1 = ((bf16[8,2,4,2,16,128]{5,4,3,2,1,0:T(8,128)(2,1)}), bf16[8,2,4,2,16,128]{5,4,3,2,1,0:T(8,128)(2,1)S(1)}, u32[]{:S(2)}, u32[]{:S(2)}) async-start(bf16[8,2,4,2,16,128]{5,4,3,2,1,0:T(8,128)(2,1)} %pack.6), calls=%async_computation.1 | async-start | bytes 1048576 | tf_op jit(solution)/shard_map/all_to_all | solution.py:228
  15.7 2.6 %pad_add_fusion.1.refs_0_ = s32[4]{0:T(128)S(1)} fusion(s32[1]{0:T(128)} %bitcast.4, s32[1]{0:T(128)} %bitcast.3, s32[1]{0:T(128)} %bitcast.2, s32[1]{0:T(128)} %bitcast.1), kind=kLoop, calls=%fused_computation.16 | loop fusion | flops 12 | bytes 32 | tf_op jit(solution)/shard_map/stack | solution.py:238
  18.3 2.4 %copy-done.1 = bf16[1,2,9728,128]{3,2,1,0:T(8,128)(2,1)S(1)} copy-done((bf16[1,2,9728,128]{3,2,1,0:T(8,128)(2,1)S(1)}, bf16[1,2,9728,128]{3,2,1,0:T(8,128)(2,1)}, u32[]{:S(2)}) %copy-start.1) | copy-done | bytes 4980760
  20.8 2.6 %pack.5 = bf16[8,1,2,17,16,128]{5,4,3,2,1,0:T(8,128)(2,1)} custom-call(s32[2,32,4]{2,1,0:T(8,128)S(1)} %copy.16.offsets, s32[2,32]{1,0:T(2,128)S(1)} %copy-done.37, bf16[2,608,16,128]{3,2,1,0:T(8,128)(2,1)S(1)} %bitcast.18, s32[4]{0:T(128)S(1)} %pad_add_fusion.1.refs_0_), custom_call_target="tpu_custom_call" | custom-call | bytes 2228224 | tf_op jit(solution)/shard_map/pack/pallas_call | solution.py:68
  23.4 1.4 all-to-all-done.1.refs_0_
  24.8 3.6 %all-to-all-start = ((bf16[8,1,2,17,16,128]{5,4,3,2,1,0:T(8,128)(2,1)}), bf16[8,1,2,17,16,128]{5,4,3,2,1,0:T(8,128)(2,1)S(1)}, u32[]{:S(2)}, u32[]{:S(2)}) async-start(bf16[8,1,2,17,16,128]{5,4,3,2,1,0:T(8,128)(2,1)} %pack.5), calls=%async_computation | async-start | bytes 2228224 | tf_op jit(solution)/shard_map/all_to_all | solution.py:228
  28.4 1.3 collective-permute-start.2
  29.7 4.6 %collective-permute-start = (bf16[8,2,4,2,16,128]{5,4,3,2,1,0:T(8,128)(2,1)S(1)}, bf16[8,2,4,2,16,128]{5,4,3,2,1,0:T(8,128)(2,1)S(1)}, u32[]{:S(2)}, u32[]{:S(2)}) collective-permute-start(bf16[8,2,4,2,16,128]{5,4,3,2,1,0:T(8,128)(2,1)S(1)} %all-to-all-done.1.refs_0_), channel_id=1, source_target_pairs={{0,1},{1,2},{2,3},{4,5},{5,6},{6,7},{8,9},{9,10},{10,11},{12,13},{... | collective-permute-start | bytes 1572872 | tf_op jit(solution)/shard_map/ppermute | solution.py:91
  34.3 10.2 %collective-permute-done.2.refs_6_ = bf16[8,2,4,2,16,128]{5,4,3,2,1,0:T(8,128)(2,1)S(1)} collective-permute-done((bf16[8,2,4,2,16,128]{5,4,3,2,1,0:T(8,128)(2,1)S(1)}, bf16[8,2,4,2,16,128]{5,4,3,2,1,0:T(8,128)(2,1)S(1)}, u32[]{:S(2)}, u32[]{:S(2)}) %collective-permute-start.2) | collective-permute-done | bytes 524320 | tf_op jit(solution)/shard_map/ppermute | solution.py:92
  44.5 1.3 collective-permute-start.3
  45.8 4.6 %collective-permute-start.1 = (bf16[8,2,4,2,16,128]{5,4,3,2,1,0:T(8,128)(2,1)S(1)}, bf16[8,2,4,2,16,128]{5,4,3,2,1,0:T(8,128)(2,1)S(1)}, u32[]{:S(2)}, u32[]{:S(2)}) collective-permute-start(bf16[8,2,4,2,16,128]{5,4,3,2,1,0:T(8,128)(2,1)S(1)} %collective-permute-done.refs_4_), channel_id=1, source_target_pairs={{0,1},{1,2},{2,3},{4,5},{5,6},{6,7},{8,9},{9,10},{10,11},{12,13},{... | collective-permute-start | bytes 1572872 | tf_op jit(solution)/shard_map/ppermute | solution.py:91
  52.5 7.3 %collective-permute-done.3.refs_7_ = bf16[8,2,4,2,16,128]{5,4,3,2,1,0:T(8,128)(2,1)S(1)} collective-permute-done((bf16[8,2,4,2,16,128]{5,4,3,2,1,0:T(8,128)(2,1)S(1)}, bf16[8,2,4,2,16,128]{5,4,3,2,1,0:T(8,128)(2,1)S(1)}, u32[]{:S(2)}, u32[]{:S(2)}) %collective-permute-start.3) | collective-permute-done | bytes 524320 | tf_op jit(solution)/shard_map/ppermute | solution.py:92
  59.7 0.8 copy-done.11
  60.9 0.8 copy-done.15
  61.8 2.4 %copy-done.2 = bf16[1,2,9728,128]{3,2,1,0:T(8,128)(2,1)S(1)} copy-done((bf16[1,2,9728,128]{3,2,1,0:T(8,128)(2,1)S(1)}, bf16[1,2,9728,128]{3,2,1,0:T(8,128)(2,1)}, u32[]{:S(2)}) %copy-start.2) | copy-done | bytes 4980760
  64.2 1.0 copy-done.12
  65.2 1.0 copy-done.16
  66.3 1.6 pack.7
  67.9 1.0 copy-done.20
  68.9 0.7 copy-done.32
  69.6 0.7 copy-done.35
  71.0 3.6 %all-to-all-start.2 = ((bf16[8,1,2,17,16,128]{5,4,3,2,1,0:T(8,128)(2,1)}), bf16[8,1,2,17,16,128]{5,4,3,2,1,0:T(8,128)(2,1)S(1)}, u32[]{:S(2)}, u32[]{:S(2)}) async-start(bf16[8,1,2,17,16,128]{5,4,3,2,1,0:T(8,128)(2,1)} %copy-done.20), calls=%async_computation.2 | async-start | bytes 2228224 | tf_op jit(solution)/shard_map/all_to_all | solution.py:228
  74.6 1.3 collective-permute-start.5
  75.9 5.8 %collective-permute-start.4 = (bf16[8,2,4,2,16,128]{5,4,3,2,1,0:T(8,128)(2,1)}, bf16[8,2,4,2,16,128]{5,4,3,2,1,0:T(8,128)(2,1)}, u32[]{:S(2)}, u32[]{:S(2)}) collective-permute-start(bf16[8,2,4,2,16,128]{5,4,3,2,1,0:T(8,128)(2,1)} %copy-done.15), channel_id=1, source_target_pairs={{0,1},{1,2},{2,3},{4,5},{5,6},{6,7},{8,9},{9,10},{10,11},{12,13},{... | collective-permute-start | bytes 1572872 | tf_op jit(solution)/shard_map/ppermute | solution.py:91
  81.7 1.9 collective-permute-start.7
  83.8 7.0 %all-to-all-done.2 = bf16[8,1,2,17,16,128]{5,4,3,2,1,0:T(8,128)(2,1)S(1)} async-done(((bf16[8,1,2,17,16,128]{5,4,3,2,1,0:T(8,128)(2,1)}), bf16[8,1,2,17,16,128]{5,4,3,2,1,0:T(8,128)(2,1)S(1)}, u32[]{:S(2)}, u32[]{:S(2)}) %all-to-all-start.2) | async-done | bytes 1114144 | tf_op jit(solution)/shard_map/all_to_all | solution.py:228
  90.8 0.8 constant_dynamic-slice_fusion.6
  91.6 7.9 %collective-permute-done.7.refs_11_.refs_14_.refs_3_ = bf16[2,2,272,128]{3,2,1,0:T(8,128)(2,1)S(1)} collective-permute-done((bf16[2,2,272,128]{3,2,1,0:T(8,128)(2,1)}, bf16[2,2,272,128]{3,2,1,0:T(8,128)(2,1)S(1)}, u32[]{:S(2)}, u32[]{:S(2)}) %collective-permute-start.7) | collective-permute-done | bytes 278560 | tf_op jit(solution)/shard_map/ppermute | solution.py:255
  99.5 6.5 %collective-permute-done.6.refs_10_.refs_12_.refs_1_ = bf16[2,2,272,128]{3,2,1,0:T(8,128)(2,1)} collective-permute-done((bf16[2,2,272,128]{3,2,1,0:T(8,128)(2,1)}, bf16[2,2,272,128]{3,2,1,0:T(8,128)(2,1)}, u32[]{:S(2)}, u32[]{:S(2)}) %collective-permute-start.6) | collective-permute-done | bytes 278560 | tf_op jit(solution)/shard_map/ppermute | solution.py:255
  106.1 2.4 %copy-done.3 = bf16[1,2,9728,128]{3,2,1,0:T(8,128)(2,1)S(1)} copy-done((bf16[1,2,9728,128]{3,2,1,0:T(8,128)(2,1)S(1)}, bf16[1,2,9728,128]{3,2,1,0:T(8,128)(2,1)}, u32[]{:S(2)}) %copy-start.3) | copy-done | bytes 4980760
  108.5 1.7 pack.8
  110.2 1.0 copy-done.21
  111.2 0.7 copy-done.33
  112.6 3.8 %all-to-all-start.3 = ((bf16[8,1,2,17,16,128]{5,4,3,2,1,0:T(8,128)(2,1)}), bf16[8,1,2,17,16,128]{5,4,3,2,1,0:T(8,128)(2,1)S(1)}, u32[]{:S(2)}, u32[]{:S(2)}) async-start(bf16[8,1,2,17,16,128]{5,4,3,2,1,0:T(8,128)(2,1)} %copy-done.21), calls=%async_computation.3 | async-start | bytes 2228224 | tf_op jit(solution)/shard_map/all_to_all | solution.py:228
  116.5 2.7 %collective-permute-start.10 = (bf16[2,2,272,128]{3,2,1,0:T(8,128)(2,1)}, bf16[2,2,272,128]{3,2,1,0:T(8,128)(2,1)}, u32[]{:S(2)}, u32[]{:S(2)}) collective-permute-start(bf16[2,2,272,128]{3,2,1,0:T(8,128)(2,1)} %copy-done.32), channel_id=1, source_target_pairs={{0,2},{1,3},{2,0},{3,1},{4,6},{5,7},{6,4},{7,5},{8,10},{9,11},{10,... | collective-permute-start | bytes 835592 | tf_op jit(solution)/shard_map/ppermute | solution.py:255
  119.2 1.9 collective-permute-start.9
  121.6 11.0 %all-to-all-done.3 = bf16[8,1,2,17,16,128]{5,4,3,2,1,0:T(8,128)(2,1)S(1)} async-done(((bf16[8,1,2,17,16,128]{5,4,3,2,1,0:T(8,128)(2,1)}), bf16[8,1,2,17,16,128]{5,4,3,2,1,0:T(8,128)(2,1)S(1)}, u32[]{:S(2)}, u32[]{:S(2)}) %all-to-all-start.3) | async-done | bytes 1114144 | tf_op jit(solution)/shard_map/all_to_all | solution.py:228
  132.6 0.9 constant_dynamic-slice_fusion.3
  133.5 7.2 %collective-permute-done.8.refs_10_.refs_1_ = bf16[2,2,272,128]{3,2,1,0:T(8,128)(2,1)} collective-permute-done((bf16[2,2,272,128]{3,2,1,0:T(8,128)(2,1)}, bf16[2,2,272,128]{3,2,1,0:T(8,128)(2,1)}, u32[]{:S(2)}, u32[]{:S(2)}) %collective-permute-start.8) | collective-permute-done | bytes 278560 | tf_op jit(solution)/shard_map/ppermute | solution.py:255
  140.8 2.4 %copy-done.4 = bf16[1,2,9728,128]{3,2,1,0:T(8,128)(2,1)S(1)} copy-done((bf16[1,2,9728,128]{3,2,1,0:T(8,128)(2,1)S(1)}, bf16[1,2,9728,128]{3,2,1,0:T(8,128)(2,1)}, u32[]{:S(2)}) %copy-start.4) | copy-done | bytes 4980760
  143.2 1.0 copy-done.18
  144.3 1.0 copy-done.23
  145.2 1.7 pack.9
  146.9 1.0 copy-done.19
  147.9 4.3 %all-to-all-start.4 = ((bf16[8,1,2,17,16,128]{5,4,3,2,1,0:T(8,128)(2,1)}), bf16[8,1,2,17,16,128]{5,4,3,2,1,0:T(8,128)(2,1)}, u32[]{:S(2)}, u32[]{:S(2)}) async-start(bf16[8,1,2,17,16,128]{5,4,3,2,1,0:T(8,128)(2,1)} %copy-done.19), calls=%async_computation.4 | async-start | bytes 2228224 | tf_op jit(solution)/shard_map/all_to_all | solution.py:228
  152.9 1.9 broadcast_select_fusion.1.refs_2_
  154.8 6.7 %collective-permute-start.17 = (bf16[2,2,272,128]{3,2,1,0:T(8,128)(2,1)}, bf16[2,2,272,128]{3,2,1,0:T(8,128)(2,1)}, u32[]{:S(2)}, u32[]{:S(2)}) collective-permute-start(bf16[2,2,272,128]{3,2,1,0:T(8,128)(2,1)} %get-tuple-element.25.refs_2_), channel_id=1, source_target_pairs={{0,2},{1,3},{2,0},{3,1},{4,6},{5,7},{6,4},{7,5},{8,10},{9,11},{10,... | collective-permute-start | bytes 835592 | tf_op jit(solution)/shard_map/ppermute | solution.py:255
  161.9 1.9 broadcast_select_fusion.2.refs_1_
  164.4 3.9 %all-to-all-done.4 = bf16[8,1,2,17,16,128]{5,4,3,2,1,0:T(8,128)(2,1)} async-done(((bf16[8,1,2,17,16,128]{5,4,3,2,1,0:T(8,128)(2,1)}), bf16[8,1,2,17,16,128]{5,4,3,2,1,0:T(8,128)(2,1)}, u32[]{:S(2)}, u32[]{:S(2)}) %all-to-all-start.4) | async-done | bytes 1114144 | tf_op jit(solution)/shard_map/all_to_all | solution.py:228
  168.3 1.2 constant_dynamic-slice_fusion
  169.6 2.8 %collective-permute-start.13 = (bf16[2,2,272,128]{3,2,1,0:T(8,128)(2,1)S(1)}, bf16[2,2,272,128]{3,2,1,0:T(8,128)(2,1)S(1)}, u32[]{:S(2)}, u32[]{:S(2)}) collective-permute-start(bf16[2,2,272,128]{3,2,1,0:T(8,128)(2,1)S(1)} %get-tuple-element.18), channel_id=1, source_target_pairs={{0,3},{1,0},{2,1},{3,2},{4,7},{5,4},{6,5},{7,6},{8,11},{9,8},{10,9... | collective-permute-start | bytes 835592 | tf_op jit(solution)/shard_map/ppermute | solution.py:255
  172.4 3.4 %collective-permute-done.17.refs_2_ = bf16[2,2,272,128]{3,2,1,0:T(8,128)(2,1)} collective-permute-done((bf16[2,2,272,128]{3,2,1,0:T(8,128)(2,1)}, bf16[2,2,272,128]{3,2,1,0:T(8,128)(2,1)}, u32[]{:S(2)}, u32[]{:S(2)}) %collective-permute-start.17) | collective-permute-done | bytes 278560 | tf_op jit(solution)/shard_map/ppermute | solution.py:255
  177.0 17.2 %collective-permute-start.11 = (bf16[2,2,272,128]{3,2,1,0:T(8,128)(2,1)S(1)}, bf16[2,2,272,128]{3,2,1,0:T(8,128)(2,1)S(1)}, u32[]{:S(2)}, u32[]{:S(2)}) collective-permute-start(bf16[2,2,272,128]{3,2,1,0:T(8,128)(2,1)S(1)} %get-tuple-element.20), channel_id=1, source_target_pairs={{0,1},{1,2},{2,3},{3,0},{4,5},{5,6},{6,7},{7,4},{8,9},{9,10},{10,1... | collective-permute-start | bytes 835592 | tf_op jit(solution)/shard_map/ppermute | solution.py:255
  194.4 1.2 assemble.1.refs_4_
  195.6 5.2 %absorb.4 = (bf16[2,4,2,4,48,512]{5,4,3,2,1,0:T(8,128)(2,1)}, bf16[2,4,2,4,224,512]{5,4,3,2,1,0:T(8,128)(2,1)}) custom-call(s32[2]{0:T(128)S(1)} %pad_add_fusion.at, bf16[8,2,272,128]{3,2,1,0:T(8,128)(2,1)S(1)} %bitcast.23, bf16[2,2,272,128]{3,2,1,0:T(8,128)(2,1)} %collective-permute-done.6.refs_10_.refs_12_.refs_1_, ...), custom_call_target="tpu_custom_call" | custom-call | flops 570425344 | bytes 5570560 | tf_op jit(solution)/shard_map/absorb/pallas_call | solution.py:164
  200.8 5.2 %absorb.5 = (bf16[2,4,2,4,48,512]{5,4,3,2,1,0:T(8,128)(2,1)}, bf16[2,4,2,4,224,512]{5,4,3,2,1,0:T(8,128)(2,1)}) custom-call(s32[2]{0:T(128)S(1)} %pad_add_fusion.at, bf16[8,2,272,128]{3,2,1,0:T(8,128)(2,1)S(1)} %bitcast.25, bf16[2,2,272,128]{3,2,1,0:T(8,128)(2,1)} %collective-permute-done.8.refs_10_.refs_1_, ...), custom_call_target="tpu_custom_call", output_to_operand_aliasing={{0}: (6, {}), {1}: (7, {})} | custom-call | flops 570425344 | bytes 5570560 | tf_op jit(solution)/shard_map/absorb/pallas_call | solution.py:164
  206.0 5.0 %collective-permute-done.15.refs_2_ = bf16[2,2,272,128]{3,2,1,0:T(8,128)(2,1)} collective-permute-done((bf16[2,2,272,128]{3,2,1,0:T(8,128)(2,1)}, bf16[2,2,272,128]{3,2,1,0:T(8,128)(2,1)}, u32[]{:S(2)}, u32[]{:S(2)}) %collective-permute-start.15) | collective-permute-done | bytes 278560 | tf_op jit(solution)/shard_map/ppermute | solution.py:255
  211.1 5.2 %absorb.6 = (bf16[2,4,2,4,48,512]{5,4,3,2,1,0:T(8,128)(2,1)}, bf16[2,4,2,4,224,512]{5,4,3,2,1,0:T(8,128)(2,1)}) custom-call(s32[2]{0:T(128)S(1)} %pad_add_fusion.at, bf16[8,2,272,128]{3,2,1,0:T(8,128)(2,1)S(1)} %bitcast.27, bf16[2,2,272,128]{3,2,1,0:T(8,128)(2,1)} %collective-permute-done.14.refs_1_, ...), custom_call_target="tpu_custom_call", output_to_operand_aliasing={{0}: (6, {}), {1}: (7, {})} | custom-call | flops 570425344 | bytes 5570560 | tf_op jit(solution)/shard_map/absorb/pallas_call | solution.py:164
  216.3 6.3 %collective-permute-done.12.refs_2_ = bf16[2,2,272,128]{3,2,1,0:T(8,128)(2,1)S(1)} collective-permute-done((bf16[2,2,272,128]{3,2,1,0:T(8,128)(2,1)S(1)}, bf16[2,2,272,128]{3,2,1,0:T(8,128)(2,1)S(1)}, u32[]{:S(2)}, u32[]{:S(2)}) %collective-permute-start.12) | collective-permute-done | bytes 278560 | tf_op jit(solution)/shard_map/ppermute | solution.py:255
  222.6 5.1 %absorb.7 = (bf16[2,4,2,4,48,512]{5,4,3,2,1,0:T(8,128)(2,1)}, bf16[2,4,2,4,224,512]{5,4,3,2,1,0:T(8,128)(2,1)}) custom-call(s32[2]{0:T(128)S(1)} %pad_add_fusion.at, bf16[8,2,272,128]{3,2,1,0:T(8,128)(2,1)} %bitcast.11.refs_0_, bf16[2,2,272,128]{3,2,1,0:T(8,128)(2,1)S(1)} %collective-permute-done.11.refs_1_, ...), custom_call_target="tpu_custom_call", output_to_operand_aliasing={{0}: (6, {}), {1}: (7, {})} | custom-call | flops 570425344 | bytes 5570560 | tf_op jit(solution)/shard_map/absorb/pallas_call | solution.py:164
  (92 shorter events, 6.3 us)
Async XLA Ops:
  1.4 60.3 %copy-start.29 = (s32[2,32,4]{2,1,0:T(8,128)}, s32[2,32,4]{2,1,0:T(8,128)S(1)}, u32[]{:S(2)}) copy-start(s32[2,32,4]{2,1,0:T(8,128)S(1)} %copy.16.offsets) | copy-start | bytes 3076
  1.4 3.2 %copy-start.37 = (s32[2,32]{1,0:T(2,128)S(1)}, s32[2,32]{1,0:T(2,128)}, u32[]{:S(2)}) copy-start(s32[2,32]{1,0:T(2,128)} %owners.9) | copy-start | bytes 772
  7.5 2.3 copy-start
  9.7 5.3 %copy-start.43 = (s32[8,4]{0,1:T(4,128)S(1)}, s32[8,4]{0,1:T(4,128)}, u32[]{:S(2)}) copy-start(s32[8,4]{0,1:T(4,128)} %param.7) | copy-start | bytes 388
  9.7 15.0 %all-to-all-start.1 = ((bf16[8,2,4,2,16,128]{5,4,3,2,1,0:T(8,128)(2,1)}), bf16[8,2,4,2,16,128]{5,4,3,2,1,0:T(8,128)(2,1)S(1)}, u32[]{:S(2)}, u32[]{:S(2)}) async-start(bf16[8,2,4,2,16,128]{5,4,3,2,1,0:T(8,128)(2,1)} %pack.6), calls=%async_computation.1 | async-start | bytes 1048576 | tf_op jit(solution)/shard_map/all_to_all | solution.py:228
  18.3 2.4 %copy-start.1 = (bf16[1,2,9728,128]{3,2,1,0:T(8,128)(2,1)S(1)}, bf16[1,2,9728,128]{3,2,1,0:T(8,128)(2,1)}, u32[]{:S(2)}) copy-start(bf16[1,2,9728,128]{3,2,1,0:T(8,128)(2,1)} %copy-done) | copy-start | bytes 14942212
  20.8 41.0 %copy-start.40 = (s32[4]{0:T(128)}, s32[4]{0:T(128)S(1)}, u32[]{:S(2)}) copy-start(s32[4]{0:T(128)S(1)} %pad_add_fusion.1.refs_0_) | copy-start | bytes 52
  24.8 4.9 %copy-start.25 = (bf16[8,2,4,2,16,128]{5,4,3,2,1,0:T(8,128)(2,1)}, bf16[8,2,4,2,16,128]{5,4,3,2,1,0:T(8,128)(2,1)S(1)}, u32[]{:S(2)}) copy-start(bf16[8,2,4,2,16,128]{5,4,3,2,1,0:T(8,128)(2,1)S(1)} %all-to-all-done.1.refs_0_) | copy-start | bytes 1572868
  24.8 27.6 %all-to-all-start = ((bf16[8,1,2,17,16,128]{5,4,3,2,1,0:T(8,128)(2,1)}), bf16[8,1,2,17,16,128]{5,4,3,2,1,0:T(8,128)(2,1)S(1)}, u32[]{:S(2)}, u32[]{:S(2)}) async-start(bf16[8,1,2,17,16,128]{5,4,3,2,1,0:T(8,128)(2,1)} %pack.5), calls=%async_computation | async-start | bytes 2228224 | tf_op jit(solution)/shard_map/all_to_all | solution.py:228
  28.4 16.1 %collective-permute-start.2 = (bf16[8,2,4,2,16,128]{5,4,3,2,1,0:T(8,128)(2,1)S(1)}, bf16[8,2,4,2,16,128]{5,4,3,2,1,0:T(8,128)(2,1)S(1)}, u32[]{:S(2)}, u32[]{:S(2)}) collective-permute-start(bf16[8,2,4,2,16,128]{5,4,3,2,1,0:T(8,128)(2,1)S(1)} %all-to-all-done.1.refs_0_), channel_id=1, source_target_pairs={{1,0},{2,1},{3,2},{5,4},{6,5},{7,6},{9,8},{10,9},{11,10},{13,12},{... | collective-permute-start | bytes 1572872 | tf_op jit(solution)/shard_map/ppermute | solution.py:92
  29.7 16.1 %collective-permute-start = (bf16[8,2,4,2,16,128]{5,4,3,2,1,0:T(8,128)(2,1)S(1)}, bf16[8,2,4,2,16,128]{5,4,3,2,1,0:T(8,128)(2,1)S(1)}, u32[]{:S(2)}, u32[]{:S(2)}) collective-permute-start(bf16[8,2,4,2,16,128]{5,4,3,2,1,0:T(8,128)(2,1)S(1)} %all-to-all-done.1.refs_0_), channel_id=1, source_target_pairs={{0,1},{1,2},{2,3},{4,5},{5,6},{6,7},{8,9},{9,10},{10,11},{12,13},{... | collective-permute-start | bytes 1572872 | tf_op jit(solution)/shard_map/ppermute | solution.py:91
  44.5 61.6 %copy-start.5 = (bf16[8,2,4,2,16,128]{5,4,3,2,1,0:T(8,128)(2,1)}, bf16[8,2,4,2,16,128]{5,4,3,2,1,0:T(8,128)(2,1)S(1)}, u32[]{:S(2)}) copy-start(bf16[8,2,4,2,16,128]{5,4,3,2,1,0:T(8,128)(2,1)S(1)} %collective-permute-done.2.refs_6_) | copy-start | bytes 1572868
  44.5 15.3 %collective-permute-start.3 = (bf16[8,2,4,2,16,128]{5,4,3,2,1,0:T(8,128)(2,1)S(1)}, bf16[8,2,4,2,16,128]{5,4,3,2,1,0:T(8,128)(2,1)S(1)}, u32[]{:S(2)}, u32[]{:S(2)}) collective-permute-start(bf16[8,2,4,2,16,128]{5,4,3,2,1,0:T(8,128)(2,1)S(1)} %collective-permute-done.2.refs_6_), channel_id=1, source_target_pairs={{1,0},{2,1},{3,2},{5,4},{6,5},{7,6},{9,8},{10,9},{11,10},{13,12},{... | collective-permute-start | bytes 1572872 | tf_op jit(solution)/shard_map/ppermute | solution.py:92
  45.8 60.3 %copy-start.8 = (bf16[8,2,4,2,16,128]{5,4,3,2,1,0:T(8,128)(2,1)}, bf16[8,2,4,2,16,128]{5,4,3,2,1,0:T(8,128)(2,1)S(1)}, u32[]{:S(2)}) copy-start(bf16[8,2,4,2,16,128]{5,4,3,2,1,0:T(8,128)(2,1)S(1)} %collective-permute-done.refs_4_) | copy-start | bytes 1572868
  45.8 15.2 %collective-permute-start.1 = (bf16[8,2,4,2,16,128]{5,4,3,2,1,0:T(8,128)(2,1)S(1)}, bf16[8,2,4,2,16,128]{5,4,3,2,1,0:T(8,128)(2,1)S(1)}, u32[]{:S(2)}, u32[]{:S(2)}) collective-permute-start(bf16[8,2,4,2,16,128]{5,4,3,2,1,0:T(8,128)(2,1)S(1)} %collective-permute-done.refs_4_), channel_id=1, source_target_pairs={{0,1},{1,2},{2,3},{4,5},{5,6},{6,7},{8,9},{9,10},{10,11},{12,13},{... | collective-permute-start | bytes 1572872 | tf_op jit(solution)/shard_map/ppermute | solution.py:91
  59.7 0.8 copy-start.11
  60.9 0.8 copy-start.15
  61.8 2.4 %copy-start.2 = (bf16[1,2,9728,128]{3,2,1,0:T(8,128)(2,1)S(1)}, bf16[1,2,9728,128]{3,2,1,0:T(8,128)(2,1)}, u32[]{:S(2)}) copy-start(bf16[1,2,9728,128]{3,2,1,0:T(8,128)(2,1)} %copy-done) | copy-start | bytes 14942212
  64.2 1.0 copy-start.12
  65.2 1.0 copy-start.16
  67.9 1.0 copy-start.20
  69.6 0.7 copy-start.35
  71.0 19.7 %all-to-all-start.2 = ((bf16[8,1,2,17,16,128]{5,4,3,2,1,0:T(8,128)(2,1)}), bf16[8,1,2,17,16,128]{5,4,3,2,1,0:T(8,128)(2,1)S(1)}, u32[]{:S(2)}, u32[]{:S(2)}) async-start(bf16[8,1,2,17,16,128]{5,4,3,2,1,0:T(8,128)(2,1)} %copy-done.20), calls=%async_computation.2 | async-start | bytes 2228224 | tf_op jit(solution)/shard_map/all_to_all | solution.py:228
  74.6 31.4 %collective-permute-start.5 = (bf16[8,2,4,2,16,128]{5,4,3,2,1,0:T(8,128)(2,1)}, bf16[8,2,4,2,16,128]{5,4,3,2,1,0:T(8,128)(2,1)}, u32[]{:S(2)}, u32[]{:S(2)}) collective-permute-start(bf16[8,2,4,2,16,128]{5,4,3,2,1,0:T(8,128)(2,1)} %copy-done.11), channel_id=1, source_target_pairs={{1,0},{2,1},{3,2},{5,4},{6,5},{7,6},{9,8},{10,9},{11,10},{13,12},{... | collective-permute-start | bytes 1572872 | tf_op jit(solution)/shard_map/ppermute | solution.py:92
  75.9 30.1 %collective-permute-start.4 = (bf16[8,2,4,2,16,128]{5,4,3,2,1,0:T(8,128)(2,1)}, bf16[8,2,4,2,16,128]{5,4,3,2,1,0:T(8,128)(2,1)}, u32[]{:S(2)}, u32[]{:S(2)}) collective-permute-start(bf16[8,2,4,2,16,128]{5,4,3,2,1,0:T(8,128)(2,1)} %copy-done.15), channel_id=1, source_target_pairs={{0,1},{1,2},{2,3},{4,5},{5,6},{6,7},{8,9},{9,10},{10,11},{12,13},{... | collective-permute-start | bytes 1572872 | tf_op jit(solution)/shard_map/ppermute | solution.py:91
  81.7 17.8 %collective-permute-start.7 = (bf16[2,2,272,128]{3,2,1,0:T(8,128)(2,1)}, bf16[2,2,272,128]{3,2,1,0:T(8,128)(2,1)S(1)}, u32[]{:S(2)}, u32[]{:S(2)}) collective-permute-start(bf16[2,2,272,128]{3,2,1,0:T(8,128)(2,1)} %copy-done.36), channel_id=1, source_target_pairs={{0,3},{1,0},{2,1},{3,2},{4,7},{5,4},{6,5},{7,6},{8,11},{9,8},{10,9... | collective-permute-start | bytes 835592 | tf_op jit(solution)/shard_map/ppermute | solution.py:255
  83.7 22.4 %collective-permute-start.6 = (bf16[2,2,272,128]{3,2,1,0:T(8,128)(2,1)}, bf16[2,2,272,128]{3,2,1,0:T(8,128)(2,1)}, u32[]{:S(2)}, u32[]{:S(2)}) collective-permute-start(bf16[2,2,272,128]{3,2,1,0:T(8,128)(2,1)} %copy-done.35), channel_id=1, source_target_pairs={{0,1},{1,2},{2,3},{3,0},{4,5},{5,6},{6,7},{7,4},{8,9},{9,10},{10,1... | collective-permute-start | bytes 835592 | tf_op jit(solution)/shard_map/ppermute | solution.py:255
  90.8 15.3 %copy-start.13 = (bf16[8,2,4,2,16,128]{5,4,3,2,1,0:T(8,128)(2,1)S(1)}, bf16[8,2,4,2,16,128]{5,4,3,2,1,0:T(8,128)(2,1)}, u32[]{:S(2)}) copy-start(bf16[8,2,4,2,16,128]{5,4,3,2,1,0:T(8,128)(2,1)} %copy-done.11) | copy-start | bytes 1572868
  90.8 15.3 %copy-start.17 = (bf16[8,2,4,2,16,128]{5,4,3,2,1,0:T(8,128)(2,1)S(1)}, bf16[8,2,4,2,16,128]{5,4,3,2,1,0:T(8,128)(2,1)}, u32[]{:S(2)}) copy-start(bf16[8,2,4,2,16,128]{5,4,3,2,1,0:T(8,128)(2,1)} %copy-done.15) | copy-start | bytes 1572868
  90.8 15.3 %copy-start.30 = (s32[2,32,4]{2,1,0:T(8,128)S(1)}, s32[2,32,4]{2,1,0:T(8,128)}, u32[]{:S(2)}) copy-start(s32[2,32,4]{2,1,0:T(8,128)} %copy-done.29) | copy-start | bytes 3076
  90.8 15.3 %copy-start.38 = (s32[2,32]{1,0:T(2,128)S(1)}, s32[2,32]{1,0:T(2,128)}, u32[]{:S(2)}) copy-start(s32[2,32]{1,0:T(2,128)} %owners.9) | copy-start | bytes 772
  90.8 15.3 %copy-start.41 = (s32[4]{0:T(128)S(1)}, s32[4]{0:T(128)}, u32[]{:S(2)}) copy-start(s32[4]{0:T(128)} %copy-done.40) | copy-start | bytes 52
  99.5 10.7 %copy-start.22 = (bf16[2,2,272,128]{3,2,1,0:T(8,128)(2,1)}, bf16[2,2,272,128]{3,2,1,0:T(8,128)(2,1)S(1)}, u32[]{:S(2)}) copy-start(bf16[2,2,272,128]{3,2,1,0:T(8,128)(2,1)S(1)} %collective-permute-done.7.refs_11_.refs_14_.refs_3_) | copy-start | bytes 835588
  106.1 2.4 %copy-start.3 = (bf16[1,2,9728,128]{3,2,1,0:T(8,128)(2,1)S(1)}, bf16[1,2,9728,128]{3,2,1,0:T(8,128)(2,1)}, u32[]{:S(2)}) copy-start(bf16[1,2,9728,128]{3,2,1,0:T(8,128)(2,1)} %copy-done) | copy-start | bytes 14942212
  110.2 1.0 copy-start.21
  111.2 0.7 copy-start.33
  112.6 20.0 %all-to-all-start.3 = ((bf16[8,1,2,17,16,128]{5,4,3,2,1,0:T(8,128)(2,1)}), bf16[8,1,2,17,16,128]{5,4,3,2,1,0:T(8,128)(2,1)S(1)}, u32[]{:S(2)}, u32[]{:S(2)}) async-start(bf16[8,1,2,17,16,128]{5,4,3,2,1,0:T(8,128)(2,1)} %copy-done.21), calls=%async_computation.3 | async-start | bytes 2228224 | tf_op jit(solution)/shard_map/all_to_all | solution.py:228
  116.5 24.3 %copy-start.31 = (s32[2,32,4]{2,1,0:T(8,128)S(1)}, s32[2,32,4]{2,1,0:T(8,128)}, u32[]{:S(2)}) copy-start(s32[2,32,4]{2,1,0:T(8,128)} %copy-done.29) | copy-start | bytes 3076
  116.5 24.3 %copy-start.39 = (s32[2,32]{1,0:T(2,128)S(1)}, s32[2,32]{1,0:T(2,128)}, u32[]{:S(2)}) copy-start(s32[2,32]{1,0:T(2,128)} %owners.9) | copy-start | bytes 772
  116.5 24.3 %copy-start.42 = (s32[4]{0:T(128)S(1)}, s32[4]{0:T(128)}, u32[]{:S(2)}) copy-start(s32[4]{0:T(128)} %copy-done.40) | copy-start | bytes 52
  116.5 17.0 %collective-permute-start.10 = (bf16[2,2,272,128]{3,2,1,0:T(8,128)(2,1)}, bf16[2,2,272,128]{3,2,1,0:T(8,128)(2,1)}, u32[]{:S(2)}, u32[]{:S(2)}) collective-permute-start(bf16[2,2,272,128]{3,2,1,0:T(8,128)(2,1)} %copy-done.32), channel_id=1, source_target_pairs={{0,2},{1,3},{2,0},{3,1},{4,6},{5,7},{6,4},{7,5},{8,10},{9,11},{10,... | collective-permute-start | bytes 835592 | tf_op jit(solution)/shard_map/ppermute | solution.py:255
  119.2 14.3 %collective-permute-start.9 = (bf16[2,2,272,128]{3,2,1,0:T(8,128)(2,1)}, bf16[2,2,272,128]{3,2,1,0:T(8,128)(2,1)}, u32[]{:S(2)}, u32[]{:S(2)}) collective-permute-start(bf16[2,2,272,128]{3,2,1,0:T(8,128)(2,1)} %copy-done.34), channel_id=1, source_target_pairs={{0,3},{1,0},{2,1},{3,2},{4,7},{5,4},{6,5},{7,6},{8,11},{9,8},{10,9... | collective-permute-start | bytes 835592 | tf_op jit(solution)/shard_map/ppermute | solution.py:255
  121.1 19.6 %collective-permute-start.8 = (bf16[2,2,272,128]{3,2,1,0:T(8,128)(2,1)}, bf16[2,2,272,128]{3,2,1,0:T(8,128)(2,1)}, u32[]{:S(2)}, u32[]{:S(2)}) collective-permute-start(bf16[2,2,272,128]{3,2,1,0:T(8,128)(2,1)} %copy-done.33), channel_id=1, source_target_pairs={{0,1},{1,2},{2,3},{3,0},{4,5},{5,6},{6,7},{7,4},{8,9},{9,10},{10,1... | collective-permute-start | bytes 835592 | tf_op jit(solution)/shard_map/ppermute | solution.py:255
  132.6 8.2 %copy-start.6 = (bf16[8,2,4,2,16,128]{5,4,3,2,1,0:T(8,128)(2,1)S(1)}, bf16[8,2,4,2,16,128]{5,4,3,2,1,0:T(8,128)(2,1)}, u32[]{:S(2)}) copy-start(bf16[8,2,4,2,16,128]{5,4,3,2,1,0:T(8,128)(2,1)} %copy-done.5) | copy-start | bytes 1572868
  132.6 8.2 %copy-start.9 = (bf16[8,2,4,2,16,128]{5,4,3,2,1,0:T(8,128)(2,1)S(1)}, bf16[8,2,4,2,16,128]{5,4,3,2,1,0:T(8,128)(2,1)}, u32[]{:S(2)}) copy-start(bf16[8,2,4,2,16,128]{5,4,3,2,1,0:T(8,128)(2,1)} %copy-done.8) | copy-start | bytes 1572868
  132.6 8.2 %copy-start.14 = (bf16[8,2,4,2,16,128]{5,4,3,2,1,0:T(8,128)(2,1)S(1)}, bf16[8,2,4,2,16,128]{5,4,3,2,1,0:T(8,128)(2,1)}, u32[]{:S(2)}) copy-start(bf16[8,2,4,2,16,128]{5,4,3,2,1,0:T(8,128)(2,1)} %copy-done.11) | copy-start | bytes 1572868
  140.8 2.4 %copy-start.4 = (bf16[1,2,9728,128]{3,2,1,0:T(8,128)(2,1)S(1)}, bf16[1,2,9728,128]{3,2,1,0:T(8,128)(2,1)}, u32[]{:S(2)}) copy-start(bf16[1,2,9728,128]{3,2,1,0:T(8,128)(2,1)} %copy-done) | copy-start | bytes 14942212
  143.2 1.0 copy-start.18
  144.3 1.0 copy-start.23
  146.9 1.0 copy-start.19
  147.9 20.4 %all-to-all-start.4 = ((bf16[8,1,2,17,16,128]{5,4,3,2,1,0:T(8,128)(2,1)}), bf16[8,1,2,17,16,128]{5,4,3,2,1,0:T(8,128)(2,1)}, u32[]{:S(2)}, u32[]{:S(2)}) async-start(bf16[8,1,2,17,16,128]{5,4,3,2,1,0:T(8,128)(2,1)} %copy-done.19), calls=%async_computation.4 | async-start | bytes 2228224 | tf_op jit(solution)/shard_map/all_to_all | solution.py:228
  152.2 9.7 %copy-start.10 = (bf16[8,2,4,2,16,128]{5,4,3,2,1,0:T(8,128)(2,1)S(1)}, bf16[8,2,4,2,16,128]{5,4,3,2,1,0:T(8,128)(2,1)}, u32[]{:S(2)}) copy-start(bf16[8,2,4,2,16,128]{5,4,3,2,1,0:T(8,128)(2,1)} %copy-done.8) | copy-start | bytes 1572868
  154.8 21.0 %collective-permute-start.17 = (bf16[2,2,272,128]{3,2,1,0:T(8,128)(2,1)}, bf16[2,2,272,128]{3,2,1,0:T(8,128)(2,1)}, u32[]{:S(2)}, u32[]{:S(2)}) collective-permute-start(bf16[2,2,272,128]{3,2,1,0:T(8,128)(2,1)} %get-tuple-element.25.refs_2_), channel_id=1, source_target_pairs={{0,2},{1,3},{2,0},{3,1},{4,6},{5,7},{6,4},{7,5},{8,10},{9,11},{10,... | collective-permute-start | bytes 835592 | tf_op jit(solution)/shard_map/ppermute | solution.py:255
  161.5 15.5 %collective-permute-start.16 = (bf16[2,2,272,128]{3,2,1,0:T(8,128)(2,1)}, bf16[2,2,272,128]{3,2,1,0:T(8,128)(2,1)}, u32[]{:S(2)}, u32[]{:S(2)}) collective-permute-start(bf16[2,2,272,128]{3,2,1,0:T(8,128)(2,1)} %get-tuple-element.21.refs_3_), channel_id=1, source_target_pairs={{0,3},{1,0},{2,1},{3,2},{4,7},{5,4},{6,5},{7,6},{8,11},{9,8},{10,9... | collective-permute-start | bytes 835592 | tf_op jit(solution)/shard_map/ppermute | solution.py:255
  163.8 47.2 %collective-permute-start.15 = (bf16[2,2,272,128]{3,2,1,0:T(8,128)(2,1)}, bf16[2,2,272,128]{3,2,1,0:T(8,128)(2,1)}, u32[]{:S(2)}, u32[]{:S(2)}) collective-permute-start(bf16[2,2,272,128]{3,2,1,0:T(8,128)(2,1)} %get-tuple-element.22.refs_2_), channel_id=1, source_target_pairs={{0,2},{1,3},{2,0},{3,1},{4,6},{5,7},{6,4},{7,5},{8,10},{9,11},{10,... | collective-permute-start | bytes 835592 | tf_op jit(solution)/shard_map/ppermute | solution.py:255
  163.8 47.2 %collective-permute-start.14 = (bf16[2,2,272,128]{3,2,1,0:T(8,128)(2,1)}, bf16[2,2,272,128]{3,2,1,0:T(8,128)(2,1)}, u32[]{:S(2)}, u32[]{:S(2)}) collective-permute-start(bf16[2,2,272,128]{3,2,1,0:T(8,128)(2,1)} %get-tuple-element.23.refs_1_), channel_id=1, source_target_pairs={{0,1},{1,2},{2,3},{3,0},{4,5},{5,6},{6,7},{7,4},{8,9},{9,10},{10,1... | collective-permute-start | bytes 835592 | tf_op jit(solution)/shard_map/ppermute | solution.py:255
  168.3 26.0 %copy-start.7 = (bf16[8,2,4,2,16,128]{5,4,3,2,1,0:T(8,128)(2,1)S(1)}, bf16[8,2,4,2,16,128]{5,4,3,2,1,0:T(8,128)(2,1)}, u32[]{:S(2)}) copy-start(bf16[8,2,4,2,16,128]{5,4,3,2,1,0:T(8,128)(2,1)} %copy-done.5) | copy-start | bytes 1572868
  169.5 24.8 %copy-start.26 = (bf16[8,2,4,2,16,128]{5,4,3,2,1,0:T(8,128)(2,1)S(1)}, bf16[8,2,4,2,16,128]{5,4,3,2,1,0:T(8,128)(2,1)}, u32[]{:S(2)}) copy-start(bf16[8,2,4,2,16,128]{5,4,3,2,1,0:T(8,128)(2,1)} %copy-done.25) | copy-start | bytes 1572868
  169.6 24.8 %copy-start.27 = (bf16[8,2,4,2,16,128]{5,4,3,2,1,0:T(8,128)(2,1)S(1)}, bf16[8,2,4,2,16,128]{5,4,3,2,1,0:T(8,128)(2,1)}, u32[]{:S(2)}) copy-start(bf16[8,2,4,2,16,128]{5,4,3,2,1,0:T(8,128)(2,1)} %broadcast_select_fusion.1.refs_2_) | copy-start | bytes 1572868
  169.6 24.8 %copy-start.28 = (bf16[8,2,4,2,16,128]{5,4,3,2,1,0:T(8,128)(2,1)S(1)}, bf16[8,2,4,2,16,128]{5,4,3,2,1,0:T(8,128)(2,1)}, u32[]{:S(2)}) copy-start(bf16[8,2,4,2,16,128]{5,4,3,2,1,0:T(8,128)(2,1)} %broadcast_select_fusion.2.refs_1_) | copy-start | bytes 1572868
  169.6 46.7 %collective-permute-start.13 = (bf16[2,2,272,128]{3,2,1,0:T(8,128)(2,1)S(1)}, bf16[2,2,272,128]{3,2,1,0:T(8,128)(2,1)S(1)}, u32[]{:S(2)}, u32[]{:S(2)}) collective-permute-start(bf16[2,2,272,128]{3,2,1,0:T(8,128)(2,1)S(1)} %get-tuple-element.18), channel_id=1, source_target_pairs={{0,3},{1,0},{2,1},{3,2},{4,7},{5,4},{6,5},{7,6},{8,11},{9,8},{10,9... | collective-permute-start | bytes 835592 | tf_op jit(solution)/shard_map/ppermute | solution.py:255
  175.8 46.8 %collective-permute-start.12 = (bf16[2,2,272,128]{3,2,1,0:T(8,128)(2,1)S(1)}, bf16[2,2,272,128]{3,2,1,0:T(8,128)(2,1)S(1)}, u32[]{:S(2)}, u32[]{:S(2)}) collective-permute-start(bf16[2,2,272,128]{3,2,1,0:T(8,128)(2,1)S(1)} %get-tuple-element.19), channel_id=1, source_target_pairs={{0,2},{1,3},{2,0},{3,1},{4,6},{5,7},{6,4},{7,5},{8,10},{9,11},{10,... | collective-permute-start | bytes 835592 | tf_op jit(solution)/shard_map/ppermute | solution.py:255
  177.0 45.6 %collective-permute-start.11 = (bf16[2,2,272,128]{3,2,1,0:T(8,128)(2,1)S(1)}, bf16[2,2,272,128]{3,2,1,0:T(8,128)(2,1)S(1)}, u32[]{:S(2)}, u32[]{:S(2)}) collective-permute-start(bf16[2,2,272,128]{3,2,1,0:T(8,128)(2,1)S(1)} %get-tuple-element.20), channel_id=1, source_target_pairs={{0,1},{1,2},{2,3},{3,0},{4,5},{5,6},{6,7},{7,4},{8,9},{9,10},{10,1... | collective-permute-start | bytes 835592 | tf_op jit(solution)/shard_map/ppermute | solution.py:255
  194.4 1.2 copy-start.24
  (3 other events, 2.1 us)

commit v4 on v3

v4 whole, which is shorter than its diff:
```python
import functools
import math

import jax
import jax.numpy as jnp
from jax import lax
from jax.experimental import pallas as pl
from jax.experimental.pallas import tpu as pltpu
from jax.sharding import PartitionSpec as P

D = 7168
QR = 1536
KVR = 512
QK_NOPE = 128
V_DIM = 128
LANES = 128
QUERY, KEY, VALUE, OUT = range(4)
HOLD_PAIRS = 2
HOLD_CHUNK = 30
VMEM_LIMIT = 16 * 1024 * 1024


def piece_widths(rank_total):
    return (
        QR * QK_NOPE // rank_total,
        QK_NOPE * KVR // rank_total,
        V_DIM * KVR // rank_total,
        D * V_DIM // rank_total,
    )


def pack(table, param_offsets, owner_map, ways, widths, granule, chunks, waits=()):
    layer_count, head_count = owner_map.shape
    per_group = head_count // ways
    steps = [[widths[kind] // granule for kind in kinds] for _, kinds in chunks]
    outs = [
        jax.ShapeDtypeStruct((ways, len(items), sum(step)) + table.shape[2:], table.dtype)
        for (items, _), step in zip(chunks, steps)
    ]

    def kernel(offsets, owners, source, *refs):
        targets, taken = refs[len(waits) : -1], refs[-1]
        for layer in range(layer_count):
            first = layer * per_group
            here = []
            for target, (items, kinds), step in zip(targets, chunks, steps):
                low, high = max(items[0], first), min(items[-1] + 1, first + per_group)
                if low < high:
                    here.append((target, kinds, step, low - first, high - first, first - items[0]))
            if not here:
                continue
            for way in range(ways):
                taken[way] = 0

            def one_head(head):
                way = owners[layer, head]
                slot = taken[way]
                taken[way] = slot + 1

                def move(target, kinds, step, shift):
                    start = 0
                    for kind, size in zip(kinds, step):
                        begin = lax.div(offsets[layer, head, kind], jnp.int32(granule))
                        target[way, slot + shift, pl.ds(start, size)] = source[layer, pl.ds(begin, size)]
                        start += size

                for target, kinds, step, low, high, shift in here:
                    if (low, high) == (0, per_group):
                        move(target, kinds, step, shift)
                    else:
                        pl.when(jnp.logical_and(slot >= low, slot < high))(
                            functools.partial(move, target, kinds, step, shift)
                        )

            pl.loop(0, head_count, unroll=min(8, head_count))(one_head)

    return pl.pallas_call(
        kernel,
        out_shape=outs,
        in_specs=[
            pl.BlockSpec(memory_space=pltpu.SMEM),
            pl.BlockSpec(memory_space=pltpu.SMEM),
            pl.BlockSpec(memory_space=pltpu.VMEM),
        ]
        + [pl.BlockSpec(memory_space=pl.ANY)] * len(waits),
        out_specs=[pl.BlockSpec(memory_space=pltpu.VMEM)] * len(outs),
        scratch_shapes=[pltpu.SMEM((ways,), jnp.int32)],
        compiler_params=pltpu.CompilerParams(vmem_limit_bytes=VMEM_LIMIT),
        cost_estimate=pl.CostEstimate(
            flops=0,
            transcendentals=0,
            bytes_accessed=sum(2 * 2 * math.prod(out.shape) for out in outs),
        ),
        name="pack",
    )(param_offsets, owner_map, table, *waits)


def first_of(x):
    return lax.slice(x, (0,) * x.ndim, (1,) * x.ndim).reshape(1)


def hold(small, waits, micros):
    def kernel(small_in, *refs):
        for i in range(small.shape[0]):
            refs[-1][i] = small_in[i]

    return pl.pallas_call(
        kernel,
        out_shape=jax.ShapeDtypeStruct(small.shape, small.dtype),
        in_specs=[pl.BlockSpec(memory_space=pltpu.SMEM)]
        + [pl.BlockSpec(memory_space=pl.ANY)] * len(waits),
        out_specs=pl.BlockSpec(memory_space=pltpu.SMEM),
        cost_estimate=pl.CostEstimate(
            flops=int(micros * 1.15e9), transcendentals=0, bytes_accessed=0
        ),
        name="hold",
    )(small, *[first_of(x) for x in waits])


def cut(rows, targets, blocks, shifts):
    shape = (blocks,) + rows.shape[1:]

    def kernel(at, source, *pieces):
        for shift, piece in zip(shifts, pieces):
            for f in range(blocks):
                piece[f] = source[at[shift] * blocks + f]

    return pl.pallas_call(
        kernel,
        out_shape=[jax.ShapeDtypeStruct(shape, rows.dtype)] * len(shifts),
        in_specs=[pl.BlockSpec(memory_space=pltpu.SMEM), pl.BlockSpec(memory_space=pltpu.VMEM)],
        out_specs=[pl.BlockSpec(memory_space=pltpu.VMEM)] * len(shifts),
        compiler_params=pltpu.CompilerParams(vmem_limit_bytes=VMEM_LIMIT),
        cost_estimate=pl.CostEstimate(
            flops=0, transcendentals=0, bytes_accessed=4 * len(shifts) * math.prod(shape)
        ),
        name="cut",
    )(targets, rows)


def line_step(up, down, axis, ways):
    return (
        lax.ppermute(up, axis, [(i, i + 1) for i in range(ways - 1)]),
        lax.ppermute(down, axis, [(i + 1, i) for i in range(ways - 1)]),
    )


def assemble(me, spread_parts):
    t_ways = len(spread_parts)
    f_ways, items, kinds, rows, _ = spread_parts[0].shape
    depth = t_ways * f_ways * rows * LANES // KVR
    cuts = KVR // LANES

    def kernel(me_ref, *refs):
        pieces, (out, scratch) = refs[:t_ways], refs[t_ways:]
        for kind in range(kinds):
            for d in range(t_ways):
                t = lax.rem(me_ref[0] - d + t_ways, t_ways)
                for f in range(f_ways):
                    scratch[pl.ds(pl.multiple_of((f * t_ways + t) * rows, rows), rows), :] = pieces[
                        d
                    ][f, 0, kind].astype(jnp.float32)
            for cut in range(cuts):
                out[0, kind, :, pl.ds(cut * LANES, LANES)] = scratch[
                    pl.ds(cut, depth, stride=cuts), :
                ].astype(jnp.bfloat16)

    return pl.pallas_call(
        kernel,
        grid_spec=pltpu.PrefetchScalarGridSpec(
            num_scalar_prefetch=1,
            grid=(items,),
            in_specs=[pl.BlockSpec((f_ways, 1, kinds, rows, LANES), lambda i, _: (0, i, 0, 0, 0))] * t_ways,
            out_specs=pl.BlockSpec((1, kinds, depth, KVR), lambda i, _: (i, 0, 0, 0)),
            scratch_shapes=[pltpu.VMEM((depth * cuts, LANES), jnp.float32)],
        ),
        out_shape=jax.ShapeDtypeStruct((items, kinds, depth, KVR), spread_parts[0].dtype),
        compiler_params=pltpu.CompilerParams(vmem_limit_bytes=VMEM_LIMIT),
        name="assemble",
    )(me.reshape(1), *spread_parts)


def absorb(where, items, own, came, matrices, outs, shapes):
    t_ways = len(came) + 1
    blocks = came[0].shape[0]
    q_rows, o_rows = shapes[0].shape[3], shapes[1].shape[3]
    rows = q_rows + o_rows

    def kernel(at, *refs):
        parts, mats = refs[:t_ways], refs[t_ways]
        q_out, o_out = refs[-2:]
        for d in range(t_ways):
            t = lax.rem(at[0] - d + t_ways, t_ways)
            for f in range(blocks):
                q_out[0, f, t] = jnp.dot(
                    parts[d][f, 0, :q_rows], mats[0, 0], preferred_element_type=jnp.float32
                ).astype(jnp.bfloat16)
                o_out[0, f, t] = jnp.dot(
                    parts[d][f, 0, q_rows:], mats[0, 1], preferred_element_type=jnp.float32
                ).astype(jnp.bfloat16)

    in_specs = [pl.BlockSpec((blocks, 1, rows, LANES), lambda j, at: (at[1], j, 0, 0))]
    in_specs += [pl.BlockSpec((blocks, 1, rows, LANES), lambda j, at: (0, j, 0, 0))] * len(came)
    in_specs += [pl.BlockSpec((1,) + matrices.shape[1:], lambda j, at: (items[0] + j, 0, 0, 0))]
    args = [own, *came, matrices]
    aliases = {}
    if outs is not None:
        in_specs += [pl.BlockSpec(memory_space=pl.ANY)] * 2
        aliases = {1 + len(args): 0, 2 + len(args): 1}
        args += list(outs)
    work = t_ways * blocks * len(items) * rows
    return pl.pallas_call(
        kernel,
        grid_spec=pltpu.PrefetchScalarGridSpec(
            num_scalar_prefetch=1,
            grid=(len(items),),
            in_specs=in_specs,
            out_specs=[
                pl.BlockSpec((1,) + shape.shape[1:], lambda j, at: (items[0] + j, 0, 0, 0, 0))
                for shape in shapes
            ],
        ),
        out_shape=shapes,
        input_output_aliases=aliases,
        compiler_params=pltpu.CompilerParams(vmem_limit_bytes=VMEM_LIMIT),
        cost_estimate=pl.CostEstimate(
            flops=2 * work * LANES * KVR,
            transcendentals=0,
            bytes_accessed=2 * work * (LANES + KVR),
        ),
        name="absorb",
    )(where, *args)


def absorb_plain(me, own, came, matrices):
    t_ways = len(came) + 1
    order = lax.rem(me - jnp.arange(t_ways, dtype=jnp.int32) + t_ways, jnp.int32(t_ways))
    rows = jnp.take(jnp.stack([own, *came]), order, axis=0).transpose(2, 1, 0, 3, 4)
    cut = rows.shape[3] * QR // (QR + D)
    return tuple(
        jnp.einsum("hrc,hck->hrk", part, mats, preferred_element_type=jnp.float32).astype(jnp.bfloat16)
        for part, mats in (
            (rows[:, :, :, :cut].reshape(rows.shape[0], -1, LANES), matrices[:, 0]),
            (rows[:, :, :, cut:].reshape(rows.shape[0], -1, LANES), matrices[:, 1]),
        )
    )


def per_device(learner_flat, param_offsets, owner_map, slice_map):
    f_ways, t_ways = lax.axis_size("fsdp"), lax.axis_size("tp")
    layer_count = learner_flat.shape[0]
    per_group = owner_map.shape[1] // f_ways
    item_count = layer_count * per_group
    widths = piece_widths(f_ways * t_ways)
    granule = functools.reduce(math.gcd, widths)
    table = learner_flat.reshape(layer_count, -1, granule // LANES, LANES)
    whole_tiles = granule % (16 * LANES) == 0
    row_counts = [width // LANES for width in widths]

    me = lax.axis_index("tp")
    slice_row = lax.dynamic_index_in_dim(slice_map, lax.axis_index("fsdp"), 0, keepdims=False)
    blocks = f_ways // t_ways
    shifts = range(1, t_ways)
    cuts = [0, item_count * 2 // 8, item_count * 5 // 8, item_count]
    chunks = [range(low, high) for low, high in zip(cuts, cuts[1:]) if low < high]

    def packed(of, waits=()):
        waits = [first_of(x) for x in waits]
        return pack(table, param_offsets, owner_map, f_ways, widths, granule, of, waits)

    def over_fsdp(x, rows):
        x = lax.all_to_all(x, "fsdp", split_axis=0, concat_axis=0, tiled=True)
        return x.reshape(x.shape[:2] + rows)

    def over_tp(rows, to):
        return [
            lax.ppermute(piece, "tp", [(i, (i + shift) % t_ways) for i in range(t_ways)])
            for shift, piece in zip(shifts, cut(rows, to, blocks, shifts))
        ]

    (pairs,) = packed([(range(item_count), (KEY, VALUE))])
    to_send = packed([(items, (QUERY, OUT)) for items in chunks])
    pairs = over_fsdp(pairs, (2, row_counts[KEY], LANES))
    targets = jnp.stack([slice_row[lax.rem(me + shift, t_ways)] for shift in range(t_ways)])
    up, down = [pairs], [pairs]
    for _ in shifts:
        above, below = line_step(up[-1], down[-1], "tp", t_ways)
        up.append(above)
        down.append(below)

    exchanged = []
    for at, items in enumerate(chunks):
        rows = over_fsdp(to_send[at], (row_counts[QUERY] + row_counts[OUT], LANES))
        waits = exchanged[at - 1][1] + up[3:] + down[3:] if at else up[1:3] + down[1:3]
        exchanged.append((rows, over_tp(rows, hold(targets, waits, HOLD_CHUNK if at else HOLD_PAIRS))))
    near = [jnp.where(me >= d, up[d], down[t_ways - d]) for d in shifts]

    if whole_tiles:
        shapes = tuple(
            jax.ShapeDtypeStruct((item_count, blocks, t_ways, row_counts[kind], KVR), jnp.bfloat16)
            for kind in (QUERY, OUT)
        )
        where = jnp.stack([me, targets[0]])
        matrices = assemble(me, [pairs] + near)
        outs = None
        for items, (rows, came) in zip(chunks, exchanged):
            outs = absorb(where, items, rows, came, matrices, outs, shapes)
        return tuple(out.reshape(layer_count, per_group, -1, KVR) for out in outs)

    order = lax.rem(me - jnp.arange(t_ways, dtype=jnp.int32) + t_ways, jnp.int32(t_ways))
    matrices = jnp.take(jnp.stack([pairs] + near), order, axis=0).transpose(2, 3, 1, 0, 4, 5)
    matrices = matrices.reshape(item_count, 2, -1, KVR)
    done = [
        absorb_plain(
            me,
            lax.dynamic_slice_in_dim(rows, targets[0] * blocks, blocks, 0),
            came,
            matrices[items[0] : items[-1] + 1],
        )
        for items, (rows, came) in zip(chunks, exchanged)
    ]
    return tuple(jnp.concatenate(kind).reshape(layer_count, per_group, -1, KVR) for kind in zip(*done))


def solution(mesh):
    placed = (P(None, ("fsdp", "tp")), P(), P(), P())
    return jax.shard_map(
        per_device,
        mesh=mesh,
        in_specs=placed,
        out_specs=(P(None, "fsdp", "tp", None), P(None, "fsdp", "tp", None)),
        check_vma=False,
    )
```

time: 230 us -> 199 us (0.87)
  the two profiles are of different devices: /device:TPU:0 before, /device:TPU:10 now
where the time goes in v4:
time: 199 us; the launch traced here: 197 us
  waiting for transfers between devices  71.7 us (36%)
  starting transfers between devices  46.2 us (23%)
  Pallas kernels  36.6 us (18%)
  local copies, waits for them, and re-layouts  22.4 us (11%)
  blocking collectives  12.3 us (6%)
  other arithmetic  6.98 us (4%)
    ppermute x9, waiting for transfers between devices, over_tp(): lax.ppermute(piece, 'tp', [(i, (i + shift) % t_ways) for i in range(t_way...  63.1 us
    pallas_call x3, Pallas kernels, absorb(): pl.pallas_call(kernel, grid_spec=pltpu.PrefetchScalarGridSpec(num_scalar_...  14.3 us
    ppermute x9, starting transfers between devices, over_tp(): lax.ppermute(piece, 'tp', [(i, (i + shift) % t_ways) for i in range(t_way...  13.6 us
    all_to_all x3, starting transfers between devices, over_fsdp(): x = lax.all_to_all(x, 'fsdp', split_axis=0, concat_axis=0, tiled=True)  13.4 us
    all_to_all x1, blocking collectives, over_fsdp(): x = lax.all_to_all(x, 'fsdp', split_axis=0, concat_axis=0, tiled=True)  12.3 us
    pallas_call x3, Pallas kernels, hold(): pl.pallas_call(kernel, out_shape=jax.ShapeDtypeStruct(small.shape, small....  12 us
    slice x12, local copies, waits for them, and re-layouts, first_of(): return lax.slice(x, (0,) * x.ndim, (1,) * x.ndim).reshape(1)  11.2 us
    unnamed x46, local copies, waits for them, and re-layouts  10.6 us
  transfers between devices with their start and end apart: 18, of which 8 were waited for; matrix products, arithmetic and copies ran while one was open for 10% of the time, Pallas kernels for 14%

profile of v4, /device:TPU:10, one launch (start us, length us, event | category | flops | bytes accessed | tf_op | source)
XLA Modules:
  0.0 197.3 jit_solution(3821536081106146885)
XLA Ops:
  0.6 4.6 %copy.12 = bf16[1,2,9728,128]{3,2,1,0:T(8,128)(2,1)} copy(bf16[1,2,9728,128]{3,1,2,0:T(2,128)(2,1)} %bitcast.35) | data formatting | bytes 9961472
  5.3 0.1 copy.10.offsets
  5.4 2.4 %copy-done = bf16[1,2,9728,128]{3,2,1,0:T(8,128)(2,1)S(1)} copy-done((bf16[1,2,9728,128]{3,2,1,0:T(8,128)(2,1)S(1)}, bf16[1,2,9728,128]{3,2,1,0:T(8,128)(2,1)}, u32[]{:S(2)}) %copy-start) | copy-done | bytes 4980760
  7.8 1.8 pack.3
  9.6 12.3 %all_to_all.20.refs_0_ = bf16[8,8,2,16,128]{4,3,2,1,0:T(8,128)(2,1)S(1)} all-to-all(bf16[8,8,2,16,128]{4,3,2,1,0:T(8,128)(2,1)S(1)} %pack.3), channel_id=1, replica_groups=mesh['fsdp'=8,'tp'=4] {'fsdp'}, dimensions={0} | all-to-all | bytes 1048576 | tf_op jit(solution)/shard_map/all_to_all | solution.py:272
  21.9 3.6 %collective-permute-start = (bf16[8,8,2,16,128]{4,3,2,1,0:T(8,128)(2,1)S(1)}, bf16[8,8,2,16,128]{4,3,2,1,0:T(8,128)(2,1)S(1)}, u32[]{:S(2)}, u32[]{:S(2)}) collective-permute-start(bf16[8,8,2,16,128]{4,3,2,1,0:T(8,128)(2,1)S(1)} %all_to_all.20.refs_0_), channel_id=1, source_target_pairs={{0,1},{1,2},{2,3},{4,5},{5,6},{6,7},{8,9},{9,10},{10,11},{12,13},{... | collective-permute-start | bytes 1572872 | tf_op jit(solution)/shard_map/ppermute | solution.py:143
  25.5 2.4 %collective-permute-start.2 = (bf16[8,8,2,16,128]{4,3,2,1,0:T(8,128)(2,1)S(1)}, bf16[8,8,2,16,128]{4,3,2,1,0:T(8,128)(2,1)S(1)}, u32[]{:S(2)}, u32[]{:S(2)}) collective-permute-start(bf16[8,8,2,16,128]{4,3,2,1,0:T(8,128)(2,1)S(1)} %all_to_all.20.refs_0_), channel_id=1, source_target_pairs={{1,0},{2,1},{3,2},{5,4},{6,5},{7,6},{9,8},{10,9},{11,10},{13,12},{... | collective-permute-start | bytes 1572872 | tf_op jit(solution)/shard_map/ppermute | solution.py:144
  27.9 4.6 %pack.2 = (bf16[8,2,17,16,128]{4,3,2,1,0:T(8,128)(2,1)}, bf16[8,3,17,16,128]{4,3,2,1,0:T(8,128)(2,1)}, bf16[8,3,17,16,128]{4,3,2,1,0:T(8,128)(2,1)S(1)}) custom-call(s32[2,32,4]{2,1,0:T(8,128)S(1)} %copy.10.offsets, s32[2,32]{1,0:T(2,128)S(1)} %copy-done.13, bf16[2,608,16,128]{3,2,1,0:T(8,128)(2,1)S(1)} %bitcast.26), custom_call_target="tpu_custom_call" | custom-call | bytes 8912896 | tf_op jit(solution)/shard_map/pack/pallas_call | solution.py:77
  32.5 1.2 copy-done.6
  33.6 4.9 %all-to-all-start.2 = ((bf16[8,2,17,16,128]{4,3,2,1,0:T(8,128)(2,1)}), bf16[8,2,17,16,128]{4,3,2,1,0:T(8,128)(2,1)S(1)}, u32[]{:S(2)}, u32[]{:S(2)}) async-start(bf16[8,2,17,16,128]{4,3,2,1,0:T(8,128)(2,1)} %get-tuple-element.21), calls=%async_computation.2 | async-start | bytes 2228224 | tf_op jit(solution)/shard_map/all_to_all | solution.py:272
  38.6 3.5 %collective-permute-start.1 = (bf16[8,8,2,16,128]{4,3,2,1,0:T(8,128)(2,1)S(1)}, bf16[8,8,2,16,128]{4,3,2,1,0:T(8,128)(2,1)}, u32[]{:S(2)}, u32[]{:S(2)}) collective-permute-start(bf16[8,8,2,16,128]{4,3,2,1,0:T(8,128)(2,1)S(1)} %collective-permute-done), channel_id=1, source_target_pairs={{0,1},{1,2},{2,3},{4,5},{5,6},{6,7},{8,9},{9,10},{10,11},{12,13},{... | collective-permute-start | bytes 1572872 | tf_op jit(solution)/shard_map/ppermute | solution.py:143
  42.1 3.2 %collective-permute-start.3 = (bf16[8,8,2,16,128]{4,3,2,1,0:T(8,128)(2,1)S(1)}, bf16[8,8,2,16,128]{4,3,2,1,0:T(8,128)(2,1)}, u32[]{:S(2)}, u32[]{:S(2)}) collective-permute-start(bf16[8,8,2,16,128]{4,3,2,1,0:T(8,128)(2,1)S(1)} %collective-permute-done.2), channel_id=1, source_target_pairs={{1,0},{2,1},{3,2},{5,4},{6,5},{7,6},{9,8},{10,9},{11,10},{13,12},{... | collective-permute-start | bytes 1572872 | tf_op jit(solution)/shard_map/ppermute | solution.py:144
  45.3 0.7 fusion
  46.0 8.6 %collective-permute-done.1 = bf16[8,8,2,16,128]{4,3,2,1,0:T(8,128)(2,1)} collective-permute-done((bf16[8,8,2,16,128]{4,3,2,1,0:T(8,128)(2,1)S(1)}, bf16[8,8,2,16,128]{4,3,2,1,0:T(8,128)(2,1)}, u32[]{:S(2)}, u32[]{:S(2)}) %collective-permute-start.1) | collective-permute-done | bytes 524320 | tf_op jit(solution)/shard_map/ppermute | solution.py:143
  54.6 3.4 %collective-permute-start.7 = (bf16[8,8,2,16,128]{4,3,2,1,0:T(8,128)(2,1)}, bf16[8,8,2,16,128]{4,3,2,1,0:T(8,128)(2,1)}, u32[]{:S(2)}, u32[]{:S(2)}) collective-permute-start(bf16[8,8,2,16,128]{4,3,2,1,0:T(8,128)(2,1)} %collective-permute-done.1), channel_id=1, source_target_pairs={{0,1},{1,2},{2,3},{4,5},{5,6},{6,7},{8,9},{9,10},{10,11},{12,13},{... | collective-permute-start | bytes 1572872 | tf_op jit(solution)/shard_map/ppermute | solution.py:143
  58.0 3.2 %collective-permute-start.8 = (bf16[8,8,2,16,128]{4,3,2,1,0:T(8,128)(2,1)}, bf16[8,8,2,16,128]{4,3,2,1,0:T(8,128)(2,1)}, u32[]{:S(2)}, u32[]{:S(2)}) collective-permute-start(bf16[8,8,2,16,128]{4,3,2,1,0:T(8,128)(2,1)} %collective-permute-done.3), channel_id=1, source_target_pairs={{1,0},{2,1},{3,2},{5,4},{6,5},{7,6},{9,8},{10,9},{11,10},{13,12},{... | collective-permute-start | bytes 1572872 | tf_op jit(solution)/shard_map/ppermute | solution.py:144
  61.2 3.2 %pad_add_fusion.1.small_in = s32[4]{0:T(128)} fusion(s32[1]{0:T(128)} %bitcast.5, s32[1]{0:T(128)} %bitcast.4, s32[1]{0:T(128)} %bitcast.3, s32[1]{0:T(128)} %bitcast.1), kind=kLoop, calls=%fused_computation.4 | loop fusion | flops 12 | bytes 32 | tf_op jit(solution)/shard_map/stack | solution.py:284
  64.4 0.6 slice.50
  65.0 0.6 slice.52
  65.5 1.2 slice.51
  66.7 1.2 slice.53
  67.9 3.7 %hold.3.at = s32[4]{0:T(128)} custom-call(s32[4]{0:T(128)} %pad_add_fusion.1.small_in, bf16[1]{0:T(256)(128)(2,1)} %bitcast.6.refs_0_, bf16[1]{0:T(256)(128)(2,1)} %bitcast.7.refs_1_, bf16[1]{0:T(256)(128)(2,1)} %bitcast.8.refs_2_, bf16[1]{0:T(256)(128)(2,1)} %bitcast.9.refs_3_), custom_call_target="tpu_custom_call" | custom-call | flops 2300000000 | tf_op jit(solution)/shard_map/hold/pallas_call | solution.py:107
  71.7 0.6 copy-done.15
  72.3 0.6 cut.3
  72.9 0.8 collective-permute-start.4
  73.7 1.9 collective-permute-start.5
  75.6 1.9 collective-permute-start.6
  77.6 4.2 %all-to-all-start.3 = ((bf16[8,3,17,16,128]{4,3,2,1,0:T(8,128)(2,1)}), bf16[8,3,17,16,128]{4,3,2,1,0:T(8,128)(2,1)S(1)}, u32[]{:S(2)}, u32[]{:S(2)}) async-start(bf16[8,3,17,16,128]{4,3,2,1,0:T(8,128)(2,1)} %get-tuple-element.25), calls=%async_computation.3 | async-start | bytes 3342336 | tf_op jit(solution)/shard_map/all_to_all | solution.py:272
  81.8 11.0 %collective-permute-done.4.refs_1_ = bf16[2,2,272,128]{3,2,1,0:T(8,128)(2,1)S(1)} collective-permute-done((bf16[2,2,272,128]{3,2,1,0:T(8,128)(2,1)S(1)}, bf16[2,2,272,128]{3,2,1,0:T(8,128)(2,1)S(1)}, u32[]{:S(2)}, u32[]{:S(2)}) %collective-permute-start.4) | collective-permute-done | bytes 278560 | tf_op jit(solution)/shard_map/ppermute | solution.py:277
  92.7 0.6 slice.54
  93.3 3.1 %collective-permute-done.5.refs_2_ = bf16[2,2,272,128]{3,2,1,0:T(8,128)(2,1)S(1)} collective-permute-done((bf16[2,2,272,128]{3,2,1,0:T(8,128)(2,1)S(1)}, bf16[2,2,272,128]{3,2,1,0:T(8,128)(2,1)S(1)}, u32[]{:S(2)}, u32[]{:S(2)}) %collective-permute-start.5) | collective-permute-done | bytes 278560 | tf_op jit(solution)/shard_map/ppermute | solution.py:277
  96.4 0.6 slice.55
  97.1 2.0 %collective-permute-done.6.refs_3_ = bf16[2,2,272,128]{3,2,1,0:T(8,128)(2,1)S(1)} collective-permute-done((bf16[2,2,272,128]{3,2,1,0:T(8,128)(2,1)S(1)}, bf16[2,2,272,128]{3,2,1,0:T(8,128)(2,1)S(1)}, u32[]{:S(2)}, u32[]{:S(2)}) %collective-permute-start.6) | collective-permute-done | bytes 278560 | tf_op jit(solution)/shard_map/ppermute | solution.py:277
  99.1 0.5 slice.56
  99.6 1.2 slice.57
  100.8 1.1 slice.58
  101.9 4.2 %hold.4.at = s32[4]{0:T(128)} custom-call(s32[4]{0:T(128)} %pad_add_fusion.1.small_in, bf16[1]{0:T(256)(128)(2,1)} %bitcast.11.refs_0_, bf16[1]{0:T(256)(128)(2,1)} %bitcast.12.refs_1_, bf16[1]{0:T(256)(128)(2,1)} %bitcast.13.refs_2_, bf16[1]{0:T(256)(128)(2,1)} %bitcast.14.refs_3_, bf16[1]{0:T(256)(128)(2,1)} %bitcast.15.refs_4_), custom_call_target="tpu_custom_call" | custom-call | flops 34500001792 | tf_op jit(solution)/shard_map/hold/pallas_call | solution.py:107
  106.1 0.7 copy-done.16
  106.8 1.7 cut.4
  108.5 1.4 collective-permute-start.10
  109.9 2.0 %collective-permute-start.11 = (bf16[2,3,272,128]{3,2,1,0:T(8,128)(2,1)}, bf16[2,3,272,128]{3,2,1,0:T(8,128)(2,1)}, u32[]{:S(2)}, u32[]{:S(2)}) collective-permute-start(bf16[2,3,272,128]{3,2,1,0:T(8,128)(2,1)} %get-tuple-element.28), channel_id=1, source_target_pairs={{0,3},{1,0},{2,1},{3,2},{4,7},{5,4},{6,5},{7,6},{8,11},{9,8},{10,9... | collective-permute-start | bytes 1253384 | tf_op jit(solution)/shard_map/ppermute | solution.py:277
  111.9 4.2 %all-to-all-start = ((bf16[8,3,17,16,128]{4,3,2,1,0:T(8,128)(2,1)}), bf16[8,3,17,16,128]{4,3,2,1,0:T(8,128)(2,1)S(1)}, u32[]{:S(2)}, u32[]{:S(2)}) async-start(bf16[8,3,17,16,128]{4,3,2,1,0:T(8,128)(2,1)} %copy-done.6), calls=%async_computation | async-start | bytes 3342336 | tf_op jit(solution)/shard_map/all_to_all | solution.py:272
  116.1 0.8 pad_add_fusion.at
  116.9 1.9 broadcast_select_fusion.1.refs_2_
  118.8 2.5 %collective-permute-done.9.refs_1_ = bf16[2,3,272,128]{3,2,1,0:T(8,128)(2,1)} collective-permute-done((bf16[2,3,272,128]{3,2,1,0:T(8,128)(2,1)}, bf16[2,3,272,128]{3,2,1,0:T(8,128)(2,1)}, u32[]{:S(2)}, u32[]{:S(2)}) %collective-permute-start.9) | collective-permute-done | bytes 417824 | tf_op jit(solution)/shard_map/ppermute | solution.py:277
  121.3 1.3 slice.59
  122.5 22.5 %collective-permute-done.10.refs_2_ = bf16[2,3,272,128]{3,2,1,0:T(8,128)(2,1)} collective-permute-done((bf16[2,3,272,128]{3,2,1,0:T(8,128)(2,1)}, bf16[2,3,272,128]{3,2,1,0:T(8,128)(2,1)}, u32[]{:S(2)}, u32[]{:S(2)}) %collective-permute-start.10) | collective-permute-done | bytes 417824 | tf_op jit(solution)/shard_map/ppermute | solution.py:277
  145.0 1.1 slice.60
  146.2 1.2 slice.61
  147.4 4.1 %hold.5.at = s32[4]{0:T(128)} custom-call(s32[4]{0:T(128)} %pad_add_fusion.1.small_in, bf16[1]{0:T(256)(128)(2,1)} %bitcast.17.refs_0_, bf16[1]{0:T(256)(128)(2,1)} %bitcast.18.refs_1_, bf16[1]{0:T(256)(128)(2,1)} %bitcast.19.refs_2_, bf16[1]{0:T(256)(128)(2,1)} %bitcast.14.refs_3_, bf16[1]{0:T(256)(128)(2,1)} %bitcast.15.refs_4_), custom_call_target="tpu_custom_call" | custom-call | flops 34500001792 | tf_op jit(solution)/shard_map/hold/pallas_call | solution.py:107
  151.5 0.7 copy-done.14
  152.3 0.6 cut.5
  153.0 3.4 %collective-permute-start.13 = (bf16[2,3,272,128]{3,2,1,0:T(8,128)(2,1)S(1)}, bf16[2,3,272,128]{3,2,1,0:T(8,128)(2,1)S(1)}, u32[]{:S(2)}, u32[]{:S(2)}) collective-permute-start(bf16[2,3,272,128]{3,2,1,0:T(8,128)(2,1)S(1)} %get-tuple-element.30), channel_id=1, source_target_pairs={{0,2},{1,3},{2,0},{3,1},{4,6},{5,7},{6,4},{7,5},{8,10},{9,11},{10,... | collective-permute-start | bytes 1253384 | tf_op jit(solution)/shard_map/ppermute | solution.py:277
  156.4 1.9 collective-permute-start.14
  158.4 1.1 broadcast_select_fusion.refs_3_
  159.5 0.1 broadcast_select_fusion.2.refs_1_
  159.6 1.1 assemble.1.refs_4_
  160.8 0.1 copy-done.10
  160.9 0.1 copy-done.12
  160.9 3.5 %absorb.3 = (bf16[8,2,4,48,512]{4,3,2,1,0:T(8,128)(2,1)}, bf16[8,2,4,224,512]{4,3,2,1,0:T(8,128)(2,1)}) custom-call(s32[2]{0:T(128)S(1)} %pad_add_fusion.at, bf16[8,2,272,128]{3,2,1,0:T(8,128)(2,1)S(1)} %bitcast.32, bf16[2,2,272,128]{3,2,1,0:T(8,128)(2,1)S(1)} %copy-done.8, bf16[2,2,272,128]{3,2,1,0:T(8,128)(2,1)S(1)} %copy-done.10, ...), custom_call_target="tpu_custom_call" | custom-call | flops 570425344 | bytes 5570560 | tf_op jit(solution)/shard_map/absorb/pallas_call | solution.py:212
  164.5 6.0 %absorb.4 = (bf16[8,2,4,48,512]{4,3,2,1,0:T(8,128)(2,1)}, bf16[8,2,4,224,512]{4,3,2,1,0:T(8,128)(2,1)}) custom-call(s32[2]{0:T(128)S(1)} %pad_add_fusion.at, bf16[8,3,272,128]{3,2,1,0:T(8,128)(2,1)S(1)} %bitcast.28, bf16[2,3,272,128]{3,2,1,0:T(8,128)(2,1)} %collective-permute-done.9.refs_1_, ...), custom_call_target="tpu_custom_call", output_to_operand_aliasing={{0}: (6, {}), {1}: (7, {})} | custom-call | flops 855638016 | bytes 8355840 | tf_op jit(solution)/shard_map/absorb/pallas_call | solution.py:212
  170.5 18.2 %collective-permute-done.13.refs_2_ = bf16[2,3,272,128]{3,2,1,0:T(8,128)(2,1)S(1)} collective-permute-done((bf16[2,3,272,128]{3,2,1,0:T(8,128)(2,1)S(1)}, bf16[2,3,272,128]{3,2,1,0:T(8,128)(2,1)S(1)}, u32[]{:S(2)}, u32[]{:S(2)}) %collective-permute-start.13) | collective-permute-done | bytes 417824 | tf_op jit(solution)/shard_map/ppermute | solution.py:277
  188.7 3.9 %collective-permute-done.14.refs_3_ = bf16[2,3,272,128]{3,2,1,0:T(8,128)(2,1)S(1)} collective-permute-done((bf16[2,3,272,128]{3,2,1,0:T(8,128)(2,1)S(1)}, bf16[2,3,272,128]{3,2,1,0:T(8,128)(2,1)S(1)}, u32[]{:S(2)}, u32[]{:S(2)}) %collective-permute-start.14) | collective-permute-done | bytes 417824 | tf_op jit(solution)/shard_map/ppermute | solution.py:277
  192.5 4.8 %absorb.5 = (bf16[8,2,4,48,512]{4,3,2,1,0:T(8,128)(2,1)}, bf16[8,2,4,224,512]{4,3,2,1,0:T(8,128)(2,1)}) custom-call(s32[2]{0:T(128)S(1)} %pad_add_fusion.at, bf16[8,3,272,128]{3,2,1,0:T(8,128)(2,1)S(1)} %bitcast.30, bf16[2,3,272,128]{3,2,1,0:T(8,128)(2,1)S(1)} %collective-permute-done.12.refs_1_, ...), custom_call_target="tpu_custom_call", output_to_operand_aliasing={{0}: (6, {}), {1}: (7, {})} | custom-call | flops 855638016 | bytes 8355840 | tf_op jit(solution)/shard_map/absorb/pallas_call | solution.py:212
  (49 shorter events, 0.2 us)
Async XLA Ops:
  0.6 4.6 %copy-start.20 = (s32[2,32,4]{1,2,0:T(4,128)S(1)}, s32[2,32,4]{1,2,0:T(4,128)}, u32[]{:S(2)}) copy-start(s32[2,32,4]{1,2,0:T(4,128)} %param.5) | copy-start | bytes 3076
  0.6 4.7 %copy-start.13 = (s32[2,32]{1,0:T(2,128)S(1)}, s32[2,32]{1,0:T(2,128)}, u32[]{:S(2)}) copy-start(s32[2,32]{1,0:T(2,128)} %owners.3) | copy-start | bytes 772
  5.4 2.4 %copy-start = (bf16[1,2,9728,128]{3,2,1,0:T(8,128)(2,1)S(1)}, bf16[1,2,9728,128]{3,2,1,0:T(8,128)(2,1)}, u32[]{:S(2)}) copy-start(bf16[1,2,9728,128]{3,2,1,0:T(8,128)(2,1)} %copy.12) | copy-start | bytes 14942212
  21.9 11.7 %copy-start.3 = (bf16[8,8,2,16,128]{4,3,2,1,0:T(8,128)(2,1)}, bf16[8,8,2,16,128]{4,3,2,1,0:T(8,128)(2,1)S(1)}, u32[]{:S(2)}) copy-start(bf16[8,8,2,16,128]{4,3,2,1,0:T(8,128)(2,1)S(1)} %all_to_all.20.refs_0_) | copy-start | bytes 1572868
  21.9 23.4 %copy-start.21 = (s32[8,4]{0,1:T(4,128)S(1)}, s32[8,4]{0,1:T(4,128)}, u32[]{:S(2)}) copy-start(s32[8,4]{0,1:T(4,128)} %param.7) | copy-start | bytes 388
  21.9 16.7 %collective-permute-start = (bf16[8,8,2,16,128]{4,3,2,1,0:T(8,128)(2,1)S(1)}, bf16[8,8,2,16,128]{4,3,2,1,0:T(8,128)(2,1)S(1)}, u32[]{:S(2)}, u32[]{:S(2)}) collective-permute-start(bf16[8,8,2,16,128]{4,3,2,1,0:T(8,128)(2,1)S(1)} %all_to_all.20.refs_0_), channel_id=1, source_target_pairs={{0,1},{1,2},{2,3},{4,5},{5,6},{6,7},{8,9},{9,10},{10,11},{12,13},{... | collective-permute-start | bytes 1572872 | tf_op jit(solution)/shard_map/ppermute | solution.py:143
  25.5 16.5 %collective-permute-start.2 = (bf16[8,8,2,16,128]{4,3,2,1,0:T(8,128)(2,1)S(1)}, bf16[8,8,2,16,128]{4,3,2,1,0:T(8,128)(2,1)S(1)}, u32[]{:S(2)}, u32[]{:S(2)}) collective-permute-start(bf16[8,8,2,16,128]{4,3,2,1,0:T(8,128)(2,1)S(1)} %all_to_all.20.refs_0_), channel_id=1, source_target_pairs={{1,0},{2,1},{3,2},{5,4},{6,5},{7,6},{9,8},{10,9},{11,10},{13,12},{... | collective-permute-start | bytes 1572872 | tf_op jit(solution)/shard_map/ppermute | solution.py:144
  32.5 1.2 copy-start.6
  33.6 38.0 %all-to-all-start.2 = ((bf16[8,2,17,16,128]{4,3,2,1,0:T(8,128)(2,1)}), bf16[8,2,17,16,128]{4,3,2,1,0:T(8,128)(2,1)S(1)}, u32[]{:S(2)}, u32[]{:S(2)}) async-start(bf16[8,2,17,16,128]{4,3,2,1,0:T(8,128)(2,1)} %get-tuple-element.21), calls=%async_computation.2 | async-start | bytes 2228224 | tf_op jit(solution)/shard_map/all_to_all | solution.py:272
  38.6 33.0 %copy-start.17 = (bf16[8,8,2,16,128]{4,3,2,1,0:T(8,128)(2,1)}, bf16[8,8,2,16,128]{4,3,2,1,0:T(8,128)(2,1)S(1)}, u32[]{:S(2)}) copy-start(bf16[8,8,2,16,128]{4,3,2,1,0:T(8,128)(2,1)S(1)} %collective-permute-done) | copy-start | bytes 1572868
  38.6 16.0 %collective-permute-start.1 = (bf16[8,8,2,16,128]{4,3,2,1,0:T(8,128)(2,1)S(1)}, bf16[8,8,2,16,128]{4,3,2,1,0:T(8,128)(2,1)}, u32[]{:S(2)}, u32[]{:S(2)}) collective-permute-start(bf16[8,8,2,16,128]{4,3,2,1,0:T(8,128)(2,1)S(1)} %collective-permute-done), channel_id=1, source_target_pairs={{0,1},{1,2},{2,3},{4,5},{5,6},{6,7},{8,9},{9,10},{10,11},{12,13},{... | collective-permute-start | bytes 1572872 | tf_op jit(solution)/shard_map/ppermute | solution.py:143
  42.1 29.6 %copy-start.19 = (bf16[8,8,2,16,128]{4,3,2,1,0:T(8,128)(2,1)}, bf16[8,8,2,16,128]{4,3,2,1,0:T(8,128)(2,1)S(1)}, u32[]{:S(2)}) copy-start(bf16[8,8,2,16,128]{4,3,2,1,0:T(8,128)(2,1)S(1)} %collective-permute-done.2) | copy-start | bytes 1572868
  42.1 15.9 %collective-permute-start.3 = (bf16[8,8,2,16,128]{4,3,2,1,0:T(8,128)(2,1)S(1)}, bf16[8,8,2,16,128]{4,3,2,1,0:T(8,128)(2,1)}, u32[]{:S(2)}, u32[]{:S(2)}) collective-permute-start(bf16[8,8,2,16,128]{4,3,2,1,0:T(8,128)(2,1)S(1)} %collective-permute-done.2), channel_id=1, source_target_pairs={{1,0},{2,1},{3,2},{5,4},{6,5},{7,6},{9,8},{10,9},{11,10},{13,12},{... | collective-permute-start | bytes 1572872 | tf_op jit(solution)/shard_map/ppermute | solution.py:144
  54.6 45.0 %collective-permute-start.7 = (bf16[8,8,2,16,128]{4,3,2,1,0:T(8,128)(2,1)}, bf16[8,8,2,16,128]{4,3,2,1,0:T(8,128)(2,1)}, u32[]{:S(2)}, u32[]{:S(2)}) collective-permute-start(bf16[8,8,2,16,128]{4,3,2,1,0:T(8,128)(2,1)} %collective-permute-done.1), channel_id=1, source_target_pairs={{0,1},{1,2},{2,3},{4,5},{5,6},{6,7},{8,9},{9,10},{10,11},{12,13},{... | collective-permute-start | bytes 1572872 | tf_op jit(solution)/shard_map/ppermute | solution.py:143
  58.0 42.7 %collective-permute-start.8 = (bf16[8,8,2,16,128]{4,3,2,1,0:T(8,128)(2,1)}, bf16[8,8,2,16,128]{4,3,2,1,0:T(8,128)(2,1)}, u32[]{:S(2)}, u32[]{:S(2)}) collective-permute-start(bf16[8,8,2,16,128]{4,3,2,1,0:T(8,128)(2,1)} %collective-permute-done.3), channel_id=1, source_target_pairs={{1,0},{2,1},{3,2},{5,4},{6,5},{7,6},{9,8},{10,9},{11,10},{13,12},{... | collective-permute-start | bytes 1572872 | tf_op jit(solution)/shard_map/ppermute | solution.py:144
  71.6 5.9 %copy-start.1 = (bf16[8,2,17,16,128]{4,3,2,1,0:T(8,128)(2,1)}, bf16[8,2,17,16,128]{4,3,2,1,0:T(8,128)(2,1)S(1)}, u32[]{:S(2)}) copy-start(bf16[8,2,17,16,128]{4,3,2,1,0:T(8,128)(2,1)S(1)} %all-to-all-done.2) | copy-start | bytes 3342340
  71.7 0.6 copy-start.15
  72.9 19.9 %collective-permute-start.4 = (bf16[2,2,272,128]{3,2,1,0:T(8,128)(2,1)S(1)}, bf16[2,2,272,128]{3,2,1,0:T(8,128)(2,1)S(1)}, u32[]{:S(2)}, u32[]{:S(2)}) collective-permute-start(bf16[2,2,272,128]{3,2,1,0:T(8,128)(2,1)S(1)} %get-tuple-element.22), channel_id=1, source_target_pairs={{0,1},{1,2},{2,3},{3,0},{4,5},{5,6},{6,7},{7,4},{8,9},{9,10},{10,1... | collective-permute-start | bytes 835592 | tf_op jit(solution)/shard_map/ppermute | solution.py:277
  73.7 22.7 %collective-permute-start.5 = (bf16[2,2,272,128]{3,2,1,0:T(8,128)(2,1)S(1)}, bf16[2,2,272,128]{3,2,1,0:T(8,128)(2,1)S(1)}, u32[]{:S(2)}, u32[]{:S(2)}) collective-permute-start(bf16[2,2,272,128]{3,2,1,0:T(8,128)(2,1)S(1)} %get-tuple-element.23), channel_id=1, source_target_pairs={{0,2},{1,3},{2,0},{3,1},{4,6},{5,7},{6,4},{7,5},{8,10},{9,11},{10,... | collective-permute-start | bytes 835592 | tf_op jit(solution)/shard_map/ppermute | solution.py:277
  75.6 23.5 %collective-permute-start.6 = (bf16[2,2,272,128]{3,2,1,0:T(8,128)(2,1)S(1)}, bf16[2,2,272,128]{3,2,1,0:T(8,128)(2,1)S(1)}, u32[]{:S(2)}, u32[]{:S(2)}) collective-permute-start(bf16[2,2,272,128]{3,2,1,0:T(8,128)(2,1)S(1)} %get-tuple-element.24), channel_id=1, source_target_pairs={{0,3},{1,0},{2,1},{3,2},{4,7},{5,4},{6,5},{7,6},{8,11},{9,8},{10,9... | collective-permute-start | bytes 835592 | tf_op jit(solution)/shard_map/ppermute | solution.py:277
  77.6 28.5 %all-to-all-start.3 = ((bf16[8,3,17,16,128]{4,3,2,1,0:T(8,128)(2,1)}), bf16[8,3,17,16,128]{4,3,2,1,0:T(8,128)(2,1)S(1)}, u32[]{:S(2)}, u32[]{:S(2)}) async-start(bf16[8,3,17,16,128]{4,3,2,1,0:T(8,128)(2,1)} %get-tuple-element.25), calls=%async_computation.3 | async-start | bytes 3342336 | tf_op jit(solution)/shard_map/all_to_all | solution.py:272
  92.7 13.3 %copy-start.7 = (bf16[2,2,272,128]{3,2,1,0:T(8,128)(2,1)}, bf16[2,2,272,128]{3,2,1,0:T(8,128)(2,1)S(1)}, u32[]{:S(2)}) copy-start(bf16[2,2,272,128]{3,2,1,0:T(8,128)(2,1)S(1)} %collective-permute-done.4.refs_1_) | copy-start | bytes 835588
  96.4 9.6 %copy-start.9 = (bf16[2,2,272,128]{3,2,1,0:T(8,128)(2,1)}, bf16[2,2,272,128]{3,2,1,0:T(8,128)(2,1)S(1)}, u32[]{:S(2)}) copy-start(bf16[2,2,272,128]{3,2,1,0:T(8,128)(2,1)S(1)} %collective-permute-done.5.refs_2_) | copy-start | bytes 835588
  99.1 7.0 %copy-start.11 = (bf16[2,2,272,128]{3,2,1,0:T(8,128)(2,1)}, bf16[2,2,272,128]{3,2,1,0:T(8,128)(2,1)S(1)}, u32[]{:S(2)}) copy-start(bf16[2,2,272,128]{3,2,1,0:T(8,128)(2,1)S(1)} %collective-permute-done.6.refs_3_) | copy-start | bytes 835588
  106.1 0.7 copy-start.16
  108.5 12.8 %collective-permute-start.9 = (bf16[2,3,272,128]{3,2,1,0:T(8,128)(2,1)}, bf16[2,3,272,128]{3,2,1,0:T(8,128)(2,1)}, u32[]{:S(2)}, u32[]{:S(2)}) collective-permute-start(bf16[2,3,272,128]{3,2,1,0:T(8,128)(2,1)} %get-tuple-element.26), channel_id=1, source_target_pairs={{0,1},{1,2},{2,3},{3,0},{4,5},{5,6},{6,7},{7,4},{8,9},{9,10},{10,1... | collective-permute-start | bytes 1253384 | tf_op jit(solution)/shard_map/ppermute | solution.py:277
  108.5 36.5 %collective-permute-start.10 = (bf16[2,3,272,128]{3,2,1,0:T(8,128)(2,1)}, bf16[2,3,272,128]{3,2,1,0:T(8,128)(2,1)}, u32[]{:S(2)}, u32[]{:S(2)}) collective-permute-start(bf16[2,3,272,128]{3,2,1,0:T(8,128)(2,1)} %get-tuple-element.27), channel_id=1, source_target_pairs={{0,2},{1,3},{2,0},{3,1},{4,6},{5,7},{6,4},{7,5},{8,10},{9,11},{10,... | collective-permute-start | bytes 1253384 | tf_op jit(solution)/shard_map/ppermute | solution.py:277
  109.9 36.3 %collective-permute-start.11 = (bf16[2,3,272,128]{3,2,1,0:T(8,128)(2,1)}, bf16[2,3,272,128]{3,2,1,0:T(8,128)(2,1)}, u32[]{:S(2)}, u32[]{:S(2)}) collective-permute-start(bf16[2,3,272,128]{3,2,1,0:T(8,128)(2,1)} %get-tuple-element.28), channel_id=1, source_target_pairs={{0,3},{1,0},{2,1},{3,2},{4,7},{5,4},{6,5},{7,6},{8,11},{9,8},{10,9... | collective-permute-start | bytes 1253384 | tf_op jit(solution)/shard_map/ppermute | solution.py:277
  111.9 39.6 %all-to-all-start = ((bf16[8,3,17,16,128]{4,3,2,1,0:T(8,128)(2,1)}), bf16[8,3,17,16,128]{4,3,2,1,0:T(8,128)(2,1)S(1)}, u32[]{:S(2)}, u32[]{:S(2)}) async-start(bf16[8,3,17,16,128]{4,3,2,1,0:T(8,128)(2,1)} %copy-done.6), calls=%async_computation | async-start | bytes 3342336 | tf_op jit(solution)/shard_map/all_to_all | solution.py:272
  151.5 8.1 %copy-start.4 = (bf16[8,8,2,16,128]{4,3,2,1,0:T(8,128)(2,1)S(1)}, bf16[8,8,2,16,128]{4,3,2,1,0:T(8,128)(2,1)}, u32[]{:S(2)}) copy-start(bf16[8,8,2,16,128]{4,3,2,1,0:T(8,128)(2,1)} %copy-done.3) | copy-start | bytes 1572868
  151.5 8.1 %copy-start.5 = (bf16[8,8,2,16,128]{4,3,2,1,0:T(8,128)(2,1)S(1)}, bf16[8,8,2,16,128]{4,3,2,1,0:T(8,128)(2,1)}, u32[]{:S(2)}) copy-start(bf16[8,8,2,16,128]{4,3,2,1,0:T(8,128)(2,1)} %broadcast_select_fusion.1.refs_2_) | copy-start | bytes 1572868
  151.5 0.7 copy-start.14
  152.3 7.2 %copy-start.18 = (bf16[8,8,2,16,128]{4,3,2,1,0:T(8,128)(2,1)S(1)}, bf16[8,8,2,16,128]{4,3,2,1,0:T(8,128)(2,1)}, u32[]{:S(2)}) copy-start(bf16[8,8,2,16,128]{4,3,2,1,0:T(8,128)(2,1)} %copy-done.17) | copy-start | bytes 1572868
  152.9 17.6 %collective-permute-start.12 = (bf16[2,3,272,128]{3,2,1,0:T(8,128)(2,1)S(1)}, bf16[2,3,272,128]{3,2,1,0:T(8,128)(2,1)S(1)}, u32[]{:S(2)}, u32[]{:S(2)}) collective-permute-start(bf16[2,3,272,128]{3,2,1,0:T(8,128)(2,1)S(1)} %get-tuple-element.29), channel_id=1, source_target_pairs={{0,1},{1,2},{2,3},{3,0},{4,5},{5,6},{6,7},{7,4},{8,9},{9,10},{10,1... | collective-permute-start | bytes 1253384 | tf_op jit(solution)/shard_map/ppermute | solution.py:277
  153.0 35.7 %collective-permute-start.13 = (bf16[2,3,272,128]{3,2,1,0:T(8,128)(2,1)S(1)}, bf16[2,3,272,128]{3,2,1,0:T(8,128)(2,1)S(1)}, u32[]{:S(2)}, u32[]{:S(2)}) collective-permute-start(bf16[2,3,272,128]{3,2,1,0:T(8,128)(2,1)S(1)} %get-tuple-element.30), channel_id=1, source_target_pairs={{0,2},{1,3},{2,0},{3,1},{4,6},{5,7},{6,4},{7,5},{8,10},{9,11},{10,... | collective-permute-start | bytes 1253384 | tf_op jit(solution)/shard_map/ppermute | solution.py:277
  156.4 36.1 %collective-permute-start.14 = (bf16[2,3,272,128]{3,2,1,0:T(8,128)(2,1)S(1)}, bf16[2,3,272,128]{3,2,1,0:T(8,128)(2,1)S(1)}, u32[]{:S(2)}, u32[]{:S(2)}) collective-permute-start(bf16[2,3,272,128]{3,2,1,0:T(8,128)(2,1)S(1)} %get-tuple-element.31), channel_id=1, source_target_pairs={{0,3},{1,0},{2,1},{3,2},{4,7},{5,4},{6,5},{7,6},{8,11},{9,8},{10,9... | collective-permute-start | bytes 1253384 | tf_op jit(solution)/shard_map/ppermute | solution.py:277
  159.5 1.2 copy-start.2
  159.5 1.3 copy-start.8
  159.5 1.4 copy-start.10
  159.5 1.4 copy-start.12

commit v5 on v4

--- a/solution.py
+++ b/solution.py
@@ -15,8 +15,7 @@
 V_DIM = 128
 LANES = 128
 QUERY, KEY, VALUE, OUT = range(4)
-HOLD_PAIRS = 2
-HOLD_CHUNK = 30
+CUT_MICROS = 10
 VMEM_LIMIT = 16 * 1024 * 1024
 
 
@@ -29,7 +28,7 @@
     )
 
 
-def pack(table, param_offsets, owner_map, ways, widths, granule, chunks, waits=()):
+def pack(table, param_offsets, owner_map, ways, widths, granule, chunks):
     layer_count, head_count = owner_map.shape
     per_group = head_count // ways
     steps = [[widths[kind] // granule for kind in kinds] for _, kinds in chunks]
@@ -39,40 +38,31 @@
     ]
 
     def kernel(offsets, owners, source, *refs):
-        targets, taken = refs[len(waits) : -1], refs[-1]
+        targets, (taken, head_at) = refs[:-2], refs[-2:]
         for layer in range(layer_count):
-            first = layer * per_group
-            here = []
-            for target, (items, kinds), step in zip(targets, chunks, steps):
-                low, high = max(items[0], first), min(items[-1] + 1, first + per_group)
-                if low < high:
-                    here.append((target, kinds, step, low - first, high - first, first - items[0]))
-            if not here:
-                continue
             for way in range(ways):
-                taken[way] = 0
-
-            def one_head(head):
+                taken[way] = layer * per_group
+
+            def place(head):
                 way = owners[layer, head]
-                slot = taken[way]
-                taken[way] = slot + 1
-
-                def move(target, kinds, step, shift):
+                item = taken[way]
+                taken[way] = item + 1
+                head_at[item * ways + way] = head
+
+            pl.loop(0, head_count, unroll=min(8, head_count))(place)
+
+        for target, (items, kinds), step in zip(targets, chunks, steps):
+            for at, item in enumerate(items):
+
+                def move(way):
+                    head = head_at[item * ways + way]
                     start = 0
                     for kind, size in zip(kinds, step):
-                        begin = lax.div(offsets[layer, head, kind], jnp.int32(granule))
-                        target[way, slot + shift, pl.ds(start, size)] = source[layer, pl.ds(begin, size)]
+                        begin = lax.div(offsets[item // per_group, head, kind], jnp.int32(granule))
+                        target[way, at, pl.ds(start, size)] = source[item // per_group, pl.ds(begin, size)]
                         start += size
 
-                for target, kinds, step, low, high, shift in here:
-                    if (low, high) == (0, per_group):
-                        move(target, kinds, step, shift)
-                    else:
-                        pl.when(jnp.logical_and(slot >= low, slot < high))(
-                            functools.partial(move, target, kinds, step, shift)
-                        )
-
-            pl.loop(0, head_count, unroll=min(8, head_count))(one_head)
+                pl.loop(0, ways, unroll=min(8, ways))(move)
 
     return pl.pallas_call(
         kernel,
@@ -81,10 +71,12 @@
             pl.BlockSpec(memory_space=pltpu.SMEM),
             pl.BlockSpec(memory_space=pltpu.SMEM),
             pl.BlockSpec(memory_space=pltpu.VMEM),
-        ]
-        + [pl.BlockSpec(memory_space=pl.ANY)] * len(waits),
+        ],
         out_specs=[pl.BlockSpec(memory_space=pltpu.VMEM)] * len(outs),
-        scratch_shapes=[pltpu.SMEM((ways,), jnp.int32)],
+        scratch_shapes=[
+            pltpu.SMEM((ways,), jnp.int32),
+            pltpu.SMEM((layer_count * head_count,), jnp.int32),
+        ],
         compiler_params=pltpu.CompilerParams(vmem_limit_bytes=VMEM_LIMIT),
         cost_estimate=pl.CostEstimate(
             flops=0,
@@ -92,50 +84,39 @@
             bytes_accessed=sum(2 * 2 * math.prod(out.shape) for out in outs),
         ),
         name="pack",
-    )(param_offsets, owner_map, table, *waits)
-
-
-def first_of(x):
-    return lax.slice(x, (0,) * x.ndim, (1,) * x.ndim).reshape(1)
-
-
-def hold(small, waits, micros):
-    def kernel(small_in, *refs):
-        for i in range(small.shape[0]):
-            refs[-1][i] = small_in[i]
+    )(param_offsets, owner_map, table)
+
+
+def cut(rows, slice_map, blocks, shifts, waits, micros):
+    shape = (blocks,) + rows.shape[1:]
+    t_ways = slice_map.shape[1]
+
+    def kernel(mapped, source, *refs):
+        f_me, t_me = lax.axis_index("fsdp"), lax.axis_index("tp")
+        for shift, piece in zip(shifts, refs[len(waits) :]):
+            block = mapped[f_me, lax.rem(t_me + shift, t_ways)]
+            for f in range(blocks):
+                piece[f] = source[block * blocks + f]
+
+    def corner(x):
+        block = (1,) * (x.ndim - 2) + (min(16, x.shape[-2]), LANES)
+        return pl.BlockSpec(block, lambda _: (0,) * x.ndim)
 
     return pl.pallas_call(
         kernel,
-        out_shape=jax.ShapeDtypeStruct(small.shape, small.dtype),
-        in_specs=[pl.BlockSpec(memory_space=pltpu.SMEM)]
-        + [pl.BlockSpec(memory_space=pl.ANY)] * len(waits),
-        out_specs=pl.BlockSpec(memory_space=pltpu.SMEM),
-        cost_estimate=pl.CostEstimate(
-            flops=int(micros * 1.15e9), transcendentals=0, bytes_accessed=0
-        ),
-        name="hold",
-    )(small, *[first_of(x) for x in waits])
-
-
-def cut(rows, targets, blocks, shifts):
-    shape = (blocks,) + rows.shape[1:]
-
-    def kernel(at, source, *pieces):
-        for shift, piece in zip(shifts, pieces):
-            for f in range(blocks):
-                piece[f] = source[at[shift] * blocks + f]
-
-    return pl.pallas_call(
-        kernel,
+        grid=(1,),
         out_shape=[jax.ShapeDtypeStruct(shape, rows.dtype)] * len(shifts),
-        in_specs=[pl.BlockSpec(memory_space=pltpu.SMEM), pl.BlockSpec(memory_space=pltpu.VMEM)],
+        in_specs=[pl.BlockSpec(memory_space=pltpu.SMEM), pl.BlockSpec(memory_space=pltpu.VMEM)]
+        + [corner(x) for x in waits],
         out_specs=[pl.BlockSpec(memory_space=pltpu.VMEM)] * len(shifts),
         compiler_params=pltpu.CompilerParams(vmem_limit_bytes=VMEM_LIMIT),
         cost_estimate=pl.CostEstimate(
-            flops=0, transcendentals=0, bytes_accessed=4 * len(shifts) * math.prod(shape)
+            flops=int(micros * 1.15e9),
+            transcendentals=0,
+            bytes_accessed=4 * len(shifts) * math.prod(shape),
         ),
         name="cut",
-    )(targets, rows)
+    )(slice_map, rows, *waits)
 
 
 def line_step(up, down, axis, ways):
@@ -258,30 +239,25 @@
     row_counts = [width // LANES for width in widths]
 
     me = lax.axis_index("tp")
-    slice_row = lax.dynamic_index_in_dim(slice_map, lax.axis_index("fsdp"), 0, keepdims=False)
     blocks = f_ways // t_ways
     shifts = range(1, t_ways)
-    cuts = [0, item_count * 2 // 8, item_count * 5 // 8, item_count]
-    chunks = [range(low, high) for low, high in zip(cuts, cuts[1:]) if low < high]
-
-    def packed(of, waits=()):
-        waits = [first_of(x) for x in waits]
-        return pack(table, param_offsets, owner_map, f_ways, widths, granule, of, waits)
+    per_chunk = max(1, item_count // 4)
+    chunks = [range(at, min(at + per_chunk, item_count)) for at in range(0, item_count, per_chunk)]
 
     def over_fsdp(x, rows):
         x = lax.all_to_all(x, "fsdp", split_axis=0, concat_axis=0, tiled=True)
         return x.reshape(x.shape[:2] + rows)
 
-    def over_tp(rows, to):
-        return [
-            lax.ppermute(piece, "tp", [(i, (i + shift) % t_ways) for i in range(t_ways)])
-            for shift, piece in zip(shifts, cut(rows, to, blocks, shifts))
-        ]
-
-    (pairs,) = packed([(range(item_count), (KEY, VALUE))])
-    to_send = packed([(items, (QUERY, OUT)) for items in chunks])
+    pairs, *to_send = pack(
+        table,
+        param_offsets,
+        owner_map,
+        f_ways,
+        widths,
+        granule,
+        [(range(item_count), (KEY, VALUE))] + [(items, (QUERY, OUT)) for items in chunks],
+    )
     pairs = over_fsdp(pairs, (2, row_counts[KEY], LANES))
-    targets = jnp.stack([slice_row[lax.rem(me + shift, t_ways)] for shift in range(t_ways)])
     up, down = [pairs], [pairs]
     for _ in shifts:
         above, below = line_step(up[-1], down[-1], "tp", t_ways)
@@ -289,10 +265,16 @@
         down.append(below)
 
     exchanged = []
-    for at, items in enumerate(chunks):
+    for at in range(len(chunks)):
         rows = over_fsdp(to_send[at], (row_counts[QUERY] + row_counts[OUT], LANES))
-        waits = exchanged[at - 1][1] + up[3:] + down[3:] if at else up[1:3] + down[1:3]
-        exchanged.append((rows, over_tp(rows, hold(targets, waits, HOLD_CHUNK if at else HOLD_PAIRS))))
+        waits = exchanged[at - 2][1] if at >= 2 else [up[2:3] + down[2:3], up[3:] + down[3:]][at]
+        pieces = cut(rows, slice_map, blocks, shifts, waits, CUT_MICROS)
+        came = [
+            lax.ppermute(piece, "tp", [(i, (i + shift) % t_ways) for i in range(t_ways)])
+            for shift, piece in zip(shifts, pieces)
+        ]
+        exchanged.append((rows, came))
+    slice_row = lax.dynamic_index_in_dim(slice_map, lax.axis_index("fsdp"), 0, keepdims=False)
     near = [jnp.where(me >= d, up[d], down[t_ways - d]) for d in shifts]
 
     if whole_tiles:
@@ -300,7 +282,7 @@
             jax.ShapeDtypeStruct((item_count, blocks, t_ways, row_counts[kind], KVR), jnp.bfloat16)
             for kind in (QUERY, OUT)
         )
-        where = jnp.stack([me, targets[0]])
+        where = jnp.stack([me, slice_row[me]])
         matrices = assemble(me, [pairs] + near)
         outs = None
         for items, (rows, came) in zip(chunks, exchanged):
@@ -313,7 +295,7 @@
     done = [
         absorb_plain(
             me,
-            lax.dynamic_slice_in_dim(rows, targets[0] * blocks, blocks, 0),
+            lax.dynamic_slice_in_dim(rows, slice_row[me] * blocks, blocks, 0),
             came,
             matrices[items[0] : items[-1] + 1],
         )

time: 199 us -> 174 us (0.87)
  local copies, waits for them, and re-layouts: 22.4 us -> 10.6 us
  Pallas kernels: 36.6 us -> 28.8 us
  waiting for transfers between devices: 71.7 us -> 65.7 us
  starting transfers between devices: 46.2 us -> 51.4 us
  other arithmetic: 6.98 us -> 3.53 us
    ppermute x9 -> x12, waiting for transfers between devices: 63.1 us -> 32.7 us  [per_device(): lax.ppermute(piece, 'tp', [(i, (i + shift) % t_ways) for i in range(t_way...]
    all_to_all x3 -> x4, waiting for transfers between devices: 0.01 us -> 21.4 us  [over_fsdp(): x = lax.all_to_all(x, 'fsdp', split_axis=0, concat_axis=0, tiled=True)]
    slice x12 -> x0, local copies, waits for them, and re-layouts: 11.2 us -> none  [first_of(): return lax.slice(x, (0,) * x.ndim, (1,) * x.ndim).reshape(1)]
    pallas_call x6 -> x4, Pallas kernels: 14.9 us -> 6.47 us  [cut(): pl.pallas_call(kernel, grid=(1,), out_shape=[jax.ShapeDtypeStruct(shape,...]
    all_to_all x3 -> x4, starting transfers between devices: 13.4 us -> 19.1 us  [over_fsdp(): x = lax.all_to_all(x, 'fsdp', split_axis=0, concat_axis=0, tiled=True)]
    pallas_call x3 -> x4, Pallas kernels: 14.3 us -> 17.8 us  [absorb(): pl.pallas_call(kernel, grid_spec=pltpu.PrefetchScalarGridSpec(num_scalar_...]
    another operation x2 -> x1, other arithmetic: 3.92 us -> 0.69 us  [per_device(): where = jnp.stack([me, slice_row[me]])]
    ppermute x3, waiting for transfers between devices: 8.59 us -> 11.7 us  [line_step(): lax.ppermute(up, axis, [(i, i + 1) for i in range(ways - 1)])]
  transfers between devices with their start and end apart: 18 -> 22, of which waited for: 8 -> 10; matrix products, arithmetic and copies ran while one was open for 10% -> 2% of each run, Pallas kernels for 14% -> 12%
where the time goes in v5:
time: 174 us; the launch traced here: 173 us
  waiting for transfers between devices  65.7 us (38%)
  starting transfers between devices  51.4 us (30%)
  Pallas kernels  28.8 us (17%)
  blocking collectives  12.3 us (7%)
  local copies, waits for them, and re-layouts  10.6 us (6%)
  other arithmetic  3.53 us (2%)
    ppermute x12, waiting for transfers between devices, per_device(): lax.ppermute(piece, 'tp', [(i, (i + shift) % t_ways) for i in range(t_way...  32.7 us
    all_to_all x4, waiting for transfers between devices, over_fsdp(): x = lax.all_to_all(x, 'fsdp', split_axis=0, concat_axis=0, tiled=True)  21.4 us
    all_to_all x4, starting transfers between devices, over_fsdp(): x = lax.all_to_all(x, 'fsdp', split_axis=0, concat_axis=0, tiled=True)  19.1 us
    pallas_call x4, Pallas kernels, absorb(): pl.pallas_call(kernel, grid_spec=pltpu.PrefetchScalarGridSpec(num_scalar_...  17.8 us
    ppermute x12, starting transfers between devices, per_device(): lax.ppermute(piece, 'tp', [(i, (i + shift) % t_ways) for i in range(t_way...  13.2 us
    all_to_all x1, blocking collectives, over_fsdp(): x = lax.all_to_all(x, 'fsdp', split_axis=0, concat_axis=0, tiled=True)  12.3 us
    ppermute x3, waiting for transfers between devices, line_step(): lax.ppermute(up, axis, [(i, i + 1) for i in range(ways - 1)])  11.7 us
    ppermute x3, starting transfers between devices, line_step(): lax.ppermute(up, axis, [(i, i + 1) for i in range(ways - 1)])  10.4 us
  transfers between devices with their start and end apart: 22, of which 10 were waited for; matrix products, arithmetic and copies ran while one was open for 2% of the time, Pallas kernels for 12%

profile of v5, /device:TPU:10, one launch (start us, length us, event | category | flops | bytes accessed | tf_op | source)
XLA Modules:
  0.0 173.3 jit_solution(6053634480030895636)
XLA Ops:
  0.6 4.6 %copy.17 = bf16[1,2,9728,128]{3,2,1,0:T(8,128)(2,1)} copy(bf16[1,2,9728,128]{3,1,2,0:T(2,128)(2,1)} %bitcast.20) | data formatting | bytes 9961472
  5.3 0.1 copy.12.offsets
  5.4 0.0 copy-start
  5.4 2.4 %copy-done = bf16[1,2,9728,128]{3,2,1,0:T(8,128)(2,1)S(1)} copy-done((bf16[1,2,9728,128]{3,2,1,0:T(8,128)(2,1)S(1)}, bf16[1,2,9728,128]{3,2,1,0:T(8,128)(2,1)}, u32[]{:S(2)}) %copy-start) | copy-done | bytes 4980760
  7.8 3.5 %pack.1 = (bf16[8,8,2,16,128]{4,3,2,1,0:T(8,128)(2,1)S(1)}, bf16[8,2,17,16,128]{4,3,2,1,0:T(8,128)(2,1)}, bf16[8,2,17,16,128]{4,3,2,1,0:T(8,128)(2,1)}, bf16[8,2...) custom-call(s32[2,32,4]{2,1,0:T(8,128)S(1)} %copy.12.offsets, s32[2,32]{1,0:T(2,128)S(1)} %copy-done.7, ...), custom_call_target="tpu_custom_call" | custom-call | bytes 9961472 | tf_op jit(solution)/shard_map/pack/pallas_call | solution.py:67
  11.3 1.0 copy-done.5
  12.3 1.0 copy-done.6
  13.3 12.3 %all_to_all.25.refs_0_ = bf16[8,8,2,16,128]{4,3,2,1,0:T(8,128)(2,1)S(1)} all-to-all(bf16[8,8,2,16,128]{4,3,2,1,0:T(8,128)(2,1)S(1)} %get-tuple-element.29), channel_id=1, replica_groups=mesh['fsdp'=8,'tp'=4] {'fsdp'}, dimensions={0} | all-to-all | bytes 1048576 | tf_op jit(solution)/shard_map/all_to_all | solution.py:248
  25.6 3.5 %collective-permute-start = (bf16[8,8,2,16,128]{4,3,2,1,0:T(8,128)(2,1)S(1)}, bf16[8,8,2,16,128]{4,3,2,1,0:T(8,128)(2,1)S(1)}, u32[]{:S(2)}, u32[]{:S(2)}) collective-permute-start(bf16[8,8,2,16,128]{4,3,2,1,0:T(8,128)(2,1)S(1)} %all_to_all.25.refs_0_), channel_id=1, source_target_pairs={{0,1},{1,2},{2,3},{4,5},{5,6},{6,7},{8,9},{9,10},{10,11},{12,13},{... | collective-permute-start | bytes 1572872 | tf_op jit(solution)/shard_map/ppermute | solution.py:124
  29.1 2.4 %collective-permute-start.3 = (bf16[8,8,2,16,128]{4,3,2,1,0:T(8,128)(2,1)S(1)}, bf16[8,8,2,16,128]{4,3,2,1,0:T(8,128)(2,1)S(1)}, u32[]{:S(2)}, u32[]{:S(2)}) collective-permute-start(bf16[8,8,2,16,128]{4,3,2,1,0:T(8,128)(2,1)S(1)} %all_to_all.25.refs_0_), channel_id=1, source_target_pairs={{1,0},{2,1},{3,2},{5,4},{6,5},{7,6},{9,8},{10,9},{11,10},{13,12},{... | collective-permute-start | bytes 1572872 | tf_op jit(solution)/shard_map/ppermute | solution.py:125
  31.5 4.9 %all-to-all-start.4 = ((bf16[8,2,17,16,128]{4,3,2,1,0:T(8,128)(2,1)}), bf16[8,2,17,16,128]{4,3,2,1,0:T(8,128)(2,1)S(1)}, u32[]{:S(2)}, u32[]{:S(2)}) async-start(bf16[8,2,17,16,128]{4,3,2,1,0:T(8,128)(2,1)} %get-tuple-element.37), calls=%async_computation.4 | async-start | bytes 2228224 | tf_op jit(solution)/shard_map/all_to_all | solution.py:248
  36.4 4.8 %collective-permute-done = bf16[8,8,2,16,128]{4,3,2,1,0:T(8,128)(2,1)S(1)} collective-permute-done((bf16[8,8,2,16,128]{4,3,2,1,0:T(8,128)(2,1)S(1)}, bf16[8,8,2,16,128]{4,3,2,1,0:T(8,128)(2,1)S(1)}, u32[]{:S(2)}, u32[]{:S(2)}) %collective-permute-start) | collective-permute-done | bytes 524320 | tf_op jit(solution)/shard_map/ppermute | solution.py:124
  41.3 3.5 %collective-permute-start.1 = (bf16[8,8,2,16,128]{4,3,2,1,0:T(8,128)(2,1)S(1)}, bf16[8,8,2,16,128]{4,3,2,1,0:T(8,128)(2,1)}, u32[]{:S(2)}, u32[]{:S(2)}) collective-permute-start(bf16[8,8,2,16,128]{4,3,2,1,0:T(8,128)(2,1)S(1)} %collective-permute-done), channel_id=1, source_target_pairs={{0,1},{1,2},{2,3},{4,5},{5,6},{6,7},{8,9},{9,10},{10,11},{12,13},{... | collective-permute-start | bytes 1572872 | tf_op jit(solution)/shard_map/ppermute | solution.py:124
  44.7 0.0 collective-permute-done.3
  44.8 3.1 %collective-permute-start.4 = (bf16[8,8,2,16,128]{4,3,2,1,0:T(8,128)(2,1)S(1)}, bf16[8,8,2,16,128]{4,3,2,1,0:T(8,128)(2,1)}, u32[]{:S(2)}, u32[]{:S(2)}) collective-permute-start(bf16[8,8,2,16,128]{4,3,2,1,0:T(8,128)(2,1)S(1)} %collective-permute-done.3), channel_id=1, source_target_pairs={{1,0},{2,1},{3,2},{5,4},{6,5},{7,6},{9,8},{10,9},{11,10},{13,12},{... | collective-permute-start | bytes 1572872 | tf_op jit(solution)/shard_map/ppermute | solution.py:125
  47.9 0.1 copy.14.mapped
  48.0 0.6 dynamic_slice.7
  48.6 0.7 pad_add_fusion.at
  49.3 6.8 %collective-permute-done.1.refs_0_ = bf16[8,8,2,16,128]{4,3,2,1,0:T(8,128)(2,1)} collective-permute-done((bf16[8,8,2,16,128]{4,3,2,1,0:T(8,128)(2,1)S(1)}, bf16[8,8,2,16,128]{4,3,2,1,0:T(8,128)(2,1)}, u32[]{:S(2)}, u32[]{:S(2)}) %collective-permute-start.1) | collective-permute-done | bytes 524320 | tf_op jit(solution)/shard_map/ppermute | solution.py:124
  56.1 3.5 %collective-permute-start.2 = (bf16[8,8,2,16,128]{4,3,2,1,0:T(8,128)(2,1)}, bf16[8,8,2,16,128]{4,3,2,1,0:T(8,128)(2,1)}, u32[]{:S(2)}, u32[]{:S(2)}) collective-permute-start(bf16[8,8,2,16,128]{4,3,2,1,0:T(8,128)(2,1)} %collective-permute-done.1.refs_0_), channel_id=1, source_target_pairs={{0,1},{1,2},{2,3},{4,5},{5,6},{6,7},{8,9},{9,10},{10,11},{12,13},{... | collective-permute-start | bytes 1572872 | tf_op jit(solution)/shard_map/ppermute | solution.py:124
  59.6 0.0 collective-permute-done.4.refs_1_
  59.6 3.1 %collective-permute-start.5 = (bf16[8,8,2,16,128]{4,3,2,1,0:T(8,128)(2,1)}, bf16[8,8,2,16,128]{4,3,2,1,0:T(8,128)(2,1)}, u32[]{:S(2)}, u32[]{:S(2)}) collective-permute-start(bf16[8,8,2,16,128]{4,3,2,1,0:T(8,128)(2,1)} %collective-permute-done.4.refs_1_), channel_id=1, source_target_pairs={{1,0},{2,1},{3,2},{5,4},{6,5},{7,6},{9,8},{10,9},{11,10},{13,12},{... | collective-permute-start | bytes 1572872 | tf_op jit(solution)/shard_map/ppermute | solution.py:125
  62.8 0.0 all-to-all-done.4
  62.8 3.5 %all-to-all-start.1 = ((bf16[8,2,17,16,128]{4,3,2,1,0:T(8,128)(2,1)}), bf16[8,2,17,16,128]{4,3,2,1,0:T(8,128)(2,1)S(1)}, u32[]{:S(2)}, u32[]{:S(2)}) async-start(bf16[8,2,17,16,128]{4,3,2,1,0:T(8,128)(2,1)} %get-tuple-element.28), calls=%async_computation.1 | async-start | bytes 2228224 | tf_op jit(solution)/shard_map/all_to_all | solution.py:248
  66.3 1.7 cut.6
  68.0 0.8 collective-permute-start.12
  68.8 1.8 %collective-permute-start.13 = (bf16[2,2,272,128]{3,2,1,0:T(8,128)(2,1)}, bf16[2,2,272,128]{3,2,1,0:T(8,128)(2,1)}, u32[]{:S(2)}, u32[]{:S(2)}) collective-permute-start(bf16[2,2,272,128]{3,2,1,0:T(8,128)(2,1)} %get-tuple-element.39), channel_id=1, source_target_pairs={{0,2},{1,3},{2,0},{3,1},{4,6},{5,7},{6,4},{7,5},{8,10},{9,11},{10,... | collective-permute-start | bytes 835592 | tf_op jit(solution)/shard_map/ppermute | solution.py:273
  70.6 2.0 %collective-permute-start.14 = (bf16[2,2,272,128]{3,2,1,0:T(8,128)(2,1)}, bf16[2,2,272,128]{3,2,1,0:T(8,128)(2,1)}, u32[]{:S(2)}, u32[]{:S(2)}) collective-permute-start(bf16[2,2,272,128]{3,2,1,0:T(8,128)(2,1)} %get-tuple-element.40), channel_id=1, source_target_pairs={{0,3},{1,0},{2,1},{3,2},{4,7},{5,4},{6,5},{7,6},{8,11},{9,8},{10,9... | collective-permute-start | bytes 835592 | tf_op jit(solution)/shard_map/ppermute | solution.py:273
  72.6 1.9 %broadcast_select_fusion.1.refs_2_ = bf16[8,8,2,16,128]{4,3,2,1,0:T(8,128)(2,1)} fusion(bf16[8,8,2,16,128]{4,3,2,1,0:T(8,128)(2,1)} %collective-permute-done.1.refs_0_, bf16[8,8,2,16,128]{4,3,2,1,0:T(8,128)(2,1)} %collective-permute-done.4.refs_1_, pred[]{:T(512)S(6)} %ge.10), kind=kLoop, calls=%fused_computation.1 | loop fusion | flops 262144 | bytes 1572865 | tf_op jit(solution)/shard_map/jit(_where)/select_n | solution.py:278
  74.5 6.3 %all-to-all-done.1 = bf16[8,2,17,16,128]{4,3,2,1,0:T(8,128)(2,1)S(1)} async-done(((bf16[8,2,17,16,128]{4,3,2,1,0:T(8,128)(2,1)}), bf16[8,2,17,16,128]{4,3,2,1,0:T(8,128)(2,1)S(1)}, u32[]{:S(2)}, u32[]{:S(2)}) %all-to-all-start.1) | async-done | bytes 1114144 | tf_op jit(solution)/shard_map/all_to_all | solution.py:248
  80.8 5.0 %all-to-all-start.3 = ((bf16[8,2,17,16,128]{4,3,2,1,0:T(8,128)(2,1)}), bf16[8,2,17,16,128]{4,3,2,1,0:T(8,128)(2,1)S(1)}, u32[]{:S(2)}, u32[]{:S(2)}) async-start(bf16[8,2,17,16,128]{4,3,2,1,0:T(8,128)(2,1)} %copy-done.6), calls=%async_computation.3 | async-start | bytes 2228224 | tf_op jit(solution)/shard_map/all_to_all | solution.py:248
  85.8 0.0 collective-permute-done.2.refs_0_
  85.8 1.6 cut.4
  87.4 0.7 copy-done.8
  88.2 0.8 collective-permute-start.6
  89.0 1.8 %collective-permute-start.7 = (bf16[2,2,272,128]{3,2,1,0:T(8,128)(2,1)}, bf16[2,2,272,128]{3,2,1,0:T(8,128)(2,1)}, u32[]{:S(2)}, u32[]{:S(2)}) collective-permute-start(bf16[2,2,272,128]{3,2,1,0:T(8,128)(2,1)} %get-tuple-element.31), channel_id=1, source_target_pairs={{0,2},{1,3},{2,0},{3,1},{4,6},{5,7},{6,4},{7,5},{8,10},{9,11},{10,... | collective-permute-start | bytes 835592 | tf_op jit(solution)/shard_map/ppermute | solution.py:273
  90.7 9.7 %all-to-all-done.3 = bf16[8,2,17,16,128]{4,3,2,1,0:T(8,128)(2,1)S(1)} async-done(((bf16[8,2,17,16,128]{4,3,2,1,0:T(8,128)(2,1)}), bf16[8,2,17,16,128]{4,3,2,1,0:T(8,128)(2,1)S(1)}, u32[]{:S(2)}, u32[]{:S(2)}) %all-to-all-start.3) | async-done | bytes 1114144 | tf_op jit(solution)/shard_map/all_to_all | solution.py:248
  100.4 5.6 %all-to-all-start = ((bf16[8,2,17,16,128]{4,3,2,1,0:T(8,128)(2,1)}), bf16[8,2,17,16,128]{4,3,2,1,0:T(8,128)(2,1)}, u32[]{:S(2)}, u32[]{:S(2)}) async-start(bf16[8,2,17,16,128]{4,3,2,1,0:T(8,128)(2,1)} %copy-done.5), calls=%async_computation | async-start | bytes 2228224 | tf_op jit(solution)/shard_map/all_to_all | solution.py:248
  106.1 0.0 collective-permute-done.12.refs_0_.refs_1_
  106.1 0.0 collective-permute-start.8
  106.1 0.0 collective-permute-done.13.refs_1_.refs_2_
  106.1 4.7 %collective-permute-done.14.refs_2_.refs_3_ = bf16[2,2,272,128]{3,2,1,0:T(8,128)(2,1)} collective-permute-done((bf16[2,2,272,128]{3,2,1,0:T(8,128)(2,1)}, bf16[2,2,272,128]{3,2,1,0:T(8,128)(2,1)}, u32[]{:S(2)}, u32[]{:S(2)}) %collective-permute-start.14) | collective-permute-done | bytes 278560 | tf_op jit(solution)/shard_map/ppermute | solution.py:273
  110.8 1.7 cut.7
  112.5 0.0 collective-permute-start.15
  112.5 1.7 collective-permute-start.16
  114.2 0.9 broadcast_select_fusion.refs_3_
  115.1 0.0 collective-permute-done.6.refs_0_.refs_1_
  115.1 0.3 collective-permute-start.17
  115.5 5.4 %all-to-all-done = bf16[8,2,17,16,128]{4,3,2,1,0:T(8,128)(2,1)} async-done(((bf16[8,2,17,16,128]{4,3,2,1,0:T(8,128)(2,1)}), bf16[8,2,17,16,128]{4,3,2,1,0:T(8,128)(2,1)}, u32[]{:S(2)}, u32[]{:S(2)}) %all-to-all-start) | async-done | bytes 1114144 | tf_op jit(solution)/shard_map/all_to_all | solution.py:248
  120.8 13.9 %collective-permute-done.8.refs_2_.refs_3_ = bf16[2,2,272,128]{3,2,1,0:T(8,128)(2,1)} collective-permute-done((bf16[2,2,272,128]{3,2,1,0:T(8,128)(2,1)}, bf16[2,2,272,128]{3,2,1,0:T(8,128)(2,1)}, u32[]{:S(2)}, u32[]{:S(2)}) %collective-permute-start.8) | collective-permute-done | bytes 278560 | tf_op jit(solution)/shard_map/ppermute | solution.py:273
  134.7 1.5 cut.5
  136.2 0.1 collective-permute-start.10
  136.3 1.0 collective-permute-start.11
  137.3 8.1 %collective-permute-done.15.refs_1_ = bf16[2,2,272,128]{3,2,1,0:T(8,128)(2,1)} collective-permute-done((bf16[2,2,272,128]{3,2,1,0:T(8,128)(2,1)}, bf16[2,2,272,128]{3,2,1,0:T(8,128)(2,1)}, u32[]{:S(2)}, u32[]{:S(2)}) %collective-permute-start.15) | collective-permute-done | bytes 278560 | tf_op jit(solution)/shard_map/ppermute | solution.py:273
  145.4 3.0 %collective-permute-start.9 = (bf16[2,2,272,128]{3,2,1,0:T(8,128)(2,1)S(1)}, bf16[2,2,272,128]{3,2,1,0:T(8,128)(2,1)S(1)}, u32[]{:S(2)}, u32[]{:S(2)}) collective-permute-start(bf16[2,2,272,128]{3,2,1,0:T(8,128)(2,1)S(1)} %get-tuple-element.33), channel_id=1, source_target_pairs={{0,1},{1,2},{2,3},{3,0},{4,5},{5,6},{6,7},{7,4},{8,9},{9,10},{10,1... | collective-permute-start | bytes 835592 | tf_op jit(solution)/shard_map/ppermute | solution.py:273
  148.4 0.1 broadcast_select_fusion.2.refs_1_
  148.5 1.1 assemble.1.refs_4_
  149.6 4.5 %absorb.4 = (bf16[8,2,4,48,512]{4,3,2,1,0:T(8,128)(2,1)}, bf16[8,2,4,224,512]{4,3,2,1,0:T(8,128)(2,1)}) custom-call(s32[2]{0:T(128)S(1)} %pad_add_fusion.at, bf16[8,2,272,128]{3,2,1,0:T(8,128)(2,1)S(1)} %bitcast.13, bf16[2,2,272,128]{3,2,1,0:T(8,128)(2,1)} %collective-permute-done.12.refs_0_.refs_1_, ...), custom_call_target="tpu_custom_call" | custom-call | flops 570425344 | bytes 5570560 | tf_op jit(solution)/shard_map/absorb/pallas_call | solution.py:193
  154.1 4.5 %absorb.5 = (bf16[8,2,4,48,512]{4,3,2,1,0:T(8,128)(2,1)}, bf16[8,2,4,224,512]{4,3,2,1,0:T(8,128)(2,1)}) custom-call(s32[2]{0:T(128)S(1)} %pad_add_fusion.at, bf16[8,2,272,128]{3,2,1,0:T(8,128)(2,1)S(1)} %bitcast.15, bf16[2,2,272,128]{3,2,1,0:T(8,128)(2,1)} %collective-permute-done.6.refs_0_.refs_1_, ...), custom_call_target="tpu_custom_call", output_to_operand_aliasing={{0}: (6, {}), {1}: (7, {})} | custom-call | flops 570425344 | bytes 5570560 | tf_op jit(solution)/shard_map/absorb/pallas_call | solution.py:193
  158.5 0.0 collective-permute-done.16.refs_2_
  158.6 0.1 collective-permute-done.17.refs_3_
  158.6 4.5 %absorb.6 = (bf16[8,2,4,48,512]{4,3,2,1,0:T(8,128)(2,1)}, bf16[8,2,4,224,512]{4,3,2,1,0:T(8,128)(2,1)}) custom-call(s32[2]{0:T(128)S(1)} %pad_add_fusion.at, bf16[8,2,272,128]{3,2,1,0:T(8,128)(2,1)S(1)} %bitcast.17, bf16[2,2,272,128]{3,2,1,0:T(8,128)(2,1)} %collective-permute-done.15.refs_1_, ...), custom_call_target="tpu_custom_call", output_to_operand_aliasing={{0}: (6, {}), {1}: (7, {})} | custom-call | flops 570425344 | bytes 5570560 | tf_op jit(solution)/shard_map/absorb/pallas_call | solution.py:193
  163.1 5.9 %collective-permute-done.11.refs_3_ = bf16[2,2,272,128]{3,2,1,0:T(8,128)(2,1)S(1)} collective-permute-done((bf16[2,2,272,128]{3,2,1,0:T(8,128)(2,1)S(1)}, bf16[2,2,272,128]{3,2,1,0:T(8,128)(2,1)S(1)}, u32[]{:S(2)}, u32[]{:S(2)}) %collective-permute-start.11) | collective-permute-done | bytes 278560 | tf_op jit(solution)/shard_map/ppermute | solution.py:273
  169.0 4.3 %absorb.7 = (bf16[8,2,4,48,512]{4,3,2,1,0:T(8,128)(2,1)}, bf16[8,2,4,224,512]{4,3,2,1,0:T(8,128)(2,1)}) custom-call(s32[2]{0:T(128)S(1)} %pad_add_fusion.at, bf16[8,2,272,128]{3,2,1,0:T(8,128)(2,1)} %bitcast.2.source.refs_0_, bf16[2,2,272,128]{3,2,1,0:T(8,128)(2,1)S(1)} %collective-permute-done.9.refs_1_, ...), custom_call_target="tpu_custom_call", output_to_operand_aliasing={{0}: (6, {}), {1}: (7, {})} | custom-call | flops 570425344 | bytes 5570560 | tf_op jit(solution)/shard_map/absorb/pallas_call | solution.py:193
  (29 shorter events, 0.1 us)
Async XLA Ops:
  0.6 4.6 %copy-start.13 = (s32[2,32,4]{1,2,0:T(4,128)S(1)}, s32[2,32,4]{1,2,0:T(4,128)}, u32[]{:S(2)}) copy-start(s32[2,32,4]{1,2,0:T(4,128)} %param.5) | copy-start | bytes 3076
  0.6 4.7 %copy-start.7 = (s32[2,32]{1,0:T(2,128)S(1)}, s32[2,32]{1,0:T(2,128)}, u32[]{:S(2)}) copy-start(s32[2,32]{1,0:T(2,128)} %owners.1) | copy-start | bytes 772
  5.4 2.4 %copy-start = (bf16[1,2,9728,128]{3,2,1,0:T(8,128)(2,1)S(1)}, bf16[1,2,9728,128]{3,2,1,0:T(8,128)(2,1)}, u32[]{:S(2)}) copy-start(bf16[1,2,9728,128]{3,2,1,0:T(8,128)(2,1)} %copy.17) | copy-start | bytes 14942212
  7.8 40.1 %copy-start.14 = (s32[8,4]{0,1:T(4,128)S(1)}, s32[8,4]{0,1:T(4,128)}, u32[]{:S(2)}) copy-start(s32[8,4]{0,1:T(4,128)} %param.7) | copy-start | bytes 388
  11.3 1.0 copy-start.5
  12.3 1.0 copy-start.6
  25.6 37.2 %copy-start.1 = (bf16[8,8,2,16,128]{4,3,2,1,0:T(8,128)(2,1)}, bf16[8,8,2,16,128]{4,3,2,1,0:T(8,128)(2,1)S(1)}, u32[]{:S(2)}) copy-start(bf16[8,8,2,16,128]{4,3,2,1,0:T(8,128)(2,1)S(1)} %all_to_all.25.refs_0_) | copy-start | bytes 1572868
  25.6 15.6 %collective-permute-start = (bf16[8,8,2,16,128]{4,3,2,1,0:T(8,128)(2,1)S(1)}, bf16[8,8,2,16,128]{4,3,2,1,0:T(8,128)(2,1)S(1)}, u32[]{:S(2)}, u32[]{:S(2)}) collective-permute-start(bf16[8,8,2,16,128]{4,3,2,1,0:T(8,128)(2,1)S(1)} %all_to_all.25.refs_0_), channel_id=1, source_target_pairs={{0,1},{1,2},{2,3},{4,5},{5,6},{6,7},{8,9},{9,10},{10,11},{12,13},{... | collective-permute-start | bytes 1572872 | tf_op jit(solution)/shard_map/ppermute | solution.py:124
  29.1 15.6 %collective-permute-start.3 = (bf16[8,8,2,16,128]{4,3,2,1,0:T(8,128)(2,1)S(1)}, bf16[8,8,2,16,128]{4,3,2,1,0:T(8,128)(2,1)S(1)}, u32[]{:S(2)}, u32[]{:S(2)}) collective-permute-start(bf16[8,8,2,16,128]{4,3,2,1,0:T(8,128)(2,1)S(1)} %all_to_all.25.refs_0_), channel_id=1, source_target_pairs={{1,0},{2,1},{3,2},{5,4},{6,5},{7,6},{9,8},{10,9},{11,10},{13,12},{... | collective-permute-start | bytes 1572872 | tf_op jit(solution)/shard_map/ppermute | solution.py:125
  31.5 31.3 %all-to-all-start.4 = ((bf16[8,2,17,16,128]{4,3,2,1,0:T(8,128)(2,1)}), bf16[8,2,17,16,128]{4,3,2,1,0:T(8,128)(2,1)S(1)}, u32[]{:S(2)}, u32[]{:S(2)}) async-start(bf16[8,2,17,16,128]{4,3,2,1,0:T(8,128)(2,1)} %get-tuple-element.37), calls=%async_computation.4 | async-start | bytes 2228224 | tf_op jit(solution)/shard_map/all_to_all | solution.py:248
  41.3 21.5 %copy-start.9 = (bf16[8,8,2,16,128]{4,3,2,1,0:T(8,128)(2,1)}, bf16[8,8,2,16,128]{4,3,2,1,0:T(8,128)(2,1)S(1)}, u32[]{:S(2)}) copy-start(bf16[8,8,2,16,128]{4,3,2,1,0:T(8,128)(2,1)S(1)} %collective-permute-done) | copy-start | bytes 1572868
  41.3 14.9 %collective-permute-start.1 = (bf16[8,8,2,16,128]{4,3,2,1,0:T(8,128)(2,1)S(1)}, bf16[8,8,2,16,128]{4,3,2,1,0:T(8,128)(2,1)}, u32[]{:S(2)}, u32[]{:S(2)}) collective-permute-start(bf16[8,8,2,16,128]{4,3,2,1,0:T(8,128)(2,1)S(1)} %collective-permute-done), channel_id=1, source_target_pairs={{0,1},{1,2},{2,3},{4,5},{5,6},{6,7},{8,9},{9,10},{10,11},{12,13},{... | collective-permute-start | bytes 1572872 | tf_op jit(solution)/shard_map/ppermute | solution.py:124
  44.7 18.1 %copy-start.11 = (bf16[8,8,2,16,128]{4,3,2,1,0:T(8,128)(2,1)}, bf16[8,8,2,16,128]{4,3,2,1,0:T(8,128)(2,1)S(1)}, u32[]{:S(2)}) copy-start(bf16[8,8,2,16,128]{4,3,2,1,0:T(8,128)(2,1)S(1)} %collective-permute-done.3) | copy-start | bytes 1572868
  44.8 14.9 %collective-permute-start.4 = (bf16[8,8,2,16,128]{4,3,2,1,0:T(8,128)(2,1)S(1)}, bf16[8,8,2,16,128]{4,3,2,1,0:T(8,128)(2,1)}, u32[]{:S(2)}, u32[]{:S(2)}) collective-permute-start(bf16[8,8,2,16,128]{4,3,2,1,0:T(8,128)(2,1)S(1)} %collective-permute-done.3), channel_id=1, source_target_pairs={{1,0},{2,1},{3,2},{5,4},{6,5},{7,6},{9,8},{10,9},{11,10},{13,12},{... | collective-permute-start | bytes 1572872 | tf_op jit(solution)/shard_map/ppermute | solution.py:125
  56.1 29.7 %collective-permute-start.2 = (bf16[8,8,2,16,128]{4,3,2,1,0:T(8,128)(2,1)}, bf16[8,8,2,16,128]{4,3,2,1,0:T(8,128)(2,1)}, u32[]{:S(2)}, u32[]{:S(2)}) collective-permute-start(bf16[8,8,2,16,128]{4,3,2,1,0:T(8,128)(2,1)} %collective-permute-done.1.refs_0_), channel_id=1, source_target_pairs={{0,1},{1,2},{2,3},{4,5},{5,6},{6,7},{8,9},{9,10},{10,11},{12,13},{... | collective-permute-start | bytes 1572872 | tf_op jit(solution)/shard_map/ppermute | solution.py:124
  59.6 26.2 %collective-permute-start.5 = (bf16[8,8,2,16,128]{4,3,2,1,0:T(8,128)(2,1)}, bf16[8,8,2,16,128]{4,3,2,1,0:T(8,128)(2,1)}, u32[]{:S(2)}, u32[]{:S(2)}) collective-permute-start(bf16[8,8,2,16,128]{4,3,2,1,0:T(8,128)(2,1)} %collective-permute-done.4.refs_1_), channel_id=1, source_target_pairs={{1,0},{2,1},{3,2},{5,4},{6,5},{7,6},{9,8},{10,9},{11,10},{13,12},{... | collective-permute-start | bytes 1572872 | tf_op jit(solution)/shard_map/ppermute | solution.py:125
  62.8 18.0 %all-to-all-start.1 = ((bf16[8,2,17,16,128]{4,3,2,1,0:T(8,128)(2,1)}), bf16[8,2,17,16,128]{4,3,2,1,0:T(8,128)(2,1)S(1)}, u32[]{:S(2)}, u32[]{:S(2)}) async-start(bf16[8,2,17,16,128]{4,3,2,1,0:T(8,128)(2,1)} %get-tuple-element.28), calls=%async_computation.1 | async-start | bytes 2228224 | tf_op jit(solution)/shard_map/all_to_all | solution.py:248
  68.0 38.1 %collective-permute-start.12 = (bf16[2,2,272,128]{3,2,1,0:T(8,128)(2,1)}, bf16[2,2,272,128]{3,2,1,0:T(8,128)(2,1)}, u32[]{:S(2)}, u32[]{:S(2)}) collective-permute-start(bf16[2,2,272,128]{3,2,1,0:T(8,128)(2,1)} %get-tuple-element.38), channel_id=1, source_target_pairs={{0,1},{1,2},{2,3},{3,0},{4,5},{5,6},{6,7},{7,4},{8,9},{9,10},{10,1... | collective-permute-start | bytes 835592 | tf_op jit(solution)/shard_map/ppermute | solution.py:273
  68.8 37.3 %collective-permute-start.13 = (bf16[2,2,272,128]{3,2,1,0:T(8,128)(2,1)}, bf16[2,2,272,128]{3,2,1,0:T(8,128)(2,1)}, u32[]{:S(2)}, u32[]{:S(2)}) collective-permute-start(bf16[2,2,272,128]{3,2,1,0:T(8,128)(2,1)} %get-tuple-element.39), channel_id=1, source_target_pairs={{0,2},{1,3},{2,0},{3,1},{4,6},{5,7},{6,4},{7,5},{8,10},{9,11},{10,... | collective-permute-start | bytes 835592 | tf_op jit(solution)/shard_map/ppermute | solution.py:273
  70.6 40.2 %collective-permute-start.14 = (bf16[2,2,272,128]{3,2,1,0:T(8,128)(2,1)}, bf16[2,2,272,128]{3,2,1,0:T(8,128)(2,1)}, u32[]{:S(2)}, u32[]{:S(2)}) collective-permute-start(bf16[2,2,272,128]{3,2,1,0:T(8,128)(2,1)} %get-tuple-element.40), channel_id=1, source_target_pairs={{0,3},{1,0},{2,1},{3,2},{4,7},{5,4},{6,5},{7,6},{8,11},{9,8},{10,9... | collective-permute-start | bytes 835592 | tf_op jit(solution)/shard_map/ppermute | solution.py:273
  80.8 19.6 %all-to-all-start.3 = ((bf16[8,2,17,16,128]{4,3,2,1,0:T(8,128)(2,1)}), bf16[8,2,17,16,128]{4,3,2,1,0:T(8,128)(2,1)S(1)}, u32[]{:S(2)}, u32[]{:S(2)}) async-start(bf16[8,2,17,16,128]{4,3,2,1,0:T(8,128)(2,1)} %copy-done.6), calls=%async_computation.3 | async-start | bytes 2228224 | tf_op jit(solution)/shard_map/all_to_all | solution.py:248
  87.4 0.7 copy-start.8
  88.2 27.0 %collective-permute-start.6 = (bf16[2,2,272,128]{3,2,1,0:T(8,128)(2,1)}, bf16[2,2,272,128]{3,2,1,0:T(8,128)(2,1)}, u32[]{:S(2)}, u32[]{:S(2)}) collective-permute-start(bf16[2,2,272,128]{3,2,1,0:T(8,128)(2,1)} %get-tuple-element.30), channel_id=1, source_target_pairs={{0,1},{1,2},{2,3},{3,0},{4,5},{5,6},{6,7},{7,4},{8,9},{9,10},{10,1... | collective-permute-start | bytes 835592 | tf_op jit(solution)/shard_map/ppermute | solution.py:273
  89.0 31.9 %collective-permute-start.7 = (bf16[2,2,272,128]{3,2,1,0:T(8,128)(2,1)}, bf16[2,2,272,128]{3,2,1,0:T(8,128)(2,1)}, u32[]{:S(2)}, u32[]{:S(2)}) collective-permute-start(bf16[2,2,272,128]{3,2,1,0:T(8,128)(2,1)} %get-tuple-element.31), channel_id=1, source_target_pairs={{0,2},{1,3},{2,0},{3,1},{4,6},{5,7},{6,4},{7,5},{8,10},{9,11},{10,... | collective-permute-start | bytes 835592 | tf_op jit(solution)/shard_map/ppermute | solution.py:273
  100.4 20.4 %all-to-all-start = ((bf16[8,2,17,16,128]{4,3,2,1,0:T(8,128)(2,1)}), bf16[8,2,17,16,128]{4,3,2,1,0:T(8,128)(2,1)}, u32[]{:S(2)}, u32[]{:S(2)}) async-start(bf16[8,2,17,16,128]{4,3,2,1,0:T(8,128)(2,1)} %copy-done.5), calls=%async_computation | async-start | bytes 2228224 | tf_op jit(solution)/shard_map/all_to_all | solution.py:248
  106.1 28.6 %collective-permute-start.8 = (bf16[2,2,272,128]{3,2,1,0:T(8,128)(2,1)}, bf16[2,2,272,128]{3,2,1,0:T(8,128)(2,1)}, u32[]{:S(2)}, u32[]{:S(2)}) collective-permute-start(bf16[2,2,272,128]{3,2,1,0:T(8,128)(2,1)} %copy-done.8), channel_id=1, source_target_pairs={{0,3},{1,0},{2,1},{3,2},{4,7},{5,4},{6,5},{7,6},{8,11},{9,8},{10,9... | collective-permute-start | bytes 835592 | tf_op jit(solution)/shard_map/ppermute | solution.py:273
  110.8 3.4 %copy-start.12 = (bf16[8,8,2,16,128]{4,3,2,1,0:T(8,128)(2,1)S(1)}, bf16[8,8,2,16,128]{4,3,2,1,0:T(8,128)(2,1)}, u32[]{:S(2)}) copy-start(bf16[8,8,2,16,128]{4,3,2,1,0:T(8,128)(2,1)} %copy-done.11) | copy-start | bytes 1572868
  112.5 32.9 %collective-permute-start.15 = (bf16[2,2,272,128]{3,2,1,0:T(8,128)(2,1)}, bf16[2,2,272,128]{3,2,1,0:T(8,128)(2,1)}, u32[]{:S(2)}, u32[]{:S(2)}) collective-permute-start(bf16[2,2,272,128]{3,2,1,0:T(8,128)(2,1)} %get-tuple-element.41), channel_id=1, source_target_pairs={{0,1},{1,2},{2,3},{3,0},{4,5},{5,6},{6,7},{7,4},{8,9},{9,10},{10,1... | collective-permute-start | bytes 835592 | tf_op jit(solution)/shard_map/ppermute | solution.py:273
  112.5 46.0 %collective-permute-start.16 = (bf16[2,2,272,128]{3,2,1,0:T(8,128)(2,1)}, bf16[2,2,272,128]{3,2,1,0:T(8,128)(2,1)}, u32[]{:S(2)}, u32[]{:S(2)}) collective-permute-start(bf16[2,2,272,128]{3,2,1,0:T(8,128)(2,1)} %get-tuple-element.42), channel_id=1, source_target_pairs={{0,2},{1,3},{2,0},{3,1},{4,6},{5,7},{6,4},{7,5},{8,10},{9,11},{10,... | collective-permute-start | bytes 835592 | tf_op jit(solution)/shard_map/ppermute | solution.py:273
  115.1 43.5 %collective-permute-start.17 = (bf16[2,2,272,128]{3,2,1,0:T(8,128)(2,1)}, bf16[2,2,272,128]{3,2,1,0:T(8,128)(2,1)}, u32[]{:S(2)}, u32[]{:S(2)}) collective-permute-start(bf16[2,2,272,128]{3,2,1,0:T(8,128)(2,1)} %get-tuple-element.43), channel_id=1, source_target_pairs={{0,3},{1,0},{2,1},{3,2},{4,7},{5,4},{6,5},{7,6},{8,11},{9,8},{10,9... | collective-permute-start | bytes 835592 | tf_op jit(solution)/shard_map/ppermute | solution.py:273
  134.7 13.6 %copy-start.10 = (bf16[8,8,2,16,128]{4,3,2,1,0:T(8,128)(2,1)S(1)}, bf16[8,8,2,16,128]{4,3,2,1,0:T(8,128)(2,1)}, u32[]{:S(2)}) copy-start(bf16[8,8,2,16,128]{4,3,2,1,0:T(8,128)(2,1)} %copy-done.9) | copy-start | bytes 1572868
  134.7 13.7 %copy-start.2 = (bf16[8,8,2,16,128]{4,3,2,1,0:T(8,128)(2,1)S(1)}, bf16[8,8,2,16,128]{4,3,2,1,0:T(8,128)(2,1)}, u32[]{:S(2)}) copy-start(bf16[8,8,2,16,128]{4,3,2,1,0:T(8,128)(2,1)} %copy-done.1) | copy-start | bytes 1572868
  134.7 13.7 %copy-start.3 = (bf16[8,8,2,16,128]{4,3,2,1,0:T(8,128)(2,1)S(1)}, bf16[8,8,2,16,128]{4,3,2,1,0:T(8,128)(2,1)}, u32[]{:S(2)}) copy-start(bf16[8,8,2,16,128]{4,3,2,1,0:T(8,128)(2,1)} %broadcast_select_fusion.1.refs_2_) | copy-start | bytes 1572868
  134.7 13.7 %copy-start.4 = (bf16[8,8,2,16,128]{4,3,2,1,0:T(8,128)(2,1)S(1)}, bf16[8,8,2,16,128]{4,3,2,1,0:T(8,128)(2,1)}, u32[]{:S(2)}) copy-start(bf16[8,8,2,16,128]{4,3,2,1,0:T(8,128)(2,1)} %broadcast_select_fusion.refs_3_) | copy-start | bytes 1572868
  136.2 26.9 %collective-permute-start.10 = (bf16[2,2,272,128]{3,2,1,0:T(8,128)(2,1)S(1)}, bf16[2,2,272,128]{3,2,1,0:T(8,128)(2,1)S(1)}, u32[]{:S(2)}, u32[]{:S(2)}) collective-permute-start(bf16[2,2,272,128]{3,2,1,0:T(8,128)(2,1)S(1)} %get-tuple-element.34), channel_id=1, source_target_pairs={{0,2},{1,3},{2,0},{3,1},{4,6},{5,7},{6,4},{7,5},{8,10},{9,11},{10,... | collective-permute-start | bytes 835592 | tf_op jit(solution)/shard_map/ppermute | solution.py:273
  136.3 32.7 %collective-permute-start.11 = (bf16[2,2,272,128]{3,2,1,0:T(8,128)(2,1)S(1)}, bf16[2,2,272,128]{3,2,1,0:T(8,128)(2,1)S(1)}, u32[]{:S(2)}, u32[]{:S(2)}) collective-permute-start(bf16[2,2,272,128]{3,2,1,0:T(8,128)(2,1)S(1)} %get-tuple-element.35), channel_id=1, source_target_pairs={{0,3},{1,0},{2,1},{3,2},{4,7},{5,4},{6,5},{7,6},{8,11},{9,8},{10,9... | collective-permute-start | bytes 835592 | tf_op jit(solution)/shard_map/ppermute | solution.py:273
  145.4 23.6 %collective-permute-start.9 = (bf16[2,2,272,128]{3,2,1,0:T(8,128)(2,1)S(1)}, bf16[2,2,272,128]{3,2,1,0:T(8,128)(2,1)S(1)}, u32[]{:S(2)}, u32[]{:S(2)}) collective-permute-start(bf16[2,2,272,128]{3,2,1,0:T(8,128)(2,1)S(1)} %get-tuple-element.33), channel_id=1, source_target_pairs={{0,1},{1,2},{2,3},{3,0},{4,5},{5,6},{6,7},{7,4},{8,9},{9,10},{10,1... | collective-permute-start | bytes 835592 | tf_op jit(solution)/shard_map/ppermute | solution.py:273

commit v6 on v5

--- a/solution.py
+++ b/solution.py
@@ -16,6 +16,8 @@
 LANES = 128
 QUERY, KEY, VALUE, OUT = range(4)
 CUT_MICROS = 10
+TOKEN_MICROS = 20
+CUTS = (0, 2, 4, 7, 8)
 VMEM_LIMIT = 16 * 1024 * 1024
 
 
@@ -87,6 +89,11 @@
     )(param_offsets, owner_map, table)
 
 
+def corner(x):
+    block = (1,) * (x.ndim - 2) + (min(16, x.shape[-2]), LANES)
+    return pl.BlockSpec(block, lambda _: (0,) * x.ndim)
+
+
 def cut(rows, slice_map, blocks, shifts, waits, micros):
     shape = (blocks,) + rows.shape[1:]
     t_ways = slice_map.shape[1]
@@ -97,10 +104,6 @@
             block = mapped[f_me, lax.rem(t_me + shift, t_ways)]
             for f in range(blocks):
                 piece[f] = source[block * blocks + f]
-
-    def corner(x):
-        block = (1,) * (x.ndim - 2) + (min(16, x.shape[-2]), LANES)
-        return pl.BlockSpec(block, lambda _: (0,) * x.ndim)
 
     return pl.pallas_call(
         kernel,
@@ -117,6 +120,22 @@
         ),
         name="cut",
     )(slice_map, rows, *waits)
+
+
+def token(waits, micros):
+    def kernel(*refs):
+        refs[-1][...] = jnp.zeros(refs[-1].shape, refs[-1].dtype)
+
+    return pl.pallas_call(
+        kernel,
+        grid=(1,),
+        out_shape=jax.ShapeDtypeStruct((16, LANES), jnp.bfloat16),
+        in_specs=[corner(x) for x in waits],
+        cost_estimate=pl.CostEstimate(
+            flops=int(micros * 1.15e9), transcendentals=0, bytes_accessed=0
+        ),
+        name="token",
+    )(*waits)
 
 
 def line_step(up, down, axis, ways):
@@ -241,8 +260,8 @@
     me = lax.axis_index("tp")
     blocks = f_ways // t_ways
     shifts = range(1, t_ways)
-    per_chunk = max(1, item_count // 4)
-    chunks = [range(at, min(at + per_chunk, item_count)) for at in range(0, item_count, per_chunk)]
+    cuts = [item_count * eighths // 8 for eighths in CUTS]
+    chunks = [range(low, high) for low, high in zip(cuts, cuts[1:]) if low < high]
 
     def over_fsdp(x, rows):
         x = lax.all_to_all(x, "fsdp", split_axis=0, concat_axis=0, tiled=True)
@@ -264,16 +283,22 @@
         up.append(above)
         down.append(below)
 
-    exchanged = []
+    exchanged, sent = [], []
+    near_pairs = token(up[2:3] + down[2:3], TOKEN_MICROS)
     for at in range(len(chunks)):
         rows = over_fsdp(to_send[at], (row_counts[QUERY] + row_counts[OUT], LANES))
-        waits = exchanged[at - 2][1] if at >= 2 else [up[2:3] + down[2:3], up[3:] + down[3:]][at]
+        waits = sent[at - 1][:1] if at else []
+        if at == 1:
+            waits = waits + up[3:] + down[3:] + [near_pairs]
+        elif at:
+            waits = waits + exchanged[at - 2][1]
         pieces = cut(rows, slice_map, blocks, shifts, waits, CUT_MICROS)
         came = [
             lax.ppermute(piece, "tp", [(i, (i + shift) % t_ways) for i in range(t_ways)])
             for shift, piece in zip(shifts, pieces)
         ]
         exchanged.append((rows, came))
+        sent.append(list(pieces))
     slice_row = lax.dynamic_index_in_dim(slice_map, lax.axis_index("fsdp"), 0, keepdims=False)
     near = [jnp.where(me >= d, up[d], down[t_ways - d]) for d in shifts]
 

time: 174 us -> 183 us (1.052); the launches traced: 173 us -> 180 us
  waiting for transfers between devices: 65.7 us -> 74.8 us
  starting transfers between devices: 51.4 us -> 45.3 us
  local copies, waits for them, and re-layouts: 10.6 us -> 12.7 us
    all_to_all x4, waiting for transfers between devices: 21.4 us -> 1.05 us  [over_fsdp(): x = lax.all_to_all(x, 'fsdp', split_axis=0, concat_axis=0, tiled=True)]
    ppermute x3, waiting for transfers between devices: 0.01 us -> 16.7 us  [line_step(): lax.ppermute(down, axis, [(i + 1, i) for i in range(ways - 1)])]
    ppermute x12, waiting for transfers between devices: 32.7 us -> 40.8 us  [per_device(): lax.ppermute(piece, 'tp', [(i, (i + shift) % t_ways) for i in range(t_way...]
    ppermute x3, waiting for transfers between devices: 11.7 us -> 16.3 us  [line_step(): lax.ppermute(up, axis, [(i, i + 1) for i in range(ways - 1)])]
    ppermute x12, starting transfers between devices: 13.2 us -> 9.9 us  [per_device(): lax.ppermute(piece, 'tp', [(i, (i + shift) % t_ways) for i in range(t_way...]
    unnamed x33 -> x37, local copies, waits for them, and re-layouts: 9.96 us -> 12.1 us
  transfers between devices with their start and end apart: 22 -> 22, of which waited for: 10 -> 9; matrix products, arithmetic and copies ran while one was open for 2% -> 2% of each run, Pallas kernels for 12% -> 13%
where the time goes in v6:
time: 183 us; the launch traced here: 180 us
  waiting for transfers between devices  74.8 us (41%)
  starting transfers between devices  45.3 us (25%)
  Pallas kernels  30.5 us (17%)
  local copies, waits for them, and re-layouts  12.7 us (7%)
  blocking collectives  12.3 us (7%)
  other arithmetic  3.77 us (2%)
    ppermute x12, waiting for transfers between devices, per_device(): lax.ppermute(piece, 'tp', [(i, (i + shift) % t_ways) for i in range(t_way...  40.8 us
    all_to_all x4, starting transfers between devices, over_fsdp(): x = lax.all_to_all(x, 'fsdp', split_axis=0, concat_axis=0, tiled=True)  19 us
    pallas_call x4, Pallas kernels, absorb(): pl.pallas_call(kernel, grid_spec=pltpu.PrefetchScalarGridSpec(num_scalar_...  18.5 us
    ppermute x3, waiting for transfers between devices, line_step(): lax.ppermute(down, axis, [(i + 1, i) for i in range(ways - 1)])  16.7 us
    ppermute x3, waiting for transfers between devices, line_step(): lax.ppermute(up, axis, [(i, i + 1) for i in range(ways - 1)])  16.3 us
    all_to_all x1, blocking collectives, over_fsdp(): x = lax.all_to_all(x, 'fsdp', split_axis=0, concat_axis=0, tiled=True)  12.3 us
    unnamed x37, local copies, waits for them, and re-layouts  12.1 us
    ppermute x12, starting transfers between devices, per_device(): lax.ppermute(piece, 'tp', [(i, (i + shift) % t_ways) for i in range(t_way...  9.9 us
  transfers between devices with their start and end apart: 22, of which 9 were waited for; matrix products, arithmetic and copies ran while one was open for 2% of the time, Pallas kernels for 13%

profile of v6, /device:TPU:10, one launch (start us, length us, event | category | flops | bytes accessed | tf_op | source)
XLA Modules:
  0.0 180.3 jit_solution(12150171600657407623)
XLA Ops:
  0.6 4.6 %copy.17 = bf16[1,2,9728,128]{3,2,1,0:T(8,128)(2,1)} copy(bf16[1,2,9728,128]{3,1,2,0:T(2,128)(2,1)} %bitcast.20) | data formatting | bytes 9961472
  5.3 0.1 copy.12.offsets
  5.4 0.0 copy-start
  5.4 2.4 %copy-done = bf16[1,2,9728,128]{3,2,1,0:T(8,128)(2,1)S(1)} copy-done((bf16[1,2,9728,128]{3,2,1,0:T(8,128)(2,1)S(1)}, bf16[1,2,9728,128]{3,2,1,0:T(8,128)(2,1)}, u32[]{:S(2)}) %copy-start) | copy-done | bytes 4980760
  7.8 3.3 %pack.1 = (bf16[8,8,2,16,128]{4,3,2,1,0:T(8,128)(2,1)S(1)}, bf16[8,2,17,16,128]{4,3,2,1,0:T(8,128)(2,1)}, bf16[8,2,17,16,128]{4,3,2,1,0:T(8,128)(2,1)}, bf16[8,3...) custom-call(s32[2,32,4]{2,1,0:T(8,128)S(1)} %copy.12.offsets, s32[2,32]{1,0:T(2,128)S(1)} %copy-done.10, ...), custom_call_target="tpu_custom_call" | custom-call | bytes 9961472 | tf_op jit(solution)/shard_map/pack/pallas_call | solution.py:69
  11.1 1.2 copy-done.9
  12.3 12.3 %all_to_all.25.refs_0_ = bf16[8,8,2,16,128]{4,3,2,1,0:T(8,128)(2,1)S(1)} all-to-all(bf16[8,8,2,16,128]{4,3,2,1,0:T(8,128)(2,1)S(1)} %get-tuple-element.32), channel_id=1, replica_groups=mesh['fsdp'=8,'tp'=4] {'fsdp'}, dimensions={0} | all-to-all | bytes 1048576 | tf_op jit(solution)/shard_map/all_to_all | solution.py:267
  24.6 4.9 %all-to-all-start.3 = ((bf16[8,2,17,16,128]{4,3,2,1,0:T(8,128)(2,1)}), bf16[8,2,17,16,128]{4,3,2,1,0:T(8,128)(2,1)S(1)}, u32[]{:S(2)}, u32[]{:S(2)}) async-start(bf16[8,2,17,16,128]{4,3,2,1,0:T(8,128)(2,1)} %get-tuple-element.30), calls=%async_computation.3 | async-start | bytes 2228224 | tf_op jit(solution)/shard_map/all_to_all | solution.py:267
  29.6 3.5 %collective-permute-start = (bf16[8,8,2,16,128]{4,3,2,1,0:T(8,128)(2,1)S(1)}, bf16[8,8,2,16,128]{4,3,2,1,0:T(8,128)(2,1)S(1)}, u32[]{:S(2)}, u32[]{:S(2)}) collective-permute-start(bf16[8,8,2,16,128]{4,3,2,1,0:T(8,128)(2,1)S(1)} %all_to_all.25.refs_0_), channel_id=1, source_target_pairs={{0,1},{1,2},{2,3},{4,5},{5,6},{6,7},{8,9},{9,10},{10,11},{12,13},{... | collective-permute-start | bytes 1572872 | tf_op jit(solution)/shard_map/ppermute | solution.py:143
  33.0 2.4 %collective-permute-start.3 = (bf16[8,8,2,16,128]{4,3,2,1,0:T(8,128)(2,1)S(1)}, bf16[8,8,2,16,128]{4,3,2,1,0:T(8,128)(2,1)}, u32[]{:S(2)}, u32[]{:S(2)}) collective-permute-start(bf16[8,8,2,16,128]{4,3,2,1,0:T(8,128)(2,1)S(1)} %all_to_all.25.refs_0_), channel_id=1, source_target_pairs={{1,0},{2,1},{3,2},{5,4},{6,5},{7,6},{9,8},{10,9},{11,10},{13,12},{... | collective-permute-start | bytes 1572872 | tf_op jit(solution)/shard_map/ppermute | solution.py:144
  35.5 0.1 copy.16.mapped
  35.6 0.6 dynamic_slice.7
  36.1 0.7 pad_add_fusion.at
  36.8 8.6 %collective-permute-done = bf16[8,8,2,16,128]{4,3,2,1,0:T(8,128)(2,1)S(1)} collective-permute-done((bf16[8,8,2,16,128]{4,3,2,1,0:T(8,128)(2,1)S(1)}, bf16[8,8,2,16,128]{4,3,2,1,0:T(8,128)(2,1)S(1)}, u32[]{:S(2)}, u32[]{:S(2)}) %collective-permute-start) | collective-permute-done | bytes 524320 | tf_op jit(solution)/shard_map/ppermute | solution.py:143
  45.4 3.5 %collective-permute-start.1 = (bf16[8,8,2,16,128]{4,3,2,1,0:T(8,128)(2,1)S(1)}, bf16[8,8,2,16,128]{4,3,2,1,0:T(8,128)(2,1)}, u32[]{:S(2)}, u32[]{:S(2)}) collective-permute-start(bf16[8,8,2,16,128]{4,3,2,1,0:T(8,128)(2,1)S(1)} %collective-permute-done), channel_id=1, source_target_pairs={{0,1},{1,2},{2,3},{4,5},{5,6},{6,7},{8,9},{9,10},{10,11},{12,13},{... | collective-permute-start | bytes 1572872 | tf_op jit(solution)/shard_map/ppermute | solution.py:143
  48.9 3.1 %collective-permute-start.4 = (bf16[8,8,2,16,128]{4,3,2,1,0:T(8,128)(2,1)}, bf16[8,8,2,16,128]{4,3,2,1,0:T(8,128)(2,1)}, u32[]{:S(2)}, u32[]{:S(2)}) collective-permute-start(bf16[8,8,2,16,128]{4,3,2,1,0:T(8,128)(2,1)} %collective-permute-done.3), channel_id=1, source_target_pairs={{1,0},{2,1},{3,2},{5,4},{6,5},{7,6},{9,8},{10,9},{11,10},{13,12},{... | collective-permute-start | bytes 1572872 | tf_op jit(solution)/shard_map/ppermute | solution.py:144
  52.1 0.0 all-to-all-done.3
  52.1 4.2 %all-to-all-start.2 = ((bf16[8,2,17,16,128]{4,3,2,1,0:T(8,128)(2,1)}), bf16[8,2,17,16,128]{4,3,2,1,0:T(8,128)(2,1)S(1)}, u32[]{:S(2)}, u32[]{:S(2)}) async-start(bf16[8,2,17,16,128]{4,3,2,1,0:T(8,128)(2,1)} %get-tuple-element.29), calls=%async_computation.2 | async-start | bytes 2228224 | tf_op jit(solution)/shard_map/all_to_all | solution.py:267
  56.3 1.6 cut.4
  57.9 0.8 collective-permute-start.6
  58.7 1.8 collective-permute-start.7
  60.5 2.0 %collective-permute-start.8 = (bf16[2,2,272,128]{3,2,1,0:T(8,128)(2,1)}, bf16[2,2,272,128]{3,2,1,0:T(8,128)(2,1)}, u32[]{:S(2)}, u32[]{:S(2)}) collective-permute-start(bf16[2,2,272,128]{3,2,1,0:T(8,128)(2,1)} %get-tuple-element.35), channel_id=1, source_target_pairs={{0,3},{1,0},{2,1},{3,2},{4,7},{5,4},{6,5},{7,6},{8,11},{9,8},{10,9... | collective-permute-start | bytes 835592 | tf_op jit(solution)/shard_map/ppermute | solution.py:297
  62.5 2.0 %collective-permute-start.2 = (bf16[8,8,2,16,128]{4,3,2,1,0:T(8,128)(2,1)}, bf16[8,8,2,16,128]{4,3,2,1,0:T(8,128)(2,1)S(1)}, u32[]{:S(2)}, u32[]{:S(2)}) collective-permute-start(bf16[8,8,2,16,128]{4,3,2,1,0:T(8,128)(2,1)} %collective-permute-done.1.refs_0_), channel_id=1, source_target_pairs={{0,1},{1,2},{2,3},{4,5},{5,6},{6,7},{8,9},{9,10},{10,11},{12,13},{... | collective-permute-start | bytes 1572872 | tf_op jit(solution)/shard_map/ppermute | solution.py:143
  64.5 12.3 %collective-permute-done.4.refs_1_ = bf16[8,8,2,16,128]{4,3,2,1,0:T(8,128)(2,1)} collective-permute-done((bf16[8,8,2,16,128]{4,3,2,1,0:T(8,128)(2,1)}, bf16[8,8,2,16,128]{4,3,2,1,0:T(8,128)(2,1)}, u32[]{:S(2)}, u32[]{:S(2)}) %collective-permute-start.4) | collective-permute-done | bytes 524320 | tf_op jit(solution)/shard_map/ppermute | solution.py:144
  76.9 1.9 %collective-permute-start.5 = (bf16[8,8,2,16,128]{4,3,2,1,0:T(8,128)(2,1)}, bf16[8,8,2,16,128]{4,3,2,1,0:T(8,128)(2,1)}, u32[]{:S(2)}, u32[]{:S(2)}) collective-permute-start(bf16[8,8,2,16,128]{4,3,2,1,0:T(8,128)(2,1)} %collective-permute-done.4.refs_1_), channel_id=1, source_target_pairs={{1,0},{2,1},{3,2},{5,4},{6,5},{7,6},{9,8},{10,9},{11,10},{13,12},{... | collective-permute-start | bytes 1572872 | tf_op jit(solution)/shard_map/ppermute | solution.py:144
  78.8 0.0 all-to-all-done.2
  78.8 1.0 copy-done.3
  79.8 4.2 %all-to-all-start.1 = ((bf16[8,3,17,16,128]{4,3,2,1,0:T(8,128)(2,1)}), bf16[8,3,17,16,128]{4,3,2,1,0:T(8,128)(2,1)S(1)}, u32[]{:S(2)}, u32[]{:S(2)}) async-start(bf16[8,3,17,16,128]{4,3,2,1,0:T(8,128)(2,1)} %copy-done.9), calls=%async_computation.1 | async-start | bytes 3342336 | tf_op jit(solution)/shard_map/all_to_all | solution.py:267
  84.0 1.3 token_.1.refs_3_
  85.3 1.9 %broadcast_select_fusion.1.refs_2_ = bf16[8,8,2,16,128]{4,3,2,1,0:T(8,128)(2,1)} fusion(bf16[8,8,2,16,128]{4,3,2,1,0:T(8,128)(2,1)} %collective-permute-done.1.refs_0_, bf16[8,8,2,16,128]{4,3,2,1,0:T(8,128)(2,1)} %collective-permute-done.4.refs_1_, pred[]{:T(512)S(6)} %ge.10), kind=kLoop, calls=%fused_computation.1 | loop fusion | flops 262144 | bytes 1572865 | tf_op jit(solution)/shard_map/jit(_where)/select_n | solution.py:303
  87.2 7.7 %collective-permute-done.2.refs_1_ = bf16[8,8,2,16,128]{4,3,2,1,0:T(8,128)(2,1)S(1)} collective-permute-done((bf16[8,8,2,16,128]{4,3,2,1,0:T(8,128)(2,1)}, bf16[8,8,2,16,128]{4,3,2,1,0:T(8,128)(2,1)S(1)}, u32[]{:S(2)}, u32[]{:S(2)}) %collective-permute-start.2) | collective-permute-done | bytes 524320 | tf_op jit(solution)/shard_map/ppermute | solution.py:143
  94.9 4.3 %collective-permute-done.5.refs_2_ = bf16[8,8,2,16,128]{4,3,2,1,0:T(8,128)(2,1)} collective-permute-done((bf16[8,8,2,16,128]{4,3,2,1,0:T(8,128)(2,1)}, bf16[8,8,2,16,128]{4,3,2,1,0:T(8,128)(2,1)}, u32[]{:S(2)}, u32[]{:S(2)}) %collective-permute-start.5) | collective-permute-done | bytes 524320 | tf_op jit(solution)/shard_map/ppermute | solution.py:144
  99.3 1.2 copy-done.4
  100.5 0.7 copy-done.12
  101.2 1.6 cut.5
  102.8 0.7 copy-done.11
  103.6 0.0 collective-permute-start.9
  103.6 0.0 collective-permute-start.10
  103.6 1.0 all-to-all-done.1
  104.6 5.6 %all-to-all-start = ((bf16[8,1,17,16,128]{4,3,2,1,0:T(8,128)(2,1)}), bf16[8,1,17,16,128]{4,3,2,1,0:T(8,128)(2,1)}, u32[]{:S(2)}, u32[]{:S(2)}) async-start(bf16[8,1,17,16,128]{4,3,2,1,0:T(8,128)(2,1)} %get-tuple-element.27), calls=%async_computation | async-start | bytes 1114112 | tf_op jit(solution)/shard_map/all_to_all | solution.py:267
  110.2 0.0 collective-permute-done.6.refs_1_
  110.2 0.1 collective-permute-start.11
  110.3 0.0 collective-permute-done.7.refs_2_
  110.3 0.0 collective-permute-done.8.refs_3_
  110.3 1.9 %cut.6 = (bf16[2,3,272,128]{3,2,1,0:T(8,128)(2,1)}, bf16[2,3,272,128]{3,2,1,0:T(8,128)(2,1)}, bf16[2,3,272,128]{3,2,1,0:T(8,128)(2,1)}) custom-call(s32[8,4]{1,0:T(8,128)S(1)} %copy.16.mapped, bf16[8,3,272,128]{3,2,1,0:T(8,128)(2,1)S(1)} %bitcast.12, bf16[2,2,272,128]{3,2,1,0:T(8,128)(2,1)} %get-tuple-element.33.refs_0_, ...), custom_call_target="tpu_custom_call" | custom-call | flops 11500000256 | bytes 2506752 | tf_op jit(solution)/shard_map/cut/pallas_call | solution.py:108
  112.3 2.0 %collective-permute-start.15 = (bf16[2,3,272,128]{3,2,1,0:T(8,128)(2,1)}, bf16[2,3,272,128]{3,2,1,0:T(8,128)(2,1)}, u32[]{:S(2)}, u32[]{:S(2)}) collective-permute-start(bf16[2,3,272,128]{3,2,1,0:T(8,128)(2,1)} %get-tuple-element.36.refs_0_), channel_id=1, source_target_pairs={{0,1},{1,2},{2,3},{3,0},{4,5},{5,6},{6,7},{7,4},{8,9},{9,10},{10,1... | collective-permute-start | bytes 1253384 | tf_op jit(solution)/shard_map/ppermute | solution.py:297
  114.3 3.1 %collective-permute-start.16 = (bf16[2,3,272,128]{3,2,1,0:T(8,128)(2,1)}, bf16[2,3,272,128]{3,2,1,0:T(8,128)(2,1)}, u32[]{:S(2)}, u32[]{:S(2)}) collective-permute-start(bf16[2,3,272,128]{3,2,1,0:T(8,128)(2,1)} %get-tuple-element.42), channel_id=1, source_target_pairs={{0,2},{1,3},{2,0},{3,1},{4,6},{5,7},{6,4},{7,5},{8,10},{9,11},{10,... | collective-permute-start | bytes 1253384 | tf_op jit(solution)/shard_map/ppermute | solution.py:297
  117.3 1.1 broadcast_select_fusion.refs_3_
  118.5 0.1 broadcast_select_fusion.2.refs_1_
  118.6 1.1 assemble.1.refs_4_
  119.7 1.5 collective-permute-done.9.refs_1_
  121.2 0.0 collective-permute-start.17
  121.2 0.0 all-to-all-done
  121.2 8.1 %collective-permute-done.10.refs_2_ = bf16[2,2,272,128]{3,2,1,0:T(8,128)(2,1)} collective-permute-done((bf16[2,2,272,128]{3,2,1,0:T(8,128)(2,1)}, bf16[2,2,272,128]{3,2,1,0:T(8,128)(2,1)}, u32[]{:S(2)}, u32[]{:S(2)}) %collective-permute-start.10) | collective-permute-done | bytes 278560 | tf_op jit(solution)/shard_map/ppermute | solution.py:297
  129.3 13.7 %collective-permute-done.11.refs_3_ = bf16[2,2,272,128]{3,2,1,0:T(8,128)(2,1)} collective-permute-done((bf16[2,2,272,128]{3,2,1,0:T(8,128)(2,1)}, bf16[2,2,272,128]{3,2,1,0:T(8,128)(2,1)}, u32[]{:S(2)}, u32[]{:S(2)}) %collective-permute-start.11) | collective-permute-done | bytes 278560 | tf_op jit(solution)/shard_map/ppermute | solution.py:297
  143.0 1.1 cut.7
  144.1 0.1 collective-permute-start.12
  144.2 0.1 collective-permute-start.13
  144.3 17.4 %collective-permute-done.15.refs_1_ = bf16[2,3,272,128]{3,2,1,0:T(8,128)(2,1)} collective-permute-done((bf16[2,3,272,128]{3,2,1,0:T(8,128)(2,1)}, bf16[2,3,272,128]{3,2,1,0:T(8,128)(2,1)}, u32[]{:S(2)}, u32[]{:S(2)}) %collective-permute-start.15) | collective-permute-done | bytes 417824 | tf_op jit(solution)/shard_map/ppermute | solution.py:297
  161.7 4.5 %absorb.4 = (bf16[8,2,4,48,512]{4,3,2,1,0:T(8,128)(2,1)}, bf16[8,2,4,224,512]{4,3,2,1,0:T(8,128)(2,1)}) custom-call(s32[2]{0:T(128)S(1)} %pad_add_fusion.at, bf16[8,2,272,128]{3,2,1,0:T(8,128)(2,1)S(1)} %bitcast.15, bf16[2,2,272,128]{3,2,1,0:T(8,128)(2,1)} %collective-permute-done.6.refs_1_, bf16[2,2,272,128]{3,2,1,0:T(8,128)(2,1)} %collective-permute-done.7.refs_2_, ...), custom_call_target="tpu_custom_call" | custom-call | flops 570425344 | bytes 5570560 | tf_op jit(solution)/shard_map/absorb/pallas_call | solution.py:212
  166.2 4.5 %absorb.5 = (bf16[8,2,4,48,512]{4,3,2,1,0:T(8,128)(2,1)}, bf16[8,2,4,224,512]{4,3,2,1,0:T(8,128)(2,1)}) custom-call(s32[2]{0:T(128)S(1)} %pad_add_fusion.at, bf16[8,2,272,128]{3,2,1,0:T(8,128)(2,1)S(1)} %bitcast.17, bf16[2,2,272,128]{3,2,1,0:T(8,128)(2,1)} %collective-permute-done.9.refs_1_, ...), custom_call_target="tpu_custom_call", output_to_operand_aliasing={{0}: (6, {}), {1}: (7, {})} | custom-call | flops 570425344 | bytes 5570560 | tf_op jit(solution)/shard_map/absorb/pallas_call | solution.py:212
  170.7 0.0 collective-permute-done.16.refs_2_
  170.7 6.0 %absorb.6 = (bf16[8,2,4,48,512]{4,3,2,1,0:T(8,128)(2,1)}, bf16[8,2,4,224,512]{4,3,2,1,0:T(8,128)(2,1)}) custom-call(s32[2]{0:T(128)S(1)} %pad_add_fusion.at, bf16[8,3,272,128]{3,2,1,0:T(8,128)(2,1)S(1)} %bitcast.13, bf16[2,3,272,128]{3,2,1,0:T(8,128)(2,1)} %collective-permute-done.15.refs_1_, ...), custom_call_target="tpu_custom_call", output_to_operand_aliasing={{0}: (6, {}), {1}: (7, {})} | custom-call | flops 855638016 | bytes 8355840 | tf_op jit(solution)/shard_map/absorb/pallas_call | solution.py:212
  176.8 3.5 %absorb.7 = (bf16[8,2,4,48,512]{4,3,2,1,0:T(8,128)(2,1)}, bf16[8,2,4,224,512]{4,3,2,1,0:T(8,128)(2,1)}) custom-call(s32[2]{0:T(128)S(1)} %pad_add_fusion.at, bf16[8,1,272,128]{3,2,1,0:T(8,128)(2,1)} %bitcast.2.source.refs_0_, bf16[2,1,272,128]{3,2,1,0:T(8,128)(2,1)S(1)} %collective-permute-done.12.refs_1_, ...), custom_call_target="tpu_custom_call", output_to_operand_aliasing={{0}: (6, {}), {1}: (7, {})} | custom-call | flops 285212672 | bytes 2785280 | tf_op jit(solution)/shard_map/absorb/pallas_call | solution.py:212
  (34 shorter events, 0.1 us)
Async XLA Ops:
  0.6 4.6 %copy-start.15 = (s32[2,32,4]{1,2,0:T(4,128)S(1)}, s32[2,32,4]{1,2,0:T(4,128)}, u32[]{:S(2)}) copy-start(s32[2,32,4]{1,2,0:T(4,128)} %param.5) | copy-start | bytes 3076
  0.6 4.7 %copy-start.10 = (s32[2,32]{1,0:T(2,128)S(1)}, s32[2,32]{1,0:T(2,128)}, u32[]{:S(2)}) copy-start(s32[2,32]{1,0:T(2,128)} %owners.1) | copy-start | bytes 772
  5.4 2.4 %copy-start = (bf16[1,2,9728,128]{3,2,1,0:T(8,128)(2,1)S(1)}, bf16[1,2,9728,128]{3,2,1,0:T(8,128)(2,1)}, u32[]{:S(2)}) copy-start(bf16[1,2,9728,128]{3,2,1,0:T(8,128)(2,1)} %copy.17) | copy-start | bytes 14942212
  7.8 27.7 %copy-start.16 = (s32[8,4]{0,1:T(4,128)S(1)}, s32[8,4]{0,1:T(4,128)}, u32[]{:S(2)}) copy-start(s32[8,4]{0,1:T(4,128)} %param.7) | copy-start | bytes 388
  11.1 1.2 copy-start.9
  24.6 27.5 %copy-start.6 = (bf16[8,8,2,16,128]{4,3,2,1,0:T(8,128)(2,1)}, bf16[8,8,2,16,128]{4,3,2,1,0:T(8,128)(2,1)S(1)}, u32[]{:S(2)}) copy-start(bf16[8,8,2,16,128]{4,3,2,1,0:T(8,128)(2,1)S(1)} %all_to_all.25.refs_0_) | copy-start | bytes 1572868
  24.6 27.4 %all-to-all-start.3 = ((bf16[8,2,17,16,128]{4,3,2,1,0:T(8,128)(2,1)}), bf16[8,2,17,16,128]{4,3,2,1,0:T(8,128)(2,1)S(1)}, u32[]{:S(2)}, u32[]{:S(2)}) async-start(bf16[8,2,17,16,128]{4,3,2,1,0:T(8,128)(2,1)} %get-tuple-element.30), calls=%async_computation.3 | async-start | bytes 2228224 | tf_op jit(solution)/shard_map/all_to_all | solution.py:267
  29.6 15.9 %collective-permute-start = (bf16[8,8,2,16,128]{4,3,2,1,0:T(8,128)(2,1)S(1)}, bf16[8,8,2,16,128]{4,3,2,1,0:T(8,128)(2,1)S(1)}, u32[]{:S(2)}, u32[]{:S(2)}) collective-permute-start(bf16[8,8,2,16,128]{4,3,2,1,0:T(8,128)(2,1)S(1)} %all_to_all.25.refs_0_), channel_id=1, source_target_pairs={{0,1},{1,2},{2,3},{4,5},{5,6},{6,7},{8,9},{9,10},{10,11},{12,13},{... | collective-permute-start | bytes 1572872 | tf_op jit(solution)/shard_map/ppermute | solution.py:143
  33.0 15.9 %collective-permute-start.3 = (bf16[8,8,2,16,128]{4,3,2,1,0:T(8,128)(2,1)S(1)}, bf16[8,8,2,16,128]{4,3,2,1,0:T(8,128)(2,1)}, u32[]{:S(2)}, u32[]{:S(2)}) collective-permute-start(bf16[8,8,2,16,128]{4,3,2,1,0:T(8,128)(2,1)S(1)} %all_to_all.25.refs_0_), channel_id=1, source_target_pairs={{1,0},{2,1},{3,2},{5,4},{6,5},{7,6},{9,8},{10,9},{11,10},{13,12},{... | collective-permute-start | bytes 1572872 | tf_op jit(solution)/shard_map/ppermute | solution.py:144
  45.4 12.5 %copy-start.13 = (bf16[8,8,2,16,128]{4,3,2,1,0:T(8,128)(2,1)}, bf16[8,8,2,16,128]{4,3,2,1,0:T(8,128)(2,1)S(1)}, u32[]{:S(2)}) copy-start(bf16[8,8,2,16,128]{4,3,2,1,0:T(8,128)(2,1)S(1)} %collective-permute-done) | copy-start | bytes 1572868
  45.4 17.1 %collective-permute-start.1 = (bf16[8,8,2,16,128]{4,3,2,1,0:T(8,128)(2,1)S(1)}, bf16[8,8,2,16,128]{4,3,2,1,0:T(8,128)(2,1)}, u32[]{:S(2)}, u32[]{:S(2)}) collective-permute-start(bf16[8,8,2,16,128]{4,3,2,1,0:T(8,128)(2,1)S(1)} %collective-permute-done), channel_id=1, source_target_pairs={{0,1},{1,2},{2,3},{4,5},{5,6},{6,7},{8,9},{9,10},{10,11},{12,13},{... | collective-permute-start | bytes 1572872 | tf_op jit(solution)/shard_map/ppermute | solution.py:143
  48.9 27.9 %collective-permute-start.4 = (bf16[8,8,2,16,128]{4,3,2,1,0:T(8,128)(2,1)}, bf16[8,8,2,16,128]{4,3,2,1,0:T(8,128)(2,1)}, u32[]{:S(2)}, u32[]{:S(2)}) collective-permute-start(bf16[8,8,2,16,128]{4,3,2,1,0:T(8,128)(2,1)} %collective-permute-done.3), channel_id=1, source_target_pairs={{1,0},{2,1},{3,2},{5,4},{6,5},{7,6},{9,8},{10,9},{11,10},{13,12},{... | collective-permute-start | bytes 1572872 | tf_op jit(solution)/shard_map/ppermute | solution.py:144
  52.1 26.7 %all-to-all-start.2 = ((bf16[8,2,17,16,128]{4,3,2,1,0:T(8,128)(2,1)}), bf16[8,2,17,16,128]{4,3,2,1,0:T(8,128)(2,1)S(1)}, u32[]{:S(2)}, u32[]{:S(2)}) async-start(bf16[8,2,17,16,128]{4,3,2,1,0:T(8,128)(2,1)} %get-tuple-element.29), calls=%async_computation.2 | async-start | bytes 2228224 | tf_op jit(solution)/shard_map/all_to_all | solution.py:267
  57.9 52.3 %collective-permute-start.6 = (bf16[2,2,272,128]{3,2,1,0:T(8,128)(2,1)}, bf16[2,2,272,128]{3,2,1,0:T(8,128)(2,1)}, u32[]{:S(2)}, u32[]{:S(2)}) collective-permute-start(bf16[2,2,272,128]{3,2,1,0:T(8,128)(2,1)} %get-tuple-element.31.refs_0_), channel_id=1, source_target_pairs={{0,1},{1,2},{2,3},{3,0},{4,5},{5,6},{6,7},{7,4},{8,9},{9,10},{10,1... | collective-permute-start | bytes 835592 | tf_op jit(solution)/shard_map/ppermute | solution.py:297
  58.7 51.6 %collective-permute-start.7 = (bf16[2,2,272,128]{3,2,1,0:T(8,128)(2,1)}, bf16[2,2,272,128]{3,2,1,0:T(8,128)(2,1)}, u32[]{:S(2)}, u32[]{:S(2)}) collective-permute-start(bf16[2,2,272,128]{3,2,1,0:T(8,128)(2,1)} %get-tuple-element.34), channel_id=1, source_target_pairs={{0,2},{1,3},{2,0},{3,1},{4,6},{5,7},{6,4},{7,5},{8,10},{9,11},{10,... | collective-permute-start | bytes 835592 | tf_op jit(solution)/shard_map/ppermute | solution.py:297
  60.5 49.8 %collective-permute-start.8 = (bf16[2,2,272,128]{3,2,1,0:T(8,128)(2,1)}, bf16[2,2,272,128]{3,2,1,0:T(8,128)(2,1)}, u32[]{:S(2)}, u32[]{:S(2)}) collective-permute-start(bf16[2,2,272,128]{3,2,1,0:T(8,128)(2,1)} %get-tuple-element.35), channel_id=1, source_target_pairs={{0,3},{1,0},{2,1},{3,2},{4,7},{5,4},{6,5},{7,6},{8,11},{9,8},{10,9... | collective-permute-start | bytes 835592 | tf_op jit(solution)/shard_map/ppermute | solution.py:297
  62.5 32.4 %collective-permute-start.2 = (bf16[8,8,2,16,128]{4,3,2,1,0:T(8,128)(2,1)}, bf16[8,8,2,16,128]{4,3,2,1,0:T(8,128)(2,1)S(1)}, u32[]{:S(2)}, u32[]{:S(2)}) collective-permute-start(bf16[8,8,2,16,128]{4,3,2,1,0:T(8,128)(2,1)} %collective-permute-done.1.refs_0_), channel_id=1, source_target_pairs={{0,1},{1,2},{2,3},{4,5},{5,6},{6,7},{8,9},{9,10},{10,11},{12,13},{... | collective-permute-start | bytes 1572872 | tf_op jit(solution)/shard_map/ppermute | solution.py:143
  76.9 22.4 %collective-permute-start.5 = (bf16[8,8,2,16,128]{4,3,2,1,0:T(8,128)(2,1)}, bf16[8,8,2,16,128]{4,3,2,1,0:T(8,128)(2,1)}, u32[]{:S(2)}, u32[]{:S(2)}) collective-permute-start(bf16[8,8,2,16,128]{4,3,2,1,0:T(8,128)(2,1)} %collective-permute-done.4.refs_1_), channel_id=1, source_target_pairs={{1,0},{2,1},{3,2},{5,4},{6,5},{7,6},{9,8},{10,9},{11,10},{13,12},{... | collective-permute-start | bytes 1572872 | tf_op jit(solution)/shard_map/ppermute | solution.py:144
  78.8 1.0 copy-start.3
  79.8 24.8 %all-to-all-start.1 = ((bf16[8,3,17,16,128]{4,3,2,1,0:T(8,128)(2,1)}), bf16[8,3,17,16,128]{4,3,2,1,0:T(8,128)(2,1)S(1)}, u32[]{:S(2)}, u32[]{:S(2)}) async-start(bf16[8,3,17,16,128]{4,3,2,1,0:T(8,128)(2,1)} %copy-done.9), calls=%async_computation.1 | async-start | bytes 3342336 | tf_op jit(solution)/shard_map/all_to_all | solution.py:267
  99.3 1.2 copy-start.4
  100.5 0.7 copy-start.12
  102.8 0.7 copy-start.11
  103.6 17.6 %collective-permute-start.9 = (bf16[2,2,272,128]{3,2,1,0:T(8,128)(2,1)}, bf16[2,2,272,128]{3,2,1,0:T(8,128)(2,1)}, u32[]{:S(2)}, u32[]{:S(2)}) collective-permute-start(bf16[2,2,272,128]{3,2,1,0:T(8,128)(2,1)} %get-tuple-element.33.refs_0_), channel_id=1, source_target_pairs={{0,1},{1,2},{2,3},{3,0},{4,5},{5,6},{6,7},{7,4},{8,9},{9,10},{10,1... | collective-permute-start | bytes 835592 | tf_op jit(solution)/shard_map/ppermute | solution.py:297
  103.6 25.7 %collective-permute-start.10 = (bf16[2,2,272,128]{3,2,1,0:T(8,128)(2,1)}, bf16[2,2,272,128]{3,2,1,0:T(8,128)(2,1)}, u32[]{:S(2)}, u32[]{:S(2)}) collective-permute-start(bf16[2,2,272,128]{3,2,1,0:T(8,128)(2,1)} %get-tuple-element.37), channel_id=1, source_target_pairs={{0,2},{1,3},{2,0},{3,1},{4,6},{5,7},{6,4},{7,5},{8,10},{9,11},{10,... | collective-permute-start | bytes 835592 | tf_op jit(solution)/shard_map/ppermute | solution.py:297
  104.6 7.6 %copy-start.1 = (bf16[8,3,17,16,128]{4,3,2,1,0:T(8,128)(2,1)}, bf16[8,3,17,16,128]{4,3,2,1,0:T(8,128)(2,1)S(1)}, u32[]{:S(2)}) copy-start(bf16[8,3,17,16,128]{4,3,2,1,0:T(8,128)(2,1)S(1)} %all-to-all-done.1) | copy-start | bytes 5013508
  104.6 16.6 %all-to-all-start = ((bf16[8,1,17,16,128]{4,3,2,1,0:T(8,128)(2,1)}), bf16[8,1,17,16,128]{4,3,2,1,0:T(8,128)(2,1)}, u32[]{:S(2)}, u32[]{:S(2)}) async-start(bf16[8,1,17,16,128]{4,3,2,1,0:T(8,128)(2,1)} %get-tuple-element.27), calls=%async_computation | async-start | bytes 1114112 | tf_op jit(solution)/shard_map/all_to_all | solution.py:267
  110.2 32.8 %collective-permute-start.11 = (bf16[2,2,272,128]{3,2,1,0:T(8,128)(2,1)}, bf16[2,2,272,128]{3,2,1,0:T(8,128)(2,1)}, u32[]{:S(2)}, u32[]{:S(2)}) collective-permute-start(bf16[2,2,272,128]{3,2,1,0:T(8,128)(2,1)} %copy-done.11), channel_id=1, source_target_pairs={{0,3},{1,0},{2,1},{3,2},{4,7},{5,4},{6,5},{7,6},{8,11},{9,8},{10,9... | collective-permute-start | bytes 835592 | tf_op jit(solution)/shard_map/ppermute | solution.py:297
  110.3 8.2 %copy-start.14 = (bf16[8,8,2,16,128]{4,3,2,1,0:T(8,128)(2,1)S(1)}, bf16[8,8,2,16,128]{4,3,2,1,0:T(8,128)(2,1)}, u32[]{:S(2)}) copy-start(bf16[8,8,2,16,128]{4,3,2,1,0:T(8,128)(2,1)} %copy-done.13) | copy-start | bytes 1572868
  112.2 6.3 %copy-start.7 = (bf16[8,8,2,16,128]{4,3,2,1,0:T(8,128)(2,1)S(1)}, bf16[8,8,2,16,128]{4,3,2,1,0:T(8,128)(2,1)}, u32[]{:S(2)}) copy-start(bf16[8,8,2,16,128]{4,3,2,1,0:T(8,128)(2,1)} %copy-done.6) | copy-start | bytes 1572868
  112.2 6.3 %copy-start.8 = (bf16[8,8,2,16,128]{4,3,2,1,0:T(8,128)(2,1)S(1)}, bf16[8,8,2,16,128]{4,3,2,1,0:T(8,128)(2,1)}, u32[]{:S(2)}) copy-start(bf16[8,8,2,16,128]{4,3,2,1,0:T(8,128)(2,1)} %broadcast_select_fusion.1.refs_2_) | copy-start | bytes 1572868
  112.3 49.5 %collective-permute-start.15 = (bf16[2,3,272,128]{3,2,1,0:T(8,128)(2,1)}, bf16[2,3,272,128]{3,2,1,0:T(8,128)(2,1)}, u32[]{:S(2)}, u32[]{:S(2)}) collective-permute-start(bf16[2,3,272,128]{3,2,1,0:T(8,128)(2,1)} %get-tuple-element.36.refs_0_), channel_id=1, source_target_pairs={{0,1},{1,2},{2,3},{3,0},{4,5},{5,6},{6,7},{7,4},{8,9},{9,10},{10,1... | collective-permute-start | bytes 1253384 | tf_op jit(solution)/shard_map/ppermute | solution.py:297
  114.3 56.4 %collective-permute-start.16 = (bf16[2,3,272,128]{3,2,1,0:T(8,128)(2,1)}, bf16[2,3,272,128]{3,2,1,0:T(8,128)(2,1)}, u32[]{:S(2)}, u32[]{:S(2)}) collective-permute-start(bf16[2,3,272,128]{3,2,1,0:T(8,128)(2,1)} %get-tuple-element.42), channel_id=1, source_target_pairs={{0,2},{1,3},{2,0},{3,1},{4,6},{5,7},{6,4},{7,5},{8,10},{9,11},{10,... | collective-permute-start | bytes 1253384 | tf_op jit(solution)/shard_map/ppermute | solution.py:297
  121.2 49.5 %collective-permute-start.17 = (bf16[2,3,272,128]{3,2,1,0:T(8,128)(2,1)}, bf16[2,3,272,128]{3,2,1,0:T(8,128)(2,1)}, u32[]{:S(2)}, u32[]{:S(2)}) collective-permute-start(bf16[2,3,272,128]{3,2,1,0:T(8,128)(2,1)} %get-tuple-element.43), channel_id=1, source_target_pairs={{0,3},{1,0},{2,1},{3,2},{4,7},{5,4},{6,5},{7,6},{8,11},{9,8},{10,9... | collective-permute-start | bytes 1253384 | tf_op jit(solution)/shard_map/ppermute | solution.py:297
  144.1 22.1 %copy-start.5 = (bf16[8,2,17,16,128]{4,3,2,1,0:T(8,128)(2,1)S(1)}, bf16[8,2,17,16,128]{4,3,2,1,0:T(8,128)(2,1)}, u32[]{:S(2)}) copy-start(bf16[8,2,17,16,128]{4,3,2,1,0:T(8,128)(2,1)} %copy-done.3) | copy-start | bytes 3342340
  144.1 32.6 %collective-permute-start.12 = (bf16[2,1,272,128]{3,2,1,0:T(8,128)(2,1)S(1)}, bf16[2,1,272,128]{3,2,1,0:T(8,128)(2,1)S(1)}, u32[]{:S(2)}, u32[]{:S(2)}) collective-permute-start(bf16[2,1,272,128]{3,2,1,0:T(8,128)(2,1)S(1)} %get-tuple-element.39), channel_id=1, source_target_pairs={{0,1},{1,2},{2,3},{3,0},{4,5},{5,6},{6,7},{7,4},{8,9},{9,10},{10,1... | collective-permute-start | bytes 417800 | tf_op jit(solution)/shard_map/ppermute | solution.py:297
  144.2 32.5 %collective-permute-start.13 = (bf16[2,1,272,128]{3,2,1,0:T(8,128)(2,1)S(1)}, bf16[2,1,272,128]{3,2,1,0:T(8,128)(2,1)S(1)}, u32[]{:S(2)}, u32[]{:S(2)}) collective-permute-start(bf16[2,1,272,128]{3,2,1,0:T(8,128)(2,1)S(1)} %get-tuple-element.40), channel_id=1, source_target_pairs={{0,2},{1,3},{2,0},{3,1},{4,6},{5,7},{6,4},{7,5},{8,10},{9,11},{10,... | collective-permute-start | bytes 417800 | tf_op jit(solution)/shard_map/ppermute | solution.py:297
  161.7 15.0 %collective-permute-start.14 = (bf16[2,1,272,128]{3,2,1,0:T(8,128)(2,1)S(1)}, bf16[2,1,272,128]{3,2,1,0:T(8,128)(2,1)S(1)}, u32[]{:S(2)}, u32[]{:S(2)}) collective-permute-start(bf16[2,1,272,128]{3,2,1,0:T(8,128)(2,1)S(1)} %get-tuple-element.41), channel_id=1, source_target_pairs={{0,3},{1,0},{2,1},{3,2},{4,7},{5,4},{6,5},{7,6},{8,11},{9,8},{10,9... | collective-permute-start | bytes 417800 | tf_op jit(solution)/shard_map/ppermute | solution.py:297
  166.2 4.5 %copy-start.2 = (bf16[8,3,17,16,128]{4,3,2,1,0:T(8,128)(2,1)S(1)}, bf16[8,3,17,16,128]{4,3,2,1,0:T(8,128)(2,1)}, u32[]{:S(2)}) copy-start(bf16[8,3,17,16,128]{4,3,2,1,0:T(8,128)(2,1)} %copy-done.1) | copy-start | bytes 5013508

commit v7 on v6

--- a/solution.py
+++ b/solution.py
@@ -17,7 +17,7 @@
 QUERY, KEY, VALUE, OUT = range(4)
 CUT_MICROS = 10
 TOKEN_MICROS = 20
-CUTS = (0, 2, 4, 7, 8)
+CUTS = (0, 2, 4, 6, 8)
 VMEM_LIMIT = 16 * 1024 * 1024
 
 
@@ -89,9 +89,12 @@
     )(param_offsets, owner_map, table)
 
 
+def corner_of(x):
+    return (1,) * (x.ndim - 2) + (min(16, x.shape[-2]), LANES)
+
+
 def corner(x):
-    block = (1,) * (x.ndim - 2) + (min(16, x.shape[-2]), LANES)
-    return pl.BlockSpec(block, lambda _: (0,) * x.ndim)
+    return pl.BlockSpec(corner_of(x), lambda _: (0,) * x.ndim)
 
 
 def cut(rows, slice_map, blocks, shifts, waits, micros):
@@ -138,11 +141,40 @@
     )(*waits)
 
 
-def line_step(up, down, axis, ways):
+def neighbours(x, axis, ways):
     return (
-        lax.ppermute(up, axis, [(i, i + 1) for i in range(ways - 1)]),
-        lax.ppermute(down, axis, [(i + 1, i) for i in range(ways - 1)]),
-    )
+        lax.ppermute(x, axis, [(i, i + 1) for i in range(ways - 1)]),
+        lax.ppermute(x, axis, [(i + 1, i) for i in range(ways - 1)]),
+    )
+
+
+def pass_on(me, across, up, down, waits):
+    def kernel(me_ref, first, above, below, *refs):
+        out = refs[-1]
+        out[0] = first[...]
+
+        @pl.when(me_ref[0] == 2)
+        def _():
+            out[1] = above[...]
+
+        @pl.when(me_ref[0] != 2)
+        def _():
+            out[1] = below[...]
+
+    whole = pl.BlockSpec(across.shape, lambda _, me_ref: (0,) * across.ndim)
+    corners = [pl.BlockSpec(corner_of(x), lambda _, me_ref, n=x.ndim: (0,) * n) for x in waits]
+    return pl.pallas_call(
+        kernel,
+        grid_spec=pltpu.PrefetchScalarGridSpec(
+            num_scalar_prefetch=1,
+            grid=(1,),
+            in_specs=[whole] * 3 + corners,
+            out_specs=pl.BlockSpec((2,) + across.shape, lambda _, me_ref: (0,) * (across.ndim + 1)),
+        ),
+        out_shape=jax.ShapeDtypeStruct((2,) + across.shape, across.dtype),
+        compiler_params=pltpu.CompilerParams(vmem_limit_bytes=VMEM_LIMIT),
+        name="pass_on",
+    )(me.reshape(1), across, up, down, *waits)
 
 
 def assemble(me, spread_parts):
@@ -277,21 +309,26 @@
         [(range(item_count), (KEY, VALUE))] + [(items, (QUERY, OUT)) for items in chunks],
     )
     pairs = over_fsdp(pairs, (2, row_counts[KEY], LANES))
-    up, down = [pairs], [pairs]
-    for _ in shifts:
-        above, below = line_step(up[-1], down[-1], "tp", t_ways)
-        up.append(above)
-        down.append(below)
+    up, down = neighbours(pairs, "tp", t_ways)
+    if t_ways == 4:
+        across = lax.ppermute(pairs, "tp", [(0, 2), (3, 1)])
+        near = token([up, down, across], TOKEN_MICROS)
+    else:
+        ups, downs = [pairs, up], [pairs, down]
+        for _ in range(2, t_ways):
+            ups.append(neighbours(ups[-1], "tp", t_ways)[0])
+            downs.append(neighbours(downs[-1], "tp", t_ways)[1])
 
     exchanged, sent = [], []
-    near_pairs = token(up[2:3] + down[2:3], TOKEN_MICROS)
     for at in range(len(chunks)):
         rows = over_fsdp(to_send[at], (row_counts[QUERY] + row_counts[OUT], LANES))
         waits = sent[at - 1][:1] if at else []
-        if at == 1:
-            waits = waits + up[3:] + down[3:] + [near_pairs]
-        elif at:
+        if at >= 2:
             waits = waits + exchanged[at - 2][1]
+        if t_ways == 4 and at == 1:
+            waits = waits + [near]
+        if t_ways == 4 and at == len(chunks) - 1:
+            waits = waits + [far]
         pieces = cut(rows, slice_map, blocks, shifts, waits, CUT_MICROS)
         came = [
             lax.ppermute(piece, "tp", [(i, (i + shift) % t_ways) for i in range(t_ways)])
@@ -299,6 +336,20 @@
         ]
         exchanged.append((rows, came))
         sent.append(list(pieces))
+        if t_ways == 4 and at == 1:
+            far = lax.ppermute(
+                pass_on(me, across, up, down, sent[1][:1]), "tp", [(1, 0), (2, 3)]
+            )
+    if t_ways == 4:
+        ends = jnp.logical_or(me == 0, me == 3)
+        spread = [
+            pairs,
+            jnp.where(me == 0, far[0], up),
+            jnp.where(ends, far[1], across),
+            jnp.where(me == 3, far[0], down),
+        ]
+    else:
+        spread = [pairs] + [jnp.where(me >= d, ups[d], downs[t_ways - d]) for d in shifts]
     slice_row = lax.dynamic_index_in_dim(slice_map, lax.axis_index("fsdp"), 0, keepdims=False)
     near = [jnp.where(me >= d, up[d], down[t_ways - d]) for d in shifts]
 
@@ -308,14 +359,14 @@
             for kind in (QUERY, OUT)
         )
         where = jnp.stack([me, slice_row[me]])
-        matrices = assemble(me, [pairs] + near)
+        matrices = assemble(me, spread)
         outs = None
         for items, (rows, came) in zip(chunks, exchanged):
             outs = absorb(where, items, rows, came, matrices, outs, shapes)
         return tuple(out.reshape(layer_count, per_group, -1, KVR) for out in outs)
 
     order = lax.rem(me - jnp.arange(t_ways, dtype=jnp.int32) + t_ways, jnp.int32(t_ways))
-    matrices = jnp.take(jnp.stack([pairs] + near), order, axis=0).transpose(2, 3, 1, 0, 4, 5)
+    matrices = jnp.take(jnp.stack(spread), order, axis=0).transpose(2, 3, 1, 0, 4, 5)
     matrices = matrices.reshape(item_count, 2, -1, KVR)
     done = [
         absorb_plain(

time: 183 us -> 171 us (0.934)
  waiting for transfers between devices: 74.8 us -> 61.6 us
  Pallas kernels: 30.5 us -> 33.6 us
    ppermute x12, waiting for transfers between devices: 40.8 us -> 23.4 us  [per_device(): lax.ppermute(piece, 'tp', [(i, (i + shift) % t_ways) for i in range(t_way...]
    all_to_all x4, waiting for transfers between devices: 1.05 us -> 12.9 us  [over_fsdp(): x = lax.all_to_all(x, 'fsdp', split_axis=0, concat_axis=0, tiled=True)]
    ppermute x6 -> x4, waiting for transfers between devices: 33 us -> 25.3 us  [the longest x1 20.5 us: per_device(): lax.ppermute(pass_on(me, across, up, down, sent[1][:1]), 'tp', [(1, 0), (...]
    ppermute x6 -> x4, starting transfers between devices: 16.4 us -> 11.1 us  [the longest x1 5.59 us: neighbours(): lax.ppermute(x, axis, [(i + 1, i) for i in range(ways - 1)])]
    ppermute x12, starting transfers between devices: 9.9 us -> 15 us  [per_device(): lax.ppermute(piece, 'tp', [(i, (i + shift) % t_ways) for i in range(t_way...]
    pallas_call x1, Pallas kernels: 1.09 us -> 4 us  [assemble(): pl.pallas_call(kernel, grid_spec=pltpu.PrefetchScalarGridSpec(num_scalar_...]
  transfers between devices with their start and end apart: 22 -> 20, of which waited for: 9 -> 10; matrix products, arithmetic and copies ran while one was open for 2% -> 2% of each run, Pallas kernels for 13% -> 15%
where the time goes in v7:
time: 171 us; the launch traced here: 170 us
  waiting for transfers between devices  61.6 us (36%)
  starting transfers between devices  46.6 us (27%)
  Pallas kernels  33.6 us (20%)
  blocking collectives  12.4 us (7%)
  local copies, waits for them, and re-layouts  12.3 us (7%)
  other arithmetic  2.26 us (1%)
    ppermute x12, waiting for transfers between devices, per_device(): lax.ppermute(piece, 'tp', [(i, (i + shift) % t_ways) for i in range(t_way...  23.4 us
    all_to_all x4, starting transfers between devices, over_fsdp(): x = lax.all_to_all(x, 'fsdp', split_axis=0, concat_axis=0, tiled=True)  20.6 us
    ppermute x1, waiting for transfers between devices, per_device(): lax.ppermute(pass_on(me, across, up, down, sent[1][:1]), 'tp', [(1, 0), (...  20.5 us
    pallas_call x4, Pallas kernels, absorb(): pl.pallas_call(kernel, grid_spec=pltpu.PrefetchScalarGridSpec(num_scalar_...  17.7 us
    ppermute x12, starting transfers between devices, per_device(): lax.ppermute(piece, 'tp', [(i, (i + shift) % t_ways) for i in range(t_way...  15 us
    all_to_all x4, waiting for transfers between devices, over_fsdp(): x = lax.all_to_all(x, 'fsdp', split_axis=0, concat_axis=0, tiled=True)  12.9 us
    all_to_all x1, blocking collectives, over_fsdp(): x = lax.all_to_all(x, 'fsdp', split_axis=0, concat_axis=0, tiled=True)  12.4 us
    unnamed x37, local copies, waits for them, and re-layouts  11.7 us
  transfers between devices with their start and end apart: 20, of which 10 were waited for; matrix products, arithmetic and copies ran while one was open for 2% of the time, Pallas kernels for 15%

profile of v7, /device:TPU:10, one launch (start us, length us, event | category | flops | bytes accessed | tf_op | source)
XLA Modules:
  0.0 169.6 jit_solution(6773682329339268720)
XLA Ops:
  0.6 0.8 copy.12.offsets
  1.4 3.1 %copy.17 = bf16[1,2,9728,128]{3,2,1,0:T(8,128)(2,1)S(1)} copy(bf16[1,2,9728,128]{3,1,2,0:T(2,128)(2,1)} %bitcast.30) | data formatting | bytes 9961472
  4.6 0.0 copy-start.16
  4.6 3.2 %pack.1 = (bf16[8,8,2,16,128]{4,3,2,1,0:T(8,128)(2,1)S(1)}, bf16[8,2,17,16,128]{4,3,2,1,0:T(8,128)(2,1)}, bf16[8,2,17,16,128]{4,3,2,1,0:T(8,128)(2,1)S(1)}, bf16...) custom-call(s32[2,32,4]{2,1,0:T(8,128)S(1)} %copy.12.offsets, s32[2,32]{1,0:T(2,128)S(1)} %copy-done.13, ...), custom_call_target="tpu_custom_call" | custom-call | bytes 9961472 | tf_op jit(solution)/shard_map/pack/pallas_call | solution.py:69
  7.7 1.0 copy-done.6
  8.7 1.0 copy-done.7
  9.7 1.0 copy-done.8
  10.7 12.4 %all_to_all.25.refs_0_ = bf16[8,8,2,16,128]{4,3,2,1,0:T(8,128)(2,1)} all-to-all(bf16[8,8,2,16,128]{4,3,2,1,0:T(8,128)(2,1)S(1)} %get-tuple-element.32), channel_id=1, replica_groups=mesh['fsdp'=8,'tp'=4] {'fsdp'}, dimensions={0} | all-to-all | bytes 1048576 | tf_op jit(solution)/shard_map/all_to_all | solution.py:299
  23.2 4.9 %all-to-all-start.3 = ((bf16[8,2,17,16,128]{4,3,2,1,0:T(8,128)(2,1)}), bf16[8,2,17,16,128]{4,3,2,1,0:T(8,128)(2,1)S(1)}, u32[]{:S(2)}, u32[]{:S(2)}) async-start(bf16[8,2,17,16,128]{4,3,2,1,0:T(8,128)(2,1)} %get-tuple-element.30), calls=%async_computation.3 | async-start | bytes 2228224 | tf_op jit(solution)/shard_map/all_to_all | solution.py:299
  28.1 0.1 copy.16.mapped
  28.2 0.6 dynamic_slice.7
  28.8 0.7 pad_add_fusion.at
  29.5 1.3 collective-permute-start.2
  30.8 5.6 %collective-permute-start.1 = (bf16[8,8,2,16,128]{4,3,2,1,0:T(8,128)(2,1)}, bf16[8,8,2,16,128]{4,3,2,1,0:T(8,128)(2,1)S(1)}, u32[]{:S(2)}, u32[]{:S(2)}) collective-permute-start(bf16[8,8,2,16,128]{4,3,2,1,0:T(8,128)(2,1)} %all_to_all.25.refs_0_), channel_id=1, source_target_pairs={{1,0},{2,1},{3,2},{5,4},{6,5},{7,6},{9,8},{10,9},{11,10},{13,12},{... | collective-permute-start | bytes 1572872 | tf_op jit(solution)/shard_map/ppermute | solution.py:147
  36.4 1.9 %collective-permute-start = (bf16[8,8,2,16,128]{4,3,2,1,0:T(8,128)(2,1)}, bf16[8,8,2,16,128]{4,3,2,1,0:T(8,128)(2,1)}, u32[]{:S(2)}, u32[]{:S(2)}) collective-permute-start(bf16[8,8,2,16,128]{4,3,2,1,0:T(8,128)(2,1)} %all_to_all.25.refs_0_), channel_id=1, source_target_pairs={{0,1},{1,2},{2,3},{4,5},{5,6},{6,7},{8,9},{9,10},{10,11},{12,13},{... | collective-permute-start | bytes 1572872 | tf_op jit(solution)/shard_map/ppermute | solution.py:146
  38.3 4.4 %all-to-all-done.3 = bf16[8,2,17,16,128]{4,3,2,1,0:T(8,128)(2,1)S(1)} async-done(((bf16[8,2,17,16,128]{4,3,2,1,0:T(8,128)(2,1)}), bf16[8,2,17,16,128]{4,3,2,1,0:T(8,128)(2,1)S(1)}, u32[]{:S(2)}, u32[]{:S(2)}) %all-to-all-start.3) | async-done | bytes 1114144 | tf_op jit(solution)/shard_map/all_to_all | solution.py:299
  42.7 5.0 %all-to-all-start.2 = ((bf16[8,2,17,16,128]{4,3,2,1,0:T(8,128)(2,1)}), bf16[8,2,17,16,128]{4,3,2,1,0:T(8,128)(2,1)S(1)}, u32[]{:S(2)}, u32[]{:S(2)}) async-start(bf16[8,2,17,16,128]{4,3,2,1,0:T(8,128)(2,1)} %copy-done.8), calls=%async_computation.2 | async-start | bytes 2228224 | tf_op jit(solution)/shard_map/all_to_all | solution.py:299
  47.7 1.6 cut.4
  49.3 2.6 %collective-permute-start.4 = (bf16[2,2,272,128]{3,2,1,0:T(8,128)(2,1)}, bf16[2,2,272,128]{3,2,1,0:T(8,128)(2,1)}, u32[]{:S(2)}, u32[]{:S(2)}) collective-permute-start(bf16[2,2,272,128]{3,2,1,0:T(8,128)(2,1)} %get-tuple-element.34), channel_id=1, source_target_pairs={{0,2},{1,3},{2,0},{3,1},{4,6},{5,7},{6,4},{7,5},{8,10},{9,11},{10,... | collective-permute-start | bytes 835592 | tf_op jit(solution)/shard_map/ppermute | solution.py:334
  51.9 0.4 collective-permute-start.5
  52.4 0.0 collective-permute-done.2.refs_2_.first
  52.4 1.6 collective-permute-start.3
  53.9 4.6 %collective-permute-done.1.refs_1_.below = bf16[8,8,2,16,128]{4,3,2,1,0:T(8,128)(2,1)S(1)} collective-permute-done((bf16[8,8,2,16,128]{4,3,2,1,0:T(8,128)(2,1)}, bf16[8,8,2,16,128]{4,3,2,1,0:T(8,128)(2,1)S(1)}, u32[]{:S(2)}, u32[]{:S(2)}) %collective-permute-start.1) | collective-permute-done | bytes 524320 | tf_op jit(solution)/shard_map/ppermute | solution.py:147
  58.6 0.2 collective-permute-done.refs_0_.above
  58.8 0.6 copy-done.3
  59.4 1.3 token_.1.refs_1_
  60.7 1.7 all-to-all-done.2
  62.3 5.0 %all-to-all-start.1 = ((bf16[8,2,17,16,128]{4,3,2,1,0:T(8,128)(2,1)}), bf16[8,2,17,16,128]{4,3,2,1,0:T(8,128)(2,1)S(1)}, u32[]{:S(2)}, u32[]{:S(2)}) async-start(bf16[8,2,17,16,128]{4,3,2,1,0:T(8,128)(2,1)} %copy-done.7), calls=%async_computation.1 | async-start | bytes 2228224 | tf_op jit(solution)/shard_map/all_to_all | solution.py:299
  67.3 0.7 copy-done.15
  68.0 1.7 cut.5
  69.7 0.7 copy-done.14
  70.4 2.6 %collective-permute-start.7 = (bf16[2,2,272,128]{3,2,1,0:T(8,128)(2,1)}, bf16[2,2,272,128]{3,2,1,0:T(8,128)(2,1)}, u32[]{:S(2)}, u32[]{:S(2)}) collective-permute-start(bf16[2,2,272,128]{3,2,1,0:T(8,128)(2,1)} %get-tuple-element.37), channel_id=1, source_target_pairs={{0,2},{1,3},{2,0},{3,1},{4,6},{5,7},{6,4},{7,5},{8,10},{9,11},{10,... | collective-permute-start | bytes 835592 | tf_op jit(solution)/shard_map/ppermute | solution.py:334
  73.0 0.0 collective-permute-start.6
  73.0 1.1 pass_on.1
  74.1 0.0 copy-start.9
  74.1 1.0 copy-done.9
  75.1 6.8 %all-to-all-done.1 = bf16[8,2,17,16,128]{4,3,2,1,0:T(8,128)(2,1)S(1)} async-done(((bf16[8,2,17,16,128]{4,3,2,1,0:T(8,128)(2,1)}), bf16[8,2,17,16,128]{4,3,2,1,0:T(8,128)(2,1)S(1)}, u32[]{:S(2)}, u32[]{:S(2)}) %all-to-all-start.1) | async-done | bytes 1114144 | tf_op jit(solution)/shard_map/all_to_all | solution.py:299
  81.9 5.7 %all-to-all-start = ((bf16[8,2,17,16,128]{4,3,2,1,0:T(8,128)(2,1)}), bf16[8,2,17,16,128]{4,3,2,1,0:T(8,128)(2,1)}, u32[]{:S(2)}, u32[]{:S(2)}) async-start(bf16[8,2,17,16,128]{4,3,2,1,0:T(8,128)(2,1)} %copy-done.6), calls=%async_computation | async-start | bytes 2228224 | tf_op jit(solution)/shard_map/all_to_all | solution.py:299
  87.6 0.0 collective-permute-done.4.refs_2_
  87.6 0.5 collective-permute-start.8
  88.1 5.6 %collective-permute-done.5.refs_3_ = bf16[2,2,272,128]{3,2,1,0:T(8,128)(2,1)} collective-permute-done((bf16[2,2,272,128]{3,2,1,0:T(8,128)(2,1)}, bf16[2,2,272,128]{3,2,1,0:T(8,128)(2,1)}, u32[]{:S(2)}, u32[]{:S(2)}) %collective-permute-start.5) | collective-permute-done | bytes 278560 | tf_op jit(solution)/shard_map/ppermute | solution.py:334
  93.7 2.3 %collective-permute-start.9 = (bf16[2,8,8,2,16,128]{5,4,3,2,1,0:T(8,128)(2,1)}, bf16[2,8,8,2,16,128]{5,4,3,2,1,0:T(8,128)(2,1)}, u32[]{:S(2)}, u32[]{:S(2)}) collective-permute-start(bf16[2,8,8,2,16,128]{5,4,3,2,1,0:T(8,128)(2,1)} %copy-done.9), channel_id=1, source_target_pairs={{1,0},{2,3},{5,4},{6,7},{9,8},{10,11},{13,12},{14,15},{17,16},{18,... | collective-permute-start | bytes 3145736 | tf_op jit(solution)/shard_map/ppermute | solution.py:340
  96.0 0.0 collective-permute-done.3.refs_1_
  96.0 1.7 %cut.6 = (bf16[2,2,272,128]{3,2,1,0:T(8,128)(2,1)}, bf16[2,2,272,128]{3,2,1,0:T(8,128)(2,1)}, bf16[2,2,272,128]{3,2,1,0:T(8,128)(2,1)}) custom-call(s32[8,4]{1,0:T(8,128)S(1)} %copy.16.mapped, bf16[8,2,272,128]{3,2,1,0:T(8,128)(2,1)S(1)} %bitcast.26, bf16[2,2,272,128]{3,2,1,0:T(8,128)(2,1)} %get-tuple-element.33.refs_0_, ...), custom_call_target="tpu_custom_call" | custom-call | flops 11500000256 | bytes 1671168 | tf_op jit(solution)/shard_map/cut/pallas_call | solution.py:111
  97.7 1.1 collective-permute-done.7.refs_2_
  98.8 2.4 %collective-permute-start.15 = (bf16[2,2,272,128]{3,2,1,0:T(8,128)(2,1)}, bf16[2,2,272,128]{3,2,1,0:T(8,128)(2,1)}, u32[]{:S(2)}, u32[]{:S(2)}) collective-permute-start(bf16[2,2,272,128]{3,2,1,0:T(8,128)(2,1)} %get-tuple-element.43), channel_id=1, source_target_pairs={{0,3},{1,0},{2,1},{3,2},{4,7},{5,4},{6,5},{7,6},{8,11},{9,8},{10,9... | collective-permute-start | bytes 835592 | tf_op jit(solution)/shard_map/ppermute | solution.py:334
  101.2 13.4 %collective-permute-done.8.refs_3_ = bf16[2,2,272,128]{3,2,1,0:T(8,128)(2,1)S(1)} collective-permute-done((bf16[2,2,272,128]{3,2,1,0:T(8,128)(2,1)}, bf16[2,2,272,128]{3,2,1,0:T(8,128)(2,1)S(1)}, u32[]{:S(2)}, u32[]{:S(2)}) %collective-permute-start.8) | collective-permute-done | bytes 278560 | tf_op jit(solution)/shard_map/ppermute | solution.py:334
  114.5 0.7 copy-done.10
  115.3 0.0 collective-permute-start.13
  115.3 20.5 %collective-permute-done.9.refs_4_ = bf16[2,8,8,2,16,128]{5,4,3,2,1,0:T(8,128)(2,1)} collective-permute-done((bf16[2,8,8,2,16,128]{5,4,3,2,1,0:T(8,128)(2,1)}, bf16[2,8,8,2,16,128]{5,4,3,2,1,0:T(8,128)(2,1)}, u32[]{:S(2)}, u32[]{:S(2)}) %collective-permute-start.9) | collective-permute-done | bytes 1048608 | tf_op jit(solution)/shard_map/ppermute | solution.py:340
  135.8 1.0 copy-done.11
  136.7 1.4 cut.7
  138.2 0.1 collective-permute-start.10
  138.2 4.8 %collective-permute-start.11 = (bf16[2,2,272,128]{3,2,1,0:T(8,128)(2,1)S(1)}, bf16[2,2,272,128]{3,2,1,0:T(8,128)(2,1)S(1)}, u32[]{:S(2)}, u32[]{:S(2)}) collective-permute-start(bf16[2,2,272,128]{3,2,1,0:T(8,128)(2,1)S(1)} %get-tuple-element.40), channel_id=1, source_target_pairs={{0,2},{1,3},{2,0},{3,1},{4,6},{5,7},{6,4},{7,5},{8,10},{9,11},{10,... | collective-permute-start | bytes 835592 | tf_op jit(solution)/shard_map/ppermute | solution.py:334
  143.1 0.0 collective-permute-done.14.refs_2_
  143.1 0.0 collective-permute-start.12
  143.1 1.6 broadcast_select_fusion
  144.7 4.0 %assemble.1.refs_4_ = bf16[8,2,128,512]{3,2,1,0:T(8,128)(2,1)S(1)} custom-call(s32[1]{0:T(128)} %bitcast.me_ref, bf16[8,8,2,16,128]{4,3,2,1,0:T(8,128)(2,1)} %all_to_all.25.refs_0_, bf16[8,8,2,16,128]{4,3,2,1,0:T(8,128)(2,1)S(1)} %get-tuple-element.54.refs_1_, bf16[8,8,2,16,128]{4,3,2,1,0:T(8,128)(2,1)S(1)} %get-tuple-element.53.refs_2_, ...), custom_call_target="tpu_custom_call" | custom-call | tf_op jit(solution)/shard_map/assemble/pallas_call | solution.py:200
  148.7 4.5 %absorb.4 = (bf16[8,2,4,48,512]{4,3,2,1,0:T(8,128)(2,1)}, bf16[8,2,4,224,512]{4,3,2,1,0:T(8,128)(2,1)}) custom-call(s32[2]{0:T(128)S(1)} %pad_add_fusion.at, bf16[8,2,272,128]{3,2,1,0:T(8,128)(2,1)S(1)} %bitcast.23, bf16[2,2,272,128]{3,2,1,0:T(8,128)(2,1)} %collective-permute-done.3.refs_1_, bf16[2,2,272,128]{3,2,1,0:T(8,128)(2,1)} %collective-permute-done.4.refs_2_, ...), custom_call_target="tpu_custom_call" | custom-call | flops 570425344 | bytes 5570560 | tf_op jit(solution)/shard_map/absorb/pallas_call | solution.py:244
  153.1 4.4 %absorb.5 = (bf16[8,2,4,48,512]{4,3,2,1,0:T(8,128)(2,1)}, bf16[8,2,4,224,512]{4,3,2,1,0:T(8,128)(2,1)}) custom-call(s32[2]{0:T(128)S(1)} %pad_add_fusion.at, bf16[8,2,272,128]{3,2,1,0:T(8,128)(2,1)S(1)} %bitcast.25, bf16[2,2,272,128]{3,2,1,0:T(8,128)(2,1)} %collective-permute-done.6.refs_1_, ...), custom_call_target="tpu_custom_call", output_to_operand_aliasing={{0}: (6, {}), {1}: (7, {})} | custom-call | flops 570425344 | bytes 5570560 | tf_op jit(solution)/shard_map/absorb/pallas_call | solution.py:244
  157.5 0.0 collective-permute-done.13.refs_1_
  157.5 4.5 %absorb.6 = (bf16[8,2,4,48,512]{4,3,2,1,0:T(8,128)(2,1)}, bf16[8,2,4,224,512]{4,3,2,1,0:T(8,128)(2,1)}) custom-call(s32[2]{0:T(128)S(1)} %pad_add_fusion.at, bf16[8,2,272,128]{3,2,1,0:T(8,128)(2,1)S(1)} %bitcast.27, bf16[2,2,272,128]{3,2,1,0:T(8,128)(2,1)} %collective-permute-done.13.refs_1_, ...), custom_call_target="tpu_custom_call", output_to_operand_aliasing={{0}: (6, {}), {1}: (7, {})} | custom-call | flops 570425344 | bytes 5570560 | tf_op jit(solution)/shard_map/absorb/pallas_call | solution.py:244
  162.0 3.3 %collective-permute-done.12.refs_3_ = bf16[2,2,272,128]{3,2,1,0:T(8,128)(2,1)S(1)} collective-permute-done((bf16[2,2,272,128]{3,2,1,0:T(8,128)(2,1)S(1)}, bf16[2,2,272,128]{3,2,1,0:T(8,128)(2,1)S(1)}, u32[]{:S(2)}, u32[]{:S(2)}) %collective-permute-start.12) | collective-permute-done | bytes 278560 | tf_op jit(solution)/shard_map/ppermute | solution.py:334
  165.3 4.3 %absorb.7 = (bf16[8,2,4,48,512]{4,3,2,1,0:T(8,128)(2,1)}, bf16[8,2,4,224,512]{4,3,2,1,0:T(8,128)(2,1)}) custom-call(s32[2]{0:T(128)S(1)} %pad_add_fusion.at, bf16[8,2,272,128]{3,2,1,0:T(8,128)(2,1)} %bitcast.2.source.refs_0_, bf16[2,2,272,128]{3,2,1,0:T(8,128)(2,1)S(1)} %collective-permute-done.10.refs_1_, ...), custom_call_target="tpu_custom_call", output_to_operand_aliasing={{0}: (6, {}), {1}: (7, {})} | custom-call | flops 570425344 | bytes 5570560 | tf_op jit(solution)/shard_map/absorb/pallas_call | solution.py:244
  (29 shorter events, 0.1 us)
Async XLA Ops:
  1.4 3.1 %copy-start.13 = (s32[2,32]{1,0:T(2,128)S(1)}, s32[2,32]{1,0:T(2,128)}, u32[]{:S(2)}) copy-start(s32[2,32]{1,0:T(2,128)} %owners.1) | copy-start | bytes 772
  4.6 23.6 %copy-start.16 = (s32[8,4]{0,1:T(4,128)S(1)}, s32[8,4]{0,1:T(4,128)}, u32[]{:S(2)}) copy-start(s32[8,4]{0,1:T(4,128)} %param.7) | copy-start | bytes 388
  7.7 1.0 copy-start.6
  8.7 1.0 copy-start.7
  9.7 1.0 copy-start.8
  23.2 19.6 %all-to-all-start.3 = ((bf16[8,2,17,16,128]{4,3,2,1,0:T(8,128)(2,1)}), bf16[8,2,17,16,128]{4,3,2,1,0:T(8,128)(2,1)S(1)}, u32[]{:S(2)}, u32[]{:S(2)}) async-start(bf16[8,2,17,16,128]{4,3,2,1,0:T(8,128)(2,1)} %get-tuple-element.30), calls=%async_computation.3 | async-start | bytes 2228224 | tf_op jit(solution)/shard_map/all_to_all | solution.py:299
  29.5 22.9 %collective-permute-start.2 = (bf16[8,8,2,16,128]{4,3,2,1,0:T(8,128)(2,1)}, bf16[8,8,2,16,128]{4,3,2,1,0:T(8,128)(2,1)S(1)}, u32[]{:S(2)}, u32[]{:S(2)}) collective-permute-start(bf16[8,8,2,16,128]{4,3,2,1,0:T(8,128)(2,1)} %all_to_all.25.refs_0_), channel_id=1, source_target_pairs={{0,2},{3,1},{4,6},{7,5},{8,10},{11,9},{12,14},{15,13},{16,18},{19,... | collective-permute-start | bytes 1572872 | tf_op jit(solution)/shard_map/ppermute | solution.py:314
  30.8 27.8 %collective-permute-start.1 = (bf16[8,8,2,16,128]{4,3,2,1,0:T(8,128)(2,1)}, bf16[8,8,2,16,128]{4,3,2,1,0:T(8,128)(2,1)S(1)}, u32[]{:S(2)}, u32[]{:S(2)}) collective-permute-start(bf16[8,8,2,16,128]{4,3,2,1,0:T(8,128)(2,1)} %all_to_all.25.refs_0_), channel_id=1, source_target_pairs={{1,0},{2,1},{3,2},{5,4},{6,5},{7,6},{9,8},{10,9},{11,10},{13,12},{... | collective-permute-start | bytes 1572872 | tf_op jit(solution)/shard_map/ppermute | solution.py:147
  36.4 22.4 %collective-permute-start = (bf16[8,8,2,16,128]{4,3,2,1,0:T(8,128)(2,1)}, bf16[8,8,2,16,128]{4,3,2,1,0:T(8,128)(2,1)}, u32[]{:S(2)}, u32[]{:S(2)}) collective-permute-start(bf16[8,8,2,16,128]{4,3,2,1,0:T(8,128)(2,1)} %all_to_all.25.refs_0_), channel_id=1, source_target_pairs={{0,1},{1,2},{2,3},{4,5},{5,6},{6,7},{8,9},{9,10},{10,11},{12,13},{... | collective-permute-start | bytes 1572872 | tf_op jit(solution)/shard_map/ppermute | solution.py:146
  42.7 19.6 %all-to-all-start.2 = ((bf16[8,2,17,16,128]{4,3,2,1,0:T(8,128)(2,1)}), bf16[8,2,17,16,128]{4,3,2,1,0:T(8,128)(2,1)S(1)}, u32[]{:S(2)}, u32[]{:S(2)}) async-start(bf16[8,2,17,16,128]{4,3,2,1,0:T(8,128)(2,1)} %copy-done.8), calls=%async_computation.2 | async-start | bytes 2228224 | tf_op jit(solution)/shard_map/all_to_all | solution.py:299
  49.3 38.3 %collective-permute-start.4 = (bf16[2,2,272,128]{3,2,1,0:T(8,128)(2,1)}, bf16[2,2,272,128]{3,2,1,0:T(8,128)(2,1)}, u32[]{:S(2)}, u32[]{:S(2)}) collective-permute-start(bf16[2,2,272,128]{3,2,1,0:T(8,128)(2,1)} %get-tuple-element.34), channel_id=1, source_target_pairs={{0,2},{1,3},{2,0},{3,1},{4,6},{5,7},{6,4},{7,5},{8,10},{9,11},{10,... | collective-permute-start | bytes 835592 | tf_op jit(solution)/shard_map/ppermute | solution.py:334
  51.9 41.8 %collective-permute-start.5 = (bf16[2,2,272,128]{3,2,1,0:T(8,128)(2,1)}, bf16[2,2,272,128]{3,2,1,0:T(8,128)(2,1)}, u32[]{:S(2)}, u32[]{:S(2)}) collective-permute-start(bf16[2,2,272,128]{3,2,1,0:T(8,128)(2,1)} %get-tuple-element.35), channel_id=1, source_target_pairs={{0,3},{1,0},{2,1},{3,2},{4,7},{5,4},{6,5},{7,6},{8,11},{9,8},{10,9... | collective-permute-start | bytes 835592 | tf_op jit(solution)/shard_map/ppermute | solution.py:334
  52.4 6.4 %copy-start = (bf16[8,8,2,16,128]{4,3,2,1,0:T(8,128)(2,1)}, bf16[8,8,2,16,128]{4,3,2,1,0:T(8,128)(2,1)S(1)}, u32[]{:S(2)}) copy-start(bf16[8,8,2,16,128]{4,3,2,1,0:T(8,128)(2,1)S(1)} %collective-permute-done.2.refs_2_.first) | copy-start | bytes 1572868
  52.4 43.6 %collective-permute-start.3 = (bf16[2,2,272,128]{3,2,1,0:T(8,128)(2,1)}, bf16[2,2,272,128]{3,2,1,0:T(8,128)(2,1)}, u32[]{:S(2)}, u32[]{:S(2)}) collective-permute-start(bf16[2,2,272,128]{3,2,1,0:T(8,128)(2,1)} %get-tuple-element.31.refs_0_), channel_id=1, source_target_pairs={{0,1},{1,2},{2,3},{3,0},{4,5},{5,6},{6,7},{7,4},{8,9},{9,10},{10,1... | collective-permute-start | bytes 835592 | tf_op jit(solution)/shard_map/ppermute | solution.py:334
  58.6 0.8 copy-start.3
  62.3 19.6 %all-to-all-start.1 = ((bf16[8,2,17,16,128]{4,3,2,1,0:T(8,128)(2,1)}), bf16[8,2,17,16,128]{4,3,2,1,0:T(8,128)(2,1)S(1)}, u32[]{:S(2)}, u32[]{:S(2)}) async-start(bf16[8,2,17,16,128]{4,3,2,1,0:T(8,128)(2,1)} %copy-done.7), calls=%async_computation.1 | async-start | bytes 2228224 | tf_op jit(solution)/shard_map/all_to_all | solution.py:299
  67.3 0.7 copy-start.15
  68.0 5.0 %copy-start.1 = (bf16[8,8,2,16,128]{4,3,2,1,0:T(8,128)(2,1)S(1)}, bf16[8,8,2,16,128]{4,3,2,1,0:T(8,128)(2,1)}, u32[]{:S(2)}) copy-start(bf16[8,8,2,16,128]{4,3,2,1,0:T(8,128)(2,1)} %copy-done) | copy-start | bytes 1572868
  68.0 5.0 %copy-start.4 = (bf16[8,8,2,16,128]{4,3,2,1,0:T(8,128)(2,1)S(1)}, bf16[8,8,2,16,128]{4,3,2,1,0:T(8,128)(2,1)}, u32[]{:S(2)}) copy-start(bf16[8,8,2,16,128]{4,3,2,1,0:T(8,128)(2,1)} %copy-done.3) | copy-start | bytes 1572868
  69.7 0.7 copy-start.14
  70.4 28.4 %collective-permute-start.7 = (bf16[2,2,272,128]{3,2,1,0:T(8,128)(2,1)}, bf16[2,2,272,128]{3,2,1,0:T(8,128)(2,1)}, u32[]{:S(2)}, u32[]{:S(2)}) collective-permute-start(bf16[2,2,272,128]{3,2,1,0:T(8,128)(2,1)} %get-tuple-element.37), channel_id=1, source_target_pairs={{0,2},{1,3},{2,0},{3,1},{4,6},{5,7},{6,4},{7,5},{8,10},{9,11},{10,... | collective-permute-start | bytes 835592 | tf_op jit(solution)/shard_map/ppermute | solution.py:334
  73.0 42.3 %collective-permute-start.6 = (bf16[2,2,272,128]{3,2,1,0:T(8,128)(2,1)}, bf16[2,2,272,128]{3,2,1,0:T(8,128)(2,1)}, u32[]{:S(2)}, u32[]{:S(2)}) collective-permute-start(bf16[2,2,272,128]{3,2,1,0:T(8,128)(2,1)} %get-tuple-element.33.refs_0_), channel_id=1, source_target_pairs={{0,1},{1,2},{2,3},{3,0},{4,5},{5,6},{6,7},{7,4},{8,9},{9,10},{10,1... | collective-permute-start | bytes 835592 | tf_op jit(solution)/shard_map/ppermute | solution.py:334
  74.1 1.0 copy-start.9
  81.9 33.3 %all-to-all-start = ((bf16[8,2,17,16,128]{4,3,2,1,0:T(8,128)(2,1)}), bf16[8,2,17,16,128]{4,3,2,1,0:T(8,128)(2,1)}, u32[]{:S(2)}, u32[]{:S(2)}) async-start(bf16[8,2,17,16,128]{4,3,2,1,0:T(8,128)(2,1)} %copy-done.6), calls=%async_computation | async-start | bytes 2228224 | tf_op jit(solution)/shard_map/all_to_all | solution.py:299
  87.6 26.9 %collective-permute-start.8 = (bf16[2,2,272,128]{3,2,1,0:T(8,128)(2,1)}, bf16[2,2,272,128]{3,2,1,0:T(8,128)(2,1)S(1)}, u32[]{:S(2)}, u32[]{:S(2)}) collective-permute-start(bf16[2,2,272,128]{3,2,1,0:T(8,128)(2,1)} %copy-done.14), channel_id=1, source_target_pairs={{0,3},{1,0},{2,1},{3,2},{4,7},{5,4},{6,5},{7,6},{8,11},{9,8},{10,9... | collective-permute-start | bytes 835592 | tf_op jit(solution)/shard_map/ppermute | solution.py:334
  93.7 42.1 %collective-permute-start.9 = (bf16[2,8,8,2,16,128]{5,4,3,2,1,0:T(8,128)(2,1)}, bf16[2,8,8,2,16,128]{5,4,3,2,1,0:T(8,128)(2,1)}, u32[]{:S(2)}, u32[]{:S(2)}) collective-permute-start(bf16[2,8,8,2,16,128]{5,4,3,2,1,0:T(8,128)(2,1)} %copy-done.9), channel_id=1, source_target_pairs={{1,0},{2,3},{5,4},{6,7},{9,8},{10,11},{13,12},{14,15},{17,16},{18,... | collective-permute-start | bytes 3145736 | tf_op jit(solution)/shard_map/ppermute | solution.py:340
  97.7 45.4 %collective-permute-start.14 = (bf16[2,2,272,128]{3,2,1,0:T(8,128)(2,1)}, bf16[2,2,272,128]{3,2,1,0:T(8,128)(2,1)}, u32[]{:S(2)}, u32[]{:S(2)}) collective-permute-start(bf16[2,2,272,128]{3,2,1,0:T(8,128)(2,1)} %get-tuple-element.42), channel_id=1, source_target_pairs={{0,2},{1,3},{2,0},{3,1},{4,6},{5,7},{6,4},{7,5},{8,10},{9,11},{10,... | collective-permute-start | bytes 835592 | tf_op jit(solution)/shard_map/ppermute | solution.py:334
  98.8 58.8 %collective-permute-start.15 = (bf16[2,2,272,128]{3,2,1,0:T(8,128)(2,1)}, bf16[2,2,272,128]{3,2,1,0:T(8,128)(2,1)}, u32[]{:S(2)}, u32[]{:S(2)}) collective-permute-start(bf16[2,2,272,128]{3,2,1,0:T(8,128)(2,1)} %get-tuple-element.43), channel_id=1, source_target_pairs={{0,3},{1,0},{2,1},{3,2},{4,7},{5,4},{6,5},{7,6},{8,11},{9,8},{10,9... | collective-permute-start | bytes 835592 | tf_op jit(solution)/shard_map/ppermute | solution.py:334
  114.5 0.8 copy-start.10
  115.3 42.3 %collective-permute-start.13 = (bf16[2,2,272,128]{3,2,1,0:T(8,128)(2,1)}, bf16[2,2,272,128]{3,2,1,0:T(8,128)(2,1)}, u32[]{:S(2)}, u32[]{:S(2)}) collective-permute-start(bf16[2,2,272,128]{3,2,1,0:T(8,128)(2,1)} %get-tuple-element.36.refs_0_), channel_id=1, source_target_pairs={{0,1},{1,2},{2,3},{3,0},{4,5},{5,6},{6,7},{7,4},{8,9},{9,10},{10,1... | collective-permute-start | bytes 835592 | tf_op jit(solution)/shard_map/ppermute | solution.py:334
  135.8 1.0 copy-start.11
  136.7 6.3 %copy-start.2 = (bf16[8,8,2,16,128]{4,3,2,1,0:T(8,128)(2,1)S(1)}, bf16[8,8,2,16,128]{4,3,2,1,0:T(8,128)(2,1)}, u32[]{:S(2)}) copy-start(bf16[8,8,2,16,128]{4,3,2,1,0:T(8,128)(2,1)} %copy-done) | copy-start | bytes 1572868
  136.7 6.3 %copy-start.5 = (bf16[8,8,2,16,128]{4,3,2,1,0:T(8,128)(2,1)S(1)}, bf16[8,8,2,16,128]{4,3,2,1,0:T(8,128)(2,1)}, u32[]{:S(2)}) copy-start(bf16[8,8,2,16,128]{4,3,2,1,0:T(8,128)(2,1)} %copy-done.3) | copy-start | bytes 1572868
  138.2 23.9 %collective-permute-start.10 = (bf16[2,2,272,128]{3,2,1,0:T(8,128)(2,1)S(1)}, bf16[2,2,272,128]{3,2,1,0:T(8,128)(2,1)S(1)}, u32[]{:S(2)}, u32[]{:S(2)}) collective-permute-start(bf16[2,2,272,128]{3,2,1,0:T(8,128)(2,1)S(1)} %get-tuple-element.39), channel_id=1, source_target_pairs={{0,1},{1,2},{2,3},{3,0},{4,5},{5,6},{6,7},{7,4},{8,9},{9,10},{10,1... | collective-permute-start | bytes 835592 | tf_op jit(solution)/shard_map/ppermute | solution.py:334
  138.2 23.8 %collective-permute-start.11 = (bf16[2,2,272,128]{3,2,1,0:T(8,128)(2,1)S(1)}, bf16[2,2,272,128]{3,2,1,0:T(8,128)(2,1)S(1)}, u32[]{:S(2)}, u32[]{:S(2)}) collective-permute-start(bf16[2,2,272,128]{3,2,1,0:T(8,128)(2,1)S(1)} %get-tuple-element.40), channel_id=1, source_target_pairs={{0,2},{1,3},{2,0},{3,1},{4,6},{5,7},{6,4},{7,5},{8,10},{9,11},{10,... | collective-permute-start | bytes 835592 | tf_op jit(solution)/shard_map/ppermute | solution.py:334
  143.1 22.2 %collective-permute-start.12 = (bf16[2,2,272,128]{3,2,1,0:T(8,128)(2,1)S(1)}, bf16[2,2,272,128]{3,2,1,0:T(8,128)(2,1)S(1)}, u32[]{:S(2)}, u32[]{:S(2)}) collective-permute-start(bf16[2,2,272,128]{3,2,1,0:T(8,128)(2,1)S(1)} %get-tuple-element.41), channel_id=1, source_target_pairs={{0,3},{1,0},{2,1},{3,2},{4,7},{5,4},{6,5},{7,6},{8,11},{9,8},{10,9... | collective-permute-start | bytes 835592 | tf_op jit(solution)/shard_map/ppermute | solution.py:334
  144.6 8.5 %copy-start.12 = (bf16[2,2,272,128]{3,2,1,0:T(8,128)(2,1)S(1)}, bf16[2,2,272,128]{3,2,1,0:T(8,128)(2,1)}, u32[]{:S(2)}) copy-start(bf16[2,2,272,128]{3,2,1,0:T(8,128)(2,1)} %copy-done.10) | copy-start | bytes 835588

commit v8 on v7

--- a/solution.py
+++ b/solution.py
@@ -17,7 +17,7 @@
 QUERY, KEY, VALUE, OUT = range(4)
 CUT_MICROS = 10
 TOKEN_MICROS = 20
-CUTS = (0, 2, 4, 6, 8)
+CUTS = (0, 1, 4, 6, 8)
 VMEM_LIMIT = 16 * 1024 * 1024
 
 
@@ -30,18 +30,22 @@
     )
 
 
-def pack(table, param_offsets, owner_map, ways, widths, granule, chunks):
+def pack(table, param_offsets, owner_map, ways, widths, granule, parts):
     layer_count, head_count = owner_map.shape
     per_group = head_count // ways
-    steps = [[widths[kind] // granule for kind in kinds] for _, kinds in chunks]
+    sizes = [width // granule for width in widths]
     outs = [
-        jax.ShapeDtypeStruct((ways, len(items), sum(step)) + table.shape[2:], table.dtype)
-        for (items, _), step in zip(chunks, steps)
+        jax.ShapeDtypeStruct(
+            (ways, sum(len(items) * sum(sizes[kind] for kind in kinds) for items, kinds in part))
+            + table.shape[2:],
+            table.dtype,
+        )
+        for part in parts
     ]
 
     def kernel(offsets, owners, source, *refs):
         targets, (taken, head_at) = refs[:-2], refs[-2:]
-        for layer in range(layer_count):
+        for layer in sorted({item // per_group for part in parts for items, _ in part for item in items}):
             for way in range(ways):
                 taken[way] = layer * per_group
 
@@ -53,18 +57,22 @@
 
             pl.loop(0, head_count, unroll=min(8, head_count))(place)
 
-        for target, (items, kinds), step in zip(targets, chunks, steps):
-            for at, item in enumerate(items):
+        for target, part in zip(targets, parts):
+            start = 0
+            for item, kinds in [(item, kinds) for items, kinds in part for item in items]:
 
                 def move(way):
                     head = head_at[item * ways + way]
-                    start = 0
-                    for kind, size in zip(kinds, step):
+                    at = start
+                    for kind in kinds:
                         begin = lax.div(offsets[item // per_group, head, kind], jnp.int32(granule))
-                        target[way, at, pl.ds(start, size)] = source[item // per_group, pl.ds(begin, size)]
-                        start += size
+                        target[way, pl.ds(at, sizes[kind])] = source[
+                            item // per_group, pl.ds(begin, sizes[kind])
+                        ]
+                        at += sizes[kind]
 
                 pl.loop(0, ways, unroll=min(8, ways))(move)
+                start += sum(sizes[kind] for kind in kinds)
 
     return pl.pallas_call(
         kernel,
@@ -97,29 +105,42 @@
     return pl.BlockSpec(corner_of(x), lambda _: (0,) * x.ndim)
 
 
-def cut(rows, slice_map, blocks, shifts, waits, micros):
-    shape = (blocks,) + rows.shape[1:]
+def cut(rows, slice_map, blocks, ahead, item_rows, waits, micros):
     t_ways = slice_map.shape[1]
+    first = math.prod(ahead)
+    items = (rows.shape[1] - first) // item_rows
+    shapes = [(rows.shape[0],) + ahead + rows.shape[2:]] if first else []
+    shapes += [(blocks, items, item_rows) + rows.shape[2:]] * t_ways
 
     def kernel(mapped, source, *refs):
         f_me, t_me = lax.axis_index("fsdp"), lax.axis_index("tp")
-        for shift, piece in zip(shifts, refs[len(waits) :]):
+        refs = refs[len(waits) :]
+        if first:
+            for f in range(rows.shape[0]):
+                for item in range(ahead[0]):
+                    for kind in range(ahead[1]):
+                        start = (item * ahead[1] + kind) * ahead[2]
+                        refs[0][f, item, kind] = source[f, start : start + ahead[2]]
+            refs = refs[1:]
+        for shift, piece in enumerate(refs):
             block = mapped[f_me, lax.rem(t_me + shift, t_ways)]
             for f in range(blocks):
-                piece[f] = source[block * blocks + f]
+                for item in range(items):
+                    start = first + item * item_rows
+                    piece[f, item] = source[block * blocks + f, start : start + item_rows]
 
     return pl.pallas_call(
         kernel,
         grid=(1,),
-        out_shape=[jax.ShapeDtypeStruct(shape, rows.dtype)] * len(shifts),
+        out_shape=[jax.ShapeDtypeStruct(shape, rows.dtype) for shape in shapes],
         in_specs=[pl.BlockSpec(memory_space=pltpu.SMEM), pl.BlockSpec(memory_space=pltpu.VMEM)]
         + [corner(x) for x in waits],
-        out_specs=[pl.BlockSpec(memory_space=pltpu.VMEM)] * len(shifts),
+        out_specs=[pl.BlockSpec(memory_space=pltpu.VMEM)] * len(shapes),
         compiler_params=pltpu.CompilerParams(vmem_limit_bytes=VMEM_LIMIT),
         cost_estimate=pl.CostEstimate(
             flops=int(micros * 1.15e9),
             transcendentals=0,
-            bytes_accessed=4 * len(shifts) * math.prod(shape),
+            bytes_accessed=4 * sum(math.prod(shape) for shape in shapes),
         ),
         name="cut",
     )(slice_map, rows, *waits)
@@ -212,9 +233,9 @@
     )(me.reshape(1), *spread_parts)
 
 
-def absorb(where, items, own, came, matrices, outs, shapes):
-    t_ways = len(came) + 1
-    blocks = came[0].shape[0]
+def absorb(me, items, parts, matrices, outs, shapes):
+    t_ways = len(parts)
+    blocks = parts[0].shape[0]
     q_rows, o_rows = shapes[0].shape[3], shapes[1].shape[3]
     rows = q_rows + o_rows
 
@@ -231,10 +252,9 @@
                     parts[d][f, 0, q_rows:], mats[0, 1], preferred_element_type=jnp.float32
                 ).astype(jnp.bfloat16)
 
-    in_specs = [pl.BlockSpec((blocks, 1, rows, LANES), lambda j, at: (at[1], j, 0, 0))]
-    in_specs += [pl.BlockSpec((blocks, 1, rows, LANES), lambda j, at: (0, j, 0, 0))] * len(came)
+    in_specs = [pl.BlockSpec((blocks, 1, rows, LANES), lambda j, at: (0, j, 0, 0))] * t_ways
     in_specs += [pl.BlockSpec((1,) + matrices.shape[1:], lambda j, at: (items[0] + j, 0, 0, 0))]
-    args = [own, *came, matrices]
+    args = [*parts, matrices]
     aliases = {}
     if outs is not None:
         in_specs += [pl.BlockSpec(memory_space=pl.ANY)] * 2
@@ -261,13 +281,13 @@
             bytes_accessed=2 * work * (LANES + KVR),
         ),
         name="absorb",
-    )(where, *args)
-
-
-def absorb_plain(me, own, came, matrices):
-    t_ways = len(came) + 1
+    )(me.reshape(1), *args)
+
+
+def absorb_plain(me, parts, matrices):
+    t_ways = len(parts)
     order = lax.rem(me - jnp.arange(t_ways, dtype=jnp.int32) + t_ways, jnp.int32(t_ways))
-    rows = jnp.take(jnp.stack([own, *came]), order, axis=0).transpose(2, 1, 0, 3, 4)
+    rows = jnp.take(jnp.stack(parts), order, axis=0).transpose(2, 1, 0, 3, 4)
     cut = rows.shape[3] * QR // (QR + D)
     return tuple(
         jnp.einsum("hrc,hck->hrk", part, mats, preferred_element_type=jnp.float32).astype(jnp.bfloat16)
@@ -288,58 +308,53 @@
     table = learner_flat.reshape(layer_count, -1, granule // LANES, LANES)
     whole_tiles = granule % (16 * LANES) == 0
     row_counts = [width // LANES for width in widths]
+    item_rows = row_counts[QUERY] + row_counts[OUT]
+    ahead = (item_count, 2, row_counts[KEY])
 
     me = lax.axis_index("tp")
     blocks = f_ways // t_ways
-    shifts = range(1, t_ways)
     cuts = [item_count * eighths // 8 for eighths in CUTS]
     chunks = [range(low, high) for low, high in zip(cuts, cuts[1:]) if low < high]
 
-    def over_fsdp(x, rows):
+    def packed(parts):
+        return pack(table, param_offsets, owner_map, f_ways, widths, granule, parts)
+
+    def over_fsdp(x):
         x = lax.all_to_all(x, "fsdp", split_axis=0, concat_axis=0, tiled=True)
-        return x.reshape(x.shape[:2] + rows)
-
-    pairs, *to_send = pack(
-        table,
-        param_offsets,
-        owner_map,
-        f_ways,
-        widths,
-        granule,
-        [(range(item_count), (KEY, VALUE))] + [(items, (QUERY, OUT)) for items in chunks],
-    )
-    pairs = over_fsdp(pairs, (2, row_counts[KEY], LANES))
-    up, down = neighbours(pairs, "tp", t_ways)
-    if t_ways == 4:
-        across = lax.ppermute(pairs, "tp", [(0, 2), (3, 1)])
-        near = token([up, down, across], TOKEN_MICROS)
-    else:
-        ups, downs = [pairs, up], [pairs, down]
-        for _ in range(2, t_ways):
-            ups.append(neighbours(ups[-1], "tp", t_ways)[0])
-            downs.append(neighbours(downs[-1], "tp", t_ways)[1])
+        return x.reshape(f_ways, -1, LANES)
+
+    first_parts = [[(range(item_count), (KEY, VALUE)), (chunks[0], (QUERY, OUT))]]
+    other_parts = [[(items, (QUERY, OUT))] for items in chunks[1:]]
+    to_send = packed(first_parts + other_parts)
 
     exchanged, sent = [], []
     for at in range(len(chunks)):
-        rows = over_fsdp(to_send[at], (row_counts[QUERY] + row_counts[OUT], LANES))
+        rows = over_fsdp(to_send[at])
         waits = sent[at - 1][:1] if at else []
         if at >= 2:
-            waits = waits + exchanged[at - 2][1]
-        if t_ways == 4 and at == 1:
-            waits = waits + [near]
-        if t_ways == 4 and at == len(chunks) - 1:
-            waits = waits + [far]
-        pieces = cut(rows, slice_map, blocks, shifts, waits, CUT_MICROS)
-        came = [
-            lax.ppermute(piece, "tp", [(i, (i + shift) % t_ways) for i in range(t_ways)])
-            for shift, piece in zip(shifts, pieces)
-        ]
-        exchanged.append((rows, came))
-        sent.append(list(pieces))
-        if t_ways == 4 and at == 1:
-            far = lax.ppermute(
-                pass_on(me, across, up, down, sent[1][:1]), "tp", [(1, 0), (2, 3)]
-            )
+            waits = waits + exchanged[at - 2][1:]
+        if at == 1:
+            waits = waits + exchanged[0][1:3]
+        if t_ways == 4 and at in (1, 2):
+            waits = waits + [near if at == 1 else far]
+        pieces = list(cut(rows, slice_map, blocks, ahead if at == 0 else (0,), item_rows, waits, CUT_MICROS))
+        if at == 0:
+            pairs = pieces.pop(0)
+            up, down = neighbours(pairs, "tp", t_ways)
+            if t_ways == 4:
+                across = lax.ppermute(pairs, "tp", [(0, 2), (3, 1)])
+                near = token([up, down, across], TOKEN_MICROS)
+                far = lax.ppermute(pass_on(me, across, up, down, []), "tp", [(1, 0), (2, 3)])
+        sent.append(pieces)
+        exchanged.append(
+            pieces[:1]
+            + [
+                lax.ppermute(piece, "tp", [(i, (i + shift) % t_ways) for i in range(t_ways)])
+                for shift, piece in enumerate(pieces)
+                if shift
+            ]
+        )
+
     if t_ways == 4:
         ends = jnp.logical_or(me == 0, me == 3)
         spread = [
@@ -349,33 +364,29 @@
             jnp.where(me == 3, far[0], down),
         ]
     else:
-        spread = [pairs] + [jnp.where(me >= d, ups[d], downs[t_ways - d]) for d in shifts]
-    slice_row = lax.dynamic_index_in_dim(slice_map, lax.axis_index("fsdp"), 0, keepdims=False)
-    near = [jnp.where(me >= d, up[d], down[t_ways - d]) for d in shifts]
+        ups, downs = [pairs, up], [pairs, down]
+        for _ in range(2, t_ways):
+            ups.append(neighbours(ups[-1], "tp", t_ways)[0])
+            downs.append(neighbours(downs[-1], "tp", t_ways)[1])
+        spread = [pairs] + [jnp.where(me >= d, ups[d], downs[t_ways - d]) for d in range(1, t_ways)]
 
     if whole_tiles:
         shapes = tuple(
             jax.ShapeDtypeStruct((item_count, blocks, t_ways, row_counts[kind], KVR), jnp.bfloat16)
             for kind in (QUERY, OUT)
         )
-        where = jnp.stack([me, slice_row[me]])
         matrices = assemble(me, spread)
         outs = None
-        for items, (rows, came) in zip(chunks, exchanged):
-            outs = absorb(where, items, rows, came, matrices, outs, shapes)
+        for items, parts in zip(chunks, exchanged):
+            outs = absorb(me, items, parts, matrices, outs, shapes)
         return tuple(out.reshape(layer_count, per_group, -1, KVR) for out in outs)
 
     order = lax.rem(me - jnp.arange(t_ways, dtype=jnp.int32) + t_ways, jnp.int32(t_ways))
     matrices = jnp.take(jnp.stack(spread), order, axis=0).transpose(2, 3, 1, 0, 4, 5)
     matrices = matrices.reshape(item_count, 2, -1, KVR)
     done = [
-        absorb_plain(
-            me,
-            lax.dynamic_slice_in_dim(rows, slice_row[me] * blocks, blocks, 0),
-            came,
-            matrices[items[0] : items[-1] + 1],
-        )
-        for items, (rows, came) in zip(chunks, exchanged)
+        absorb_plain(me, parts, matrices[items[0] : items[-1] + 1])
+        for items, parts in zip(chunks, exchanged)
     ]
     return tuple(jnp.concatenate(kind).reshape(layer_count, per_group, -1, KVR) for kind in zip(*done))
 

time: 171 us -> 164 us (0.959)
  waiting for transfers between devices: 61.6 us -> 74.7 us
  blocking collectives: 12.4 us -> 0 us
  local copies, waits for them, and re-layouts: 12.3 us -> 6.65 us
  Pallas kernels: 33.6 us -> 30.4 us
  starting transfers between devices: 46.6 us -> 48.7 us
    all_to_all x1 -> x0, blocking collectives: 12.4 us -> none  [over_fsdp(): x = lax.all_to_all(x, 'fsdp', split_axis=0, concat_axis=0, tiled=True)]
    all_to_all x4, waiting for transfers between devices: 12.9 us -> 21.3 us  [over_fsdp(): x = lax.all_to_all(x, 'fsdp', split_axis=0, concat_axis=0, tiled=True)]
    ppermute x1, waiting for transfers between devices: 4.63 us -> 10.8 us  [neighbours(): lax.ppermute(x, axis, [(i + 1, i) for i in range(ways - 1)])]
    unnamed x37 -> x39, local copies, waits for them, and re-layouts: 11.7 us -> 6.65 us
    pallas_call x4, Pallas kernels: 17.7 us -> 14.1 us  [absorb(): pl.pallas_call(kernel, grid_spec=pltpu.PrefetchScalarGridSpec(num_scalar_...]
    ppermute x1, waiting for transfers between devices: 20.5 us -> 17 us  [per_device(): lax.ppermute(pass_on(me, across, up, down, []), 'tp', [(1, 0), (2, 3)])]
    ppermute x12, starting transfers between devices: 15 us -> 18.2 us  [per_device(): lax.ppermute(piece, 'tp', [(i, (i + shift) % t_ways) for i in range(t_way...]
    ppermute x12, waiting for transfers between devices: 23.4 us -> 25.4 us  [per_device(): lax.ppermute(piece, 'tp', [(i, (i + shift) % t_ways) for i in range(t_way...]
  transfers between devices with their start and end apart: 20 -> 20, of which waited for: 10 -> 11; matrix products, arithmetic and copies ran while one was open for 2% -> 1% of each run, Pallas kernels for 15% -> 14%
where the time goes in v8:
time: 164 us; the launch traced here: 163 us
  waiting for transfers between devices  74.7 us (46%)
  starting transfers between devices  48.7 us (30%)
  Pallas kernels  30.4 us (19%)
  local copies, waits for them, and re-layouts  6.65 us (4%)
    ppermute x12, waiting for transfers between devices, per_device(): lax.ppermute(piece, 'tp', [(i, (i + shift) % t_ways) for i in range(t_way...  25.4 us
    all_to_all x4, waiting for transfers between devices, over_fsdp(): x = lax.all_to_all(x, 'fsdp', split_axis=0, concat_axis=0, tiled=True)  21.3 us
    all_to_all x4, starting transfers between devices, over_fsdp(): x = lax.all_to_all(x, 'fsdp', split_axis=0, concat_axis=0, tiled=True)  19.3 us
    ppermute x12, starting transfers between devices, per_device(): lax.ppermute(piece, 'tp', [(i, (i + shift) % t_ways) for i in range(t_way...  18.2 us
    ppermute x1, waiting for transfers between devices, per_device(): lax.ppermute(pass_on(me, across, up, down, []), 'tp', [(1, 0), (2, 3)])  17 us
    pallas_call x4, Pallas kernels, absorb(): pl.pallas_call(kernel, grid_spec=pltpu.PrefetchScalarGridSpec(num_scalar_...  14.1 us
    ppermute x1, waiting for transfers between devices, neighbours(): lax.ppermute(x, axis, [(i + 1, i) for i in range(ways - 1)])  10.8 us
    unnamed x39, local copies, waits for them, and re-layouts  6.65 us
  transfers between devices with their start and end apart: 20, of which 11 were waited for; matrix products, arithmetic and copies ran while one was open for 1% of the time, Pallas kernels for 14%

profile of v8, /device:TPU:10, one launch (start us, length us, event | category | flops | bytes accessed | tf_op | source)
XLA Modules:
  0.0 162.7 jit_solution(16280067118335241379)
XLA Ops:
  0.6 0.8 copy.12.offsets
  1.4 3.1 %copy.17 = bf16[1,2,9728,128]{3,2,1,0:T(8,128)(2,1)S(1)} copy(bf16[1,2,9728,128]{3,1,2,0:T(2,128)(2,1)} %bitcast.27) | data formatting | bytes 9961472
  4.6 0.0 copy-start.17
  4.6 4.0 %pack.1 = (bf16[8,33,16,128]{3,2,1,0:T(8,128)(2,1)}, bf16[8,51,16,128]{3,2,1,0:T(8,128)(2,1)}, bf16[8,34,16,128]{3,2,1,0:T(8,128)(2,1)S(1)}, bf16[8,34,16,128]{3,2,1,0:T(8,128)(2,1)}) custom-call(s32[2,32,4]{2,1,0:T(8,128)S(1)} %copy.12.offsets, s32[2,32]{1,0:T(2,128)S(1)} %copy-done.12, bf16[2,608,16,128]{3,2,1,0:T(8,128)(2,1)S(1)} %bitcast.20), custom_call_target="tpu_custom_call" | custom-call | bytes 9961472 | tf_op jit(solution)/shard_map/pack/pallas_call | solution.py:77
  8.5 1.0 copy-done.6
  9.5 4.3 %all-to-all-start.3 = ((bf16[8,33,16,128]{3,2,1,0:T(8,128)(2,1)}), bf16[8,33,16,128]{3,2,1,0:T(8,128)(2,1)S(1)}, u32[]{:S(2)}, u32[]{:S(2)}) async-start(bf16[8,33,16,128]{3,2,1,0:T(8,128)(2,1)} %get-tuple-element.34), calls=%async_computation.3 | async-start | bytes 2162688 | tf_op jit(solution)/shard_map/all_to_all | solution.py:323
  13.8 0.1 copy.16.mapped
  13.9 14.2 %all-to-all-done.3 = bf16[8,33,16,128]{3,2,1,0:T(8,128)(2,1)S(1)} async-done(((bf16[8,33,16,128]{3,2,1,0:T(8,128)(2,1)}), bf16[8,33,16,128]{3,2,1,0:T(8,128)(2,1)S(1)}, u32[]{:S(2)}, u32[]{:S(2)}) %all-to-all-start.3) | async-done | bytes 1081376 | tf_op jit(solution)/shard_map/all_to_all | solution.py:323
  28.1 1.5 cut.4
  29.5 1.3 collective-permute-start.4
  30.8 5.6 %collective-permute-start.3 = (bf16[8,8,2,16,128]{4,3,2,1,0:T(8,128)(2,1)}, bf16[8,8,2,16,128]{4,3,2,1,0:T(8,128)(2,1)S(1)}, u32[]{:S(2)}, u32[]{:S(2)}) collective-permute-start(bf16[8,8,2,16,128]{4,3,2,1,0:T(8,128)(2,1)} %get-tuple-element.38.refs_0_), channel_id=1, source_target_pairs={{1,0},{2,1},{3,2},{5,4},{6,5},{7,6},{9,8},{10,9},{11,10},{13,12},{... | collective-permute-start | bytes 1572872 | tf_op jit(solution)/shard_map/ppermute | solution.py:168
  36.4 1.9 %collective-permute-start.2 = (bf16[8,8,2,16,128]{4,3,2,1,0:T(8,128)(2,1)}, bf16[8,8,2,16,128]{4,3,2,1,0:T(8,128)(2,1)S(1)}, u32[]{:S(2)}, u32[]{:S(2)}) collective-permute-start(bf16[8,8,2,16,128]{4,3,2,1,0:T(8,128)(2,1)} %get-tuple-element.38.refs_0_), channel_id=1, source_target_pairs={{0,1},{1,2},{2,3},{4,5},{5,6},{6,7},{8,9},{9,10},{10,11},{12,13},{... | collective-permute-start | bytes 1572872 | tf_op jit(solution)/shard_map/ppermute | solution.py:167
  38.4 5.0 %all-to-all-start.2 = ((bf16[8,51,16,128]{3,2,1,0:T(8,128)(2,1)}), bf16[8,51,16,128]{3,2,1,0:T(8,128)(2,1)S(1)}, u32[]{:S(2)}, u32[]{:S(2)}) async-start(bf16[8,51,16,128]{3,2,1,0:T(8,128)(2,1)} %get-tuple-element.33), calls=%async_computation.2 | async-start | bytes 3342336 | tf_op jit(solution)/shard_map/all_to_all | solution.py:323
  43.4 0.0 collective-permute-start
  43.4 4.4 %collective-permute-start.1 = (bf16[2,1,272,128]{3,2,1,0:T(8,128)(2,1)}, bf16[2,1,272,128]{3,2,1,0:T(8,128)(2,1)}, u32[]{:S(2)}, u32[]{:S(2)}) collective-permute-start(bf16[2,1,272,128]{3,2,1,0:T(8,128)(2,1)} %copy-done.14), channel_id=1, source_target_pairs={{0,2},{1,3},{2,0},{3,1},{4,6},{5,7},{6,4},{7,5},{8,10},{9,11},{10,... | collective-permute-start | bytes 417800 | tf_op jit(solution)/shard_map/ppermute | solution.py:352
  47.8 0.0 collective-permute-done.4.refs_2_.first
  47.8 0.0 collective-permute-start.5
  47.8 10.8 %collective-permute-done.3.refs_1_.below = bf16[8,8,2,16,128]{4,3,2,1,0:T(8,128)(2,1)S(1)} collective-permute-done((bf16[8,8,2,16,128]{4,3,2,1,0:T(8,128)(2,1)}, bf16[8,8,2,16,128]{4,3,2,1,0:T(8,128)(2,1)S(1)}, u32[]{:S(2)}, u32[]{:S(2)}) %collective-permute-start.3) | collective-permute-done | bytes 524320 | tf_op jit(solution)/shard_map/ppermute | solution.py:168
  58.6 0.1 collective-permute-done.2.refs_0_.above
  58.7 1.1 pass_on.1
  59.9 2.5 %collective-permute-start.6 = (bf16[2,8,8,2,16,128]{5,4,3,2,1,0:T(8,128)(2,1)}, bf16[2,8,8,2,16,128]{5,4,3,2,1,0:T(8,128)(2,1)}, u32[]{:S(2)}, u32[]{:S(2)}) collective-permute-start(bf16[2,8,8,2,16,128]{5,4,3,2,1,0:T(8,128)(2,1)} %pass_on.1), channel_id=1, source_target_pairs={{1,0},{2,3},{5,4},{6,7},{9,8},{10,11},{13,12},{14,15},{17,16},{18,... | collective-permute-start | bytes 3145736 | tf_op jit(solution)/shard_map/ppermute | solution.py:347
  62.3 1.3 token_.1.refs_3_
  63.6 0.4 all-to-all-done.2
  64.0 5.0 %all-to-all-start.1 = ((bf16[8,34,16,128]{3,2,1,0:T(8,128)(2,1)}), bf16[8,34,16,128]{3,2,1,0:T(8,128)(2,1)S(1)}, u32[]{:S(2)}, u32[]{:S(2)}) async-start(bf16[8,34,16,128]{3,2,1,0:T(8,128)(2,1)} %copy-done.6), calls=%async_computation.1 | async-start | bytes 2228224 | tf_op jit(solution)/shard_map/all_to_all | solution.py:323
  69.0 0.0 collective-permute-done.refs_1_
  69.0 0.0 collective-permute-done.1.refs_2_
  69.0 0.7 copy-done.16
  69.7 1.8 %cut.5 = (bf16[2,3,272,128]{3,2,1,0:T(8,128)(2,1)S(1)}, bf16[2,3,272,128]{3,2,1,0:T(8,128)(2,1)}, bf16[2,3,272,128]{3,2,1,0:T(8,128)(2,1)}, bf16[2,3,272,128]{3,2,1,0:T(8,128)(2,1)}) custom-call(s32[8,4]{1,0:T(8,128)S(1)} %copy.16.mapped, bf16[8,816,128]{2,1,0:T(8,128)(2,1)S(1)} %bitcast.21, bf16[2,1,272,128]{3,2,1,0:T(8,128)(2,1)S(1)} %get-tuple-element.35.refs_0_, ...), custom_call_target="tpu_custom_call" | custom-call | flops 11500000256 | bytes 3342336 | tf_op jit(solution)/shard_map/cut/pallas_call | solution.py:132
  71.5 0.2 collective-permute-start.7
  71.7 4.3 %collective-permute-start.8 = (bf16[2,3,272,128]{3,2,1,0:T(8,128)(2,1)}, bf16[2,3,272,128]{3,2,1,0:T(8,128)(2,1)}, u32[]{:S(2)}, u32[]{:S(2)}) collective-permute-start(bf16[2,3,272,128]{3,2,1,0:T(8,128)(2,1)} %get-tuple-element.43), channel_id=1, source_target_pairs={{0,2},{1,3},{2,0},{3,1},{4,6},{5,7},{6,4},{7,5},{8,10},{9,11},{10,... | collective-permute-start | bytes 1253384 | tf_op jit(solution)/shard_map/ppermute | solution.py:352
  75.9 0.9 collective-permute-start.9
  76.8 6.8 %all-to-all-done.1 = bf16[8,34,16,128]{3,2,1,0:T(8,128)(2,1)S(1)} async-done(((bf16[8,34,16,128]{3,2,1,0:T(8,128)(2,1)}), bf16[8,34,16,128]{3,2,1,0:T(8,128)(2,1)S(1)}, u32[]{:S(2)}, u32[]{:S(2)}) %all-to-all-start.1) | async-done | bytes 1114144 | tf_op jit(solution)/shard_map/all_to_all | solution.py:323
  83.6 5.0 %all-to-all-start = ((bf16[8,34,16,128]{3,2,1,0:T(8,128)(2,1)}), bf16[8,34,16,128]{3,2,1,0:T(8,128)(2,1)S(1)}, u32[]{:S(2)}, u32[]{:S(2)}) async-start(bf16[8,34,16,128]{3,2,1,0:T(8,128)(2,1)} %get-tuple-element.31), calls=%async_computation | async-start | bytes 2228224 | tf_op jit(solution)/shard_map/all_to_all | solution.py:323
  88.6 0.0 collective-permute-done.5.refs_3_
  88.6 17.0 %collective-permute-done.6.refs_4_ = bf16[2,8,8,2,16,128]{5,4,3,2,1,0:T(8,128)(2,1)} collective-permute-done((bf16[2,8,8,2,16,128]{5,4,3,2,1,0:T(8,128)(2,1)}, bf16[2,8,8,2,16,128]{5,4,3,2,1,0:T(8,128)(2,1)}, u32[]{:S(2)}, u32[]{:S(2)}) %collective-permute-start.6) | collective-permute-done | bytes 1048608 | tf_op jit(solution)/shard_map/ppermute | solution.py:347
  105.6 0.9 copy-done.10
  106.5 1.7 %cut.6 = (bf16[2,2,272,128]{3,2,1,0:T(8,128)(2,1)S(1)}, bf16[2,2,272,128]{3,2,1,0:T(8,128)(2,1)}, bf16[2,2,272,128]{3,2,1,0:T(8,128)(2,1)}, bf16[2,2,272,128]{3,2,1,0:T(8,128)(2,1)}) custom-call(s32[8,4]{1,0:T(8,128)S(1)} %copy.16.mapped, bf16[8,544,128]{2,1,0:T(8,128)(2,1)S(1)} %bitcast.22, bf16[2,3,272,128]{3,2,1,0:T(8,128)(2,1)S(1)} %get-tuple-element.39.refs_0_, ...), custom_call_target="tpu_custom_call" | custom-call | flops 11500000256 | bytes 2228224 | tf_op jit(solution)/shard_map/cut/pallas_call | solution.py:132
  108.2 0.0 collective-permute-start.13
  108.2 4.8 %collective-permute-start.14 = (bf16[2,2,272,128]{3,2,1,0:T(8,128)(2,1)}, bf16[2,2,272,128]{3,2,1,0:T(8,128)(2,1)S(1)}, u32[]{:S(2)}, u32[]{:S(2)}) collective-permute-start(bf16[2,2,272,128]{3,2,1,0:T(8,128)(2,1)} %get-tuple-element.50), channel_id=1, source_target_pairs={{0,2},{1,3},{2,0},{3,1},{4,6},{5,7},{6,4},{7,5},{8,10},{9,11},{10,... | collective-permute-start | bytes 835592 | tf_op jit(solution)/shard_map/ppermute | solution.py:352
  113.1 0.0 collective-permute-done.7.refs_1_
  113.1 0.0 collective-permute-start.15
  113.1 0.0 all-to-all-done
  113.1 0.0 collective-permute-done.8.refs_2_
  113.1 9.2 %collective-permute-done.9.refs_3_ = bf16[2,3,272,128]{3,2,1,0:T(8,128)(2,1)} collective-permute-done((bf16[2,3,272,128]{3,2,1,0:T(8,128)(2,1)}, bf16[2,3,272,128]{3,2,1,0:T(8,128)(2,1)}, u32[]{:S(2)}, u32[]{:S(2)}) %collective-permute-start.9) | collective-permute-done | bytes 417824 | tf_op jit(solution)/shard_map/ppermute | solution.py:352
  122.3 0.9 cut.7
  123.2 0.1 collective-permute-start.10
  123.3 3.6 %collective-permute-start.11 = (bf16[2,2,272,128]{3,2,1,0:T(8,128)(2,1)S(1)}, bf16[2,2,272,128]{3,2,1,0:T(8,128)(2,1)S(1)}, u32[]{:S(2)}, u32[]{:S(2)}) collective-permute-start(bf16[2,2,272,128]{3,2,1,0:T(8,128)(2,1)S(1)} %get-tuple-element.47), channel_id=1, source_target_pairs={{0,2},{1,3},{2,0},{3,1},{4,6},{5,7},{6,4},{7,5},{8,10},{9,11},{10,... | collective-permute-start | bytes 835592 | tf_op jit(solution)/shard_map/ppermute | solution.py:352
  126.9 0.0 collective-permute-done.13.refs_1_
  126.9 0.0 collective-permute-start.12
  126.9 1.4 broadcast_select_fusion
  128.3 0.0 copy-start.8
  128.3 0.0 copy-start.11
  128.3 4.1 %assemble.1.refs_4_ = bf16[8,2,128,512]{3,2,1,0:T(8,128)(2,1)S(1)} custom-call(s32[1]{0:T(128)} %bitcast.me_ref.at, bf16[8,8,2,16,128]{4,3,2,1,0:T(8,128)(2,1)} %get-tuple-element.38.refs_0_, bf16[8,8,2,16,128]{4,3,2,1,0:T(8,128)(2,1)S(1)} %get-tuple-element.62.refs_1_, bf16[8,8,2,16,128]{4,3,2,1,0:T(8,128)(2,1)S(1)} %get-tuple-element.61.refs_2_, ...), custom_call_target="tpu_custom_call" | custom-call | tf_op jit(solution)/shard_map/assemble/pallas_call | solution.py:221
  132.4 0.0 copy-done.8
  132.4 0.0 copy-done.11
  132.4 3.0 %absorb.4 = (bf16[8,2,4,48,512]{4,3,2,1,0:T(8,128)(2,1)}, bf16[8,2,4,224,512]{4,3,2,1,0:T(8,128)(2,1)}) custom-call(s32[1]{0:T(128)} %bitcast.me_ref.at, bf16[2,1,272,128]{3,2,1,0:T(8,128)(2,1)S(1)} %copy-done.8, bf16[2,1,272,128]{3,2,1,0:T(8,128)(2,1)S(1)} %copy-done.11, bf16[2,1,272,128]{3,2,1,0:T(8,128)(2,1)} %collective-permute-done.1.refs_2_, ...), custom_call_target="tpu_custom_call" | custom-call | flops 285212672 | bytes 2785280 | tf_op jit(solution)/shard_map/absorb/pallas_call | solution.py:264
  135.4 5.2 %absorb.5 = (bf16[8,2,4,48,512]{4,3,2,1,0:T(8,128)(2,1)}, bf16[8,2,4,224,512]{4,3,2,1,0:T(8,128)(2,1)}) custom-call(s32[1]{0:T(128)} %bitcast.me_ref.at, bf16[2,3,272,128]{3,2,1,0:T(8,128)(2,1)S(1)} %get-tuple-element.39.refs_0_, bf16[2,3,272,128]{3,2,1,0:T(8,128)(2,1)S(1)} %collective-permute-done.7.refs_1_, ...), custom_call_target="tpu_custom_call", output_to_operand_aliasing={{0}: (6, {}), {1}: (7, {})} | custom-call | flops 855638016 | bytes 8355840 | tf_op jit(solution)/shard_map/absorb/pallas_call | solution.py:264
  140.6 0.0 collective-permute-done.14.refs_2_
  140.6 7.8 %collective-permute-done.15.refs_3_ = bf16[2,2,272,128]{3,2,1,0:T(8,128)(2,1)S(1)} collective-permute-done((bf16[2,2,272,128]{3,2,1,0:T(8,128)(2,1)}, bf16[2,2,272,128]{3,2,1,0:T(8,128)(2,1)S(1)}, u32[]{:S(2)}, u32[]{:S(2)}) %collective-permute-start.15) | collective-permute-done | bytes 278560 | tf_op jit(solution)/shard_map/ppermute | solution.py:352
  148.4 3.0 %absorb.6 = (bf16[8,2,4,48,512]{4,3,2,1,0:T(8,128)(2,1)}, bf16[8,2,4,224,512]{4,3,2,1,0:T(8,128)(2,1)}) custom-call(s32[1]{0:T(128)} %bitcast.me_ref.at, bf16[2,2,272,128]{3,2,1,0:T(8,128)(2,1)S(1)} %get-tuple-element.41.refs_0_, bf16[2,2,272,128]{3,2,1,0:T(8,128)(2,1)S(1)} %collective-permute-done.13.refs_1_, ...), custom_call_target="tpu_custom_call", output_to_operand_aliasing={{0}: (6, {}), {1}: (7, {})} | custom-call | flops 570425344 | bytes 5570560 | tf_op jit(solution)/shard_map/absorb/pallas_call | solution.py:264
  151.4 0.1 collective-permute-done.10.refs_1_
  151.4 4.5 %collective-permute-done.11.refs_2_ = bf16[2,2,272,128]{3,2,1,0:T(8,128)(2,1)S(1)} collective-permute-done((bf16[2,2,272,128]{3,2,1,0:T(8,128)(2,1)S(1)}, bf16[2,2,272,128]{3,2,1,0:T(8,128)(2,1)S(1)}, u32[]{:S(2)}, u32[]{:S(2)}) %collective-permute-start.11) | collective-permute-done | bytes 278560 | tf_op jit(solution)/shard_map/ppermute | solution.py:352
  156.0 3.8 %collective-permute-done.12.refs_3_ = bf16[2,2,272,128]{3,2,1,0:T(8,128)(2,1)S(1)} collective-permute-done((bf16[2,2,272,128]{3,2,1,0:T(8,128)(2,1)S(1)}, bf16[2,2,272,128]{3,2,1,0:T(8,128)(2,1)S(1)}, u32[]{:S(2)}, u32[]{:S(2)}) %collective-permute-start.12) | collective-permute-done | bytes 278560 | tf_op jit(solution)/shard_map/ppermute | solution.py:352
  159.8 3.0 %absorb.7 = (bf16[8,2,4,48,512]{4,3,2,1,0:T(8,128)(2,1)}, bf16[8,2,4,224,512]{4,3,2,1,0:T(8,128)(2,1)}) custom-call(s32[1]{0:T(128)} %bitcast.me_ref.at, bf16[2,2,272,128]{3,2,1,0:T(8,128)(2,1)S(1)} %get-tuple-element.45.refs_0_, bf16[2,2,272,128]{3,2,1,0:T(8,128)(2,1)S(1)} %collective-permute-done.10.refs_1_, ...), custom_call_target="tpu_custom_call", output_to_operand_aliasing={{0}: (6, {}), {1}: (7, {})} | custom-call | flops 570425344 | bytes 5570560 | tf_op jit(solution)/shard_map/absorb/pallas_call | solution.py:264
  (28 shorter events, 0.1 us)
Async XLA Ops:
  1.4 3.1 %copy-start.12 = (s32[2,32]{1,0:T(2,128)S(1)}, s32[2,32]{1,0:T(2,128)}, u32[]{:S(2)}) copy-start(s32[2,32]{1,0:T(2,128)} %owners.1) | copy-start | bytes 772
  4.6 9.3 %copy-start.17 = (s32[8,4]{0,1:T(4,128)S(1)}, s32[8,4]{0,1:T(4,128)}, u32[]{:S(2)}) copy-start(s32[8,4]{0,1:T(4,128)} %param.7) | copy-start | bytes 388
  8.5 1.0 copy-start.6
  9.5 18.5 %all-to-all-start.3 = ((bf16[8,33,16,128]{3,2,1,0:T(8,128)(2,1)}), bf16[8,33,16,128]{3,2,1,0:T(8,128)(2,1)S(1)}, u32[]{:S(2)}, u32[]{:S(2)}) async-start(bf16[8,33,16,128]{3,2,1,0:T(8,128)(2,1)} %get-tuple-element.34), calls=%async_computation.3 | async-start | bytes 2162688 | tf_op jit(solution)/shard_map/all_to_all | solution.py:323
  29.5 1.3 copy-start.13
  29.5 6.9 %copy-start.15 = (bf16[2,1,272,128]{3,2,1,0:T(8,128)(2,1)}, bf16[2,1,272,128]{3,2,1,0:T(8,128)(2,1)S(1)}, u32[]{:S(2)}) copy-start(bf16[2,1,272,128]{3,2,1,0:T(8,128)(2,1)S(1)} %get-tuple-element.36) | copy-start | bytes 417796
  29.5 13.9 %copy-start.14 = (bf16[2,1,272,128]{3,2,1,0:T(8,128)(2,1)}, bf16[2,1,272,128]{3,2,1,0:T(8,128)(2,1)S(1)}, u32[]{:S(2)}) copy-start(bf16[2,1,272,128]{3,2,1,0:T(8,128)(2,1)S(1)} %get-tuple-element.37) | copy-start | bytes 417796
  29.5 39.5 %copy-start.7 = (bf16[2,1,272,128]{3,2,1,0:T(8,128)(2,1)}, bf16[2,1,272,128]{3,2,1,0:T(8,128)(2,1)S(1)}, u32[]{:S(2)}) copy-start(bf16[2,1,272,128]{3,2,1,0:T(8,128)(2,1)S(1)} %get-tuple-element.35.refs_0_) | copy-start | bytes 417796
  29.5 18.3 %collective-permute-start.4 = (bf16[8,8,2,16,128]{4,3,2,1,0:T(8,128)(2,1)}, bf16[8,8,2,16,128]{4,3,2,1,0:T(8,128)(2,1)S(1)}, u32[]{:S(2)}, u32[]{:S(2)}) collective-permute-start(bf16[8,8,2,16,128]{4,3,2,1,0:T(8,128)(2,1)} %get-tuple-element.38.refs_0_), channel_id=1, source_target_pairs={{0,2},{3,1},{4,6},{7,5},{8,10},{11,9},{12,14},{15,13},{16,18},{19,... | collective-permute-start | bytes 1572872 | tf_op jit(solution)/shard_map/ppermute | solution.py:345
  30.8 27.8 %collective-permute-start.3 = (bf16[8,8,2,16,128]{4,3,2,1,0:T(8,128)(2,1)}, bf16[8,8,2,16,128]{4,3,2,1,0:T(8,128)(2,1)S(1)}, u32[]{:S(2)}, u32[]{:S(2)}) collective-permute-start(bf16[8,8,2,16,128]{4,3,2,1,0:T(8,128)(2,1)} %get-tuple-element.38.refs_0_), channel_id=1, source_target_pairs={{1,0},{2,1},{3,2},{5,4},{6,5},{7,6},{9,8},{10,9},{11,10},{13,12},{... | collective-permute-start | bytes 1572872 | tf_op jit(solution)/shard_map/ppermute | solution.py:168
  36.4 22.3 %collective-permute-start.2 = (bf16[8,8,2,16,128]{4,3,2,1,0:T(8,128)(2,1)}, bf16[8,8,2,16,128]{4,3,2,1,0:T(8,128)(2,1)S(1)}, u32[]{:S(2)}, u32[]{:S(2)}) collective-permute-start(bf16[8,8,2,16,128]{4,3,2,1,0:T(8,128)(2,1)} %get-tuple-element.38.refs_0_), channel_id=1, source_target_pairs={{0,1},{1,2},{2,3},{4,5},{5,6},{6,7},{8,9},{9,10},{10,11},{12,13},{... | collective-permute-start | bytes 1572872 | tf_op jit(solution)/shard_map/ppermute | solution.py:167
  38.4 25.6 %all-to-all-start.2 = ((bf16[8,51,16,128]{3,2,1,0:T(8,128)(2,1)}), bf16[8,51,16,128]{3,2,1,0:T(8,128)(2,1)S(1)}, u32[]{:S(2)}, u32[]{:S(2)}) async-start(bf16[8,51,16,128]{3,2,1,0:T(8,128)(2,1)} %get-tuple-element.33), calls=%async_computation.2 | async-start | bytes 3342336 | tf_op jit(solution)/shard_map/all_to_all | solution.py:323
  43.4 25.6 %collective-permute-start = (bf16[2,1,272,128]{3,2,1,0:T(8,128)(2,1)}, bf16[2,1,272,128]{3,2,1,0:T(8,128)(2,1)S(1)}, u32[]{:S(2)}, u32[]{:S(2)}) collective-permute-start(bf16[2,1,272,128]{3,2,1,0:T(8,128)(2,1)} %copy-done.15), channel_id=1, source_target_pairs={{0,1},{1,2},{2,3},{3,0},{4,5},{5,6},{6,7},{7,4},{8,9},{9,10},{10,1... | collective-permute-start | bytes 417800 | tf_op jit(solution)/shard_map/ppermute | solution.py:352
  43.4 25.6 %collective-permute-start.1 = (bf16[2,1,272,128]{3,2,1,0:T(8,128)(2,1)}, bf16[2,1,272,128]{3,2,1,0:T(8,128)(2,1)}, u32[]{:S(2)}, u32[]{:S(2)}) collective-permute-start(bf16[2,1,272,128]{3,2,1,0:T(8,128)(2,1)} %copy-done.14), channel_id=1, source_target_pairs={{0,2},{1,3},{2,0},{3,1},{4,6},{5,7},{6,4},{7,5},{8,10},{9,11},{10,... | collective-permute-start | bytes 417800 | tf_op jit(solution)/shard_map/ppermute | solution.py:352
  47.8 14.5 %copy-start = (bf16[8,8,2,16,128]{4,3,2,1,0:T(8,128)(2,1)}, bf16[8,8,2,16,128]{4,3,2,1,0:T(8,128)(2,1)S(1)}, u32[]{:S(2)}) copy-start(bf16[8,8,2,16,128]{4,3,2,1,0:T(8,128)(2,1)S(1)} %collective-permute-done.4.refs_2_.first) | copy-start | bytes 1572868
  47.8 40.8 %collective-permute-start.5 = (bf16[2,1,272,128]{3,2,1,0:T(8,128)(2,1)}, bf16[2,1,272,128]{3,2,1,0:T(8,128)(2,1)}, u32[]{:S(2)}, u32[]{:S(2)}) collective-permute-start(bf16[2,1,272,128]{3,2,1,0:T(8,128)(2,1)} %copy-done.13), channel_id=1, source_target_pairs={{0,3},{1,0},{2,1},{3,2},{4,7},{5,4},{6,5},{7,6},{8,11},{9,8},{10,9... | collective-permute-start | bytes 417800 | tf_op jit(solution)/shard_map/ppermute | solution.py:352
  58.6 3.7 %copy-start.2 = (bf16[8,8,2,16,128]{4,3,2,1,0:T(8,128)(2,1)}, bf16[8,8,2,16,128]{4,3,2,1,0:T(8,128)(2,1)S(1)}, u32[]{:S(2)}) copy-start(bf16[8,8,2,16,128]{4,3,2,1,0:T(8,128)(2,1)S(1)} %collective-permute-done.3.refs_1_.below) | copy-start | bytes 1572868
  58.7 3.6 %copy-start.4 = (bf16[8,8,2,16,128]{4,3,2,1,0:T(8,128)(2,1)}, bf16[8,8,2,16,128]{4,3,2,1,0:T(8,128)(2,1)S(1)}, u32[]{:S(2)}) copy-start(bf16[8,8,2,16,128]{4,3,2,1,0:T(8,128)(2,1)S(1)} %collective-permute-done.2.refs_0_.above) | copy-start | bytes 1572868
  59.9 45.8 %collective-permute-start.6 = (bf16[2,8,8,2,16,128]{5,4,3,2,1,0:T(8,128)(2,1)}, bf16[2,8,8,2,16,128]{5,4,3,2,1,0:T(8,128)(2,1)}, u32[]{:S(2)}, u32[]{:S(2)}) collective-permute-start(bf16[2,8,8,2,16,128]{5,4,3,2,1,0:T(8,128)(2,1)} %pass_on.1), channel_id=1, source_target_pairs={{1,0},{2,3},{5,4},{6,7},{9,8},{10,11},{13,12},{14,15},{17,16},{18,... | collective-permute-start | bytes 3145736 | tf_op jit(solution)/shard_map/ppermute | solution.py:347
  64.0 19.6 %all-to-all-start.1 = ((bf16[8,34,16,128]{3,2,1,0:T(8,128)(2,1)}), bf16[8,34,16,128]{3,2,1,0:T(8,128)(2,1)S(1)}, u32[]{:S(2)}, u32[]{:S(2)}) async-start(bf16[8,34,16,128]{3,2,1,0:T(8,128)(2,1)} %copy-done.6), calls=%async_computation.1 | async-start | bytes 2228224 | tf_op jit(solution)/shard_map/all_to_all | solution.py:323
  69.0 2.5 %copy-start.9 = (bf16[2,1,272,128]{3,2,1,0:T(8,128)(2,1)}, bf16[2,1,272,128]{3,2,1,0:T(8,128)(2,1)S(1)}, u32[]{:S(2)}) copy-start(bf16[2,1,272,128]{3,2,1,0:T(8,128)(2,1)S(1)} %collective-permute-done.refs_1_) | copy-start | bytes 417796
  69.0 0.7 copy-start.16
  71.5 41.5 %collective-permute-start.7 = (bf16[2,3,272,128]{3,2,1,0:T(8,128)(2,1)}, bf16[2,3,272,128]{3,2,1,0:T(8,128)(2,1)S(1)}, u32[]{:S(2)}, u32[]{:S(2)}) collective-permute-start(bf16[2,3,272,128]{3,2,1,0:T(8,128)(2,1)} %get-tuple-element.42), channel_id=1, source_target_pairs={{0,1},{1,2},{2,3},{3,0},{4,5},{5,6},{6,7},{7,4},{8,9},{9,10},{10,1... | collective-permute-start | bytes 1253384 | tf_op jit(solution)/shard_map/ppermute | solution.py:352
  71.7 41.4 %collective-permute-start.8 = (bf16[2,3,272,128]{3,2,1,0:T(8,128)(2,1)}, bf16[2,3,272,128]{3,2,1,0:T(8,128)(2,1)}, u32[]{:S(2)}, u32[]{:S(2)}) collective-permute-start(bf16[2,3,272,128]{3,2,1,0:T(8,128)(2,1)} %get-tuple-element.43), channel_id=1, source_target_pairs={{0,2},{1,3},{2,0},{3,1},{4,6},{5,7},{6,4},{7,5},{8,10},{9,11},{10,... | collective-permute-start | bytes 1253384 | tf_op jit(solution)/shard_map/ppermute | solution.py:352
  75.9 46.4 %collective-permute-start.9 = (bf16[2,3,272,128]{3,2,1,0:T(8,128)(2,1)}, bf16[2,3,272,128]{3,2,1,0:T(8,128)(2,1)}, u32[]{:S(2)}, u32[]{:S(2)}) collective-permute-start(bf16[2,3,272,128]{3,2,1,0:T(8,128)(2,1)} %get-tuple-element.44), channel_id=1, source_target_pairs={{0,3},{1,0},{2,1},{3,2},{4,7},{5,4},{6,5},{7,6},{8,11},{9,8},{10,9... | collective-permute-start | bytes 1253384 | tf_op jit(solution)/shard_map/ppermute | solution.py:352
  83.6 29.5 %all-to-all-start = ((bf16[8,34,16,128]{3,2,1,0:T(8,128)(2,1)}), bf16[8,34,16,128]{3,2,1,0:T(8,128)(2,1)S(1)}, u32[]{:S(2)}, u32[]{:S(2)}) async-start(bf16[8,34,16,128]{3,2,1,0:T(8,128)(2,1)} %get-tuple-element.31), calls=%async_computation | async-start | bytes 2228224 | tf_op jit(solution)/shard_map/all_to_all | solution.py:323
  105.6 0.9 copy-start.10
  108.2 18.7 %collective-permute-start.13 = (bf16[2,2,272,128]{3,2,1,0:T(8,128)(2,1)}, bf16[2,2,272,128]{3,2,1,0:T(8,128)(2,1)S(1)}, u32[]{:S(2)}, u32[]{:S(2)}) collective-permute-start(bf16[2,2,272,128]{3,2,1,0:T(8,128)(2,1)} %get-tuple-element.49), channel_id=1, source_target_pairs={{0,1},{1,2},{2,3},{3,0},{4,5},{5,6},{6,7},{7,4},{8,9},{9,10},{10,1... | collective-permute-start | bytes 835592 | tf_op jit(solution)/shard_map/ppermute | solution.py:352
  108.2 32.4 %collective-permute-start.14 = (bf16[2,2,272,128]{3,2,1,0:T(8,128)(2,1)}, bf16[2,2,272,128]{3,2,1,0:T(8,128)(2,1)S(1)}, u32[]{:S(2)}, u32[]{:S(2)}) collective-permute-start(bf16[2,2,272,128]{3,2,1,0:T(8,128)(2,1)} %get-tuple-element.50), channel_id=1, source_target_pairs={{0,2},{1,3},{2,0},{3,1},{4,6},{5,7},{6,4},{7,5},{8,10},{9,11},{10,... | collective-permute-start | bytes 835592 | tf_op jit(solution)/shard_map/ppermute | solution.py:352
  113.1 35.4 %collective-permute-start.15 = (bf16[2,2,272,128]{3,2,1,0:T(8,128)(2,1)}, bf16[2,2,272,128]{3,2,1,0:T(8,128)(2,1)S(1)}, u32[]{:S(2)}, u32[]{:S(2)}) collective-permute-start(bf16[2,2,272,128]{3,2,1,0:T(8,128)(2,1)} %get-tuple-element.51), channel_id=1, source_target_pairs={{0,3},{1,0},{2,1},{3,2},{4,7},{5,4},{6,5},{7,6},{8,11},{9,8},{10,9... | collective-permute-start | bytes 835592 | tf_op jit(solution)/shard_map/ppermute | solution.py:352
  122.3 4.6 %copy-start.1 = (bf16[8,8,2,16,128]{4,3,2,1,0:T(8,128)(2,1)S(1)}, bf16[8,8,2,16,128]{4,3,2,1,0:T(8,128)(2,1)}, u32[]{:S(2)}) copy-start(bf16[8,8,2,16,128]{4,3,2,1,0:T(8,128)(2,1)} %copy-done) | copy-start | bytes 1572868
  122.3 4.6 %copy-start.3 = (bf16[8,8,2,16,128]{4,3,2,1,0:T(8,128)(2,1)S(1)}, bf16[8,8,2,16,128]{4,3,2,1,0:T(8,128)(2,1)}, u32[]{:S(2)}) copy-start(bf16[8,8,2,16,128]{4,3,2,1,0:T(8,128)(2,1)} %copy-done.2) | copy-start | bytes 1572868
  122.3 4.6 %copy-start.5 = (bf16[8,8,2,16,128]{4,3,2,1,0:T(8,128)(2,1)S(1)}, bf16[8,8,2,16,128]{4,3,2,1,0:T(8,128)(2,1)}, u32[]{:S(2)}) copy-start(bf16[8,8,2,16,128]{4,3,2,1,0:T(8,128)(2,1)} %copy-done.4) | copy-start | bytes 1572868
  123.2 28.2 %collective-permute-start.10 = (bf16[2,2,272,128]{3,2,1,0:T(8,128)(2,1)S(1)}, bf16[2,2,272,128]{3,2,1,0:T(8,128)(2,1)S(1)}, u32[]{:S(2)}, u32[]{:S(2)}) collective-permute-start(bf16[2,2,272,128]{3,2,1,0:T(8,128)(2,1)S(1)} %get-tuple-element.46), channel_id=1, source_target_pairs={{0,1},{1,2},{2,3},{3,0},{4,5},{5,6},{6,7},{7,4},{8,9},{9,10},{10,1... | collective-permute-start | bytes 835592 | tf_op jit(solution)/shard_map/ppermute | solution.py:352
  123.3 32.7 %collective-permute-start.11 = (bf16[2,2,272,128]{3,2,1,0:T(8,128)(2,1)S(1)}, bf16[2,2,272,128]{3,2,1,0:T(8,128)(2,1)S(1)}, u32[]{:S(2)}, u32[]{:S(2)}) collective-permute-start(bf16[2,2,272,128]{3,2,1,0:T(8,128)(2,1)S(1)} %get-tuple-element.47), channel_id=1, source_target_pairs={{0,2},{1,3},{2,0},{3,1},{4,6},{5,7},{6,4},{7,5},{8,10},{9,11},{10,... | collective-permute-start | bytes 835592 | tf_op jit(solution)/shard_map/ppermute | solution.py:352
  126.9 32.9 %collective-permute-start.12 = (bf16[2,2,272,128]{3,2,1,0:T(8,128)(2,1)S(1)}, bf16[2,2,272,128]{3,2,1,0:T(8,128)(2,1)S(1)}, u32[]{:S(2)}, u32[]{:S(2)}) collective-permute-start(bf16[2,2,272,128]{3,2,1,0:T(8,128)(2,1)S(1)} %get-tuple-element.48), channel_id=1, source_target_pairs={{0,3},{1,0},{2,1},{3,2},{4,7},{5,4},{6,5},{7,6},{8,11},{9,8},{10,9... | collective-permute-start | bytes 835592 | tf_op jit(solution)/shard_map/ppermute | solution.py:352
  128.3 4.1 %copy-start.8 = (bf16[2,1,272,128]{3,2,1,0:T(8,128)(2,1)S(1)}, bf16[2,1,272,128]{3,2,1,0:T(8,128)(2,1)}, u32[]{:S(2)}) copy-start(bf16[2,1,272,128]{3,2,1,0:T(8,128)(2,1)} %copy-done.7) | copy-start | bytes 417796
  128.3 4.1 %copy-start.11 = (bf16[2,1,272,128]{3,2,1,0:T(8,128)(2,1)S(1)}, bf16[2,1,272,128]{3,2,1,0:T(8,128)(2,1)}, u32[]{:S(2)}) copy-start(bf16[2,1,272,128]{3,2,1,0:T(8,128)(2,1)} %copy-done.9) | copy-start | bytes 417796

commit v9 on v8

--- a/solution.py
+++ b/solution.py
@@ -15,9 +15,9 @@
 V_DIM = 128
 LANES = 128
 QUERY, KEY, VALUE, OUT = range(4)
-CUT_MICROS = 10
-TOKEN_MICROS = 20
-CUTS = (0, 1, 4, 6, 8)
+CUT_MICROS = 30
+TOKEN_MICROS = 40
+CUTS = (0, 1, 3, 5, 8)
 VMEM_LIMIT = 16 * 1024 * 1024
 
 
@@ -335,7 +335,7 @@
             waits = waits + exchanged[at - 2][1:]
         if at == 1:
             waits = waits + exchanged[0][1:3]
-        if t_ways == 4 and at in (1, 2):
+        if t_ways == 4 and at in (1, len(chunks) - 1):
             waits = waits + [near if at == 1 else far]
         pieces = list(cut(rows, slice_map, blocks, ahead if at == 0 else (0,), item_rows, waits, CUT_MICROS))
         if at == 0:

time: 164 us -> 178 us (1.085)
  waiting for transfers between devices: 74.7 us -> 85.2 us
  local copies, waits for them, and re-layouts: 6.65 us -> 15.7 us
  starting transfers between devices: 48.7 us -> 45.8 us
  Pallas kernels: 30.4 us -> 28.3 us
    ppermute x12, waiting for transfers between devices: 25.4 us -> 37 us  [per_device(): lax.ppermute(piece, 'tp', [(i, (i + shift) % t_ways) for i in range(t_way...]
    unnamed x39 -> x59, local copies, waits for them, and re-layouts: 6.65 us -> 15.7 us
    pallas_call x1, Pallas kernels: 4.05 us -> 1.09 us  [assemble(): pl.pallas_call(kernel, grid_spec=pltpu.PrefetchScalarGridSpec(num_scalar_...]
    ppermute x12, starting transfers between devices: 18.2 us -> 16.3 us  [per_device(): lax.ppermute(piece, 'tp', [(i, (i + shift) % t_ways) for i in range(t_way...]
  transfers between devices with their start and end apart: 20 -> 20, of which waited for: 11 -> 11; matrix products, arithmetic and copies ran while one was open for 1% -> 1% of each run, Pallas kernels for 14% -> 11%
where the time goes in v9:
time: 178 us; the launch traced here: 177 us
  waiting for transfers between devices  85.2 us (48%)
  starting transfers between devices  45.8 us (26%)
  Pallas kernels  28.3 us (16%)
  local copies, waits for them, and re-layouts  15.7 us (9%)
    ppermute x12, waiting for transfers between devices, per_device(): lax.ppermute(piece, 'tp', [(i, (i + shift) % t_ways) for i in range(t_way...  37 us
    all_to_all x4, waiting for transfers between devices, over_fsdp(): x = lax.all_to_all(x, 'fsdp', split_axis=0, concat_axis=0, tiled=True)  22 us
    all_to_all x4, starting transfers between devices, over_fsdp(): x = lax.all_to_all(x, 'fsdp', split_axis=0, concat_axis=0, tiled=True)  17.8 us
    ppermute x12, starting transfers between devices, per_device(): lax.ppermute(piece, 'tp', [(i, (i + shift) % t_ways) for i in range(t_way...  16.3 us
    unnamed x59, local copies, waits for them, and re-layouts  15.7 us
    ppermute x1, waiting for transfers between devices, per_device(): lax.ppermute(pass_on(me, across, up, down, []), 'tp', [(1, 0), (2, 3)])  15.4 us
    pallas_call x4, Pallas kernels, absorb(): pl.pallas_call(kernel, grid_spec=pltpu.PrefetchScalarGridSpec(num_scalar_...  15.1 us
    ppermute x1, waiting for transfers between devices, neighbours(): lax.ppermute(x, axis, [(i + 1, i) for i in range(ways - 1)])  10.7 us
  transfers between devices with their start and end apart: 20, of which 11 were waited for; matrix products, arithmetic and copies ran while one was open for 1% of the time, Pallas kernels for 11%

profile of v9, /device:TPU:10, one launch (start us, length us, event | category | flops | bytes accessed | tf_op | source)
XLA Modules:
  0.0 177.2 jit_solution(1556413474657649008)
XLA Ops:
  0.6 0.8 copy.12.offsets
  1.4 3.1 %copy.17 = bf16[1,2,9728,128]{3,2,1,0:T(8,128)(2,1)S(1)} copy(bf16[1,2,9728,128]{3,1,2,0:T(2,128)(2,1)} %bitcast.26) | data formatting | bytes 9961472
  4.6 0.0 copy-start.27
  4.6 4.4 %pack.1 = (bf16[8,33,16,128]{3,2,1,0:T(8,128)(2,1)}, bf16[8,34,16,128]{3,2,1,0:T(8,128)(2,1)}, bf16[8,34,16,128]{3,2,1,0:T(8,128)(2,1)}, bf16[8,51,16,128]{3,2,1,0:T(8,128)(2,1)}) custom-call(s32[2,32,4]{2,1,0:T(8,128)S(1)} %copy.12.offsets, s32[2,32]{1,0:T(2,128)S(1)} %copy-done.22, bf16[2,608,16,128]{3,2,1,0:T(8,128)(2,1)S(1)} %bitcast.20), custom_call_target="tpu_custom_call" | custom-call | bytes 9961472 | tf_op jit(solution)/shard_map/pack/pallas_call | solution.py:77
  9.0 4.3 %all-to-all-start.3 = ((bf16[8,33,16,128]{3,2,1,0:T(8,128)(2,1)}), bf16[8,33,16,128]{3,2,1,0:T(8,128)(2,1)S(1)}, u32[]{:S(2)}, u32[]{:S(2)}) async-start(bf16[8,33,16,128]{3,2,1,0:T(8,128)(2,1)} %get-tuple-element.34), calls=%async_computation.3 | async-start | bytes 2162688 | tf_op jit(solution)/shard_map/all_to_all | solution.py:323
  13.2 0.1 copy.16.mapped
  13.3 14.2 %all-to-all-done.3 = bf16[8,33,16,128]{3,2,1,0:T(8,128)(2,1)S(1)} async-done(((bf16[8,33,16,128]{3,2,1,0:T(8,128)(2,1)}), bf16[8,33,16,128]{3,2,1,0:T(8,128)(2,1)S(1)}, u32[]{:S(2)}, u32[]{:S(2)}) %all-to-all-start.3) | async-done | bytes 1081376 | tf_op jit(solution)/shard_map/all_to_all | solution.py:323
  27.5 0.7 cut.4
  28.2 0.6 copy-done.11
  28.8 0.6 copy-done.24
  29.5 0.6 copy-done.25
  30.1 1.3 collective-permute-start.4
  31.4 5.6 %collective-permute-start.3 = (bf16[8,8,2,16,128]{4,3,2,1,0:T(8,128)(2,1)S(1)}, bf16[8,8,2,16,128]{4,3,2,1,0:T(8,128)(2,1)S(1)}, u32[]{:S(2)}, u32[]{:S(2)}) collective-permute-start(bf16[8,8,2,16,128]{4,3,2,1,0:T(8,128)(2,1)S(1)} %get-tuple-element.38.refs_0_), channel_id=1, source_target_pairs={{1,0},{2,1},{3,2},{5,4},{6,5},{7,6},{9,8},{10,9},{11,10},{13,12},{... | collective-permute-start | bytes 1572872 | tf_op jit(solution)/shard_map/ppermute | solution.py:168
  37.0 1.9 %collective-permute-start.2 = (bf16[8,8,2,16,128]{4,3,2,1,0:T(8,128)(2,1)S(1)}, bf16[8,8,2,16,128]{4,3,2,1,0:T(8,128)(2,1)S(1)}, u32[]{:S(2)}, u32[]{:S(2)}) collective-permute-start(bf16[8,8,2,16,128]{4,3,2,1,0:T(8,128)(2,1)S(1)} %get-tuple-element.38.refs_0_), channel_id=1, source_target_pairs={{0,1},{1,2},{2,3},{4,5},{5,6},{6,7},{8,9},{9,10},{10,11},{12,13},{... | collective-permute-start | bytes 1572872 | tf_op jit(solution)/shard_map/ppermute | solution.py:167
  38.9 5.0 %all-to-all-start.2 = ((bf16[8,34,16,128]{3,2,1,0:T(8,128)(2,1)}), bf16[8,34,16,128]{3,2,1,0:T(8,128)(2,1)S(1)}, u32[]{:S(2)}, u32[]{:S(2)}) async-start(bf16[8,34,16,128]{3,2,1,0:T(8,128)(2,1)} %get-tuple-element.33), calls=%async_computation.2 | async-start | bytes 2228224 | tf_op jit(solution)/shard_map/all_to_all | solution.py:323
  43.9 0.0 collective-permute-start
  43.9 4.4 %collective-permute-start.1 = (bf16[2,1,272,128]{3,2,1,0:T(8,128)(2,1)}, bf16[2,1,272,128]{3,2,1,0:T(8,128)(2,1)S(1)}, u32[]{:S(2)}, u32[]{:S(2)}) collective-permute-start(bf16[2,1,272,128]{3,2,1,0:T(8,128)(2,1)} %copy-done.24), channel_id=1, source_target_pairs={{0,2},{1,3},{2,0},{3,1},{4,6},{5,7},{6,4},{7,5},{8,10},{9,11},{10,... | collective-permute-start | bytes 417800 | tf_op jit(solution)/shard_map/ppermute | solution.py:352
  48.3 0.0 collective-permute-done.4.refs_2_.first
  48.3 0.0 collective-permute-start.5
  48.3 10.7 %collective-permute-done.3.refs_1_.below = bf16[8,8,2,16,128]{4,3,2,1,0:T(8,128)(2,1)S(1)} collective-permute-done((bf16[8,8,2,16,128]{4,3,2,1,0:T(8,128)(2,1)S(1)}, bf16[8,8,2,16,128]{4,3,2,1,0:T(8,128)(2,1)S(1)}, u32[]{:S(2)}, u32[]{:S(2)}) %collective-permute-start.3) | collective-permute-done | bytes 524320 | tf_op jit(solution)/shard_map/ppermute | solution.py:168
  59.0 0.1 collective-permute-done.2.refs_0_.above
  59.1 0.7 copy-done.2
  59.8 0.8 copy-done.4
  60.6 1.3 token_.1.refs_3_
  61.9 5.0 %all-to-all-start.1 = ((bf16[8,34,16,128]{3,2,1,0:T(8,128)(2,1)}), bf16[8,34,16,128]{3,2,1,0:T(8,128)(2,1)}, u32[]{:S(2)}, u32[]{:S(2)}) async-start(bf16[8,34,16,128]{3,2,1,0:T(8,128)(2,1)} %get-tuple-element.32), calls=%async_computation.1 | async-start | bytes 2228224 | tf_op jit(solution)/shard_map/all_to_all | solution.py:323
  66.9 0.0 collective-permute-done.refs_1_
  66.9 0.6 copy-done.14
  67.5 1.6 collective-permute-done.1.refs_2_
  69.2 0.6 copy-done.18
  69.8 0.9 copy-done.12
  70.7 0.9 copy-done.15
  71.6 0.9 copy-done.19
  72.5 0.7 copy-done.26
  73.2 1.6 cut.5
  74.8 3.3 %collective-permute-start.7 = (bf16[2,2,272,128]{3,2,1,0:T(8,128)(2,1)}, bf16[2,2,272,128]{3,2,1,0:T(8,128)(2,1)}, u32[]{:S(2)}, u32[]{:S(2)}) collective-permute-start(bf16[2,2,272,128]{3,2,1,0:T(8,128)(2,1)} %get-tuple-element.43), channel_id=1, source_target_pairs={{0,2},{1,3},{2,0},{3,1},{4,6},{5,7},{6,4},{7,5},{8,10},{9,11},{10,... | collective-permute-start | bytes 835592 | tf_op jit(solution)/shard_map/ppermute | solution.py:352
  78.1 2.0 %collective-permute-start.8 = (bf16[2,2,272,128]{3,2,1,0:T(8,128)(2,1)}, bf16[2,2,272,128]{3,2,1,0:T(8,128)(2,1)}, u32[]{:S(2)}, u32[]{:S(2)}) collective-permute-start(bf16[2,2,272,128]{3,2,1,0:T(8,128)(2,1)} %get-tuple-element.44), channel_id=1, source_target_pairs={{0,3},{1,0},{2,1},{3,2},{4,7},{5,4},{6,5},{7,6},{8,11},{9,8},{10,9... | collective-permute-start | bytes 835592 | tf_op jit(solution)/shard_map/ppermute | solution.py:352
  80.1 1.0 pass_on.1
  81.2 2.9 %collective-permute-start.9 = (bf16[2,8,8,2,16,128]{5,4,3,2,1,0:T(8,128)(2,1)}, bf16[2,8,8,2,16,128]{5,4,3,2,1,0:T(8,128)(2,1)}, u32[]{:S(2)}, u32[]{:S(2)}) collective-permute-start(bf16[2,8,8,2,16,128]{5,4,3,2,1,0:T(8,128)(2,1)} %pass_on.1), channel_id=1, source_target_pairs={{1,0},{2,3},{5,4},{6,7},{9,8},{10,11},{13,12},{14,15},{17,16},{18,... | collective-permute-start | bytes 3145736 | tf_op jit(solution)/shard_map/ppermute | solution.py:347
  84.1 0.0 all-to-all-done.1
  84.1 3.5 %all-to-all-start = ((bf16[8,51,16,128]{3,2,1,0:T(8,128)(2,1)}), bf16[8,51,16,128]{3,2,1,0:T(8,128)(2,1)S(1)}, u32[]{:S(2)}, u32[]{:S(2)}) async-start(bf16[8,51,16,128]{3,2,1,0:T(8,128)(2,1)} %get-tuple-element.31), calls=%async_computation | async-start | bytes 3342336 | tf_op jit(solution)/shard_map/all_to_all | solution.py:323
  87.6 0.9 copy-done.16
  88.5 0.9 copy-done.20
  89.4 2.2 %cut.6 = (bf16[2,2,272,128]{3,2,1,0:T(8,128)(2,1)S(1)}, bf16[2,2,272,128]{3,2,1,0:T(8,128)(2,1)}, bf16[2,2,272,128]{3,2,1,0:T(8,128)(2,1)}, bf16[2,2,272,128]{3,2,1,0:T(8,128)(2,1)}) custom-call(s32[8,4]{1,0:T(8,128)S(1)} %copy.16.mapped, bf16[8,544,128]{2,1,0:T(8,128)(2,1)} %bitcast.2.source, bf16[2,2,272,128]{3,2,1,0:T(8,128)(2,1)S(1)} %get-tuple-element.39.refs_0_, ...), custom_call_target="tpu_custom_call" | custom-call | flops 34500001792 | bytes 2228224 | tf_op jit(solution)/shard_map/cut/pallas_call | solution.py:132
  91.7 0.7 copy-done.8
  92.4 0.5 collective-permute-start.13
  92.9 0.4 collective-permute-start.14
  93.3 6.8 %collective-permute-done.7.refs_2_ = bf16[2,2,272,128]{3,2,1,0:T(8,128)(2,1)} collective-permute-done((bf16[2,2,272,128]{3,2,1,0:T(8,128)(2,1)}, bf16[2,2,272,128]{3,2,1,0:T(8,128)(2,1)}, u32[]{:S(2)}, u32[]{:S(2)}) %collective-permute-start.7) | collective-permute-done | bytes 278560 | tf_op jit(solution)/shard_map/ppermute | solution.py:352
  100.1 7.9 %all-to-all-done = bf16[8,51,16,128]{3,2,1,0:T(8,128)(2,1)S(1)} async-done(((bf16[8,51,16,128]{3,2,1,0:T(8,128)(2,1)}), bf16[8,51,16,128]{3,2,1,0:T(8,128)(2,1)S(1)}, u32[]{:S(2)}, u32[]{:S(2)}) %all-to-all-start) | async-done | bytes 1671200 | tf_op jit(solution)/shard_map/all_to_all | solution.py:323
  107.9 7.3 %collective-permute-done.8.refs_3_ = bf16[2,2,272,128]{3,2,1,0:T(8,128)(2,1)} collective-permute-done((bf16[2,2,272,128]{3,2,1,0:T(8,128)(2,1)}, bf16[2,2,272,128]{3,2,1,0:T(8,128)(2,1)}, u32[]{:S(2)}, u32[]{:S(2)}) %collective-permute-start.8) | collective-permute-done | bytes 278560 | tf_op jit(solution)/shard_map/ppermute | solution.py:352
  115.2 15.4 %collective-permute-done.9.refs_4_ = bf16[2,8,8,2,16,128]{5,4,3,2,1,0:T(8,128)(2,1)} collective-permute-done((bf16[2,8,8,2,16,128]{5,4,3,2,1,0:T(8,128)(2,1)}, bf16[2,8,8,2,16,128]{5,4,3,2,1,0:T(8,128)(2,1)}, u32[]{:S(2)}, u32[]{:S(2)}) %collective-permute-start.9) | collective-permute-done | bytes 1048608 | tf_op jit(solution)/shard_map/ppermute | solution.py:347
  130.7 1.0 copy-done.9
  131.6 0.8 cut.7
  132.5 1.7 collective-permute-start.10
  134.2 3.2 %collective-permute-start.11 = (bf16[2,3,272,128]{3,2,1,0:T(8,128)(2,1)S(1)}, bf16[2,3,272,128]{3,2,1,0:T(8,128)(2,1)S(1)}, u32[]{:S(2)}, u32[]{:S(2)}) collective-permute-start(bf16[2,3,272,128]{3,2,1,0:T(8,128)(2,1)S(1)} %get-tuple-element.47), channel_id=1, source_target_pairs={{0,2},{1,3},{2,0},{3,1},{4,6},{5,7},{6,4},{7,5},{8,10},{9,11},{10,... | collective-permute-start | bytes 1253384 | tf_op jit(solution)/shard_map/ppermute | solution.py:352
  137.4 0.8 collective-permute-start.12
  138.2 1.4 broadcast_select_fusion
  139.6 1.1 assemble.1.refs_4_
  140.7 3.0 %absorb.4 = (bf16[8,2,4,48,512]{4,3,2,1,0:T(8,128)(2,1)}, bf16[8,2,4,224,512]{4,3,2,1,0:T(8,128)(2,1)}) custom-call(s32[1]{0:T(128)} %bitcast.me_ref.at, bf16[2,1,272,128]{3,2,1,0:T(8,128)(2,1)S(1)} %copy-done.13, bf16[2,1,272,128]{3,2,1,0:T(8,128)(2,1)S(1)} %copy-done.17, bf16[2,1,272,128]{3,2,1,0:T(8,128)(2,1)S(1)} %copy-done.21, ...), custom_call_target="tpu_custom_call" | custom-call | flops 285212672 | bytes 2785280 | tf_op jit(solution)/shard_map/absorb/pallas_call | solution.py:264
  143.7 4.0 %absorb.5 = (bf16[8,2,4,48,512]{4,3,2,1,0:T(8,128)(2,1)}, bf16[8,2,4,224,512]{4,3,2,1,0:T(8,128)(2,1)}) custom-call(s32[1]{0:T(128)} %bitcast.me_ref.at, bf16[2,2,272,128]{3,2,1,0:T(8,128)(2,1)S(1)} %get-tuple-element.39.refs_0_, bf16[2,2,272,128]{3,2,1,0:T(8,128)(2,1)} %collective-permute-done.6.refs_1_, ...), custom_call_target="tpu_custom_call", output_to_operand_aliasing={{0}: (6, {}), {1}: (7, {})} | custom-call | flops 570425344 | bytes 5570560 | tf_op jit(solution)/shard_map/absorb/pallas_call | solution.py:264
  147.7 3.9 %absorb.6 = (bf16[8,2,4,48,512]{4,3,2,1,0:T(8,128)(2,1)}, bf16[8,2,4,224,512]{4,3,2,1,0:T(8,128)(2,1)}) custom-call(s32[1]{0:T(128)} %bitcast.me_ref.at, bf16[2,2,272,128]{3,2,1,0:T(8,128)(2,1)S(1)} %copy-done.10, bf16[2,2,272,128]{3,2,1,0:T(8,128)(2,1)} %collective-permute-done.13.refs_1_, ...), custom_call_target="tpu_custom_call", output_to_operand_aliasing={{0}: (6, {}), {1}: (7, {})} | custom-call | flops 570425344 | bytes 5570560 | tf_op jit(solution)/shard_map/absorb/pallas_call | solution.py:264
  151.6 10.4 %collective-permute-done.10.refs_1_ = bf16[2,3,272,128]{3,2,1,0:T(8,128)(2,1)S(1)} collective-permute-done((bf16[2,3,272,128]{3,2,1,0:T(8,128)(2,1)S(1)}, bf16[2,3,272,128]{3,2,1,0:T(8,128)(2,1)S(1)}, u32[]{:S(2)}, u32[]{:S(2)}) %collective-permute-start.10) | collective-permute-done | bytes 417824 | tf_op jit(solution)/shard_map/ppermute | solution.py:352
  162.1 6.6 %collective-permute-done.11.refs_2_ = bf16[2,3,272,128]{3,2,1,0:T(8,128)(2,1)S(1)} collective-permute-done((bf16[2,3,272,128]{3,2,1,0:T(8,128)(2,1)S(1)}, bf16[2,3,272,128]{3,2,1,0:T(8,128)(2,1)S(1)}, u32[]{:S(2)}, u32[]{:S(2)}) %collective-permute-start.11) | collective-permute-done | bytes 417824 | tf_op jit(solution)/shard_map/ppermute | solution.py:352
  168.7 4.3 %collective-permute-done.12.refs_3_ = bf16[2,3,272,128]{3,2,1,0:T(8,128)(2,1)S(1)} collective-permute-done((bf16[2,3,272,128]{3,2,1,0:T(8,128)(2,1)S(1)}, bf16[2,3,272,128]{3,2,1,0:T(8,128)(2,1)S(1)}, u32[]{:S(2)}, u32[]{:S(2)}) %collective-permute-start.12) | collective-permute-done | bytes 417824 | tf_op jit(solution)/shard_map/ppermute | solution.py:352
  172.9 4.2 %absorb.7 = (bf16[8,2,4,48,512]{4,3,2,1,0:T(8,128)(2,1)}, bf16[8,2,4,224,512]{4,3,2,1,0:T(8,128)(2,1)}) custom-call(s32[1]{0:T(128)} %bitcast.me_ref.at, bf16[2,3,272,128]{3,2,1,0:T(8,128)(2,1)S(1)} %get-tuple-element.45.refs_0_, bf16[2,3,272,128]{3,2,1,0:T(8,128)(2,1)S(1)} %collective-permute-done.10.refs_1_, ...), custom_call_target="tpu_custom_call", output_to_operand_aliasing={{0}: (6, {}), {1}: (7, {})} | custom-call | flops 855638016 | bytes 8355840 | tf_op jit(solution)/shard_map/absorb/pallas_call | solution.py:264
  (48 shorter events, 0.1 us)
Async XLA Ops:
  1.4 3.1 %copy-start.22 = (s32[2,32]{1,0:T(2,128)S(1)}, s32[2,32]{1,0:T(2,128)}, u32[]{:S(2)}) copy-start(s32[2,32]{1,0:T(2,128)} %owners.1) | copy-start | bytes 772
  4.6 8.7 %copy-start.27 = (s32[8,4]{0,1:T(4,128)S(1)}, s32[8,4]{0,1:T(4,128)}, u32[]{:S(2)}) copy-start(s32[8,4]{0,1:T(4,128)} %param.7) | copy-start | bytes 388
  9.0 18.5 %all-to-all-start.3 = ((bf16[8,33,16,128]{3,2,1,0:T(8,128)(2,1)}), bf16[8,33,16,128]{3,2,1,0:T(8,128)(2,1)S(1)}, u32[]{:S(2)}, u32[]{:S(2)}) async-start(bf16[8,33,16,128]{3,2,1,0:T(8,128)(2,1)} %get-tuple-element.34), calls=%async_computation.3 | async-start | bytes 2162688 | tf_op jit(solution)/shard_map/all_to_all | solution.py:323
  28.2 0.6 copy-start.11
  28.8 0.6 copy-start.24
  29.5 0.6 copy-start.25
  30.1 13.8 %copy-start.23 = (bf16[2,1,272,128]{3,2,1,0:T(8,128)(2,1)}, bf16[2,1,272,128]{3,2,1,0:T(8,128)(2,1)S(1)}, u32[]{:S(2)}) copy-start(bf16[2,1,272,128]{3,2,1,0:T(8,128)(2,1)S(1)} %get-tuple-element.40) | copy-start | bytes 417796
  30.1 31.8 %copy-start.6 = (bf16[8,8,2,16,128]{4,3,2,1,0:T(8,128)(2,1)}, bf16[8,8,2,16,128]{4,3,2,1,0:T(8,128)(2,1)S(1)}, u32[]{:S(2)}) copy-start(bf16[8,8,2,16,128]{4,3,2,1,0:T(8,128)(2,1)S(1)} %get-tuple-element.38.refs_0_) | copy-start | bytes 1572868
  30.1 18.2 %collective-permute-start.4 = (bf16[8,8,2,16,128]{4,3,2,1,0:T(8,128)(2,1)S(1)}, bf16[8,8,2,16,128]{4,3,2,1,0:T(8,128)(2,1)S(1)}, u32[]{:S(2)}, u32[]{:S(2)}) collective-permute-start(bf16[8,8,2,16,128]{4,3,2,1,0:T(8,128)(2,1)S(1)} %get-tuple-element.38.refs_0_), channel_id=1, source_target_pairs={{0,2},{3,1},{4,6},{7,5},{8,10},{11,9},{12,14},{15,13},{16,18},{19,... | collective-permute-start | bytes 1572872 | tf_op jit(solution)/shard_map/ppermute | solution.py:345
  31.4 27.6 %collective-permute-start.3 = (bf16[8,8,2,16,128]{4,3,2,1,0:T(8,128)(2,1)S(1)}, bf16[8,8,2,16,128]{4,3,2,1,0:T(8,128)(2,1)S(1)}, u32[]{:S(2)}, u32[]{:S(2)}) collective-permute-start(bf16[8,8,2,16,128]{4,3,2,1,0:T(8,128)(2,1)S(1)} %get-tuple-element.38.refs_0_), channel_id=1, source_target_pairs={{1,0},{2,1},{3,2},{5,4},{6,5},{7,6},{9,8},{10,9},{11,10},{13,12},{... | collective-permute-start | bytes 1572872 | tf_op jit(solution)/shard_map/ppermute | solution.py:168
  37.0 22.1 %collective-permute-start.2 = (bf16[8,8,2,16,128]{4,3,2,1,0:T(8,128)(2,1)S(1)}, bf16[8,8,2,16,128]{4,3,2,1,0:T(8,128)(2,1)S(1)}, u32[]{:S(2)}, u32[]{:S(2)}) collective-permute-start(bf16[8,8,2,16,128]{4,3,2,1,0:T(8,128)(2,1)S(1)} %get-tuple-element.38.refs_0_), channel_id=1, source_target_pairs={{0,1},{1,2},{2,3},{4,5},{5,6},{6,7},{8,9},{9,10},{10,11},{12,13},{... | collective-permute-start | bytes 1572872 | tf_op jit(solution)/shard_map/ppermute | solution.py:167
  38.9 23.0 %all-to-all-start.2 = ((bf16[8,34,16,128]{3,2,1,0:T(8,128)(2,1)}), bf16[8,34,16,128]{3,2,1,0:T(8,128)(2,1)S(1)}, u32[]{:S(2)}, u32[]{:S(2)}) async-start(bf16[8,34,16,128]{3,2,1,0:T(8,128)(2,1)} %get-tuple-element.33), calls=%async_computation.2 | async-start | bytes 2228224 | tf_op jit(solution)/shard_map/all_to_all | solution.py:323
  43.9 23.0 %collective-permute-start = (bf16[2,1,272,128]{3,2,1,0:T(8,128)(2,1)}, bf16[2,1,272,128]{3,2,1,0:T(8,128)(2,1)S(1)}, u32[]{:S(2)}, u32[]{:S(2)}) collective-permute-start(bf16[2,1,272,128]{3,2,1,0:T(8,128)(2,1)} %copy-done.25), channel_id=1, source_target_pairs={{0,1},{1,2},{2,3},{3,0},{4,5},{5,6},{6,7},{7,4},{8,9},{9,10},{10,1... | collective-permute-start | bytes 417800 | tf_op jit(solution)/shard_map/ppermute | solution.py:352
  43.9 25.2 %collective-permute-start.1 = (bf16[2,1,272,128]{3,2,1,0:T(8,128)(2,1)}, bf16[2,1,272,128]{3,2,1,0:T(8,128)(2,1)S(1)}, u32[]{:S(2)}, u32[]{:S(2)}) collective-permute-start(bf16[2,1,272,128]{3,2,1,0:T(8,128)(2,1)} %copy-done.24), channel_id=1, source_target_pairs={{0,2},{1,3},{2,0},{3,1},{4,6},{5,7},{6,4},{7,5},{8,10},{9,11},{10,... | collective-permute-start | bytes 417800 | tf_op jit(solution)/shard_map/ppermute | solution.py:352
  48.3 10.7 %copy-start = (bf16[8,8,2,16,128]{4,3,2,1,0:T(8,128)(2,1)}, bf16[8,8,2,16,128]{4,3,2,1,0:T(8,128)(2,1)S(1)}, u32[]{:S(2)}) copy-start(bf16[8,8,2,16,128]{4,3,2,1,0:T(8,128)(2,1)S(1)} %collective-permute-done.4.refs_2_.first) | copy-start | bytes 1572868
  48.3 39.3 %collective-permute-start.5 = (bf16[2,1,272,128]{3,2,1,0:T(8,128)(2,1)}, bf16[2,1,272,128]{3,2,1,0:T(8,128)(2,1)}, u32[]{:S(2)}, u32[]{:S(2)}) collective-permute-start(bf16[2,1,272,128]{3,2,1,0:T(8,128)(2,1)} %copy-done.23), channel_id=1, source_target_pairs={{0,3},{1,0},{2,1},{3,2},{4,7},{5,4},{6,5},{7,6},{8,11},{9,8},{10,9... | collective-permute-start | bytes 417800 | tf_op jit(solution)/shard_map/ppermute | solution.py:352
  59.0 0.8 copy-start.2
  59.8 0.8 copy-start.4
  61.9 22.2 %all-to-all-start.1 = ((bf16[8,34,16,128]{3,2,1,0:T(8,128)(2,1)}), bf16[8,34,16,128]{3,2,1,0:T(8,128)(2,1)}, u32[]{:S(2)}, u32[]{:S(2)}) async-start(bf16[8,34,16,128]{3,2,1,0:T(8,128)(2,1)} %get-tuple-element.32), calls=%async_computation.1 | async-start | bytes 2228224 | tf_op jit(solution)/shard_map/all_to_all | solution.py:323
  66.9 0.6 copy-start.14
  69.2 0.6 copy-start.18
  69.8 0.9 copy-start.12
  70.7 0.9 copy-start.15
  71.6 0.9 copy-start.19
  72.5 0.7 copy-start.26
  73.2 6.9 %copy-start.1 = (bf16[8,8,2,16,128]{4,3,2,1,0:T(8,128)(2,1)S(1)}, bf16[8,8,2,16,128]{4,3,2,1,0:T(8,128)(2,1)}, u32[]{:S(2)}) copy-start(bf16[8,8,2,16,128]{4,3,2,1,0:T(8,128)(2,1)} %copy-done) | copy-start | bytes 1572868
  73.2 6.9 %copy-start.3 = (bf16[8,8,2,16,128]{4,3,2,1,0:T(8,128)(2,1)S(1)}, bf16[8,8,2,16,128]{4,3,2,1,0:T(8,128)(2,1)}, u32[]{:S(2)}) copy-start(bf16[8,8,2,16,128]{4,3,2,1,0:T(8,128)(2,1)} %copy-done.2) | copy-start | bytes 1572868
  73.2 6.9 %copy-start.5 = (bf16[8,8,2,16,128]{4,3,2,1,0:T(8,128)(2,1)S(1)}, bf16[8,8,2,16,128]{4,3,2,1,0:T(8,128)(2,1)}, u32[]{:S(2)}) copy-start(bf16[8,8,2,16,128]{4,3,2,1,0:T(8,128)(2,1)} %copy-done.4) | copy-start | bytes 1572868
  74.8 18.1 %collective-permute-start.6 = (bf16[2,2,272,128]{3,2,1,0:T(8,128)(2,1)}, bf16[2,2,272,128]{3,2,1,0:T(8,128)(2,1)}, u32[]{:S(2)}, u32[]{:S(2)}) collective-permute-start(bf16[2,2,272,128]{3,2,1,0:T(8,128)(2,1)} %get-tuple-element.42), channel_id=1, source_target_pairs={{0,1},{1,2},{2,3},{3,0},{4,5},{5,6},{6,7},{7,4},{8,9},{9,10},{10,1... | collective-permute-start | bytes 835592 | tf_op jit(solution)/shard_map/ppermute | solution.py:352
  74.8 25.3 %collective-permute-start.7 = (bf16[2,2,272,128]{3,2,1,0:T(8,128)(2,1)}, bf16[2,2,272,128]{3,2,1,0:T(8,128)(2,1)}, u32[]{:S(2)}, u32[]{:S(2)}) collective-permute-start(bf16[2,2,272,128]{3,2,1,0:T(8,128)(2,1)} %get-tuple-element.43), channel_id=1, source_target_pairs={{0,2},{1,3},{2,0},{3,1},{4,6},{5,7},{6,4},{7,5},{8,10},{9,11},{10,... | collective-permute-start | bytes 835592 | tf_op jit(solution)/shard_map/ppermute | solution.py:352
  78.1 37.2 %collective-permute-start.8 = (bf16[2,2,272,128]{3,2,1,0:T(8,128)(2,1)}, bf16[2,2,272,128]{3,2,1,0:T(8,128)(2,1)}, u32[]{:S(2)}, u32[]{:S(2)}) collective-permute-start(bf16[2,2,272,128]{3,2,1,0:T(8,128)(2,1)} %get-tuple-element.44), channel_id=1, source_target_pairs={{0,3},{1,0},{2,1},{3,2},{4,7},{5,4},{6,5},{7,6},{8,11},{9,8},{10,9... | collective-permute-start | bytes 835592 | tf_op jit(solution)/shard_map/ppermute | solution.py:352
  81.2 49.5 %collective-permute-start.9 = (bf16[2,8,8,2,16,128]{5,4,3,2,1,0:T(8,128)(2,1)}, bf16[2,8,8,2,16,128]{5,4,3,2,1,0:T(8,128)(2,1)}, u32[]{:S(2)}, u32[]{:S(2)}) collective-permute-start(bf16[2,8,8,2,16,128]{5,4,3,2,1,0:T(8,128)(2,1)} %pass_on.1), channel_id=1, source_target_pairs={{1,0},{2,3},{5,4},{6,7},{9,8},{10,11},{13,12},{14,15},{17,16},{18,... | collective-permute-start | bytes 3145736 | tf_op jit(solution)/shard_map/ppermute | solution.py:347
  84.1 23.9 %all-to-all-start = ((bf16[8,51,16,128]{3,2,1,0:T(8,128)(2,1)}), bf16[8,51,16,128]{3,2,1,0:T(8,128)(2,1)S(1)}, u32[]{:S(2)}, u32[]{:S(2)}) async-start(bf16[8,51,16,128]{3,2,1,0:T(8,128)(2,1)} %get-tuple-element.31), calls=%async_computation | async-start | bytes 3342336 | tf_op jit(solution)/shard_map/all_to_all | solution.py:323
  87.6 0.9 copy-start.16
  88.5 0.9 copy-start.20
  91.7 0.7 copy-start.8
  92.4 45.0 %collective-permute-start.13 = (bf16[2,2,272,128]{3,2,1,0:T(8,128)(2,1)}, bf16[2,2,272,128]{3,2,1,0:T(8,128)(2,1)}, u32[]{:S(2)}, u32[]{:S(2)}) collective-permute-start(bf16[2,2,272,128]{3,2,1,0:T(8,128)(2,1)} %get-tuple-element.49), channel_id=1, source_target_pairs={{0,1},{1,2},{2,3},{3,0},{4,5},{5,6},{6,7},{7,4},{8,9},{9,10},{10,1... | collective-permute-start | bytes 835592 | tf_op jit(solution)/shard_map/ppermute | solution.py:352
  92.9 54.7 %collective-permute-start.14 = (bf16[2,2,272,128]{3,2,1,0:T(8,128)(2,1)}, bf16[2,2,272,128]{3,2,1,0:T(8,128)(2,1)}, u32[]{:S(2)}, u32[]{:S(2)}) collective-permute-start(bf16[2,2,272,128]{3,2,1,0:T(8,128)(2,1)} %get-tuple-element.50), channel_id=1, source_target_pairs={{0,2},{1,3},{2,0},{3,1},{4,6},{5,7},{6,4},{7,5},{8,10},{9,11},{10,... | collective-permute-start | bytes 835592 | tf_op jit(solution)/shard_map/ppermute | solution.py:352
  100.1 47.6 %collective-permute-start.15 = (bf16[2,2,272,128]{3,2,1,0:T(8,128)(2,1)}, bf16[2,2,272,128]{3,2,1,0:T(8,128)(2,1)}, u32[]{:S(2)}, u32[]{:S(2)}) collective-permute-start(bf16[2,2,272,128]{3,2,1,0:T(8,128)(2,1)} %get-tuple-element.51), channel_id=1, source_target_pairs={{0,3},{1,0},{2,1},{3,2},{4,7},{5,4},{6,5},{7,6},{8,11},{9,8},{10,9... | collective-permute-start | bytes 835592 | tf_op jit(solution)/shard_map/ppermute | solution.py:352
  130.6 1.0 copy-start.9
  132.5 7.1 %copy-start.7 = (bf16[8,8,2,16,128]{4,3,2,1,0:T(8,128)(2,1)S(1)}, bf16[8,8,2,16,128]{4,3,2,1,0:T(8,128)(2,1)}, u32[]{:S(2)}) copy-start(bf16[8,8,2,16,128]{4,3,2,1,0:T(8,128)(2,1)} %copy-done.6) | copy-start | bytes 1572868
  132.5 29.6 %collective-permute-start.10 = (bf16[2,3,272,128]{3,2,1,0:T(8,128)(2,1)S(1)}, bf16[2,3,272,128]{3,2,1,0:T(8,128)(2,1)S(1)}, u32[]{:S(2)}, u32[]{:S(2)}) collective-permute-start(bf16[2,3,272,128]{3,2,1,0:T(8,128)(2,1)S(1)} %get-tuple-element.46), channel_id=1, source_target_pairs={{0,1},{1,2},{2,3},{3,0},{4,5},{5,6},{6,7},{7,4},{8,9},{9,10},{10,1... | collective-permute-start | bytes 1253384 | tf_op jit(solution)/shard_map/ppermute | solution.py:352
  134.2 34.4 %collective-permute-start.11 = (bf16[2,3,272,128]{3,2,1,0:T(8,128)(2,1)S(1)}, bf16[2,3,272,128]{3,2,1,0:T(8,128)(2,1)S(1)}, u32[]{:S(2)}, u32[]{:S(2)}) collective-permute-start(bf16[2,3,272,128]{3,2,1,0:T(8,128)(2,1)S(1)} %get-tuple-element.47), channel_id=1, source_target_pairs={{0,2},{1,3},{2,0},{3,1},{4,6},{5,7},{6,4},{7,5},{8,10},{9,11},{10,... | collective-permute-start | bytes 1253384 | tf_op jit(solution)/shard_map/ppermute | solution.py:352
  137.4 35.6 %collective-permute-start.12 = (bf16[2,3,272,128]{3,2,1,0:T(8,128)(2,1)S(1)}, bf16[2,3,272,128]{3,2,1,0:T(8,128)(2,1)S(1)}, u32[]{:S(2)}, u32[]{:S(2)}) collective-permute-start(bf16[2,3,272,128]{3,2,1,0:T(8,128)(2,1)S(1)} %get-tuple-element.48), channel_id=1, source_target_pairs={{0,3},{1,0},{2,1},{3,2},{4,7},{5,4},{6,5},{7,6},{8,11},{9,8},{10,9... | collective-permute-start | bytes 1253384 | tf_op jit(solution)/shard_map/ppermute | solution.py:352
  139.6 1.1 copy-start.13
  139.6 1.1 copy-start.17
  139.6 1.1 copy-start.21
  143.7 4.0 %copy-start.10 = (bf16[2,2,272,128]{3,2,1,0:T(8,128)(2,1)S(1)}, bf16[2,2,272,128]{3,2,1,0:T(8,128)(2,1)}, u32[]{:S(2)}) copy-start(bf16[2,2,272,128]{3,2,1,0:T(8,128)(2,1)} %copy-done.8) | copy-start | bytes 835588

commit v10 on v8

--- a/solution.py
+++ b/solution.py
@@ -335,8 +335,8 @@
             waits = waits + exchanged[at - 2][1:]
         if at == 1:
             waits = waits + exchanged[0][1:3]
-        if t_ways == 4 and at in (1, 2):
-            waits = waits + [near if at == 1 else far]
+        if t_ways == 4 and at == 1:
+            waits = waits + [near, passed]
         pieces = list(cut(rows, slice_map, blocks, ahead if at == 0 else (0,), item_rows, waits, CUT_MICROS))
         if at == 0:
             pairs = pieces.pop(0)
@@ -344,7 +344,8 @@
             if t_ways == 4:
                 across = lax.ppermute(pairs, "tp", [(0, 2), (3, 1)])
                 near = token([up, down, across], TOKEN_MICROS)
-                far = lax.ppermute(pass_on(me, across, up, down, []), "tp", [(1, 0), (2, 3)])
+                passed = pass_on(me, across, up, down, [])
+                far = lax.ppermute(passed, "tp", [(1, 0), (2, 3)])
         sent.append(pieces)
         exchanged.append(
             pieces[:1]

time: 164 us -> 165 us (level)
  waiting for transfers between devices: 74.7 us -> 48.5 us
  starting transfers between devices: 48.7 us -> 74.1 us
    ppermute x12, starting transfers between devices: 18.2 us -> 43.6 us  [per_device(): lax.ppermute(piece, 'tp', [(i, (i + shift) % t_ways) for i in range(t_way...]
    ppermute x1, waiting for transfers between devices: 17 us -> 0.01 us  [per_device(): far = lax.ppermute(passed, 'tp', [(1, 0), (2, 3)])]
    ppermute x12, waiting for transfers between devices: 25.4 us -> 16.3 us  [per_device(): lax.ppermute(piece, 'tp', [(i, (i + shift) % t_ways) for i in range(t_way...]
  transfers between devices with their start and end apart: 20 -> 20, of which waited for: 11 -> 9; matrix products, arithmetic and copies ran while one was open for 1% -> 1% of each run, Pallas kernels for 14% -> 14%
where the time goes in v10:
time: 165 us; the launch traced here: 163 us
  starting transfers between devices  74.1 us (45%)
  waiting for transfers between devices  48.5 us (29%)
  Pallas kernels  31.3 us (19%)
  local copies, waits for them, and re-layouts  6.65 us (4%)
    ppermute x12, starting transfers between devices, per_device(): lax.ppermute(piece, 'tp', [(i, (i + shift) % t_ways) for i in range(t_way...  43.6 us
    all_to_all x4, waiting for transfers between devices, over_fsdp(): x = lax.all_to_all(x, 'fsdp', split_axis=0, concat_axis=0, tiled=True)  21.3 us
    all_to_all x4, starting transfers between devices, over_fsdp(): x = lax.all_to_all(x, 'fsdp', split_axis=0, concat_axis=0, tiled=True)  19.3 us
    ppermute x12, waiting for transfers between devices, per_device(): lax.ppermute(piece, 'tp', [(i, (i + shift) % t_ways) for i in range(t_way...  16.3 us
    pallas_call x4, Pallas kernels, absorb(): pl.pallas_call(kernel, grid_spec=pltpu.PrefetchScalarGridSpec(num_scalar_...  15 us
    ppermute x1, waiting for transfers between devices, neighbours(): lax.ppermute(x, axis, [(i + 1, i) for i in range(ways - 1)])  10.8 us
    unnamed x39, local copies, waits for them, and re-layouts  6.65 us
    pallas_call x4, Pallas kernels, cut(): pl.pallas_call(kernel, grid=(1,), out_shape=[jax.ShapeDtypeStruct(shape,...  5.88 us
  transfers between devices with their start and end apart: 20, of which 9 were waited for; matrix products, arithmetic and copies ran while one was open for 1% of the time, Pallas kernels for 14%

profile of v10, /device:TPU:10, one launch (start us, length us, event | category | flops | bytes accessed | tf_op | source)
XLA Modules:
  0.0 162.8 jit_solution(17665153845491821746)
XLA Ops:
  0.6 0.8 copy.12.offsets
  1.4 3.1 %copy.17 = bf16[1,2,9728,128]{3,2,1,0:T(8,128)(2,1)S(1)} copy(bf16[1,2,9728,128]{3,1,2,0:T(2,128)(2,1)} %bitcast.27) | data formatting | bytes 9961472
  4.6 0.0 copy-start.17
  4.6 4.0 %pack.1 = (bf16[8,33,16,128]{3,2,1,0:T(8,128)(2,1)}, bf16[8,51,16,128]{3,2,1,0:T(8,128)(2,1)}, bf16[8,34,16,128]{3,2,1,0:T(8,128)(2,1)S(1)}, bf16[8,34,16,128]{3,2,1,0:T(8,128)(2,1)}) custom-call(s32[2,32,4]{2,1,0:T(8,128)S(1)} %copy.12.offsets, s32[2,32]{1,0:T(2,128)S(1)} %copy-done.12, bf16[2,608,16,128]{3,2,1,0:T(8,128)(2,1)S(1)} %bitcast.20), custom_call_target="tpu_custom_call" | custom-call | bytes 9961472 | tf_op jit(solution)/shard_map/pack/pallas_call | solution.py:77
  8.5 1.0 copy-done.6
  9.5 4.3 %all-to-all-start.3 = ((bf16[8,33,16,128]{3,2,1,0:T(8,128)(2,1)}), bf16[8,33,16,128]{3,2,1,0:T(8,128)(2,1)S(1)}, u32[]{:S(2)}, u32[]{:S(2)}) async-start(bf16[8,33,16,128]{3,2,1,0:T(8,128)(2,1)} %get-tuple-element.34), calls=%async_computation.3 | async-start | bytes 2162688 | tf_op jit(solution)/shard_map/all_to_all | solution.py:323
  13.8 0.0 copy-done.17
  13.8 0.1 copy.16.mapped
  13.9 14.2 %all-to-all-done.3 = bf16[8,33,16,128]{3,2,1,0:T(8,128)(2,1)S(1)} async-done(((bf16[8,33,16,128]{3,2,1,0:T(8,128)(2,1)}), bf16[8,33,16,128]{3,2,1,0:T(8,128)(2,1)S(1)}, u32[]{:S(2)}, u32[]{:S(2)}) %all-to-all-start.3) | async-done | bytes 1081376 | tf_op jit(solution)/shard_map/all_to_all | solution.py:323
  28.1 1.5 cut.4
  29.5 1.3 collective-permute-start.4
  30.8 5.6 %collective-permute-start.3 = (bf16[8,8,2,16,128]{4,3,2,1,0:T(8,128)(2,1)}, bf16[8,8,2,16,128]{4,3,2,1,0:T(8,128)(2,1)S(1)}, u32[]{:S(2)}, u32[]{:S(2)}) collective-permute-start(bf16[8,8,2,16,128]{4,3,2,1,0:T(8,128)(2,1)} %get-tuple-element.38.refs_0_), channel_id=1, source_target_pairs={{1,0},{2,1},{3,2},{5,4},{6,5},{7,6},{9,8},{10,9},{11,10},{13,12},{... | collective-permute-start | bytes 1572872 | tf_op jit(solution)/shard_map/ppermute | solution.py:168
  36.4 0.0 copy-done.15
  36.4 1.9 %collective-permute-start.2 = (bf16[8,8,2,16,128]{4,3,2,1,0:T(8,128)(2,1)}, bf16[8,8,2,16,128]{4,3,2,1,0:T(8,128)(2,1)S(1)}, u32[]{:S(2)}, u32[]{:S(2)}) collective-permute-start(bf16[8,8,2,16,128]{4,3,2,1,0:T(8,128)(2,1)} %get-tuple-element.38.refs_0_), channel_id=1, source_target_pairs={{0,1},{1,2},{2,3},{4,5},{5,6},{6,7},{8,9},{9,10},{10,11},{12,13},{... | collective-permute-start | bytes 1572872 | tf_op jit(solution)/shard_map/ppermute | solution.py:167
  38.4 5.0 %all-to-all-start.2 = ((bf16[8,51,16,128]{3,2,1,0:T(8,128)(2,1)}), bf16[8,51,16,128]{3,2,1,0:T(8,128)(2,1)S(1)}, u32[]{:S(2)}, u32[]{:S(2)}) async-start(bf16[8,51,16,128]{3,2,1,0:T(8,128)(2,1)} %get-tuple-element.33), calls=%async_computation.2 | async-start | bytes 3342336 | tf_op jit(solution)/shard_map/all_to_all | solution.py:323
  43.4 0.0 collective-permute-start
  43.4 4.4 %collective-permute-start.1 = (bf16[2,1,272,128]{3,2,1,0:T(8,128)(2,1)}, bf16[2,1,272,128]{3,2,1,0:T(8,128)(2,1)}, u32[]{:S(2)}, u32[]{:S(2)}) collective-permute-start(bf16[2,1,272,128]{3,2,1,0:T(8,128)(2,1)} %copy-done.14), channel_id=1, source_target_pairs={{0,2},{1,3},{2,0},{3,1},{4,6},{5,7},{6,4},{7,5},{8,10},{9,11},{10,... | collective-permute-start | bytes 417800 | tf_op jit(solution)/shard_map/ppermute | solution.py:353
  47.8 0.0 collective-permute-done.4.refs_2_.first
  47.8 0.0 collective-permute-start.5
  47.8 10.8 %collective-permute-done.3.refs_1_.below = bf16[8,8,2,16,128]{4,3,2,1,0:T(8,128)(2,1)S(1)} collective-permute-done((bf16[8,8,2,16,128]{4,3,2,1,0:T(8,128)(2,1)}, bf16[8,8,2,16,128]{4,3,2,1,0:T(8,128)(2,1)S(1)}, u32[]{:S(2)}, u32[]{:S(2)}) %collective-permute-start.3) | collective-permute-done | bytes 524320 | tf_op jit(solution)/shard_map/ppermute | solution.py:168
  58.6 0.1 collective-permute-done.2.refs_0_.above
  58.7 1.1 pass_on.1.refs_4_
  59.9 2.5 %collective-permute-start.12 = (bf16[2,8,8,2,16,128]{5,4,3,2,1,0:T(8,128)(2,1)}, bf16[2,8,8,2,16,128]{5,4,3,2,1,0:T(8,128)(2,1)}, u32[]{:S(2)}, u32[]{:S(2)}) collective-permute-start(bf16[2,8,8,2,16,128]{5,4,3,2,1,0:T(8,128)(2,1)} %pass_on.1.refs_4_), channel_id=1, source_target_pairs={{1,0},{2,3},{5,4},{6,7},{9,8},{10,11},{13,12},{14,15},{17,16},{18,... | collective-permute-start | bytes 3145736 | tf_op jit(solution)/shard_map/ppermute | solution.py:348
  62.3 0.0 copy-done
  62.3 1.3 token_.1.refs_3_
  63.6 0.4 all-to-all-done.2
  64.0 5.0 %all-to-all-start.1 = ((bf16[8,34,16,128]{3,2,1,0:T(8,128)(2,1)}), bf16[8,34,16,128]{3,2,1,0:T(8,128)(2,1)S(1)}, u32[]{:S(2)}, u32[]{:S(2)}) async-start(bf16[8,34,16,128]{3,2,1,0:T(8,128)(2,1)} %copy-done.6), calls=%async_computation.1 | async-start | bytes 2228224 | tf_op jit(solution)/shard_map/all_to_all | solution.py:323
  69.0 0.0 collective-permute-done.refs_1_
  69.0 0.0 collective-permute-done.1.refs_2_
  69.0 0.0 copy-done.7
  69.0 0.7 copy-done.16
  69.7 1.8 %cut.5 = (bf16[2,3,272,128]{3,2,1,0:T(8,128)(2,1)S(1)}, bf16[2,3,272,128]{3,2,1,0:T(8,128)(2,1)}, bf16[2,3,272,128]{3,2,1,0:T(8,128)(2,1)}, bf16[2,3,272,128]{3,2,1,0:T(8,128)(2,1)}) custom-call(s32[8,4]{1,0:T(8,128)S(1)} %copy.16.mapped, bf16[8,816,128]{2,1,0:T(8,128)(2,1)S(1)} %bitcast.21, bf16[2,1,272,128]{3,2,1,0:T(8,128)(2,1)S(1)} %get-tuple-element.35.refs_0_, ...), custom_call_target="tpu_custom_call" | custom-call | flops 11500000256 | bytes 3342336 | tf_op jit(solution)/shard_map/cut/pallas_call | solution.py:132
  71.5 0.2 collective-permute-start.6
  71.7 4.3 %collective-permute-start.7 = (bf16[2,3,272,128]{3,2,1,0:T(8,128)(2,1)}, bf16[2,3,272,128]{3,2,1,0:T(8,128)(2,1)}, u32[]{:S(2)}, u32[]{:S(2)}) collective-permute-start(bf16[2,3,272,128]{3,2,1,0:T(8,128)(2,1)} %get-tuple-element.43), channel_id=1, source_target_pairs={{0,2},{1,3},{2,0},{3,1},{4,6},{5,7},{6,4},{7,5},{8,10},{9,11},{10,... | collective-permute-start | bytes 1253384 | tf_op jit(solution)/shard_map/ppermute | solution.py:353
  75.9 0.9 collective-permute-start.8
  76.8 6.8 %all-to-all-done.1 = bf16[8,34,16,128]{3,2,1,0:T(8,128)(2,1)S(1)} async-done(((bf16[8,34,16,128]{3,2,1,0:T(8,128)(2,1)}), bf16[8,34,16,128]{3,2,1,0:T(8,128)(2,1)S(1)}, u32[]{:S(2)}, u32[]{:S(2)}) %all-to-all-start.1) | async-done | bytes 1114144 | tf_op jit(solution)/shard_map/all_to_all | solution.py:323
  83.6 5.0 %all-to-all-start = ((bf16[8,34,16,128]{3,2,1,0:T(8,128)(2,1)}), bf16[8,34,16,128]{3,2,1,0:T(8,128)(2,1)S(1)}, u32[]{:S(2)}, u32[]{:S(2)}) async-start(bf16[8,34,16,128]{3,2,1,0:T(8,128)(2,1)} %get-tuple-element.31), calls=%async_computation | async-start | bytes 2228224 | tf_op jit(solution)/shard_map/all_to_all | solution.py:323
  88.6 0.0 collective-permute-done.5.refs_3_
  88.6 0.9 copy-done.10
  89.5 1.7 %cut.6 = (bf16[2,2,272,128]{3,2,1,0:T(8,128)(2,1)S(1)}, bf16[2,2,272,128]{3,2,1,0:T(8,128)(2,1)}, bf16[2,2,272,128]{3,2,1,0:T(8,128)(2,1)}, bf16[2,2,272,128]{3,2,1,0:T(8,128)(2,1)}) custom-call(s32[8,4]{1,0:T(8,128)S(1)} %copy.16.mapped, bf16[8,544,128]{2,1,0:T(8,128)(2,1)S(1)} %bitcast.22, bf16[2,3,272,128]{3,2,1,0:T(8,128)(2,1)S(1)} %get-tuple-element.39.refs_0_, ...), custom_call_target="tpu_custom_call" | custom-call | flops 11500000256 | bytes 2228224 | tf_op jit(solution)/shard_map/cut/pallas_call | solution.py:132
  91.2 0.2 collective-permute-start.13
  91.3 0.0 collective-permute-done.6.refs_1_
  91.3 28.8 %collective-permute-start.14 = (bf16[2,2,272,128]{3,2,1,0:T(8,128)(2,1)}, bf16[2,2,272,128]{3,2,1,0:T(8,128)(2,1)S(1)}, u32[]{:S(2)}, u32[]{:S(2)}) collective-permute-start(bf16[2,2,272,128]{3,2,1,0:T(8,128)(2,1)} %get-tuple-element.50), channel_id=1, source_target_pairs={{0,2},{1,3},{2,0},{3,1},{4,6},{5,7},{6,4},{7,5},{8,10},{9,11},{10,... | collective-permute-start | bytes 835592 | tf_op jit(solution)/shard_map/ppermute | solution.py:353
  120.2 0.0 collective-permute-done.7.refs_2_
  120.2 0.0 collective-permute-start.15
  120.2 0.0 all-to-all-done
  120.2 2.1 %collective-permute-done.8.refs_3_ = bf16[2,3,272,128]{3,2,1,0:T(8,128)(2,1)} collective-permute-done((bf16[2,3,272,128]{3,2,1,0:T(8,128)(2,1)}, bf16[2,3,272,128]{3,2,1,0:T(8,128)(2,1)}, u32[]{:S(2)}, u32[]{:S(2)}) %collective-permute-start.8) | collective-permute-done | bytes 417824 | tf_op jit(solution)/shard_map/ppermute | solution.py:353
  122.3 0.9 cut.7
  123.2 0.1 collective-permute-start.9
  123.3 0.0 collective-permute-done.13.refs_1_
  123.3 4.8 %collective-permute-start.10 = (bf16[2,2,272,128]{3,2,1,0:T(8,128)(2,1)S(1)}, bf16[2,2,272,128]{3,2,1,0:T(8,128)(2,1)S(1)}, u32[]{:S(2)}, u32[]{:S(2)}) collective-permute-start(bf16[2,2,272,128]{3,2,1,0:T(8,128)(2,1)S(1)} %get-tuple-element.47), channel_id=1, source_target_pairs={{0,2},{1,3},{2,0},{3,1},{4,6},{5,7},{6,4},{7,5},{8,10},{9,11},{10,... | collective-permute-start | bytes 835592 | tf_op jit(solution)/shard_map/ppermute | solution.py:353
  128.1 0.0 collective-permute-done.12
  128.1 0.0 collective-permute-start.11
  128.1 1.4 broadcast_select_fusion
  129.5 4.1 %assemble.1.refs_4_ = bf16[8,2,128,512]{3,2,1,0:T(8,128)(2,1)S(1)} custom-call(s32[1]{0:T(128)} %bitcast.me_ref.at, bf16[8,8,2,16,128]{4,3,2,1,0:T(8,128)(2,1)} %get-tuple-element.38.refs_0_, bf16[8,8,2,16,128]{4,3,2,1,0:T(8,128)(2,1)S(1)} %get-tuple-element.62.refs_1_, bf16[8,8,2,16,128]{4,3,2,1,0:T(8,128)(2,1)S(1)} %get-tuple-element.61.refs_2_, ...), custom_call_target="tpu_custom_call" | custom-call | tf_op jit(solution)/shard_map/assemble/pallas_call | solution.py:221
  133.6 3.0 %absorb.4 = (bf16[8,2,4,48,512]{4,3,2,1,0:T(8,128)(2,1)}, bf16[8,2,4,224,512]{4,3,2,1,0:T(8,128)(2,1)}) custom-call(s32[1]{0:T(128)} %bitcast.me_ref.at, bf16[2,1,272,128]{3,2,1,0:T(8,128)(2,1)S(1)} %copy-done.8, bf16[2,1,272,128]{3,2,1,0:T(8,128)(2,1)S(1)} %copy-done.11, bf16[2,1,272,128]{3,2,1,0:T(8,128)(2,1)} %collective-permute-done.1.refs_2_, ...), custom_call_target="tpu_custom_call" | custom-call | flops 285212672 | bytes 2785280 | tf_op jit(solution)/shard_map/absorb/pallas_call | solution.py:264
  136.6 5.2 %absorb.5 = (bf16[8,2,4,48,512]{4,3,2,1,0:T(8,128)(2,1)}, bf16[8,2,4,224,512]{4,3,2,1,0:T(8,128)(2,1)}) custom-call(s32[1]{0:T(128)} %bitcast.me_ref.at, bf16[2,3,272,128]{3,2,1,0:T(8,128)(2,1)S(1)} %get-tuple-element.39.refs_0_, bf16[2,3,272,128]{3,2,1,0:T(8,128)(2,1)S(1)} %collective-permute-done.6.refs_1_, ...), custom_call_target="tpu_custom_call", output_to_operand_aliasing={{0}: (6, {}), {1}: (7, {})} | custom-call | flops 855638016 | bytes 8355840 | tf_op jit(solution)/shard_map/absorb/pallas_call | solution.py:264
  141.8 0.0 collective-permute-done.14.refs_2_
  141.8 7.9 %collective-permute-done.15.refs_3_ = bf16[2,2,272,128]{3,2,1,0:T(8,128)(2,1)} collective-permute-done((bf16[2,2,272,128]{3,2,1,0:T(8,128)(2,1)}, bf16[2,2,272,128]{3,2,1,0:T(8,128)(2,1)}, u32[]{:S(2)}, u32[]{:S(2)}) %collective-permute-start.15) | collective-permute-done | bytes 278560 | tf_op jit(solution)/shard_map/ppermute | solution.py:353
  149.8 3.8 %absorb.6 = (bf16[8,2,4,48,512]{4,3,2,1,0:T(8,128)(2,1)}, bf16[8,2,4,224,512]{4,3,2,1,0:T(8,128)(2,1)}) custom-call(s32[1]{0:T(128)} %bitcast.me_ref.at, bf16[2,2,272,128]{3,2,1,0:T(8,128)(2,1)S(1)} %get-tuple-element.41.refs_0_, bf16[2,2,272,128]{3,2,1,0:T(8,128)(2,1)S(1)} %collective-permute-done.13.refs_1_, ...), custom_call_target="tpu_custom_call", output_to_operand_aliasing={{0}: (6, {}), {1}: (7, {})} | custom-call | flops 570425344 | bytes 5570560 | tf_op jit(solution)/shard_map/absorb/pallas_call | solution.py:264
  153.5 0.4 collective-permute-done.9.refs_1_
  153.9 5.9 %collective-permute-done.10.refs_2_ = bf16[2,2,272,128]{3,2,1,0:T(8,128)(2,1)S(1)} collective-permute-done((bf16[2,2,272,128]{3,2,1,0:T(8,128)(2,1)S(1)}, bf16[2,2,272,128]{3,2,1,0:T(8,128)(2,1)S(1)}, u32[]{:S(2)}, u32[]{:S(2)}) %collective-permute-start.10) | collective-permute-done | bytes 278560 | tf_op jit(solution)/shard_map/ppermute | solution.py:353
  159.8 0.0 collective-permute-done.11.refs_3_
  159.8 3.0 %absorb.7 = (bf16[8,2,4,48,512]{4,3,2,1,0:T(8,128)(2,1)}, bf16[8,2,4,224,512]{4,3,2,1,0:T(8,128)(2,1)}) custom-call(s32[1]{0:T(128)} %bitcast.me_ref.at, bf16[2,2,272,128]{3,2,1,0:T(8,128)(2,1)S(1)} %get-tuple-element.45.refs_0_, bf16[2,2,272,128]{3,2,1,0:T(8,128)(2,1)S(1)} %collective-permute-done.9.refs_1_, ...), custom_call_target="tpu_custom_call", output_to_operand_aliasing={{0}: (6, {}), {1}: (7, {})} | custom-call | flops 570425344 | bytes 5570560 | tf_op jit(solution)/shard_map/absorb/pallas_call | solution.py:264
  (28 shorter events, 0.1 us)
Async XLA Ops:
  1.4 3.1 %copy-start.12 = (s32[2,32]{1,0:T(2,128)S(1)}, s32[2,32]{1,0:T(2,128)}, u32[]{:S(2)}) copy-start(s32[2,32]{1,0:T(2,128)} %owners.1) | copy-start | bytes 772
  4.6 9.3 %copy-start.17 = (s32[8,4]{0,1:T(4,128)S(1)}, s32[8,4]{0,1:T(4,128)}, u32[]{:S(2)}) copy-start(s32[8,4]{0,1:T(4,128)} %param.7) | copy-start | bytes 388
  8.5 1.0 copy-start.6
  9.5 18.5 %all-to-all-start.3 = ((bf16[8,33,16,128]{3,2,1,0:T(8,128)(2,1)}), bf16[8,33,16,128]{3,2,1,0:T(8,128)(2,1)S(1)}, u32[]{:S(2)}, u32[]{:S(2)}) async-start(bf16[8,33,16,128]{3,2,1,0:T(8,128)(2,1)} %get-tuple-element.34), calls=%async_computation.3 | async-start | bytes 2162688 | tf_op jit(solution)/shard_map/all_to_all | solution.py:323
  29.5 1.3 copy-start.13
  29.5 6.9 %copy-start.15 = (bf16[2,1,272,128]{3,2,1,0:T(8,128)(2,1)}, bf16[2,1,272,128]{3,2,1,0:T(8,128)(2,1)S(1)}, u32[]{:S(2)}) copy-start(bf16[2,1,272,128]{3,2,1,0:T(8,128)(2,1)S(1)} %get-tuple-element.36) | copy-start | bytes 417796
  29.5 13.9 %copy-start.14 = (bf16[2,1,272,128]{3,2,1,0:T(8,128)(2,1)}, bf16[2,1,272,128]{3,2,1,0:T(8,128)(2,1)S(1)}, u32[]{:S(2)}) copy-start(bf16[2,1,272,128]{3,2,1,0:T(8,128)(2,1)S(1)} %get-tuple-element.37) | copy-start | bytes 417796
  29.5 39.5 %copy-start.7 = (bf16[2,1,272,128]{3,2,1,0:T(8,128)(2,1)}, bf16[2,1,272,128]{3,2,1,0:T(8,128)(2,1)S(1)}, u32[]{:S(2)}) copy-start(bf16[2,1,272,128]{3,2,1,0:T(8,128)(2,1)S(1)} %get-tuple-element.35.refs_0_) | copy-start | bytes 417796
  29.5 18.3 %collective-permute-start.4 = (bf16[8,8,2,16,128]{4,3,2,1,0:T(8,128)(2,1)}, bf16[8,8,2,16,128]{4,3,2,1,0:T(8,128)(2,1)S(1)}, u32[]{:S(2)}, u32[]{:S(2)}) collective-permute-start(bf16[8,8,2,16,128]{4,3,2,1,0:T(8,128)(2,1)} %get-tuple-element.38.refs_0_), channel_id=1, source_target_pairs={{0,2},{3,1},{4,6},{7,5},{8,10},{11,9},{12,14},{15,13},{16,18},{19,... | collective-permute-start | bytes 1572872 | tf_op jit(solution)/shard_map/ppermute | solution.py:345
  30.8 27.8 %collective-permute-start.3 = (bf16[8,8,2,16,128]{4,3,2,1,0:T(8,128)(2,1)}, bf16[8,8,2,16,128]{4,3,2,1,0:T(8,128)(2,1)S(1)}, u32[]{:S(2)}, u32[]{:S(2)}) collective-permute-start(bf16[8,8,2,16,128]{4,3,2,1,0:T(8,128)(2,1)} %get-tuple-element.38.refs_0_), channel_id=1, source_target_pairs={{1,0},{2,1},{3,2},{5,4},{6,5},{7,6},{9,8},{10,9},{11,10},{13,12},{... | collective-permute-start | bytes 1572872 | tf_op jit(solution)/shard_map/ppermute | solution.py:168
  36.4 22.3 %collective-permute-start.2 = (bf16[8,8,2,16,128]{4,3,2,1,0:T(8,128)(2,1)}, bf16[8,8,2,16,128]{4,3,2,1,0:T(8,128)(2,1)S(1)}, u32[]{:S(2)}, u32[]{:S(2)}) collective-permute-start(bf16[8,8,2,16,128]{4,3,2,1,0:T(8,128)(2,1)} %get-tuple-element.38.refs_0_), channel_id=1, source_target_pairs={{0,1},{1,2},{2,3},{4,5},{5,6},{6,7},{8,9},{9,10},{10,11},{12,13},{... | collective-permute-start | bytes 1572872 | tf_op jit(solution)/shard_map/ppermute | solution.py:167
  38.4 25.6 %all-to-all-start.2 = ((bf16[8,51,16,128]{3,2,1,0:T(8,128)(2,1)}), bf16[8,51,16,128]{3,2,1,0:T(8,128)(2,1)S(1)}, u32[]{:S(2)}, u32[]{:S(2)}) async-start(bf16[8,51,16,128]{3,2,1,0:T(8,128)(2,1)} %get-tuple-element.33), calls=%async_computation.2 | async-start | bytes 3342336 | tf_op jit(solution)/shard_map/all_to_all | solution.py:323
  43.4 25.6 %collective-permute-start = (bf16[2,1,272,128]{3,2,1,0:T(8,128)(2,1)}, bf16[2,1,272,128]{3,2,1,0:T(8,128)(2,1)S(1)}, u32[]{:S(2)}, u32[]{:S(2)}) collective-permute-start(bf16[2,1,272,128]{3,2,1,0:T(8,128)(2,1)} %copy-done.15), channel_id=1, source_target_pairs={{0,1},{1,2},{2,3},{3,0},{4,5},{5,6},{6,7},{7,4},{8,9},{9,10},{10,1... | collective-permute-start | bytes 417800 | tf_op jit(solution)/shard_map/ppermute | solution.py:353
  43.4 25.6 %collective-permute-start.1 = (bf16[2,1,272,128]{3,2,1,0:T(8,128)(2,1)}, bf16[2,1,272,128]{3,2,1,0:T(8,128)(2,1)}, u32[]{:S(2)}, u32[]{:S(2)}) collective-permute-start(bf16[2,1,272,128]{3,2,1,0:T(8,128)(2,1)} %copy-done.14), channel_id=1, source_target_pairs={{0,2},{1,3},{2,0},{3,1},{4,6},{5,7},{6,4},{7,5},{8,10},{9,11},{10,... | collective-permute-start | bytes 417800 | tf_op jit(solution)/shard_map/ppermute | solution.py:353
  47.8 14.5 %copy-start = (bf16[8,8,2,16,128]{4,3,2,1,0:T(8,128)(2,1)}, bf16[8,8,2,16,128]{4,3,2,1,0:T(8,128)(2,1)S(1)}, u32[]{:S(2)}) copy-start(bf16[8,8,2,16,128]{4,3,2,1,0:T(8,128)(2,1)S(1)} %collective-permute-done.4.refs_2_.first) | copy-start | bytes 1572868
  47.8 40.8 %collective-permute-start.5 = (bf16[2,1,272,128]{3,2,1,0:T(8,128)(2,1)}, bf16[2,1,272,128]{3,2,1,0:T(8,128)(2,1)}, u32[]{:S(2)}, u32[]{:S(2)}) collective-permute-start(bf16[2,1,272,128]{3,2,1,0:T(8,128)(2,1)} %copy-done.13), channel_id=1, source_target_pairs={{0,3},{1,0},{2,1},{3,2},{4,7},{5,4},{6,5},{7,6},{8,11},{9,8},{10,9... | collective-permute-start | bytes 417800 | tf_op jit(solution)/shard_map/ppermute | solution.py:353
  58.6 3.7 %copy-start.2 = (bf16[8,8,2,16,128]{4,3,2,1,0:T(8,128)(2,1)}, bf16[8,8,2,16,128]{4,3,2,1,0:T(8,128)(2,1)S(1)}, u32[]{:S(2)}) copy-start(bf16[8,8,2,16,128]{4,3,2,1,0:T(8,128)(2,1)S(1)} %collective-permute-done.3.refs_1_.below) | copy-start | bytes 1572868
  58.7 3.6 %copy-start.4 = (bf16[8,8,2,16,128]{4,3,2,1,0:T(8,128)(2,1)}, bf16[8,8,2,16,128]{4,3,2,1,0:T(8,128)(2,1)S(1)}, u32[]{:S(2)}) copy-start(bf16[8,8,2,16,128]{4,3,2,1,0:T(8,128)(2,1)S(1)} %collective-permute-done.2.refs_0_.above) | copy-start | bytes 1572868
  59.9 68.2 %collective-permute-start.12 = (bf16[2,8,8,2,16,128]{5,4,3,2,1,0:T(8,128)(2,1)}, bf16[2,8,8,2,16,128]{5,4,3,2,1,0:T(8,128)(2,1)}, u32[]{:S(2)}, u32[]{:S(2)}) collective-permute-start(bf16[2,8,8,2,16,128]{5,4,3,2,1,0:T(8,128)(2,1)} %pass_on.1.refs_4_), channel_id=1, source_target_pairs={{1,0},{2,3},{5,4},{6,7},{9,8},{10,11},{13,12},{14,15},{17,16},{18,... | collective-permute-start | bytes 3145736 | tf_op jit(solution)/shard_map/ppermute | solution.py:348
  64.0 19.6 %all-to-all-start.1 = ((bf16[8,34,16,128]{3,2,1,0:T(8,128)(2,1)}), bf16[8,34,16,128]{3,2,1,0:T(8,128)(2,1)S(1)}, u32[]{:S(2)}, u32[]{:S(2)}) async-start(bf16[8,34,16,128]{3,2,1,0:T(8,128)(2,1)} %copy-done.6), calls=%async_computation.1 | async-start | bytes 2228224 | tf_op jit(solution)/shard_map/all_to_all | solution.py:323
  69.0 2.6 %copy-start.9 = (bf16[2,1,272,128]{3,2,1,0:T(8,128)(2,1)}, bf16[2,1,272,128]{3,2,1,0:T(8,128)(2,1)S(1)}, u32[]{:S(2)}) copy-start(bf16[2,1,272,128]{3,2,1,0:T(8,128)(2,1)S(1)} %collective-permute-done.refs_1_) | copy-start | bytes 417796
  69.0 0.7 copy-start.16
  71.5 19.8 %collective-permute-start.6 = (bf16[2,3,272,128]{3,2,1,0:T(8,128)(2,1)}, bf16[2,3,272,128]{3,2,1,0:T(8,128)(2,1)S(1)}, u32[]{:S(2)}, u32[]{:S(2)}) collective-permute-start(bf16[2,3,272,128]{3,2,1,0:T(8,128)(2,1)} %get-tuple-element.42), channel_id=1, source_target_pairs={{0,1},{1,2},{2,3},{3,0},{4,5},{5,6},{6,7},{7,4},{8,9},{9,10},{10,1... | collective-permute-start | bytes 1253384 | tf_op jit(solution)/shard_map/ppermute | solution.py:353
  71.7 48.5 %collective-permute-start.7 = (bf16[2,3,272,128]{3,2,1,0:T(8,128)(2,1)}, bf16[2,3,272,128]{3,2,1,0:T(8,128)(2,1)}, u32[]{:S(2)}, u32[]{:S(2)}) collective-permute-start(bf16[2,3,272,128]{3,2,1,0:T(8,128)(2,1)} %get-tuple-element.43), channel_id=1, source_target_pairs={{0,2},{1,3},{2,0},{3,1},{4,6},{5,7},{6,4},{7,5},{8,10},{9,11},{10,... | collective-permute-start | bytes 1253384 | tf_op jit(solution)/shard_map/ppermute | solution.py:353
  75.9 46.3 %collective-permute-start.8 = (bf16[2,3,272,128]{3,2,1,0:T(8,128)(2,1)}, bf16[2,3,272,128]{3,2,1,0:T(8,128)(2,1)}, u32[]{:S(2)}, u32[]{:S(2)}) collective-permute-start(bf16[2,3,272,128]{3,2,1,0:T(8,128)(2,1)} %get-tuple-element.44), channel_id=1, source_target_pairs={{0,3},{1,0},{2,1},{3,2},{4,7},{5,4},{6,5},{7,6},{8,11},{9,8},{10,9... | collective-permute-start | bytes 1253384 | tf_op jit(solution)/shard_map/ppermute | solution.py:353
  83.6 36.6 %all-to-all-start = ((bf16[8,34,16,128]{3,2,1,0:T(8,128)(2,1)}), bf16[8,34,16,128]{3,2,1,0:T(8,128)(2,1)S(1)}, u32[]{:S(2)}, u32[]{:S(2)}) async-start(bf16[8,34,16,128]{3,2,1,0:T(8,128)(2,1)} %get-tuple-element.31), calls=%async_computation | async-start | bytes 2228224 | tf_op jit(solution)/shard_map/all_to_all | solution.py:323
  88.6 0.9 copy-start.10
  91.2 32.1 %collective-permute-start.13 = (bf16[2,2,272,128]{3,2,1,0:T(8,128)(2,1)}, bf16[2,2,272,128]{3,2,1,0:T(8,128)(2,1)S(1)}, u32[]{:S(2)}, u32[]{:S(2)}) collective-permute-start(bf16[2,2,272,128]{3,2,1,0:T(8,128)(2,1)} %get-tuple-element.49), channel_id=1, source_target_pairs={{0,1},{1,2},{2,3},{3,0},{4,5},{5,6},{6,7},{7,4},{8,9},{9,10},{10,1... | collective-permute-start | bytes 835592 | tf_op jit(solution)/shard_map/ppermute | solution.py:353
  91.3 50.5 %collective-permute-start.14 = (bf16[2,2,272,128]{3,2,1,0:T(8,128)(2,1)}, bf16[2,2,272,128]{3,2,1,0:T(8,128)(2,1)S(1)}, u32[]{:S(2)}, u32[]{:S(2)}) collective-permute-start(bf16[2,2,272,128]{3,2,1,0:T(8,128)(2,1)} %get-tuple-element.50), channel_id=1, source_target_pairs={{0,2},{1,3},{2,0},{3,1},{4,6},{5,7},{6,4},{7,5},{8,10},{9,11},{10,... | collective-permute-start | bytes 835592 | tf_op jit(solution)/shard_map/ppermute | solution.py:353
  120.2 29.6 %collective-permute-start.15 = (bf16[2,2,272,128]{3,2,1,0:T(8,128)(2,1)}, bf16[2,2,272,128]{3,2,1,0:T(8,128)(2,1)}, u32[]{:S(2)}, u32[]{:S(2)}) collective-permute-start(bf16[2,2,272,128]{3,2,1,0:T(8,128)(2,1)} %get-tuple-element.51), channel_id=1, source_target_pairs={{0,3},{1,0},{2,1},{3,2},{4,7},{5,4},{6,5},{7,6},{8,11},{9,8},{10,9... | collective-permute-start | bytes 835592 | tf_op jit(solution)/shard_map/ppermute | solution.py:353
  122.3 5.8 %copy-start.1 = (bf16[8,8,2,16,128]{4,3,2,1,0:T(8,128)(2,1)S(1)}, bf16[8,8,2,16,128]{4,3,2,1,0:T(8,128)(2,1)}, u32[]{:S(2)}) copy-start(bf16[8,8,2,16,128]{4,3,2,1,0:T(8,128)(2,1)} %copy-done) | copy-start | bytes 1572868
  122.3 5.8 %copy-start.3 = (bf16[8,8,2,16,128]{4,3,2,1,0:T(8,128)(2,1)S(1)}, bf16[8,8,2,16,128]{4,3,2,1,0:T(8,128)(2,1)}, u32[]{:S(2)}) copy-start(bf16[8,8,2,16,128]{4,3,2,1,0:T(8,128)(2,1)} %copy-done.2) | copy-start | bytes 1572868
  122.3 5.8 %copy-start.5 = (bf16[8,8,2,16,128]{4,3,2,1,0:T(8,128)(2,1)S(1)}, bf16[8,8,2,16,128]{4,3,2,1,0:T(8,128)(2,1)}, u32[]{:S(2)}) copy-start(bf16[8,8,2,16,128]{4,3,2,1,0:T(8,128)(2,1)} %copy-done.4) | copy-start | bytes 1572868
  123.2 30.7 %collective-permute-start.9 = (bf16[2,2,272,128]{3,2,1,0:T(8,128)(2,1)S(1)}, bf16[2,2,272,128]{3,2,1,0:T(8,128)(2,1)S(1)}, u32[]{:S(2)}, u32[]{:S(2)}) collective-permute-start(bf16[2,2,272,128]{3,2,1,0:T(8,128)(2,1)S(1)} %get-tuple-element.46), channel_id=1, source_target_pairs={{0,1},{1,2},{2,3},{3,0},{4,5},{5,6},{6,7},{7,4},{8,9},{9,10},{10,1... | collective-permute-start | bytes 835592 | tf_op jit(solution)/shard_map/ppermute | solution.py:353
  123.3 36.5 %collective-permute-start.10 = (bf16[2,2,272,128]{3,2,1,0:T(8,128)(2,1)S(1)}, bf16[2,2,272,128]{3,2,1,0:T(8,128)(2,1)S(1)}, u32[]{:S(2)}, u32[]{:S(2)}) collective-permute-start(bf16[2,2,272,128]{3,2,1,0:T(8,128)(2,1)S(1)} %get-tuple-element.47), channel_id=1, source_target_pairs={{0,2},{1,3},{2,0},{3,1},{4,6},{5,7},{6,4},{7,5},{8,10},{9,11},{10,... | collective-permute-start | bytes 835592 | tf_op jit(solution)/shard_map/ppermute | solution.py:353
  128.1 31.7 %collective-permute-start.11 = (bf16[2,2,272,128]{3,2,1,0:T(8,128)(2,1)S(1)}, bf16[2,2,272,128]{3,2,1,0:T(8,128)(2,1)S(1)}, u32[]{:S(2)}, u32[]{:S(2)}) collective-permute-start(bf16[2,2,272,128]{3,2,1,0:T(8,128)(2,1)S(1)} %get-tuple-element.48), channel_id=1, source_target_pairs={{0,3},{1,0},{2,1},{3,2},{4,7},{5,4},{6,5},{7,6},{8,11},{9,8},{10,9... | collective-permute-start | bytes 835592 | tf_op jit(solution)/shard_map/ppermute | solution.py:353
  129.5 4.1 %copy-start.8 = (bf16[2,1,272,128]{3,2,1,0:T(8,128)(2,1)S(1)}, bf16[2,1,272,128]{3,2,1,0:T(8,128)(2,1)}, u32[]{:S(2)}) copy-start(bf16[2,1,272,128]{3,2,1,0:T(8,128)(2,1)} %copy-done.7) | copy-start | bytes 417796
  129.5 4.1 %copy-start.11 = (bf16[2,1,272,128]{3,2,1,0:T(8,128)(2,1)S(1)}, bf16[2,1,272,128]{3,2,1,0:T(8,128)(2,1)}, u32[]{:S(2)}) copy-start(bf16[2,1,272,128]{3,2,1,0:T(8,128)(2,1)} %copy-done.9) | copy-start | bytes 417796

commit v11 on v10

--- a/solution.py
+++ b/solution.py
@@ -15,9 +15,10 @@
 V_DIM = 128
 LANES = 128
 QUERY, KEY, VALUE, OUT = range(4)
-CUT_MICROS = 10
-TOKEN_MICROS = 20
+CUT_MICROS = 30
+TOKEN_MICROS = 6
 CUTS = (0, 1, 4, 6, 8)
+GROUPS = (0, 1, 2, 4)
 VMEM_LIMIT = 16 * 1024 * 1024
 
 
@@ -105,17 +106,15 @@
     return pl.BlockSpec(corner_of(x), lambda _: (0,) * x.ndim)
 
 
-def cut(rows, slice_map, blocks, ahead, item_rows, waits, micros):
+def cut(rows, slice_map, blocks, ahead, first, items, item_rows, waits, micros):
     t_ways = slice_map.shape[1]
-    first = math.prod(ahead)
-    items = (rows.shape[1] - first) // item_rows
-    shapes = [(rows.shape[0],) + ahead + rows.shape[2:]] if first else []
+    shapes = [(rows.shape[0],) + ahead + rows.shape[2:]] if ahead else []
     shapes += [(blocks, items, item_rows) + rows.shape[2:]] * t_ways
 
     def kernel(mapped, source, *refs):
         f_me, t_me = lax.axis_index("fsdp"), lax.axis_index("tp")
         refs = refs[len(waits) :]
-        if first:
+        if ahead:
             for f in range(rows.shape[0]):
                 for item in range(ahead[0]):
                     for kind in range(ahead[1]):
@@ -169,33 +168,28 @@
     )
 
 
-def pass_on(me, across, up, down, waits):
-    def kernel(me_ref, first, above, below, *refs):
-        out = refs[-1]
-        out[0] = first[...]
-
-        @pl.when(me_ref[0] == 2)
-        def _():
-            out[1] = above[...]
-
-        @pl.when(me_ref[0] != 2)
-        def _():
-            out[1] = below[...]
-
-    whole = pl.BlockSpec(across.shape, lambda _, me_ref: (0,) * across.ndim)
-    corners = [pl.BlockSpec(corner_of(x), lambda _, me_ref, n=x.ndim: (0,) * n) for x in waits]
+def pass_on(me, own, up, down):
+    def kernel(me_ref, own_ref, up_ref, down_ref, out):
+        for source, mine in (
+            (own_ref, jnp.logical_or(me_ref[0] == 0, me_ref[0] == 3)),
+            (up_ref, me_ref[0] == 2),
+            (down_ref, me_ref[0] == 1),
+        ):
+
+            @pl.when(mine)
+            def _():
+                out[...] = source[...]
+
+    whole = pl.BlockSpec(own.shape, lambda _, me_ref: (0,) * own.ndim)
     return pl.pallas_call(
         kernel,
         grid_spec=pltpu.PrefetchScalarGridSpec(
-            num_scalar_prefetch=1,
-            grid=(1,),
-            in_specs=[whole] * 3 + corners,
-            out_specs=pl.BlockSpec((2,) + across.shape, lambda _, me_ref: (0,) * (across.ndim + 1)),
-        ),
-        out_shape=jax.ShapeDtypeStruct((2,) + across.shape, across.dtype),
+            num_scalar_prefetch=1, grid=(1,), in_specs=[whole] * 3, out_specs=whole
+        ),
+        out_shape=jax.ShapeDtypeStruct(own.shape, own.dtype),
         compiler_params=pltpu.CompilerParams(vmem_limit_bytes=VMEM_LIMIT),
         name="pass_on",
-    )(me.reshape(1), across, up, down, *waits)
+    )(me.reshape(1), own, up, down)
 
 
 def assemble(me, spread_parts):
@@ -316,36 +310,60 @@
     cuts = [item_count * eighths // 8 for eighths in CUTS]
     chunks = [range(low, high) for low, high in zip(cuts, cuts[1:]) if low < high]
 
-    def packed(parts):
-        return pack(table, param_offsets, owner_map, f_ways, widths, granule, parts)
-
     def over_fsdp(x):
         x = lax.all_to_all(x, "fsdp", split_axis=0, concat_axis=0, tiled=True)
         return x.reshape(f_ways, -1, LANES)
 
-    first_parts = [[(range(item_count), (KEY, VALUE)), (chunks[0], (QUERY, OUT))]]
-    other_parts = [[(items, (QUERY, OUT))] for items in chunks[1:]]
-    to_send = packed(first_parts + other_parts)
+    groups = [chunks[low:high] for low, high in zip(GROUPS, GROUPS[1:]) if chunks[low:high]]
+    to_send = pack(
+        table,
+        param_offsets,
+        owner_map,
+        f_ways,
+        widths,
+        granule,
+        [
+            ([] if at else [(range(item_count), (KEY, VALUE))])
+            + [(items, (QUERY, OUT)) for items in group]
+            for at, group in enumerate(groups)
+        ],
+    )
 
     exchanged, sent = [], []
     for at in range(len(chunks)):
-        rows = over_fsdp(to_send[at])
+        group = [at in range(low, high) for low, high in zip(GROUPS, GROUPS[1:])].index(True)
+        if at == GROUPS[group]:
+            rows, first = over_fsdp(to_send[group]), 0 if at else math.prod(ahead)
         waits = sent[at - 1][:1] if at else []
         if at >= 2:
             waits = waits + exchanged[at - 2][1:]
         if at == 1:
             waits = waits + exchanged[0][1:3]
         if t_ways == 4 and at == 1:
-            waits = waits + [near, passed]
-        pieces = list(cut(rows, slice_map, blocks, ahead if at == 0 else (0,), item_rows, waits, CUT_MICROS))
+            waits = waits + [near]
+        pieces = list(
+            cut(
+                rows,
+                slice_map,
+                blocks,
+                () if at else ahead,
+                first,
+                len(chunks[at]),
+                item_rows,
+                waits,
+                CUT_MICROS,
+            )
+        )
+        first += len(chunks[at]) * item_rows
         if at == 0:
             pairs = pieces.pop(0)
             up, down = neighbours(pairs, "tp", t_ways)
             if t_ways == 4:
-                across = lax.ppermute(pairs, "tp", [(0, 2), (3, 1)])
-                near = token([up, down, across], TOKEN_MICROS)
-                passed = pass_on(me, across, up, down, [])
-                far = lax.ppermute(passed, "tp", [(1, 0), (2, 3)])
+                second = lax.ppermute(
+                    pass_on(me, pairs, up, down), "tp", [(0, 2), (1, 0), (2, 3), (3, 1)]
+                )
+                third = lax.ppermute(second, "tp", [(1, 0), (2, 3)])
+                near = token([up, down, second], TOKEN_MICROS)
         sent.append(pieces)
         exchanged.append(
             pieces[:1]
@@ -357,12 +375,11 @@
         )
 
     if t_ways == 4:
-        ends = jnp.logical_or(me == 0, me == 3)
         spread = [
             pairs,
-            jnp.where(me == 0, far[0], up),
-            jnp.where(ends, far[1], across),
-            jnp.where(me == 3, far[0], down),
+            jnp.where(me == 0, third, up),
+            second,
+            jnp.where(me == 3, third, down),
         ]
     else:
         ups, downs = [pairs, up], [pairs, down]

time: 165 us -> 173 us (1.048)
  waiting for transfers between devices: 48.5 us -> 93.7 us
  starting transfers between devices: 74.1 us -> 38.9 us
  Pallas kernels: 31.3 us -> 29.2 us
  local copies, waits for them, and re-layouts: 6.65 us -> 8.59 us
    ppermute x2, waiting for transfers between devices: 0.01 us -> 27.9 us  [the longest x1 17.2 us: per_device(): third = lax.ppermute(second, 'tp', [(1, 0), (2, 3)])]
    ppermute x12, starting transfers between devices: 43.6 us -> 18.9 us  [per_device(): lax.ppermute(piece, 'tp', [(i, (i + shift) % t_ways) for i in range(t_way...]
    ppermute x12, waiting for transfers between devices: 16.3 us -> 29.8 us  [per_device(): lax.ppermute(piece, 'tp', [(i, (i + shift) % t_ways) for i in range(t_way...]
    all_to_all x4 -> x3, waiting for transfers between devices: 21.3 us -> 29 us  [over_fsdp(): x = lax.all_to_all(x, 'fsdp', split_axis=0, concat_axis=0, tiled=True)]
    all_to_all x4 -> x3, starting transfers between devices: 19.3 us -> 12.8 us  [over_fsdp(): x = lax.all_to_all(x, 'fsdp', split_axis=0, concat_axis=0, tiled=True)]
    ppermute x1, waiting for transfers between devices: 10.8 us -> 4.91 us  [neighbours(): lax.ppermute(x, axis, [(i + 1, i) for i in range(ways - 1)])]
    ppermute x1, starting transfers between devices: 5.59 us -> 2.35 us  [neighbours(): lax.ppermute(x, axis, [(i + 1, i) for i in range(ways - 1)])]
    ppermute x2, starting transfers between devices: 3.76 us -> 1.31 us  [the longest x1 1.31 us: per_device(): third = lax.ppermute(second, 'tp', [(1, 0), (2, 3)])]
  transfers between devices with their start and end apart: 20 -> 19, of which waited for: 9 -> 9; matrix products, arithmetic and copies ran while one was open for 1% -> 0% of each run, Pallas kernels for 14% -> 12%
where the time goes in v11:
time: 173 us; the launch traced here: 171 us
  waiting for transfers between devices  93.7 us (54%)
  starting transfers between devices  38.9 us (22%)
  Pallas kernels  29.2 us (17%)
  local copies, waits for them, and re-layouts  8.59 us (5%)
    ppermute x12, waiting for transfers between devices, per_device(): lax.ppermute(piece, 'tp', [(i, (i + shift) % t_ways) for i in range(t_way...  29.8 us
    all_to_all x3, waiting for transfers between devices, over_fsdp(): x = lax.all_to_all(x, 'fsdp', split_axis=0, concat_axis=0, tiled=True)  29 us
    ppermute x12, starting transfers between devices, per_device(): lax.ppermute(piece, 'tp', [(i, (i + shift) % t_ways) for i in range(t_way...  18.9 us
    ppermute x1, waiting for transfers between devices, per_device(): third = lax.ppermute(second, 'tp', [(1, 0), (2, 3)])  17.2 us
    pallas_call x4, Pallas kernels, absorb(): pl.pallas_call(kernel, grid_spec=pltpu.PrefetchScalarGridSpec(num_scalar_...  14.5 us
    all_to_all x3, starting transfers between devices, over_fsdp(): x = lax.all_to_all(x, 'fsdp', split_axis=0, concat_axis=0, tiled=True)  12.8 us
    ppermute x1, waiting for transfers between devices, per_device(): lax.ppermute(pass_on(me, pairs, up, down), 'tp', [(0, 2), (1, 0), (2, 3),...  10.8 us
    unnamed x31, local copies, waits for them, and re-layouts  8.59 us
  transfers between devices with their start and end apart: 19, of which 9 were waited for; matrix products, arithmetic and copies ran while one was open for 0% of the time, Pallas kernels for 12%

profile of v11, /device:TPU:10, one launch (start us, length us, event | category | flops | bytes accessed | tf_op | source)
XLA Modules:
  0.0 171.3 jit_solution(14621210865279200889)
XLA Ops:
  0.6 0.8 copy.12.offsets
  1.4 3.1 %copy.17 = bf16[1,2,9728,128]{3,2,1,0:T(8,128)(2,1)S(1)} copy(bf16[1,2,9728,128]{3,1,2,0:T(2,128)(2,1)} %bitcast.16) | data formatting | bytes 9961472
  4.6 0.0 copy-start.13
  4.6 4.4 %pack.1 = (bf16[8,33,16,128]{3,2,1,0:T(8,128)(2,1)}, bf16[8,51,16,128]{3,2,1,0:T(8,128)(2,1)}, bf16[8,68,16,128]{3,2,1,0:T(8,128)(2,1)}) custom-call(s32[2,32,4]{2,1,0:T(8,128)S(1)} %copy.12.offsets, s32[2,32]{1,0:T(2,128)S(1)} %copy-done.8, bf16[2,608,16,128]{3,2,1,0:T(8,128)(2,1)S(1)} %bitcast.9), custom_call_target="tpu_custom_call" | custom-call | bytes 9961472 | tf_op jit(solution)/shard_map/pack/pallas_call | solution.py:78
  9.0 4.3 %all-to-all-start.2 = ((bf16[8,33,16,128]{3,2,1,0:T(8,128)(2,1)}), bf16[8,33,16,128]{3,2,1,0:T(8,128)(2,1)S(1)}, u32[]{:S(2)}, u32[]{:S(2)}) async-start(bf16[8,33,16,128]{3,2,1,0:T(8,128)(2,1)} %get-tuple-element.32), calls=%async_computation.2 | async-start | bytes 2162688 | tf_op jit(solution)/shard_map/all_to_all | solution.py:314
  13.2 0.0 copy-done.13
  13.2 0.1 copy.16.mapped
  13.3 14.2 %all-to-all-done.2 = bf16[8,33,16,128]{3,2,1,0:T(8,128)(2,1)S(1)} async-done(((bf16[8,33,16,128]{3,2,1,0:T(8,128)(2,1)}), bf16[8,33,16,128]{3,2,1,0:T(8,128)(2,1)S(1)}, u32[]{:S(2)}, u32[]{:S(2)}) %all-to-all-start.2) | async-done | bytes 1081376 | tf_op jit(solution)/shard_map/all_to_all | solution.py:314
  27.5 0.7 cut.4
  28.2 0.6 copy-done.9
  28.8 0.6 copy-done.10
  29.5 0.7 copy-done.11
  30.2 2.3 %collective-permute-start.3 = (bf16[8,8,2,16,128]{4,3,2,1,0:T(8,128)(2,1)S(1)}, bf16[8,8,2,16,128]{4,3,2,1,0:T(8,128)(2,1)S(1)}, u32[]{:S(2)}, u32[]{:S(2)}) collective-permute-start(bf16[8,8,2,16,128]{4,3,2,1,0:T(8,128)(2,1)S(1)} %get-tuple-element.36.own_ref.refs_0_), channel_id=1, source_target_pairs={{1,0},{2,1},{3,2},{5,4},{6,5},{7,6},{9,8},{10,9},{11,10},{13,12},{... | collective-permute-start | bytes 1572872 | tf_op jit(solution)/shard_map/ppermute | solution.py:167
  32.5 3.5 %collective-permute-start.2 = (bf16[8,8,2,16,128]{4,3,2,1,0:T(8,128)(2,1)S(1)}, bf16[8,8,2,16,128]{4,3,2,1,0:T(8,128)(2,1)S(1)}, u32[]{:S(2)}, u32[]{:S(2)}) collective-permute-start(bf16[8,8,2,16,128]{4,3,2,1,0:T(8,128)(2,1)S(1)} %get-tuple-element.36.own_ref.refs_0_), channel_id=1, source_target_pairs={{0,1},{1,2},{2,3},{4,5},{5,6},{6,7},{8,9},{9,10},{10,11},{12,13},{... | collective-permute-start | bytes 1572872 | tf_op jit(solution)/shard_map/ppermute | solution.py:166
  36.0 5.0 %all-to-all-start.1 = ((bf16[8,51,16,128]{3,2,1,0:T(8,128)(2,1)}), bf16[8,51,16,128]{3,2,1,0:T(8,128)(2,1)S(1)}, u32[]{:S(2)}, u32[]{:S(2)}) async-start(bf16[8,51,16,128]{3,2,1,0:T(8,128)(2,1)} %get-tuple-element.31), calls=%async_computation.1 | async-start | bytes 3342336 | tf_op jit(solution)/shard_map/all_to_all | solution.py:314
  41.0 4.9 %collective-permute-done.3.down_ref.refs_1_ = bf16[8,8,2,16,128]{4,3,2,1,0:T(8,128)(2,1)S(1)} collective-permute-done((bf16[8,8,2,16,128]{4,3,2,1,0:T(8,128)(2,1)S(1)}, bf16[8,8,2,16,128]{4,3,2,1,0:T(8,128)(2,1)S(1)}, u32[]{:S(2)}, u32[]{:S(2)}) %collective-permute-start.3) | collective-permute-done | bytes 524320 | tf_op jit(solution)/shard_map/ppermute | solution.py:167
  45.9 2.1 %collective-permute-done.2.up_ref.refs_0_ = bf16[8,8,2,16,128]{4,3,2,1,0:T(8,128)(2,1)S(1)} collective-permute-done((bf16[8,8,2,16,128]{4,3,2,1,0:T(8,128)(2,1)S(1)}, bf16[8,8,2,16,128]{4,3,2,1,0:T(8,128)(2,1)S(1)}, u32[]{:S(2)}, u32[]{:S(2)}) %collective-permute-start.2) | collective-permute-done | bytes 524320 | tf_op jit(solution)/shard_map/ppermute | solution.py:166
  48.0 0.9 pass_on.1
  48.9 0.0 collective-permute-start.4
  48.9 3.2 %collective-permute-start = (bf16[2,1,272,128]{3,2,1,0:T(8,128)(2,1)}, bf16[2,1,272,128]{3,2,1,0:T(8,128)(2,1)S(1)}, u32[]{:S(2)}, u32[]{:S(2)}) collective-permute-start(bf16[2,1,272,128]{3,2,1,0:T(8,128)(2,1)} %copy-done.11), channel_id=1, source_target_pairs={{0,1},{1,2},{2,3},{3,0},{4,5},{5,6},{6,7},{7,4},{8,9},{9,10},{10,1... | collective-permute-start | bytes 417800 | tf_op jit(solution)/shard_map/ppermute | solution.py:371
  52.1 2.2 %collective-permute-start.1 = (bf16[2,1,272,128]{3,2,1,0:T(8,128)(2,1)}, bf16[2,1,272,128]{3,2,1,0:T(8,128)(2,1)}, u32[]{:S(2)}, u32[]{:S(2)}) collective-permute-start(bf16[2,1,272,128]{3,2,1,0:T(8,128)(2,1)} %copy-done.10), channel_id=1, source_target_pairs={{0,2},{1,3},{2,0},{3,1},{4,6},{5,7},{6,4},{7,5},{8,10},{9,11},{10,... | collective-permute-start | bytes 417800 | tf_op jit(solution)/shard_map/ppermute | solution.py:371
  54.3 0.0 collective-permute-start.5
  54.3 10.8 %collective-permute-done.4.refs_2_ = bf16[8,8,2,16,128]{4,3,2,1,0:T(8,128)(2,1)} collective-permute-done((bf16[8,8,2,16,128]{4,3,2,1,0:T(8,128)(2,1)}, bf16[8,8,2,16,128]{4,3,2,1,0:T(8,128)(2,1)}, u32[]{:S(2)}, u32[]{:S(2)}) %collective-permute-start.4) | collective-permute-done | bytes 524320 | tf_op jit(solution)/shard_map/ppermute | solution.py:362
  65.1 1.3 token_.1.refs_3_
  66.4 0.0 all-to-all-done.1
  66.4 0.0 copy-start.4
  66.4 1.2 copy-done.4
  67.5 3.6 %all-to-all-start = ((bf16[8,68,16,128]{3,2,1,0:T(8,128)(2,1)}), bf16[8,68,16,128]{3,2,1,0:T(8,128)(2,1)S(1)}, u32[]{:S(2)}, u32[]{:S(2)}) async-start(bf16[8,68,16,128]{3,2,1,0:T(8,128)(2,1)} %get-tuple-element.30), calls=%async_computation | async-start | bytes 4456448 | tf_op jit(solution)/shard_map/all_to_all | solution.py:314
  71.1 0.0 collective-permute-done.refs_1_
  71.1 2.8 %collective-permute-done.1.refs_2_ = bf16[2,1,272,128]{3,2,1,0:T(8,128)(2,1)} collective-permute-done((bf16[2,1,272,128]{3,2,1,0:T(8,128)(2,1)}, bf16[2,1,272,128]{3,2,1,0:T(8,128)(2,1)}, u32[]{:S(2)}, u32[]{:S(2)}) %collective-permute-start.1) | collective-permute-done | bytes 139296 | tf_op jit(solution)/shard_map/ppermute | solution.py:371
  73.9 0.0 copy-done.7
  73.9 1.4 copy-done.5
  75.3 1.8 %cut.5 = (bf16[2,3,272,128]{3,2,1,0:T(8,128)(2,1)S(1)}, bf16[2,3,272,128]{3,2,1,0:T(8,128)(2,1)}, bf16[2,3,272,128]{3,2,1,0:T(8,128)(2,1)}, bf16[2,3,272,128]{3,2,1,0:T(8,128)(2,1)}) custom-call(s32[8,4]{1,0:T(8,128)S(1)} %copy-done.7, bf16[8,816,128]{2,1,0:T(8,128)(2,1)S(1)} %bitcast.12, bf16[2,1,272,128]{3,2,1,0:T(8,128)(2,1)S(1)} %get-tuple-element.33.refs_0_, ...), custom_call_target="tpu_custom_call" | custom-call | flops 34500001792 | bytes 3342336 | tf_op jit(solution)/shard_map/cut/pallas_call | solution.py:131
  77.1 0.0 collective-permute-start.6
  77.1 3.4 %collective-permute-start.7 = (bf16[2,3,272,128]{3,2,1,0:T(8,128)(2,1)}, bf16[2,3,272,128]{3,2,1,0:T(8,128)(2,1)}, u32[]{:S(2)}, u32[]{:S(2)}) collective-permute-start(bf16[2,3,272,128]{3,2,1,0:T(8,128)(2,1)} %get-tuple-element.41), channel_id=1, source_target_pairs={{0,2},{1,3},{2,0},{3,1},{4,6},{5,7},{6,4},{7,5},{8,10},{9,11},{10,... | collective-permute-start | bytes 1253384 | tf_op jit(solution)/shard_map/ppermute | solution.py:371
  80.5 2.0 %collective-permute-start.8 = (bf16[2,3,272,128]{3,2,1,0:T(8,128)(2,1)}, bf16[2,3,272,128]{3,2,1,0:T(8,128)(2,1)}, u32[]{:S(2)}, u32[]{:S(2)}) collective-permute-start(bf16[2,3,272,128]{3,2,1,0:T(8,128)(2,1)} %get-tuple-element.42), channel_id=1, source_target_pairs={{0,3},{1,0},{2,1},{3,2},{4,7},{5,4},{6,5},{7,6},{8,11},{9,8},{10,9... | collective-permute-start | bytes 1253384 | tf_op jit(solution)/shard_map/ppermute | solution.py:371
  82.6 0.0 collective-permute-done.5.refs_3_
  82.6 14.8 %all-to-all-done = bf16[8,68,16,128]{3,2,1,0:T(8,128)(2,1)S(1)} async-done(((bf16[8,68,16,128]{3,2,1,0:T(8,128)(2,1)}), bf16[8,68,16,128]{3,2,1,0:T(8,128)(2,1)S(1)}, u32[]{:S(2)}, u32[]{:S(2)}) %all-to-all-start) | async-done | bytes 2228256 | tf_op jit(solution)/shard_map/all_to_all | solution.py:314
  97.4 0.8 cut.6
  98.2 1.6 collective-permute-start.13
  99.8 1.1 collective-permute-start.14
  100.8 0.0 collective-permute-done.6.refs_1_
  100.8 0.5 collective-permute-start.15
  101.3 25.0 %collective-permute-done.7.refs_2_ = bf16[2,3,272,128]{3,2,1,0:T(8,128)(2,1)} collective-permute-done((bf16[2,3,272,128]{3,2,1,0:T(8,128)(2,1)}, bf16[2,3,272,128]{3,2,1,0:T(8,128)(2,1)}, u32[]{:S(2)}, u32[]{:S(2)}) %collective-permute-start.7) | collective-permute-done | bytes 417824 | tf_op jit(solution)/shard_map/ppermute | solution.py:371
  126.3 1.3 collective-permute-start.12
  127.6 2.0 %collective-permute-done.8.refs_3_ = bf16[2,3,272,128]{3,2,1,0:T(8,128)(2,1)} collective-permute-done((bf16[2,3,272,128]{3,2,1,0:T(8,128)(2,1)}, bf16[2,3,272,128]{3,2,1,0:T(8,128)(2,1)}, u32[]{:S(2)}, u32[]{:S(2)}) %collective-permute-start.8) | collective-permute-done | bytes 417824 | tf_op jit(solution)/shard_map/ppermute | solution.py:371
  129.6 0.9 cut.7
  130.5 2.6 %collective-permute-start.9 = (bf16[2,2,272,128]{3,2,1,0:T(8,128)(2,1)S(1)}, bf16[2,2,272,128]{3,2,1,0:T(8,128)(2,1)S(1)}, u32[]{:S(2)}, u32[]{:S(2)}) collective-permute-start(bf16[2,2,272,128]{3,2,1,0:T(8,128)(2,1)S(1)} %get-tuple-element.44), channel_id=1, source_target_pairs={{0,1},{1,2},{2,3},{3,0},{4,5},{5,6},{6,7},{7,4},{8,9},{9,10},{10,1... | collective-permute-start | bytes 835592 | tf_op jit(solution)/shard_map/ppermute | solution.py:371
  133.1 0.0 collective-permute-done.13.refs_1_
  133.1 0.0 collective-permute-start.10
  133.1 17.2 %collective-permute-done.12 = bf16[8,8,2,16,128]{4,3,2,1,0:T(8,128)(2,1)S(1)} collective-permute-done((bf16[8,8,2,16,128]{4,3,2,1,0:T(8,128)(2,1)}, bf16[8,8,2,16,128]{4,3,2,1,0:T(8,128)(2,1)S(1)}, u32[]{:S(2)}, u32[]{:S(2)}) %collective-permute-start.12) | collective-permute-done | bytes 524320 | tf_op jit(solution)/shard_map/ppermute | solution.py:365
  150.3 2.4 %collective-permute-start.11 = (bf16[2,2,272,128]{3,2,1,0:T(8,128)(2,1)S(1)}, bf16[2,2,272,128]{3,2,1,0:T(8,128)(2,1)S(1)}, u32[]{:S(2)}, u32[]{:S(2)}) collective-permute-start(bf16[2,2,272,128]{3,2,1,0:T(8,128)(2,1)S(1)} %get-tuple-element.46), channel_id=1, source_target_pairs={{0,3},{1,0},{2,1},{3,2},{4,7},{5,4},{6,5},{7,6},{8,11},{9,8},{10,9... | collective-permute-start | bytes 835592 | tf_op jit(solution)/shard_map/ppermute | solution.py:371
  152.7 0.0 copy-done.3
  152.7 0.1 broadcast_select_fusion
  152.8 4.0 %assemble.1.refs_4_ = bf16[8,2,128,512]{3,2,1,0:T(8,128)(2,1)S(1)} custom-call(s32[1]{0:T(128)} %bitcast.me_ref.at, bf16[8,8,2,16,128]{4,3,2,1,0:T(8,128)(2,1)S(1)} %get-tuple-element.36.own_ref.refs_0_, bf16[8,8,2,16,128]{4,3,2,1,0:T(8,128)(2,1)S(1)} %get-tuple-element.59.refs_1_, bf16[8,8,2,16,128]{4,3,2,1,0:T(8,128)(2,1)} %collective-permute-done.4.refs_2_, ...), custom_call_target="tpu_custom_call" | custom-call | tf_op jit(solution)/shard_map/assemble/pallas_call | solution.py:215
  156.8 3.0 %absorb.4 = (bf16[8,2,4,48,512]{4,3,2,1,0:T(8,128)(2,1)}, bf16[8,2,4,224,512]{4,3,2,1,0:T(8,128)(2,1)}) custom-call(s32[1]{0:T(128)} %bitcast.me_ref.at, bf16[2,1,272,128]{3,2,1,0:T(8,128)(2,1)S(1)} %get-tuple-element.33.refs_0_, bf16[2,1,272,128]{3,2,1,0:T(8,128)(2,1)S(1)} %collective-permute-done.refs_1_, ...), custom_call_target="tpu_custom_call" | custom-call | flops 285212672 | bytes 2785280 | tf_op jit(solution)/shard_map/absorb/pallas_call | solution.py:258
  159.9 5.5 %absorb.5 = (bf16[8,2,4,48,512]{4,3,2,1,0:T(8,128)(2,1)}, bf16[8,2,4,224,512]{4,3,2,1,0:T(8,128)(2,1)}) custom-call(s32[1]{0:T(128)} %bitcast.me_ref.at, bf16[2,3,272,128]{3,2,1,0:T(8,128)(2,1)S(1)} %get-tuple-element.37.refs_0_, bf16[2,3,272,128]{3,2,1,0:T(8,128)(2,1)} %collective-permute-done.6.refs_1_, ...), custom_call_target="tpu_custom_call", output_to_operand_aliasing={{0}: (6, {}), {1}: (7, {})} | custom-call | flops 855638016 | bytes 8355840 | tf_op jit(solution)/shard_map/absorb/pallas_call | solution.py:258
  165.3 0.0 collective-permute-done.14.refs_2_
  165.3 0.0 collective-permute-done.15.refs_3_
  165.4 3.0 %absorb.6 = (bf16[8,2,4,48,512]{4,3,2,1,0:T(8,128)(2,1)}, bf16[8,2,4,224,512]{4,3,2,1,0:T(8,128)(2,1)}) custom-call(s32[1]{0:T(128)} %bitcast.me_ref.at, bf16[2,2,272,128]{3,2,1,0:T(8,128)(2,1)S(1)} %get-tuple-element.39.refs_0_, bf16[2,2,272,128]{3,2,1,0:T(8,128)(2,1)S(1)} %collective-permute-done.13.refs_1_, ...), custom_call_target="tpu_custom_call", output_to_operand_aliasing={{0}: (6, {}), {1}: (7, {})} | custom-call | flops 570425344 | bytes 5570560 | tf_op jit(solution)/shard_map/absorb/pallas_call | solution.py:258
  168.3 0.0 collective-permute-done.9.refs_1_
  168.3 0.0 collective-permute-done.10.refs_2_
  168.3 0.0 collective-permute-done.11.refs_3_
  168.3 3.0 %absorb.7 = (bf16[8,2,4,48,512]{4,3,2,1,0:T(8,128)(2,1)}, bf16[8,2,4,224,512]{4,3,2,1,0:T(8,128)(2,1)}) custom-call(s32[1]{0:T(128)} %bitcast.me_ref.at, bf16[2,2,272,128]{3,2,1,0:T(8,128)(2,1)S(1)} %get-tuple-element.43.refs_0_, bf16[2,2,272,128]{3,2,1,0:T(8,128)(2,1)S(1)} %collective-permute-done.9.refs_1_, ...), custom_call_target="tpu_custom_call", output_to_operand_aliasing={{0}: (6, {}), {1}: (7, {})} | custom-call | flops 570425344 | bytes 5570560 | tf_op jit(solution)/shard_map/absorb/pallas_call | solution.py:258
  (18 shorter events, 0.0 us)
Async XLA Ops:
  1.4 3.1 %copy-start.8 = (s32[2,32]{1,0:T(2,128)S(1)}, s32[2,32]{1,0:T(2,128)}, u32[]{:S(2)}) copy-start(s32[2,32]{1,0:T(2,128)} %owners.1) | copy-start | bytes 772
  4.6 8.7 %copy-start.13 = (s32[8,4]{0,1:T(4,128)S(1)}, s32[8,4]{0,1:T(4,128)}, u32[]{:S(2)}) copy-start(s32[8,4]{0,1:T(4,128)} %param.7) | copy-start | bytes 388
  9.0 18.5 %all-to-all-start.2 = ((bf16[8,33,16,128]{3,2,1,0:T(8,128)(2,1)}), bf16[8,33,16,128]{3,2,1,0:T(8,128)(2,1)S(1)}, u32[]{:S(2)}, u32[]{:S(2)}) async-start(bf16[8,33,16,128]{3,2,1,0:T(8,128)(2,1)} %get-tuple-element.32), calls=%async_computation.2 | async-start | bytes 2162688 | tf_op jit(solution)/shard_map/all_to_all | solution.py:314
  13.3 14.9 %copy-start.6 = (s32[8,4]{1,0:T(8,128)}, s32[8,4]{1,0:T(8,128)S(1)}, u32[]{:S(2)}) copy-start(s32[8,4]{1,0:T(8,128)S(1)} %copy.16.mapped) | copy-start | bytes 388
  28.2 0.7 copy-start.9
  28.8 0.6 copy-start.10
  29.5 0.7 copy-start.11
  30.2 15.8 %collective-permute-start.3 = (bf16[8,8,2,16,128]{4,3,2,1,0:T(8,128)(2,1)S(1)}, bf16[8,8,2,16,128]{4,3,2,1,0:T(8,128)(2,1)S(1)}, u32[]{:S(2)}, u32[]{:S(2)}) collective-permute-start(bf16[8,8,2,16,128]{4,3,2,1,0:T(8,128)(2,1)S(1)} %get-tuple-element.36.own_ref.refs_0_), channel_id=1, source_target_pairs={{1,0},{2,1},{3,2},{5,4},{6,5},{7,6},{9,8},{10,9},{11,10},{13,12},{... | collective-permute-start | bytes 1572872 | tf_op jit(solution)/shard_map/ppermute | solution.py:167
  32.5 15.5 %collective-permute-start.2 = (bf16[8,8,2,16,128]{4,3,2,1,0:T(8,128)(2,1)S(1)}, bf16[8,8,2,16,128]{4,3,2,1,0:T(8,128)(2,1)S(1)}, u32[]{:S(2)}, u32[]{:S(2)}) collective-permute-start(bf16[8,8,2,16,128]{4,3,2,1,0:T(8,128)(2,1)S(1)} %get-tuple-element.36.own_ref.refs_0_), channel_id=1, source_target_pairs={{0,1},{1,2},{2,3},{4,5},{5,6},{6,7},{8,9},{9,10},{10,11},{12,13},{... | collective-permute-start | bytes 1572872 | tf_op jit(solution)/shard_map/ppermute | solution.py:166
  36.0 30.4 %all-to-all-start.1 = ((bf16[8,51,16,128]{3,2,1,0:T(8,128)(2,1)}), bf16[8,51,16,128]{3,2,1,0:T(8,128)(2,1)S(1)}, u32[]{:S(2)}, u32[]{:S(2)}) async-start(bf16[8,51,16,128]{3,2,1,0:T(8,128)(2,1)} %get-tuple-element.31), calls=%async_computation.1 | async-start | bytes 3342336 | tf_op jit(solution)/shard_map/all_to_all | solution.py:314
  45.9 19.1 %copy-start = (bf16[8,8,2,16,128]{4,3,2,1,0:T(8,128)(2,1)}, bf16[8,8,2,16,128]{4,3,2,1,0:T(8,128)(2,1)S(1)}, u32[]{:S(2)}) copy-start(bf16[8,8,2,16,128]{4,3,2,1,0:T(8,128)(2,1)S(1)} %collective-permute-done.3.down_ref.refs_1_) | copy-start | bytes 1572868
  48.0 17.1 %copy-start.2 = (bf16[8,8,2,16,128]{4,3,2,1,0:T(8,128)(2,1)}, bf16[8,8,2,16,128]{4,3,2,1,0:T(8,128)(2,1)S(1)}, u32[]{:S(2)}) copy-start(bf16[8,8,2,16,128]{4,3,2,1,0:T(8,128)(2,1)S(1)} %collective-permute-done.2.up_ref.refs_0_) | copy-start | bytes 1572868
  48.9 16.2 %collective-permute-start.4 = (bf16[8,8,2,16,128]{4,3,2,1,0:T(8,128)(2,1)}, bf16[8,8,2,16,128]{4,3,2,1,0:T(8,128)(2,1)}, u32[]{:S(2)}, u32[]{:S(2)}) collective-permute-start(bf16[8,8,2,16,128]{4,3,2,1,0:T(8,128)(2,1)} %pass_on.1), channel_id=1, source_target_pairs={{0,2},{1,0},{2,3},{3,1},{4,6},{5,4},{6,7},{7,5},{8,10},{9,8},{10,1... | collective-permute-start | bytes 1572872 | tf_op jit(solution)/shard_map/ppermute | solution.py:362
  48.9 22.2 %collective-permute-start = (bf16[2,1,272,128]{3,2,1,0:T(8,128)(2,1)}, bf16[2,1,272,128]{3,2,1,0:T(8,128)(2,1)S(1)}, u32[]{:S(2)}, u32[]{:S(2)}) collective-permute-start(bf16[2,1,272,128]{3,2,1,0:T(8,128)(2,1)} %copy-done.11), channel_id=1, source_target_pairs={{0,1},{1,2},{2,3},{3,0},{4,5},{5,6},{6,7},{7,4},{8,9},{9,10},{10,1... | collective-permute-start | bytes 417800 | tf_op jit(solution)/shard_map/ppermute | solution.py:371
  52.1 21.8 %collective-permute-start.1 = (bf16[2,1,272,128]{3,2,1,0:T(8,128)(2,1)}, bf16[2,1,272,128]{3,2,1,0:T(8,128)(2,1)}, u32[]{:S(2)}, u32[]{:S(2)}) collective-permute-start(bf16[2,1,272,128]{3,2,1,0:T(8,128)(2,1)} %copy-done.10), channel_id=1, source_target_pairs={{0,2},{1,3},{2,0},{3,1},{4,6},{5,7},{6,4},{7,5},{8,10},{9,11},{10,... | collective-permute-start | bytes 417800 | tf_op jit(solution)/shard_map/ppermute | solution.py:371
  54.3 28.3 %collective-permute-start.5 = (bf16[2,1,272,128]{3,2,1,0:T(8,128)(2,1)}, bf16[2,1,272,128]{3,2,1,0:T(8,128)(2,1)}, u32[]{:S(2)}, u32[]{:S(2)}) collective-permute-start(bf16[2,1,272,128]{3,2,1,0:T(8,128)(2,1)} %copy-done.9), channel_id=1, source_target_pairs={{0,3},{1,0},{2,1},{3,2},{4,7},{5,4},{6,5},{7,6},{8,11},{9,8},{10,9... | collective-permute-start | bytes 417800 | tf_op jit(solution)/shard_map/ppermute | solution.py:371
  66.4 7.5 %copy-start.7 = (s32[8,4]{1,0:T(8,128)S(1)}, s32[8,4]{1,0:T(8,128)}, u32[]{:S(2)}) copy-start(s32[8,4]{1,0:T(8,128)} %copy-done.6) | copy-start | bytes 388
  66.4 7.5 %copy-start.12 = (bf16[16,128]{1,0:T(8,128)(2,1)S(1)}, bf16[16,128]{1,0:T(8,128)(2,1)}, u32[]{:S(2)}) copy-start(bf16[16,128]{1,0:T(8,128)(2,1)} %token_.1.refs_3_) | copy-start | bytes 12292
  66.4 1.2 copy-start.4
  67.5 29.8 %all-to-all-start = ((bf16[8,68,16,128]{3,2,1,0:T(8,128)(2,1)}), bf16[8,68,16,128]{3,2,1,0:T(8,128)(2,1)S(1)}, u32[]{:S(2)}, u32[]{:S(2)}) async-start(bf16[8,68,16,128]{3,2,1,0:T(8,128)(2,1)} %get-tuple-element.30), calls=%async_computation | async-start | bytes 4456448 | tf_op jit(solution)/shard_map/all_to_all | solution.py:314
  73.9 1.4 copy-start.5
  77.1 23.7 %collective-permute-start.6 = (bf16[2,3,272,128]{3,2,1,0:T(8,128)(2,1)}, bf16[2,3,272,128]{3,2,1,0:T(8,128)(2,1)}, u32[]{:S(2)}, u32[]{:S(2)}) collective-permute-start(bf16[2,3,272,128]{3,2,1,0:T(8,128)(2,1)} %get-tuple-element.40), channel_id=1, source_target_pairs={{0,1},{1,2},{2,3},{3,0},{4,5},{5,6},{6,7},{7,4},{8,9},{9,10},{10,1... | collective-permute-start | bytes 1253384 | tf_op jit(solution)/shard_map/ppermute | solution.py:371
  77.1 49.1 %collective-permute-start.7 = (bf16[2,3,272,128]{3,2,1,0:T(8,128)(2,1)}, bf16[2,3,272,128]{3,2,1,0:T(8,128)(2,1)}, u32[]{:S(2)}, u32[]{:S(2)}) collective-permute-start(bf16[2,3,272,128]{3,2,1,0:T(8,128)(2,1)} %get-tuple-element.41), channel_id=1, source_target_pairs={{0,2},{1,3},{2,0},{3,1},{4,6},{5,7},{6,4},{7,5},{8,10},{9,11},{10,... | collective-permute-start | bytes 1253384 | tf_op jit(solution)/shard_map/ppermute | solution.py:371
  80.5 49.1 %collective-permute-start.8 = (bf16[2,3,272,128]{3,2,1,0:T(8,128)(2,1)}, bf16[2,3,272,128]{3,2,1,0:T(8,128)(2,1)}, u32[]{:S(2)}, u32[]{:S(2)}) collective-permute-start(bf16[2,3,272,128]{3,2,1,0:T(8,128)(2,1)} %get-tuple-element.42), channel_id=1, source_target_pairs={{0,3},{1,0},{2,1},{3,2},{4,7},{5,4},{6,5},{7,6},{8,11},{9,8},{10,9... | collective-permute-start | bytes 1253384 | tf_op jit(solution)/shard_map/ppermute | solution.py:371
  98.2 35.0 %collective-permute-start.13 = (bf16[2,2,272,128]{3,2,1,0:T(8,128)(2,1)S(1)}, bf16[2,2,272,128]{3,2,1,0:T(8,128)(2,1)S(1)}, u32[]{:S(2)}, u32[]{:S(2)}) collective-permute-start(bf16[2,2,272,128]{3,2,1,0:T(8,128)(2,1)S(1)} %get-tuple-element.47), channel_id=1, source_target_pairs={{0,1},{1,2},{2,3},{3,0},{4,5},{5,6},{6,7},{7,4},{8,9},{9,10},{10,1... | collective-permute-start | bytes 835592 | tf_op jit(solution)/shard_map/ppermute | solution.py:371
  99.8 65.6 %collective-permute-start.14 = (bf16[2,2,272,128]{3,2,1,0:T(8,128)(2,1)S(1)}, bf16[2,2,272,128]{3,2,1,0:T(8,128)(2,1)S(1)}, u32[]{:S(2)}, u32[]{:S(2)}) collective-permute-start(bf16[2,2,272,128]{3,2,1,0:T(8,128)(2,1)S(1)} %get-tuple-element.48), channel_id=1, source_target_pairs={{0,2},{1,3},{2,0},{3,1},{4,6},{5,7},{6,4},{7,5},{8,10},{9,11},{10,... | collective-permute-start | bytes 835592 | tf_op jit(solution)/shard_map/ppermute | solution.py:371
  100.8 64.5 %collective-permute-start.15 = (bf16[2,2,272,128]{3,2,1,0:T(8,128)(2,1)S(1)}, bf16[2,2,272,128]{3,2,1,0:T(8,128)(2,1)S(1)}, u32[]{:S(2)}, u32[]{:S(2)}) collective-permute-start(bf16[2,2,272,128]{3,2,1,0:T(8,128)(2,1)S(1)} %get-tuple-element.49), channel_id=1, source_target_pairs={{0,3},{1,0},{2,1},{3,2},{4,7},{5,4},{6,5},{7,6},{8,11},{9,8},{10,9... | collective-permute-start | bytes 835592 | tf_op jit(solution)/shard_map/ppermute | solution.py:371
  126.3 24.0 %collective-permute-start.12 = (bf16[8,8,2,16,128]{4,3,2,1,0:T(8,128)(2,1)}, bf16[8,8,2,16,128]{4,3,2,1,0:T(8,128)(2,1)S(1)}, u32[]{:S(2)}, u32[]{:S(2)}) collective-permute-start(bf16[8,8,2,16,128]{4,3,2,1,0:T(8,128)(2,1)} %collective-permute-done.4.refs_2_), channel_id=1, source_target_pairs={{1,0},{2,3},{5,4},{6,7},{9,8},{10,11},{13,12},{14,15},{17,16},{18,... | collective-permute-start | bytes 1572872 | tf_op jit(solution)/shard_map/ppermute | solution.py:365
  129.6 23.1 %copy-start.1 = (bf16[8,8,2,16,128]{4,3,2,1,0:T(8,128)(2,1)S(1)}, bf16[8,8,2,16,128]{4,3,2,1,0:T(8,128)(2,1)}, u32[]{:S(2)}) copy-start(bf16[8,8,2,16,128]{4,3,2,1,0:T(8,128)(2,1)} %copy-done) | copy-start | bytes 1572868
  129.6 23.1 %copy-start.3 = (bf16[8,8,2,16,128]{4,3,2,1,0:T(8,128)(2,1)S(1)}, bf16[8,8,2,16,128]{4,3,2,1,0:T(8,128)(2,1)}, u32[]{:S(2)}) copy-start(bf16[8,8,2,16,128]{4,3,2,1,0:T(8,128)(2,1)} %copy-done.2) | copy-start | bytes 1572868
  130.5 37.8 %collective-permute-start.9 = (bf16[2,2,272,128]{3,2,1,0:T(8,128)(2,1)S(1)}, bf16[2,2,272,128]{3,2,1,0:T(8,128)(2,1)S(1)}, u32[]{:S(2)}, u32[]{:S(2)}) collective-permute-start(bf16[2,2,272,128]{3,2,1,0:T(8,128)(2,1)S(1)} %get-tuple-element.44), channel_id=1, source_target_pairs={{0,1},{1,2},{2,3},{3,0},{4,5},{5,6},{6,7},{7,4},{8,9},{9,10},{10,1... | collective-permute-start | bytes 835592 | tf_op jit(solution)/shard_map/ppermute | solution.py:371
  133.1 35.2 %collective-permute-start.10 = (bf16[2,2,272,128]{3,2,1,0:T(8,128)(2,1)S(1)}, bf16[2,2,272,128]{3,2,1,0:T(8,128)(2,1)S(1)}, u32[]{:S(2)}, u32[]{:S(2)}) collective-permute-start(bf16[2,2,272,128]{3,2,1,0:T(8,128)(2,1)S(1)} %get-tuple-element.45), channel_id=1, source_target_pairs={{0,2},{1,3},{2,0},{3,1},{4,6},{5,7},{6,4},{7,5},{8,10},{9,11},{10,... | collective-permute-start | bytes 835592 | tf_op jit(solution)/shard_map/ppermute | solution.py:371
  150.3 18.0 %collective-permute-start.11 = (bf16[2,2,272,128]{3,2,1,0:T(8,128)(2,1)S(1)}, bf16[2,2,272,128]{3,2,1,0:T(8,128)(2,1)S(1)}, u32[]{:S(2)}, u32[]{:S(2)}) collective-permute-start(bf16[2,2,272,128]{3,2,1,0:T(8,128)(2,1)S(1)} %get-tuple-element.46), channel_id=1, source_target_pairs={{0,3},{1,0},{2,1},{3,2},{4,7},{5,4},{6,5},{7,6},{8,11},{9,8},{10,9... | collective-permute-start | bytes 835592 | tf_op jit(solution)/shard_map/ppermute | solution.py:371

commit v12 on v11

--- a/solution.py
+++ b/solution.py
@@ -339,8 +339,8 @@
             waits = waits + exchanged[at - 2][1:]
         if at == 1:
             waits = waits + exchanged[0][1:3]
-        if t_ways == 4 and at == 1:
-            waits = waits + [near]
+        if t_ways == 4 and at in (1, len(chunks) - 1):
+            waits = waits + [near if at == 1 else third]
         pieces = list(
             cut(
                 rows,

time: 173 us -> 170 us (0.983)
  starting transfers between devices: 38.9 us -> 34.6 us
  local copies, waits for them, and re-layouts: 8.59 us -> 11 us
    ppermute x12, waiting for transfers between devices: 29.8 us -> 49.2 us  [per_device(): lax.ppermute(piece, 'tp', [(i, (i + shift) % t_ways) for i in range(t_way...]
    ppermute x1, waiting for transfers between devices: 17.2 us -> 0.01 us  [per_device(): third = lax.ppermute(second, 'tp', [(1, 0), (2, 3)])]
    ppermute x12, starting transfers between devices: 18.9 us -> 14 us  [per_device(): lax.ppermute(piece, 'tp', [(i, (i + shift) % t_ways) for i in range(t_way...]
    all_to_all x3, waiting for transfers between devices: 29 us -> 26.3 us  [over_fsdp(): x = lax.all_to_all(x, 'fsdp', split_axis=0, concat_axis=0, tiled=True)]
    unnamed x31 -> x39, local copies, waits for them, and re-layouts: 8.59 us -> 11 us
  transfers between devices with their start and end apart: 19 -> 19, of which waited for: 9 -> 12; matrix products, arithmetic and copies ran while one was open for 0% -> 0% of each run, Pallas kernels for 12% -> 13%
where the time goes in v12:
time: 170 us; the launch traced here: 169 us
  waiting for transfers between devices  93.2 us (55%)
  starting transfers between devices  34.6 us (20%)
  Pallas kernels  29.3 us (17%)
  local copies, waits for them, and re-layouts  11 us (6%)
    ppermute x12, waiting for transfers between devices, per_device(): lax.ppermute(piece, 'tp', [(i, (i + shift) % t_ways) for i in range(t_way...  49.2 us
    all_to_all x3, waiting for transfers between devices, over_fsdp(): x = lax.all_to_all(x, 'fsdp', split_axis=0, concat_axis=0, tiled=True)  26.3 us
    pallas_call x4, Pallas kernels, absorb(): pl.pallas_call(kernel, grid_spec=pltpu.PrefetchScalarGridSpec(num_scalar_...  14.5 us
    ppermute x12, starting transfers between devices, per_device(): lax.ppermute(piece, 'tp', [(i, (i + shift) % t_ways) for i in range(t_way...  14 us
    all_to_all x3, starting transfers between devices, over_fsdp(): x = lax.all_to_all(x, 'fsdp', split_axis=0, concat_axis=0, tiled=True)  12.8 us
    unnamed x39, local copies, waits for them, and re-layouts  11 us
    ppermute x1, waiting for transfers between devices, per_device(): lax.ppermute(pass_on(me, pairs, up, down), 'tp', [(0, 2), (1, 0), (2, 3),...  10.8 us
    ppermute x1, waiting for transfers between devices, neighbours(): lax.ppermute(x, axis, [(i + 1, i) for i in range(ways - 1)])  4.91 us
  transfers between devices with their start and end apart: 19, of which 12 were waited for; matrix products, arithmetic and copies ran while one was open for 0% of the time, Pallas kernels for 13%

profile of v12, /device:TPU:10, one launch (start us, length us, event | category | flops | bytes accessed | tf_op | source)
XLA Modules:
  0.0 169.1 jit_solution(11118691907088746891)
XLA Ops:
  0.6 0.8 copy.12.offsets
  1.4 3.1 %copy.17 = bf16[1,2,9728,128]{3,2,1,0:T(8,128)(2,1)S(1)} copy(bf16[1,2,9728,128]{3,1,2,0:T(2,128)(2,1)} %bitcast.16) | data formatting | bytes 9961472
  4.6 0.0 copy-start.17
  4.6 4.4 %pack.1 = (bf16[8,33,16,128]{3,2,1,0:T(8,128)(2,1)}, bf16[8,51,16,128]{3,2,1,0:T(8,128)(2,1)}, bf16[8,68,16,128]{3,2,1,0:T(8,128)(2,1)}) custom-call(s32[2,32,4]{2,1,0:T(8,128)S(1)} %copy.12.offsets, s32[2,32]{1,0:T(2,128)S(1)} %copy-done.12, bf16[2,608,16,128]{3,2,1,0:T(8,128)(2,1)S(1)} %bitcast.9), custom_call_target="tpu_custom_call" | custom-call | bytes 9961472 | tf_op jit(solution)/shard_map/pack/pallas_call | solution.py:78
  9.0 4.3 %all-to-all-start.2 = ((bf16[8,33,16,128]{3,2,1,0:T(8,128)(2,1)}), bf16[8,33,16,128]{3,2,1,0:T(8,128)(2,1)S(1)}, u32[]{:S(2)}, u32[]{:S(2)}) async-start(bf16[8,33,16,128]{3,2,1,0:T(8,128)(2,1)} %get-tuple-element.32), calls=%async_computation.2 | async-start | bytes 2162688 | tf_op jit(solution)/shard_map/all_to_all | solution.py:314
  13.2 0.1 copy.16.mapped
  13.3 14.2 %all-to-all-done.2 = bf16[8,33,16,128]{3,2,1,0:T(8,128)(2,1)S(1)} async-done(((bf16[8,33,16,128]{3,2,1,0:T(8,128)(2,1)}), bf16[8,33,16,128]{3,2,1,0:T(8,128)(2,1)S(1)}, u32[]{:S(2)}, u32[]{:S(2)}) %all-to-all-start.2) | async-done | bytes 1081376 | tf_op jit(solution)/shard_map/all_to_all | solution.py:314
  27.5 0.7 cut.4
  28.2 0.6 copy-done.13
  28.8 0.6 copy-done.14
  29.5 0.7 copy-done.15
  30.2 2.3 %collective-permute-start.3 = (bf16[8,8,2,16,128]{4,3,2,1,0:T(8,128)(2,1)S(1)}, bf16[8,8,2,16,128]{4,3,2,1,0:T(8,128)(2,1)S(1)}, u32[]{:S(2)}, u32[]{:S(2)}) collective-permute-start(bf16[8,8,2,16,128]{4,3,2,1,0:T(8,128)(2,1)S(1)} %get-tuple-element.36.own_ref.refs_0_), channel_id=1, source_target_pairs={{1,0},{2,1},{3,2},{5,4},{6,5},{7,6},{9,8},{10,9},{11,10},{13,12},{... | collective-permute-start | bytes 1572872 | tf_op jit(solution)/shard_map/ppermute | solution.py:167
  32.5 3.5 %collective-permute-start.2 = (bf16[8,8,2,16,128]{4,3,2,1,0:T(8,128)(2,1)S(1)}, bf16[8,8,2,16,128]{4,3,2,1,0:T(8,128)(2,1)S(1)}, u32[]{:S(2)}, u32[]{:S(2)}) collective-permute-start(bf16[8,8,2,16,128]{4,3,2,1,0:T(8,128)(2,1)S(1)} %get-tuple-element.36.own_ref.refs_0_), channel_id=1, source_target_pairs={{0,1},{1,2},{2,3},{4,5},{5,6},{6,7},{8,9},{9,10},{10,11},{12,13},{... | collective-permute-start | bytes 1572872 | tf_op jit(solution)/shard_map/ppermute | solution.py:166
  36.0 5.0 %all-to-all-start.1 = ((bf16[8,51,16,128]{3,2,1,0:T(8,128)(2,1)}), bf16[8,51,16,128]{3,2,1,0:T(8,128)(2,1)S(1)}, u32[]{:S(2)}, u32[]{:S(2)}) async-start(bf16[8,51,16,128]{3,2,1,0:T(8,128)(2,1)} %get-tuple-element.31), calls=%async_computation.1 | async-start | bytes 3342336 | tf_op jit(solution)/shard_map/all_to_all | solution.py:314
  41.0 4.9 %collective-permute-done.3.down_ref.refs_1_ = bf16[8,8,2,16,128]{4,3,2,1,0:T(8,128)(2,1)S(1)} collective-permute-done((bf16[8,8,2,16,128]{4,3,2,1,0:T(8,128)(2,1)S(1)}, bf16[8,8,2,16,128]{4,3,2,1,0:T(8,128)(2,1)S(1)}, u32[]{:S(2)}, u32[]{:S(2)}) %collective-permute-start.3) | collective-permute-done | bytes 524320 | tf_op jit(solution)/shard_map/ppermute | solution.py:167
  45.9 2.1 %collective-permute-done.2.up_ref.refs_0_ = bf16[8,8,2,16,128]{4,3,2,1,0:T(8,128)(2,1)S(1)} collective-permute-done((bf16[8,8,2,16,128]{4,3,2,1,0:T(8,128)(2,1)S(1)}, bf16[8,8,2,16,128]{4,3,2,1,0:T(8,128)(2,1)S(1)}, u32[]{:S(2)}, u32[]{:S(2)}) %collective-permute-start.2) | collective-permute-done | bytes 524320 | tf_op jit(solution)/shard_map/ppermute | solution.py:166
  48.0 0.9 pass_on.1
  48.9 0.0 collective-permute-start.4
  48.9 3.2 %collective-permute-start = (bf16[2,1,272,128]{3,2,1,0:T(8,128)(2,1)}, bf16[2,1,272,128]{3,2,1,0:T(8,128)(2,1)S(1)}, u32[]{:S(2)}, u32[]{:S(2)}) collective-permute-start(bf16[2,1,272,128]{3,2,1,0:T(8,128)(2,1)} %copy-done.15), channel_id=1, source_target_pairs={{0,1},{1,2},{2,3},{3,0},{4,5},{5,6},{6,7},{7,4},{8,9},{9,10},{10,1... | collective-permute-start | bytes 417800 | tf_op jit(solution)/shard_map/ppermute | solution.py:371
  52.1 2.2 %collective-permute-start.1 = (bf16[2,1,272,128]{3,2,1,0:T(8,128)(2,1)}, bf16[2,1,272,128]{3,2,1,0:T(8,128)(2,1)}, u32[]{:S(2)}, u32[]{:S(2)}) collective-permute-start(bf16[2,1,272,128]{3,2,1,0:T(8,128)(2,1)} %copy-done.14), channel_id=1, source_target_pairs={{0,2},{1,3},{2,0},{3,1},{4,6},{5,7},{6,4},{7,5},{8,10},{9,11},{10,... | collective-permute-start | bytes 417800 | tf_op jit(solution)/shard_map/ppermute | solution.py:371
  54.3 0.0 collective-permute-start.5
  54.3 10.8 %collective-permute-done.4.refs_2_ = bf16[8,8,2,16,128]{4,3,2,1,0:T(8,128)(2,1)} collective-permute-done((bf16[8,8,2,16,128]{4,3,2,1,0:T(8,128)(2,1)}, bf16[8,8,2,16,128]{4,3,2,1,0:T(8,128)(2,1)}, u32[]{:S(2)}, u32[]{:S(2)}) %collective-permute-start.4) | collective-permute-done | bytes 524320 | tf_op jit(solution)/shard_map/ppermute | solution.py:362
  65.1 1.3 token_.1.refs_3_
  66.4 0.0 all-to-all-done.1
  66.4 0.0 copy-start.4
  66.4 1.2 copy-done.4
  67.6 3.6 %all-to-all-start = ((bf16[8,68,16,128]{3,2,1,0:T(8,128)(2,1)}), bf16[8,68,16,128]{3,2,1,0:T(8,128)(2,1)S(1)}, u32[]{:S(2)}, u32[]{:S(2)}) async-start(bf16[8,68,16,128]{3,2,1,0:T(8,128)(2,1)} %get-tuple-element.30), calls=%async_computation | async-start | bytes 4456448 | tf_op jit(solution)/shard_map/all_to_all | solution.py:314
  71.1 0.0 collective-permute-done.refs_1_
  71.1 2.8 %collective-permute-done.1.refs_2_ = bf16[2,1,272,128]{3,2,1,0:T(8,128)(2,1)} collective-permute-done((bf16[2,1,272,128]{3,2,1,0:T(8,128)(2,1)}, bf16[2,1,272,128]{3,2,1,0:T(8,128)(2,1)}, u32[]{:S(2)}, u32[]{:S(2)}) %collective-permute-start.1) | collective-permute-done | bytes 139296 | tf_op jit(solution)/shard_map/ppermute | solution.py:371
  73.9 1.4 copy-done.5
  75.4 1.8 %cut.5 = (bf16[2,3,272,128]{3,2,1,0:T(8,128)(2,1)S(1)}, bf16[2,3,272,128]{3,2,1,0:T(8,128)(2,1)}, bf16[2,3,272,128]{3,2,1,0:T(8,128)(2,1)}, bf16[2,3,272,128]{3,2,1,0:T(8,128)(2,1)}) custom-call(s32[8,4]{1,0:T(8,128)S(1)} %copy-done.10, bf16[8,816,128]{2,1,0:T(8,128)(2,1)S(1)} %bitcast.12, bf16[2,1,272,128]{3,2,1,0:T(8,128)(2,1)S(1)} %get-tuple-element.33.refs_0_, ...), custom_call_target="tpu_custom_call" | custom-call | flops 34500001792 | bytes 3342336 | tf_op jit(solution)/shard_map/cut/pallas_call | solution.py:131
  77.2 0.8 copy-done.6
  77.9 0.0 collective-permute-start.6
  77.9 3.4 %collective-permute-start.7 = (bf16[2,3,272,128]{3,2,1,0:T(8,128)(2,1)}, bf16[2,3,272,128]{3,2,1,0:T(8,128)(2,1)}, u32[]{:S(2)}, u32[]{:S(2)}) collective-permute-start(bf16[2,3,272,128]{3,2,1,0:T(8,128)(2,1)} %get-tuple-element.41), channel_id=1, source_target_pairs={{0,2},{1,3},{2,0},{3,1},{4,6},{5,7},{6,4},{7,5},{8,10},{9,11},{10,... | collective-permute-start | bytes 1253384 | tf_op jit(solution)/shard_map/ppermute | solution.py:371
  81.3 2.0 %collective-permute-start.8 = (bf16[2,3,272,128]{3,2,1,0:T(8,128)(2,1)}, bf16[2,3,272,128]{3,2,1,0:T(8,128)(2,1)}, u32[]{:S(2)}, u32[]{:S(2)}) collective-permute-start(bf16[2,3,272,128]{3,2,1,0:T(8,128)(2,1)} %get-tuple-element.42), channel_id=1, source_target_pairs={{0,3},{1,0},{2,1},{3,2},{4,7},{5,4},{6,5},{7,6},{8,11},{9,8},{10,9... | collective-permute-start | bytes 1253384 | tf_op jit(solution)/shard_map/ppermute | solution.py:371
  83.3 1.9 %collective-permute-start.9 = (bf16[8,8,2,16,128]{4,3,2,1,0:T(8,128)(2,1)}, bf16[8,8,2,16,128]{4,3,2,1,0:T(8,128)(2,1)S(1)}, u32[]{:S(2)}, u32[]{:S(2)}) collective-permute-start(bf16[8,8,2,16,128]{4,3,2,1,0:T(8,128)(2,1)} %collective-permute-done.4.refs_2_), channel_id=1, source_target_pairs={{1,0},{2,3},{5,4},{6,7},{9,8},{10,11},{13,12},{14,15},{17,16},{18,... | collective-permute-start | bytes 1572872 | tf_op jit(solution)/shard_map/ppermute | solution.py:365
  85.3 0.0 collective-permute-done.5.refs_3_
  85.3 12.1 %all-to-all-done = bf16[8,68,16,128]{3,2,1,0:T(8,128)(2,1)S(1)} async-done(((bf16[8,68,16,128]{3,2,1,0:T(8,128)(2,1)}), bf16[8,68,16,128]{3,2,1,0:T(8,128)(2,1)S(1)}, u32[]{:S(2)}, u32[]{:S(2)}) %all-to-all-start) | async-done | bytes 2228256 | tf_op jit(solution)/shard_map/all_to_all | solution.py:314
  97.4 1.0 copy-done.7
  98.4 0.7 copy-done.11
  99.1 0.8 cut.6
  99.9 1.6 collective-permute-start.13
  101.5 0.0 collective-permute-done.6.refs_1_
  101.5 1.1 collective-permute-start.14
  102.6 18.6 %collective-permute-done.7.refs_2_ = bf16[2,3,272,128]{3,2,1,0:T(8,128)(2,1)} collective-permute-done((bf16[2,3,272,128]{3,2,1,0:T(8,128)(2,1)}, bf16[2,3,272,128]{3,2,1,0:T(8,128)(2,1)}, u32[]{:S(2)}, u32[]{:S(2)}) %collective-permute-start.7) | collective-permute-done | bytes 417824 | tf_op jit(solution)/shard_map/ppermute | solution.py:371
  121.2 0.0 collective-permute-start.15
  121.2 9.3 %collective-permute-done.8.refs_3_ = bf16[2,3,272,128]{3,2,1,0:T(8,128)(2,1)} collective-permute-done((bf16[2,3,272,128]{3,2,1,0:T(8,128)(2,1)}, bf16[2,3,272,128]{3,2,1,0:T(8,128)(2,1)}, u32[]{:S(2)}, u32[]{:S(2)}) %collective-permute-start.8) | collective-permute-done | bytes 417824 | tf_op jit(solution)/shard_map/ppermute | solution.py:371
  130.4 0.0 collective-permute-done.9.refs_4_
  130.4 0.9 cut.7
  131.3 0.1 collective-permute-start.10
  131.4 0.1 collective-permute-start.11
  131.5 1.5 collective-permute-done.13.refs_1_
  133.0 0.4 collective-permute-start.12
  133.4 0.1 broadcast_select_fusion
  133.5 4.1 %assemble.1.refs_4_ = bf16[8,2,128,512]{3,2,1,0:T(8,128)(2,1)S(1)} custom-call(s32[1]{0:T(128)} %bitcast.me_ref.at, bf16[8,8,2,16,128]{4,3,2,1,0:T(8,128)(2,1)S(1)} %get-tuple-element.36.own_ref.refs_0_, bf16[8,8,2,16,128]{4,3,2,1,0:T(8,128)(2,1)S(1)} %get-tuple-element.59.refs_1_, bf16[8,8,2,16,128]{4,3,2,1,0:T(8,128)(2,1)} %collective-permute-done.4.refs_2_, ...), custom_call_target="tpu_custom_call" | custom-call | tf_op jit(solution)/shard_map/assemble/pallas_call | solution.py:215
  137.6 3.0 %absorb.4 = (bf16[8,2,4,48,512]{4,3,2,1,0:T(8,128)(2,1)}, bf16[8,2,4,224,512]{4,3,2,1,0:T(8,128)(2,1)}) custom-call(s32[1]{0:T(128)} %bitcast.me_ref.at, bf16[2,1,272,128]{3,2,1,0:T(8,128)(2,1)S(1)} %get-tuple-element.33.refs_0_, bf16[2,1,272,128]{3,2,1,0:T(8,128)(2,1)S(1)} %collective-permute-done.refs_1_, ...), custom_call_target="tpu_custom_call" | custom-call | flops 285212672 | bytes 2785280 | tf_op jit(solution)/shard_map/absorb/pallas_call | solution.py:258
  140.7 5.5 %absorb.5 = (bf16[8,2,4,48,512]{4,3,2,1,0:T(8,128)(2,1)}, bf16[8,2,4,224,512]{4,3,2,1,0:T(8,128)(2,1)}) custom-call(s32[1]{0:T(128)} %bitcast.me_ref.at, bf16[2,3,272,128]{3,2,1,0:T(8,128)(2,1)S(1)} %copy-done.8, bf16[2,3,272,128]{3,2,1,0:T(8,128)(2,1)} %collective-permute-done.6.refs_1_, ...), custom_call_target="tpu_custom_call", output_to_operand_aliasing={{0}: (6, {}), {1}: (7, {})} | custom-call | flops 855638016 | bytes 8355840 | tf_op jit(solution)/shard_map/absorb/pallas_call | solution.py:258
  146.2 0.0 collective-permute-done.14.refs_2_
  146.2 8.1 %collective-permute-done.15.refs_3_ = bf16[2,2,272,128]{3,2,1,0:T(8,128)(2,1)S(1)} collective-permute-done((bf16[2,2,272,128]{3,2,1,0:T(8,128)(2,1)S(1)}, bf16[2,2,272,128]{3,2,1,0:T(8,128)(2,1)S(1)}, u32[]{:S(2)}, u32[]{:S(2)}) %collective-permute-start.15) | collective-permute-done | bytes 278560 | tf_op jit(solution)/shard_map/ppermute | solution.py:371
  154.3 3.0 %absorb.6 = (bf16[8,2,4,48,512]{4,3,2,1,0:T(8,128)(2,1)}, bf16[8,2,4,224,512]{4,3,2,1,0:T(8,128)(2,1)}) custom-call(s32[1]{0:T(128)} %bitcast.me_ref.at, bf16[2,2,272,128]{3,2,1,0:T(8,128)(2,1)S(1)} %get-tuple-element.39.refs_0_, bf16[2,2,272,128]{3,2,1,0:T(8,128)(2,1)S(1)} %collective-permute-done.13.refs_1_, ...), custom_call_target="tpu_custom_call", output_to_operand_aliasing={{0}: (6, {}), {1}: (7, {})} | custom-call | flops 570425344 | bytes 5570560 | tf_op jit(solution)/shard_map/absorb/pallas_call | solution.py:258
  157.2 0.0 collective-permute-done.10.refs_1_
  157.2 5.0 %collective-permute-done.11.refs_2_ = bf16[2,2,272,128]{3,2,1,0:T(8,128)(2,1)S(1)} collective-permute-done((bf16[2,2,272,128]{3,2,1,0:T(8,128)(2,1)S(1)}, bf16[2,2,272,128]{3,2,1,0:T(8,128)(2,1)S(1)}, u32[]{:S(2)}, u32[]{:S(2)}) %collective-permute-start.11) | collective-permute-done | bytes 278560 | tf_op jit(solution)/shard_map/ppermute | solution.py:371
  162.3 3.9 %collective-permute-done.12.refs_3_ = bf16[2,2,272,128]{3,2,1,0:T(8,128)(2,1)S(1)} collective-permute-done((bf16[2,2,272,128]{3,2,1,0:T(8,128)(2,1)S(1)}, bf16[2,2,272,128]{3,2,1,0:T(8,128)(2,1)S(1)}, u32[]{:S(2)}, u32[]{:S(2)}) %collective-permute-start.12) | collective-permute-done | bytes 278560 | tf_op jit(solution)/shard_map/ppermute | solution.py:371
  166.1 3.0 %absorb.7 = (bf16[8,2,4,48,512]{4,3,2,1,0:T(8,128)(2,1)}, bf16[8,2,4,224,512]{4,3,2,1,0:T(8,128)(2,1)}) custom-call(s32[1]{0:T(128)} %bitcast.me_ref.at, bf16[2,2,272,128]{3,2,1,0:T(8,128)(2,1)S(1)} %get-tuple-element.43.refs_0_, bf16[2,2,272,128]{3,2,1,0:T(8,128)(2,1)S(1)} %collective-permute-done.10.refs_1_, ...), custom_call_target="tpu_custom_call", output_to_operand_aliasing={{0}: (6, {}), {1}: (7, {})} | custom-call | flops 570425344 | bytes 5570560 | tf_op jit(solution)/shard_map/absorb/pallas_call | solution.py:258
  (26 shorter events, 0.0 us)
Async XLA Ops:
  1.4 3.1 %copy-start.12 = (s32[2,32]{1,0:T(2,128)S(1)}, s32[2,32]{1,0:T(2,128)}, u32[]{:S(2)}) copy-start(s32[2,32]{1,0:T(2,128)} %owners.1) | copy-start | bytes 772
  4.6 8.7 %copy-start.17 = (s32[8,4]{0,1:T(4,128)S(1)}, s32[8,4]{0,1:T(4,128)}, u32[]{:S(2)}) copy-start(s32[8,4]{0,1:T(4,128)} %param.7) | copy-start | bytes 388
  9.0 18.5 %all-to-all-start.2 = ((bf16[8,33,16,128]{3,2,1,0:T(8,128)(2,1)}), bf16[8,33,16,128]{3,2,1,0:T(8,128)(2,1)S(1)}, u32[]{:S(2)}, u32[]{:S(2)}) async-start(bf16[8,33,16,128]{3,2,1,0:T(8,128)(2,1)} %get-tuple-element.32), calls=%async_computation.2 | async-start | bytes 2162688 | tf_op jit(solution)/shard_map/all_to_all | solution.py:314
  13.3 14.9 %copy-start.9 = (s32[8,4]{1,0:T(8,128)}, s32[8,4]{1,0:T(8,128)S(1)}, u32[]{:S(2)}) copy-start(s32[8,4]{1,0:T(8,128)S(1)} %copy.16.mapped) | copy-start | bytes 388
  28.2 0.7 copy-start.13
  28.8 0.7 copy-start.14
  29.5 0.7 copy-start.15
  30.2 15.8 %collective-permute-start.3 = (bf16[8,8,2,16,128]{4,3,2,1,0:T(8,128)(2,1)S(1)}, bf16[8,8,2,16,128]{4,3,2,1,0:T(8,128)(2,1)S(1)}, u32[]{:S(2)}, u32[]{:S(2)}) collective-permute-start(bf16[8,8,2,16,128]{4,3,2,1,0:T(8,128)(2,1)S(1)} %get-tuple-element.36.own_ref.refs_0_), channel_id=1, source_target_pairs={{1,0},{2,1},{3,2},{5,4},{6,5},{7,6},{9,8},{10,9},{11,10},{13,12},{... | collective-permute-start | bytes 1572872 | tf_op jit(solution)/shard_map/ppermute | solution.py:167
  32.5 15.5 %collective-permute-start.2 = (bf16[8,8,2,16,128]{4,3,2,1,0:T(8,128)(2,1)S(1)}, bf16[8,8,2,16,128]{4,3,2,1,0:T(8,128)(2,1)S(1)}, u32[]{:S(2)}, u32[]{:S(2)}) collective-permute-start(bf16[8,8,2,16,128]{4,3,2,1,0:T(8,128)(2,1)S(1)} %get-tuple-element.36.own_ref.refs_0_), channel_id=1, source_target_pairs={{0,1},{1,2},{2,3},{4,5},{5,6},{6,7},{8,9},{9,10},{10,11},{12,13},{... | collective-permute-start | bytes 1572872 | tf_op jit(solution)/shard_map/ppermute | solution.py:166
  36.0 30.4 %all-to-all-start.1 = ((bf16[8,51,16,128]{3,2,1,0:T(8,128)(2,1)}), bf16[8,51,16,128]{3,2,1,0:T(8,128)(2,1)S(1)}, u32[]{:S(2)}, u32[]{:S(2)}) async-start(bf16[8,51,16,128]{3,2,1,0:T(8,128)(2,1)} %get-tuple-element.31), calls=%async_computation.1 | async-start | bytes 3342336 | tf_op jit(solution)/shard_map/all_to_all | solution.py:314
  45.9 19.2 %copy-start = (bf16[8,8,2,16,128]{4,3,2,1,0:T(8,128)(2,1)}, bf16[8,8,2,16,128]{4,3,2,1,0:T(8,128)(2,1)S(1)}, u32[]{:S(2)}) copy-start(bf16[8,8,2,16,128]{4,3,2,1,0:T(8,128)(2,1)S(1)} %collective-permute-done.3.down_ref.refs_1_) | copy-start | bytes 1572868
  48.0 17.1 %copy-start.2 = (bf16[8,8,2,16,128]{4,3,2,1,0:T(8,128)(2,1)}, bf16[8,8,2,16,128]{4,3,2,1,0:T(8,128)(2,1)S(1)}, u32[]{:S(2)}) copy-start(bf16[8,8,2,16,128]{4,3,2,1,0:T(8,128)(2,1)S(1)} %collective-permute-done.2.up_ref.refs_0_) | copy-start | bytes 1572868
  48.9 16.2 %collective-permute-start.4 = (bf16[8,8,2,16,128]{4,3,2,1,0:T(8,128)(2,1)}, bf16[8,8,2,16,128]{4,3,2,1,0:T(8,128)(2,1)}, u32[]{:S(2)}, u32[]{:S(2)}) collective-permute-start(bf16[8,8,2,16,128]{4,3,2,1,0:T(8,128)(2,1)} %pass_on.1), channel_id=1, source_target_pairs={{0,2},{1,0},{2,3},{3,1},{4,6},{5,4},{6,7},{7,5},{8,10},{9,8},{10,1... | collective-permute-start | bytes 1572872 | tf_op jit(solution)/shard_map/ppermute | solution.py:362
  48.9 22.2 %collective-permute-start = (bf16[2,1,272,128]{3,2,1,0:T(8,128)(2,1)}, bf16[2,1,272,128]{3,2,1,0:T(8,128)(2,1)S(1)}, u32[]{:S(2)}, u32[]{:S(2)}) collective-permute-start(bf16[2,1,272,128]{3,2,1,0:T(8,128)(2,1)} %copy-done.15), channel_id=1, source_target_pairs={{0,1},{1,2},{2,3},{3,0},{4,5},{5,6},{6,7},{7,4},{8,9},{9,10},{10,1... | collective-permute-start | bytes 417800 | tf_op jit(solution)/shard_map/ppermute | solution.py:371
  52.1 21.8 %collective-permute-start.1 = (bf16[2,1,272,128]{3,2,1,0:T(8,128)(2,1)}, bf16[2,1,272,128]{3,2,1,0:T(8,128)(2,1)}, u32[]{:S(2)}, u32[]{:S(2)}) collective-permute-start(bf16[2,1,272,128]{3,2,1,0:T(8,128)(2,1)} %copy-done.14), channel_id=1, source_target_pairs={{0,2},{1,3},{2,0},{3,1},{4,6},{5,7},{6,4},{7,5},{8,10},{9,11},{10,... | collective-permute-start | bytes 417800 | tf_op jit(solution)/shard_map/ppermute | solution.py:371
  54.3 31.0 %collective-permute-start.5 = (bf16[2,1,272,128]{3,2,1,0:T(8,128)(2,1)}, bf16[2,1,272,128]{3,2,1,0:T(8,128)(2,1)}, u32[]{:S(2)}, u32[]{:S(2)}) collective-permute-start(bf16[2,1,272,128]{3,2,1,0:T(8,128)(2,1)} %copy-done.13), channel_id=1, source_target_pairs={{0,3},{1,0},{2,1},{3,2},{4,7},{5,4},{6,5},{7,6},{8,11},{9,8},{10,9... | collective-permute-start | bytes 417800 | tf_op jit(solution)/shard_map/ppermute | solution.py:371
  66.4 7.5 %copy-start.10 = (s32[8,4]{1,0:T(8,128)S(1)}, s32[8,4]{1,0:T(8,128)}, u32[]{:S(2)}) copy-start(s32[8,4]{1,0:T(8,128)} %copy-done.9) | copy-start | bytes 388
  66.4 7.5 %copy-start.16 = (bf16[16,128]{1,0:T(8,128)(2,1)S(1)}, bf16[16,128]{1,0:T(8,128)(2,1)}, u32[]{:S(2)}) copy-start(bf16[16,128]{1,0:T(8,128)(2,1)} %token_.1.refs_3_) | copy-start | bytes 12292
  66.4 1.2 copy-start.4
  67.6 29.8 %all-to-all-start = ((bf16[8,68,16,128]{3,2,1,0:T(8,128)(2,1)}), bf16[8,68,16,128]{3,2,1,0:T(8,128)(2,1)S(1)}, u32[]{:S(2)}, u32[]{:S(2)}) async-start(bf16[8,68,16,128]{3,2,1,0:T(8,128)(2,1)} %get-tuple-element.30), calls=%async_computation | async-start | bytes 4456448 | tf_op jit(solution)/shard_map/all_to_all | solution.py:314
  73.9 1.4 copy-start.5
  77.2 0.8 copy-start.6
  77.9 23.6 %collective-permute-start.6 = (bf16[2,3,272,128]{3,2,1,0:T(8,128)(2,1)}, bf16[2,3,272,128]{3,2,1,0:T(8,128)(2,1)}, u32[]{:S(2)}, u32[]{:S(2)}) collective-permute-start(bf16[2,3,272,128]{3,2,1,0:T(8,128)(2,1)} %get-tuple-element.40), channel_id=1, source_target_pairs={{0,1},{1,2},{2,3},{3,0},{4,5},{5,6},{6,7},{7,4},{8,9},{9,10},{10,1... | collective-permute-start | bytes 1253384 | tf_op jit(solution)/shard_map/ppermute | solution.py:371
  77.9 43.2 %collective-permute-start.7 = (bf16[2,3,272,128]{3,2,1,0:T(8,128)(2,1)}, bf16[2,3,272,128]{3,2,1,0:T(8,128)(2,1)}, u32[]{:S(2)}, u32[]{:S(2)}) collective-permute-start(bf16[2,3,272,128]{3,2,1,0:T(8,128)(2,1)} %get-tuple-element.41), channel_id=1, source_target_pairs={{0,2},{1,3},{2,0},{3,1},{4,6},{5,7},{6,4},{7,5},{8,10},{9,11},{10,... | collective-permute-start | bytes 1253384 | tf_op jit(solution)/shard_map/ppermute | solution.py:371
  81.3 49.1 %collective-permute-start.8 = (bf16[2,3,272,128]{3,2,1,0:T(8,128)(2,1)}, bf16[2,3,272,128]{3,2,1,0:T(8,128)(2,1)}, u32[]{:S(2)}, u32[]{:S(2)}) collective-permute-start(bf16[2,3,272,128]{3,2,1,0:T(8,128)(2,1)} %get-tuple-element.42), channel_id=1, source_target_pairs={{0,3},{1,0},{2,1},{3,2},{4,7},{5,4},{6,5},{7,6},{8,11},{9,8},{10,9... | collective-permute-start | bytes 1253384 | tf_op jit(solution)/shard_map/ppermute | solution.py:371
  83.3 47.1 %collective-permute-start.9 = (bf16[8,8,2,16,128]{4,3,2,1,0:T(8,128)(2,1)}, bf16[8,8,2,16,128]{4,3,2,1,0:T(8,128)(2,1)S(1)}, u32[]{:S(2)}, u32[]{:S(2)}) collective-permute-start(bf16[8,8,2,16,128]{4,3,2,1,0:T(8,128)(2,1)} %collective-permute-done.4.refs_2_), channel_id=1, source_target_pairs={{1,0},{2,3},{5,4},{6,7},{9,8},{10,11},{13,12},{14,15},{17,16},{18,... | collective-permute-start | bytes 1572872 | tf_op jit(solution)/shard_map/ppermute | solution.py:365
  97.4 1.0 copy-start.7
  98.4 0.7 copy-start.11
  99.9 33.1 %collective-permute-start.13 = (bf16[2,2,272,128]{3,2,1,0:T(8,128)(2,1)S(1)}, bf16[2,2,272,128]{3,2,1,0:T(8,128)(2,1)S(1)}, u32[]{:S(2)}, u32[]{:S(2)}) collective-permute-start(bf16[2,2,272,128]{3,2,1,0:T(8,128)(2,1)S(1)} %get-tuple-element.47), channel_id=1, source_target_pairs={{0,1},{1,2},{2,3},{3,0},{4,5},{5,6},{6,7},{7,4},{8,9},{9,10},{10,1... | collective-permute-start | bytes 835592 | tf_op jit(solution)/shard_map/ppermute | solution.py:371
  101.5 44.7 %collective-permute-start.14 = (bf16[2,2,272,128]{3,2,1,0:T(8,128)(2,1)S(1)}, bf16[2,2,272,128]{3,2,1,0:T(8,128)(2,1)S(1)}, u32[]{:S(2)}, u32[]{:S(2)}) collective-permute-start(bf16[2,2,272,128]{3,2,1,0:T(8,128)(2,1)S(1)} %get-tuple-element.48), channel_id=1, source_target_pairs={{0,2},{1,3},{2,0},{3,1},{4,6},{5,7},{6,4},{7,5},{8,10},{9,11},{10,... | collective-permute-start | bytes 835592 | tf_op jit(solution)/shard_map/ppermute | solution.py:371
  121.2 33.1 %collective-permute-start.15 = (bf16[2,2,272,128]{3,2,1,0:T(8,128)(2,1)S(1)}, bf16[2,2,272,128]{3,2,1,0:T(8,128)(2,1)S(1)}, u32[]{:S(2)}, u32[]{:S(2)}) collective-permute-start(bf16[2,2,272,128]{3,2,1,0:T(8,128)(2,1)S(1)} %get-tuple-element.49), channel_id=1, source_target_pairs={{0,3},{1,0},{2,1},{3,2},{4,7},{5,4},{6,5},{7,6},{8,11},{9,8},{10,9... | collective-permute-start | bytes 835592 | tf_op jit(solution)/shard_map/ppermute | solution.py:371
  130.4 3.0 %copy-start.1 = (bf16[8,8,2,16,128]{4,3,2,1,0:T(8,128)(2,1)S(1)}, bf16[8,8,2,16,128]{4,3,2,1,0:T(8,128)(2,1)}, u32[]{:S(2)}) copy-start(bf16[8,8,2,16,128]{4,3,2,1,0:T(8,128)(2,1)} %copy-done) | copy-start | bytes 1572868
  130.4 3.0 %copy-start.3 = (bf16[8,8,2,16,128]{4,3,2,1,0:T(8,128)(2,1)S(1)}, bf16[8,8,2,16,128]{4,3,2,1,0:T(8,128)(2,1)}, u32[]{:S(2)}) copy-start(bf16[8,8,2,16,128]{4,3,2,1,0:T(8,128)(2,1)} %copy-done.2) | copy-start | bytes 1572868
  131.3 25.9 %collective-permute-start.10 = (bf16[2,2,272,128]{3,2,1,0:T(8,128)(2,1)S(1)}, bf16[2,2,272,128]{3,2,1,0:T(8,128)(2,1)S(1)}, u32[]{:S(2)}, u32[]{:S(2)}) collective-permute-start(bf16[2,2,272,128]{3,2,1,0:T(8,128)(2,1)S(1)} %get-tuple-element.44), channel_id=1, source_target_pairs={{0,1},{1,2},{2,3},{3,0},{4,5},{5,6},{6,7},{7,4},{8,9},{9,10},{10,1... | collective-permute-start | bytes 835592 | tf_op jit(solution)/shard_map/ppermute | solution.py:371
  131.4 30.9 %collective-permute-start.11 = (bf16[2,2,272,128]{3,2,1,0:T(8,128)(2,1)S(1)}, bf16[2,2,272,128]{3,2,1,0:T(8,128)(2,1)S(1)}, u32[]{:S(2)}, u32[]{:S(2)}) collective-permute-start(bf16[2,2,272,128]{3,2,1,0:T(8,128)(2,1)S(1)} %get-tuple-element.45), channel_id=1, source_target_pairs={{0,2},{1,3},{2,0},{3,1},{4,6},{5,7},{6,4},{7,5},{8,10},{9,11},{10,... | collective-permute-start | bytes 835592 | tf_op jit(solution)/shard_map/ppermute | solution.py:371
  133.0 33.1 %collective-permute-start.12 = (bf16[2,2,272,128]{3,2,1,0:T(8,128)(2,1)S(1)}, bf16[2,2,272,128]{3,2,1,0:T(8,128)(2,1)S(1)}, u32[]{:S(2)}, u32[]{:S(2)}) collective-permute-start(bf16[2,2,272,128]{3,2,1,0:T(8,128)(2,1)S(1)} %get-tuple-element.46), channel_id=1, source_target_pairs={{0,3},{1,0},{2,1},{3,2},{4,7},{5,4},{6,5},{7,6},{8,11},{9,8},{10,9... | collective-permute-start | bytes 835592 | tf_op jit(solution)/shard_map/ppermute | solution.py:371
  133.5 7.1 %copy-start.8 = (bf16[2,3,272,128]{3,2,1,0:T(8,128)(2,1)S(1)}, bf16[2,3,272,128]{3,2,1,0:T(8,128)(2,1)}, u32[]{:S(2)}) copy-start(bf16[2,3,272,128]{3,2,1,0:T(8,128)(2,1)} %copy-done.6) | copy-start | bytes 1253380

commit v13 on v10

--- a/solution.py
+++ b/solution.py
@@ -15,9 +15,10 @@
 V_DIM = 128
 LANES = 128
 QUERY, KEY, VALUE, OUT = range(4)
-CUT_MICROS = 10
-TOKEN_MICROS = 20
-CUTS = (0, 1, 4, 6, 8)
+CUT_MICROS = 30
+TOKEN_MICROS = 40
+CUTS = (0, 2, 5, 8)
+GROUPS = (0, 1, 2, 3)
 VMEM_LIMIT = 16 * 1024 * 1024
 
 
@@ -105,17 +106,15 @@
     return pl.BlockSpec(corner_of(x), lambda _: (0,) * x.ndim)
 
 
-def cut(rows, slice_map, blocks, ahead, item_rows, waits, micros):
+def cut(rows, slice_map, blocks, ahead, first, items, item_rows, waits, micros):
     t_ways = slice_map.shape[1]
-    first = math.prod(ahead)
-    items = (rows.shape[1] - first) // item_rows
-    shapes = [(rows.shape[0],) + ahead + rows.shape[2:]] if first else []
+    shapes = [(rows.shape[0],) + ahead + rows.shape[2:]] if ahead else []
     shapes += [(blocks, items, item_rows) + rows.shape[2:]] * t_ways
 
     def kernel(mapped, source, *refs):
         f_me, t_me = lax.axis_index("fsdp"), lax.axis_index("tp")
         refs = refs[len(waits) :]
-        if first:
+        if ahead:
             for f in range(rows.shape[0]):
                 for item in range(ahead[0]):
                     for kind in range(ahead[1]):
@@ -316,28 +315,49 @@
     cuts = [item_count * eighths // 8 for eighths in CUTS]
     chunks = [range(low, high) for low, high in zip(cuts, cuts[1:]) if low < high]
 
-    def packed(parts):
-        return pack(table, param_offsets, owner_map, f_ways, widths, granule, parts)
-
     def over_fsdp(x):
         x = lax.all_to_all(x, "fsdp", split_axis=0, concat_axis=0, tiled=True)
         return x.reshape(f_ways, -1, LANES)
 
-    first_parts = [[(range(item_count), (KEY, VALUE)), (chunks[0], (QUERY, OUT))]]
-    other_parts = [[(items, (QUERY, OUT))] for items in chunks[1:]]
-    to_send = packed(first_parts + other_parts)
+    groups = [chunks[low:high] for low, high in zip(GROUPS, GROUPS[1:]) if chunks[low:high]]
+    to_send = pack(
+        table,
+        param_offsets,
+        owner_map,
+        f_ways,
+        widths,
+        granule,
+        [
+            ([] if at else [(range(item_count), (KEY, VALUE))])
+            + [(items, (QUERY, OUT)) for items in group]
+            for at, group in enumerate(groups)
+        ],
+    )
 
     exchanged, sent = [], []
     for at in range(len(chunks)):
-        rows = over_fsdp(to_send[at])
+        group = [at in range(low, high) for low, high in zip(GROUPS, GROUPS[1:])].index(True)
+        if at == GROUPS[group]:
+            rows, first = over_fsdp(to_send[group]), 0 if at else math.prod(ahead)
         waits = sent[at - 1][:1] if at else []
         if at >= 2:
             waits = waits + exchanged[at - 2][1:]
-        if at == 1:
-            waits = waits + exchanged[0][1:3]
         if t_ways == 4 and at == 1:
             waits = waits + [near, passed]
-        pieces = list(cut(rows, slice_map, blocks, ahead if at == 0 else (0,), item_rows, waits, CUT_MICROS))
+        pieces = list(
+            cut(
+                rows,
+                slice_map,
+                blocks,
+                () if at else ahead,
+                first,
+                len(chunks[at]),
+                item_rows,
+                waits,
+                CUT_MICROS,
+            )
+        )
+        first += len(chunks[at]) * item_rows
         if at == 0:
             pairs = pieces.pop(0)
             up, down = neighbours(pairs, "tp", t_ways)

time: 165 us -> 164 us (level)
  waiting for transfers between devices: 48.5 us -> 74.8 us
  starting transfers between devices: 74.1 us -> 53.6 us
  Pallas kernels: 31.3 us -> 28.3 us
  local copies, waits for them, and re-layouts: 6.65 us -> 4.03 us
    ppermute x12 -> x9, waiting for transfers between devices: 16.3 us -> 33.9 us  [per_device(): lax.ppermute(piece, 'tp', [(i, (i + shift) % t_ways) for i in range(t_way...]
    ppermute x12 -> x9, starting transfers between devices: 43.6 us -> 27.4 us  [per_device(): lax.ppermute(piece, 'tp', [(i, (i + shift) % t_ways) for i in range(t_way...]
    all_to_all x4 -> x3, waiting for transfers between devices: 21.3 us -> 30 us  [over_fsdp(): x = lax.all_to_all(x, 'fsdp', split_axis=0, concat_axis=0, tiled=True)]
    all_to_all x4 -> x3, starting transfers between devices: 19.3 us -> 15 us  [over_fsdp(): x = lax.all_to_all(x, 'fsdp', split_axis=0, concat_axis=0, tiled=True)]
    unnamed x39 -> x27, local copies, waits for them, and re-layouts: 6.65 us -> 4.03 us
    pallas_call x4 -> x3, Pallas kernels: 15 us -> 12.4 us  [absorb(): pl.pallas_call(kernel, grid_spec=pltpu.PrefetchScalarGridSpec(num_scalar_...]
    pallas_call x4 -> x3, Pallas kernels: 5.88 us -> 5.03 us  [cut(): pl.pallas_call(kernel, grid=(1,), out_shape=[jax.ShapeDtypeStruct(shape,...]
  transfers between devices with their start and end apart: 20 -> 16, of which waited for: 9 -> 11; matrix products, arithmetic and copies ran while one was open for 1% -> 1% of each run, Pallas kernels for 14% -> 11%
where the time goes in v13:
time: 164 us; the launch traced here: 163 us
  waiting for transfers between devices  74.8 us (46%)
  starting transfers between devices  53.6 us (33%)
  Pallas kernels  28.3 us (17%)
  local copies, waits for them, and re-layouts  4.03 us (2%)
    ppermute x9, waiting for transfers between devices, per_device(): lax.ppermute(piece, 'tp', [(i, (i + shift) % t_ways) for i in range(t_way...  33.9 us
    all_to_all x3, waiting for transfers between devices, over_fsdp(): x = lax.all_to_all(x, 'fsdp', split_axis=0, concat_axis=0, tiled=True)  30 us
    ppermute x9, starting transfers between devices, per_device(): lax.ppermute(piece, 'tp', [(i, (i + shift) % t_ways) for i in range(t_way...  27.4 us
    all_to_all x3, starting transfers between devices, over_fsdp(): x = lax.all_to_all(x, 'fsdp', split_axis=0, concat_axis=0, tiled=True)  15 us
    pallas_call x3, Pallas kernels, absorb(): pl.pallas_call(kernel, grid_spec=pltpu.PrefetchScalarGridSpec(num_scalar_...  12.4 us
    ppermute x1, waiting for transfers between devices, neighbours(): lax.ppermute(x, axis, [(i + 1, i) for i in range(ways - 1)])  10.8 us
    ppermute x1, starting transfers between devices, neighbours(): lax.ppermute(x, axis, [(i + 1, i) for i in range(ways - 1)])  5.59 us
    pallas_call x3, Pallas kernels, cut(): pl.pallas_call(kernel, grid=(1,), out_shape=[jax.ShapeDtypeStruct(shape,...  5.03 us
  transfers between devices with their start and end apart: 16, of which 11 were waited for; matrix products, arithmetic and copies ran while one was open for 1% of the time, Pallas kernels for 11%

profile of v13, /device:TPU:10, one launch (start us, length us, event | category | flops | bytes accessed | tf_op | source)
XLA Modules:
  0.0 163.0 jit_solution(5121994172399691356)
XLA Ops:
  0.6 0.8 copy.10.offsets
  1.4 0.0 copy-start.6
  1.4 3.1 %copy.14 = bf16[1,2,9728,128]{3,2,1,0:T(8,128)(2,1)S(1)} copy(bf16[1,2,9728,128]{3,1,2,0:T(2,128)(2,1)} %bitcast.24) | data formatting | bytes 9961472
  4.5 0.0 copy-done.6
  4.6 0.0 copy-start.11
  4.6 4.4 %pack.1 = (bf16[8,50,16,128]{3,2,1,0:T(8,128)(2,1)}, bf16[8,51,16,128]{3,2,1,0:T(8,128)(2,1)}, bf16[8,51,16,128]{3,2,1,0:T(8,128)(2,1)}) custom-call(s32[2,32,4]{2,1,0:T(8,128)S(1)} %copy.10.offsets, s32[2,32]{1,0:T(2,128)S(1)} %copy-done.6, bf16[2,608,16,128]{3,2,1,0:T(8,128)(2,1)S(1)} %bitcast.19), custom_call_target="tpu_custom_call" | custom-call | bytes 9961472 | tf_op jit(solution)/shard_map/pack/pallas_call | solution.py:78
  9.0 4.3 %all-to-all-start.2 = ((bf16[8,50,16,128]{3,2,1,0:T(8,128)(2,1)}), bf16[8,50,16,128]{3,2,1,0:T(8,128)(2,1)S(1)}, u32[]{:S(2)}, u32[]{:S(2)}) async-start(bf16[8,50,16,128]{3,2,1,0:T(8,128)(2,1)} %get-tuple-element.26), calls=%async_computation.2 | async-start | bytes 3276800 | tf_op jit(solution)/shard_map/all_to_all | solution.py:319
  13.2 0.0 copy-done.11
  13.2 0.1 copy.13.mapped
  13.3 20.1 %all-to-all-done.2 = bf16[8,50,16,128]{3,2,1,0:T(8,128)(2,1)S(1)} async-done(((bf16[8,50,16,128]{3,2,1,0:T(8,128)(2,1)}), bf16[8,50,16,128]{3,2,1,0:T(8,128)(2,1)S(1)}, u32[]{:S(2)}, u32[]{:S(2)}) %all-to-all-start.2) | async-done | bytes 1638432 | tf_op jit(solution)/shard_map/all_to_all | solution.py:319
  33.5 1.5 cut.3
  35.0 0.0 copy-start.7
  35.0 0.0 copy-start.8
  35.0 0.0 copy-start.9
  35.0 1.3 collective-permute-start.2
  36.3 0.0 copy-done.7
  36.3 5.6 %collective-permute-start.1 = (bf16[8,8,2,16,128]{4,3,2,1,0:T(8,128)(2,1)}, bf16[8,8,2,16,128]{4,3,2,1,0:T(8,128)(2,1)S(1)}, u32[]{:S(2)}, u32[]{:S(2)}) collective-permute-start(bf16[8,8,2,16,128]{4,3,2,1,0:T(8,128)(2,1)} %get-tuple-element.28.refs_0_), channel_id=1, source_target_pairs={{1,0},{2,1},{3,2},{5,4},{6,5},{7,6},{9,8},{10,9},{11,10},{13,12},{... | collective-permute-start | bytes 1572872 | tf_op jit(solution)/shard_map/ppermute | solution.py:167
  41.9 1.9 %collective-permute-start = (bf16[8,8,2,16,128]{4,3,2,1,0:T(8,128)(2,1)}, bf16[8,8,2,16,128]{4,3,2,1,0:T(8,128)(2,1)S(1)}, u32[]{:S(2)}, u32[]{:S(2)}) collective-permute-start(bf16[8,8,2,16,128]{4,3,2,1,0:T(8,128)(2,1)} %get-tuple-element.28.refs_0_), channel_id=1, source_target_pairs={{0,1},{1,2},{2,3},{4,5},{5,6},{6,7},{8,9},{9,10},{10,11},{12,13},{... | collective-permute-start | bytes 1572872 | tf_op jit(solution)/shard_map/ppermute | solution.py:166
  43.8 0.0 copy-done.8
  43.8 0.0 copy-done.9
  43.8 5.0 %all-to-all-start.1 = ((bf16[8,51,16,128]{3,2,1,0:T(8,128)(2,1)}), bf16[8,51,16,128]{3,2,1,0:T(8,128)(2,1)S(1)}, u32[]{:S(2)}, u32[]{:S(2)}) async-start(bf16[8,51,16,128]{3,2,1,0:T(8,128)(2,1)} %get-tuple-element.25), calls=%async_computation.1 | async-start | bytes 3342336 | tf_op jit(solution)/shard_map/all_to_all | solution.py:319
  48.8 0.0 collective-permute-start.3
  48.8 4.4 %collective-permute-start.4 = (bf16[2,2,272,128]{3,2,1,0:T(8,128)(2,1)}, bf16[2,2,272,128]{3,2,1,0:T(8,128)(2,1)}, u32[]{:S(2)}, u32[]{:S(2)}) collective-permute-start(bf16[2,2,272,128]{3,2,1,0:T(8,128)(2,1)} %copy-done.8), channel_id=1, source_target_pairs={{0,2},{1,3},{2,0},{3,1},{4,6},{5,7},{6,4},{7,5},{8,10},{9,11},{10,... | collective-permute-start | bytes 835592 | tf_op jit(solution)/shard_map/ppermute | solution.py:373
  53.2 0.0 collective-permute-done.2.refs_2_.first
  53.2 0.0 copy-start
  53.2 0.0 collective-permute-start.5
  53.2 10.8 %collective-permute-done.1.refs_1_.below = bf16[8,8,2,16,128]{4,3,2,1,0:T(8,128)(2,1)S(1)} collective-permute-done((bf16[8,8,2,16,128]{4,3,2,1,0:T(8,128)(2,1)}, bf16[8,8,2,16,128]{4,3,2,1,0:T(8,128)(2,1)S(1)}, u32[]{:S(2)}, u32[]{:S(2)}) %collective-permute-start.1) | collective-permute-done | bytes 524320 | tf_op jit(solution)/shard_map/ppermute | solution.py:167
  64.1 0.1 collective-permute-done.refs_0_.above
  64.1 1.2 pass_on.1.refs_2_
  65.3 2.5 %collective-permute-start.9 = (bf16[2,8,8,2,16,128]{5,4,3,2,1,0:T(8,128)(2,1)}, bf16[2,8,8,2,16,128]{5,4,3,2,1,0:T(8,128)(2,1)}, u32[]{:S(2)}, u32[]{:S(2)}) collective-permute-start(bf16[2,8,8,2,16,128]{5,4,3,2,1,0:T(8,128)(2,1)} %pass_on.1.refs_2_), channel_id=1, source_target_pairs={{1,0},{2,3},{5,4},{6,7},{9,8},{10,11},{13,12},{14,15},{17,16},{18,... | collective-permute-start | bytes 3145736 | tf_op jit(solution)/shard_map/ppermute | solution.py:368
  67.8 0.0 copy-done
  67.8 0.0 copy-done.2
  67.8 0.0 copy-done.4
  67.8 1.3 token_.1.refs_1_
  69.1 0.3 all-to-all-done.1
  69.4 5.7 %all-to-all-start = ((bf16[8,51,16,128]{3,2,1,0:T(8,128)(2,1)}), bf16[8,51,16,128]{3,2,1,0:T(8,128)(2,1)}, u32[]{:S(2)}, u32[]{:S(2)}) async-start(bf16[8,51,16,128]{3,2,1,0:T(8,128)(2,1)} %get-tuple-element.24), calls=%async_computation | async-start | bytes 3342336 | tf_op jit(solution)/shard_map/all_to_all | solution.py:319
  75.1 0.0 copy-done.10
  75.1 1.8 %cut.4 = (bf16[2,3,272,128]{3,2,1,0:T(8,128)(2,1)S(1)}, bf16[2,3,272,128]{3,2,1,0:T(8,128)(2,1)}, bf16[2,3,272,128]{3,2,1,0:T(8,128)(2,1)}, bf16[2,3,272,128]{3,2,1,0:T(8,128)(2,1)}) custom-call(s32[8,4]{1,0:T(8,128)S(1)} %copy.13.mapped, bf16[8,816,128]{2,1,0:T(8,128)(2,1)S(1)} %bitcast.20, bf16[2,2,272,128]{3,2,1,0:T(8,128)(2,1)S(1)} %get-tuple-element.27.refs_0_, ...), custom_call_target="tpu_custom_call" | custom-call | flops 34500001792 | bytes 3342336 | tf_op jit(solution)/shard_map/cut/pallas_call | solution.py:131
  77.0 0.2 collective-permute-start.10
  77.1 0.0 collective-permute-done.3.refs_1_
  77.1 4.3 %collective-permute-start.11 = (bf16[2,3,272,128]{3,2,1,0:T(8,128)(2,1)}, bf16[2,3,272,128]{3,2,1,0:T(8,128)(2,1)S(1)}, u32[]{:S(2)}, u32[]{:S(2)}) collective-permute-start(bf16[2,3,272,128]{3,2,1,0:T(8,128)(2,1)} %get-tuple-element.38), channel_id=1, source_target_pairs={{0,2},{1,3},{2,0},{3,1},{4,6},{5,7},{6,4},{7,5},{8,10},{9,11},{10,... | collective-permute-start | bytes 1253384 | tf_op jit(solution)/shard_map/ppermute | solution.py:373
  81.4 4.9 %collective-permute-done.4.refs_2_ = bf16[2,2,272,128]{3,2,1,0:T(8,128)(2,1)} collective-permute-done((bf16[2,2,272,128]{3,2,1,0:T(8,128)(2,1)}, bf16[2,2,272,128]{3,2,1,0:T(8,128)(2,1)}, u32[]{:S(2)}, u32[]{:S(2)}) %collective-permute-start.4) | collective-permute-done | bytes 278560 | tf_op jit(solution)/shard_map/ppermute | solution.py:373
  86.3 0.0 collective-permute-start.12
  86.3 9.5 %all-to-all-done = bf16[8,51,16,128]{3,2,1,0:T(8,128)(2,1)} async-done(((bf16[8,51,16,128]{3,2,1,0:T(8,128)(2,1)}), bf16[8,51,16,128]{3,2,1,0:T(8,128)(2,1)}, u32[]{:S(2)}, u32[]{:S(2)}) %all-to-all-start) | async-done | bytes 1671200 | tf_op jit(solution)/shard_map/all_to_all | solution.py:319
  95.8 9.3 %collective-permute-done.5.refs_3_ = bf16[2,2,272,128]{3,2,1,0:T(8,128)(2,1)} collective-permute-done((bf16[2,2,272,128]{3,2,1,0:T(8,128)(2,1)}, bf16[2,2,272,128]{3,2,1,0:T(8,128)(2,1)}, u32[]{:S(2)}, u32[]{:S(2)}) %collective-permute-start.5) | collective-permute-done | bytes 278560 | tf_op jit(solution)/shard_map/ppermute | solution.py:373
  105.1 1.7 %cut.5 = (bf16[2,3,272,128]{3,2,1,0:T(8,128)(2,1)S(1)}, bf16[2,3,272,128]{3,2,1,0:T(8,128)(2,1)S(1)}, bf16[2,3,272,128]{3,2,1,0:T(8,128)(2,1)S(1)}, bf16[2,3,272,128]{3,2,1,0:T(8,128)(2,1)S(1)}) custom-call(s32[8,4]{1,0:T(8,128)S(1)} %copy.13.mapped, bf16[8,816,128]{2,1,0:T(8,128)(2,1)} %bitcast.1.source, ...), custom_call_target="tpu_custom_call" | custom-call | flops 34500001792 | bytes 3342336 | tf_op jit(solution)/shard_map/cut/pallas_call | solution.py:131
  106.8 0.1 collective-permute-start.6
  106.9 6.3 %collective-permute-done.10.refs_1_ = bf16[2,3,272,128]{3,2,1,0:T(8,128)(2,1)S(1)} collective-permute-done((bf16[2,3,272,128]{3,2,1,0:T(8,128)(2,1)}, bf16[2,3,272,128]{3,2,1,0:T(8,128)(2,1)S(1)}, u32[]{:S(2)}, u32[]{:S(2)}) %collective-permute-start.10) | collective-permute-done | bytes 417824 | tf_op jit(solution)/shard_map/ppermute | solution.py:373
  113.2 18.5 %collective-permute-start.7 = (bf16[2,3,272,128]{3,2,1,0:T(8,128)(2,1)S(1)}, bf16[2,3,272,128]{3,2,1,0:T(8,128)(2,1)S(1)}, u32[]{:S(2)}, u32[]{:S(2)}) collective-permute-start(bf16[2,3,272,128]{3,2,1,0:T(8,128)(2,1)S(1)} %get-tuple-element.35), channel_id=1, source_target_pairs={{0,2},{1,3},{2,0},{3,1},{4,6},{5,7},{6,4},{7,5},{8,10},{9,11},{10,... | collective-permute-start | bytes 1253384 | tf_op jit(solution)/shard_map/ppermute | solution.py:373
  131.7 0.0 collective-permute-done.9
  131.7 0.0 collective-permute-start.8
  131.7 0.0 copy-done.1
  131.7 0.0 copy-done.3
  131.7 0.0 copy-done.5
  131.7 1.4 broadcast_select_fusion
  133.1 4.0 %assemble.1.refs_4_ = bf16[8,2,128,512]{3,2,1,0:T(8,128)(2,1)S(1)} custom-call(s32[1]{0:T(128)} %bitcast.me_ref.at, bf16[8,8,2,16,128]{4,3,2,1,0:T(8,128)(2,1)} %get-tuple-element.28.refs_0_, bf16[8,8,2,16,128]{4,3,2,1,0:T(8,128)(2,1)S(1)} %get-tuple-element.48.refs_1_, bf16[8,8,2,16,128]{4,3,2,1,0:T(8,128)(2,1)S(1)} %get-tuple-element.47.refs_2_, ...), custom_call_target="tpu_custom_call" | custom-call | tf_op jit(solution)/shard_map/assemble/pallas_call | solution.py:220
  137.1 4.0 %absorb.3 = (bf16[8,2,4,48,512]{4,3,2,1,0:T(8,128)(2,1)}, bf16[8,2,4,224,512]{4,3,2,1,0:T(8,128)(2,1)}) custom-call(s32[1]{0:T(128)} %bitcast.me_ref.at, bf16[2,2,272,128]{3,2,1,0:T(8,128)(2,1)S(1)} %get-tuple-element.27.refs_0_, bf16[2,2,272,128]{3,2,1,0:T(8,128)(2,1)} %collective-permute-done.3.refs_1_, ...), custom_call_target="tpu_custom_call" | custom-call | flops 570425344 | bytes 5570560 | tf_op jit(solution)/shard_map/absorb/pallas_call | solution.py:263
  141.1 0.0 collective-permute-done.11.refs_2_
  141.1 0.0 collective-permute-done.12.refs_3_
  141.1 4.2 %absorb.4 = (bf16[8,2,4,48,512]{4,3,2,1,0:T(8,128)(2,1)}, bf16[8,2,4,224,512]{4,3,2,1,0:T(8,128)(2,1)}) custom-call(s32[1]{0:T(128)} %bitcast.me_ref.at, bf16[2,3,272,128]{3,2,1,0:T(8,128)(2,1)S(1)} %get-tuple-element.29.refs_0_, bf16[2,3,272,128]{3,2,1,0:T(8,128)(2,1)S(1)} %collective-permute-done.10.refs_1_, ...), custom_call_target="tpu_custom_call", output_to_operand_aliasing={{0}: (6, {}), {1}: (7, {})} | custom-call | flops 855638016 | bytes 8355840 | tf_op jit(solution)/shard_map/absorb/pallas_call | solution.py:263
  145.3 3.6 %collective-permute-done.6.refs_1_ = bf16[2,3,272,128]{3,2,1,0:T(8,128)(2,1)S(1)} collective-permute-done((bf16[2,3,272,128]{3,2,1,0:T(8,128)(2,1)S(1)}, bf16[2,3,272,128]{3,2,1,0:T(8,128)(2,1)S(1)}, u32[]{:S(2)}, u32[]{:S(2)}) %collective-permute-start.6) | collective-permute-done | bytes 417824 | tf_op jit(solution)/shard_map/ppermute | solution.py:373
  148.9 8.9 %collective-permute-done.7.refs_2_ = bf16[2,3,272,128]{3,2,1,0:T(8,128)(2,1)S(1)} collective-permute-done((bf16[2,3,272,128]{3,2,1,0:T(8,128)(2,1)S(1)}, bf16[2,3,272,128]{3,2,1,0:T(8,128)(2,1)S(1)}, u32[]{:S(2)}, u32[]{:S(2)}) %collective-permute-start.7) | collective-permute-done | bytes 417824 | tf_op jit(solution)/shard_map/ppermute | solution.py:373
  157.8 0.9 collective-permute-done.8.refs_3_
  158.7 4.2 %absorb.5 = (bf16[8,2,4,48,512]{4,3,2,1,0:T(8,128)(2,1)}, bf16[8,2,4,224,512]{4,3,2,1,0:T(8,128)(2,1)}) custom-call(s32[1]{0:T(128)} %bitcast.me_ref.at, bf16[2,3,272,128]{3,2,1,0:T(8,128)(2,1)S(1)} %get-tuple-element.33.refs_0_, bf16[2,3,272,128]{3,2,1,0:T(8,128)(2,1)S(1)} %collective-permute-done.6.refs_1_, ...), custom_call_target="tpu_custom_call", output_to_operand_aliasing={{0}: (6, {}), {1}: (7, {})} | custom-call | flops 855638016 | bytes 8355840 | tf_op jit(solution)/shard_map/absorb/pallas_call | solution.py:263
  (6 shorter events, 0.0 us)
Async XLA Ops:
  1.4 3.1 %copy-start.6 = (s32[2,32]{1,0:T(2,128)S(1)}, s32[2,32]{1,0:T(2,128)}, u32[]{:S(2)}) copy-start(s32[2,32]{1,0:T(2,128)} %owners.1) | copy-start | bytes 772
  4.6 8.7 %copy-start.11 = (s32[8,4]{0,1:T(4,128)S(1)}, s32[8,4]{0,1:T(4,128)}, u32[]{:S(2)}) copy-start(s32[8,4]{0,1:T(4,128)} %param.7) | copy-start | bytes 388
  9.0 24.5 %all-to-all-start.2 = ((bf16[8,50,16,128]{3,2,1,0:T(8,128)(2,1)}), bf16[8,50,16,128]{3,2,1,0:T(8,128)(2,1)S(1)}, u32[]{:S(2)}, u32[]{:S(2)}) async-start(bf16[8,50,16,128]{3,2,1,0:T(8,128)(2,1)} %get-tuple-element.26), calls=%async_computation.2 | async-start | bytes 3276800 | tf_op jit(solution)/shard_map/all_to_all | solution.py:319
  35.0 1.3 copy-start.7
  35.0 8.8 %copy-start.8 = (bf16[2,2,272,128]{3,2,1,0:T(8,128)(2,1)}, bf16[2,2,272,128]{3,2,1,0:T(8,128)(2,1)S(1)}, u32[]{:S(2)}) copy-start(bf16[2,2,272,128]{3,2,1,0:T(8,128)(2,1)S(1)} %get-tuple-element.31) | copy-start | bytes 835588
  35.0 8.8 %copy-start.9 = (bf16[2,2,272,128]{3,2,1,0:T(8,128)(2,1)}, bf16[2,2,272,128]{3,2,1,0:T(8,128)(2,1)S(1)}, u32[]{:S(2)}) copy-start(bf16[2,2,272,128]{3,2,1,0:T(8,128)(2,1)S(1)} %get-tuple-element.30) | copy-start | bytes 835588
  35.0 18.3 %collective-permute-start.2 = (bf16[8,8,2,16,128]{4,3,2,1,0:T(8,128)(2,1)}, bf16[8,8,2,16,128]{4,3,2,1,0:T(8,128)(2,1)S(1)}, u32[]{:S(2)}, u32[]{:S(2)}) collective-permute-start(bf16[8,8,2,16,128]{4,3,2,1,0:T(8,128)(2,1)} %get-tuple-element.28.refs_0_), channel_id=1, source_target_pairs={{0,2},{3,1},{4,6},{7,5},{8,10},{11,9},{12,14},{15,13},{16,18},{19,... | collective-permute-start | bytes 1572872 | tf_op jit(solution)/shard_map/ppermute | solution.py:365
  36.3 27.8 %collective-permute-start.1 = (bf16[8,8,2,16,128]{4,3,2,1,0:T(8,128)(2,1)}, bf16[8,8,2,16,128]{4,3,2,1,0:T(8,128)(2,1)S(1)}, u32[]{:S(2)}, u32[]{:S(2)}) collective-permute-start(bf16[8,8,2,16,128]{4,3,2,1,0:T(8,128)(2,1)} %get-tuple-element.28.refs_0_), channel_id=1, source_target_pairs={{1,0},{2,1},{3,2},{5,4},{6,5},{7,6},{9,8},{10,9},{11,10},{13,12},{... | collective-permute-start | bytes 1572872 | tf_op jit(solution)/shard_map/ppermute | solution.py:167
  41.9 22.3 %collective-permute-start = (bf16[8,8,2,16,128]{4,3,2,1,0:T(8,128)(2,1)}, bf16[8,8,2,16,128]{4,3,2,1,0:T(8,128)(2,1)S(1)}, u32[]{:S(2)}, u32[]{:S(2)}) collective-permute-start(bf16[8,8,2,16,128]{4,3,2,1,0:T(8,128)(2,1)} %get-tuple-element.28.refs_0_), channel_id=1, source_target_pairs={{0,1},{1,2},{2,3},{4,5},{5,6},{6,7},{8,9},{9,10},{10,11},{12,13},{... | collective-permute-start | bytes 1572872 | tf_op jit(solution)/shard_map/ppermute | solution.py:166
  43.8 25.6 %all-to-all-start.1 = ((bf16[8,51,16,128]{3,2,1,0:T(8,128)(2,1)}), bf16[8,51,16,128]{3,2,1,0:T(8,128)(2,1)S(1)}, u32[]{:S(2)}, u32[]{:S(2)}) async-start(bf16[8,51,16,128]{3,2,1,0:T(8,128)(2,1)} %get-tuple-element.25), calls=%async_computation.1 | async-start | bytes 3342336 | tf_op jit(solution)/shard_map/all_to_all | solution.py:319
  48.8 28.3 %collective-permute-start.3 = (bf16[2,2,272,128]{3,2,1,0:T(8,128)(2,1)}, bf16[2,2,272,128]{3,2,1,0:T(8,128)(2,1)}, u32[]{:S(2)}, u32[]{:S(2)}) collective-permute-start(bf16[2,2,272,128]{3,2,1,0:T(8,128)(2,1)} %copy-done.9), channel_id=1, source_target_pairs={{0,1},{1,2},{2,3},{3,0},{4,5},{5,6},{6,7},{7,4},{8,9},{9,10},{10,1... | collective-permute-start | bytes 835592 | tf_op jit(solution)/shard_map/ppermute | solution.py:373
  48.8 37.5 %collective-permute-start.4 = (bf16[2,2,272,128]{3,2,1,0:T(8,128)(2,1)}, bf16[2,2,272,128]{3,2,1,0:T(8,128)(2,1)}, u32[]{:S(2)}, u32[]{:S(2)}) collective-permute-start(bf16[2,2,272,128]{3,2,1,0:T(8,128)(2,1)} %copy-done.8), channel_id=1, source_target_pairs={{0,2},{1,3},{2,0},{3,1},{4,6},{5,7},{6,4},{7,5},{8,10},{9,11},{10,... | collective-permute-start | bytes 835592 | tf_op jit(solution)/shard_map/ppermute | solution.py:373
  53.2 14.6 %copy-start = (bf16[8,8,2,16,128]{4,3,2,1,0:T(8,128)(2,1)}, bf16[8,8,2,16,128]{4,3,2,1,0:T(8,128)(2,1)S(1)}, u32[]{:S(2)}) copy-start(bf16[8,8,2,16,128]{4,3,2,1,0:T(8,128)(2,1)S(1)} %collective-permute-done.2.refs_2_.first) | copy-start | bytes 1572868
  53.2 51.9 %collective-permute-start.5 = (bf16[2,2,272,128]{3,2,1,0:T(8,128)(2,1)}, bf16[2,2,272,128]{3,2,1,0:T(8,128)(2,1)}, u32[]{:S(2)}, u32[]{:S(2)}) collective-permute-start(bf16[2,2,272,128]{3,2,1,0:T(8,128)(2,1)} %copy-done.7), channel_id=1, source_target_pairs={{0,3},{1,0},{2,1},{3,2},{4,7},{5,4},{6,5},{7,6},{8,11},{9,8},{10,9... | collective-permute-start | bytes 835592 | tf_op jit(solution)/shard_map/ppermute | solution.py:373
  64.1 3.7 %copy-start.2 = (bf16[8,8,2,16,128]{4,3,2,1,0:T(8,128)(2,1)}, bf16[8,8,2,16,128]{4,3,2,1,0:T(8,128)(2,1)S(1)}, u32[]{:S(2)}) copy-start(bf16[8,8,2,16,128]{4,3,2,1,0:T(8,128)(2,1)S(1)} %collective-permute-done.1.refs_1_.below) | copy-start | bytes 1572868
  64.1 3.7 %copy-start.4 = (bf16[8,8,2,16,128]{4,3,2,1,0:T(8,128)(2,1)}, bf16[8,8,2,16,128]{4,3,2,1,0:T(8,128)(2,1)S(1)}, u32[]{:S(2)}) copy-start(bf16[8,8,2,16,128]{4,3,2,1,0:T(8,128)(2,1)S(1)} %collective-permute-done.refs_0_.above) | copy-start | bytes 1572868
  65.3 66.4 %collective-permute-start.9 = (bf16[2,8,8,2,16,128]{5,4,3,2,1,0:T(8,128)(2,1)}, bf16[2,8,8,2,16,128]{5,4,3,2,1,0:T(8,128)(2,1)}, u32[]{:S(2)}, u32[]{:S(2)}) collective-permute-start(bf16[2,8,8,2,16,128]{5,4,3,2,1,0:T(8,128)(2,1)} %pass_on.1.refs_2_), channel_id=1, source_target_pairs={{1,0},{2,3},{5,4},{6,7},{9,8},{10,11},{13,12},{14,15},{17,16},{18,... | collective-permute-start | bytes 3145736 | tf_op jit(solution)/shard_map/ppermute | solution.py:368
  69.1 6.0 %copy-start.10 = (bf16[16,128]{1,0:T(8,128)(2,1)S(1)}, bf16[16,128]{1,0:T(8,128)(2,1)}, u32[]{:S(2)}) copy-start(bf16[16,128]{1,0:T(8,128)(2,1)} %token_.1.refs_1_) | copy-start | bytes 12292
  69.4 26.4 %all-to-all-start = ((bf16[8,51,16,128]{3,2,1,0:T(8,128)(2,1)}), bf16[8,51,16,128]{3,2,1,0:T(8,128)(2,1)}, u32[]{:S(2)}, u32[]{:S(2)}) async-start(bf16[8,51,16,128]{3,2,1,0:T(8,128)(2,1)} %get-tuple-element.24), calls=%async_computation | async-start | bytes 3342336 | tf_op jit(solution)/shard_map/all_to_all | solution.py:319
  77.0 36.2 %collective-permute-start.10 = (bf16[2,3,272,128]{3,2,1,0:T(8,128)(2,1)}, bf16[2,3,272,128]{3,2,1,0:T(8,128)(2,1)S(1)}, u32[]{:S(2)}, u32[]{:S(2)}) collective-permute-start(bf16[2,3,272,128]{3,2,1,0:T(8,128)(2,1)} %get-tuple-element.37), channel_id=1, source_target_pairs={{0,1},{1,2},{2,3},{3,0},{4,5},{5,6},{6,7},{7,4},{8,9},{9,10},{10,1... | collective-permute-start | bytes 1253384 | tf_op jit(solution)/shard_map/ppermute | solution.py:373
  77.1 64.0 %collective-permute-start.11 = (bf16[2,3,272,128]{3,2,1,0:T(8,128)(2,1)}, bf16[2,3,272,128]{3,2,1,0:T(8,128)(2,1)S(1)}, u32[]{:S(2)}, u32[]{:S(2)}) collective-permute-start(bf16[2,3,272,128]{3,2,1,0:T(8,128)(2,1)} %get-tuple-element.38), channel_id=1, source_target_pairs={{0,2},{1,3},{2,0},{3,1},{4,6},{5,7},{6,4},{7,5},{8,10},{9,11},{10,... | collective-permute-start | bytes 1253384 | tf_op jit(solution)/shard_map/ppermute | solution.py:373
  86.3 54.8 %collective-permute-start.12 = (bf16[2,3,272,128]{3,2,1,0:T(8,128)(2,1)}, bf16[2,3,272,128]{3,2,1,0:T(8,128)(2,1)S(1)}, u32[]{:S(2)}, u32[]{:S(2)}) collective-permute-start(bf16[2,3,272,128]{3,2,1,0:T(8,128)(2,1)} %get-tuple-element.39), channel_id=1, source_target_pairs={{0,3},{1,0},{2,1},{3,2},{4,7},{5,4},{6,5},{7,6},{8,11},{9,8},{10,9... | collective-permute-start | bytes 1253384 | tf_op jit(solution)/shard_map/ppermute | solution.py:373
  105.1 26.6 %copy-start.1 = (bf16[8,8,2,16,128]{4,3,2,1,0:T(8,128)(2,1)S(1)}, bf16[8,8,2,16,128]{4,3,2,1,0:T(8,128)(2,1)}, u32[]{:S(2)}) copy-start(bf16[8,8,2,16,128]{4,3,2,1,0:T(8,128)(2,1)} %copy-done) | copy-start | bytes 1572868
  105.1 26.6 %copy-start.3 = (bf16[8,8,2,16,128]{4,3,2,1,0:T(8,128)(2,1)S(1)}, bf16[8,8,2,16,128]{4,3,2,1,0:T(8,128)(2,1)}, u32[]{:S(2)}) copy-start(bf16[8,8,2,16,128]{4,3,2,1,0:T(8,128)(2,1)} %copy-done.2) | copy-start | bytes 1572868
  105.1 26.6 %copy-start.5 = (bf16[8,8,2,16,128]{4,3,2,1,0:T(8,128)(2,1)S(1)}, bf16[8,8,2,16,128]{4,3,2,1,0:T(8,128)(2,1)}, u32[]{:S(2)}) copy-start(bf16[8,8,2,16,128]{4,3,2,1,0:T(8,128)(2,1)} %copy-done.4) | copy-start | bytes 1572868
  106.8 42.1 %collective-permute-start.6 = (bf16[2,3,272,128]{3,2,1,0:T(8,128)(2,1)S(1)}, bf16[2,3,272,128]{3,2,1,0:T(8,128)(2,1)S(1)}, u32[]{:S(2)}, u32[]{:S(2)}) collective-permute-start(bf16[2,3,272,128]{3,2,1,0:T(8,128)(2,1)S(1)} %get-tuple-element.34), channel_id=1, source_target_pairs={{0,1},{1,2},{2,3},{3,0},{4,5},{5,6},{6,7},{7,4},{8,9},{9,10},{10,1... | collective-permute-start | bytes 1253384 | tf_op jit(solution)/shard_map/ppermute | solution.py:373
  113.2 44.6 %collective-permute-start.7 = (bf16[2,3,272,128]{3,2,1,0:T(8,128)(2,1)S(1)}, bf16[2,3,272,128]{3,2,1,0:T(8,128)(2,1)S(1)}, u32[]{:S(2)}, u32[]{:S(2)}) collective-permute-start(bf16[2,3,272,128]{3,2,1,0:T(8,128)(2,1)S(1)} %get-tuple-element.35), channel_id=1, source_target_pairs={{0,2},{1,3},{2,0},{3,1},{4,6},{5,7},{6,4},{7,5},{8,10},{9,11},{10,... | collective-permute-start | bytes 1253384 | tf_op jit(solution)/shard_map/ppermute | solution.py:373
  131.7 27.0 %collective-permute-start.8 = (bf16[2,3,272,128]{3,2,1,0:T(8,128)(2,1)S(1)}, bf16[2,3,272,128]{3,2,1,0:T(8,128)(2,1)S(1)}, u32[]{:S(2)}, u32[]{:S(2)}) collective-permute-start(bf16[2,3,272,128]{3,2,1,0:T(8,128)(2,1)S(1)} %get-tuple-element.36), channel_id=1, source_target_pairs={{0,3},{1,0},{2,1},{3,2},{4,7},{5,4},{6,5},{7,6},{8,11},{9,8},{10,9... | collective-permute-start | bytes 1253384 | tf_op jit(solution)/shard_map/ppermute | solution.py:373

commit v14 on v9

--- a/solution.py
+++ b/solution.py
@@ -17,7 +17,7 @@
 QUERY, KEY, VALUE, OUT = range(4)
 CUT_MICROS = 30
 TOKEN_MICROS = 40
-CUTS = (0, 1, 3, 5, 8)
+CUTS = (0, 2, 5, 8)
 VMEM_LIMIT = 16 * 1024 * 1024
 
 
@@ -105,24 +105,13 @@
     return pl.BlockSpec(corner_of(x), lambda _: (0,) * x.ndim)
 
 
-def cut(rows, slice_map, blocks, ahead, item_rows, waits, micros):
+def cut(rows, slice_map, blocks, first, items, item_rows, waits, micros):
     t_ways = slice_map.shape[1]
-    first = math.prod(ahead)
-    items = (rows.shape[1] - first) // item_rows
-    shapes = [(rows.shape[0],) + ahead + rows.shape[2:]] if first else []
-    shapes += [(blocks, items, item_rows) + rows.shape[2:]] * t_ways
+    shapes = [(blocks, items, item_rows) + rows.shape[2:]] * t_ways
 
     def kernel(mapped, source, *refs):
         f_me, t_me = lax.axis_index("fsdp"), lax.axis_index("tp")
-        refs = refs[len(waits) :]
-        if first:
-            for f in range(rows.shape[0]):
-                for item in range(ahead[0]):
-                    for kind in range(ahead[1]):
-                        start = (item * ahead[1] + kind) * ahead[2]
-                        refs[0][f, item, kind] = source[f, start : start + ahead[2]]
-            refs = refs[1:]
-        for shift, piece in enumerate(refs):
+        for shift, piece in enumerate(refs[len(waits) :]):
             block = mapped[f_me, lax.rem(t_me + shift, t_ways)]
             for f in range(blocks):
                 for item in range(items):
@@ -198,21 +187,59 @@
     )(me.reshape(1), across, up, down, *waits)
 
 
-def assemble(me, spread_parts):
-    t_ways = len(spread_parts)
-    f_ways, items, kinds, rows, _ = spread_parts[0].shape
+def join(me, own, up, down, across, far, waits):
+    def kernel(me_ref, own_ref, up_ref, down_ref, across_ref, far_ref, *refs):
+        out = refs[-1]
+        first, last = me_ref[0] == 0, me_ref[0] == 3
+
+        def pick(d, end, far_at, other):
+            @pl.when(end)
+            def _():
+                out[0, d] = far_ref[far_at, 0]
+
+            @pl.when(jnp.logical_not(end))
+            def _():
+                out[0, d] = other[0]
+
+        out[0, 0] = own_ref[0]
+        pick(1, first, 0, up_ref)
+        pick(2, jnp.logical_or(first, last), 1, across_ref)
+        pick(3, last, 0, down_ref)
+
+    inner = own.shape[1:]
+    zeros = (0,) * len(inner)
+    one = pl.BlockSpec((1,) + inner, lambda f, me_ref: (f,) + zeros)
+    corners = [pl.BlockSpec(corner_of(x), lambda f, me_ref, n=x.ndim: (0,) * n) for x in waits]
+    return pl.pallas_call(
+        kernel,
+        grid_spec=pltpu.PrefetchScalarGridSpec(
+            num_scalar_prefetch=1,
+            grid=own.shape[:1],
+            in_specs=[one] * 4
+            + [pl.BlockSpec((2, 1) + inner, lambda f, me_ref: (0, f) + zeros)]
+            + corners,
+            out_specs=pl.BlockSpec((1, 4) + inner, lambda f, me_ref: (f, 0) + zeros),
+        ),
+        out_shape=jax.ShapeDtypeStruct(own.shape[:1] + (4,) + inner, own.dtype),
+        compiler_params=pltpu.CompilerParams(vmem_limit_bytes=VMEM_LIMIT),
+        name="join",
+    )(me.reshape(1), own, up, down, across, far, *waits)
+
+
+def assemble(me, joined, waits):
+    f_ways, t_ways, items, kinds, rows, _ = joined.shape
     depth = t_ways * f_ways * rows * LANES // KVR
     cuts = KVR // LANES
 
-    def kernel(me_ref, *refs):
-        pieces, (out, scratch) = refs[:t_ways], refs[t_ways:]
+    def kernel(me_ref, pieces, *refs):
+        out, scratch = refs[-2:]
         for kind in range(kinds):
             for d in range(t_ways):
                 t = lax.rem(me_ref[0] - d + t_ways, t_ways)
                 for f in range(f_ways):
                     scratch[pl.ds(pl.multiple_of((f * t_ways + t) * rows, rows), rows), :] = pieces[
-                        d
-                    ][f, 0, kind].astype(jnp.float32)
+                        f, d, 0, kind
+                    ].astype(jnp.float32)
             for cut in range(cuts):
                 out[0, kind, :, pl.ds(cut * LANES, LANES)] = scratch[
                     pl.ds(cut, depth, stride=cuts), :
@@ -223,14 +250,19 @@
         grid_spec=pltpu.PrefetchScalarGridSpec(
             num_scalar_prefetch=1,
             grid=(items,),
-            in_specs=[pl.BlockSpec((f_ways, 1, kinds, rows, LANES), lambda i, _: (0, i, 0, 0, 0))] * t_ways,
+            in_specs=[
+                pl.BlockSpec(
+                    (f_ways, t_ways, 1, kinds, rows, LANES), lambda i, _: (0, 0, i, 0, 0, 0)
+                )
+            ]
+            + [pl.BlockSpec(corner_of(x), lambda i, _, n=x.ndim: (0,) * n) for x in waits],
             out_specs=pl.BlockSpec((1, kinds, depth, KVR), lambda i, _: (i, 0, 0, 0)),
             scratch_shapes=[pltpu.VMEM((depth * cuts, LANES), jnp.float32)],
         ),
-        out_shape=jax.ShapeDtypeStruct((items, kinds, depth, KVR), spread_parts[0].dtype),
+        out_shape=jax.ShapeDtypeStruct((items, kinds, depth, KVR), joined.dtype),
         compiler_params=pltpu.CompilerParams(vmem_limit_bytes=VMEM_LIMIT),
         name="assemble",
-    )(me.reshape(1), *spread_parts)
+    )(me.reshape(1), joined, *waits)
 
 
 def absorb(me, items, parts, matrices, outs, shapes):
@@ -309,42 +341,44 @@
     whole_tiles = granule % (16 * LANES) == 0
     row_counts = [width // LANES for width in widths]
     item_rows = row_counts[QUERY] + row_counts[OUT]
-    ahead = (item_count, 2, row_counts[KEY])
 
     me = lax.axis_index("tp")
     blocks = f_ways // t_ways
     cuts = [item_count * eighths // 8 for eighths in CUTS]
     chunks = [range(low, high) for low, high in zip(cuts, cuts[1:]) if low < high]
 
-    def packed(parts):
-        return pack(table, param_offsets, owner_map, f_ways, widths, granule, parts)
-
     def over_fsdp(x):
         x = lax.all_to_all(x, "fsdp", split_axis=0, concat_axis=0, tiled=True)
         return x.reshape(f_ways, -1, LANES)
 
-    first_parts = [[(range(item_count), (KEY, VALUE)), (chunks[0], (QUERY, OUT))]]
-    other_parts = [[(items, (QUERY, OUT))] for items in chunks[1:]]
-    to_send = packed(first_parts + other_parts)
+    pairs, *to_send = pack(
+        table,
+        param_offsets,
+        owner_map,
+        f_ways,
+        widths,
+        granule,
+        [[(range(item_count), (KEY, VALUE))]] + [[(items, (QUERY, OUT))] for items in chunks],
+    )
+    pairs = pairs.reshape(f_ways, item_count, 2, row_counts[KEY], LANES)
+    up, down = neighbours(pairs, "tp", t_ways)
+    if t_ways == 4:
+        across = lax.ppermute(pairs, "tp", [(0, 2), (3, 1)])
+        near = token([up, down, across], TOKEN_MICROS)
+        passed = pass_on(me, across, up, down, [])
+        far = lax.ppermute(passed, "tp", [(1, 0), (2, 3)])
 
     exchanged, sent = [], []
-    for at in range(len(chunks)):
+    for at, items in enumerate(chunks):
         rows = over_fsdp(to_send[at])
         waits = sent[at - 1][:1] if at else []
         if at >= 2:
             waits = waits + exchanged[at - 2][1:]
-        if at == 1:
-            waits = waits + exchanged[0][1:3]
-        if t_ways == 4 and at in (1, len(chunks) - 1):
-            waits = waits + [near if at == 1 else far]
-        pieces = list(cut(rows, slice_map, blocks, ahead if at == 0 else (0,), item_rows, waits, CUT_MICROS))
-        if at == 0:
-            pairs = pieces.pop(0)
-            up, down = neighbours(pairs, "tp", t_ways)
-            if t_ways == 4:
-                across = lax.ppermute(pairs, "tp", [(0, 2), (3, 1)])
-                near = token([up, down, across], TOKEN_MICROS)
-                far = lax.ppermute(pass_on(me, across, up, down, []), "tp", [(1, 0), (2, 3)])
+        if t_ways == 4:
+            waits = waits + [[near], [passed], [far]][min(at, 2)]
+        pieces = list(
+            cut(rows, slice_map, blocks, 0, len(items), item_rows, waits, CUT_MICROS)
+        )
         sent.append(pieces)
         exchanged.append(
             pieces[:1]
@@ -356,33 +390,30 @@
         )
 
     if t_ways == 4:
-        ends = jnp.logical_or(me == 0, me == 3)
-        spread = [
-            pairs,
-            jnp.where(me == 0, far[0], up),
-            jnp.where(ends, far[1], across),
-            jnp.where(me == 3, far[0], down),
-        ]
+        joined = join(me, pairs, up, down, across, far, sent[-1][:1])
     else:
         ups, downs = [pairs, up], [pairs, down]
         for _ in range(2, t_ways):
             ups.append(neighbours(ups[-1], "tp", t_ways)[0])
             downs.append(neighbours(downs[-1], "tp", t_ways)[1])
-        spread = [pairs] + [jnp.where(me >= d, ups[d], downs[t_ways - d]) for d in range(1, t_ways)]
+        joined = jnp.stack(
+            [pairs] + [jnp.where(me >= d, ups[d], downs[t_ways - d]) for d in range(1, t_ways)], axis=1
+        )
+    joined = over_fsdp(joined).reshape(joined.shape)
 
     if whole_tiles:
         shapes = tuple(
             jax.ShapeDtypeStruct((item_count, blocks, t_ways, row_counts[kind], KVR), jnp.bfloat16)
             for kind in (QUERY, OUT)
         )
-        matrices = assemble(me, spread)
+        matrices = assemble(me, joined, [token(exchanged[-2][1:], TOKEN_MICROS)])
         outs = None
         for items, parts in zip(chunks, exchanged):
             outs = absorb(me, items, parts, matrices, outs, shapes)
         return tuple(out.reshape(layer_count, per_group, -1, KVR) for out in outs)
 
     order = lax.rem(me - jnp.arange(t_ways, dtype=jnp.int32) + t_ways, jnp.int32(t_ways))
-    matrices = jnp.take(jnp.stack(spread), order, axis=0).transpose(2, 3, 1, 0, 4, 5)
+    matrices = jnp.take(joined, order, axis=1).transpose(2, 3, 0, 1, 4, 5)
     matrices = matrices.reshape(item_count, 2, -1, KVR)
     done = [
         absorb_plain(me, parts, matrices[items[0] : items[-1] + 1])

time: 178 us -> 157 us (0.88)
  waiting for transfers between devices: 85.2 us -> 66.1 us
  Pallas kernels: 28.3 us -> 31.6 us
  local copies, waits for them, and re-layouts: 15.7 us -> 12.8 us
  starting transfers between devices: 45.8 us -> 43.5 us
    ppermute x1, waiting for transfers between devices: 15.4 us -> 0.01 us  [per_device(): far = lax.ppermute(passed, 'tp', [(1, 0), (2, 3)])]
    ppermute x1, waiting for transfers between devices: 0.01 us -> 4.47 us  [per_device(): across = lax.ppermute(pairs, 'tp', [(0, 2), (3, 1)])]
    ppermute x12 -> x9, waiting for transfers between devices: 37 us -> 32.9 us  [per_device(): lax.ppermute(piece, 'tp', [(i, (i + shift) % t_ways) for i in range(t_way...]
    pallas_call x0 -> x1, Pallas kernels: none -> 3.92 us  [join(): pl.pallas_call(kernel, grid_spec=pltpu.PrefetchScalarGridSpec(num_scalar_...]
    all_to_all x4, waiting for transfers between devices: 22 us -> 18.6 us  [over_fsdp(): x = lax.all_to_all(x, 'fsdp', split_axis=0, concat_axis=0, tiled=True)]
    unnamed x59, local copies, waits for them, and re-layouts: 15.7 us -> 12.8 us
    ppermute x12 -> x9, starting transfers between devices: 16.3 us -> 13.5 us  [per_device(): lax.ppermute(piece, 'tp', [(i, (i + shift) % t_ways) for i in range(t_way...]
    pallas_call x4 -> x3, Pallas kernels: 5.33 us -> 4.47 us  [cut(): pl.pallas_call(kernel, grid=(1,), out_shape=[jax.ShapeDtypeStruct(shape,...]
  transfers between devices with their start and end apart: 20 -> 17, of which waited for: 11 -> 9; matrix products, arithmetic and copies ran while one was open for 1% -> 0% of each run, Pallas kernels for 11% -> 14%
where the time goes in v14:
time: 157 us; the launch traced here: 155 us
  waiting for transfers between devices  66.1 us (42%)
  starting transfers between devices  43.5 us (28%)
  Pallas kernels  31.6 us (20%)
  local copies, waits for them, and re-layouts  12.8 us (8%)
    ppermute x9, waiting for transfers between devices, per_device(): lax.ppermute(piece, 'tp', [(i, (i + shift) % t_ways) for i in range(t_way...  32.9 us
    all_to_all x4, starting transfers between devices, over_fsdp(): x = lax.all_to_all(x, 'fsdp', split_axis=0, concat_axis=0, tiled=True)  18.7 us
    all_to_all x4, waiting for transfers between devices, over_fsdp(): x = lax.all_to_all(x, 'fsdp', split_axis=0, concat_axis=0, tiled=True)  18.6 us
    pallas_call x3, Pallas kernels, absorb(): pl.pallas_call(kernel, grid_spec=pltpu.PrefetchScalarGridSpec(num_scalar_...  14.6 us
    ppermute x9, starting transfers between devices, per_device(): lax.ppermute(piece, 'tp', [(i, (i + shift) % t_ways) for i in range(t_way...  13.5 us
    unnamed x59, local copies, waits for them, and re-layouts  12.8 us
    ppermute x1, waiting for transfers between devices, neighbours(): lax.ppermute(x, axis, [(i + 1, i) for i in range(ways - 1)])  10 us
    ppermute x1, starting transfers between devices, neighbours(): lax.ppermute(x, axis, [(i + 1, i) for i in range(ways - 1)])  5.59 us
  transfers between devices with their start and end apart: 17, of which 9 were waited for; matrix products, arithmetic and copies ran while one was open for 0% of the time, Pallas kernels for 14%

profile of v14, /device:TPU:10, one launch (start us, length us, event | category | flops | bytes accessed | tf_op | source)
XLA Modules:
  0.0 154.9 jit_solution(11590019952673013050)
XLA Ops:
  0.6 0.8 copy.10.offsets
  1.4 3.1 %copy.14 = bf16[1,2,9728,128]{3,2,1,0:T(8,128)(2,1)S(1)} copy(bf16[1,2,9728,128]{3,1,2,0:T(2,128)(2,1)} %bitcast.20) | data formatting | bytes 9961472
  4.5 0.0 copy-done.22
  4.6 3.9 %pack.1 = (bf16[8,16,16,128]{3,2,1,0:T(8,128)(2,1)S(1)}, bf16[8,34,16,128]{3,2,1,0:T(8,128)(2,1)}, bf16[8,51,16,128]{3,2,1,0:T(8,128)(2,1)}, bf16[8,51,16,128]{3,2,1,0:T(8,128)(2,1)}) custom-call(s32[2,32,4]{2,1,0:T(8,128)S(1)} %copy.10.offsets, s32[2,32]{1,0:T(2,128)S(1)} %copy-done.22, bf16[2,608,16,128]{3,2,1,0:T(8,128)(2,1)S(1)} %bitcast.10), custom_call_target="tpu_custom_call" | custom-call | bytes 9961472 | tf_op jit(solution)/shard_map/pack/pallas_call | solution.py:77
  8.4 1.4 collective-permute-start.2
  9.8 5.6 %collective-permute-start.1 = (bf16[8,8,2,16,128]{4,3,2,1,0:T(8,128)(2,1)S(1)}, bf16[8,8,2,16,128]{4,3,2,1,0:T(8,128)(2,1)S(1)}, u32[]{:S(2)}, u32[]{:S(2)}) collective-permute-start(bf16[8,8,2,16,128]{4,3,2,1,0:T(8,128)(2,1)S(1)} %bitcast.15), channel_id=1, source_target_pairs={{1,0},{2,1},{3,2},{5,4},{6,5},{7,6},{9,8},{10,9},{11,10},{13,12},{... | collective-permute-start | bytes 1572872 | tf_op jit(solution)/shard_map/ppermute | solution.py:157
  15.4 1.9 %collective-permute-start = (bf16[8,8,2,16,128]{4,3,2,1,0:T(8,128)(2,1)S(1)}, bf16[8,8,2,16,128]{4,3,2,1,0:T(8,128)(2,1)S(1)}, u32[]{:S(2)}, u32[]{:S(2)}) collective-permute-start(bf16[8,8,2,16,128]{4,3,2,1,0:T(8,128)(2,1)S(1)} %bitcast.16), channel_id=1, source_target_pairs={{0,1},{1,2},{2,3},{4,5},{5,6},{6,7},{8,9},{9,10},{10,11},{12,13},{... | collective-permute-start | bytes 1572872 | tf_op jit(solution)/shard_map/ppermute | solution.py:156
  17.4 4.3 %all-to-all-start.2 = ((bf16[8,34,16,128]{3,2,1,0:T(8,128)(2,1)}), bf16[8,34,16,128]{3,2,1,0:T(8,128)(2,1)S(1)}, u32[]{:S(2)}, u32[]{:S(2)}) async-start(bf16[8,34,16,128]{3,2,1,0:T(8,128)(2,1)} %get-tuple-element.26), calls=%async_computation.2 | async-start | bytes 2228224 | tf_op jit(solution)/shard_map/all_to_all | solution.py:351
  21.6 0.0 copy-done.27
  21.6 0.1 copy.13.mapped
  21.7 4.5 %collective-permute-done.2.refs_2_.first.across_ref = bf16[8,8,2,16,128]{4,3,2,1,0:T(8,128)(2,1)S(1)} collective-permute-done((bf16[8,8,2,16,128]{4,3,2,1,0:T(8,128)(2,1)S(1)}, bf16[8,8,2,16,128]{4,3,2,1,0:T(8,128)(2,1)S(1)}, u32[]{:S(2)}, u32[]{:S(2)}) %collective-permute-start.2) | collective-permute-done | bytes 524320 | tf_op jit(solution)/shard_map/ppermute | solution.py:366
  26.2 10.0 %collective-permute-done.1.refs_1_.below.down_ref = bf16[8,8,2,16,128]{4,3,2,1,0:T(8,128)(2,1)S(1)} collective-permute-done((bf16[8,8,2,16,128]{4,3,2,1,0:T(8,128)(2,1)S(1)}, bf16[8,8,2,16,128]{4,3,2,1,0:T(8,128)(2,1)S(1)}, u32[]{:S(2)}, u32[]{:S(2)}) %collective-permute-start.1) | collective-permute-done | bytes 524320 | tf_op jit(solution)/shard_map/ppermute | solution.py:157
  36.2 0.2 collective-permute-done.refs_0_.above.up_ref
  36.4 1.2 pass_on.1.refs_1_
  37.6 2.4 %collective-permute-start.6 = (bf16[2,8,8,2,16,128]{5,4,3,2,1,0:T(8,128)(2,1)}, bf16[2,8,8,2,16,128]{5,4,3,2,1,0:T(8,128)(2,1)}, u32[]{:S(2)}, u32[]{:S(2)}) collective-permute-start(bf16[2,8,8,2,16,128]{5,4,3,2,1,0:T(8,128)(2,1)} %pass_on.1.refs_1_), channel_id=1, source_target_pairs={{1,0},{2,3},{5,4},{6,7},{9,8},{10,11},{13,12},{14,15},{17,16},{18,... | collective-permute-start | bytes 3145736 | tf_op jit(solution)/shard_map/ppermute | solution.py:369
  40.0 0.0 copy-done.5
  40.0 1.3 token_.2.refs_0_
  41.3 0.0 all-to-all-done.2
  41.3 1.0 copy-done.7
  42.3 4.4 %all-to-all-start.1 = ((bf16[8,51,16,128]{3,2,1,0:T(8,128)(2,1)}), bf16[8,51,16,128]{3,2,1,0:T(8,128)(2,1)S(1)}, u32[]{:S(2)}, u32[]{:S(2)}) async-start(bf16[8,51,16,128]{3,2,1,0:T(8,128)(2,1)} %get-tuple-element.25), calls=%async_computation.1 | async-start | bytes 3342336 | tf_op jit(solution)/shard_map/all_to_all | solution.py:351
  46.7 1.6 %cut.3 = (bf16[2,2,272,128]{3,2,1,0:T(8,128)(2,1)S(1)}, bf16[2,2,272,128]{3,2,1,0:T(8,128)(2,1)}, bf16[2,2,272,128]{3,2,1,0:T(8,128)(2,1)}, bf16[2,2,272,128]{3,2,1,0:T(8,128)(2,1)}) custom-call(s32[8,4]{1,0:T(8,128)S(1)} %copy.13.mapped, bf16[8,544,128]{2,1,0:T(8,128)(2,1)S(1)} %bitcast.13, bf16[16,128]{1,0:T(8,128)(2,1)S(1)} %copy-done.26), custom_call_target="tpu_custom_call" | custom-call | flops 34500001792 | bytes 2228224 | tf_op jit(solution)/shard_map/cut/pallas_call | solution.py:121
  48.3 0.7 copy-done.18
  48.9 1.3 collective-permute-start.3
  50.2 0.0 collective-permute-start.4
  50.2 1.5 collective-permute-start.5
  51.7 15.6 %all-to-all-done.1 = bf16[8,51,16,128]{3,2,1,0:T(8,128)(2,1)S(1)} async-done(((bf16[8,51,16,128]{3,2,1,0:T(8,128)(2,1)}), bf16[8,51,16,128]{3,2,1,0:T(8,128)(2,1)S(1)}, u32[]{:S(2)}, u32[]{:S(2)}) %all-to-all-start.1) | async-done | bytes 1671200 | tf_op jit(solution)/shard_map/all_to_all | solution.py:351
  67.2 5.0 %all-to-all-start = ((bf16[8,51,16,128]{3,2,1,0:T(8,128)(2,1)}), bf16[8,51,16,128]{3,2,1,0:T(8,128)(2,1)S(1)}, u32[]{:S(2)}, u32[]{:S(2)}) async-start(bf16[8,51,16,128]{3,2,1,0:T(8,128)(2,1)} %get-tuple-element.24), calls=%async_computation | async-start | bytes 3342336 | tf_op jit(solution)/shard_map/all_to_all | solution.py:351
  72.2 1.0 copy-done.19
  73.2 1.9 %cut.4 = (bf16[2,3,272,128]{3,2,1,0:T(8,128)(2,1)S(1)}, bf16[2,3,272,128]{3,2,1,0:T(8,128)(2,1)}, bf16[2,3,272,128]{3,2,1,0:T(8,128)(2,1)}, bf16[2,3,272,128]{3,2,1,0:T(8,128)(2,1)}) custom-call(s32[8,4]{1,0:T(8,128)S(1)} %copy.13.mapped, bf16[8,816,128]{2,1,0:T(8,128)(2,1)S(1)} %bitcast.12, bf16[2,2,272,128]{3,2,1,0:T(8,128)(2,1)S(1)} %copy-done.19, ...), custom_call_target="tpu_custom_call" | custom-call | flops 34500001792 | bytes 3342336 | tf_op jit(solution)/shard_map/cut/pallas_call | solution.py:121
  75.1 0.8 copy-done.11
  75.9 1.3 collective-permute-start.10
  77.1 0.0 collective-permute-done.3.refs_1_
  77.1 6.8 %collective-permute-start.11 = (bf16[2,3,272,128]{3,2,1,0:T(8,128)(2,1)}, bf16[2,3,272,128]{3,2,1,0:T(8,128)(2,1)S(1)}, u32[]{:S(2)}, u32[]{:S(2)}) collective-permute-start(bf16[2,3,272,128]{3,2,1,0:T(8,128)(2,1)} %get-tuple-element.38), channel_id=1, source_target_pairs={{0,2},{1,3},{2,0},{3,1},{4,6},{5,7},{6,4},{7,5},{8,10},{9,11},{10,... | collective-permute-start | bytes 1253384 | tf_op jit(solution)/shard_map/ppermute | solution.py:386
  83.9 0.0 collective-permute-done.4.refs_2_
  83.9 0.0 collective-permute-start.12
  83.9 5.9 %collective-permute-done.5.refs_3_ = bf16[2,2,272,128]{3,2,1,0:T(8,128)(2,1)} collective-permute-done((bf16[2,2,272,128]{3,2,1,0:T(8,128)(2,1)}, bf16[2,2,272,128]{3,2,1,0:T(8,128)(2,1)}, u32[]{:S(2)}, u32[]{:S(2)}) %collective-permute-start.5) | collective-permute-done | bytes 278560 | tf_op jit(solution)/shard_map/ppermute | solution.py:386
  89.8 3.0 %all-to-all-done = bf16[8,51,16,128]{3,2,1,0:T(8,128)(2,1)S(1)} async-done(((bf16[8,51,16,128]{3,2,1,0:T(8,128)(2,1)}), bf16[8,51,16,128]{3,2,1,0:T(8,128)(2,1)S(1)}, u32[]{:S(2)}, u32[]{:S(2)}) %all-to-all-start) | async-done | bytes 1671200 | tf_op jit(solution)/shard_map/all_to_all | solution.py:351
  92.8 0.0 collective-permute-done.6.refs_4_.far_ref
  92.8 1.0 copy-done.12
  93.8 1.0 cut.5
  94.8 0.8 copy-done.23
  95.6 0.8 copy-done.25
  96.4 0.8 copy-done.24
  97.2 3.9 %join.1 = bf16[8,4,8,2,16,128]{5,4,3,2,1,0:T(8,128)(2,1)S(1)} custom-call(s32[1]{0:T(128)} %bitcast.me_ref.at, bf16[8,8,2,16,128]{4,3,2,1,0:T(8,128)(2,1)S(1)} %bitcast.17, bf16[8,8,2,16,128]{4,3,2,1,0:T(8,128)(2,1)S(1)} %copy-done.6, bf16[8,8,2,16,128]{4,3,2,1,0:T(8,128)(2,1)S(1)} %copy-done.4, bf16[8,8,2,16,128]{4,3,2,1,0:T(8,128)(2,1)S(1)} %copy-done.2, ...), custom_call_target="tpu_custom_call" | custom-call | tf_op jit(solution)/shard_map/join/pallas_call | solution.py:213
  101.1 0.0 copy-start
  101.1 1.3 copy-done
  102.4 5.0 %all-to-all-start.3 = ((bf16[8,4,8,2,16,128]{5,4,3,2,1,0:T(8,128)(2,1)}), bf16[8,4,8,2,16,128]{5,4,3,2,1,0:T(8,128)(2,1)S(1)}, u32[]{:S(2)}, u32[]{:S(2)}) async-start(bf16[8,4,8,2,16,128]{5,4,3,2,1,0:T(8,128)(2,1)} %copy-done), calls=%async_computation.3 | async-start | bytes 4194304 | tf_op jit(solution)/shard_map/all_to_all | solution.py:351
  107.5 1.3 collective-permute-start.7
  108.7 0.0 collective-permute-start.8
  108.7 0.0 collective-permute-done.10.refs_0_.refs_1_
  108.7 1.5 collective-permute-start.9
  110.2 4.2 %collective-permute-done.11.refs_1_.refs_2_ = bf16[2,3,272,128]{3,2,1,0:T(8,128)(2,1)S(1)} collective-permute-done((bf16[2,3,272,128]{3,2,1,0:T(8,128)(2,1)}, bf16[2,3,272,128]{3,2,1,0:T(8,128)(2,1)S(1)}, u32[]{:S(2)}, u32[]{:S(2)}) %collective-permute-start.11) | collective-permute-done | bytes 417824 | tf_op jit(solution)/shard_map/ppermute | solution.py:386
  114.3 17.2 %collective-permute-done.12.refs_2_.refs_3_ = bf16[2,3,272,128]{3,2,1,0:T(8,128)(2,1)} collective-permute-done((bf16[2,3,272,128]{3,2,1,0:T(8,128)(2,1)}, bf16[2,3,272,128]{3,2,1,0:T(8,128)(2,1)}, u32[]{:S(2)}, u32[]{:S(2)}) %collective-permute-start.12) | collective-permute-done | bytes 417824 | tf_op jit(solution)/shard_map/ppermute | solution.py:386
  131.6 1.3 token_.3.refs_0_
  132.9 0.0 all-to-all-done.3.pieces
  132.9 0.7 copy-done.21
  133.6 1.0 assemble.1.refs_4_
  134.7 4.0 %absorb.3 = (bf16[8,2,4,48,512]{4,3,2,1,0:T(8,128)(2,1)}, bf16[8,2,4,224,512]{4,3,2,1,0:T(8,128)(2,1)}) custom-call(s32[1]{0:T(128)} %bitcast.me_ref.at, bf16[2,2,272,128]{3,2,1,0:T(8,128)(2,1)S(1)} %copy-done.20, bf16[2,2,272,128]{3,2,1,0:T(8,128)(2,1)} %collective-permute-done.3.refs_1_, bf16[2,2,272,128]{3,2,1,0:T(8,128)(2,1)} %collective-permute-done.4.refs_2_, ...), custom_call_target="tpu_custom_call" | custom-call | flops 570425344 | bytes 5570560 | tf_op jit(solution)/shard_map/absorb/pallas_call | solution.py:296
  138.7 0.0 copy-done.17
  138.7 5.1 %absorb.4 = (bf16[8,2,4,48,512]{4,3,2,1,0:T(8,128)(2,1)}, bf16[8,2,4,224,512]{4,3,2,1,0:T(8,128)(2,1)}) custom-call(s32[1]{0:T(128)} %bitcast.me_ref.at, bf16[2,3,272,128]{3,2,1,0:T(8,128)(2,1)S(1)} %copy-done.13, bf16[2,3,272,128]{3,2,1,0:T(8,128)(2,1)S(1)} %copy-done.15, ...), custom_call_target="tpu_custom_call", output_to_operand_aliasing={{0}: (6, {}), {1}: (7, {})} | custom-call | flops 855638016 | bytes 8355840 | tf_op jit(solution)/shard_map/absorb/pallas_call | solution.py:296
  143.8 0.0 collective-permute-done.7.refs_1_
  143.8 5.5 %collective-permute-done.8.refs_2_ = bf16[2,3,272,128]{3,2,1,0:T(8,128)(2,1)} collective-permute-done((bf16[2,3,272,128]{3,2,1,0:T(8,128)(2,1)}, bf16[2,3,272,128]{3,2,1,0:T(8,128)(2,1)}, u32[]{:S(2)}, u32[]{:S(2)}) %collective-permute-start.8) | collective-permute-done | bytes 417824 | tf_op jit(solution)/shard_map/ppermute | solution.py:386
  149.4 0.0 collective-permute-done.9.refs_3_
  149.4 5.5 %absorb.5 = (bf16[8,2,4,48,512]{4,3,2,1,0:T(8,128)(2,1)}, bf16[8,2,4,224,512]{4,3,2,1,0:T(8,128)(2,1)}) custom-call(s32[1]{0:T(128)} %bitcast.me_ref.at, bf16[2,3,272,128]{3,2,1,0:T(8,128)(2,1)S(1)} %get-tuple-element.33.refs_0_, bf16[2,3,272,128]{3,2,1,0:T(8,128)(2,1)} %collective-permute-done.7.refs_1_, ...), custom_call_target="tpu_custom_call", output_to_operand_aliasing={{0}: (6, {}), {1}: (7, {})} | custom-call | flops 855638016 | bytes 8355840 | tf_op jit(solution)/shard_map/absorb/pallas_call | solution.py:296
  (41 shorter events, 0.1 us)
Async XLA Ops:
  1.4 3.1 %copy-start.22 = (s32[2,32]{1,0:T(2,128)S(1)}, s32[2,32]{1,0:T(2,128)}, u32[]{:S(2)}) copy-start(s32[2,32]{1,0:T(2,128)} %owners.1) | copy-start | bytes 772
  8.4 29.1 %copy-start.9 = (bf16[8,16,16,128]{3,2,1,0:T(8,128)(2,1)}, bf16[8,16,16,128]{3,2,1,0:T(8,128)(2,1)S(1)}, u32[]{:S(2)}) copy-start(bf16[8,16,16,128]{3,2,1,0:T(8,128)(2,1)S(1)} %get-tuple-element.27) | copy-start | bytes 1572868
  8.4 13.2 %copy-start.27 = (s32[8,4]{0,1:T(4,128)S(1)}, s32[8,4]{0,1:T(4,128)}, u32[]{:S(2)}) copy-start(s32[8,4]{0,1:T(4,128)} %param.7) | copy-start | bytes 388
  8.4 17.8 %collective-permute-start.2 = (bf16[8,8,2,16,128]{4,3,2,1,0:T(8,128)(2,1)S(1)}, bf16[8,8,2,16,128]{4,3,2,1,0:T(8,128)(2,1)S(1)}, u32[]{:S(2)}, u32[]{:S(2)}) collective-permute-start(bf16[8,8,2,16,128]{4,3,2,1,0:T(8,128)(2,1)S(1)} %bitcast.14), channel_id=1, source_target_pairs={{0,2},{3,1},{4,6},{7,5},{8,10},{11,9},{12,14},{15,13},{16,18},{19,... | collective-permute-start | bytes 1572872 | tf_op jit(solution)/shard_map/ppermute | solution.py:366
  9.8 26.4 %collective-permute-start.1 = (bf16[8,8,2,16,128]{4,3,2,1,0:T(8,128)(2,1)S(1)}, bf16[8,8,2,16,128]{4,3,2,1,0:T(8,128)(2,1)S(1)}, u32[]{:S(2)}, u32[]{:S(2)}) collective-permute-start(bf16[8,8,2,16,128]{4,3,2,1,0:T(8,128)(2,1)S(1)} %bitcast.15), channel_id=1, source_target_pairs={{1,0},{2,1},{3,2},{5,4},{6,5},{7,6},{9,8},{10,9},{11,10},{13,12},{... | collective-permute-start | bytes 1572872 | tf_op jit(solution)/shard_map/ppermute | solution.py:157
  15.4 20.9 %collective-permute-start = (bf16[8,8,2,16,128]{4,3,2,1,0:T(8,128)(2,1)S(1)}, bf16[8,8,2,16,128]{4,3,2,1,0:T(8,128)(2,1)S(1)}, u32[]{:S(2)}, u32[]{:S(2)}) collective-permute-start(bf16[8,8,2,16,128]{4,3,2,1,0:T(8,128)(2,1)S(1)} %bitcast.16), channel_id=1, source_target_pairs={{0,1},{1,2},{2,3},{4,5},{5,6},{6,7},{8,9},{9,10},{10,11},{12,13},{... | collective-permute-start | bytes 1572872 | tf_op jit(solution)/shard_map/ppermute | solution.py:156
  17.4 23.9 %all-to-all-start.2 = ((bf16[8,34,16,128]{3,2,1,0:T(8,128)(2,1)}), bf16[8,34,16,128]{3,2,1,0:T(8,128)(2,1)S(1)}, u32[]{:S(2)}, u32[]{:S(2)}) async-start(bf16[8,34,16,128]{3,2,1,0:T(8,128)(2,1)} %get-tuple-element.26), calls=%async_computation.2 | async-start | bytes 2228224 | tf_op jit(solution)/shard_map/all_to_all | solution.py:351
  26.2 13.8 %copy-start.1 = (bf16[8,8,2,16,128]{4,3,2,1,0:T(8,128)(2,1)}, bf16[8,8,2,16,128]{4,3,2,1,0:T(8,128)(2,1)S(1)}, u32[]{:S(2)}) copy-start(bf16[8,8,2,16,128]{4,3,2,1,0:T(8,128)(2,1)S(1)} %collective-permute-done.2.refs_2_.first.across_ref) | copy-start | bytes 1572868
  36.2 3.7 %copy-start.3 = (bf16[8,8,2,16,128]{4,3,2,1,0:T(8,128)(2,1)}, bf16[8,8,2,16,128]{4,3,2,1,0:T(8,128)(2,1)S(1)}, u32[]{:S(2)}) copy-start(bf16[8,8,2,16,128]{4,3,2,1,0:T(8,128)(2,1)S(1)} %collective-permute-done.1.refs_1_.below.down_ref) | copy-start | bytes 1572868
  36.4 3.6 %copy-start.5 = (bf16[8,8,2,16,128]{4,3,2,1,0:T(8,128)(2,1)}, bf16[8,8,2,16,128]{4,3,2,1,0:T(8,128)(2,1)S(1)}, u32[]{:S(2)}) copy-start(bf16[8,8,2,16,128]{4,3,2,1,0:T(8,128)(2,1)S(1)} %collective-permute-done.refs_0_.above.up_ref) | copy-start | bytes 1572868
  37.6 55.3 %collective-permute-start.6 = (bf16[2,8,8,2,16,128]{5,4,3,2,1,0:T(8,128)(2,1)}, bf16[2,8,8,2,16,128]{5,4,3,2,1,0:T(8,128)(2,1)}, u32[]{:S(2)}, u32[]{:S(2)}) collective-permute-start(bf16[2,8,8,2,16,128]{5,4,3,2,1,0:T(8,128)(2,1)} %pass_on.1.refs_1_), channel_id=1, source_target_pairs={{1,0},{2,3},{5,4},{6,7},{9,8},{10,11},{13,12},{14,15},{17,16},{18,... | collective-permute-start | bytes 3145736 | tf_op jit(solution)/shard_map/ppermute | solution.py:369
  41.3 5.4 %copy-start.26 = (bf16[16,128]{1,0:T(8,128)(2,1)S(1)}, bf16[16,128]{1,0:T(8,128)(2,1)}, u32[]{:S(2)}) copy-start(bf16[16,128]{1,0:T(8,128)(2,1)} %token_.2.refs_0_) | copy-start | bytes 12292
  41.3 1.0 copy-start.7
  42.3 4.4 %copy-start.8 = (bf16[8,34,16,128]{3,2,1,0:T(8,128)(2,1)S(1)}, bf16[8,34,16,128]{3,2,1,0:T(8,128)(2,1)}, u32[]{:S(2)}) copy-start(bf16[8,34,16,128]{3,2,1,0:T(8,128)(2,1)} %copy-done.7) | copy-start | bytes 3342340
  42.3 25.0 %all-to-all-start.1 = ((bf16[8,51,16,128]{3,2,1,0:T(8,128)(2,1)}), bf16[8,51,16,128]{3,2,1,0:T(8,128)(2,1)S(1)}, u32[]{:S(2)}, u32[]{:S(2)}) async-start(bf16[8,51,16,128]{3,2,1,0:T(8,128)(2,1)} %get-tuple-element.25), calls=%async_computation.1 | async-start | bytes 3342336 | tf_op jit(solution)/shard_map/all_to_all | solution.py:351
  48.3 0.7 copy-start.18
  48.9 28.2 %collective-permute-start.3 = (bf16[2,2,272,128]{3,2,1,0:T(8,128)(2,1)}, bf16[2,2,272,128]{3,2,1,0:T(8,128)(2,1)}, u32[]{:S(2)}, u32[]{:S(2)}) collective-permute-start(bf16[2,2,272,128]{3,2,1,0:T(8,128)(2,1)} %get-tuple-element.30), channel_id=1, source_target_pairs={{0,1},{1,2},{2,3},{3,0},{4,5},{5,6},{6,7},{7,4},{8,9},{9,10},{10,1... | collective-permute-start | bytes 835592 | tf_op jit(solution)/shard_map/ppermute | solution.py:386
  50.2 33.7 %collective-permute-start.4 = (bf16[2,2,272,128]{3,2,1,0:T(8,128)(2,1)}, bf16[2,2,272,128]{3,2,1,0:T(8,128)(2,1)}, u32[]{:S(2)}, u32[]{:S(2)}) collective-permute-start(bf16[2,2,272,128]{3,2,1,0:T(8,128)(2,1)} %get-tuple-element.31), channel_id=1, source_target_pairs={{0,2},{1,3},{2,0},{3,1},{4,6},{5,7},{6,4},{7,5},{8,10},{9,11},{10,... | collective-permute-start | bytes 835592 | tf_op jit(solution)/shard_map/ppermute | solution.py:386
  50.2 39.6 %collective-permute-start.5 = (bf16[2,2,272,128]{3,2,1,0:T(8,128)(2,1)}, bf16[2,2,272,128]{3,2,1,0:T(8,128)(2,1)}, u32[]{:S(2)}, u32[]{:S(2)}) collective-permute-start(bf16[2,2,272,128]{3,2,1,0:T(8,128)(2,1)} %get-tuple-element.32), channel_id=1, source_target_pairs={{0,3},{1,0},{2,1},{3,2},{4,7},{5,4},{6,5},{7,6},{8,11},{9,8},{10,9... | collective-permute-start | bytes 835592 | tf_op jit(solution)/shard_map/ppermute | solution.py:386
  67.2 25.6 %all-to-all-start = ((bf16[8,51,16,128]{3,2,1,0:T(8,128)(2,1)}), bf16[8,51,16,128]{3,2,1,0:T(8,128)(2,1)S(1)}, u32[]{:S(2)}, u32[]{:S(2)}) async-start(bf16[8,51,16,128]{3,2,1,0:T(8,128)(2,1)} %get-tuple-element.24), calls=%async_computation | async-start | bytes 3342336 | tf_op jit(solution)/shard_map/all_to_all | solution.py:351
  72.2 1.0 copy-start.19
  75.1 0.8 copy-start.11
  75.9 32.9 %collective-permute-start.10 = (bf16[2,3,272,128]{3,2,1,0:T(8,128)(2,1)}, bf16[2,3,272,128]{3,2,1,0:T(8,128)(2,1)S(1)}, u32[]{:S(2)}, u32[]{:S(2)}) collective-permute-start(bf16[2,3,272,128]{3,2,1,0:T(8,128)(2,1)} %get-tuple-element.37), channel_id=1, source_target_pairs={{0,1},{1,2},{2,3},{3,0},{4,5},{5,6},{6,7},{7,4},{8,9},{9,10},{10,1... | collective-permute-start | bytes 1253384 | tf_op jit(solution)/shard_map/ppermute | solution.py:386
  77.1 37.2 %collective-permute-start.11 = (bf16[2,3,272,128]{3,2,1,0:T(8,128)(2,1)}, bf16[2,3,272,128]{3,2,1,0:T(8,128)(2,1)S(1)}, u32[]{:S(2)}, u32[]{:S(2)}) collective-permute-start(bf16[2,3,272,128]{3,2,1,0:T(8,128)(2,1)} %get-tuple-element.38), channel_id=1, source_target_pairs={{0,2},{1,3},{2,0},{3,1},{4,6},{5,7},{6,4},{7,5},{8,10},{9,11},{10,... | collective-permute-start | bytes 1253384 | tf_op jit(solution)/shard_map/ppermute | solution.py:386
  83.9 47.7 %collective-permute-start.12 = (bf16[2,3,272,128]{3,2,1,0:T(8,128)(2,1)}, bf16[2,3,272,128]{3,2,1,0:T(8,128)(2,1)}, u32[]{:S(2)}, u32[]{:S(2)}) collective-permute-start(bf16[2,3,272,128]{3,2,1,0:T(8,128)(2,1)} %get-tuple-element.39), channel_id=1, source_target_pairs={{0,3},{1,0},{2,1},{3,2},{4,7},{5,4},{6,5},{7,6},{8,11},{9,8},{10,9... | collective-permute-start | bytes 1253384 | tf_op jit(solution)/shard_map/ppermute | solution.py:386
  92.8 1.0 copy-start.12
  93.8 3.3 %copy-start.2 = (bf16[8,8,2,16,128]{4,3,2,1,0:T(8,128)(2,1)S(1)}, bf16[8,8,2,16,128]{4,3,2,1,0:T(8,128)(2,1)}, u32[]{:S(2)}) copy-start(bf16[8,8,2,16,128]{4,3,2,1,0:T(8,128)(2,1)} %copy-done.1) | copy-start | bytes 1572868
  93.8 3.3 %copy-start.4 = (bf16[8,8,2,16,128]{4,3,2,1,0:T(8,128)(2,1)S(1)}, bf16[8,8,2,16,128]{4,3,2,1,0:T(8,128)(2,1)}, u32[]{:S(2)}) copy-start(bf16[8,8,2,16,128]{4,3,2,1,0:T(8,128)(2,1)} %copy-done.3) | copy-start | bytes 1572868
  93.8 3.3 %copy-start.6 = (bf16[8,8,2,16,128]{4,3,2,1,0:T(8,128)(2,1)S(1)}, bf16[8,8,2,16,128]{4,3,2,1,0:T(8,128)(2,1)}, u32[]{:S(2)}) copy-start(bf16[8,8,2,16,128]{4,3,2,1,0:T(8,128)(2,1)} %copy-done.5) | copy-start | bytes 1572868
  93.8 3.3 %copy-start.10 = (bf16[8,16,16,128]{3,2,1,0:T(8,128)(2,1)S(1)}, bf16[8,16,16,128]{3,2,1,0:T(8,128)(2,1)}, u32[]{:S(2)}) copy-start(bf16[8,16,16,128]{3,2,1,0:T(8,128)(2,1)} %copy-done.9) | copy-start | bytes 1572868
  94.8 0.8 copy-start.23
  95.6 0.8 copy-start.25
  96.4 0.8 copy-start.24
  101.1 1.3 copy-start
  102.4 30.5 %all-to-all-start.3 = ((bf16[8,4,8,2,16,128]{5,4,3,2,1,0:T(8,128)(2,1)}), bf16[8,4,8,2,16,128]{5,4,3,2,1,0:T(8,128)(2,1)S(1)}, u32[]{:S(2)}, u32[]{:S(2)}) async-start(bf16[8,4,8,2,16,128]{5,4,3,2,1,0:T(8,128)(2,1)} %copy-done), calls=%async_computation.3 | async-start | bytes 4194304 | tf_op jit(solution)/shard_map/all_to_all | solution.py:351
  107.5 36.4 %collective-permute-start.7 = (bf16[2,3,272,128]{3,2,1,0:T(8,128)(2,1)}, bf16[2,3,272,128]{3,2,1,0:T(8,128)(2,1)}, u32[]{:S(2)}, u32[]{:S(2)}) collective-permute-start(bf16[2,3,272,128]{3,2,1,0:T(8,128)(2,1)} %copy-done.25), channel_id=1, source_target_pairs={{0,1},{1,2},{2,3},{3,0},{4,5},{5,6},{6,7},{7,4},{8,9},{9,10},{10,1... | collective-permute-start | bytes 1253384 | tf_op jit(solution)/shard_map/ppermute | solution.py:386
  108.7 40.6 %collective-permute-start.8 = (bf16[2,3,272,128]{3,2,1,0:T(8,128)(2,1)}, bf16[2,3,272,128]{3,2,1,0:T(8,128)(2,1)}, u32[]{:S(2)}, u32[]{:S(2)}) collective-permute-start(bf16[2,3,272,128]{3,2,1,0:T(8,128)(2,1)} %copy-done.24), channel_id=1, source_target_pairs={{0,2},{1,3},{2,0},{3,1},{4,6},{5,7},{6,4},{7,5},{8,10},{9,11},{10,... | collective-permute-start | bytes 1253384 | tf_op jit(solution)/shard_map/ppermute | solution.py:386
  108.7 22.9 %copy-start.14 = (bf16[2,3,272,128]{3,2,1,0:T(8,128)(2,1)}, bf16[2,3,272,128]{3,2,1,0:T(8,128)(2,1)S(1)}, u32[]{:S(2)}) copy-start(bf16[2,3,272,128]{3,2,1,0:T(8,128)(2,1)S(1)} %collective-permute-done.10.refs_0_.refs_1_) | copy-start | bytes 1253380
  108.7 40.7 %collective-permute-start.9 = (bf16[2,3,272,128]{3,2,1,0:T(8,128)(2,1)}, bf16[2,3,272,128]{3,2,1,0:T(8,128)(2,1)}, u32[]{:S(2)}, u32[]{:S(2)}) collective-permute-start(bf16[2,3,272,128]{3,2,1,0:T(8,128)(2,1)} %copy-done.23), channel_id=1, source_target_pairs={{0,3},{1,0},{2,1},{3,2},{4,7},{5,4},{6,5},{7,6},{8,11},{9,8},{10,9... | collective-permute-start | bytes 1253384 | tf_op jit(solution)/shard_map/ppermute | solution.py:386
  114.3 17.3 %copy-start.16 = (bf16[2,3,272,128]{3,2,1,0:T(8,128)(2,1)}, bf16[2,3,272,128]{3,2,1,0:T(8,128)(2,1)S(1)}, u32[]{:S(2)}) copy-start(bf16[2,3,272,128]{3,2,1,0:T(8,128)(2,1)S(1)} %collective-permute-done.11.refs_1_.refs_2_) | copy-start | bytes 1253380
  132.9 1.8 %copy-start.20 = (bf16[2,2,272,128]{3,2,1,0:T(8,128)(2,1)S(1)}, bf16[2,2,272,128]{3,2,1,0:T(8,128)(2,1)}, u32[]{:S(2)}) copy-start(bf16[2,2,272,128]{3,2,1,0:T(8,128)(2,1)} %copy-done.18) | copy-start | bytes 835588
  132.9 0.7 copy-start.21
  134.7 4.0 %copy-start.13 = (bf16[2,3,272,128]{3,2,1,0:T(8,128)(2,1)S(1)}, bf16[2,3,272,128]{3,2,1,0:T(8,128)(2,1)}, u32[]{:S(2)}) copy-start(bf16[2,3,272,128]{3,2,1,0:T(8,128)(2,1)} %copy-done.11) | copy-start | bytes 1253380
  134.7 4.0 %copy-start.15 = (bf16[2,3,272,128]{3,2,1,0:T(8,128)(2,1)S(1)}, bf16[2,3,272,128]{3,2,1,0:T(8,128)(2,1)}, u32[]{:S(2)}) copy-start(bf16[2,3,272,128]{3,2,1,0:T(8,128)(2,1)} %copy-done.14) | copy-start | bytes 1253380
  134.7 4.0 %copy-start.17 = (bf16[2,3,272,128]{3,2,1,0:T(8,128)(2,1)S(1)}, bf16[2,3,272,128]{3,2,1,0:T(8,128)(2,1)}, u32[]{:S(2)}) copy-start(bf16[2,3,272,128]{3,2,1,0:T(8,128)(2,1)} %copy-done.16) | copy-start | bytes 1253380

commit v15 on v14

--- a/solution.py
+++ b/solution.py
@@ -195,30 +195,31 @@
         def pick(d, end, far_at, other):
             @pl.when(end)
             def _():
-                out[0, d] = far_ref[far_at, 0]
+                out[:, d] = far_ref[far_at]
 
             @pl.when(jnp.logical_not(end))
             def _():
-                out[0, d] = other[0]
-
-        out[0, 0] = own_ref[0]
+                out[:, d] = other[...]
+
+        out[:, 0] = own_ref[...]
         pick(1, first, 0, up_ref)
         pick(2, jnp.logical_or(first, last), 1, across_ref)
         pick(3, last, 0, down_ref)
 
     inner = own.shape[1:]
+    step = max(1, own.shape[0] // 2)
     zeros = (0,) * len(inner)
-    one = pl.BlockSpec((1,) + inner, lambda f, me_ref: (f,) + zeros)
+    one = pl.BlockSpec((step,) + inner, lambda f, me_ref: (f,) + zeros)
     corners = [pl.BlockSpec(corner_of(x), lambda f, me_ref, n=x.ndim: (0,) * n) for x in waits]
     return pl.pallas_call(
         kernel,
         grid_spec=pltpu.PrefetchScalarGridSpec(
             num_scalar_prefetch=1,
-            grid=own.shape[:1],
+            grid=(own.shape[0] // step,),
             in_specs=[one] * 4
-            + [pl.BlockSpec((2, 1) + inner, lambda f, me_ref: (0, f) + zeros)]
+            + [pl.BlockSpec((2, step) + inner, lambda f, me_ref: (0, f) + zeros)]
             + corners,
-            out_specs=pl.BlockSpec((1, 4) + inner, lambda f, me_ref: (f, 0) + zeros),
+            out_specs=pl.BlockSpec((step, 4) + inner, lambda f, me_ref: (f, 0) + zeros),
         ),
         out_shape=jax.ShapeDtypeStruct(own.shape[:1] + (4,) + inner, own.dtype),
         compiler_params=pltpu.CompilerParams(vmem_limit_bytes=VMEM_LIMIT),
@@ -364,9 +365,6 @@
     up, down = neighbours(pairs, "tp", t_ways)
     if t_ways == 4:
         across = lax.ppermute(pairs, "tp", [(0, 2), (3, 1)])
-        near = token([up, down, across], TOKEN_MICROS)
-        passed = pass_on(me, across, up, down, [])
-        far = lax.ppermute(passed, "tp", [(1, 0), (2, 3)])
 
     exchanged, sent = [], []
     for at, items in enumerate(chunks):
@@ -374,12 +372,15 @@
         waits = sent[at - 1][:1] if at else []
         if at >= 2:
             waits = waits + exchanged[at - 2][1:]
-        if t_ways == 4:
-            waits = waits + [[near], [passed], [far]][min(at, 2)]
+        if t_ways == 4 and at:
+            waits = waits + ([passed] if at == 1 else [far])
         pieces = list(
             cut(rows, slice_map, blocks, 0, len(items), item_rows, waits, CUT_MICROS)
         )
         sent.append(pieces)
+        if t_ways == 4 and at == 0:
+            passed = pass_on(me, across, up, down, pieces[:1])
+            far = lax.ppermute(passed, "tp", [(1, 0), (2, 3)])
         exchanged.append(
             pieces[:1]
             + [

time: 157 us -> 158 us (level)
  waiting for transfers between devices: 66.1 us -> 70.3 us
  Pallas kernels: 31.6 us -> 29 us
    ppermute x9, waiting for transfers between devices: 32.9 us -> 4.88 us  [per_device(): lax.ppermute(piece, 'tp', [(i, (i + shift) % t_ways) for i in range(t_way...]
    all_to_all x4, waiting for transfers between devices: 18.6 us -> 46.1 us  [over_fsdp(): x = lax.all_to_all(x, 'fsdp', split_axis=0, concat_axis=0, tiled=True)]
    ppermute x1, waiting for transfers between devices: 0.01 us -> 18.2 us  [per_device(): far = lax.ppermute(passed, 'tp', [(1, 0), (2, 3)])]
    ppermute x1, waiting for transfers between devices: 10 us -> 0.01 us  [neighbours(): lax.ppermute(x, axis, [(i + 1, i) for i in range(ways - 1)])]
    ppermute x1, waiting for transfers between devices: 4.47 us -> 1.08 us  [per_device(): across = lax.ppermute(pairs, 'tp', [(0, 2), (3, 1)])]
    ppermute x1, starting transfers between devices: 5.59 us -> 2.35 us  [neighbours(): lax.ppermute(x, axis, [(i + 1, i) for i in range(ways - 1)])]
    pallas_call x1, Pallas kernels: 3.92 us -> 1.46 us  [join(): pl.pallas_call(kernel, grid_spec=pltpu.PrefetchScalarGridSpec(num_scalar_...]
    unnamed x59 -> x31, local copies, waits for them, and re-layouts: 12.8 us -> 13 us
  transfers between devices with their start and end apart: 17 -> 17, of which waited for: 9 -> 9; matrix products, arithmetic and copies ran while one was open for 0% -> 0% of each run, Pallas kernels for 14% -> 12%
where the time goes in v15:
time: 158 us; the launch traced here: 157 us
  waiting for transfers between devices  70.3 us (44%)
  starting transfers between devices  44.2 us (28%)
  Pallas kernels  29 us (18%)
  local copies, waits for them, and re-layouts  13 us (8%)
    all_to_all x4, waiting for transfers between devices, over_fsdp(): x = lax.all_to_all(x, 'fsdp', split_axis=0, concat_axis=0, tiled=True)  46.1 us
    all_to_all x4, starting transfers between devices, over_fsdp(): x = lax.all_to_all(x, 'fsdp', split_axis=0, concat_axis=0, tiled=True)  19.3 us
    ppermute x1, waiting for transfers between devices, per_device(): far = lax.ppermute(passed, 'tp', [(1, 0), (2, 3)])  18.2 us
    pallas_call x3, Pallas kernels, absorb(): pl.pallas_call(kernel, grid_spec=pltpu.PrefetchScalarGridSpec(num_scalar_...  14.7 us
    ppermute x9, starting transfers between devices, per_device(): lax.ppermute(piece, 'tp', [(i, (i + shift) % t_ways) for i in range(t_way...  14 us
    unnamed x31, local copies, waits for them, and re-layouts  13 us
    pallas_call x3, Pallas kernels, cut(): pl.pallas_call(kernel, grid=(1,), out_shape=[jax.ShapeDtypeStruct(shape,...  5.04 us
    ppermute x9, waiting for transfers between devices, per_device(): lax.ppermute(piece, 'tp', [(i, (i + shift) % t_ways) for i in range(t_way...  4.88 us
  transfers between devices with their start and end apart: 17, of which 9 were waited for; matrix products, arithmetic and copies ran while one was open for 0% of the time, Pallas kernels for 12%

profile of v15, /device:TPU:10, one launch (start us, length us, event | category | flops | bytes accessed | tf_op | source)
XLA Modules:
  0.0 157.3 jit_solution(10264121621460584960)
XLA Ops:
  0.6 0.8 copy.10.offsets
  1.4 3.1 %copy.14 = bf16[1,2,9728,128]{3,2,1,0:T(8,128)(2,1)S(1)} copy(bf16[1,2,9728,128]{3,1,2,0:T(2,128)(2,1)} %bitcast.15) | data formatting | bytes 9961472
  4.5 0.0 copy-done.9
  4.6 4.4 %pack.1 = (bf16[8,16,16,128]{3,2,1,0:T(8,128)(2,1)}, bf16[8,34,16,128]{3,2,1,0:T(8,128)(2,1)}, bf16[8,51,16,128]{3,2,1,0:T(8,128)(2,1)}, bf16[8,51,16,128]{3,2,1,0:T(8,128)(2,1)}) custom-call(s32[2,32,4]{2,1,0:T(8,128)S(1)} %copy.10.offsets, s32[2,32]{1,0:T(2,128)S(1)} %copy-done.9, bf16[2,608,16,128]{3,2,1,0:T(8,128)(2,1)S(1)} %bitcast.10), custom_call_target="tpu_custom_call" | custom-call | bytes 9961472 | tf_op jit(solution)/shard_map/pack/pallas_call | solution.py:77
  9.0 4.4 %all-to-all-start.2 = ((bf16[8,34,16,128]{3,2,1,0:T(8,128)(2,1)}), bf16[8,34,16,128]{3,2,1,0:T(8,128)(2,1)S(1)}, u32[]{:S(2)}, u32[]{:S(2)}) async-start(bf16[8,34,16,128]{3,2,1,0:T(8,128)(2,1)} %get-tuple-element.26), calls=%async_computation.2 | async-start | bytes 2228224 | tf_op jit(solution)/shard_map/all_to_all | solution.py:352
  13.4 2.3 %collective-permute-start.2 = (bf16[8,8,2,16,128]{4,3,2,1,0:T(8,128)(2,1)}, bf16[8,8,2,16,128]{4,3,2,1,0:T(8,128)(2,1)S(1)}, u32[]{:S(2)}, u32[]{:S(2)}) collective-permute-start(bf16[8,8,2,16,128]{4,3,2,1,0:T(8,128)(2,1)} %bitcast.4.own_ref), channel_id=1, source_target_pairs={{1,0},{2,1},{3,2},{5,4},{6,5},{7,6},{9,8},{10,9},{11,10},{13,12},{... | collective-permute-start | bytes 1572872 | tf_op jit(solution)/shard_map/ppermute | solution.py:157
  15.7 3.5 %collective-permute-start.1 = (bf16[8,8,2,16,128]{4,3,2,1,0:T(8,128)(2,1)}, bf16[8,8,2,16,128]{4,3,2,1,0:T(8,128)(2,1)S(1)}, u32[]{:S(2)}, u32[]{:S(2)}) collective-permute-start(bf16[8,8,2,16,128]{4,3,2,1,0:T(8,128)(2,1)} %bitcast.4.own_ref), channel_id=1, source_target_pairs={{0,1},{1,2},{2,3},{4,5},{5,6},{6,7},{8,9},{9,10},{10,11},{12,13},{... | collective-permute-start | bytes 1572872 | tf_op jit(solution)/shard_map/ppermute | solution.py:156
  19.2 1.3 collective-permute-start
  20.5 0.0 copy-done.13
  20.5 0.1 copy.13.mapped
  20.6 7.4 %all-to-all-done.2 = bf16[8,34,16,128]{3,2,1,0:T(8,128)(2,1)S(1)} async-done(((bf16[8,34,16,128]{3,2,1,0:T(8,128)(2,1)}), bf16[8,34,16,128]{3,2,1,0:T(8,128)(2,1)S(1)}, u32[]{:S(2)}, u32[]{:S(2)}) %all-to-all-start.2) | async-done | bytes 1114144 | tf_op jit(solution)/shard_map/all_to_all | solution.py:352
  28.0 1.0 copy-done.1
  29.0 5.0 %all-to-all-start.1 = ((bf16[8,51,16,128]{3,2,1,0:T(8,128)(2,1)}), bf16[8,51,16,128]{3,2,1,0:T(8,128)(2,1)S(1)}, u32[]{:S(2)}, u32[]{:S(2)}) async-start(bf16[8,51,16,128]{3,2,1,0:T(8,128)(2,1)} %get-tuple-element.25), calls=%async_computation.1 | async-start | bytes 3342336 | tf_op jit(solution)/shard_map/all_to_all | solution.py:352
  34.0 1.2 copy-done.2
  35.2 1.6 %cut.3 = (bf16[2,2,272,128]{3,2,1,0:T(8,128)(2,1)S(1)}, bf16[2,2,272,128]{3,2,1,0:T(8,128)(2,1)}, bf16[2,2,272,128]{3,2,1,0:T(8,128)(2,1)}, bf16[2,2,272,128]{3,2,1,0:T(8,128)(2,1)}) custom-call(s32[8,4]{1,0:T(8,128)S(1)} %copy.13.mapped, bf16[8,544,128]{2,1,0:T(8,128)(2,1)S(1)} %bitcast.12), custom_call_target="tpu_custom_call" | custom-call | flops 34500001792 | bytes 2228224 | tf_op jit(solution)/shard_map/cut/pallas_call | solution.py:121
  36.9 1.6 %collective-permute-start.3 = (bf16[2,2,272,128]{3,2,1,0:T(8,128)(2,1)}, bf16[2,2,272,128]{3,2,1,0:T(8,128)(2,1)}, u32[]{:S(2)}, u32[]{:S(2)}) collective-permute-start(bf16[2,2,272,128]{3,2,1,0:T(8,128)(2,1)} %get-tuple-element.30), channel_id=1, source_target_pairs={{0,1},{1,2},{2,3},{3,0},{4,5},{5,6},{6,7},{7,4},{8,9},{9,10},{10,1... | collective-permute-start | bytes 835592 | tf_op jit(solution)/shard_map/ppermute | solution.py:387
  38.4 1.2 collective-permute-start.4
  39.7 0.0 collective-permute-done.2.below.down_ref
  39.7 1.8 %collective-permute-start.5 = (bf16[2,2,272,128]{3,2,1,0:T(8,128)(2,1)}, bf16[2,2,272,128]{3,2,1,0:T(8,128)(2,1)}, u32[]{:S(2)}, u32[]{:S(2)}) collective-permute-start(bf16[2,2,272,128]{3,2,1,0:T(8,128)(2,1)} %get-tuple-element.32), channel_id=1, source_target_pairs={{0,3},{1,0},{2,1},{3,2},{4,7},{5,4},{6,5},{7,6},{8,11},{9,8},{10,9... | collective-permute-start | bytes 835592 | tf_op jit(solution)/shard_map/ppermute | solution.py:387
  41.5 0.0 collective-permute-done.1.above.up_ref
  41.5 1.1 collective-permute-done.first.across_ref
  42.6 1.1 pass_on.1.refs_1_
  43.6 3.9 %collective-permute-start.6 = (bf16[2,8,8,2,16,128]{5,4,3,2,1,0:T(8,128)(2,1)}, bf16[2,8,8,2,16,128]{5,4,3,2,1,0:T(8,128)(2,1)}, u32[]{:S(2)}, u32[]{:S(2)}) collective-permute-start(bf16[2,8,8,2,16,128]{5,4,3,2,1,0:T(8,128)(2,1)} %pass_on.1.refs_1_), channel_id=1, source_target_pairs={{1,0},{2,3},{5,4},{6,7},{9,8},{10,11},{13,12},{14,15},{17,16},{18,... | collective-permute-start | bytes 3145736 | tf_op jit(solution)/shard_map/ppermute | solution.py:383
  47.5 7.1 %all-to-all-done.1 = bf16[8,51,16,128]{3,2,1,0:T(8,128)(2,1)S(1)} async-done(((bf16[8,51,16,128]{3,2,1,0:T(8,128)(2,1)}), bf16[8,51,16,128]{3,2,1,0:T(8,128)(2,1)S(1)}, u32[]{:S(2)}, u32[]{:S(2)}) %all-to-all-start.1) | async-done | bytes 1671200 | tf_op jit(solution)/shard_map/all_to_all | solution.py:352
  54.6 5.7 %all-to-all-start = ((bf16[8,51,16,128]{3,2,1,0:T(8,128)(2,1)}), bf16[8,51,16,128]{3,2,1,0:T(8,128)(2,1)}, u32[]{:S(2)}, u32[]{:S(2)}) async-start(bf16[8,51,16,128]{3,2,1,0:T(8,128)(2,1)} %get-tuple-element.24), calls=%async_computation | async-start | bytes 3342336 | tf_op jit(solution)/shard_map/all_to_all | solution.py:352
  60.3 1.8 %cut.4 = (bf16[2,3,272,128]{3,2,1,0:T(8,128)(2,1)S(1)}, bf16[2,3,272,128]{3,2,1,0:T(8,128)(2,1)}, bf16[2,3,272,128]{3,2,1,0:T(8,128)(2,1)}, bf16[2,3,272,128]{3,2,1,0:T(8,128)(2,1)}) custom-call(s32[8,4]{1,0:T(8,128)S(1)} %copy.13.mapped, bf16[8,816,128]{2,1,0:T(8,128)(2,1)S(1)} %bitcast.11, bf16[2,2,272,128]{3,2,1,0:T(8,128)(2,1)S(1)} %get-tuple-element.27.refs_0_, ...), custom_call_target="tpu_custom_call" | custom-call | flops 34500001792 | bytes 3342336 | tf_op jit(solution)/shard_map/cut/pallas_call | solution.py:121
  62.1 0.7 copy-done.3
  62.9 1.6 %collective-permute-start.10 = (bf16[2,3,272,128]{3,2,1,0:T(8,128)(2,1)}, bf16[2,3,272,128]{3,2,1,0:T(8,128)(2,1)S(1)}, u32[]{:S(2)}, u32[]{:S(2)}) collective-permute-start(bf16[2,3,272,128]{3,2,1,0:T(8,128)(2,1)} %get-tuple-element.37), channel_id=1, source_target_pairs={{0,1},{1,2},{2,3},{3,0},{4,5},{5,6},{6,7},{7,4},{8,9},{9,10},{10,1... | collective-permute-start | bytes 1253384 | tf_op jit(solution)/shard_map/ppermute | solution.py:387
  64.5 0.0 collective-permute-done.3.refs_1_
  64.5 1.2 collective-permute-start.11
  65.7 0.1 collective-permute-done.4.refs_2_
  65.8 1.7 %collective-permute-start.12 = (bf16[2,3,272,128]{3,2,1,0:T(8,128)(2,1)}, bf16[2,3,272,128]{3,2,1,0:T(8,128)(2,1)}, u32[]{:S(2)}, u32[]{:S(2)}) collective-permute-start(bf16[2,3,272,128]{3,2,1,0:T(8,128)(2,1)} %get-tuple-element.39), channel_id=1, source_target_pairs={{0,3},{1,0},{2,1},{3,2},{4,7},{5,4},{6,5},{7,6},{8,11},{9,8},{10,9... | collective-permute-start | bytes 1253384 | tf_op jit(solution)/shard_map/ppermute | solution.py:387
  67.5 0.0 collective-permute-done.5.refs_3_
  67.5 13.5 %all-to-all-done = bf16[8,51,16,128]{3,2,1,0:T(8,128)(2,1)} async-done(((bf16[8,51,16,128]{3,2,1,0:T(8,128)(2,1)}), bf16[8,51,16,128]{3,2,1,0:T(8,128)(2,1)}, u32[]{:S(2)}, u32[]{:S(2)}) %all-to-all-start) | async-done | bytes 1671200 | tf_op jit(solution)/shard_map/all_to_all | solution.py:352
  81.0 18.2 %collective-permute-done.6.refs_4_.far_ref = bf16[2,8,8,2,16,128]{5,4,3,2,1,0:T(8,128)(2,1)} collective-permute-done((bf16[2,8,8,2,16,128]{5,4,3,2,1,0:T(8,128)(2,1)}, bf16[2,8,8,2,16,128]{5,4,3,2,1,0:T(8,128)(2,1)}, u32[]{:S(2)}, u32[]{:S(2)}) %collective-permute-start.6) | collective-permute-done | bytes 1048608 | tf_op jit(solution)/shard_map/ppermute | solution.py:383
  99.1 1.0 copy-done.4
  100.2 1.6 %cut.5 = (bf16[2,3,272,128]{3,2,1,0:T(8,128)(2,1)S(1)}, bf16[2,3,272,128]{3,2,1,0:T(8,128)(2,1)S(1)}, bf16[2,3,272,128]{3,2,1,0:T(8,128)(2,1)S(1)}, bf16[2,3,272,128]{3,2,1,0:T(8,128)(2,1)S(1)}) custom-call(s32[8,4]{1,0:T(8,128)S(1)} %copy.13.mapped, bf16[8,816,128]{2,1,0:T(8,128)(2,1)} %bitcast.1.source, bf16[2,3,272,128]{3,2,1,0:T(8,128)(2,1)S(1)} %copy-done.4, ...), custom_call_target="tpu_custom_call" | custom-call | flops 34500001792 | bytes 3342336 | tf_op jit(solution)/shard_map/cut/pallas_call | solution.py:121
  101.7 0.0 copy-start.10
  101.8 0.8 copy-done.10
  102.5 0.8 copy-done.12
  103.3 0.7 copy-done.11
  104.0 1.5 join.1
  105.5 0.0 copy-start
  105.5 1.3 copy-done
  106.8 4.2 %all-to-all-start.3 = ((bf16[8,4,8,2,16,128]{5,4,3,2,1,0:T(8,128)(2,1)}), bf16[8,4,8,2,16,128]{5,4,3,2,1,0:T(8,128)(2,1)S(1)}, u32[]{:S(2)}, u32[]{:S(2)}) async-start(bf16[8,4,8,2,16,128]{5,4,3,2,1,0:T(8,128)(2,1)} %copy-done), calls=%async_computation.3 | async-start | bytes 4194304 | tf_op jit(solution)/shard_map/all_to_all | solution.py:352
  111.0 0.0 collective-permute-start.7
  111.0 4.8 %collective-permute-start.8 = (bf16[2,3,272,128]{3,2,1,0:T(8,128)(2,1)}, bf16[2,3,272,128]{3,2,1,0:T(8,128)(2,1)}, u32[]{:S(2)}, u32[]{:S(2)}) collective-permute-start(bf16[2,3,272,128]{3,2,1,0:T(8,128)(2,1)} %copy-done.11), channel_id=1, source_target_pairs={{0,2},{1,3},{2,0},{3,1},{4,6},{5,7},{6,4},{7,5},{8,10},{9,11},{10,... | collective-permute-start | bytes 1253384 | tf_op jit(solution)/shard_map/ppermute | solution.py:387
  115.8 0.0 collective-permute-done.10.refs_0_.refs_1_
  115.9 0.0 collective-permute-start.9
  115.9 0.0 collective-permute-done.11.refs_1_.refs_2_
  115.9 0.0 collective-permute-done.12.refs_2_.refs_3_
  115.9 0.8 copy-done.6
  116.6 1.3 token_.1.refs_0_
  117.9 18.2 %all-to-all-done.3.pieces = bf16[8,4,8,2,16,128]{5,4,3,2,1,0:T(8,128)(2,1)S(1)} async-done(((bf16[8,4,8,2,16,128]{5,4,3,2,1,0:T(8,128)(2,1)}), bf16[8,4,8,2,16,128]{5,4,3,2,1,0:T(8,128)(2,1)S(1)}, u32[]{:S(2)}, u32[]{:S(2)}) %all-to-all-start.3) | async-done | bytes 2097184 | tf_op jit(solution)/shard_map/all_to_all | solution.py:352
  136.1 0.7 copy-done.8
  136.8 1.0 assemble.1.refs_4_
  137.9 0.0 copy-start.5
  137.9 4.0 %absorb.3 = (bf16[8,2,4,48,512]{4,3,2,1,0:T(8,128)(2,1)}, bf16[8,2,4,224,512]{4,3,2,1,0:T(8,128)(2,1)}) custom-call(s32[1]{0:T(128)} %bitcast.me_ref.at, bf16[2,2,272,128]{3,2,1,0:T(8,128)(2,1)S(1)} %get-tuple-element.27.refs_0_, bf16[2,2,272,128]{3,2,1,0:T(8,128)(2,1)} %collective-permute-done.3.refs_1_, ...), custom_call_target="tpu_custom_call" | custom-call | flops 570425344 | bytes 5570560 | tf_op jit(solution)/shard_map/absorb/pallas_call | solution.py:297
  141.9 0.0 copy-done.7
  141.9 5.2 %absorb.4 = (bf16[8,2,4,48,512]{4,3,2,1,0:T(8,128)(2,1)}, bf16[8,2,4,224,512]{4,3,2,1,0:T(8,128)(2,1)}) custom-call(s32[1]{0:T(128)} %bitcast.me_ref.at, bf16[2,3,272,128]{3,2,1,0:T(8,128)(2,1)S(1)} %copy-done.5, bf16[2,3,272,128]{3,2,1,0:T(8,128)(2,1)S(1)} %copy-done.7, ...), custom_call_target="tpu_custom_call", output_to_operand_aliasing={{0}: (6, {}), {1}: (7, {})} | custom-call | flops 855638016 | bytes 8355840 | tf_op jit(solution)/shard_map/absorb/pallas_call | solution.py:297
  147.1 0.0 collective-permute-done.7.refs_1_
  147.1 0.6 collective-permute-done.8.refs_2_
  147.7 4.2 %collective-permute-done.9.refs_3_ = bf16[2,3,272,128]{3,2,1,0:T(8,128)(2,1)} collective-permute-done((bf16[2,3,272,128]{3,2,1,0:T(8,128)(2,1)}, bf16[2,3,272,128]{3,2,1,0:T(8,128)(2,1)}, u32[]{:S(2)}, u32[]{:S(2)}) %collective-permute-start.9) | collective-permute-done | bytes 417824 | tf_op jit(solution)/shard_map/ppermute | solution.py:387
  151.8 5.5 %absorb.5 = (bf16[8,2,4,48,512]{4,3,2,1,0:T(8,128)(2,1)}, bf16[8,2,4,224,512]{4,3,2,1,0:T(8,128)(2,1)}) custom-call(s32[1]{0:T(128)} %bitcast.me_ref.at, bf16[2,3,272,128]{3,2,1,0:T(8,128)(2,1)S(1)} %get-tuple-element.33.refs_0_, bf16[2,3,272,128]{3,2,1,0:T(8,128)(2,1)} %collective-permute-done.7.refs_1_, ...), custom_call_target="tpu_custom_call", output_to_operand_aliasing={{0}: (6, {}), {1}: (7, {})} | custom-call | flops 855638016 | bytes 8355840 | tf_op jit(solution)/shard_map/absorb/pallas_call | solution.py:297
  (12 shorter events, 0.0 us)
Async XLA Ops:
  1.4 3.1 %copy-start.9 = (s32[2,32]{1,0:T(2,128)S(1)}, s32[2,32]{1,0:T(2,128)}, u32[]{:S(2)}) copy-start(s32[2,32]{1,0:T(2,128)} %owners.1) | copy-start | bytes 772
  9.0 11.5 %copy-start.13 = (s32[8,4]{0,1:T(4,128)S(1)}, s32[8,4]{0,1:T(4,128)}, u32[]{:S(2)}) copy-start(s32[8,4]{0,1:T(4,128)} %param.7) | copy-start | bytes 388
  9.0 19.0 %all-to-all-start.2 = ((bf16[8,34,16,128]{3,2,1,0:T(8,128)(2,1)}), bf16[8,34,16,128]{3,2,1,0:T(8,128)(2,1)S(1)}, u32[]{:S(2)}, u32[]{:S(2)}) async-start(bf16[8,34,16,128]{3,2,1,0:T(8,128)(2,1)} %get-tuple-element.26), calls=%async_computation.2 | async-start | bytes 2228224 | tf_op jit(solution)/shard_map/all_to_all | solution.py:352
  13.4 26.3 %collective-permute-start.2 = (bf16[8,8,2,16,128]{4,3,2,1,0:T(8,128)(2,1)}, bf16[8,8,2,16,128]{4,3,2,1,0:T(8,128)(2,1)S(1)}, u32[]{:S(2)}, u32[]{:S(2)}) collective-permute-start(bf16[8,8,2,16,128]{4,3,2,1,0:T(8,128)(2,1)} %bitcast.4.own_ref), channel_id=1, source_target_pairs={{1,0},{2,1},{3,2},{5,4},{6,5},{7,6},{9,8},{10,9},{11,10},{13,12},{... | collective-permute-start | bytes 1572872 | tf_op jit(solution)/shard_map/ppermute | solution.py:157
  15.7 25.8 %collective-permute-start.1 = (bf16[8,8,2,16,128]{4,3,2,1,0:T(8,128)(2,1)}, bf16[8,8,2,16,128]{4,3,2,1,0:T(8,128)(2,1)S(1)}, u32[]{:S(2)}, u32[]{:S(2)}) collective-permute-start(bf16[8,8,2,16,128]{4,3,2,1,0:T(8,128)(2,1)} %bitcast.4.own_ref), channel_id=1, source_target_pairs={{0,1},{1,2},{2,3},{4,5},{5,6},{6,7},{8,9},{9,10},{10,11},{12,13},{... | collective-permute-start | bytes 1572872 | tf_op jit(solution)/shard_map/ppermute | solution.py:156
  19.2 23.4 %collective-permute-start = (bf16[8,8,2,16,128]{4,3,2,1,0:T(8,128)(2,1)}, bf16[8,8,2,16,128]{4,3,2,1,0:T(8,128)(2,1)S(1)}, u32[]{:S(2)}, u32[]{:S(2)}) collective-permute-start(bf16[8,8,2,16,128]{4,3,2,1,0:T(8,128)(2,1)} %bitcast.4.own_ref), channel_id=1, source_target_pairs={{0,2},{3,1},{4,6},{7,5},{8,10},{11,9},{12,14},{15,13},{16,18},{19,... | collective-permute-start | bytes 1572872 | tf_op jit(solution)/shard_map/ppermute | solution.py:367
  28.0 1.0 copy-start.1
  29.0 25.6 %all-to-all-start.1 = ((bf16[8,51,16,128]{3,2,1,0:T(8,128)(2,1)}), bf16[8,51,16,128]{3,2,1,0:T(8,128)(2,1)S(1)}, u32[]{:S(2)}, u32[]{:S(2)}) async-start(bf16[8,51,16,128]{3,2,1,0:T(8,128)(2,1)} %get-tuple-element.25), calls=%async_computation.1 | async-start | bytes 3342336 | tf_op jit(solution)/shard_map/all_to_all | solution.py:352
  34.0 1.2 copy-start.2
  36.9 27.6 %collective-permute-start.3 = (bf16[2,2,272,128]{3,2,1,0:T(8,128)(2,1)}, bf16[2,2,272,128]{3,2,1,0:T(8,128)(2,1)}, u32[]{:S(2)}, u32[]{:S(2)}) collective-permute-start(bf16[2,2,272,128]{3,2,1,0:T(8,128)(2,1)} %get-tuple-element.30), channel_id=1, source_target_pairs={{0,1},{1,2},{2,3},{3,0},{4,5},{5,6},{6,7},{7,4},{8,9},{9,10},{10,1... | collective-permute-start | bytes 835592 | tf_op jit(solution)/shard_map/ppermute | solution.py:387
  38.4 27.4 %collective-permute-start.4 = (bf16[2,2,272,128]{3,2,1,0:T(8,128)(2,1)}, bf16[2,2,272,128]{3,2,1,0:T(8,128)(2,1)}, u32[]{:S(2)}, u32[]{:S(2)}) collective-permute-start(bf16[2,2,272,128]{3,2,1,0:T(8,128)(2,1)} %get-tuple-element.31), channel_id=1, source_target_pairs={{0,2},{1,3},{2,0},{3,1},{4,6},{5,7},{6,4},{7,5},{8,10},{9,11},{10,... | collective-permute-start | bytes 835592 | tf_op jit(solution)/shard_map/ppermute | solution.py:387
  39.7 27.8 %collective-permute-start.5 = (bf16[2,2,272,128]{3,2,1,0:T(8,128)(2,1)}, bf16[2,2,272,128]{3,2,1,0:T(8,128)(2,1)}, u32[]{:S(2)}, u32[]{:S(2)}) collective-permute-start(bf16[2,2,272,128]{3,2,1,0:T(8,128)(2,1)} %get-tuple-element.32), channel_id=1, source_target_pairs={{0,3},{1,0},{2,1},{3,2},{4,7},{5,4},{6,5},{7,6},{8,11},{9,8},{10,9... | collective-permute-start | bytes 835592 | tf_op jit(solution)/shard_map/ppermute | solution.py:387
  43.6 55.5 %collective-permute-start.6 = (bf16[2,8,8,2,16,128]{5,4,3,2,1,0:T(8,128)(2,1)}, bf16[2,8,8,2,16,128]{5,4,3,2,1,0:T(8,128)(2,1)}, u32[]{:S(2)}, u32[]{:S(2)}) collective-permute-start(bf16[2,8,8,2,16,128]{5,4,3,2,1,0:T(8,128)(2,1)} %pass_on.1.refs_1_), channel_id=1, source_target_pairs={{1,0},{2,3},{5,4},{6,7},{9,8},{10,11},{13,12},{14,15},{17,16},{18,... | collective-permute-start | bytes 3145736 | tf_op jit(solution)/shard_map/ppermute | solution.py:383
  54.6 26.4 %all-to-all-start = ((bf16[8,51,16,128]{3,2,1,0:T(8,128)(2,1)}), bf16[8,51,16,128]{3,2,1,0:T(8,128)(2,1)}, u32[]{:S(2)}, u32[]{:S(2)}) async-start(bf16[8,51,16,128]{3,2,1,0:T(8,128)(2,1)} %get-tuple-element.24), calls=%async_computation | async-start | bytes 3342336 | tf_op jit(solution)/shard_map/all_to_all | solution.py:352
  62.1 0.7 copy-start.3
  62.9 53.0 %collective-permute-start.10 = (bf16[2,3,272,128]{3,2,1,0:T(8,128)(2,1)}, bf16[2,3,272,128]{3,2,1,0:T(8,128)(2,1)S(1)}, u32[]{:S(2)}, u32[]{:S(2)}) collective-permute-start(bf16[2,3,272,128]{3,2,1,0:T(8,128)(2,1)} %get-tuple-element.37), channel_id=1, source_target_pairs={{0,1},{1,2},{2,3},{3,0},{4,5},{5,6},{6,7},{7,4},{8,9},{9,10},{10,1... | collective-permute-start | bytes 1253384 | tf_op jit(solution)/shard_map/ppermute | solution.py:387
  64.5 51.4 %collective-permute-start.11 = (bf16[2,3,272,128]{3,2,1,0:T(8,128)(2,1)}, bf16[2,3,272,128]{3,2,1,0:T(8,128)(2,1)}, u32[]{:S(2)}, u32[]{:S(2)}) collective-permute-start(bf16[2,3,272,128]{3,2,1,0:T(8,128)(2,1)} %get-tuple-element.38), channel_id=1, source_target_pairs={{0,2},{1,3},{2,0},{3,1},{4,6},{5,7},{6,4},{7,5},{8,10},{9,11},{10,... | collective-permute-start | bytes 1253384 | tf_op jit(solution)/shard_map/ppermute | solution.py:387
  65.8 50.1 %collective-permute-start.12 = (bf16[2,3,272,128]{3,2,1,0:T(8,128)(2,1)}, bf16[2,3,272,128]{3,2,1,0:T(8,128)(2,1)}, u32[]{:S(2)}, u32[]{:S(2)}) collective-permute-start(bf16[2,3,272,128]{3,2,1,0:T(8,128)(2,1)} %get-tuple-element.39), channel_id=1, source_target_pairs={{0,3},{1,0},{2,1},{3,2},{4,7},{5,4},{6,5},{7,6},{8,11},{9,8},{10,9... | collective-permute-start | bytes 1253384 | tf_op jit(solution)/shard_map/ppermute | solution.py:387
  99.1 1.0 copy-start.4
  101.7 0.8 copy-start.10
  102.5 0.8 copy-start.12
  103.3 0.7 copy-start.11
  105.5 1.3 copy-start
  106.8 29.3 %all-to-all-start.3 = ((bf16[8,4,8,2,16,128]{5,4,3,2,1,0:T(8,128)(2,1)}), bf16[8,4,8,2,16,128]{5,4,3,2,1,0:T(8,128)(2,1)S(1)}, u32[]{:S(2)}, u32[]{:S(2)}) async-start(bf16[8,4,8,2,16,128]{5,4,3,2,1,0:T(8,128)(2,1)} %copy-done), calls=%async_computation.3 | async-start | bytes 4194304 | tf_op jit(solution)/shard_map/all_to_all | solution.py:352
  111.0 36.1 %collective-permute-start.7 = (bf16[2,3,272,128]{3,2,1,0:T(8,128)(2,1)}, bf16[2,3,272,128]{3,2,1,0:T(8,128)(2,1)}, u32[]{:S(2)}, u32[]{:S(2)}) collective-permute-start(bf16[2,3,272,128]{3,2,1,0:T(8,128)(2,1)} %copy-done.12), channel_id=1, source_target_pairs={{0,1},{1,2},{2,3},{3,0},{4,5},{5,6},{6,7},{7,4},{8,9},{9,10},{10,1... | collective-permute-start | bytes 1253384 | tf_op jit(solution)/shard_map/ppermute | solution.py:387
  111.0 36.7 %collective-permute-start.8 = (bf16[2,3,272,128]{3,2,1,0:T(8,128)(2,1)}, bf16[2,3,272,128]{3,2,1,0:T(8,128)(2,1)}, u32[]{:S(2)}, u32[]{:S(2)}) collective-permute-start(bf16[2,3,272,128]{3,2,1,0:T(8,128)(2,1)} %copy-done.11), channel_id=1, source_target_pairs={{0,2},{1,3},{2,0},{3,1},{4,6},{5,7},{6,4},{7,5},{8,10},{9,11},{10,... | collective-permute-start | bytes 1253384 | tf_op jit(solution)/shard_map/ppermute | solution.py:387
  115.9 0.8 copy-start.6
  115.9 36.0 %collective-permute-start.9 = (bf16[2,3,272,128]{3,2,1,0:T(8,128)(2,1)}, bf16[2,3,272,128]{3,2,1,0:T(8,128)(2,1)}, u32[]{:S(2)}, u32[]{:S(2)}) collective-permute-start(bf16[2,3,272,128]{3,2,1,0:T(8,128)(2,1)} %copy-done.10), channel_id=1, source_target_pairs={{0,3},{1,0},{2,1},{3,2},{4,7},{5,4},{6,5},{7,6},{8,11},{9,8},{10,9... | collective-permute-start | bytes 1253384 | tf_op jit(solution)/shard_map/ppermute | solution.py:387
  136.1 0.7 copy-start.8
  137.9 4.0 %copy-start.5 = (bf16[2,3,272,128]{3,2,1,0:T(8,128)(2,1)S(1)}, bf16[2,3,272,128]{3,2,1,0:T(8,128)(2,1)}, u32[]{:S(2)}) copy-start(bf16[2,3,272,128]{3,2,1,0:T(8,128)(2,1)} %copy-done.3) | copy-start | bytes 1253380
  137.9 4.0 %copy-start.7 = (bf16[2,3,272,128]{3,2,1,0:T(8,128)(2,1)S(1)}, bf16[2,3,272,128]{3,2,1,0:T(8,128)(2,1)}, u32[]{:S(2)}) copy-start(bf16[2,3,272,128]{3,2,1,0:T(8,128)(2,1)} %copy-done.6) | copy-start | bytes 1253380

commit v16 on v15

--- a/solution.py
+++ b/solution.py
@@ -16,7 +16,7 @@
 LANES = 128
 QUERY, KEY, VALUE, OUT = range(4)
 CUT_MICROS = 30
-TOKEN_MICROS = 40
+TOKEN_MICROS = 80
 CUTS = (0, 2, 5, 8)
 VMEM_LIMIT = 16 * 1024 * 1024
 
@@ -158,53 +158,44 @@
     )
 
 
-def pass_on(me, across, up, down, waits):
-    def kernel(me_ref, first, above, below, *refs):
+def pass_on(me, own, up, down):
+    def kernel(me_ref, own_ref, up_ref, down_ref, out):
+        for source, mine in (
+            (own_ref, jnp.logical_or(me_ref[0] == 0, me_ref[0] == 3)),
+            (up_ref, me_ref[0] == 2),
+            (down_ref, me_ref[0] == 1),
+        ):
+
+            @pl.when(mine)
+            def _():
+                out[...] = source[...]
+
+    whole = pl.BlockSpec(own.shape, lambda _, me_ref: (0,) * own.ndim)
+    return pl.pallas_call(
+        kernel,
+        grid_spec=pltpu.PrefetchScalarGridSpec(
+            num_scalar_prefetch=1, grid=(1,), in_specs=[whole] * 3, out_specs=whole
+        ),
+        out_shape=jax.ShapeDtypeStruct(own.shape, own.dtype),
+        compiler_params=pltpu.CompilerParams(vmem_limit_bytes=VMEM_LIMIT),
+        name="pass_on",
+    )(me.reshape(1), own, up, down)
+
+
+def join(me, own, up, down, second, third, waits):
+    def kernel(me_ref, own_ref, up_ref, down_ref, second_ref, third_ref, *refs):
         out = refs[-1]
-        out[0] = first[...]
-
-        @pl.when(me_ref[0] == 2)
-        def _():
-            out[1] = above[...]
-
-        @pl.when(me_ref[0] != 2)
-        def _():
-            out[1] = below[...]
-
-    whole = pl.BlockSpec(across.shape, lambda _, me_ref: (0,) * across.ndim)
-    corners = [pl.BlockSpec(corner_of(x), lambda _, me_ref, n=x.ndim: (0,) * n) for x in waits]
-    return pl.pallas_call(
-        kernel,
-        grid_spec=pltpu.PrefetchScalarGridSpec(
-            num_scalar_prefetch=1,
-            grid=(1,),
-            in_specs=[whole] * 3 + corners,
-            out_specs=pl.BlockSpec((2,) + across.shape, lambda _, me_ref: (0,) * (across.ndim + 1)),
-        ),
-        out_shape=jax.ShapeDtypeStruct((2,) + across.shape, across.dtype),
-        compiler_params=pltpu.CompilerParams(vmem_limit_bytes=VMEM_LIMIT),
-        name="pass_on",
-    )(me.reshape(1), across, up, down, *waits)
-
-
-def join(me, own, up, down, across, far, waits):
-    def kernel(me_ref, own_ref, up_ref, down_ref, across_ref, far_ref, *refs):
-        out = refs[-1]
-        first, last = me_ref[0] == 0, me_ref[0] == 3
-
-        def pick(d, end, far_at, other):
+        out[:, 0] = own_ref[...]
+        out[:, 2] = second_ref[...]
+        for d, end, other in ((1, me_ref[0] == 0, up_ref), (3, me_ref[0] == 3, down_ref)):
+
             @pl.when(end)
             def _():
-                out[:, d] = far_ref[far_at]
+                out[:, d] = third_ref[...]
 
             @pl.when(jnp.logical_not(end))
             def _():
                 out[:, d] = other[...]
-
-        out[:, 0] = own_ref[...]
-        pick(1, first, 0, up_ref)
-        pick(2, jnp.logical_or(first, last), 1, across_ref)
-        pick(3, last, 0, down_ref)
 
     inner = own.shape[1:]
     step = max(1, own.shape[0] // 2)
@@ -216,15 +207,13 @@
         grid_spec=pltpu.PrefetchScalarGridSpec(
             num_scalar_prefetch=1,
             grid=(own.shape[0] // step,),
-            in_specs=[one] * 4
-            + [pl.BlockSpec((2, step) + inner, lambda f, me_ref: (0, f) + zeros)]
-            + corners,
+            in_specs=[one] * 5 + corners,
             out_specs=pl.BlockSpec((step, 4) + inner, lambda f, me_ref: (f, 0) + zeros),
         ),
         out_shape=jax.ShapeDtypeStruct(own.shape[:1] + (4,) + inner, own.dtype),
         compiler_params=pltpu.CompilerParams(vmem_limit_bytes=VMEM_LIMIT),
         name="join",
-    )(me.reshape(1), own, up, down, across, far, *waits)
+    )(me.reshape(1), own, up, down, second, third, *waits)
 
 
 def assemble(me, joined, waits):
@@ -364,7 +353,9 @@
     pairs = pairs.reshape(f_ways, item_count, 2, row_counts[KEY], LANES)
     up, down = neighbours(pairs, "tp", t_ways)
     if t_ways == 4:
-        across = lax.ppermute(pairs, "tp", [(0, 2), (3, 1)])
+        passed = pass_on(me, pairs, up, down)
+        second = lax.ppermute(passed, "tp", [(0, 2), (1, 0), (2, 3), (3, 1)])
+        third = lax.ppermute(second, "tp", [(1, 0), (2, 3)])
 
     exchanged, sent = [], []
     for at, items in enumerate(chunks):
@@ -372,15 +363,12 @@
         waits = sent[at - 1][:1] if at else []
         if at >= 2:
             waits = waits + exchanged[at - 2][1:]
-        if t_ways == 4 and at:
-            waits = waits + ([passed] if at == 1 else [far])
+        if t_ways == 4:
+            waits = waits + [[passed], [second], [third]][min(at, 2)]
         pieces = list(
             cut(rows, slice_map, blocks, 0, len(items), item_rows, waits, CUT_MICROS)
         )
         sent.append(pieces)
-        if t_ways == 4 and at == 0:
-            passed = pass_on(me, across, up, down, pieces[:1])
-            far = lax.ppermute(passed, "tp", [(1, 0), (2, 3)])
         exchanged.append(
             pieces[:1]
             + [
@@ -391,7 +379,7 @@
         )
 
     if t_ways == 4:
-        joined = join(me, pairs, up, down, across, far, sent[-1][:1])
+        joined = join(me, pairs, up, down, second, third, sent[-1][:1])
     else:
         ups, downs = [pairs, up], [pairs, down]
         for _ in range(2, t_ways):
@@ -407,7 +395,7 @@
             jax.ShapeDtypeStruct((item_count, blocks, t_ways, row_counts[kind], KVR), jnp.bfloat16)
             for kind in (QUERY, OUT)
         )
-        matrices = assemble(me, joined, [token(exchanged[-2][1:], TOKEN_MICROS)])
+        matrices = assemble(me, joined, [token(exchanged[-2][1:] + exchanged[-1][1:3], TOKEN_MICROS)])
         outs = None
         for items, parts in zip(chunks, exchanged):
             outs = absorb(me, items, parts, matrices, outs, shapes)

time: 158 us -> 164 us (1.038)
  waiting for transfers between devices: 70.3 us -> 73.4 us
  local copies, waits for them, and re-layouts: 13 us -> 15.9 us
  Pallas kernels: 29 us -> 27.3 us
    ppermute x9, waiting for transfers between devices: 4.88 us -> 43 us  [per_device(): lax.ppermute(piece, 'tp', [(i, (i + shift) % t_ways) for i in range(t_way...]
    all_to_all x4, waiting for transfers between devices: 46.1 us -> 17.8 us  [over_fsdp(): x = lax.all_to_all(x, 'fsdp', split_axis=0, concat_axis=0, tiled=True)]
    ppermute x2, waiting for transfers between devices: 19.2 us -> 0.55 us  [the longest x1 0.55 us: per_device(): second = lax.ppermute(passed, 'tp', [(0, 2), (1, 0), (2, 3), (3, 1)])]
    ppermute x1, waiting for transfers between devices: 0.01 us -> 9.92 us  [neighbours(): lax.ppermute(x, axis, [(i + 1, i) for i in range(ways - 1)])]
    unnamed x31 -> x45, local copies, waits for them, and re-layouts: 13 us -> 15.9 us
    ppermute x9, starting transfers between devices: 14 us -> 16.2 us  [per_device(): lax.ppermute(piece, 'tp', [(i, (i + shift) % t_ways) for i in range(t_way...]
    ppermute x1, waiting for transfers between devices: 0.01 us -> 2.09 us  [neighbours(): lax.ppermute(x, axis, [(i, i + 1) for i in range(ways - 1)])]
where the time goes in v16:
time: 164 us; the launch traced here: 162 us
  waiting for transfers between devices  73.4 us (45%)
  starting transfers between devices  45 us (27%)
  Pallas kernels  27.3 us (17%)
  local copies, waits for them, and re-layouts  15.9 us (10%)
    ppermute x9, waiting for transfers between devices, per_device(): lax.ppermute(piece, 'tp', [(i, (i + shift) % t_ways) for i in range(t_way...  43 us
    all_to_all x4, starting transfers between devices, over_fsdp(): x = lax.all_to_all(x, 'fsdp', split_axis=0, concat_axis=0, tiled=True)  18.6 us
    all_to_all x4, waiting for transfers between devices, over_fsdp(): x = lax.all_to_all(x, 'fsdp', split_axis=0, concat_axis=0, tiled=True)  17.8 us
    ppermute x9, starting transfers between devices, per_device(): lax.ppermute(piece, 'tp', [(i, (i + shift) % t_ways) for i in range(t_way...  16.2 us
    unnamed x45, local copies, waits for them, and re-layouts  15.9 us
    pallas_call x3, Pallas kernels, absorb(): pl.pallas_call(kernel, grid_spec=pltpu.PrefetchScalarGridSpec(num_scalar_...  13.8 us
    ppermute x1, waiting for transfers between devices, neighbours(): lax.ppermute(x, axis, [(i + 1, i) for i in range(ways - 1)])  9.92 us
    pallas_call x3, Pallas kernels, cut(): pl.pallas_call(kernel, grid=(1,), out_shape=[jax.ShapeDtypeStruct(shape,...  5.23 us
  transfers between devices with their start and end apart: 17, of which 9 were waited for; matrix products, arithmetic and copies ran while one was open for 0% of the time, Pallas kernels for 12%

profile of v16, /device:TPU:10, one launch (start us, length us, event | category | flops | bytes accessed | tf_op | source)
XLA Modules:
  0.0 162.4 jit_solution(15280690616413663032)
XLA Ops:
  0.6 0.8 copy.10.offsets
  1.4 3.1 %copy.14 = bf16[1,2,9728,128]{3,2,1,0:T(8,128)(2,1)S(1)} copy(bf16[1,2,9728,128]{3,1,2,0:T(2,128)(2,1)} %bitcast.20) | data formatting | bytes 9961472
  4.6 3.9 %pack.1 = (bf16[8,16,16,128]{3,2,1,0:T(8,128)(2,1)S(1)}, bf16[8,34,16,128]{3,2,1,0:T(8,128)(2,1)S(1)}, bf16[8,51,16,128]{3,2,1,0:T(8,128)(2,1)}, bf16[8,51,16,128]{3,2,1,0:T(8,128)(2,1)}) custom-call(s32[2,32,4]{2,1,0:T(8,128)S(1)} %copy.10.offsets, s32[2,32]{1,0:T(2,128)S(1)} %copy-done.18, bf16[2,608,16,128]{3,2,1,0:T(8,128)(2,1)S(1)} %bitcast.10), custom_call_target="tpu_custom_call" | custom-call | bytes 9961472 | tf_op jit(solution)/shard_map/pack/pallas_call | solution.py:77
  8.4 1.0 copy-done.7
  9.4 4.4 %all-to-all-start.2 = ((bf16[8,34,16,128]{3,2,1,0:T(8,128)(2,1)}), bf16[8,34,16,128]{3,2,1,0:T(8,128)(2,1)S(1)}, u32[]{:S(2)}, u32[]{:S(2)}) async-start(bf16[8,34,16,128]{3,2,1,0:T(8,128)(2,1)} %copy-done.7), calls=%async_computation.2 | async-start | bytes 2228224 | tf_op jit(solution)/shard_map/all_to_all | solution.py:341
  13.8 2.3 %collective-permute-start.1 = (bf16[8,8,2,16,128]{4,3,2,1,0:T(8,128)(2,1)S(1)}, bf16[8,8,2,16,128]{4,3,2,1,0:T(8,128)(2,1)S(1)}, u32[]{:S(2)}, u32[]{:S(2)}) collective-permute-start(bf16[8,8,2,16,128]{4,3,2,1,0:T(8,128)(2,1)S(1)} %bitcast.11), channel_id=1, source_target_pairs={{1,0},{2,1},{3,2},{5,4},{6,5},{7,6},{9,8},{10,9},{11,10},{13,12},{... | collective-permute-start | bytes 1572872 | tf_op jit(solution)/shard_map/ppermute | solution.py:157
  16.2 3.5 %collective-permute-start = (bf16[8,8,2,16,128]{4,3,2,1,0:T(8,128)(2,1)S(1)}, bf16[8,8,2,16,128]{4,3,2,1,0:T(8,128)(2,1)S(1)}, u32[]{:S(2)}, u32[]{:S(2)}) collective-permute-start(bf16[8,8,2,16,128]{4,3,2,1,0:T(8,128)(2,1)S(1)} %bitcast.12), channel_id=1, source_target_pairs={{0,1},{1,2},{2,3},{4,5},{5,6},{6,7},{8,9},{9,10},{10,11},{12,13},{... | collective-permute-start | bytes 1572872 | tf_op jit(solution)/shard_map/ppermute | solution.py:156
  19.7 0.1 copy.13.mapped
  19.8 9.9 %collective-permute-done.1.down_ref = bf16[8,8,2,16,128]{4,3,2,1,0:T(8,128)(2,1)S(1)} collective-permute-done((bf16[8,8,2,16,128]{4,3,2,1,0:T(8,128)(2,1)S(1)}, bf16[8,8,2,16,128]{4,3,2,1,0:T(8,128)(2,1)S(1)}, u32[]{:S(2)}, u32[]{:S(2)}) %collective-permute-start.1) | collective-permute-done | bytes 524320 | tf_op jit(solution)/shard_map/ppermute | solution.py:157
  29.7 2.1 %collective-permute-done.up_ref = bf16[8,8,2,16,128]{4,3,2,1,0:T(8,128)(2,1)S(1)} collective-permute-done((bf16[8,8,2,16,128]{4,3,2,1,0:T(8,128)(2,1)S(1)}, bf16[8,8,2,16,128]{4,3,2,1,0:T(8,128)(2,1)S(1)}, u32[]{:S(2)}, u32[]{:S(2)}) %collective-permute-start) | collective-permute-done | bytes 524320 | tf_op jit(solution)/shard_map/ppermute | solution.py:156
  31.8 0.8 pass_on.1.refs_0_
  32.6 0.0 collective-permute-start.2
  32.6 0.0 all-to-all-done.2
  32.6 1.0 copy-done.5
  33.6 4.2 %all-to-all-start.1 = ((bf16[8,51,16,128]{3,2,1,0:T(8,128)(2,1)}), bf16[8,51,16,128]{3,2,1,0:T(8,128)(2,1)S(1)}, u32[]{:S(2)}, u32[]{:S(2)}) async-start(bf16[8,51,16,128]{3,2,1,0:T(8,128)(2,1)} %get-tuple-element.25), calls=%async_computation.1 | async-start | bytes 3342336 | tf_op jit(solution)/shard_map/all_to_all | solution.py:341
  37.8 1.2 copy-done.6
  39.1 1.7 %cut.3 = (bf16[2,2,272,128]{3,2,1,0:T(8,128)(2,1)S(1)}, bf16[2,2,272,128]{3,2,1,0:T(8,128)(2,1)}, bf16[2,2,272,128]{3,2,1,0:T(8,128)(2,1)}, bf16[2,2,272,128]{3,2,1,0:T(8,128)(2,1)}) custom-call(s32[8,4]{1,0:T(8,128)S(1)} %copy.13.mapped, bf16[8,544,128]{2,1,0:T(8,128)(2,1)S(1)} %bitcast.17, bf16[8,8,2,16,128]{4,3,2,1,0:T(8,128)(2,1)} %pass_on.1.refs_0_), custom_call_target="tpu_custom_call" | custom-call | flops 34500001792 | bytes 2228224 | tf_op jit(solution)/shard_map/cut/pallas_call | solution.py:121
  40.7 3.2 %collective-permute-start.3 = (bf16[2,2,272,128]{3,2,1,0:T(8,128)(2,1)}, bf16[2,2,272,128]{3,2,1,0:T(8,128)(2,1)}, u32[]{:S(2)}, u32[]{:S(2)}) collective-permute-start(bf16[2,2,272,128]{3,2,1,0:T(8,128)(2,1)} %get-tuple-element.30), channel_id=1, source_target_pairs={{0,1},{1,2},{2,3},{3,0},{4,5},{5,6},{6,7},{7,4},{8,9},{9,10},{10,1... | collective-permute-start | bytes 835592 | tf_op jit(solution)/shard_map/ppermute | solution.py:375
  43.9 2.2 %collective-permute-start.4 = (bf16[2,2,272,128]{3,2,1,0:T(8,128)(2,1)}, bf16[2,2,272,128]{3,2,1,0:T(8,128)(2,1)}, u32[]{:S(2)}, u32[]{:S(2)}) collective-permute-start(bf16[2,2,272,128]{3,2,1,0:T(8,128)(2,1)} %get-tuple-element.31), channel_id=1, source_target_pairs={{0,2},{1,3},{2,0},{3,1},{4,6},{5,7},{6,4},{7,5},{8,10},{9,11},{10,... | collective-permute-start | bytes 835592 | tf_op jit(solution)/shard_map/ppermute | solution.py:375
  46.1 0.0 collective-permute-start.5
  46.1 0.6 collective-permute-done.2.refs_1_.second_ref
  46.7 4.3 %collective-permute-start.6 = (bf16[8,8,2,16,128]{4,3,2,1,0:T(8,128)(2,1)}, bf16[8,8,2,16,128]{4,3,2,1,0:T(8,128)(2,1)}, u32[]{:S(2)}, u32[]{:S(2)}) collective-permute-start(bf16[8,8,2,16,128]{4,3,2,1,0:T(8,128)(2,1)} %collective-permute-done.2.refs_1_.second_ref), channel_id=1, source_target_pairs={{1,0},{2,3},{5,4},{6,7},{9,8},{10,11},{13,12},{14,15},{17,16},{18,... | collective-permute-start | bytes 1572872 | tf_op jit(solution)/shard_map/ppermute | solution.py:358
  51.0 7.4 %all-to-all-done.1 = bf16[8,51,16,128]{3,2,1,0:T(8,128)(2,1)S(1)} async-done(((bf16[8,51,16,128]{3,2,1,0:T(8,128)(2,1)}), bf16[8,51,16,128]{3,2,1,0:T(8,128)(2,1)S(1)}, u32[]{:S(2)}, u32[]{:S(2)}) %all-to-all-start.1) | async-done | bytes 1671200 | tf_op jit(solution)/shard_map/all_to_all | solution.py:341
  58.4 1.2 copy-done.1
  59.6 5.0 %all-to-all-start = ((bf16[8,51,16,128]{3,2,1,0:T(8,128)(2,1)}), bf16[8,51,16,128]{3,2,1,0:T(8,128)(2,1)S(1)}, u32[]{:S(2)}, u32[]{:S(2)}) async-start(bf16[8,51,16,128]{3,2,1,0:T(8,128)(2,1)} %get-tuple-element.24), calls=%async_computation | async-start | bytes 3342336 | tf_op jit(solution)/shard_map/all_to_all | solution.py:341
  64.6 1.4 copy-done.2
  66.0 1.8 %cut.4 = (bf16[2,3,272,128]{3,2,1,0:T(8,128)(2,1)S(1)}, bf16[2,3,272,128]{3,2,1,0:T(8,128)(2,1)}, bf16[2,3,272,128]{3,2,1,0:T(8,128)(2,1)}, bf16[2,3,272,128]{3,2,1,0:T(8,128)(2,1)}) custom-call(s32[8,4]{1,0:T(8,128)S(1)} %copy.13.mapped, bf16[8,816,128]{2,1,0:T(8,128)(2,1)S(1)} %bitcast.16, bf16[2,2,272,128]{3,2,1,0:T(8,128)(2,1)S(1)} %get-tuple-element.28.refs_0_, ...), custom_call_target="tpu_custom_call" | custom-call | flops 34500001792 | bytes 3342336 | tf_op jit(solution)/shard_map/cut/pallas_call | solution.py:121
  67.9 0.8 copy-done.8
  68.6 0.7 copy-done.15
  69.3 3.2 %collective-permute-start.10 = (bf16[2,3,272,128]{3,2,1,0:T(8,128)(2,1)}, bf16[2,3,272,128]{3,2,1,0:T(8,128)(2,1)}, u32[]{:S(2)}, u32[]{:S(2)}) collective-permute-start(bf16[2,3,272,128]{3,2,1,0:T(8,128)(2,1)} %get-tuple-element.37), channel_id=1, source_target_pairs={{0,1},{1,2},{2,3},{3,0},{4,5},{5,6},{6,7},{7,4},{8,9},{9,10},{10,1... | collective-permute-start | bytes 1253384 | tf_op jit(solution)/shard_map/ppermute | solution.py:375
  72.5 0.0 collective-permute-done.3.refs_1_
  72.5 2.2 %collective-permute-start.11 = (bf16[2,3,272,128]{3,2,1,0:T(8,128)(2,1)}, bf16[2,3,272,128]{3,2,1,0:T(8,128)(2,1)}, u32[]{:S(2)}, u32[]{:S(2)}) collective-permute-start(bf16[2,3,272,128]{3,2,1,0:T(8,128)(2,1)} %get-tuple-element.38), channel_id=1, source_target_pairs={{0,2},{1,3},{2,0},{3,1},{4,6},{5,7},{6,4},{7,5},{8,10},{9,11},{10,... | collective-permute-start | bytes 1253384 | tf_op jit(solution)/shard_map/ppermute | solution.py:375
  74.7 0.0 collective-permute-done.4.refs_2_
  74.7 0.0 collective-permute-start.12
  74.7 0.0 collective-permute-done.5.refs_3_
  74.7 10.4 %all-to-all-done = bf16[8,51,16,128]{3,2,1,0:T(8,128)(2,1)S(1)} async-done(((bf16[8,51,16,128]{3,2,1,0:T(8,128)(2,1)}), bf16[8,51,16,128]{3,2,1,0:T(8,128)(2,1)S(1)}, u32[]{:S(2)}, u32[]{:S(2)}) %all-to-all-start) | async-done | bytes 1671200 | tf_op jit(solution)/shard_map/all_to_all | solution.py:341
  85.2 0.0 collective-permute-done.6.refs_4_.third_ref
  85.2 1.0 copy-done.9
  86.2 1.7 %cut.5 = (bf16[2,3,272,128]{3,2,1,0:T(8,128)(2,1)S(1)}, bf16[2,3,272,128]{3,2,1,0:T(8,128)(2,1)}, bf16[2,3,272,128]{3,2,1,0:T(8,128)(2,1)}, bf16[2,3,272,128]{3,2,1,0:T(8,128)(2,1)S(1)}) custom-call(s32[8,4]{1,0:T(8,128)S(1)} %copy.13.mapped, bf16[8,816,128]{2,1,0:T(8,128)(2,1)S(1)} %bitcast.15, bf16[2,3,272,128]{3,2,1,0:T(8,128)(2,1)S(1)} %copy-done.9, ...), custom_call_target="tpu_custom_call" | custom-call | flops 34500001792 | bytes 3342336 | tf_op jit(solution)/shard_map/cut/pallas_call | solution.py:121
  87.9 3.2 %collective-permute-start.7 = (bf16[2,3,272,128]{3,2,1,0:T(8,128)(2,1)}, bf16[2,3,272,128]{3,2,1,0:T(8,128)(2,1)S(1)}, u32[]{:S(2)}, u32[]{:S(2)}) collective-permute-start(bf16[2,3,272,128]{3,2,1,0:T(8,128)(2,1)} %get-tuple-element.34), channel_id=1, source_target_pairs={{0,1},{1,2},{2,3},{3,0},{4,5},{5,6},{6,7},{7,4},{8,9},{9,10},{10,1... | collective-permute-start | bytes 1253384 | tf_op jit(solution)/shard_map/ppermute | solution.py:375
  91.1 2.2 %collective-permute-start.8 = (bf16[2,3,272,128]{3,2,1,0:T(8,128)(2,1)}, bf16[2,3,272,128]{3,2,1,0:T(8,128)(2,1)S(1)}, u32[]{:S(2)}, u32[]{:S(2)}) collective-permute-start(bf16[2,3,272,128]{3,2,1,0:T(8,128)(2,1)} %get-tuple-element.35), channel_id=1, source_target_pairs={{0,2},{1,3},{2,0},{3,1},{4,6},{5,7},{6,4},{7,5},{8,10},{9,11},{10,... | collective-permute-start | bytes 1253384 | tf_op jit(solution)/shard_map/ppermute | solution.py:375
  93.3 1.3 join.1
  94.6 0.0 copy-start
  94.6 1.3 copy-done
  95.9 0.8 copy-done.3
  96.7 5.0 %all-to-all-start.3 = ((bf16[8,4,8,2,16,128]{5,4,3,2,1,0:T(8,128)(2,1)}), bf16[8,4,8,2,16,128]{5,4,3,2,1,0:T(8,128)(2,1)S(1)}, u32[]{:S(2)}, u32[]{:S(2)}) async-start(bf16[8,4,8,2,16,128]{5,4,3,2,1,0:T(8,128)(2,1)} %copy-done), calls=%async_computation.3 | async-start | bytes 4194304 | tf_op jit(solution)/shard_map/all_to_all | solution.py:341
  101.7 0.0 collective-permute-done.10.refs_0_.refs_1_
  101.7 0.0 collective-permute-start.9
  101.7 25.9 %collective-permute-done.11.refs_1_.refs_2_ = bf16[2,3,272,128]{3,2,1,0:T(8,128)(2,1)} collective-permute-done((bf16[2,3,272,128]{3,2,1,0:T(8,128)(2,1)}, bf16[2,3,272,128]{3,2,1,0:T(8,128)(2,1)}, u32[]{:S(2)}, u32[]{:S(2)}) %collective-permute-start.11) | collective-permute-done | bytes 417824 | tf_op jit(solution)/shard_map/ppermute | solution.py:375
  127.6 1.8 %collective-permute-done.12.refs_2_.refs_3_ = bf16[2,3,272,128]{3,2,1,0:T(8,128)(2,1)} collective-permute-done((bf16[2,3,272,128]{3,2,1,0:T(8,128)(2,1)}, bf16[2,3,272,128]{3,2,1,0:T(8,128)(2,1)}, u32[]{:S(2)}, u32[]{:S(2)}) %collective-permute-start.12) | collective-permute-done | bytes 417824 | tf_op jit(solution)/shard_map/ppermute | solution.py:375
  129.5 7.1 %collective-permute-done.7.refs_3_.refs_1_ = bf16[2,3,272,128]{3,2,1,0:T(8,128)(2,1)S(1)} collective-permute-done((bf16[2,3,272,128]{3,2,1,0:T(8,128)(2,1)}, bf16[2,3,272,128]{3,2,1,0:T(8,128)(2,1)S(1)}, u32[]{:S(2)}, u32[]{:S(2)}) %collective-permute-start.7) | collective-permute-done | bytes 417824 | tf_op jit(solution)/shard_map/ppermute | solution.py:375
  136.6 8.2 %collective-permute-done.8.refs_4_.refs_2_ = bf16[2,3,272,128]{3,2,1,0:T(8,128)(2,1)S(1)} collective-permute-done((bf16[2,3,272,128]{3,2,1,0:T(8,128)(2,1)}, bf16[2,3,272,128]{3,2,1,0:T(8,128)(2,1)S(1)}, u32[]{:S(2)}, u32[]{:S(2)}) %collective-permute-start.8) | collective-permute-done | bytes 417824 | tf_op jit(solution)/shard_map/ppermute | solution.py:375
  144.8 0.8 copy-done.13
  145.5 1.3 token_.1.refs_0_
  146.8 0.0 all-to-all-done.3.pieces
  146.8 0.7 copy-done.17
  147.5 1.0 assemble.1.refs_4_
  148.6 0.0 copy-done.16
  148.6 0.0 copy-start.10
  148.6 4.0 %absorb.3 = (bf16[8,2,4,48,512]{4,3,2,1,0:T(8,128)(2,1)}, bf16[8,2,4,224,512]{4,3,2,1,0:T(8,128)(2,1)}) custom-call(s32[1]{0:T(128)} %bitcast.me_ref.at, bf16[2,2,272,128]{3,2,1,0:T(8,128)(2,1)S(1)} %copy-done.16, bf16[2,2,272,128]{3,2,1,0:T(8,128)(2,1)} %collective-permute-done.3.refs_1_, bf16[2,2,272,128]{3,2,1,0:T(8,128)(2,1)} %collective-permute-done.4.refs_2_, ...), custom_call_target="tpu_custom_call" | custom-call | flops 570425344 | bytes 5570560 | tf_op jit(solution)/shard_map/absorb/pallas_call | solution.py:286
  152.6 0.0 copy-start.12
  152.6 5.6 %absorb.4 = (bf16[8,2,4,48,512]{4,3,2,1,0:T(8,128)(2,1)}, bf16[8,2,4,224,512]{4,3,2,1,0:T(8,128)(2,1)}) custom-call(s32[1]{0:T(128)} %bitcast.me_ref.at, bf16[2,3,272,128]{3,2,1,0:T(8,128)(2,1)S(1)} %copy-done.10, bf16[2,3,272,128]{3,2,1,0:T(8,128)(2,1)} %collective-permute-done.10.refs_0_.refs_1_, ...), custom_call_target="tpu_custom_call", output_to_operand_aliasing={{0}: (6, {}), {1}: (7, {})} | custom-call | flops 855638016 | bytes 8355840 | tf_op jit(solution)/shard_map/absorb/pallas_call | solution.py:286
  158.2 0.0 collective-permute-done.9.refs_3_
  158.2 4.2 %absorb.5 = (bf16[8,2,4,48,512]{4,3,2,1,0:T(8,128)(2,1)}, bf16[8,2,4,224,512]{4,3,2,1,0:T(8,128)(2,1)}) custom-call(s32[1]{0:T(128)} %bitcast.me_ref.at, bf16[2,3,272,128]{3,2,1,0:T(8,128)(2,1)S(1)} %copy-done.4, bf16[2,3,272,128]{3,2,1,0:T(8,128)(2,1)S(1)} %copy-done.12, ...), custom_call_target="tpu_custom_call", output_to_operand_aliasing={{0}: (6, {}), {1}: (7, {})} | custom-call | flops 855638016 | bytes 8355840 | tf_op jit(solution)/shard_map/absorb/pallas_call | solution.py:286
  (26 shorter events, 0.0 us)
Async XLA Ops:
  1.4 3.1 %copy-start.18 = (s32[2,32]{1,0:T(2,128)S(1)}, s32[2,32]{1,0:T(2,128)}, u32[]{:S(2)}) copy-start(s32[2,32]{1,0:T(2,128)} %owners.1) | copy-start | bytes 772
  8.4 1.0 copy-start.7
  9.4 10.2 %copy-start.20 = (s32[8,4]{0,1:T(4,128)S(1)}, s32[8,4]{0,1:T(4,128)}, u32[]{:S(2)}) copy-start(s32[8,4]{0,1:T(4,128)} %param.7) | copy-start | bytes 388
  9.4 23.2 %all-to-all-start.2 = ((bf16[8,34,16,128]{3,2,1,0:T(8,128)(2,1)}), bf16[8,34,16,128]{3,2,1,0:T(8,128)(2,1)S(1)}, u32[]{:S(2)}, u32[]{:S(2)}) async-start(bf16[8,34,16,128]{3,2,1,0:T(8,128)(2,1)} %copy-done.7), calls=%async_computation.2 | async-start | bytes 2228224 | tf_op jit(solution)/shard_map/all_to_all | solution.py:341
  13.8 15.9 %collective-permute-start.1 = (bf16[8,8,2,16,128]{4,3,2,1,0:T(8,128)(2,1)S(1)}, bf16[8,8,2,16,128]{4,3,2,1,0:T(8,128)(2,1)S(1)}, u32[]{:S(2)}, u32[]{:S(2)}) collective-permute-start(bf16[8,8,2,16,128]{4,3,2,1,0:T(8,128)(2,1)S(1)} %bitcast.11), channel_id=1, source_target_pairs={{1,0},{2,1},{3,2},{5,4},{6,5},{7,6},{9,8},{10,9},{11,10},{13,12},{... | collective-permute-start | bytes 1572872 | tf_op jit(solution)/shard_map/ppermute | solution.py:157
  16.2 15.6 %collective-permute-start = (bf16[8,8,2,16,128]{4,3,2,1,0:T(8,128)(2,1)S(1)}, bf16[8,8,2,16,128]{4,3,2,1,0:T(8,128)(2,1)S(1)}, u32[]{:S(2)}, u32[]{:S(2)}) collective-permute-start(bf16[8,8,2,16,128]{4,3,2,1,0:T(8,128)(2,1)S(1)} %bitcast.12), channel_id=1, source_target_pairs={{0,1},{1,2},{2,3},{4,5},{5,6},{6,7},{8,9},{9,10},{10,11},{12,13},{... | collective-permute-start | bytes 1572872 | tf_op jit(solution)/shard_map/ppermute | solution.py:156
  32.6 14.1 %collective-permute-start.2 = (bf16[8,8,2,16,128]{4,3,2,1,0:T(8,128)(2,1)}, bf16[8,8,2,16,128]{4,3,2,1,0:T(8,128)(2,1)}, u32[]{:S(2)}, u32[]{:S(2)}) collective-permute-start(bf16[8,8,2,16,128]{4,3,2,1,0:T(8,128)(2,1)} %pass_on.1.refs_0_), channel_id=1, source_target_pairs={{0,2},{1,0},{2,3},{3,1},{4,6},{5,4},{6,7},{7,5},{8,10},{9,8},{10,1... | collective-permute-start | bytes 1572872 | tf_op jit(solution)/shard_map/ppermute | solution.py:357
  32.6 1.0 copy-start.5
  33.6 24.8 %all-to-all-start.1 = ((bf16[8,51,16,128]{3,2,1,0:T(8,128)(2,1)}), bf16[8,51,16,128]{3,2,1,0:T(8,128)(2,1)S(1)}, u32[]{:S(2)}, u32[]{:S(2)}) async-start(bf16[8,51,16,128]{3,2,1,0:T(8,128)(2,1)} %get-tuple-element.25), calls=%async_computation.1 | async-start | bytes 3342336 | tf_op jit(solution)/shard_map/all_to_all | solution.py:341
  37.8 1.2 copy-start.6
  40.7 31.8 %collective-permute-start.3 = (bf16[2,2,272,128]{3,2,1,0:T(8,128)(2,1)}, bf16[2,2,272,128]{3,2,1,0:T(8,128)(2,1)}, u32[]{:S(2)}, u32[]{:S(2)}) collective-permute-start(bf16[2,2,272,128]{3,2,1,0:T(8,128)(2,1)} %get-tuple-element.30), channel_id=1, source_target_pairs={{0,1},{1,2},{2,3},{3,0},{4,5},{5,6},{6,7},{7,4},{8,9},{9,10},{10,1... | collective-permute-start | bytes 835592 | tf_op jit(solution)/shard_map/ppermute | solution.py:375
  43.9 30.8 %collective-permute-start.4 = (bf16[2,2,272,128]{3,2,1,0:T(8,128)(2,1)}, bf16[2,2,272,128]{3,2,1,0:T(8,128)(2,1)}, u32[]{:S(2)}, u32[]{:S(2)}) collective-permute-start(bf16[2,2,272,128]{3,2,1,0:T(8,128)(2,1)} %get-tuple-element.31), channel_id=1, source_target_pairs={{0,2},{1,3},{2,0},{3,1},{4,6},{5,7},{6,4},{7,5},{8,10},{9,11},{10,... | collective-permute-start | bytes 835592 | tf_op jit(solution)/shard_map/ppermute | solution.py:375
  46.1 28.6 %collective-permute-start.5 = (bf16[2,2,272,128]{3,2,1,0:T(8,128)(2,1)}, bf16[2,2,272,128]{3,2,1,0:T(8,128)(2,1)}, u32[]{:S(2)}, u32[]{:S(2)}) collective-permute-start(bf16[2,2,272,128]{3,2,1,0:T(8,128)(2,1)} %get-tuple-element.32), channel_id=1, source_target_pairs={{0,3},{1,0},{2,1},{3,2},{4,7},{5,4},{6,5},{7,6},{8,11},{9,8},{10,9... | collective-permute-start | bytes 835592 | tf_op jit(solution)/shard_map/ppermute | solution.py:375
  46.7 38.5 %collective-permute-start.6 = (bf16[8,8,2,16,128]{4,3,2,1,0:T(8,128)(2,1)}, bf16[8,8,2,16,128]{4,3,2,1,0:T(8,128)(2,1)}, u32[]{:S(2)}, u32[]{:S(2)}) collective-permute-start(bf16[8,8,2,16,128]{4,3,2,1,0:T(8,128)(2,1)} %collective-permute-done.2.refs_1_.second_ref), channel_id=1, source_target_pairs={{1,0},{2,3},{5,4},{6,7},{9,8},{10,11},{13,12},{14,15},{17,16},{18,... | collective-permute-start | bytes 1572872 | tf_op jit(solution)/shard_map/ppermute | solution.py:358
  58.4 1.2 copy-start.1
  59.6 25.6 %all-to-all-start = ((bf16[8,51,16,128]{3,2,1,0:T(8,128)(2,1)}), bf16[8,51,16,128]{3,2,1,0:T(8,128)(2,1)S(1)}, u32[]{:S(2)}, u32[]{:S(2)}) async-start(bf16[8,51,16,128]{3,2,1,0:T(8,128)(2,1)} %get-tuple-element.24), calls=%async_computation | async-start | bytes 3342336 | tf_op jit(solution)/shard_map/all_to_all | solution.py:341
  64.6 1.4 copy-start.2
  67.9 0.8 copy-start.8
  68.6 0.7 copy-start.15
  69.3 32.4 %collective-permute-start.10 = (bf16[2,3,272,128]{3,2,1,0:T(8,128)(2,1)}, bf16[2,3,272,128]{3,2,1,0:T(8,128)(2,1)}, u32[]{:S(2)}, u32[]{:S(2)}) collective-permute-start(bf16[2,3,272,128]{3,2,1,0:T(8,128)(2,1)} %get-tuple-element.37), channel_id=1, source_target_pairs={{0,1},{1,2},{2,3},{3,0},{4,5},{5,6},{6,7},{7,4},{8,9},{9,10},{10,1... | collective-permute-start | bytes 1253384 | tf_op jit(solution)/shard_map/ppermute | solution.py:375
  72.5 55.1 %collective-permute-start.11 = (bf16[2,3,272,128]{3,2,1,0:T(8,128)(2,1)}, bf16[2,3,272,128]{3,2,1,0:T(8,128)(2,1)}, u32[]{:S(2)}, u32[]{:S(2)}) collective-permute-start(bf16[2,3,272,128]{3,2,1,0:T(8,128)(2,1)} %get-tuple-element.38), channel_id=1, source_target_pairs={{0,2},{1,3},{2,0},{3,1},{4,6},{5,7},{6,4},{7,5},{8,10},{9,11},{10,... | collective-permute-start | bytes 1253384 | tf_op jit(solution)/shard_map/ppermute | solution.py:375
  74.7 54.7 %collective-permute-start.12 = (bf16[2,3,272,128]{3,2,1,0:T(8,128)(2,1)}, bf16[2,3,272,128]{3,2,1,0:T(8,128)(2,1)}, u32[]{:S(2)}, u32[]{:S(2)}) collective-permute-start(bf16[2,3,272,128]{3,2,1,0:T(8,128)(2,1)} %get-tuple-element.39), channel_id=1, source_target_pairs={{0,3},{1,0},{2,1},{3,2},{4,7},{5,4},{6,5},{7,6},{8,11},{9,8},{10,9... | collective-permute-start | bytes 1253384 | tf_op jit(solution)/shard_map/ppermute | solution.py:375
  85.2 1.0 copy-start.9
  87.9 5.4 %copy-start.19 = (bf16[2,3,272,128]{3,2,1,0:T(8,128)(2,1)}, bf16[2,3,272,128]{3,2,1,0:T(8,128)(2,1)S(1)}, u32[]{:S(2)}) copy-start(bf16[2,3,272,128]{3,2,1,0:T(8,128)(2,1)S(1)} %get-tuple-element.36) | copy-start | bytes 1253380
  87.9 48.7 %collective-permute-start.7 = (bf16[2,3,272,128]{3,2,1,0:T(8,128)(2,1)}, bf16[2,3,272,128]{3,2,1,0:T(8,128)(2,1)S(1)}, u32[]{:S(2)}, u32[]{:S(2)}) collective-permute-start(bf16[2,3,272,128]{3,2,1,0:T(8,128)(2,1)} %get-tuple-element.34), channel_id=1, source_target_pairs={{0,1},{1,2},{2,3},{3,0},{4,5},{5,6},{6,7},{7,4},{8,9},{9,10},{10,1... | collective-permute-start | bytes 1253384 | tf_op jit(solution)/shard_map/ppermute | solution.py:375
  91.1 53.7 %collective-permute-start.8 = (bf16[2,3,272,128]{3,2,1,0:T(8,128)(2,1)}, bf16[2,3,272,128]{3,2,1,0:T(8,128)(2,1)S(1)}, u32[]{:S(2)}, u32[]{:S(2)}) collective-permute-start(bf16[2,3,272,128]{3,2,1,0:T(8,128)(2,1)} %get-tuple-element.35), channel_id=1, source_target_pairs={{0,2},{1,3},{2,0},{3,1},{4,6},{5,7},{6,4},{7,5},{8,10},{9,11},{10,... | collective-permute-start | bytes 1253384 | tf_op jit(solution)/shard_map/ppermute | solution.py:375
  94.6 1.3 copy-start
  95.9 0.8 copy-start.3
  96.7 50.1 %all-to-all-start.3 = ((bf16[8,4,8,2,16,128]{5,4,3,2,1,0:T(8,128)(2,1)}), bf16[8,4,8,2,16,128]{5,4,3,2,1,0:T(8,128)(2,1)S(1)}, u32[]{:S(2)}, u32[]{:S(2)}) async-start(bf16[8,4,8,2,16,128]{5,4,3,2,1,0:T(8,128)(2,1)} %copy-done), calls=%async_computation.3 | async-start | bytes 4194304 | tf_op jit(solution)/shard_map/all_to_all | solution.py:341
  101.7 56.5 %collective-permute-start.9 = (bf16[2,3,272,128]{3,2,1,0:T(8,128)(2,1)}, bf16[2,3,272,128]{3,2,1,0:T(8,128)(2,1)S(1)}, u32[]{:S(2)}, u32[]{:S(2)}) collective-permute-start(bf16[2,3,272,128]{3,2,1,0:T(8,128)(2,1)} %copy-done.19), channel_id=1, source_target_pairs={{0,3},{1,0},{2,1},{3,2},{4,7},{5,4},{6,5},{7,6},{8,11},{9,8},{10,9... | collective-permute-start | bytes 1253384 | tf_op jit(solution)/shard_map/ppermute | solution.py:375
  136.6 8.2 %copy-start.11 = (bf16[2,3,272,128]{3,2,1,0:T(8,128)(2,1)}, bf16[2,3,272,128]{3,2,1,0:T(8,128)(2,1)S(1)}, u32[]{:S(2)}) copy-start(bf16[2,3,272,128]{3,2,1,0:T(8,128)(2,1)S(1)} %collective-permute-done.7.refs_3_.refs_1_) | copy-start | bytes 1253380
  144.8 0.8 copy-start.13
  146.8 1.8 %copy-start.16 = (bf16[2,2,272,128]{3,2,1,0:T(8,128)(2,1)S(1)}, bf16[2,2,272,128]{3,2,1,0:T(8,128)(2,1)}, u32[]{:S(2)}) copy-start(bf16[2,2,272,128]{3,2,1,0:T(8,128)(2,1)} %copy-done.15) | copy-start | bytes 835588
  146.8 0.7 copy-start.17
  148.6 4.0 %copy-start.10 = (bf16[2,3,272,128]{3,2,1,0:T(8,128)(2,1)S(1)}, bf16[2,3,272,128]{3,2,1,0:T(8,128)(2,1)}, u32[]{:S(2)}) copy-start(bf16[2,3,272,128]{3,2,1,0:T(8,128)(2,1)} %copy-done.8) | copy-start | bytes 1253380
  152.6 5.6 %copy-start.4 = (bf16[2,3,272,128]{3,2,1,0:T(8,128)(2,1)S(1)}, bf16[2,3,272,128]{3,2,1,0:T(8,128)(2,1)}, u32[]{:S(2)}) copy-start(bf16[2,3,272,128]{3,2,1,0:T(8,128)(2,1)} %copy-done.3) | copy-start | bytes 1253380
  152.6 5.6 %copy-start.12 = (bf16[2,3,272,128]{3,2,1,0:T(8,128)(2,1)S(1)}, bf16[2,3,272,128]{3,2,1,0:T(8,128)(2,1)}, u32[]{:S(2)}) copy-start(bf16[2,3,272,128]{3,2,1,0:T(8,128)(2,1)} %copy-done.11) | copy-start | bytes 1253380
  152.6 5.6 %copy-start.14 = (bf16[2,3,272,128]{3,2,1,0:T(8,128)(2,1)S(1)}, bf16[2,3,272,128]{3,2,1,0:T(8,128)(2,1)}, u32[]{:S(2)}) copy-start(bf16[2,3,272,128]{3,2,1,0:T(8,128)(2,1)} %copy-done.13) | copy-start | bytes 1253380

commit v17 on v16

--- a/solution.py
+++ b/solution.py
@@ -364,7 +364,7 @@
         if at >= 2:
             waits = waits + exchanged[at - 2][1:]
         if t_ways == 4:
-            waits = waits + [[passed], [second], [third]][min(at, 2)]
+            waits = waits + [[passed], [second], []][min(at, 2)]
         pieces = list(
             cut(rows, slice_map, blocks, 0, len(items), item_rows, waits, CUT_MICROS)
         )
@@ -395,7 +395,7 @@
             jax.ShapeDtypeStruct((item_count, blocks, t_ways, row_counts[kind], KVR), jnp.bfloat16)
             for kind in (QUERY, OUT)
         )
-        matrices = assemble(me, joined, [token(exchanged[-2][1:] + exchanged[-1][1:3], TOKEN_MICROS)])
+        matrices = assemble(me, joined, [token(exchanged[-2][1:], TOKEN_MICROS)])
         outs = None
         for items, parts in zip(chunks, exchanged):
             outs = absorb(me, items, parts, matrices, outs, shapes)

time: 164 us -> 150 us (0.915)
  waiting for transfers between devices: 73.4 us -> 62.8 us
  local copies, waits for them, and re-layouts: 15.9 us -> 11.1 us
    ppermute x9, waiting for transfers between devices: 43 us -> 30.3 us  [per_device(): lax.ppermute(piece, 'tp', [(i, (i + shift) % t_ways) for i in range(t_way...]
    unnamed x45 -> x37, local copies, waits for them, and re-layouts: 15.9 us -> 11.1 us
    all_to_all x4, waiting for transfers between devices: 17.8 us -> 20 us  [over_fsdp(): x = lax.all_to_all(x, 'fsdp', split_axis=0, concat_axis=0, tiled=True)]
  transfers between devices with their start and end apart: 17 -> 17, of which waited for: 9 -> 9; matrix products, arithmetic and copies ran while one was open for 0% -> 0% of each run, Pallas kernels for 12% -> 13%
where the time goes in v17:
time: 150 us; the launch traced here: 149 us
  waiting for transfers between devices  62.8 us (42%)
  starting transfers between devices  45.8 us (31%)
  Pallas kernels  28.9 us (19%)
  local copies, waits for them, and re-layouts  11.1 us (7%)
    ppermute x9, waiting for transfers between devices, per_device(): lax.ppermute(piece, 'tp', [(i, (i + shift) % t_ways) for i in range(t_way...  30.3 us
    all_to_all x4, waiting for transfers between devices, over_fsdp(): x = lax.all_to_all(x, 'fsdp', split_axis=0, concat_axis=0, tiled=True)  20 us
    all_to_all x4, starting transfers between devices, over_fsdp(): x = lax.all_to_all(x, 'fsdp', split_axis=0, concat_axis=0, tiled=True)  19.3 us
    ppermute x9, starting transfers between devices, per_device(): lax.ppermute(piece, 'tp', [(i, (i + shift) % t_ways) for i in range(t_way...  16.3 us
    pallas_call x3, Pallas kernels, absorb(): pl.pallas_call(kernel, grid_spec=pltpu.PrefetchScalarGridSpec(num_scalar_...  14.6 us
    unnamed x37, local copies, waits for them, and re-layouts  11.1 us
    ppermute x1, waiting for transfers between devices, neighbours(): lax.ppermute(x, axis, [(i + 1, i) for i in range(ways - 1)])  9.92 us
    pallas_call x3, Pallas kernels, cut(): pl.pallas_call(kernel, grid=(1,), out_shape=[jax.ShapeDtypeStruct(shape,...  6 us
  transfers between devices with their start and end apart: 17, of which 9 were waited for; matrix products, arithmetic and copies ran while one was open for 0% of the time, Pallas kernels for 13%

profile of v17, /device:TPU:10, one launch (start us, length us, event | category | flops | bytes accessed | tf_op | source)
XLA Modules:
  0.0 149.5 jit_solution(10993843478168216766)
XLA Ops:
  0.6 0.8 copy.10.offsets
  1.4 3.1 %copy.14 = bf16[1,2,9728,128]{3,2,1,0:T(8,128)(2,1)S(1)} copy(bf16[1,2,9728,128]{3,1,2,0:T(2,128)(2,1)} %bitcast.19) | data formatting | bytes 9961472
  4.5 0.0 copy-done.14
  4.6 3.9 %pack.1 = (bf16[8,16,16,128]{3,2,1,0:T(8,128)(2,1)S(1)}, bf16[8,34,16,128]{3,2,1,0:T(8,128)(2,1)S(1)}, bf16[8,51,16,128]{3,2,1,0:T(8,128)(2,1)}, bf16[8,51,16,128]{3,2,1,0:T(8,128)(2,1)}) custom-call(s32[2,32,4]{2,1,0:T(8,128)S(1)} %copy.10.offsets, s32[2,32]{1,0:T(2,128)S(1)} %copy-done.14, bf16[2,608,16,128]{3,2,1,0:T(8,128)(2,1)S(1)} %bitcast.10), custom_call_target="tpu_custom_call" | custom-call | bytes 9961472 | tf_op jit(solution)/shard_map/pack/pallas_call | solution.py:77
  8.4 1.0 copy-done.3
  9.5 4.4 %all-to-all-start.2 = ((bf16[8,34,16,128]{3,2,1,0:T(8,128)(2,1)}), bf16[8,34,16,128]{3,2,1,0:T(8,128)(2,1)S(1)}, u32[]{:S(2)}, u32[]{:S(2)}) async-start(bf16[8,34,16,128]{3,2,1,0:T(8,128)(2,1)} %copy-done.3), calls=%async_computation.2 | async-start | bytes 2228224 | tf_op jit(solution)/shard_map/all_to_all | solution.py:341
  13.8 2.3 %collective-permute-start.1 = (bf16[8,8,2,16,128]{4,3,2,1,0:T(8,128)(2,1)S(1)}, bf16[8,8,2,16,128]{4,3,2,1,0:T(8,128)(2,1)S(1)}, u32[]{:S(2)}, u32[]{:S(2)}) collective-permute-start(bf16[8,8,2,16,128]{4,3,2,1,0:T(8,128)(2,1)S(1)} %bitcast.11), channel_id=1, source_target_pairs={{1,0},{2,1},{3,2},{5,4},{6,5},{7,6},{9,8},{10,9},{11,10},{13,12},{... | collective-permute-start | bytes 1572872 | tf_op jit(solution)/shard_map/ppermute | solution.py:157
  16.2 3.5 %collective-permute-start = (bf16[8,8,2,16,128]{4,3,2,1,0:T(8,128)(2,1)S(1)}, bf16[8,8,2,16,128]{4,3,2,1,0:T(8,128)(2,1)S(1)}, u32[]{:S(2)}, u32[]{:S(2)}) collective-permute-start(bf16[8,8,2,16,128]{4,3,2,1,0:T(8,128)(2,1)S(1)} %bitcast.12), channel_id=1, source_target_pairs={{0,1},{1,2},{2,3},{4,5},{5,6},{6,7},{8,9},{9,10},{10,11},{12,13},{... | collective-permute-start | bytes 1572872 | tf_op jit(solution)/shard_map/ppermute | solution.py:156
  19.7 0.0 copy-done.16
  19.7 0.1 copy.13.mapped
  19.8 9.9 %collective-permute-done.1.down_ref = bf16[8,8,2,16,128]{4,3,2,1,0:T(8,128)(2,1)S(1)} collective-permute-done((bf16[8,8,2,16,128]{4,3,2,1,0:T(8,128)(2,1)S(1)}, bf16[8,8,2,16,128]{4,3,2,1,0:T(8,128)(2,1)S(1)}, u32[]{:S(2)}, u32[]{:S(2)}) %collective-permute-start.1) | collective-permute-done | bytes 524320 | tf_op jit(solution)/shard_map/ppermute | solution.py:157
  29.7 2.1 %collective-permute-done.up_ref = bf16[8,8,2,16,128]{4,3,2,1,0:T(8,128)(2,1)S(1)} collective-permute-done((bf16[8,8,2,16,128]{4,3,2,1,0:T(8,128)(2,1)S(1)}, bf16[8,8,2,16,128]{4,3,2,1,0:T(8,128)(2,1)S(1)}, u32[]{:S(2)}, u32[]{:S(2)}) %collective-permute-start) | collective-permute-done | bytes 524320 | tf_op jit(solution)/shard_map/ppermute | solution.py:156
  31.8 0.9 pass_on.1.refs_0_
  32.7 0.0 collective-permute-start.2
  32.7 0.0 all-to-all-done.2
  32.7 1.0 copy-done.1
  33.7 4.2 %all-to-all-start.1 = ((bf16[8,51,16,128]{3,2,1,0:T(8,128)(2,1)}), bf16[8,51,16,128]{3,2,1,0:T(8,128)(2,1)S(1)}, u32[]{:S(2)}, u32[]{:S(2)}) async-start(bf16[8,51,16,128]{3,2,1,0:T(8,128)(2,1)} %get-tuple-element.25), calls=%async_computation.1 | async-start | bytes 3342336 | tf_op jit(solution)/shard_map/all_to_all | solution.py:341
  37.9 1.2 copy-done.2
  39.1 1.7 %cut.3 = (bf16[2,2,272,128]{3,2,1,0:T(8,128)(2,1)S(1)}, bf16[2,2,272,128]{3,2,1,0:T(8,128)(2,1)}, bf16[2,2,272,128]{3,2,1,0:T(8,128)(2,1)}, bf16[2,2,272,128]{3,2,1,0:T(8,128)(2,1)}) custom-call(s32[8,4]{1,0:T(8,128)S(1)} %copy.13.mapped, bf16[8,544,128]{2,1,0:T(8,128)(2,1)S(1)} %bitcast.16, bf16[8,8,2,16,128]{4,3,2,1,0:T(8,128)(2,1)} %pass_on.1.refs_0_), custom_call_target="tpu_custom_call" | custom-call | flops 34500001792 | bytes 2228224 | tf_op jit(solution)/shard_map/cut/pallas_call | solution.py:121
  40.8 3.2 %collective-permute-start.3 = (bf16[2,2,272,128]{3,2,1,0:T(8,128)(2,1)}, bf16[2,2,272,128]{3,2,1,0:T(8,128)(2,1)}, u32[]{:S(2)}, u32[]{:S(2)}) collective-permute-start(bf16[2,2,272,128]{3,2,1,0:T(8,128)(2,1)} %get-tuple-element.30), channel_id=1, source_target_pairs={{0,1},{1,2},{2,3},{3,0},{4,5},{5,6},{6,7},{7,4},{8,9},{9,10},{10,1... | collective-permute-start | bytes 835592 | tf_op jit(solution)/shard_map/ppermute | solution.py:375
  44.0 2.2 %collective-permute-start.4 = (bf16[2,2,272,128]{3,2,1,0:T(8,128)(2,1)}, bf16[2,2,272,128]{3,2,1,0:T(8,128)(2,1)}, u32[]{:S(2)}, u32[]{:S(2)}) collective-permute-start(bf16[2,2,272,128]{3,2,1,0:T(8,128)(2,1)} %get-tuple-element.31), channel_id=1, source_target_pairs={{0,2},{1,3},{2,0},{3,1},{4,6},{5,7},{6,4},{7,5},{8,10},{9,11},{10,... | collective-permute-start | bytes 835592 | tf_op jit(solution)/shard_map/ppermute | solution.py:375
  46.2 0.0 collective-permute-start.5
  46.3 0.5 collective-permute-done.2.refs_1_.second_ref
  46.7 4.4 %collective-permute-start.9 = (bf16[8,8,2,16,128]{4,3,2,1,0:T(8,128)(2,1)}, bf16[8,8,2,16,128]{4,3,2,1,0:T(8,128)(2,1)}, u32[]{:S(2)}, u32[]{:S(2)}) collective-permute-start(bf16[8,8,2,16,128]{4,3,2,1,0:T(8,128)(2,1)} %collective-permute-done.2.refs_1_.second_ref), channel_id=1, source_target_pairs={{1,0},{2,3},{5,4},{6,7},{9,8},{10,11},{13,12},{14,15},{17,16},{18,... | collective-permute-start | bytes 1572872 | tf_op jit(solution)/shard_map/ppermute | solution.py:358
  51.1 7.3 %all-to-all-done.1 = bf16[8,51,16,128]{3,2,1,0:T(8,128)(2,1)S(1)} async-done(((bf16[8,51,16,128]{3,2,1,0:T(8,128)(2,1)}), bf16[8,51,16,128]{3,2,1,0:T(8,128)(2,1)S(1)}, u32[]{:S(2)}, u32[]{:S(2)}) %all-to-all-start.1) | async-done | bytes 1671200 | tf_op jit(solution)/shard_map/all_to_all | solution.py:341
  58.5 5.7 %all-to-all-start = ((bf16[8,51,16,128]{3,2,1,0:T(8,128)(2,1)}), bf16[8,51,16,128]{3,2,1,0:T(8,128)(2,1)}, u32[]{:S(2)}, u32[]{:S(2)}) async-start(bf16[8,51,16,128]{3,2,1,0:T(8,128)(2,1)} %get-tuple-element.24), calls=%async_computation | async-start | bytes 3342336 | tf_op jit(solution)/shard_map/all_to_all | solution.py:341
  64.2 1.8 %cut.4 = (bf16[2,3,272,128]{3,2,1,0:T(8,128)(2,1)S(1)}, bf16[2,3,272,128]{3,2,1,0:T(8,128)(2,1)}, bf16[2,3,272,128]{3,2,1,0:T(8,128)(2,1)}, bf16[2,3,272,128]{3,2,1,0:T(8,128)(2,1)}) custom-call(s32[8,4]{1,0:T(8,128)S(1)} %copy.13.mapped, bf16[8,816,128]{2,1,0:T(8,128)(2,1)S(1)} %bitcast.15, bf16[2,2,272,128]{3,2,1,0:T(8,128)(2,1)S(1)} %get-tuple-element.28.refs_0_, ...), custom_call_target="tpu_custom_call" | custom-call | flops 34500001792 | bytes 3342336 | tf_op jit(solution)/shard_map/cut/pallas_call | solution.py:121
  66.0 0.8 copy-done.4
  66.7 3.2 %collective-permute-start.10 = (bf16[2,3,272,128]{3,2,1,0:T(8,128)(2,1)}, bf16[2,3,272,128]{3,2,1,0:T(8,128)(2,1)S(1)}, u32[]{:S(2)}, u32[]{:S(2)}) collective-permute-start(bf16[2,3,272,128]{3,2,1,0:T(8,128)(2,1)} %get-tuple-element.37), channel_id=1, source_target_pairs={{0,1},{1,2},{2,3},{3,0},{4,5},{5,6},{6,7},{7,4},{8,9},{9,10},{10,1... | collective-permute-start | bytes 1253384 | tf_op jit(solution)/shard_map/ppermute | solution.py:375
  69.9 0.0 collective-permute-done.3.refs_1_
  69.9 2.2 %collective-permute-start.11 = (bf16[2,3,272,128]{3,2,1,0:T(8,128)(2,1)}, bf16[2,3,272,128]{3,2,1,0:T(8,128)(2,1)S(1)}, u32[]{:S(2)}, u32[]{:S(2)}) collective-permute-start(bf16[2,3,272,128]{3,2,1,0:T(8,128)(2,1)} %get-tuple-element.38), channel_id=1, source_target_pairs={{0,2},{1,3},{2,0},{3,1},{4,6},{5,7},{6,4},{7,5},{8,10},{9,11},{10,... | collective-permute-start | bytes 1253384 | tf_op jit(solution)/shard_map/ppermute | solution.py:375
  72.1 0.0 collective-permute-done.4.refs_2_
  72.2 0.0 collective-permute-start.12
  72.2 0.0 collective-permute-done.5.refs_3_
  72.2 12.7 %all-to-all-done = bf16[8,51,16,128]{3,2,1,0:T(8,128)(2,1)} async-done(((bf16[8,51,16,128]{3,2,1,0:T(8,128)(2,1)}), bf16[8,51,16,128]{3,2,1,0:T(8,128)(2,1)}, u32[]{:S(2)}, u32[]{:S(2)}) %all-to-all-start) | async-done | bytes 1671200 | tf_op jit(solution)/shard_map/all_to_all | solution.py:341
  84.9 1.0 copy-done.5
  85.9 2.5 %cut.5 = (bf16[2,3,272,128]{3,2,1,0:T(8,128)(2,1)S(1)}, bf16[2,3,272,128]{3,2,1,0:T(8,128)(2,1)}, bf16[2,3,272,128]{3,2,1,0:T(8,128)(2,1)}, bf16[2,3,272,128]{3,2,1,0:T(8,128)(2,1)S(1)}) custom-call(s32[8,4]{1,0:T(8,128)S(1)} %copy.13.mapped, bf16[8,816,128]{2,1,0:T(8,128)(2,1)} %bitcast.1.source, bf16[2,3,272,128]{3,2,1,0:T(8,128)(2,1)S(1)} %copy-done.5, ...), custom_call_target="tpu_custom_call" | custom-call | flops 34500001792 | bytes 3342336 | tf_op jit(solution)/shard_map/cut/pallas_call | solution.py:121
  88.3 3.2 %collective-permute-start.6 = (bf16[2,3,272,128]{3,2,1,0:T(8,128)(2,1)}, bf16[2,3,272,128]{3,2,1,0:T(8,128)(2,1)}, u32[]{:S(2)}, u32[]{:S(2)}) collective-permute-start(bf16[2,3,272,128]{3,2,1,0:T(8,128)(2,1)} %get-tuple-element.34), channel_id=1, source_target_pairs={{0,1},{1,2},{2,3},{3,0},{4,5},{5,6},{6,7},{7,4},{8,9},{9,10},{10,1... | collective-permute-start | bytes 1253384 | tf_op jit(solution)/shard_map/ppermute | solution.py:375
  91.5 0.0 collective-permute-done.9.third_ref
  91.5 2.2 %collective-permute-start.7 = (bf16[2,3,272,128]{3,2,1,0:T(8,128)(2,1)}, bf16[2,3,272,128]{3,2,1,0:T(8,128)(2,1)}, u32[]{:S(2)}, u32[]{:S(2)}) collective-permute-start(bf16[2,3,272,128]{3,2,1,0:T(8,128)(2,1)} %get-tuple-element.35), channel_id=1, source_target_pairs={{0,2},{1,3},{2,0},{3,1},{4,6},{5,7},{6,4},{7,5},{8,10},{9,11},{10,... | collective-permute-start | bytes 1253384 | tf_op jit(solution)/shard_map/ppermute | solution.py:375
  93.7 1.3 join.1
  95.0 0.0 copy-start
  95.1 1.3 copy-done
  96.4 5.0 %all-to-all-start.3 = ((bf16[8,4,8,2,16,128]{5,4,3,2,1,0:T(8,128)(2,1)}), bf16[8,4,8,2,16,128]{5,4,3,2,1,0:T(8,128)(2,1)S(1)}, u32[]{:S(2)}, u32[]{:S(2)}) async-start(bf16[8,4,8,2,16,128]{5,4,3,2,1,0:T(8,128)(2,1)} %copy-done), calls=%async_computation.3 | async-start | bytes 4194304 | tf_op jit(solution)/shard_map/all_to_all | solution.py:341
  101.4 0.0 collective-permute-done.10.refs_0_.refs_1_
  101.4 0.1 collective-permute-start.8
  101.5 23.6 %collective-permute-done.11.refs_1_.refs_2_ = bf16[2,3,272,128]{3,2,1,0:T(8,128)(2,1)S(1)} collective-permute-done((bf16[2,3,272,128]{3,2,1,0:T(8,128)(2,1)}, bf16[2,3,272,128]{3,2,1,0:T(8,128)(2,1)S(1)}, u32[]{:S(2)}, u32[]{:S(2)}) %collective-permute-start.11) | collective-permute-done | bytes 417824 | tf_op jit(solution)/shard_map/ppermute | solution.py:375
  125.1 1.8 %collective-permute-done.12.refs_2_.refs_3_ = bf16[2,3,272,128]{3,2,1,0:T(8,128)(2,1)} collective-permute-done((bf16[2,3,272,128]{3,2,1,0:T(8,128)(2,1)}, bf16[2,3,272,128]{3,2,1,0:T(8,128)(2,1)}, u32[]{:S(2)}, u32[]{:S(2)}) %collective-permute-start.12) | collective-permute-done | bytes 417824 | tf_op jit(solution)/shard_map/ppermute | solution.py:375
  126.9 0.0 copy-done.7
  126.9 1.3 token_.1.refs_0_
  128.2 0.0 all-to-all-done.3.pieces
  128.2 0.7 copy-done.13
  128.9 1.0 assemble.1.refs_4_
  130.0 0.0 copy-done.12
  130.0 0.0 copy-start.6
  130.0 0.0 copy-start.8
  130.0 0.0 copy-start.10
  130.0 4.0 %absorb.3 = (bf16[8,2,4,48,512]{4,3,2,1,0:T(8,128)(2,1)}, bf16[8,2,4,224,512]{4,3,2,1,0:T(8,128)(2,1)}) custom-call(s32[1]{0:T(128)} %bitcast.me_ref.at, bf16[2,2,272,128]{3,2,1,0:T(8,128)(2,1)S(1)} %copy-done.12, bf16[2,2,272,128]{3,2,1,0:T(8,128)(2,1)} %collective-permute-done.3.refs_1_, bf16[2,2,272,128]{3,2,1,0:T(8,128)(2,1)} %collective-permute-done.4.refs_2_, ...), custom_call_target="tpu_custom_call" | custom-call | flops 570425344 | bytes 5570560 | tf_op jit(solution)/shard_map/absorb/pallas_call | solution.py:286
  134.0 0.0 copy-done.6
  134.0 5.1 %absorb.4 = (bf16[8,2,4,48,512]{4,3,2,1,0:T(8,128)(2,1)}, bf16[8,2,4,224,512]{4,3,2,1,0:T(8,128)(2,1)}) custom-call(s32[1]{0:T(128)} %bitcast.me_ref.at, bf16[2,3,272,128]{3,2,1,0:T(8,128)(2,1)S(1)} %copy-done.6, bf16[2,3,272,128]{3,2,1,0:T(8,128)(2,1)S(1)} %copy-done.8, ...), custom_call_target="tpu_custom_call", output_to_operand_aliasing={{0}: (6, {}), {1}: (7, {})} | custom-call | flops 855638016 | bytes 8355840 | tf_op jit(solution)/shard_map/absorb/pallas_call | solution.py:286
  139.1 0.0 collective-permute-done.6.refs_1_
  139.1 3.0 %collective-permute-done.7.refs_2_ = bf16[2,3,272,128]{3,2,1,0:T(8,128)(2,1)} collective-permute-done((bf16[2,3,272,128]{3,2,1,0:T(8,128)(2,1)}, bf16[2,3,272,128]{3,2,1,0:T(8,128)(2,1)}, u32[]{:S(2)}, u32[]{:S(2)}) %collective-permute-start.7) | collective-permute-done | bytes 417824 | tf_op jit(solution)/shard_map/ppermute | solution.py:375
  142.2 1.8 %collective-permute-done.8.refs_3_ = bf16[2,3,272,128]{3,2,1,0:T(8,128)(2,1)} collective-permute-done((bf16[2,3,272,128]{3,2,1,0:T(8,128)(2,1)}, bf16[2,3,272,128]{3,2,1,0:T(8,128)(2,1)}, u32[]{:S(2)}, u32[]{:S(2)}) %collective-permute-start.8) | collective-permute-done | bytes 417824 | tf_op jit(solution)/shard_map/ppermute | solution.py:375
  144.0 5.5 %absorb.5 = (bf16[8,2,4,48,512]{4,3,2,1,0:T(8,128)(2,1)}, bf16[8,2,4,224,512]{4,3,2,1,0:T(8,128)(2,1)}) custom-call(s32[1]{0:T(128)} %bitcast.me_ref.at, bf16[2,3,272,128]{3,2,1,0:T(8,128)(2,1)S(1)} %get-tuple-element.33.refs_0_, bf16[2,3,272,128]{3,2,1,0:T(8,128)(2,1)} %collective-permute-done.6.refs_1_, ...), custom_call_target="tpu_custom_call", output_to_operand_aliasing={{0}: (6, {}), {1}: (7, {})} | custom-call | flops 855638016 | bytes 8355840 | tf_op jit(solution)/shard_map/absorb/pallas_call | solution.py:286
  (18 shorter events, 0.0 us)
Async XLA Ops:
  1.4 3.1 %copy-start.14 = (s32[2,32]{1,0:T(2,128)S(1)}, s32[2,32]{1,0:T(2,128)}, u32[]{:S(2)}) copy-start(s32[2,32]{1,0:T(2,128)} %owners.1) | copy-start | bytes 772
  8.4 1.0 copy-start.3
  9.5 10.2 %copy-start.16 = (s32[8,4]{0,1:T(4,128)S(1)}, s32[8,4]{0,1:T(4,128)}, u32[]{:S(2)}) copy-start(s32[8,4]{0,1:T(4,128)} %param.7) | copy-start | bytes 388
  9.5 23.2 %all-to-all-start.2 = ((bf16[8,34,16,128]{3,2,1,0:T(8,128)(2,1)}), bf16[8,34,16,128]{3,2,1,0:T(8,128)(2,1)S(1)}, u32[]{:S(2)}, u32[]{:S(2)}) async-start(bf16[8,34,16,128]{3,2,1,0:T(8,128)(2,1)} %copy-done.3), calls=%async_computation.2 | async-start | bytes 2228224 | tf_op jit(solution)/shard_map/all_to_all | solution.py:341
  13.8 15.9 %collective-permute-start.1 = (bf16[8,8,2,16,128]{4,3,2,1,0:T(8,128)(2,1)S(1)}, bf16[8,8,2,16,128]{4,3,2,1,0:T(8,128)(2,1)S(1)}, u32[]{:S(2)}, u32[]{:S(2)}) collective-permute-start(bf16[8,8,2,16,128]{4,3,2,1,0:T(8,128)(2,1)S(1)} %bitcast.11), channel_id=1, source_target_pairs={{1,0},{2,1},{3,2},{5,4},{6,5},{7,6},{9,8},{10,9},{11,10},{13,12},{... | collective-permute-start | bytes 1572872 | tf_op jit(solution)/shard_map/ppermute | solution.py:157
  16.2 15.6 %collective-permute-start = (bf16[8,8,2,16,128]{4,3,2,1,0:T(8,128)(2,1)S(1)}, bf16[8,8,2,16,128]{4,3,2,1,0:T(8,128)(2,1)S(1)}, u32[]{:S(2)}, u32[]{:S(2)}) collective-permute-start(bf16[8,8,2,16,128]{4,3,2,1,0:T(8,128)(2,1)S(1)} %bitcast.12), channel_id=1, source_target_pairs={{0,1},{1,2},{2,3},{4,5},{5,6},{6,7},{8,9},{9,10},{10,11},{12,13},{... | collective-permute-start | bytes 1572872 | tf_op jit(solution)/shard_map/ppermute | solution.py:156
  32.7 14.1 %collective-permute-start.2 = (bf16[8,8,2,16,128]{4,3,2,1,0:T(8,128)(2,1)}, bf16[8,8,2,16,128]{4,3,2,1,0:T(8,128)(2,1)}, u32[]{:S(2)}, u32[]{:S(2)}) collective-permute-start(bf16[8,8,2,16,128]{4,3,2,1,0:T(8,128)(2,1)} %pass_on.1.refs_0_), channel_id=1, source_target_pairs={{0,2},{1,0},{2,3},{3,1},{4,6},{5,4},{6,7},{7,5},{8,10},{9,8},{10,1... | collective-permute-start | bytes 1572872 | tf_op jit(solution)/shard_map/ppermute | solution.py:357
  32.7 1.0 copy-start.1
  33.7 24.8 %all-to-all-start.1 = ((bf16[8,51,16,128]{3,2,1,0:T(8,128)(2,1)}), bf16[8,51,16,128]{3,2,1,0:T(8,128)(2,1)S(1)}, u32[]{:S(2)}, u32[]{:S(2)}) async-start(bf16[8,51,16,128]{3,2,1,0:T(8,128)(2,1)} %get-tuple-element.25), calls=%async_computation.1 | async-start | bytes 3342336 | tf_op jit(solution)/shard_map/all_to_all | solution.py:341
  37.9 1.2 copy-start.2
  40.8 25.1 %copy-start.11 = (bf16[2,2,272,128]{3,2,1,0:T(8,128)(2,1)}, bf16[2,2,272,128]{3,2,1,0:T(8,128)(2,1)S(1)}, u32[]{:S(2)}) copy-start(bf16[2,2,272,128]{3,2,1,0:T(8,128)(2,1)S(1)} %get-tuple-element.28.refs_0_) | copy-start | bytes 835588
  40.8 29.1 %collective-permute-start.3 = (bf16[2,2,272,128]{3,2,1,0:T(8,128)(2,1)}, bf16[2,2,272,128]{3,2,1,0:T(8,128)(2,1)}, u32[]{:S(2)}, u32[]{:S(2)}) collective-permute-start(bf16[2,2,272,128]{3,2,1,0:T(8,128)(2,1)} %get-tuple-element.30), channel_id=1, source_target_pairs={{0,1},{1,2},{2,3},{3,0},{4,5},{5,6},{6,7},{7,4},{8,9},{9,10},{10,1... | collective-permute-start | bytes 835592 | tf_op jit(solution)/shard_map/ppermute | solution.py:375
  44.0 28.1 %collective-permute-start.4 = (bf16[2,2,272,128]{3,2,1,0:T(8,128)(2,1)}, bf16[2,2,272,128]{3,2,1,0:T(8,128)(2,1)}, u32[]{:S(2)}, u32[]{:S(2)}) collective-permute-start(bf16[2,2,272,128]{3,2,1,0:T(8,128)(2,1)} %get-tuple-element.31), channel_id=1, source_target_pairs={{0,2},{1,3},{2,0},{3,1},{4,6},{5,7},{6,4},{7,5},{8,10},{9,11},{10,... | collective-permute-start | bytes 835592 | tf_op jit(solution)/shard_map/ppermute | solution.py:375
  46.2 25.9 %collective-permute-start.5 = (bf16[2,2,272,128]{3,2,1,0:T(8,128)(2,1)}, bf16[2,2,272,128]{3,2,1,0:T(8,128)(2,1)}, u32[]{:S(2)}, u32[]{:S(2)}) collective-permute-start(bf16[2,2,272,128]{3,2,1,0:T(8,128)(2,1)} %get-tuple-element.32), channel_id=1, source_target_pairs={{0,3},{1,0},{2,1},{3,2},{4,7},{5,4},{6,5},{7,6},{8,11},{9,8},{10,9... | collective-permute-start | bytes 835592 | tf_op jit(solution)/shard_map/ppermute | solution.py:375
  46.7 44.8 %collective-permute-start.9 = (bf16[8,8,2,16,128]{4,3,2,1,0:T(8,128)(2,1)}, bf16[8,8,2,16,128]{4,3,2,1,0:T(8,128)(2,1)}, u32[]{:S(2)}, u32[]{:S(2)}) collective-permute-start(bf16[8,8,2,16,128]{4,3,2,1,0:T(8,128)(2,1)} %collective-permute-done.2.refs_1_.second_ref), channel_id=1, source_target_pairs={{1,0},{2,3},{5,4},{6,7},{9,8},{10,11},{13,12},{14,15},{17,16},{18,... | collective-permute-start | bytes 1572872 | tf_op jit(solution)/shard_map/ppermute | solution.py:358
  58.5 26.4 %all-to-all-start = ((bf16[8,51,16,128]{3,2,1,0:T(8,128)(2,1)}), bf16[8,51,16,128]{3,2,1,0:T(8,128)(2,1)}, u32[]{:S(2)}, u32[]{:S(2)}) async-start(bf16[8,51,16,128]{3,2,1,0:T(8,128)(2,1)} %get-tuple-element.24), calls=%async_computation | async-start | bytes 3342336 | tf_op jit(solution)/shard_map/all_to_all | solution.py:341
  66.0 0.8 copy-start.4
  66.7 34.7 %collective-permute-start.10 = (bf16[2,3,272,128]{3,2,1,0:T(8,128)(2,1)}, bf16[2,3,272,128]{3,2,1,0:T(8,128)(2,1)S(1)}, u32[]{:S(2)}, u32[]{:S(2)}) collective-permute-start(bf16[2,3,272,128]{3,2,1,0:T(8,128)(2,1)} %get-tuple-element.37), channel_id=1, source_target_pairs={{0,1},{1,2},{2,3},{3,0},{4,5},{5,6},{6,7},{7,4},{8,9},{9,10},{10,1... | collective-permute-start | bytes 1253384 | tf_op jit(solution)/shard_map/ppermute | solution.py:375
  69.9 55.1 %collective-permute-start.11 = (bf16[2,3,272,128]{3,2,1,0:T(8,128)(2,1)}, bf16[2,3,272,128]{3,2,1,0:T(8,128)(2,1)S(1)}, u32[]{:S(2)}, u32[]{:S(2)}) collective-permute-start(bf16[2,3,272,128]{3,2,1,0:T(8,128)(2,1)} %get-tuple-element.38), channel_id=1, source_target_pairs={{0,2},{1,3},{2,0},{3,1},{4,6},{5,7},{6,4},{7,5},{8,10},{9,11},{10,... | collective-permute-start | bytes 1253384 | tf_op jit(solution)/shard_map/ppermute | solution.py:375
  72.2 54.7 %collective-permute-start.12 = (bf16[2,3,272,128]{3,2,1,0:T(8,128)(2,1)}, bf16[2,3,272,128]{3,2,1,0:T(8,128)(2,1)}, u32[]{:S(2)}, u32[]{:S(2)}) collective-permute-start(bf16[2,3,272,128]{3,2,1,0:T(8,128)(2,1)} %get-tuple-element.39), channel_id=1, source_target_pairs={{0,3},{1,0},{2,1},{3,2},{4,7},{5,4},{6,5},{7,6},{8,11},{9,8},{10,9... | collective-permute-start | bytes 1253384 | tf_op jit(solution)/shard_map/ppermute | solution.py:375
  84.9 1.0 copy-start.5
  88.3 5.4 %copy-start.15 = (bf16[2,3,272,128]{3,2,1,0:T(8,128)(2,1)}, bf16[2,3,272,128]{3,2,1,0:T(8,128)(2,1)S(1)}, u32[]{:S(2)}) copy-start(bf16[2,3,272,128]{3,2,1,0:T(8,128)(2,1)S(1)} %get-tuple-element.36) | copy-start | bytes 1253380
  88.3 50.8 %collective-permute-start.6 = (bf16[2,3,272,128]{3,2,1,0:T(8,128)(2,1)}, bf16[2,3,272,128]{3,2,1,0:T(8,128)(2,1)}, u32[]{:S(2)}, u32[]{:S(2)}) collective-permute-start(bf16[2,3,272,128]{3,2,1,0:T(8,128)(2,1)} %get-tuple-element.34), channel_id=1, source_target_pairs={{0,1},{1,2},{2,3},{3,0},{4,5},{5,6},{6,7},{7,4},{8,9},{9,10},{10,1... | collective-permute-start | bytes 1253384 | tf_op jit(solution)/shard_map/ppermute | solution.py:375
  91.5 50.6 %collective-permute-start.7 = (bf16[2,3,272,128]{3,2,1,0:T(8,128)(2,1)}, bf16[2,3,272,128]{3,2,1,0:T(8,128)(2,1)}, u32[]{:S(2)}, u32[]{:S(2)}) collective-permute-start(bf16[2,3,272,128]{3,2,1,0:T(8,128)(2,1)} %get-tuple-element.35), channel_id=1, source_target_pairs={{0,2},{1,3},{2,0},{3,1},{4,6},{5,7},{6,4},{7,5},{8,10},{9,11},{10,... | collective-permute-start | bytes 1253384 | tf_op jit(solution)/shard_map/ppermute | solution.py:375
  95.0 1.3 copy-start
  96.4 31.8 %all-to-all-start.3 = ((bf16[8,4,8,2,16,128]{5,4,3,2,1,0:T(8,128)(2,1)}), bf16[8,4,8,2,16,128]{5,4,3,2,1,0:T(8,128)(2,1)S(1)}, u32[]{:S(2)}, u32[]{:S(2)}) async-start(bf16[8,4,8,2,16,128]{5,4,3,2,1,0:T(8,128)(2,1)} %copy-done), calls=%async_computation.3 | async-start | bytes 4194304 | tf_op jit(solution)/shard_map/all_to_all | solution.py:341
  101.4 25.5 %copy-start.7 = (bf16[2,3,272,128]{3,2,1,0:T(8,128)(2,1)}, bf16[2,3,272,128]{3,2,1,0:T(8,128)(2,1)S(1)}, u32[]{:S(2)}) copy-start(bf16[2,3,272,128]{3,2,1,0:T(8,128)(2,1)S(1)} %collective-permute-done.10.refs_0_.refs_1_) | copy-start | bytes 1253380
  101.4 42.6 %collective-permute-start.8 = (bf16[2,3,272,128]{3,2,1,0:T(8,128)(2,1)}, bf16[2,3,272,128]{3,2,1,0:T(8,128)(2,1)}, u32[]{:S(2)}, u32[]{:S(2)}) collective-permute-start(bf16[2,3,272,128]{3,2,1,0:T(8,128)(2,1)} %copy-done.15), channel_id=1, source_target_pairs={{0,3},{1,0},{2,1},{3,2},{4,7},{5,4},{6,5},{7,6},{8,11},{9,8},{10,9... | collective-permute-start | bytes 1253384 | tf_op jit(solution)/shard_map/ppermute | solution.py:375
  125.1 1.8 %copy-start.9 = (bf16[2,3,272,128]{3,2,1,0:T(8,128)(2,1)}, bf16[2,3,272,128]{3,2,1,0:T(8,128)(2,1)S(1)}, u32[]{:S(2)}) copy-start(bf16[2,3,272,128]{3,2,1,0:T(8,128)(2,1)S(1)} %collective-permute-done.11.refs_1_.refs_2_) | copy-start | bytes 1253380
  128.2 1.8 %copy-start.12 = (bf16[2,2,272,128]{3,2,1,0:T(8,128)(2,1)S(1)}, bf16[2,2,272,128]{3,2,1,0:T(8,128)(2,1)}, u32[]{:S(2)}) copy-start(bf16[2,2,272,128]{3,2,1,0:T(8,128)(2,1)} %copy-done.11) | copy-start | bytes 835588
  128.2 0.7 copy-start.13
  130.0 4.0 %copy-start.6 = (bf16[2,3,272,128]{3,2,1,0:T(8,128)(2,1)S(1)}, bf16[2,3,272,128]{3,2,1,0:T(8,128)(2,1)}, u32[]{:S(2)}) copy-start(bf16[2,3,272,128]{3,2,1,0:T(8,128)(2,1)} %copy-done.4) | copy-start | bytes 1253380
  130.0 4.0 %copy-start.8 = (bf16[2,3,272,128]{3,2,1,0:T(8,128)(2,1)S(1)}, bf16[2,3,272,128]{3,2,1,0:T(8,128)(2,1)}, u32[]{:S(2)}) copy-start(bf16[2,3,272,128]{3,2,1,0:T(8,128)(2,1)} %copy-done.7) | copy-start | bytes 1253380
  130.0 4.0 %copy-start.10 = (bf16[2,3,272,128]{3,2,1,0:T(8,128)(2,1)S(1)}, bf16[2,3,272,128]{3,2,1,0:T(8,128)(2,1)}, u32[]{:S(2)}) copy-start(bf16[2,3,272,128]{3,2,1,0:T(8,128)(2,1)} %copy-done.9) | copy-start | bytes 1253380

commit v18 on v17

--- a/solution.py
+++ b/solution.py
@@ -264,15 +264,23 @@
     def kernel(at, *refs):
         parts, mats = refs[:t_ways], refs[t_ways]
         q_out, o_out = refs[-2:]
+        came_from = [lax.rem(at[0] - d + t_ways, t_ways) for d in range(t_ways)]
+        pairs = [(d, f) for d in range(t_ways) for f in range(blocks)]
+        product = jnp.dot(
+            jnp.concatenate([parts[d][f, 0, :q_rows] for d, f in pairs]),
+            mats[0, 0],
+            preferred_element_type=jnp.float32,
+        ).astype(jnp.bfloat16)
+        for n, (d, f) in enumerate(pairs):
+            q_out[0, f, came_from[d]] = product[n * q_rows : (n + 1) * q_rows]
         for d in range(t_ways):
-            t = lax.rem(at[0] - d + t_ways, t_ways)
+            product = jnp.dot(
+                jnp.concatenate([parts[d][f, 0, q_rows:] for f in range(blocks)]),
+                mats[0, 1],
+                preferred_element_type=jnp.float32,
+            ).astype(jnp.bfloat16)
             for f in range(blocks):
-                q_out[0, f, t] = jnp.dot(
-                    parts[d][f, 0, :q_rows], mats[0, 0], preferred_element_type=jnp.float32
-                ).astype(jnp.bfloat16)
-                o_out[0, f, t] = jnp.dot(
-                    parts[d][f, 0, q_rows:], mats[0, 1], preferred_element_type=jnp.float32
-                ).astype(jnp.bfloat16)
+                o_out[0, f, came_from[d]] = product[f * o_rows : (f + 1) * o_rows]
 
     in_specs = [pl.BlockSpec((blocks, 1, rows, LANES), lambda j, at: (0, j, 0, 0))] * t_ways
     in_specs += [pl.BlockSpec((1,) + matrices.shape[1:], lambda j, at: (items[0] + j, 0, 0, 0))]

time: 150 us -> 150 us (level)
  no operation moved by 1% of the time
where the time goes in v18:
time: 150 us; the launch traced here: 149 us
  waiting for transfers between devices  63.1 us (42%)
  starting transfers between devices  45.8 us (31%)
  Pallas kernels  28.5 us (19%)
  local copies, waits for them, and re-layouts  11.1 us (7%)
    ppermute x9, waiting for transfers between devices, per_device(): lax.ppermute(piece, 'tp', [(i, (i + shift) % t_ways) for i in range(t_way...  30.6 us
    all_to_all x4, waiting for transfers between devices, over_fsdp(): x = lax.all_to_all(x, 'fsdp', split_axis=0, concat_axis=0, tiled=True)  20 us
    all_to_all x4, starting transfers between devices, over_fsdp(): x = lax.all_to_all(x, 'fsdp', split_axis=0, concat_axis=0, tiled=True)  19.3 us
    ppermute x9, starting transfers between devices, per_device(): lax.ppermute(piece, 'tp', [(i, (i + shift) % t_ways) for i in range(t_way...  16.3 us
    pallas_call x3, Pallas kernels, absorb(): pl.pallas_call(kernel, grid_spec=pltpu.PrefetchScalarGridSpec(num_scalar_...  14.1 us
    unnamed x37, local copies, waits for them, and re-layouts  11.1 us
    ppermute x1, waiting for transfers between devices, neighbours(): lax.ppermute(x, axis, [(i + 1, i) for i in range(ways - 1)])  9.92 us
    pallas_call x3, Pallas kernels, cut(): pl.pallas_call(kernel, grid=(1,), out_shape=[jax.ShapeDtypeStruct(shape,...  6 us
  transfers between devices with their start and end apart: 17, of which 9 were waited for; matrix products, arithmetic and copies ran while one was open for 0% of the time, Pallas kernels for 13%

profile of v18, /device:TPU:10, one launch (start us, length us, event | category | flops | bytes accessed | tf_op | source)
XLA Modules:
  0.0 149.3 jit_solution(14421894597903775846)
XLA Ops:
  0.6 0.8 copy.10.offsets
  1.4 3.1 %copy.14 = bf16[1,2,9728,128]{3,2,1,0:T(8,128)(2,1)S(1)} copy(bf16[1,2,9728,128]{3,1,2,0:T(2,128)(2,1)} %bitcast.19) | data formatting | bytes 9961472
  4.5 0.0 copy-done.14
  4.6 3.9 %pack.1 = (bf16[8,16,16,128]{3,2,1,0:T(8,128)(2,1)S(1)}, bf16[8,34,16,128]{3,2,1,0:T(8,128)(2,1)S(1)}, bf16[8,51,16,128]{3,2,1,0:T(8,128)(2,1)}, bf16[8,51,16,128]{3,2,1,0:T(8,128)(2,1)}) custom-call(s32[2,32,4]{2,1,0:T(8,128)S(1)} %copy.10.offsets, s32[2,32]{1,0:T(2,128)S(1)} %copy-done.14, bf16[2,608,16,128]{3,2,1,0:T(8,128)(2,1)S(1)} %bitcast.10), custom_call_target="tpu_custom_call" | custom-call | bytes 9961472 | tf_op jit(solution)/shard_map/pack/pallas_call | solution.py:77
  8.4 1.0 copy-done.3
  9.5 4.4 %all-to-all-start.2 = ((bf16[8,34,16,128]{3,2,1,0:T(8,128)(2,1)}), bf16[8,34,16,128]{3,2,1,0:T(8,128)(2,1)S(1)}, u32[]{:S(2)}, u32[]{:S(2)}) async-start(bf16[8,34,16,128]{3,2,1,0:T(8,128)(2,1)} %copy-done.3), calls=%async_computation.2 | async-start | bytes 2228224 | tf_op jit(solution)/shard_map/all_to_all | solution.py:349
  13.8 2.3 %collective-permute-start.1 = (bf16[8,8,2,16,128]{4,3,2,1,0:T(8,128)(2,1)S(1)}, bf16[8,8,2,16,128]{4,3,2,1,0:T(8,128)(2,1)S(1)}, u32[]{:S(2)}, u32[]{:S(2)}) collective-permute-start(bf16[8,8,2,16,128]{4,3,2,1,0:T(8,128)(2,1)S(1)} %bitcast.11), channel_id=1, source_target_pairs={{1,0},{2,1},{3,2},{5,4},{6,5},{7,6},{9,8},{10,9},{11,10},{13,12},{... | collective-permute-start | bytes 1572872 | tf_op jit(solution)/shard_map/ppermute | solution.py:157
  16.2 3.5 %collective-permute-start = (bf16[8,8,2,16,128]{4,3,2,1,0:T(8,128)(2,1)S(1)}, bf16[8,8,2,16,128]{4,3,2,1,0:T(8,128)(2,1)S(1)}, u32[]{:S(2)}, u32[]{:S(2)}) collective-permute-start(bf16[8,8,2,16,128]{4,3,2,1,0:T(8,128)(2,1)S(1)} %bitcast.12), channel_id=1, source_target_pairs={{0,1},{1,2},{2,3},{4,5},{5,6},{6,7},{8,9},{9,10},{10,11},{12,13},{... | collective-permute-start | bytes 1572872 | tf_op jit(solution)/shard_map/ppermute | solution.py:156
  19.7 0.0 copy-done.16
  19.7 0.1 copy.13.mapped
  19.8 9.9 %collective-permute-done.1.down_ref = bf16[8,8,2,16,128]{4,3,2,1,0:T(8,128)(2,1)S(1)} collective-permute-done((bf16[8,8,2,16,128]{4,3,2,1,0:T(8,128)(2,1)S(1)}, bf16[8,8,2,16,128]{4,3,2,1,0:T(8,128)(2,1)S(1)}, u32[]{:S(2)}, u32[]{:S(2)}) %collective-permute-start.1) | collective-permute-done | bytes 524320 | tf_op jit(solution)/shard_map/ppermute | solution.py:157
  29.7 2.1 %collective-permute-done.up_ref = bf16[8,8,2,16,128]{4,3,2,1,0:T(8,128)(2,1)S(1)} collective-permute-done((bf16[8,8,2,16,128]{4,3,2,1,0:T(8,128)(2,1)S(1)}, bf16[8,8,2,16,128]{4,3,2,1,0:T(8,128)(2,1)S(1)}, u32[]{:S(2)}, u32[]{:S(2)}) %collective-permute-start) | collective-permute-done | bytes 524320 | tf_op jit(solution)/shard_map/ppermute | solution.py:156
  31.8 0.9 pass_on.1.refs_0_
  32.7 0.0 collective-permute-start.2
  32.7 0.0 all-to-all-done.2
  32.7 1.0 copy-done.1
  33.7 4.2 %all-to-all-start.1 = ((bf16[8,51,16,128]{3,2,1,0:T(8,128)(2,1)}), bf16[8,51,16,128]{3,2,1,0:T(8,128)(2,1)S(1)}, u32[]{:S(2)}, u32[]{:S(2)}) async-start(bf16[8,51,16,128]{3,2,1,0:T(8,128)(2,1)} %get-tuple-element.25), calls=%async_computation.1 | async-start | bytes 3342336 | tf_op jit(solution)/shard_map/all_to_all | solution.py:349
  37.9 1.2 copy-done.2
  39.1 1.7 %cut.3 = (bf16[2,2,272,128]{3,2,1,0:T(8,128)(2,1)S(1)}, bf16[2,2,272,128]{3,2,1,0:T(8,128)(2,1)}, bf16[2,2,272,128]{3,2,1,0:T(8,128)(2,1)}, bf16[2,2,272,128]{3,2,1,0:T(8,128)(2,1)}) custom-call(s32[8,4]{1,0:T(8,128)S(1)} %copy.13.mapped, bf16[8,544,128]{2,1,0:T(8,128)(2,1)S(1)} %bitcast.16, bf16[8,8,2,16,128]{4,3,2,1,0:T(8,128)(2,1)} %pass_on.1.refs_0_), custom_call_target="tpu_custom_call" | custom-call | flops 34500001792 | bytes 2228224 | tf_op jit(solution)/shard_map/cut/pallas_call | solution.py:121
  40.8 3.2 %collective-permute-start.3 = (bf16[2,2,272,128]{3,2,1,0:T(8,128)(2,1)}, bf16[2,2,272,128]{3,2,1,0:T(8,128)(2,1)}, u32[]{:S(2)}, u32[]{:S(2)}) collective-permute-start(bf16[2,2,272,128]{3,2,1,0:T(8,128)(2,1)} %get-tuple-element.30), channel_id=1, source_target_pairs={{0,1},{1,2},{2,3},{3,0},{4,5},{5,6},{6,7},{7,4},{8,9},{9,10},{10,1... | collective-permute-start | bytes 835592 | tf_op jit(solution)/shard_map/ppermute | solution.py:383
  44.0 2.2 %collective-permute-start.4 = (bf16[2,2,272,128]{3,2,1,0:T(8,128)(2,1)}, bf16[2,2,272,128]{3,2,1,0:T(8,128)(2,1)}, u32[]{:S(2)}, u32[]{:S(2)}) collective-permute-start(bf16[2,2,272,128]{3,2,1,0:T(8,128)(2,1)} %get-tuple-element.31), channel_id=1, source_target_pairs={{0,2},{1,3},{2,0},{3,1},{4,6},{5,7},{6,4},{7,5},{8,10},{9,11},{10,... | collective-permute-start | bytes 835592 | tf_op jit(solution)/shard_map/ppermute | solution.py:383
  46.2 0.0 collective-permute-start.5
  46.3 0.5 collective-permute-done.2.refs_1_.second_ref
  46.7 4.4 %collective-permute-start.9 = (bf16[8,8,2,16,128]{4,3,2,1,0:T(8,128)(2,1)}, bf16[8,8,2,16,128]{4,3,2,1,0:T(8,128)(2,1)}, u32[]{:S(2)}, u32[]{:S(2)}) collective-permute-start(bf16[8,8,2,16,128]{4,3,2,1,0:T(8,128)(2,1)} %collective-permute-done.2.refs_1_.second_ref), channel_id=1, source_target_pairs={{1,0},{2,3},{5,4},{6,7},{9,8},{10,11},{13,12},{14,15},{17,16},{18,... | collective-permute-start | bytes 1572872 | tf_op jit(solution)/shard_map/ppermute | solution.py:366
  51.1 7.3 %all-to-all-done.1 = bf16[8,51,16,128]{3,2,1,0:T(8,128)(2,1)S(1)} async-done(((bf16[8,51,16,128]{3,2,1,0:T(8,128)(2,1)}), bf16[8,51,16,128]{3,2,1,0:T(8,128)(2,1)S(1)}, u32[]{:S(2)}, u32[]{:S(2)}) %all-to-all-start.1) | async-done | bytes 1671200 | tf_op jit(solution)/shard_map/all_to_all | solution.py:349
  58.5 5.7 %all-to-all-start = ((bf16[8,51,16,128]{3,2,1,0:T(8,128)(2,1)}), bf16[8,51,16,128]{3,2,1,0:T(8,128)(2,1)}, u32[]{:S(2)}, u32[]{:S(2)}) async-start(bf16[8,51,16,128]{3,2,1,0:T(8,128)(2,1)} %get-tuple-element.24), calls=%async_computation | async-start | bytes 3342336 | tf_op jit(solution)/shard_map/all_to_all | solution.py:349
  64.2 1.8 %cut.4 = (bf16[2,3,272,128]{3,2,1,0:T(8,128)(2,1)S(1)}, bf16[2,3,272,128]{3,2,1,0:T(8,128)(2,1)}, bf16[2,3,272,128]{3,2,1,0:T(8,128)(2,1)}, bf16[2,3,272,128]{3,2,1,0:T(8,128)(2,1)}) custom-call(s32[8,4]{1,0:T(8,128)S(1)} %copy.13.mapped, bf16[8,816,128]{2,1,0:T(8,128)(2,1)S(1)} %bitcast.15, bf16[2,2,272,128]{3,2,1,0:T(8,128)(2,1)S(1)} %get-tuple-element.28.refs_0_, ...), custom_call_target="tpu_custom_call" | custom-call | flops 34500001792 | bytes 3342336 | tf_op jit(solution)/shard_map/cut/pallas_call | solution.py:121
  66.0 0.0 copy-done.11
  66.0 0.8 copy-done.4
  66.7 3.2 %collective-permute-start.10 = (bf16[2,3,272,128]{3,2,1,0:T(8,128)(2,1)}, bf16[2,3,272,128]{3,2,1,0:T(8,128)(2,1)S(1)}, u32[]{:S(2)}, u32[]{:S(2)}) collective-permute-start(bf16[2,3,272,128]{3,2,1,0:T(8,128)(2,1)} %get-tuple-element.37), channel_id=1, source_target_pairs={{0,1},{1,2},{2,3},{3,0},{4,5},{5,6},{6,7},{7,4},{8,9},{9,10},{10,1... | collective-permute-start | bytes 1253384 | tf_op jit(solution)/shard_map/ppermute | solution.py:383
  69.9 0.0 collective-permute-done.3.refs_1_
  69.9 2.2 %collective-permute-start.11 = (bf16[2,3,272,128]{3,2,1,0:T(8,128)(2,1)}, bf16[2,3,272,128]{3,2,1,0:T(8,128)(2,1)S(1)}, u32[]{:S(2)}, u32[]{:S(2)}) collective-permute-start(bf16[2,3,272,128]{3,2,1,0:T(8,128)(2,1)} %get-tuple-element.38), channel_id=1, source_target_pairs={{0,2},{1,3},{2,0},{3,1},{4,6},{5,7},{6,4},{7,5},{8,10},{9,11},{10,... | collective-permute-start | bytes 1253384 | tf_op jit(solution)/shard_map/ppermute | solution.py:383
  72.1 0.0 collective-permute-done.4.refs_2_
  72.2 0.0 collective-permute-start.12
  72.2 0.0 collective-permute-done.5.refs_3_
  72.2 12.7 %all-to-all-done = bf16[8,51,16,128]{3,2,1,0:T(8,128)(2,1)} async-done(((bf16[8,51,16,128]{3,2,1,0:T(8,128)(2,1)}), bf16[8,51,16,128]{3,2,1,0:T(8,128)(2,1)}, u32[]{:S(2)}, u32[]{:S(2)}) %all-to-all-start) | async-done | bytes 1671200 | tf_op jit(solution)/shard_map/all_to_all | solution.py:349
  84.9 1.0 copy-done.5
  85.9 2.5 %cut.5 = (bf16[2,3,272,128]{3,2,1,0:T(8,128)(2,1)S(1)}, bf16[2,3,272,128]{3,2,1,0:T(8,128)(2,1)}, bf16[2,3,272,128]{3,2,1,0:T(8,128)(2,1)}, bf16[2,3,272,128]{3,2,1,0:T(8,128)(2,1)S(1)}) custom-call(s32[8,4]{1,0:T(8,128)S(1)} %copy.13.mapped, bf16[8,816,128]{2,1,0:T(8,128)(2,1)} %bitcast.1.source, bf16[2,3,272,128]{3,2,1,0:T(8,128)(2,1)S(1)} %copy-done.5, ...), custom_call_target="tpu_custom_call" | custom-call | flops 34500001792 | bytes 3342336 | tf_op jit(solution)/shard_map/cut/pallas_call | solution.py:121
  88.3 3.2 %collective-permute-start.6 = (bf16[2,3,272,128]{3,2,1,0:T(8,128)(2,1)}, bf16[2,3,272,128]{3,2,1,0:T(8,128)(2,1)}, u32[]{:S(2)}, u32[]{:S(2)}) collective-permute-start(bf16[2,3,272,128]{3,2,1,0:T(8,128)(2,1)} %get-tuple-element.34), channel_id=1, source_target_pairs={{0,1},{1,2},{2,3},{3,0},{4,5},{5,6},{6,7},{7,4},{8,9},{9,10},{10,1... | collective-permute-start | bytes 1253384 | tf_op jit(solution)/shard_map/ppermute | solution.py:383
  91.5 0.0 collective-permute-done.9.third_ref
  91.5 2.2 %collective-permute-start.7 = (bf16[2,3,272,128]{3,2,1,0:T(8,128)(2,1)}, bf16[2,3,272,128]{3,2,1,0:T(8,128)(2,1)}, u32[]{:S(2)}, u32[]{:S(2)}) collective-permute-start(bf16[2,3,272,128]{3,2,1,0:T(8,128)(2,1)} %get-tuple-element.35), channel_id=1, source_target_pairs={{0,2},{1,3},{2,0},{3,1},{4,6},{5,7},{6,4},{7,5},{8,10},{9,11},{10,... | collective-permute-start | bytes 1253384 | tf_op jit(solution)/shard_map/ppermute | solution.py:383
  93.7 0.0 copy-done.15
  93.7 1.3 join.1
  95.0 0.0 copy-start
  95.1 1.3 copy-done
  96.4 5.0 %all-to-all-start.3 = ((bf16[8,4,8,2,16,128]{5,4,3,2,1,0:T(8,128)(2,1)}), bf16[8,4,8,2,16,128]{5,4,3,2,1,0:T(8,128)(2,1)S(1)}, u32[]{:S(2)}, u32[]{:S(2)}) async-start(bf16[8,4,8,2,16,128]{5,4,3,2,1,0:T(8,128)(2,1)} %copy-done), calls=%async_computation.3 | async-start | bytes 4194304 | tf_op jit(solution)/shard_map/all_to_all | solution.py:349
  101.4 0.0 collective-permute-done.10.refs_0_.refs_1_
  101.4 0.1 collective-permute-start.8
  101.5 23.6 %collective-permute-done.11.refs_1_.refs_2_ = bf16[2,3,272,128]{3,2,1,0:T(8,128)(2,1)S(1)} collective-permute-done((bf16[2,3,272,128]{3,2,1,0:T(8,128)(2,1)}, bf16[2,3,272,128]{3,2,1,0:T(8,128)(2,1)S(1)}, u32[]{:S(2)}, u32[]{:S(2)}) %collective-permute-start.11) | collective-permute-done | bytes 417824 | tf_op jit(solution)/shard_map/ppermute | solution.py:383
  125.1 1.8 %collective-permute-done.12.refs_2_.refs_3_ = bf16[2,3,272,128]{3,2,1,0:T(8,128)(2,1)} collective-permute-done((bf16[2,3,272,128]{3,2,1,0:T(8,128)(2,1)}, bf16[2,3,272,128]{3,2,1,0:T(8,128)(2,1)}, u32[]{:S(2)}, u32[]{:S(2)}) %collective-permute-start.12) | collective-permute-done | bytes 417824 | tf_op jit(solution)/shard_map/ppermute | solution.py:383
  126.9 0.0 copy-done.7
  126.9 0.0 copy-done.9
  126.9 1.3 token_.1.refs_0_
  128.2 0.0 all-to-all-done.3.pieces
  128.2 0.7 copy-done.13
  128.9 1.0 assemble.1.refs_4_
  130.0 0.0 copy-done.12
  130.0 3.9 %absorb.3 = (bf16[8,2,4,48,512]{4,3,2,1,0:T(8,128)(2,1)}, bf16[8,2,4,224,512]{4,3,2,1,0:T(8,128)(2,1)}) custom-call(s32[1]{0:T(128)} %bitcast.me_ref.at, bf16[2,2,272,128]{3,2,1,0:T(8,128)(2,1)S(1)} %copy-done.12, bf16[2,2,272,128]{3,2,1,0:T(8,128)(2,1)} %collective-permute-done.3.refs_1_, bf16[2,2,272,128]{3,2,1,0:T(8,128)(2,1)} %collective-permute-done.4.refs_2_, ...), custom_call_target="tpu_custom_call" | custom-call | flops 570425344 | bytes 5570560 | tf_op jit(solution)/shard_map/absorb/pallas_call | solution.py:294
  133.9 0.0 copy-done.8
  133.9 4.9 %absorb.4 = (bf16[8,2,4,48,512]{4,3,2,1,0:T(8,128)(2,1)}, bf16[8,2,4,224,512]{4,3,2,1,0:T(8,128)(2,1)}) custom-call(s32[1]{0:T(128)} %bitcast.me_ref.at, bf16[2,3,272,128]{3,2,1,0:T(8,128)(2,1)S(1)} %copy-done.6, bf16[2,3,272,128]{3,2,1,0:T(8,128)(2,1)S(1)} %copy-done.8, ...), custom_call_target="tpu_custom_call", output_to_operand_aliasing={{0}: (6, {}), {1}: (7, {})} | custom-call | flops 855638016 | bytes 8355840 | tf_op jit(solution)/shard_map/absorb/pallas_call | solution.py:294
  138.8 0.0 collective-permute-done.6.refs_1_
  138.8 3.4 %collective-permute-done.7.refs_2_ = bf16[2,3,272,128]{3,2,1,0:T(8,128)(2,1)} collective-permute-done((bf16[2,3,272,128]{3,2,1,0:T(8,128)(2,1)}, bf16[2,3,272,128]{3,2,1,0:T(8,128)(2,1)}, u32[]{:S(2)}, u32[]{:S(2)}) %collective-permute-start.7) | collective-permute-done | bytes 417824 | tf_op jit(solution)/shard_map/ppermute | solution.py:383
  142.2 1.8 %collective-permute-done.8.refs_3_ = bf16[2,3,272,128]{3,2,1,0:T(8,128)(2,1)} collective-permute-done((bf16[2,3,272,128]{3,2,1,0:T(8,128)(2,1)}, bf16[2,3,272,128]{3,2,1,0:T(8,128)(2,1)}, u32[]{:S(2)}, u32[]{:S(2)}) %collective-permute-start.8) | collective-permute-done | bytes 417824 | tf_op jit(solution)/shard_map/ppermute | solution.py:383
  144.0 5.3 %absorb.5 = (bf16[8,2,4,48,512]{4,3,2,1,0:T(8,128)(2,1)}, bf16[8,2,4,224,512]{4,3,2,1,0:T(8,128)(2,1)}) custom-call(s32[1]{0:T(128)} %bitcast.me_ref.at, bf16[2,3,272,128]{3,2,1,0:T(8,128)(2,1)S(1)} %get-tuple-element.33.refs_0_, bf16[2,3,272,128]{3,2,1,0:T(8,128)(2,1)} %collective-permute-done.6.refs_1_, ...), custom_call_target="tpu_custom_call", output_to_operand_aliasing={{0}: (6, {}), {1}: (7, {})} | custom-call | flops 855638016 | bytes 8355840 | tf_op jit(solution)/shard_map/absorb/pallas_call | solution.py:294
  (18 shorter events, 0.0 us)
Async XLA Ops:
  1.4 3.1 %copy-start.14 = (s32[2,32]{1,0:T(2,128)S(1)}, s32[2,32]{1,0:T(2,128)}, u32[]{:S(2)}) copy-start(s32[2,32]{1,0:T(2,128)} %owners.1) | copy-start | bytes 772
  8.4 1.0 copy-start.3
  9.5 10.2 %copy-start.16 = (s32[8,4]{0,1:T(4,128)S(1)}, s32[8,4]{0,1:T(4,128)}, u32[]{:S(2)}) copy-start(s32[8,4]{0,1:T(4,128)} %param.7) | copy-start | bytes 388
  9.5 23.2 %all-to-all-start.2 = ((bf16[8,34,16,128]{3,2,1,0:T(8,128)(2,1)}), bf16[8,34,16,128]{3,2,1,0:T(8,128)(2,1)S(1)}, u32[]{:S(2)}, u32[]{:S(2)}) async-start(bf16[8,34,16,128]{3,2,1,0:T(8,128)(2,1)} %copy-done.3), calls=%async_computation.2 | async-start | bytes 2228224 | tf_op jit(solution)/shard_map/all_to_all | solution.py:349
  13.8 15.9 %collective-permute-start.1 = (bf16[8,8,2,16,128]{4,3,2,1,0:T(8,128)(2,1)S(1)}, bf16[8,8,2,16,128]{4,3,2,1,0:T(8,128)(2,1)S(1)}, u32[]{:S(2)}, u32[]{:S(2)}) collective-permute-start(bf16[8,8,2,16,128]{4,3,2,1,0:T(8,128)(2,1)S(1)} %bitcast.11), channel_id=1, source_target_pairs={{1,0},{2,1},{3,2},{5,4},{6,5},{7,6},{9,8},{10,9},{11,10},{13,12},{... | collective-permute-start | bytes 1572872 | tf_op jit(solution)/shard_map/ppermute | solution.py:157
  16.2 15.6 %collective-permute-start = (bf16[8,8,2,16,128]{4,3,2,1,0:T(8,128)(2,1)S(1)}, bf16[8,8,2,16,128]{4,3,2,1,0:T(8,128)(2,1)S(1)}, u32[]{:S(2)}, u32[]{:S(2)}) collective-permute-start(bf16[8,8,2,16,128]{4,3,2,1,0:T(8,128)(2,1)S(1)} %bitcast.12), channel_id=1, source_target_pairs={{0,1},{1,2},{2,3},{4,5},{5,6},{6,7},{8,9},{9,10},{10,11},{12,13},{... | collective-permute-start | bytes 1572872 | tf_op jit(solution)/shard_map/ppermute | solution.py:156
  32.7 14.1 %collective-permute-start.2 = (bf16[8,8,2,16,128]{4,3,2,1,0:T(8,128)(2,1)}, bf16[8,8,2,16,128]{4,3,2,1,0:T(8,128)(2,1)}, u32[]{:S(2)}, u32[]{:S(2)}) collective-permute-start(bf16[8,8,2,16,128]{4,3,2,1,0:T(8,128)(2,1)} %pass_on.1.refs_0_), channel_id=1, source_target_pairs={{0,2},{1,0},{2,3},{3,1},{4,6},{5,4},{6,7},{7,5},{8,10},{9,8},{10,1... | collective-permute-start | bytes 1572872 | tf_op jit(solution)/shard_map/ppermute | solution.py:365
  32.7 1.0 copy-start.1
  33.7 24.8 %all-to-all-start.1 = ((bf16[8,51,16,128]{3,2,1,0:T(8,128)(2,1)}), bf16[8,51,16,128]{3,2,1,0:T(8,128)(2,1)S(1)}, u32[]{:S(2)}, u32[]{:S(2)}) async-start(bf16[8,51,16,128]{3,2,1,0:T(8,128)(2,1)} %get-tuple-element.25), calls=%async_computation.1 | async-start | bytes 3342336 | tf_op jit(solution)/shard_map/all_to_all | solution.py:349
  37.9 1.2 copy-start.2
  40.8 25.1 %copy-start.11 = (bf16[2,2,272,128]{3,2,1,0:T(8,128)(2,1)}, bf16[2,2,272,128]{3,2,1,0:T(8,128)(2,1)S(1)}, u32[]{:S(2)}) copy-start(bf16[2,2,272,128]{3,2,1,0:T(8,128)(2,1)S(1)} %get-tuple-element.28.refs_0_) | copy-start | bytes 835588
  40.8 29.1 %collective-permute-start.3 = (bf16[2,2,272,128]{3,2,1,0:T(8,128)(2,1)}, bf16[2,2,272,128]{3,2,1,0:T(8,128)(2,1)}, u32[]{:S(2)}, u32[]{:S(2)}) collective-permute-start(bf16[2,2,272,128]{3,2,1,0:T(8,128)(2,1)} %get-tuple-element.30), channel_id=1, source_target_pairs={{0,1},{1,2},{2,3},{3,0},{4,5},{5,6},{6,7},{7,4},{8,9},{9,10},{10,1... | collective-permute-start | bytes 835592 | tf_op jit(solution)/shard_map/ppermute | solution.py:383
  44.0 28.1 %collective-permute-start.4 = (bf16[2,2,272,128]{3,2,1,0:T(8,128)(2,1)}, bf16[2,2,272,128]{3,2,1,0:T(8,128)(2,1)}, u32[]{:S(2)}, u32[]{:S(2)}) collective-permute-start(bf16[2,2,272,128]{3,2,1,0:T(8,128)(2,1)} %get-tuple-element.31), channel_id=1, source_target_pairs={{0,2},{1,3},{2,0},{3,1},{4,6},{5,7},{6,4},{7,5},{8,10},{9,11},{10,... | collective-permute-start | bytes 835592 | tf_op jit(solution)/shard_map/ppermute | solution.py:383
  46.2 25.9 %collective-permute-start.5 = (bf16[2,2,272,128]{3,2,1,0:T(8,128)(2,1)}, bf16[2,2,272,128]{3,2,1,0:T(8,128)(2,1)}, u32[]{:S(2)}, u32[]{:S(2)}) collective-permute-start(bf16[2,2,272,128]{3,2,1,0:T(8,128)(2,1)} %get-tuple-element.32), channel_id=1, source_target_pairs={{0,3},{1,0},{2,1},{3,2},{4,7},{5,4},{6,5},{7,6},{8,11},{9,8},{10,9... | collective-permute-start | bytes 835592 | tf_op jit(solution)/shard_map/ppermute | solution.py:383
  46.7 44.8 %collective-permute-start.9 = (bf16[8,8,2,16,128]{4,3,2,1,0:T(8,128)(2,1)}, bf16[8,8,2,16,128]{4,3,2,1,0:T(8,128)(2,1)}, u32[]{:S(2)}, u32[]{:S(2)}) collective-permute-start(bf16[8,8,2,16,128]{4,3,2,1,0:T(8,128)(2,1)} %collective-permute-done.2.refs_1_.second_ref), channel_id=1, source_target_pairs={{1,0},{2,3},{5,4},{6,7},{9,8},{10,11},{13,12},{14,15},{17,16},{18,... | collective-permute-start | bytes 1572872 | tf_op jit(solution)/shard_map/ppermute | solution.py:366
  58.5 26.4 %all-to-all-start = ((bf16[8,51,16,128]{3,2,1,0:T(8,128)(2,1)}), bf16[8,51,16,128]{3,2,1,0:T(8,128)(2,1)}, u32[]{:S(2)}, u32[]{:S(2)}) async-start(bf16[8,51,16,128]{3,2,1,0:T(8,128)(2,1)} %get-tuple-element.24), calls=%async_computation | async-start | bytes 3342336 | tf_op jit(solution)/shard_map/all_to_all | solution.py:349
  66.0 0.8 copy-start.4
  66.7 34.7 %collective-permute-start.10 = (bf16[2,3,272,128]{3,2,1,0:T(8,128)(2,1)}, bf16[2,3,272,128]{3,2,1,0:T(8,128)(2,1)S(1)}, u32[]{:S(2)}, u32[]{:S(2)}) collective-permute-start(bf16[2,3,272,128]{3,2,1,0:T(8,128)(2,1)} %get-tuple-element.37), channel_id=1, source_target_pairs={{0,1},{1,2},{2,3},{3,0},{4,5},{5,6},{6,7},{7,4},{8,9},{9,10},{10,1... | collective-permute-start | bytes 1253384 | tf_op jit(solution)/shard_map/ppermute | solution.py:383
  69.9 55.1 %collective-permute-start.11 = (bf16[2,3,272,128]{3,2,1,0:T(8,128)(2,1)}, bf16[2,3,272,128]{3,2,1,0:T(8,128)(2,1)S(1)}, u32[]{:S(2)}, u32[]{:S(2)}) collective-permute-start(bf16[2,3,272,128]{3,2,1,0:T(8,128)(2,1)} %get-tuple-element.38), channel_id=1, source_target_pairs={{0,2},{1,3},{2,0},{3,1},{4,6},{5,7},{6,4},{7,5},{8,10},{9,11},{10,... | collective-permute-start | bytes 1253384 | tf_op jit(solution)/shard_map/ppermute | solution.py:383
  72.2 54.7 %collective-permute-start.12 = (bf16[2,3,272,128]{3,2,1,0:T(8,128)(2,1)}, bf16[2,3,272,128]{3,2,1,0:T(8,128)(2,1)}, u32[]{:S(2)}, u32[]{:S(2)}) collective-permute-start(bf16[2,3,272,128]{3,2,1,0:T(8,128)(2,1)} %get-tuple-element.39), channel_id=1, source_target_pairs={{0,3},{1,0},{2,1},{3,2},{4,7},{5,4},{6,5},{7,6},{8,11},{9,8},{10,9... | collective-permute-start | bytes 1253384 | tf_op jit(solution)/shard_map/ppermute | solution.py:383
  84.9 1.0 copy-start.5
  88.3 5.4 %copy-start.15 = (bf16[2,3,272,128]{3,2,1,0:T(8,128)(2,1)}, bf16[2,3,272,128]{3,2,1,0:T(8,128)(2,1)S(1)}, u32[]{:S(2)}) copy-start(bf16[2,3,272,128]{3,2,1,0:T(8,128)(2,1)S(1)} %get-tuple-element.36) | copy-start | bytes 1253380
  88.3 50.5 %collective-permute-start.6 = (bf16[2,3,272,128]{3,2,1,0:T(8,128)(2,1)}, bf16[2,3,272,128]{3,2,1,0:T(8,128)(2,1)}, u32[]{:S(2)}, u32[]{:S(2)}) collective-permute-start(bf16[2,3,272,128]{3,2,1,0:T(8,128)(2,1)} %get-tuple-element.34), channel_id=1, source_target_pairs={{0,1},{1,2},{2,3},{3,0},{4,5},{5,6},{6,7},{7,4},{8,9},{9,10},{10,1... | collective-permute-start | bytes 1253384 | tf_op jit(solution)/shard_map/ppermute | solution.py:383
  91.5 50.6 %collective-permute-start.7 = (bf16[2,3,272,128]{3,2,1,0:T(8,128)(2,1)}, bf16[2,3,272,128]{3,2,1,0:T(8,128)(2,1)}, u32[]{:S(2)}, u32[]{:S(2)}) collective-permute-start(bf16[2,3,272,128]{3,2,1,0:T(8,128)(2,1)} %get-tuple-element.35), channel_id=1, source_target_pairs={{0,2},{1,3},{2,0},{3,1},{4,6},{5,7},{6,4},{7,5},{8,10},{9,11},{10,... | collective-permute-start | bytes 1253384 | tf_op jit(solution)/shard_map/ppermute | solution.py:383
  95.0 1.3 copy-start
  96.4 31.8 %all-to-all-start.3 = ((bf16[8,4,8,2,16,128]{5,4,3,2,1,0:T(8,128)(2,1)}), bf16[8,4,8,2,16,128]{5,4,3,2,1,0:T(8,128)(2,1)S(1)}, u32[]{:S(2)}, u32[]{:S(2)}) async-start(bf16[8,4,8,2,16,128]{5,4,3,2,1,0:T(8,128)(2,1)} %copy-done), calls=%async_computation.3 | async-start | bytes 4194304 | tf_op jit(solution)/shard_map/all_to_all | solution.py:349
  101.4 25.5 %copy-start.7 = (bf16[2,3,272,128]{3,2,1,0:T(8,128)(2,1)}, bf16[2,3,272,128]{3,2,1,0:T(8,128)(2,1)S(1)}, u32[]{:S(2)}) copy-start(bf16[2,3,272,128]{3,2,1,0:T(8,128)(2,1)S(1)} %collective-permute-done.10.refs_0_.refs_1_) | copy-start | bytes 1253380
  101.4 42.6 %collective-permute-start.8 = (bf16[2,3,272,128]{3,2,1,0:T(8,128)(2,1)}, bf16[2,3,272,128]{3,2,1,0:T(8,128)(2,1)}, u32[]{:S(2)}, u32[]{:S(2)}) collective-permute-start(bf16[2,3,272,128]{3,2,1,0:T(8,128)(2,1)} %copy-done.15), channel_id=1, source_target_pairs={{0,3},{1,0},{2,1},{3,2},{4,7},{5,4},{6,5},{7,6},{8,11},{9,8},{10,9... | collective-permute-start | bytes 1253384 | tf_op jit(solution)/shard_map/ppermute | solution.py:383
  125.1 1.8 %copy-start.9 = (bf16[2,3,272,128]{3,2,1,0:T(8,128)(2,1)}, bf16[2,3,272,128]{3,2,1,0:T(8,128)(2,1)S(1)}, u32[]{:S(2)}) copy-start(bf16[2,3,272,128]{3,2,1,0:T(8,128)(2,1)S(1)} %collective-permute-done.11.refs_1_.refs_2_) | copy-start | bytes 1253380
  128.2 1.8 %copy-start.12 = (bf16[2,2,272,128]{3,2,1,0:T(8,128)(2,1)S(1)}, bf16[2,2,272,128]{3,2,1,0:T(8,128)(2,1)}, u32[]{:S(2)}) copy-start(bf16[2,2,272,128]{3,2,1,0:T(8,128)(2,1)} %copy-done.11) | copy-start | bytes 835588
  128.2 0.7 copy-start.13
  130.0 3.9 %copy-start.6 = (bf16[2,3,272,128]{3,2,1,0:T(8,128)(2,1)S(1)}, bf16[2,3,272,128]{3,2,1,0:T(8,128)(2,1)}, u32[]{:S(2)}) copy-start(bf16[2,3,272,128]{3,2,1,0:T(8,128)(2,1)} %copy-done.4) | copy-start | bytes 1253380
  130.0 3.9 %copy-start.8 = (bf16[2,3,272,128]{3,2,1,0:T(8,128)(2,1)S(1)}, bf16[2,3,272,128]{3,2,1,0:T(8,128)(2,1)}, u32[]{:S(2)}) copy-start(bf16[2,3,272,128]{3,2,1,0:T(8,128)(2,1)} %copy-done.7) | copy-start | bytes 1253380
  130.0 3.9 %copy-start.10 = (bf16[2,3,272,128]{3,2,1,0:T(8,128)(2,1)S(1)}, bf16[2,3,272,128]{3,2,1,0:T(8,128)(2,1)}, u32[]{:S(2)}) copy-start(bf16[2,3,272,128]{3,2,1,0:T(8,128)(2,1)} %copy-done.9) | copy-start | bytes 1253380

commit v19 on v18

--- a/solution.py
+++ b/solution.py
@@ -17,7 +17,7 @@
 QUERY, KEY, VALUE, OUT = range(4)
 CUT_MICROS = 30
 TOKEN_MICROS = 80
-CUTS = (0, 2, 5, 8)
+CUTS = (0, 3, 6, 8)
 VMEM_LIMIT = 16 * 1024 * 1024
 
 

time: 150 us -> 169 us (1.13)
  the two profiles are of different devices: /device:TPU:10 before, /device:TPU:0 now
where the time goes in v19:
time: 169 us; the launch traced here: 168 us
  starting transfers between devices  71.7 us (42%)
  waiting for transfers between devices  56.5 us (33%)
  Pallas kernels  28.2 us (17%)
  local copies, waits for them, and re-layouts  10.7 us (6%)
    ppermute x9, starting transfers between devices, per_device(): lax.ppermute(piece, 'tp', [(i, (i + shift) % t_ways) for i in range(t_way...  44 us
    all_to_all x4, waiting for transfers between devices, over_fsdp(): x = lax.all_to_all(x, 'fsdp', split_axis=0, concat_axis=0, tiled=True)  25.1 us
    all_to_all x4, starting transfers between devices, over_fsdp(): x = lax.all_to_all(x, 'fsdp', split_axis=0, concat_axis=0, tiled=True)  17.1 us
    pallas_call x3, Pallas kernels, absorb(): pl.pallas_call(kernel, grid_spec=pltpu.PrefetchScalarGridSpec(num_scalar_...  14.4 us
    ppermute x1, waiting for transfers between devices, per_device(): second = lax.ppermute(passed, 'tp', [(0, 2), (1, 0), (2, 3), (3, 1)])  11 us
    unnamed x27, local copies, waits for them, and re-layouts  10.7 us
    ppermute x1, waiting for transfers between devices, neighbours(): lax.ppermute(x, axis, [(i + 1, i) for i in range(ways - 1)])  10.3 us
    ppermute x9, waiting for transfers between devices, per_device(): lax.ppermute(piece, 'tp', [(i, (i + shift) % t_ways) for i in range(t_way...  8.85 us
  transfers between devices with their start and end apart: 17, of which 6 were waited for; matrix products, arithmetic and copies ran while one was open for 0% of the time, Pallas kernels for 13%

profile of v19, /device:TPU:0, one launch (start us, length us, event | category | flops | bytes accessed | tf_op | source)
XLA Modules:
  0.0 167.9 jit_solution(17056514263027323895)
XLA Ops:
  0.6 0.8 copy.10.offsets
  1.4 0.0 copy-start.9
  1.4 3.1 %copy.14 = bf16[1,2,9728,128]{3,2,1,0:T(8,128)(2,1)S(1)} copy(bf16[1,2,9728,128]{3,1,2,0:T(2,128)(2,1)} %bitcast.19) | data formatting | bytes 9961472
  4.5 0.0 copy-done.9
  4.6 3.3 %pack.1 = (bf16[8,16,16,128]{3,2,1,0:T(8,128)(2,1)S(1)}, bf16[8,51,16,128]{3,2,1,0:T(8,128)(2,1)S(1)}, bf16[8,51,16,128]{3,2,1,0:T(8,128)(2,1)}, bf16[8,34,16,128]{3,2,1,0:T(8,128)(2,1)S(1)}) custom-call(s32[2,32,4]{2,1,0:T(8,128)S(1)} %copy.10.offsets, s32[2,32]{1,0:T(2,128)S(1)} %copy-done.9, bf16[2,608,16,128]{3,2,1,0:T(8,128)(2,1)S(1)} %bitcast.10), custom_call_target="tpu_custom_call" | custom-call | bytes 9961472 | tf_op jit(solution)/shard_map/pack/pallas_call | solution.py:77
  7.9 0.0 copy-start.1
  7.9 1.2 copy-done.1
  9.1 1.0 copy-done.2
  10.1 5.3 %all-to-all-start.2 = ((bf16[8,51,16,128]{3,2,1,0:T(8,128)(2,1)}), bf16[8,51,16,128]{3,2,1,0:T(8,128)(2,1)S(1)}, u32[]{:S(2)}, u32[]{:S(2)}) async-start(bf16[8,51,16,128]{3,2,1,0:T(8,128)(2,1)} %copy-done.1), calls=%async_computation.2 | async-start | bytes 3342336 | tf_op jit(solution)/shard_map/all_to_all | solution.py:349
  15.4 1.3 collective-permute-start.1
  16.6 4.6 %collective-permute-start = (bf16[8,8,2,16,128]{4,3,2,1,0:T(8,128)(2,1)S(1)}, bf16[8,8,2,16,128]{4,3,2,1,0:T(8,128)(2,1)S(1)}, u32[]{:S(2)}, u32[]{:S(2)}) collective-permute-start(bf16[8,8,2,16,128]{4,3,2,1,0:T(8,128)(2,1)S(1)} %bitcast.12), channel_id=1, source_target_pairs={{0,1},{1,2},{2,3},{4,5},{5,6},{6,7},{8,9},{9,10},{10,11},{12,13},{... | collective-permute-start | bytes 1572872 | tf_op jit(solution)/shard_map/ppermute | solution.py:156
  21.2 10.3 %collective-permute-done.1.down_ref = bf16[8,8,2,16,128]{4,3,2,1,0:T(8,128)(2,1)S(1)} collective-permute-done((bf16[8,8,2,16,128]{4,3,2,1,0:T(8,128)(2,1)S(1)}, bf16[8,8,2,16,128]{4,3,2,1,0:T(8,128)(2,1)S(1)}, u32[]{:S(2)}, u32[]{:S(2)}) %collective-permute-start.1) | collective-permute-done | bytes 524320 | tf_op jit(solution)/shard_map/ppermute | solution.py:157
  31.6 1.2 collective-permute-done.up_ref
  32.8 0.8 pass_on.1.refs_0_
  33.6 3.5 %collective-permute-start.2 = (bf16[8,8,2,16,128]{4,3,2,1,0:T(8,128)(2,1)}, bf16[8,8,2,16,128]{4,3,2,1,0:T(8,128)(2,1)}, u32[]{:S(2)}, u32[]{:S(2)}) collective-permute-start(bf16[8,8,2,16,128]{4,3,2,1,0:T(8,128)(2,1)} %pass_on.1.refs_0_), channel_id=1, source_target_pairs={{0,2},{1,0},{2,3},{3,1},{4,6},{5,4},{6,7},{7,5},{8,10},{9,8},{10,1... | collective-permute-start | bytes 1572872 | tf_op jit(solution)/shard_map/ppermute | solution.py:365
  37.1 0.0 copy-done.11
  37.1 0.1 copy.13.mapped
  37.2 11.0 %collective-permute-done.2.refs_1_.second_ref = bf16[8,8,2,16,128]{4,3,2,1,0:T(8,128)(2,1)} collective-permute-done((bf16[8,8,2,16,128]{4,3,2,1,0:T(8,128)(2,1)}, bf16[8,8,2,16,128]{4,3,2,1,0:T(8,128)(2,1)}, u32[]{:S(2)}, u32[]{:S(2)}) %collective-permute-start.2) | collective-permute-done | bytes 524320 | tf_op jit(solution)/shard_map/ppermute | solution.py:365
  48.2 1.3 collective-permute-start.9
  49.4 0.0 all-to-all-done.2
  49.4 4.3 %all-to-all-start.1 = ((bf16[8,51,16,128]{3,2,1,0:T(8,128)(2,1)}), bf16[8,51,16,128]{3,2,1,0:T(8,128)(2,1)}, u32[]{:S(2)}, u32[]{:S(2)}) async-start(bf16[8,51,16,128]{3,2,1,0:T(8,128)(2,1)} %get-tuple-element.25), calls=%async_computation.1 | async-start | bytes 3342336 | tf_op jit(solution)/shard_map/all_to_all | solution.py:349
  53.8 1.8 %cut.3 = (bf16[2,3,272,128]{3,2,1,0:T(8,128)(2,1)S(1)}, bf16[2,3,272,128]{3,2,1,0:T(8,128)(2,1)}, bf16[2,3,272,128]{3,2,1,0:T(8,128)(2,1)}, bf16[2,3,272,128]{3,2,1,0:T(8,128)(2,1)}) custom-call(s32[8,4]{1,0:T(8,128)S(1)} %copy.13.mapped, bf16[8,816,128]{2,1,0:T(8,128)(2,1)S(1)} %bitcast.15, bf16[8,8,2,16,128]{4,3,2,1,0:T(8,128)(2,1)} %pass_on.1.refs_0_), custom_call_target="tpu_custom_call" | custom-call | flops 34500001792 | bytes 3342336 | tf_op jit(solution)/shard_map/cut/pallas_call | solution.py:121
  55.6 0.8 copy-done.3
  56.4 3.4 %collective-permute-start.3 = (bf16[2,3,272,128]{3,2,1,0:T(8,128)(2,1)}, bf16[2,3,272,128]{3,2,1,0:T(8,128)(2,1)}, u32[]{:S(2)}, u32[]{:S(2)}) collective-permute-start(bf16[2,3,272,128]{3,2,1,0:T(8,128)(2,1)} %get-tuple-element.30), channel_id=1, source_target_pairs={{0,1},{1,2},{2,3},{3,0},{4,5},{5,6},{6,7},{7,4},{8,9},{9,10},{10,1... | collective-permute-start | bytes 1253384 | tf_op jit(solution)/shard_map/ppermute | solution.py:383
  59.8 2.1 %collective-permute-start.4 = (bf16[2,3,272,128]{3,2,1,0:T(8,128)(2,1)}, bf16[2,3,272,128]{3,2,1,0:T(8,128)(2,1)}, u32[]{:S(2)}, u32[]{:S(2)}) collective-permute-start(bf16[2,3,272,128]{3,2,1,0:T(8,128)(2,1)} %get-tuple-element.31), channel_id=1, source_target_pairs={{0,2},{1,3},{2,0},{3,1},{4,6},{5,7},{6,4},{7,5},{8,10},{9,11},{10,... | collective-permute-start | bytes 1253384 | tf_op jit(solution)/shard_map/ppermute | solution.py:383
  61.9 2.9 %collective-permute-start.5 = (bf16[2,3,272,128]{3,2,1,0:T(8,128)(2,1)}, bf16[2,3,272,128]{3,2,1,0:T(8,128)(2,1)}, u32[]{:S(2)}, u32[]{:S(2)}) collective-permute-start(bf16[2,3,272,128]{3,2,1,0:T(8,128)(2,1)} %get-tuple-element.32), channel_id=1, source_target_pairs={{0,3},{1,0},{2,1},{3,2},{4,7},{5,4},{6,5},{7,6},{8,11},{9,8},{10,9... | collective-permute-start | bytes 1253384 | tf_op jit(solution)/shard_map/ppermute | solution.py:383
  64.8 11.1 %all-to-all-done.1 = bf16[8,51,16,128]{3,2,1,0:T(8,128)(2,1)} async-done(((bf16[8,51,16,128]{3,2,1,0:T(8,128)(2,1)}), bf16[8,51,16,128]{3,2,1,0:T(8,128)(2,1)}, u32[]{:S(2)}, u32[]{:S(2)}) %all-to-all-start.1) | async-done | bytes 1671200 | tf_op jit(solution)/shard_map/all_to_all | solution.py:349
  75.9 3.6 %all-to-all-start = ((bf16[8,34,16,128]{3,2,1,0:T(8,128)(2,1)}), bf16[8,34,16,128]{3,2,1,0:T(8,128)(2,1)S(1)}, u32[]{:S(2)}, u32[]{:S(2)}) async-start(bf16[8,34,16,128]{3,2,1,0:T(8,128)(2,1)} %copy-done.2), calls=%async_computation | async-start | bytes 2228224 | tf_op jit(solution)/shard_map/all_to_all | solution.py:349
  79.4 0.0 copy-done.4
  79.4 2.6 %cut.4 = (bf16[2,3,272,128]{3,2,1,0:T(8,128)(2,1)S(1)}, bf16[2,3,272,128]{3,2,1,0:T(8,128)(2,1)}, bf16[2,3,272,128]{3,2,1,0:T(8,128)(2,1)}, bf16[2,3,272,128]{3,2,1,0:T(8,128)(2,1)}) custom-call(s32[8,4]{1,0:T(8,128)S(1)} %copy.13.mapped, bf16[8,816,128]{2,1,0:T(8,128)(2,1)} %bitcast.2.source, bf16[2,3,272,128]{3,2,1,0:T(8,128)(2,1)S(1)} %copy-done.4, ...), custom_call_target="tpu_custom_call" | custom-call | flops 34500001792 | bytes 3342336 | tf_op jit(solution)/shard_map/cut/pallas_call | solution.py:121
  82.0 0.8 copy-done.5
  82.8 3.5 %collective-permute-start.10 = (bf16[2,3,272,128]{3,2,1,0:T(8,128)(2,1)}, bf16[2,3,272,128]{3,2,1,0:T(8,128)(2,1)}, u32[]{:S(2)}, u32[]{:S(2)}) collective-permute-start(bf16[2,3,272,128]{3,2,1,0:T(8,128)(2,1)} %get-tuple-element.37), channel_id=1, source_target_pairs={{0,1},{1,2},{2,3},{3,0},{4,5},{5,6},{6,7},{7,4},{8,9},{9,10},{10,1... | collective-permute-start | bytes 1253384 | tf_op jit(solution)/shard_map/ppermute | solution.py:383
  86.3 0.0 collective-permute-done.3.refs_1_
  86.3 6.3 %collective-permute-start.11 = (bf16[2,3,272,128]{3,2,1,0:T(8,128)(2,1)}, bf16[2,3,272,128]{3,2,1,0:T(8,128)(2,1)}, u32[]{:S(2)}, u32[]{:S(2)}) collective-permute-start(bf16[2,3,272,128]{3,2,1,0:T(8,128)(2,1)} %get-tuple-element.38), channel_id=1, source_target_pairs={{0,2},{1,3},{2,0},{3,1},{4,6},{5,7},{6,4},{7,5},{8,10},{9,11},{10,... | collective-permute-start | bytes 1253384 | tf_op jit(solution)/shard_map/ppermute | solution.py:383
  92.6 0.0 collective-permute-done.4.refs_2_
  92.6 18.8 %collective-permute-start.12 = (bf16[2,3,272,128]{3,2,1,0:T(8,128)(2,1)}, bf16[2,3,272,128]{3,2,1,0:T(8,128)(2,1)}, u32[]{:S(2)}, u32[]{:S(2)}) collective-permute-start(bf16[2,3,272,128]{3,2,1,0:T(8,128)(2,1)} %get-tuple-element.39), channel_id=1, source_target_pairs={{0,3},{1,0},{2,1},{3,2},{4,7},{5,4},{6,5},{7,6},{8,11},{9,8},{10,9... | collective-permute-start | bytes 1253384 | tf_op jit(solution)/shard_map/ppermute | solution.py:383
  111.4 0.0 all-to-all-done
  111.4 0.0 collective-permute-done.5.refs_3_
  111.4 1.0 copy-done.6
  112.4 1.6 cut.5
  114.0 4.5 %collective-permute-start.6 = (bf16[2,2,272,128]{3,2,1,0:T(8,128)(2,1)}, bf16[2,2,272,128]{3,2,1,0:T(8,128)(2,1)S(1)}, u32[]{:S(2)}, u32[]{:S(2)}) collective-permute-start(bf16[2,2,272,128]{3,2,1,0:T(8,128)(2,1)} %get-tuple-element.34), channel_id=1, source_target_pairs={{0,1},{1,2},{2,3},{3,0},{4,5},{5,6},{6,7},{7,4},{8,9},{9,10},{10,1... | collective-permute-start | bytes 835592 | tf_op jit(solution)/shard_map/ppermute | solution.py:383
  118.5 0.0 collective-permute-done.9.third_ref
  118.5 0.0 collective-permute-start.7
  118.5 0.0 copy-done.10
  118.5 1.3 join.1
  119.8 0.0 copy-start
  119.8 1.3 copy-done
  121.1 3.9 %all-to-all-start.3 = ((bf16[8,4,8,2,16,128]{5,4,3,2,1,0:T(8,128)(2,1)}), bf16[8,4,8,2,16,128]{5,4,3,2,1,0:T(8,128)(2,1)S(1)}, u32[]{:S(2)}, u32[]{:S(2)}) async-start(bf16[8,4,8,2,16,128]{5,4,3,2,1,0:T(8,128)(2,1)} %copy-done), calls=%async_computation.3 | async-start | bytes 4194304 | tf_op jit(solution)/shard_map/all_to_all | solution.py:349
  125.0 0.0 collective-permute-done.10.refs_0_.refs_1_
  125.0 2.5 %collective-permute-start.8 = (bf16[2,2,272,128]{3,2,1,0:T(8,128)(2,1)}, bf16[2,2,272,128]{3,2,1,0:T(8,128)(2,1)}, u32[]{:S(2)}, u32[]{:S(2)}) collective-permute-start(bf16[2,2,272,128]{3,2,1,0:T(8,128)(2,1)} %copy-done.10), channel_id=1, source_target_pairs={{0,3},{1,0},{2,1},{3,2},{4,7},{5,4},{6,5},{7,6},{8,11},{9,8},{10,9... | collective-permute-start | bytes 835592 | tf_op jit(solution)/shard_map/ppermute | solution.py:383
  127.5 8.8 %collective-permute-done.11.refs_1_.refs_2_ = bf16[2,3,272,128]{3,2,1,0:T(8,128)(2,1)} collective-permute-done((bf16[2,3,272,128]{3,2,1,0:T(8,128)(2,1)}, bf16[2,3,272,128]{3,2,1,0:T(8,128)(2,1)}, u32[]{:S(2)}, u32[]{:S(2)}) %collective-permute-start.11) | collective-permute-done | bytes 417824 | tf_op jit(solution)/shard_map/ppermute | solution.py:383
  136.3 0.0 collective-permute-done.12.refs_2_.refs_3_
  136.3 1.3 token_.1.refs_0_
  137.6 14.1 %all-to-all-done.3.pieces = bf16[8,4,8,2,16,128]{5,4,3,2,1,0:T(8,128)(2,1)S(1)} async-done(((bf16[8,4,8,2,16,128]{5,4,3,2,1,0:T(8,128)(2,1)}), bf16[8,4,8,2,16,128]{5,4,3,2,1,0:T(8,128)(2,1)S(1)}, u32[]{:S(2)}, u32[]{:S(2)}) %all-to-all-start.3) | async-done | bytes 2097184 | tf_op jit(solution)/shard_map/all_to_all | solution.py:349
  151.7 0.7 copy-done.8
  152.4 1.0 assemble.1.refs_4_
  153.4 0.0 copy-start.7
  153.4 5.4 %absorb.3 = (bf16[8,2,4,48,512]{4,3,2,1,0:T(8,128)(2,1)}, bf16[8,2,4,224,512]{4,3,2,1,0:T(8,128)(2,1)}) custom-call(s32[1]{0:T(128)} %bitcast.me_ref.at, bf16[2,3,272,128]{3,2,1,0:T(8,128)(2,1)S(1)} %copy-done.4, bf16[2,3,272,128]{3,2,1,0:T(8,128)(2,1)} %collective-permute-done.3.refs_1_, bf16[2,3,272,128]{3,2,1,0:T(8,128)(2,1)} %collective-permute-done.4.refs_2_, ...), custom_call_target="tpu_custom_call" | custom-call | flops 855638016 | bytes 8355840 | tf_op jit(solution)/shard_map/absorb/pallas_call | solution.py:294
  158.8 0.0 copy-done.7
  158.8 5.4 %absorb.4 = (bf16[8,2,4,48,512]{4,3,2,1,0:T(8,128)(2,1)}, bf16[8,2,4,224,512]{4,3,2,1,0:T(8,128)(2,1)}) custom-call(s32[1]{0:T(128)} %bitcast.me_ref.at, bf16[2,3,272,128]{3,2,1,0:T(8,128)(2,1)S(1)} %copy-done.7, bf16[2,3,272,128]{3,2,1,0:T(8,128)(2,1)} %collective-permute-done.10.refs_0_.refs_1_, ...), custom_call_target="tpu_custom_call", output_to_operand_aliasing={{0}: (6, {}), {1}: (7, {})} | custom-call | flops 855638016 | bytes 8355840 | tf_op jit(solution)/shard_map/absorb/pallas_call | solution.py:294
  164.1 0.0 collective-permute-done.6.refs_1_
  164.2 0.0 collective-permute-done.7.refs_2_
  164.2 0.0 collective-permute-done.8.refs_3_
  164.2 3.7 %absorb.5 = (bf16[8,2,4,48,512]{4,3,2,1,0:T(8,128)(2,1)}, bf16[8,2,4,224,512]{4,3,2,1,0:T(8,128)(2,1)}) custom-call(s32[1]{0:T(128)} %bitcast.me_ref.at, bf16[2,2,272,128]{3,2,1,0:T(8,128)(2,1)S(1)} %get-tuple-element.33.refs_0_, bf16[2,2,272,128]{3,2,1,0:T(8,128)(2,1)S(1)} %collective-permute-done.6.refs_1_, ...), custom_call_target="tpu_custom_call", output_to_operand_aliasing={{0}: (6, {}), {1}: (7, {})} | custom-call | flops 570425344 | bytes 5570560 | tf_op jit(solution)/shard_map/absorb/pallas_call | solution.py:294
  (8 shorter events, 0.0 us)
Async XLA Ops:
  1.4 3.1 %copy-start.9 = (s32[2,32]{1,0:T(2,128)S(1)}, s32[2,32]{1,0:T(2,128)}, u32[]{:S(2)}) copy-start(s32[2,32]{1,0:T(2,128)} %owners.1) | copy-start | bytes 772
  7.9 1.2 copy-start.1
  9.1 1.0 copy-start.2
  10.1 27.0 %copy-start.11 = (s32[8,4]{0,1:T(4,128)S(1)}, s32[8,4]{0,1:T(4,128)}, u32[]{:S(2)}) copy-start(s32[8,4]{0,1:T(4,128)} %param.7) | copy-start | bytes 388
  10.1 39.4 %all-to-all-start.2 = ((bf16[8,51,16,128]{3,2,1,0:T(8,128)(2,1)}), bf16[8,51,16,128]{3,2,1,0:T(8,128)(2,1)S(1)}, u32[]{:S(2)}, u32[]{:S(2)}) async-start(bf16[8,51,16,128]{3,2,1,0:T(8,128)(2,1)} %copy-done.1), calls=%async_computation.2 | async-start | bytes 3342336 | tf_op jit(solution)/shard_map/all_to_all | solution.py:349
  15.4 16.2 %collective-permute-start.1 = (bf16[8,8,2,16,128]{4,3,2,1,0:T(8,128)(2,1)S(1)}, bf16[8,8,2,16,128]{4,3,2,1,0:T(8,128)(2,1)S(1)}, u32[]{:S(2)}, u32[]{:S(2)}) collective-permute-start(bf16[8,8,2,16,128]{4,3,2,1,0:T(8,128)(2,1)S(1)} %bitcast.11), channel_id=1, source_target_pairs={{1,0},{2,1},{3,2},{5,4},{6,5},{7,6},{9,8},{10,9},{11,10},{13,12},{... | collective-permute-start | bytes 1572872 | tf_op jit(solution)/shard_map/ppermute | solution.py:157
  16.6 16.1 %collective-permute-start = (bf16[8,8,2,16,128]{4,3,2,1,0:T(8,128)(2,1)S(1)}, bf16[8,8,2,16,128]{4,3,2,1,0:T(8,128)(2,1)S(1)}, u32[]{:S(2)}, u32[]{:S(2)}) collective-permute-start(bf16[8,8,2,16,128]{4,3,2,1,0:T(8,128)(2,1)S(1)} %bitcast.12), channel_id=1, source_target_pairs={{0,1},{1,2},{2,3},{4,5},{5,6},{6,7},{8,9},{9,10},{10,11},{12,13},{... | collective-permute-start | bytes 1572872 | tf_op jit(solution)/shard_map/ppermute | solution.py:156
  33.6 14.6 %collective-permute-start.2 = (bf16[8,8,2,16,128]{4,3,2,1,0:T(8,128)(2,1)}, bf16[8,8,2,16,128]{4,3,2,1,0:T(8,128)(2,1)}, u32[]{:S(2)}, u32[]{:S(2)}) collective-permute-start(bf16[8,8,2,16,128]{4,3,2,1,0:T(8,128)(2,1)} %pass_on.1.refs_0_), channel_id=1, source_target_pairs={{0,2},{1,0},{2,3},{3,1},{4,6},{5,4},{6,7},{7,5},{8,10},{9,8},{10,1... | collective-permute-start | bytes 1572872 | tf_op jit(solution)/shard_map/ppermute | solution.py:365
  48.2 70.3 %collective-permute-start.9 = (bf16[8,8,2,16,128]{4,3,2,1,0:T(8,128)(2,1)}, bf16[8,8,2,16,128]{4,3,2,1,0:T(8,128)(2,1)}, u32[]{:S(2)}, u32[]{:S(2)}) collective-permute-start(bf16[8,8,2,16,128]{4,3,2,1,0:T(8,128)(2,1)} %collective-permute-done.2.refs_1_.second_ref), channel_id=1, source_target_pairs={{1,0},{2,3},{5,4},{6,7},{9,8},{10,11},{13,12},{14,15},{17,16},{18,... | collective-permute-start | bytes 1572872 | tf_op jit(solution)/shard_map/ppermute | solution.py:366
  49.4 26.4 %all-to-all-start.1 = ((bf16[8,51,16,128]{3,2,1,0:T(8,128)(2,1)}), bf16[8,51,16,128]{3,2,1,0:T(8,128)(2,1)}, u32[]{:S(2)}, u32[]{:S(2)}) async-start(bf16[8,51,16,128]{3,2,1,0:T(8,128)(2,1)} %get-tuple-element.25), calls=%async_computation.1 | async-start | bytes 3342336 | tf_op jit(solution)/shard_map/all_to_all | solution.py:349
  55.6 0.8 copy-start.3
  56.4 23.1 %copy-start.4 = (bf16[2,3,272,128]{3,2,1,0:T(8,128)(2,1)S(1)}, bf16[2,3,272,128]{3,2,1,0:T(8,128)(2,1)}, u32[]{:S(2)}) copy-start(bf16[2,3,272,128]{3,2,1,0:T(8,128)(2,1)} %copy-done.3) | copy-start | bytes 1253380
  56.4 29.9 %collective-permute-start.3 = (bf16[2,3,272,128]{3,2,1,0:T(8,128)(2,1)}, bf16[2,3,272,128]{3,2,1,0:T(8,128)(2,1)}, u32[]{:S(2)}, u32[]{:S(2)}) collective-permute-start(bf16[2,3,272,128]{3,2,1,0:T(8,128)(2,1)} %get-tuple-element.30), channel_id=1, source_target_pairs={{0,1},{1,2},{2,3},{3,0},{4,5},{5,6},{6,7},{7,4},{8,9},{9,10},{10,1... | collective-permute-start | bytes 1253384 | tf_op jit(solution)/shard_map/ppermute | solution.py:383
  59.8 32.7 %collective-permute-start.4 = (bf16[2,3,272,128]{3,2,1,0:T(8,128)(2,1)}, bf16[2,3,272,128]{3,2,1,0:T(8,128)(2,1)}, u32[]{:S(2)}, u32[]{:S(2)}) collective-permute-start(bf16[2,3,272,128]{3,2,1,0:T(8,128)(2,1)} %get-tuple-element.31), channel_id=1, source_target_pairs={{0,2},{1,3},{2,0},{3,1},{4,6},{5,7},{6,4},{7,5},{8,10},{9,11},{10,... | collective-permute-start | bytes 1253384 | tf_op jit(solution)/shard_map/ppermute | solution.py:383
  61.9 49.5 %collective-permute-start.5 = (bf16[2,3,272,128]{3,2,1,0:T(8,128)(2,1)}, bf16[2,3,272,128]{3,2,1,0:T(8,128)(2,1)}, u32[]{:S(2)}, u32[]{:S(2)}) collective-permute-start(bf16[2,3,272,128]{3,2,1,0:T(8,128)(2,1)} %get-tuple-element.32), channel_id=1, source_target_pairs={{0,3},{1,0},{2,1},{3,2},{4,7},{5,4},{6,5},{7,6},{8,11},{9,8},{10,9... | collective-permute-start | bytes 1253384 | tf_op jit(solution)/shard_map/ppermute | solution.py:383
  75.9 35.5 %all-to-all-start = ((bf16[8,34,16,128]{3,2,1,0:T(8,128)(2,1)}), bf16[8,34,16,128]{3,2,1,0:T(8,128)(2,1)S(1)}, u32[]{:S(2)}, u32[]{:S(2)}) async-start(bf16[8,34,16,128]{3,2,1,0:T(8,128)(2,1)} %copy-done.2), calls=%async_computation | async-start | bytes 2228224 | tf_op jit(solution)/shard_map/all_to_all | solution.py:349
  82.0 0.8 copy-start.5
  82.8 42.2 %collective-permute-start.10 = (bf16[2,3,272,128]{3,2,1,0:T(8,128)(2,1)}, bf16[2,3,272,128]{3,2,1,0:T(8,128)(2,1)}, u32[]{:S(2)}, u32[]{:S(2)}) collective-permute-start(bf16[2,3,272,128]{3,2,1,0:T(8,128)(2,1)} %get-tuple-element.37), channel_id=1, source_target_pairs={{0,1},{1,2},{2,3},{3,0},{4,5},{5,6},{6,7},{7,4},{8,9},{9,10},{10,1... | collective-permute-start | bytes 1253384 | tf_op jit(solution)/shard_map/ppermute | solution.py:383
  86.3 50.1 %collective-permute-start.11 = (bf16[2,3,272,128]{3,2,1,0:T(8,128)(2,1)}, bf16[2,3,272,128]{3,2,1,0:T(8,128)(2,1)}, u32[]{:S(2)}, u32[]{:S(2)}) collective-permute-start(bf16[2,3,272,128]{3,2,1,0:T(8,128)(2,1)} %get-tuple-element.38), channel_id=1, source_target_pairs={{0,2},{1,3},{2,0},{3,1},{4,6},{5,7},{6,4},{7,5},{8,10},{9,11},{10,... | collective-permute-start | bytes 1253384 | tf_op jit(solution)/shard_map/ppermute | solution.py:383
  92.6 43.8 %collective-permute-start.12 = (bf16[2,3,272,128]{3,2,1,0:T(8,128)(2,1)}, bf16[2,3,272,128]{3,2,1,0:T(8,128)(2,1)}, u32[]{:S(2)}, u32[]{:S(2)}) collective-permute-start(bf16[2,3,272,128]{3,2,1,0:T(8,128)(2,1)} %get-tuple-element.39), channel_id=1, source_target_pairs={{0,3},{1,0},{2,1},{3,2},{4,7},{5,4},{6,5},{7,6},{8,11},{9,8},{10,9... | collective-permute-start | bytes 1253384 | tf_op jit(solution)/shard_map/ppermute | solution.py:383
  111.4 1.0 copy-start.6
  114.0 4.5 %copy-start.10 = (bf16[2,2,272,128]{3,2,1,0:T(8,128)(2,1)}, bf16[2,2,272,128]{3,2,1,0:T(8,128)(2,1)S(1)}, u32[]{:S(2)}) copy-start(bf16[2,2,272,128]{3,2,1,0:T(8,128)(2,1)S(1)} %get-tuple-element.36) | copy-start | bytes 835588
  114.0 50.2 %collective-permute-start.6 = (bf16[2,2,272,128]{3,2,1,0:T(8,128)(2,1)}, bf16[2,2,272,128]{3,2,1,0:T(8,128)(2,1)S(1)}, u32[]{:S(2)}, u32[]{:S(2)}) collective-permute-start(bf16[2,2,272,128]{3,2,1,0:T(8,128)(2,1)} %get-tuple-element.34), channel_id=1, source_target_pairs={{0,1},{1,2},{2,3},{3,0},{4,5},{5,6},{6,7},{7,4},{8,9},{9,10},{10,1... | collective-permute-start | bytes 835592 | tf_op jit(solution)/shard_map/ppermute | solution.py:383
  118.5 45.7 %collective-permute-start.7 = (bf16[2,2,272,128]{3,2,1,0:T(8,128)(2,1)}, bf16[2,2,272,128]{3,2,1,0:T(8,128)(2,1)S(1)}, u32[]{:S(2)}, u32[]{:S(2)}) collective-permute-start(bf16[2,2,272,128]{3,2,1,0:T(8,128)(2,1)} %get-tuple-element.35), channel_id=1, source_target_pairs={{0,2},{1,3},{2,0},{3,1},{4,6},{5,7},{6,4},{7,5},{8,10},{9,11},{10,... | collective-permute-start | bytes 835592 | tf_op jit(solution)/shard_map/ppermute | solution.py:383
  119.8 1.3 copy-start
  121.1 30.5 %all-to-all-start.3 = ((bf16[8,4,8,2,16,128]{5,4,3,2,1,0:T(8,128)(2,1)}), bf16[8,4,8,2,16,128]{5,4,3,2,1,0:T(8,128)(2,1)S(1)}, u32[]{:S(2)}, u32[]{:S(2)}) async-start(bf16[8,4,8,2,16,128]{5,4,3,2,1,0:T(8,128)(2,1)} %copy-done), calls=%async_computation.3 | async-start | bytes 4194304 | tf_op jit(solution)/shard_map/all_to_all | solution.py:349
  125.0 39.1 %collective-permute-start.8 = (bf16[2,2,272,128]{3,2,1,0:T(8,128)(2,1)}, bf16[2,2,272,128]{3,2,1,0:T(8,128)(2,1)}, u32[]{:S(2)}, u32[]{:S(2)}) collective-permute-start(bf16[2,2,272,128]{3,2,1,0:T(8,128)(2,1)} %copy-done.10), channel_id=1, source_target_pairs={{0,3},{1,0},{2,1},{3,2},{4,7},{5,4},{6,5},{7,6},{8,11},{9,8},{10,9... | collective-permute-start | bytes 835592 | tf_op jit(solution)/shard_map/ppermute | solution.py:383
  151.7 0.7 copy-start.8
  153.4 5.4 %copy-start.7 = (bf16[2,3,272,128]{3,2,1,0:T(8,128)(2,1)S(1)}, bf16[2,3,272,128]{3,2,1,0:T(8,128)(2,1)}, u32[]{:S(2)}) copy-start(bf16[2,3,272,128]{3,2,1,0:T(8,128)(2,1)} %copy-done.5) | copy-start | bytes 1253380
